TPU v7x, 128 devices: a whole 4x4x4 slice. The times are simulated.
128 devices in a mesh: row: 8 (over z, core), col: 8 (over x, y_hi), dp: 2 (over y_lo).
Axes of the slice: x: 4, y: 4 (y_hi: 2, y_lo: 2; y = y_hi * 2 + y_lo), z: 4, core: 2. Of those that a mesh axis runs over, the one named last changes fastest.
Arguments:
- tokens: bfloat16 [2048, 8192], P(('col', 'dp'), 'row'), may hold values from -6 to 6
- out_grad: bfloat16 [2048, 8192], P(('col', 'dp'), 'row'), may hold values from -6 to 6
- weight_in: bfloat16 [8192, 16384], P('row', 'col'), may hold values from -0.0625 to 0.0625
- weight_out: bfloat16 [16384, 8192], P('col', 'row'), may hold values from -0.046875 to 0.046875
Outputs:
- mixed: bfloat16 [2048, 8192], P(('col', 'dp'), 'row')
- token_grad: bfloat16 [2048, 8192], P(('col', 'dp'), 'row')
- grad_in: float32 [8192, 16384], P('row', ('col', 'dp'))
- grad_out: float32 [16384, 8192], P(('col', 'dp'), 'row')
All inputs are finite; a program needn't handle non-finite values.
Results may differ from a plain program's by a relative error of at most 0.035.
Values may be sent and summed in bfloat16 or wider, within the bound.
No kernel may reach another device: no remote copies, remote signals or barrier semaphores. Data moves between devices by JAX's collectives and lax.ppermute only.
A program may use at most 128 MiB of HBM per device.

v0:
```python
import math

import jax
import jax.numpy as jnp
from jax import lax
from jax.sharding import PartitionSpec as P


def gelu_parts(pre):
    cdf = 0.5 * (1.0 + jax.scipy.special.erf(pre * (1.0 / math.sqrt(2.0))))
    activated = pre * cdf
    slope = cdf + pre * jnp.exp(-0.5 * pre * pre) * (1.0 / math.sqrt(2.0 * math.pi))
    return (activated, slope)


def shards(tokens, out_grad, weight_in, weight_out):
    panel = lax.all_gather(tokens, "col", axis=0, tiled=True)
    count_all = panel.shape[0]
    factor = 1.0 / math.sqrt(count_all * lax.axis_size("dp"))
    pre = lax.psum_scatter(
        jnp.dot(panel, weight_in, preferred_element_type=jnp.float32).astype(jnp.bfloat16),
        "row",
        scatter_dimension=0,
        tiled=True,
    ).astype(jnp.float32)
    activated, slope = gelu_parts(pre)
    act = lax.all_gather(activated.astype(jnp.bfloat16), "row", axis=0, tiled=True)
    mixed = lax.psum_scatter(
        jnp.dot(act, weight_out, preferred_element_type=jnp.float32).astype(jnp.bfloat16),
        "col",
        scatter_dimension=0,
        tiled=True,
    )
    grad_panel = lax.all_gather(out_grad, "col", axis=0, tiled=True)
    out_local = lax.dot_general(
        act, grad_panel, (((0,), (0,)), ((), ())), preferred_element_type=jnp.float32
    )
    grad_out = (
        lax.psum_scatter(
            out_local.astype(jnp.bfloat16), "dp", scatter_dimension=0, tiled=True
        ).astype(jnp.float32)
        * factor
    )
    back = lax.psum_scatter(
        lax.dot_general(
            grad_panel, weight_out, (((1,), (1,)), ((), ())), preferred_element_type=jnp.float32
        ).astype(jnp.bfloat16),
        "row",
        scatter_dimension=0,
        tiled=True,
    ).astype(jnp.float32)
    dpre = lax.all_gather((back * slope).astype(jnp.bfloat16), "row", axis=0, tiled=True)
    token_grad = lax.psum_scatter(
        lax.dot_general(
            dpre, weight_in, (((1,), (1,)), ((), ())), preferred_element_type=jnp.float32
        ).astype(jnp.bfloat16),
        "col",
        scatter_dimension=0,
        tiled=True,
    )
    in_local = lax.dot_general(
        panel, dpre, (((0,), (0,)), ((), ())), preferred_element_type=jnp.float32
    )
    grad_in = (
        lax.psum_scatter(
            in_local.astype(jnp.bfloat16), "dp", scatter_dimension=1, tiled=True
        ).astype(jnp.float32)
        * factor
    )
    return (mixed, token_grad, grad_in, grad_out)


def solution(mesh):
    placed = (P(("col", "dp"), "row"), P(("col", "dp"), "row"), P("row", "col"), P("col", "row"))
    return jax.shard_map(
        shards,
        mesh=mesh,
        in_specs=placed,
        out_specs=(
            P(("col", "dp"), "row"),
            P(("col", "dp"), "row"),
            P("row", ("col", "dp")),
            P(("col", "dp"), "row"),
        ),
        check_vma=False,
    )
```

profile of v0, /device:TPU:8, one launch (start us, length us, event | category | flops | bytes accessed | tf_op | source)
XLA Modules:
  0.0 557.9 jit_solution(6864496747568961133)
XLA Ops:
  7.2 0.0 all-gather.9.cloned.1.call-start
  7.2 0.7 all-gather.9.cloned.1.call-update
  7.9 0.0 all-gather.5.cloned.1.call-start
  7.9 0.7 all-gather.5.cloned.1.call-update
  8.6 0.0 reduce-scatter.11.cloned.1.call-start
  8.7 58.0 %all-gather.9.cloned.1.call-done = bf16[1024,1024]{1,0:T(8,128)(2,1)} async-done(((bf16[128,1024]{1,0:T(8,128)(2,1)}), bf16[1024,1024]{1,0:T(8,128)(2,1)}) %all-gather.9.cloned.1.call-update) | async-done | bytes 2097168 | tf_op jit(solution)/shard_map/all_gather | solution.py:34
  66.7 9.4 %convolution_convert_fusion.1 = bf16[1024,2048]{1,0:T(8,128)(2,1)} fusion(bf16[1024,1024]{1,0:T(8,128)(2,1)} %all-gather.9.cloned.1.call-done, bf16[2048,1024]{1,0:T(8,128)(2,1)} %param.7), kind=kOutput, calls=%fused_computation.4 | convolution fusion | flops 4297064448 | bytes 10485760 | tf_op jit(solution)/shard_map/dot_general | solution.py:45
  76.0 0.0 reduce-scatter.11.cloned.1.call-update
  76.1 0.0 reduce-scatter.7.cloned.1.call-start
  76.1 46.7 %all-gather.5.cloned.1.call-done = bf16[1024,1024]{1,0:T(8,128)(2,1)} async-done(((bf16[128,1024]{1,0:T(8,128)(2,1)}), bf16[1024,1024]{1,0:T(8,128)(2,1)}) %all-gather.5.cloned.1.call-update) | async-done | bytes 2097168 | tf_op jit(solution)/shard_map/all_gather | solution.py:17
  122.8 9.3 %convolution_convert_fusion.2 = bf16[1024,2048]{1,0:T(8,128)(2,1)} fusion(bf16[1024,1024]{1,0:T(8,128)(2,1)} %all-gather.5.cloned.1.call-done, bf16[1024,2048]{1,0:T(8,128)(2,1)} %param.6), kind=kOutput, calls=%fused_computation.5 | convolution fusion | flops 4297064448 | bytes 10485760 | tf_op jit(solution)/shard_map/dot_general | solution.py:21
  132.1 0.0 copy-start.1
  132.1 0.0 reduce-scatter.7.cloned.1.call-update
  132.2 0.0 all-gather.7.cloned.1.call-start
  132.2 31.5 %reduce-scatter.11.cloned.1.call-done = bf16[128,2048]{1,0:T(8,128)(2,1)} async-done(((bf16[1024,2048]{1,0:T(8,128)(2,1)}), bf16[128,2048]{1,0:T(8,128)(2,1)}) %reduce-scatter.11.cloned.1.call-update) | async-done | bytes 524304 | tf_op jit(solution)/shard_map/reduce_scatter | solution.py:44
  163.7 40.1 %reduce-scatter.7.cloned.1.call-done = bf16[128,2048]{1,0:T(8,128)(2,1)} async-done(((bf16[1024,2048]{1,0:T(8,128)(2,1)}), bf16[128,2048]{1,0:T(8,128)(2,1)}) %reduce-scatter.7.cloned.1.call-update) | async-done | bytes 524304 | tf_op jit(solution)/shard_map/reduce_scatter | solution.py:20
  203.7 2.7 fusion.8
  206.4 0.0 all-gather.7.cloned.1.call-update
  206.5 0.0 all-gather.11.cloned.1.call-start
  206.5 0.5 all-gather.11.cloned.1.call-update
  207.0 0.0 reduce-scatter.17.cloned.1.call-start
  207.1 30.6 %all-gather.7.cloned.1.call-done = bf16[1024,2048]{1,0:T(8,128)(2,1)} async-done(((bf16[128,2048]{1,0:T(8,128)(2,1)}), bf16[1024,2048]{1,0:T(8,128)(2,1)}) %all-gather.7.cloned.1.call-update) | async-done | bytes 4194320 | tf_op jit(solution)/shard_map/all_gather | solution.py:27
  237.6 0.0 copy-done.1
  237.6 8.3 %convolution_convert_fusion = bf16[2048,1024]{0,1:T(8,128)(2,1)} fusion(bf16[1024,2048]{1,0:T(8,128)(2,1)} %all-gather.7.cloned.1.call-done, bf16[1024,1024]{1,0:T(8,128)(2,1)S(1)} %copy-done.1), kind=kOutput, calls=%fused_computation.3 | convolution fusion | flops 4297064448 | bytes 10485760 | tf_op jit(solution)/shard_map/dot_general | solution.py:35
  246.0 0.0 copy-start
  246.0 0.0 reduce-scatter.17.cloned.1.call-update
  246.0 0.2 reduce-scatter.15.cloned.1.call-start
  246.2 25.7 %all-gather.11.cloned.1.call-done = bf16[1024,2048]{1,0:T(8,128)(2,1)} async-done(((bf16[128,2048]{1,0:T(8,128)(2,1)}), bf16[1024,2048]{1,0:T(8,128)(2,1)}) %all-gather.11.cloned.1.call-update) | async-done | bytes 4194320 | tf_op jit(solution)/shard_map/all_gather | solution.py:52
  272.0 0.0 copy-done
  272.0 8.3 %convert_bitcast_fusion = bf16[1024,2048]{0,1:T(8,128)(2,1)} fusion(bf16[1024,2048]{1,0:T(8,128)(2,1)} %all-gather.11.cloned.1.call-done, bf16[1024,1024]{1,0:T(8,128)(2,1)S(1)} %copy-done), kind=kOutput, calls=%fused_computation.2 | convolution fusion | flops 4297064448 | bytes 10485760 | tf_op jit(solution)/shard_map/dot_general | solution.py:61
  280.3 0.0 reduce-scatter.15.cloned.1.call-update
  280.3 0.0 reduce-scatter.9.cloned.1.call-start
  280.3 9.5 %convolution_convert_fusion.4 = bf16[1024,1024]{1,0:T(8,128)(2,1)} fusion(bf16[1024,2048]{1,0:T(8,128)(2,1)} %all-gather.7.cloned.1.call-done, bf16[2048,1024]{1,0:T(8,128)(2,1)} %param.7), kind=kOutput, calls=%fused_computation.12 | convolution fusion | flops 4296015872 | bytes 10485760 | tf_op jit(solution)/shard_map/dot_general | solution.py:29
  289.8 0.0 reduce-scatter.9.cloned.1.call-update
  289.9 0.0 reduce-scatter.13.cloned.1.call-start
  289.9 9.6 %convolution_convert_fusion.3 = bf16[1024,1024]{1,0:T(8,128)(2,1)} fusion(bf16[1024,2048]{1,0:T(8,128)(2,1)} %all-gather.11.cloned.1.call-done, bf16[1024,2048]{1,0:T(8,128)(2,1)} %param.6), kind=kOutput, calls=%fused_computation.11 | convolution fusion | flops 4296015872 | bytes 10485760 | tf_op jit(solution)/shard_map/dot_general | solution.py:54
  299.5 0.0 reduce-scatter.13.cloned.1.call-update
  299.5 30.9 %reduce-scatter.17.cloned.1.call-done = bf16[1024,1024]{0,1:T(8,128)(2,1)} async-done(((bf16[2048,1024]{0,1:T(8,128)(2,1)}), bf16[1024,1024]{0,1:T(8,128)(2,1)}) %reduce-scatter.17.cloned.1.call-update) | async-done | bytes 2097168 | tf_op jit(solution)/shard_map/reduce_scatter | solution.py:39
  330.4 4.1 convert_multiply_fusion
  334.5 5.3 copy.10
  339.9 51.4 %reduce-scatter.15.cloned.1.call-done = bf16[1024,1024]{0,1:T(8,128)(2,1)} async-done(((bf16[1024,2048]{0,1:T(8,128)(2,1)}), bf16[1024,1024]{0,1:T(8,128)(2,1)}) %reduce-scatter.15.cloned.1.call-update) | async-done | bytes 2097168 | tf_op jit(solution)/shard_map/reduce_scatter | solution.py:65
  391.3 4.1 convert_multiply_fusion.1
  395.5 5.3 copy.9
  400.8 71.5 %reduce-scatter.9.cloned.1.call-done = bf16[128,1024]{1,0:T(8,128)(2,1)} async-done(((bf16[1024,1024]{1,0:T(8,128)(2,1)}), bf16[128,1024]{1,0:T(8,128)(2,1)}) %reduce-scatter.9.cloned.1.call-update) | async-done | bytes 262160 | tf_op jit(solution)/shard_map/reduce_scatter | solution.py:28
  472.3 78.7 %reduce-scatter.13.cloned.1.call-done = bf16[128,1024]{1,0:T(8,128)(2,1)} async-done(((bf16[1024,1024]{1,0:T(8,128)(2,1)}), bf16[128,1024]{1,0:T(8,128)(2,1)}) %reduce-scatter.13.cloned.1.call-update) | async-done | bytes 262160 | tf_op jit(solution)/shard_map/reduce_scatter | solution.py:53
Async XLA Ops:
  7.2 59.5 %all-gather.9.cloned.1.call-start = ((), (), s32[]{:S(2)}) async-start(), calls=%async_computation.10 | async-start | bytes 2359296 | tf_op jit(solution)/shard_map/all_gather | solution.py:34
  7.9 114.9 %all-gather.5.cloned.1.call-start = ((), (), s32[]{:S(2)}) async-start(), calls=%async_computation.6 | async-start | bytes 2359296 | tf_op jit(solution)/shard_map/all_gather | solution.py:17
  8.6 155.0 %reduce-scatter.11.cloned.1.call-start = ((), (), s32[]{:S(2)}) async-start(), calls=%async_computation.11 | async-start | bytes 4718592 | tf_op jit(solution)/shard_map/reduce_scatter | solution.py:44
  76.1 127.7 %reduce-scatter.7.cloned.1.call-start = ((), (), s32[]{:S(2)}) async-start(), calls=%async_computation.7 | async-start | bytes 4718592 | tf_op jit(solution)/shard_map/reduce_scatter | solution.py:20
  132.1 105.5 %copy-start.1 = (bf16[1024,1024]{1,0:T(8,128)(2,1)S(1)}, bf16[1024,1024]{1,0:T(8,128)(2,1)}, u32[]{:S(2)}) copy-start(bf16[1024,1024]{1,0:T(8,128)(2,1)} %all-gather.9.cloned.1.call-done) | copy-start | bytes 6291460
  132.2 105.5 %all-gather.7.cloned.1.call-start = ((), (), s32[]{:S(2)}) async-start(), calls=%async_computation.8 | async-start | bytes 4718592 | tf_op jit(solution)/shard_map/all_gather | solution.py:27
  206.5 65.5 %all-gather.11.cloned.1.call-start = ((), (), s32[]{:S(2)}) async-start(), calls=%async_computation.12 | async-start | bytes 4718592 | tf_op jit(solution)/shard_map/all_gather | solution.py:52
  207.0 123.4 %reduce-scatter.17.cloned.1.call-start = ((), (), s32[]{:S(2)}) async-start(), calls=%async_computation.15 | async-start | bytes 6291456 | tf_op jit(solution)/shard_map/reduce_scatter | solution.py:39
  246.0 26.0 %copy-start = (bf16[1024,1024]{1,0:T(8,128)(2,1)S(1)}, bf16[1024,1024]{1,0:T(8,128)(2,1)}, u32[]{:S(2)}) copy-start(bf16[1024,1024]{1,0:T(8,128)(2,1)} %all-gather.5.cloned.1.call-done) | copy-start | bytes 6291460
  246.0 145.3 %reduce-scatter.15.cloned.1.call-start = ((), (), s32[]{:S(2)}) async-start(), calls=%async_computation.14 | async-start | bytes 6291456 | tf_op jit(solution)/shard_map/reduce_scatter | solution.py:65
  280.3 192.0 %reduce-scatter.9.cloned.1.call-start = ((), (), s32[]{:S(2)}) async-start(), calls=%async_computation.9 | async-start | bytes 2359296 | tf_op jit(solution)/shard_map/reduce_scatter | solution.py:28
  289.9 261.2 %reduce-scatter.13.cloned.1.call-start = ((), (), s32[]{:S(2)}) async-start(), calls=%async_computation.13 | async-start | bytes 2359296 | tf_op jit(solution)/shard_map/reduce_scatter | solution.py:53
Sparse Core Ops, SparseCore 0:
  10.3 56.2 all-gather.8
  69.0 53.7 all-gather.4
  125.8 37.8 reduce-scatter.10
  166.5 37.1 reduce-scatter.6
  206.6 31.0 all-gather.6
  239.8 32.1 all-gather.10
  274.9 55.4 reduce-scatter.16
  333.5 57.7 reduce-scatter.14
  395.7 76.5 reduce-scatter.8
  476.9 74.0 reduce-scatter.12
where the time goes:
time: 559 us; the launch traced here: 558 us
  waiting for transfers between devices  467 us (84%)
  matrix products  54.4 us (10%)
  between operations  14.2 us (3%)
  other arithmetic  11 us (2%)
  local copies, waits for them, and re-layouts  10.7 us (2%)
    reduce_scatter x1, waiting for transfers between devices, shards(): lax.psum_scatter(lax.dot_general(dpre, weight_in, (((1,), (1,)), ((), ())...  78.7 us
    reduce_scatter x1, waiting for transfers between devices, shards(): lax.psum_scatter(jnp.dot(act, weight_out, preferred_element_type=jnp.floa...  71.5 us
    all_gather x1, waiting for transfers between devices, shards(): grad_panel = lax.all_gather(out_grad, 'col', axis=0, tiled=True)  58 us
    reduce_scatter x1, waiting for transfers between devices, shards(): lax.psum_scatter(in_local.astype(jnp.bfloat16), 'dp', scatter_dimension=1...  51.4 us
    all_gather x1, waiting for transfers between devices, shards(): panel = lax.all_gather(tokens, 'col', axis=0, tiled=True)  46.7 us
    reduce_scatter x1, waiting for transfers between devices, shards(): lax.psum_scatter(jnp.dot(panel, weight_in, preferred_element_type=jnp.flo...  40.1 us
    reduce_scatter x1, waiting for transfers between devices, shards(): lax.psum_scatter(lax.dot_general(grad_panel, weight_out, (((1,), (1,)), (...  31.5 us
    reduce_scatter x1, waiting for transfers between devices, shards(): lax.psum_scatter(out_local.astype(jnp.bfloat16), 'dp', scatter_dimension=...  30.9 us
  transfers between devices with their start and end apart: 10, of which 10 were waited for; matrix products, arithmetic and copies ran while one was open for 13% of the time, Pallas kernels for 0%

commit v1 on v0

v1 whole, which is shorter than its diff:
```python
import functools
import math

import jax
import jax.numpy as jnp
from jax import lax
from jax.experimental import pallas as pl
from jax.experimental.pallas import tpu as pltpu
from jax.sharding import PartitionSpec as P

AXES = ("row", "col", "dp")
RING = 4
BF = jnp.bfloat16
F32 = jnp.float32
NN = (((1,), (0,)), ((), ()))
NT = (((1,), (1,)), ((), ()))
TN = (((0,), (0,)), ((), ()))


def gelu_parts(pre):
    cdf = 0.5 * (1.0 + jax.scipy.special.erf(pre * (1.0 / math.sqrt(2.0))))
    activated = pre * cdf
    slope = cdf + pre * jnp.exp(-0.5 * pre * pre) * (1.0 / math.sqrt(2.0 * math.pi))
    return (activated, slope)


def flat(z, c, x, y):
    return ((z % RING * 2 + c) * RING + x % RING) * RING + y % RING


def receive(array, source):
    pairs = []
    for z in range(RING):
        for c in range(2):
            for x in range(RING):
                for y in range(RING):
                    pairs.append((flat(*source(z, c, x, y)), flat(z, c, x, y)))
    return lax.ppermute(array, AXES, pairs)


def turn(c, k):
    return k if c == 0 else -k


def along(half, first, step, z, c, x, y):
    if (half == 0) == first:
        return (z, c, x + step, y)
    return (z, c, x, y + step)


def own(c, keep):
    return c if keep else 1 - c


def first_from(array, keep, k):
    def source(z, c, x, y):
        half = own(c, keep)
        return along(half, True, (z + turn(half, k)) % RING, z, c, x, y)

    return receive(array, source)


def first_to(array, keep, k):
    def source(z, c, x, y):
        half = own(c, keep)
        return along(half, True, -((z + turn(half, k)) % RING), z, c, x, y)

    return receive(array, source)


def second_from(array, keep, step):
    return receive(array, lambda z, c, x, y: along(own(c, keep), False, step, z, c, x, y))


def z_from(array, k):
    return receive(array, lambda z, c, x, y: (z + turn(c, k), c, x, y))


def swap(array):
    return receive(array, lambda z, c, x, y: (z, 1 - c, x, y))


def pair_kernel(added, *refs):
    if added:
        a_ref, left_ref, right_ref, more_ref, out_ref = refs
    else:
        a_ref, left_ref, right_ref, out_ref = refs

    def finish(total):
        if added:
            total = total + more_ref[...].astype(F32)
        out_ref[...] = total.astype(BF)

    @pl.when(pl.program_id(0) == 0)
    def _():
        finish(lax.dot_general(a_ref[...], left_ref[...], NN, preferred_element_type=F32))

    @pl.when(pl.program_id(0) == 1)
    def _():
        finish(lax.dot_general(a_ref[...], right_ref[...], NT, preferred_element_type=F32))


def pair_dot(a, left, right, more=None, tile=512):
    rows, depth = a.shape[0], left.shape[0]
    wide = left.shape[1]
    tiles = wide // tile
    in_specs = [
        pl.BlockSpec((rows, depth), lambda h, n: (0, h)),
        pl.BlockSpec((depth, tile), lambda h, n: (0, n * (1 - h) + (tiles - 1) * h)),
        pl.BlockSpec((tile, depth), lambda h, n: (n * h, 0)),
    ]
    args = [a, left, right]
    if more is not None:
        in_specs.append(pl.BlockSpec((rows, tile), lambda h, n: (0, h * tiles + n)))
        args.append(more)
    return pl.pallas_call(
        functools.partial(pair_kernel, more is not None),
        grid=(2, tiles),
        in_specs=in_specs,
        out_specs=pl.BlockSpec((rows, tile), lambda h, n: (0, h * tiles + n)),
        out_shape=jax.ShapeDtypeStruct((rows, 2 * wide), BF),
        compiler_params=pltpu.CompilerParams(vmem_limit_bytes=24 * 2**20),
        cost_estimate=pl.CostEstimate(
            flops=4 * rows * depth * wide,
            bytes_accessed=4 * depth * wide + 8 * rows * wide,
            transcendentals=0,
        ),
    )(*args)


def grad_kernel(count, factor, *refs):
    out_ref = refs[-1]
    total = None
    for i in range(count):
        term = lax.dot_general(
            refs[i][...], refs[count + i][...], TN, preferred_element_type=F32
        )
        total = term if total is None else total + term
    out_ref[...] = total * factor


def grad_dot(lefts, left_part, rights, right_part, factor, tile=256):
    count = len(lefts)
    rows = lefts[0].shape[0]
    wide = lefts[0].shape[1] // 2
    tiles = wide // tile
    return pl.pallas_call(
        functools.partial(grad_kernel, count, factor),
        grid=(tiles,),
        in_specs=[pl.BlockSpec((rows, wide), lambda n: (0, left_part))] * count
        + [pl.BlockSpec((rows, tile), lambda n: (0, right_part * tiles + n))] * count,
        out_specs=pl.BlockSpec((wide, tile), lambda n: (0, n)),
        out_shape=jax.ShapeDtypeStruct((wide, wide), F32),
        compiler_params=pltpu.CompilerParams(vmem_limit_bytes=40 * 2**20),
        cost_estimate=pl.CostEstimate(
            flops=2 * count * rows * wide * wide,
            bytes_accessed=4 * count * rows * wide + 4 * wide * wide,
            transcendentals=0,
        ),
    )(*lefts, *rights)


def total_of(parts):
    total = parts[0].astype(F32)
    for part in parts[1:]:
        total = total + part.astype(F32)
    return total


def shards(tokens, out_grad, weight_in, weight_out):
    core = lax.axis_index("row") % 2
    dp = lax.axis_index("dp")
    block, width = tokens.shape
    half = block // 2
    inner = weight_in.shape[1] // 2
    factor = 1.0 / math.sqrt(block * 16)

    both = jnp.concatenate([tokens, out_grad], axis=1)
    start = {
        True: lax.dynamic_slice_in_dim(both, core * half, half, 0),
        False: lax.dynamic_slice_in_dim(both, (1 - core) * half, half, 0),
    }
    w_in = lax.dynamic_slice_in_dim(weight_in, dp * inner, inner, 1)
    w_out = lax.dynamic_slice_in_dim(weight_out, dp * inner, inner, 0)

    panel = {}
    for keep in (True, False):
        panel[keep, 0] = jnp.concatenate(
            [first_from(start[keep], keep, k) for k in range(RING)], axis=0
        )
    for step in (1, 3, 2):
        for keep in (True, False):
            panel[keep, step] = second_from(panel[keep, 0], keep, step)

    hidden = {}
    partial = {}
    for step in (0, 1, 3, 2):
        sent = pair_dot(panel[False, step], w_in, w_out)
        summed = pair_dot(panel[True, step], w_in, w_out, swap(sent))
        slots = [summed[k * half:(k + 1) * half] for k in range(RING)]
        value = total_of([slots[0]] + [z_from(slots[k], -k) for k in range(1, RING)])
        pre, back = value[:, :width], value[:, width:]
        activated, slope = gelu_parts(pre)
        mine = jnp.concatenate([activated.astype(BF), (back * slope).astype(BF)], axis=1)
        hidden[True, step] = jnp.concatenate(
            [mine] + [z_from(mine, k) for k in range(1, RING)], axis=0
        )
        hidden[False, step] = swap(hidden[True, step])
        for keep in (True, False):
            partial[keep, step] = pair_dot(hidden[keep, step], w_out, w_in)

    done = {}
    for keep in (True, False):
        arrived = [partial[keep, 0]] + [
            second_from(partial[keep, step], keep, -step) for step in (1, 3, 2)
        ]
        near = total_of(arrived).astype(BF)
        done[keep] = total_of(
            [first_to(near[k * half:(k + 1) * half], keep, k) for k in range(RING)]
        ).astype(BF)

    order = [(keep, step) for step in (0, 1, 3, 2) for keep in (True, False)]
    panels = [panel[o] for o in order]
    hiddens = [hidden[o] for o in order]
    grad_in = grad_dot(panels, 0, hiddens, 1, factor)
    grad_out = grad_dot(hiddens, 0, panels, 1, factor)

    low = jnp.where(core == 0, done[True], done[False])
    high = jnp.where(core == 0, done[False], done[True])
    result = jnp.concatenate([low, high], axis=0)
    return (result[:, :width], result[:, width:], grad_in, grad_out)


def solution(mesh):
    placed = (P(("col", "dp"), "row"), P(("col", "dp"), "row"), P("row", "col"), P("col", "row"))
    return jax.shard_map(
        shards,
        mesh=mesh,
        in_specs=placed,
        out_specs=(
            P(("col", "dp"), "row"),
            P(("col", "dp"), "row"),
            P("row", ("col", "dp")),
            P(("col", "dp"), "row"),
        ),
        check_vma=False,
    )
```

time: 559 us -> 276 us (0.49)
  waiting for transfers between devices: 467 us -> 73.5 us
  starting transfers between devices: 0.58 us -> 117 us
  Pallas kernels: 0 us -> 61.5 us
  matrix products: 54.4 us -> 0 us
  between operations: 14.2 us -> 1.7 us
    reduce_scatter x6 -> x0, waiting for transfers between devices: 304 us -> none  [the longest x1 78.7 us: shards(): lax.psum_scatter(lax.dot_general(dpre, weight_in, (((1,), (1,)), ((), ())...]
    all_gather x4 -> x0, waiting for transfers between devices: 161 us -> none  [the longest x1 58 us: shards(): grad_panel = lax.all_gather(out_grad, 'col', axis=0, tiled=True)]
    ppermute x0 -> x60, starting transfers between devices: none -> 117 us  [receive(): return lax.ppermute(array, AXES, pairs)]
    ppermute x0 -> x60, waiting for transfers between devices: none -> 73.5 us  [receive(): return lax.ppermute(array, AXES, pairs)]
    pallas_call x0 -> x18, Pallas kernels: none -> 61.5 us  [the longest x16 44.9 us: pair_dot(): pl.pallas_call(functools.partial(pair_kernel, more is not None), grid=(2,...]
    dot_general x6 -> x0, matrix products: 54.4 us -> none  [the longest x1 9.6 us: shards(): lax.dot_general(dpre, weight_in, (((1,), (1,)), ((), ())), preferred_elem...]
    mul x2 -> x0, other arithmetic: 8.29 us -> none  [the longest x1 4.14 us: shards(): lax.psum_scatter(out_local.astype(jnp.bfloat16), 'dp', scatter_dimension=...]
  transfers between devices with their start and end apart: 10 -> 60, of which waited for: 10 -> 15; matrix products, arithmetic and copies ran while one was open for 13% -> 5% of each run, Pallas kernels for 0% -> 23%
where the time goes in v1:
time: 276 us; the launch traced here: 273 us
  starting transfers between devices  117 us (42%)
  waiting for transfers between devices  73.5 us (27%)
  Pallas kernels  61.5 us (22%)
  local copies, waits for them, and re-layouts  11 us (4%)
  other arithmetic  8.2 us (3%)
    ppermute x60, starting transfers between devices, receive(): return lax.ppermute(array, AXES, pairs)  117 us
    ppermute x60, waiting for transfers between devices, receive(): return lax.ppermute(array, AXES, pairs)  73.5 us
    pallas_call x16, Pallas kernels, pair_dot(): pl.pallas_call(functools.partial(pair_kernel, more is not None), grid=(2,...  44.9 us
    pallas_call x2, Pallas kernels, grad_dot(): pl.pallas_call(functools.partial(grad_kernel, count, factor), grid=(tiles...  16.6 us
    unnamed x57, local copies, waits for them, and re-layouts  6.83 us
  transfers between devices with their start and end apart: 60, of which 15 were waited for; matrix products, arithmetic and copies ran while one was open for 5% of the time, Pallas kernels for 23%

profile of v1, /device:TPU:8, one launch (start us, length us, event | category | flops | bytes accessed | tf_op | source)
XLA Modules:
  0.0 273.1 jit_solution(3655149270170066263)
XLA Ops:
  4.0 3.5 %collective-permute-start.5 = (bf16[64,2048]{1,0:T(8,128)(2,1)S(1)}, bf16[64,2048]{1,0:T(8,128)(2,1)}, u32[]{:S(2)}, u32[]{:S(2)}) collective-permute-start(bf16[64,2048]{1,0:T(8,128)(2,1)S(1)} %get-tuple-element.37), channel_id=1, source_target_pairs={{3,0},{0,1},{1,2},{2,3},{7,4},{4,5},{5,6},{6,7},{11,8},{8,9},{9,10... | collective-permute-start | bytes 786440 | tf_op jit(solution)/shard_map/ppermute | solution.py:38
  7.5 2.8 %collective-permute-start.6 = (bf16[64,2048]{1,0:T(8,128)(2,1)S(1)}, bf16[64,2048]{1,0:T(8,128)(2,1)S(1)}, u32[]{:S(2)}, u32[]{:S(2)}) collective-permute-start(bf16[64,2048]{1,0:T(8,128)(2,1)S(1)} %get-tuple-element.37), channel_id=1, source_target_pairs={{2,0},{3,1},{0,2},{1,3},{6,4},{7,5},{4,6},{5,7},{10,8},{11,9},{8,1... | collective-permute-start | bytes 786440 | tf_op jit(solution)/shard_map/ppermute | solution.py:38
  10.3 4.4 %collective-permute-start.7 = (bf16[64,2048]{1,0:T(8,128)(2,1)S(1)}, bf16[64,2048]{1,0:T(8,128)(2,1)S(1)}, u32[]{:S(2)}, u32[]{:S(2)}) collective-permute-start(bf16[64,2048]{1,0:T(8,128)(2,1)S(1)} %get-tuple-element.37), channel_id=1, source_target_pairs={{1,0},{2,1},{3,2},{0,3},{5,4},{6,5},{7,6},{4,7},{9,8},{10,9},{11,1... | collective-permute-start | bytes 786440 | tf_op jit(solution)/shard_map/ppermute | solution.py:38
  15.4 2.7 constant_dynamic-slice_fusion.1
  20.3 2.3 shard_map.75
  22.7 4.7 %collective-permute-start.1 = (bf16[64,2048]{1,0:T(8,128)(2,1)S(1)}, bf16[64,2048]{1,0:T(8,128)(2,1)S(1)}, u32[]{:S(2)}, u32[]{:S(2)}) collective-permute-start(bf16[64,2048]{1,0:T(8,128)(2,1)S(1)} %get-tuple-element.38), channel_id=1, source_target_pairs={{4,0},{5,1},{6,2},{7,3},{8,4},{9,5},{10,6},{11,7},{12,8},{13,9},{1... | collective-permute-start | bytes 786440 | tf_op jit(solution)/shard_map/ppermute | solution.py:38
  27.4 2.7 collective-permute-start.2
  30.1 2.8 %collective-permute-start.3 = (bf16[64,2048]{1,0:T(8,128)(2,1)S(1)}, bf16[64,2048]{1,0:T(8,128)(2,1)S(1)}, u32[]{:S(2)}, u32[]{:S(2)}) collective-permute-start(bf16[64,2048]{1,0:T(8,128)(2,1)S(1)} %get-tuple-element.38), channel_id=1, source_target_pairs={{12,0},{13,1},{14,2},{15,3},{0,4},{1,5},{2,6},{3,7},{4,8},{5,9},{6... | collective-permute-start | bytes 786440 | tf_op jit(solution)/shard_map/ppermute | solution.py:38
  37.2 2.7 %collective-permute-done.3 = bf16[64,2048]{1,0:T(8,128)(2,1)S(1)} collective-permute-done((bf16[64,2048]{1,0:T(8,128)(2,1)S(1)}, bf16[64,2048]{1,0:T(8,128)(2,1)S(1)}, u32[]{:S(2)}, u32[]{:S(2)}) %collective-permute-start.3) | collective-permute-done | bytes 262176 | tf_op jit(solution)/shard_map/ppermute | solution.py:38
  40.0 2.4 shard_map.76
  42.5 3.0 %collective-permute-start.11 = (bf16[64,2048]{1,0:T(8,128)(2,1)S(1)}, bf16[64,2048]{1,0:T(8,128)(2,1)S(1)}, u32[]{:S(2)}, u32[]{:S(2)}) collective-permute-start(bf16[64,2048]{1,0:T(8,128)(2,1)S(1)} %get-tuple-element.16), channel_id=1, source_target_pairs={{32,0},{33,1},{34,2},{35,3},{36,4},{37,5},{38,6},{39,7},{40,8},{41... | collective-permute-start | bytes 786440 | tf_op jit(solution)/shard_map/ppermute | solution.py:38
  45.6 9.6 %collective-permute-start.10 = (bf16[64,2048]{1,0:T(8,128)(2,1)S(1)}, bf16[64,2048]{1,0:T(8,128)(2,1)S(1)}, u32[]{:S(2)}, u32[]{:S(2)}) collective-permute-start(bf16[64,2048]{1,0:T(8,128)(2,1)S(1)} %get-tuple-element.17), channel_id=1, source_target_pairs={{64,0},{65,1},{66,2},{67,3},{68,4},{69,5},{70,6},{71,7},{72,8},{73... | collective-permute-start | bytes 786440 | tf_op jit(solution)/shard_map/ppermute | solution.py:38
  56.5 2.4 collective-permute-start.35
  59.0 2.3 shard_map.84
  61.4 3.7 %collective-permute-start.16 = (bf16[256,2048]{1,0:T(8,128)(2,1)S(1)}, bf16[256,2048]{1,0:T(8,128)(2,1)S(1)}, u32[]{:S(2)}, u32[]{:S(2)}) collective-permute-start(bf16[256,2048]{1,0:T(8,128)(2,1)S(1)} %constant_dynamic-update-slice_fusion.6.refs_0_.refs_1_.refs_9_), channel_id=1, source_target_pairs={{4,0},{5,1},{6,2},{7,3},{8,4},{9,5},{10,6},{11,7},{12,8},{13,9},{1... | collective-permute-start | bytes 3145736 | tf_op jit(solution)/shard_map/ppermute | solution.py:38
  66.5 2.6 collective-permute-start.14
  69.1 11.4 %collective-permute-done.26.refs_0_.refs_5_.refs_13_ = bf16[256,2048]{1,0:T(8,128)(2,1)S(1)} collective-permute-done((bf16[256,2048]{1,0:T(8,128)(2,1)S(1)}, bf16[256,2048]{1,0:T(8,128)(2,1)S(1)}, u32[]{:S(2)}, u32[]{:S(2)}) %collective-permute-start.26) | collective-permute-done | bytes 1048608 | tf_op jit(solution)/shard_map/ppermute | solution.py:38
  80.4 2.6 collective-permute-start.13
  83.1 3.2 %collective-permute-start.25 = (bf16[256,2048]{1,0:T(8,128)(2,1)S(1)}, bf16[256,2048]{1,0:T(8,128)(2,1)S(1)}, u32[]{:S(2)}, u32[]{:S(2)}) collective-permute-start(bf16[256,2048]{1,0:T(8,128)(2,1)S(1)} %constant_dynamic-update-slice_fusion.2.refs_0_.refs_8_), channel_id=1, source_target_pairs={{3,0},{0,1},{1,2},{2,3},{7,4},{4,5},{5,6},{6,7},{11,8},{8,9},{9,10... | collective-permute-start | bytes 3145736 | tf_op jit(solution)/shard_map/ppermute | solution.py:38
  93.0 6.7 %collective-permute-start.15 = (bf16[256,2048]{1,0:T(8,128)(2,1)S(1)}, bf16[256,2048]{1,0:T(8,128)(2,1)S(1)}, u32[]{:S(2)}, u32[]{:S(2)}) collective-permute-start(bf16[256,2048]{1,0:T(8,128)(2,1)S(1)} %constant_dynamic-update-slice_fusion.2.refs_0_.refs_8_), channel_id=1, source_target_pairs={{1,0},{2,1},{3,2},{0,3},{5,4},{6,5},{7,6},{4,7},{9,8},{10,9},{11,1... | collective-permute-start | bytes 3145736 | tf_op jit(solution)/shard_map/ppermute | solution.py:38
  100.4 2.4 shard_map.85
  103.9 2.4 shard_map.82
  106.4 5.6 %collective-permute-done.15.refs_0_.refs_2_.refs_10_ = bf16[256,2048]{1,0:T(8,128)(2,1)S(1)} collective-permute-done((bf16[256,2048]{1,0:T(8,128)(2,1)S(1)}, bf16[256,2048]{1,0:T(8,128)(2,1)S(1)}, u32[]{:S(2)}, u32[]{:S(2)}) %collective-permute-start.15) | collective-permute-done | bytes 1048608 | tf_op jit(solution)/shard_map/ppermute | solution.py:38
  112.0 3.2 %collective-permute-start.30 = (bf16[64,2048]{1,0:T(8,128)(2,1)S(1)}, bf16[64,2048]{1,0:T(8,128)(2,1)S(1)}, u32[]{:S(2)}, u32[]{:S(2)}) collective-permute-start(bf16[64,2048]{1,0:T(8,128)(2,1)S(1)} %get-tuple-element.22), channel_id=1, source_target_pairs={{32,0},{33,1},{34,2},{35,3},{36,4},{37,5},{38,6},{39,7},{40,8},{41... | collective-permute-start | bytes 786440 | tf_op jit(solution)/shard_map/ppermute | solution.py:38
  115.2 2.4 shard_map.79
  118.7 8.2 %collective-permute-done.38 = bf16[64,2048]{1,0:T(8,128)(2,1)S(1)} collective-permute-done((bf16[64,2048]{1,0:T(8,128)(2,1)S(1)}, bf16[64,2048]{1,0:T(8,128)(2,1)S(1)}, u32[]{:S(2)}, u32[]{:S(2)}) %collective-permute-start.38) | collective-permute-done | bytes 262176 | tf_op jit(solution)/shard_map/ppermute | solution.py:38
  128.5 3.7 %collective-permute-start.18 = (bf16[64,2048]{1,0:T(8,128)(2,1)S(1)}, bf16[64,2048]{1,0:T(8,128)(2,1)S(1)}, u32[]{:S(2)}, u32[]{:S(2)}) collective-permute-start(bf16[64,2048]{1,0:T(8,128)(2,1)S(1)} %get-tuple-element.18), channel_id=1, source_target_pairs={{96,0},{97,1},{98,2},{99,3},{100,4},{101,5},{102,6},{103,7},{104,8... | collective-permute-start | bytes 786440 | tf_op jit(solution)/shard_map/ppermute | solution.py:38
  132.2 5.7 %collective-permute-done.28 = bf16[64,2048]{1,0:T(8,128)(2,1)S(1)} collective-permute-done((bf16[64,2048]{1,0:T(8,128)(2,1)S(1)}, bf16[64,2048]{1,0:T(8,128)(2,1)S(1)}, u32[]{:S(2)}, u32[]{:S(2)}) %collective-permute-start.28) | collective-permute-done | bytes 262176 | tf_op jit(solution)/shard_map/ppermute | solution.py:38
  139.3 5.1 %collective-permute-start.41 = (bf16[64,2048]{1,0:T(8,128)(2,1)S(1)}, bf16[64,2048]{1,0:T(8,128)(2,1)S(1)}, u32[]{:S(2)}, u32[]{:S(2)}) collective-permute-start(bf16[64,2048]{1,0:T(8,128)(2,1)S(1)} %pad_maximum_fusion.8), channel_id=1, source_target_pairs={{32,0},{33,1},{34,2},{35,3},{36,4},{37,5},{38,6},{39,7},{40,8},{41... | collective-permute-start | bytes 786440 | tf_op jit(solution)/shard_map/ppermute | solution.py:38
  144.5 8.1 %collective-permute-done.43 = bf16[64,2048]{1,0:T(8,128)(2,1)S(1)} collective-permute-done((bf16[64,2048]{1,0:T(8,128)(2,1)S(1)}, bf16[64,2048]{1,0:T(8,128)(2,1)S(1)}, u32[]{:S(2)}, u32[]{:S(2)}) %collective-permute-start.43) | collective-permute-done | bytes 262176 | tf_op jit(solution)/shard_map/ppermute | solution.py:38
  152.7 2.6 collective-permute-done.41
  155.6 10.5 %collective-permute-done.33 = bf16[64,2048]{1,0:T(8,128)(2,1)S(1)} collective-permute-done((bf16[64,2048]{1,0:T(8,128)(2,1)S(1)}, bf16[64,2048]{1,0:T(8,128)(2,1)S(1)}, u32[]{:S(2)}, u32[]{:S(2)}) %collective-permute-start.33) | collective-permute-done | bytes 262176 | tf_op jit(solution)/shard_map/ppermute | solution.py:38
  170.5 6.0 %collective-permute-done.23 = bf16[64,2048]{1,0:T(8,128)(2,1)S(1)} collective-permute-done((bf16[64,2048]{1,0:T(8,128)(2,1)S(1)}, bf16[64,2048]{1,0:T(8,128)(2,1)S(1)}, u32[]{:S(2)}, u32[]{:S(2)}) %collective-permute-start.23) | collective-permute-done | bytes 262176 | tf_op jit(solution)/shard_map/ppermute | solution.py:38
  178.6 3.1 %shard_map.86 = bf16[256,2048]{1,0:T(8,128)(2,1)} custom-call(bf16[256,2048]{1,0:T(8,128)(2,1)S(1)} %pad_maximum_fusion.3.refs_0_.refs_14_.refs_6_, bf16[1024,1024]{1,0:T(8,128)(2,1)S(1)} %get-tuple-element.39.refs_2_.refs_1_, bf16[1024,1024]{1,0:T(8,128)(2,1)S(1)} %get-tuple-element.40.refs_1_.refs_2_), custom_call_target="tpu_custom_call" | custom-call | flops 1073741824 | bytes 6291456 | tf_op jit(solution)/shard_map/pallas_call | solution.py:116
  181.7 4.3 %shard_map.83 = bf16[256,2048]{1,0:T(8,128)(2,1)} custom-call(bf16[256,2048]{1,0:T(8,128)(2,1)} %pad_maximum_fusion.2.refs_0_.refs_12_.refs_4_, bf16[1024,1024]{1,0:T(8,128)(2,1)S(1)} %get-tuple-element.39.refs_2_.refs_1_, bf16[1024,1024]{1,0:T(8,128)(2,1)S(1)} %get-tuple-element.40.refs_1_.refs_2_), custom_call_target="tpu_custom_call" | custom-call | flops 1073741824 | bytes 6291456 | tf_op jit(solution)/shard_map/pallas_call | solution.py:116
  186.0 3.6 %collective-permute-start.44 = (bf16[256,2048]{1,0:T(8,128)(2,1)}, bf16[256,2048]{1,0:T(8,128)(2,1)}, u32[]{:S(2)}, u32[]{:S(2)}) collective-permute-start(bf16[256,2048]{1,0:T(8,128)(2,1)} %shard_map.86), channel_id=1, source_target_pairs={{2,0},{3,1},{0,2},{1,3},{6,4},{7,5},{4,6},{5,7},{10,8},{11,9},{8,1... | collective-permute-start | bytes 3145736 | tf_op jit(solution)/shard_map/ppermute | solution.py:38
  189.6 4.4 %shard_map.80 = bf16[256,2048]{1,0:T(8,128)(2,1)} custom-call(bf16[256,2048]{1,0:T(8,128)(2,1)} %pad_maximum_fusion.1.refs_0_.refs_10_.refs_2_, bf16[1024,1024]{1,0:T(8,128)(2,1)S(1)} %get-tuple-element.39.refs_2_.refs_1_, bf16[1024,1024]{1,0:T(8,128)(2,1)S(1)} %get-tuple-element.40.refs_1_.refs_2_), custom_call_target="tpu_custom_call" | custom-call | flops 1073741824 | bytes 6291456 | tf_op jit(solution)/shard_map/pallas_call | solution.py:116
  201.9 2.3 shard_map.87
  208.7 3.6 %shard_map.89 = bf16[256,2048]{1,0:T(8,128)(2,1)S(1)} custom-call(bf16[256,2048]{1,0:T(8,128)(2,1)} %collective-permute-done.52.refs_0_.refs_13_.refs_5_, bf16[1024,1024]{1,0:T(8,128)(2,1)S(1)} %get-tuple-element.39.refs_2_.refs_1_, bf16[1024,1024]{1,0:T(8,128)(2,1)S(1)} %copy-done.1), custom_call_target="tpu_custom_call" | custom-call | flops 1073741824 | bytes 6291456 | tf_op jit(solution)/shard_map/pallas_call | solution.py:116
  214.3 3.7 %shard_map.88 = bf16[256,2048]{1,0:T(8,128)(2,1)S(1)} custom-call(bf16[256,2048]{1,0:T(8,128)(2,1)} %collective-permute-done.50.refs_0_.refs_11_.refs_3_, bf16[1024,1024]{1,0:T(8,128)(2,1)S(1)} %get-tuple-element.39.refs_2_.refs_1_, bf16[1024,1024]{1,0:T(8,128)(2,1)S(1)} %copy-done.1), custom_call_target="tpu_custom_call" | custom-call | flops 1073741824 | bytes 6291456 | tf_op jit(solution)/shard_map/pallas_call | solution.py:116
  219.0 7.7 %collective-permute-done.34 = bf16[256,2048]{1,0:T(8,128)(2,1)} collective-permute-done((bf16[256,2048]{1,0:T(8,128)(2,1)}, bf16[256,2048]{1,0:T(8,128)(2,1)}, u32[]{:S(2)}, u32[]{:S(2)}) %collective-permute-start.34) | collective-permute-done | bytes 1048608 | tf_op jit(solution)/shard_map/ppermute | solution.py:38
  226.7 2.8 %add_convert_fusion.1 = bf16[256,2048]{1,0:T(8,128)(2,1)S(1)} fusion(bf16[256,2048]{1,0:T(8,128)(2,1)} %collective-permute-done.44, bf16[256,2048]{1,0:T(8,128)(2,1)} %collective-permute-done.34, bf16[256,2048]{1,0:T(8,128)(2,1)} %collective-permute-done.24, bf16[256,2048]{1,0:T(8,128)(2,1)S(1)} %shard_map.77), kind=kLoop, calls=%fused_computation.1 | loop fusion | flops 4194304 | bytes 5242880 | tf_op jit(solution)/shard_map/convert_element_type | solution.py:217
  229.6 6.7 %collective-permute-start.48 = (bf16[64,2048]{1,0:T(8,128)(2,1)S(1)}, bf16[64,2048]{1,0:T(8,128)(2,1)S(1)}, u32[]{:S(2)}, u32[]{:S(2)}) collective-permute-start(bf16[64,2048]{1,0:T(8,128)(2,1)S(1)} %get-tuple-element.8), channel_id=1, source_target_pairs={{4,0},{5,1},{6,2},{7,3},{8,4},{9,5},{10,6},{11,7},{12,8},{13,9},{1... | collective-permute-start | bytes 786440 | tf_op jit(solution)/shard_map/ppermute | solution.py:38
  238.3 8.0 %shard_map.91 = f32[1024,1024]{1,0:T(8,128)} custom-call(bf16[256,2048]{1,0:T(8,128)(2,1)S(1)} %copy-done.5, bf16[256,2048]{1,0:T(8,128)(2,1)S(1)} %copy-done.7, bf16[256,2048]{1,0:T(8,128)(2,1)S(1)} %copy-done.13, bf16[256,2048]{1,0:T(8,128)(2,1)S(1)} %copy-done.19, bf16[256,2048]{1,0:T(8,128)(2,1)S(1)} %copy-done.11, bf16[256,2048]{1,0:T(8,128)(2,1)S(1)} %copy-done.17, ...), custom_call_target="tpu_custom_call" | custom-call | flops 4294967296 | bytes 12582912 | tf_op jit(solution)/shard_map/pallas_call | solution.py:147
  246.3 2.8 %collective-permute-start.46 = (bf16[64,2048]{1,0:T(8,128)(2,1)S(1)}, bf16[64,2048]{1,0:T(8,128)(2,1)S(1)}, u32[]{:S(2)}, u32[]{:S(2)}) collective-permute-start(bf16[64,2048]{1,0:T(8,128)(2,1)S(1)} %get-tuple-element.10), channel_id=1, source_target_pairs={{12,0},{13,1},{14,2},{15,3},{0,4},{1,5},{2,6},{3,7},{4,8},{5,9},{6... | collective-permute-start | bytes 786440 | tf_op jit(solution)/shard_map/ppermute | solution.py:38
  250.7 2.9 %collective-permute-start.59 = (bf16[64,2048]{1,0:T(8,128)(2,1)S(1)}, bf16[64,2048]{1,0:T(8,128)(2,1)S(1)}, u32[]{:S(2)}, u32[]{:S(2)}) collective-permute-start(bf16[64,2048]{1,0:T(8,128)(2,1)S(1)} %get-tuple-element.12), channel_id=1, source_target_pairs={{3,0},{0,1},{1,2},{2,3},{7,4},{4,5},{5,6},{6,7},{11,8},{8,9},{9,10... | collective-permute-start | bytes 786440 | tf_op jit(solution)/shard_map/ppermute | solution.py:38
  253.6 6.9 %collective-permute-start.58 = (bf16[64,2048]{1,0:T(8,128)(2,1)S(1)}, bf16[64,2048]{1,0:T(8,128)(2,1)S(1)}, u32[]{:S(2)}, u32[]{:S(2)}) collective-permute-start(bf16[64,2048]{1,0:T(8,128)(2,1)S(1)} %get-tuple-element.13), channel_id=1, source_target_pairs={{2,0},{3,1},{0,2},{1,3},{6,4},{7,5},{4,6},{5,7},{10,8},{11,9},{8,1... | collective-permute-start | bytes 786440 | tf_op jit(solution)/shard_map/ppermute | solution.py:38
  263.2 8.6 %shard_map.92 = f32[1024,1024]{1,0:T(8,128)} custom-call(bf16[256,2048]{1,0:T(8,128)(2,1)S(1)} %pad_maximum_fusion.refs_0_.refs_8_, bf16[256,2048]{1,0:T(8,128)(2,1)S(1)} %copy-done.21, bf16[256,2048]{1,0:T(8,128)(2,1)} %pad_maximum_fusion.1.refs_0_.refs_10_.refs_2_, bf16[256,2048]{1,0:T(8,128)(2,1)} %collective-permute-done.50.refs_0_.refs_11_.refs_3_, ...), custom_call_target="tpu_custom_call" | custom-call | flops 4294967296 | bytes 12582912 | tf_op jit(solution)/shard_map/pallas_call | solution.py:147
  (179 shorter events, 55.5 us)
Async XLA Ops:
  2.7 15.4 %collective-permute-start.4 = (bf16[64,2048]{1,0:T(8,128)(2,1)S(1)}, bf16[64,2048]{1,0:T(8,128)(2,1)}, u32[]{:S(2)}, u32[]{:S(2)}) collective-permute-start(bf16[64,2048]{1,0:T(8,128)(2,1)S(1)} %get-tuple-element.37), channel_id=1, source_target_pairs={{0,0},{1,1},{2,2},{3,3},{4,4},{5,5},{6,6},{7,7},{8,8},{9,9},{10,10... | collective-permute-start | bytes 786440 | tf_op jit(solution)/shard_map/ppermute | solution.py:38
  4.0 15.2 %collective-permute-start.5 = (bf16[64,2048]{1,0:T(8,128)(2,1)S(1)}, bf16[64,2048]{1,0:T(8,128)(2,1)}, u32[]{:S(2)}, u32[]{:S(2)}) collective-permute-start(bf16[64,2048]{1,0:T(8,128)(2,1)S(1)} %get-tuple-element.37), channel_id=1, source_target_pairs={{3,0},{0,1},{1,2},{2,3},{7,4},{4,5},{5,6},{6,7},{11,8},{8,9},{9,10... | collective-permute-start | bytes 786440 | tf_op jit(solution)/shard_map/ppermute | solution.py:38
  7.5 12.7 %collective-permute-start.6 = (bf16[64,2048]{1,0:T(8,128)(2,1)S(1)}, bf16[64,2048]{1,0:T(8,128)(2,1)S(1)}, u32[]{:S(2)}, u32[]{:S(2)}) collective-permute-start(bf16[64,2048]{1,0:T(8,128)(2,1)S(1)} %get-tuple-element.37), channel_id=1, source_target_pairs={{2,0},{3,1},{0,2},{1,3},{6,4},{7,5},{4,6},{5,7},{10,8},{11,9},{8,1... | collective-permute-start | bytes 786440 | tf_op jit(solution)/shard_map/ppermute | solution.py:38
  14.7 18.3 %collective-permute-start = (bf16[64,2048]{1,0:T(8,128)(2,1)S(1)}, bf16[64,2048]{1,0:T(8,128)(2,1)S(1)}, u32[]{:S(2)}, u32[]{:S(2)}) collective-permute-start(bf16[64,2048]{1,0:T(8,128)(2,1)S(1)} %get-tuple-element.38), channel_id=1, source_target_pairs={{0,0},{1,1},{2,2},{3,3},{4,4},{5,5},{6,6},{7,7},{8,8},{9,9},{10,10... | collective-permute-start | bytes 786440 | tf_op jit(solution)/shard_map/ppermute | solution.py:38
  22.6 17.4 %collective-permute-start.8 = (bf16[256,2048]{1,0:T(8,128)(2,1)S(1)}, bf16[256,2048]{1,0:T(8,128)(2,1)S(1)}, u32[]{:S(2)}, u32[]{:S(2)}) collective-permute-start(bf16[256,2048]{1,0:T(8,128)(2,1)S(1)} %shard_map.75), channel_id=1, source_target_pairs={{16,0},{17,1},{18,2},{19,3},{20,4},{21,5},{22,6},{23,7},{24,8},{25... | collective-permute-start | bytes 3145736 | tf_op jit(solution)/shard_map/ppermute | solution.py:38
  22.7 12.2 %collective-permute-start.1 = (bf16[64,2048]{1,0:T(8,128)(2,1)S(1)}, bf16[64,2048]{1,0:T(8,128)(2,1)S(1)}, u32[]{:S(2)}, u32[]{:S(2)}) collective-permute-start(bf16[64,2048]{1,0:T(8,128)(2,1)S(1)} %get-tuple-element.38), channel_id=1, source_target_pairs={{4,0},{5,1},{6,2},{7,3},{8,4},{9,5},{10,6},{11,7},{12,8},{13,9},{1... | collective-permute-start | bytes 786440 | tf_op jit(solution)/shard_map/ppermute | solution.py:38
  32.9 26.0 %collective-permute-start.36 = (bf16[256,2048]{1,0:T(8,128)(2,1)S(1)}, bf16[256,2048]{1,0:T(8,128)(2,1)S(1)}, u32[]{:S(2)}, u32[]{:S(2)}) collective-permute-start(bf16[256,2048]{1,0:T(8,128)(2,1)S(1)} %constant_dynamic-update-slice_fusion.6.refs_0_.refs_1_.refs_9_), channel_id=1, source_target_pairs={{8,0},{9,1},{10,2},{11,3},{12,4},{13,5},{14,6},{15,7},{0,8},{1,9},... | collective-permute-start | bytes 3145736 | tf_op jit(solution)/shard_map/ppermute | solution.py:38
  42.5 18.8 %collective-permute-start.11 = (bf16[64,2048]{1,0:T(8,128)(2,1)S(1)}, bf16[64,2048]{1,0:T(8,128)(2,1)S(1)}, u32[]{:S(2)}, u32[]{:S(2)}) collective-permute-start(bf16[64,2048]{1,0:T(8,128)(2,1)S(1)} %get-tuple-element.16), channel_id=1, source_target_pairs={{32,0},{33,1},{34,2},{35,3},{36,4},{37,5},{38,6},{39,7},{40,8},{41... | collective-permute-start | bytes 786440 | tf_op jit(solution)/shard_map/ppermute | solution.py:38
  45.6 19.5 %collective-permute-start.10 = (bf16[64,2048]{1,0:T(8,128)(2,1)S(1)}, bf16[64,2048]{1,0:T(8,128)(2,1)S(1)}, u32[]{:S(2)}, u32[]{:S(2)}) collective-permute-start(bf16[64,2048]{1,0:T(8,128)(2,1)S(1)} %get-tuple-element.17), channel_id=1, source_target_pairs={{64,0},{65,1},{66,2},{67,3},{68,4},{69,5},{70,6},{71,7},{72,8},{73... | collective-permute-start | bytes 786440 | tf_op jit(solution)/shard_map/ppermute | solution.py:38
  56.5 43.2 %collective-permute-start.35 = (bf16[256,2048]{1,0:T(8,128)(2,1)S(1)}, bf16[256,2048]{1,0:T(8,128)(2,1)S(1)}, u32[]{:S(2)}, u32[]{:S(2)}) collective-permute-start(bf16[256,2048]{1,0:T(8,128)(2,1)S(1)} %constant_dynamic-update-slice_fusion.2.refs_0_.refs_8_), channel_id=1, source_target_pairs={{2,0},{3,1},{0,2},{1,3},{6,4},{7,5},{4,6},{5,7},{10,8},{11,9},{8,1... | collective-permute-start | bytes 3145736 | tf_op jit(solution)/shard_map/ppermute | solution.py:38
  59.0 21.4 %collective-permute-start.26 = (bf16[256,2048]{1,0:T(8,128)(2,1)S(1)}, bf16[256,2048]{1,0:T(8,128)(2,1)S(1)}, u32[]{:S(2)}, u32[]{:S(2)}) collective-permute-start(bf16[256,2048]{1,0:T(8,128)(2,1)S(1)} %constant_dynamic-update-slice_fusion.6.refs_0_.refs_1_.refs_9_), channel_id=1, source_target_pairs={{12,0},{13,1},{14,2},{15,3},{0,4},{1,5},{2,6},{3,7},{4,8},{5,9},{6... | collective-permute-start | bytes 3145736 | tf_op jit(solution)/shard_map/ppermute | solution.py:38
  61.4 21.7 %collective-permute-start.16 = (bf16[256,2048]{1,0:T(8,128)(2,1)S(1)}, bf16[256,2048]{1,0:T(8,128)(2,1)S(1)}, u32[]{:S(2)}, u32[]{:S(2)}) collective-permute-start(bf16[256,2048]{1,0:T(8,128)(2,1)S(1)} %constant_dynamic-update-slice_fusion.6.refs_0_.refs_1_.refs_9_), channel_id=1, source_target_pairs={{4,0},{5,1},{6,2},{7,3},{8,4},{9,5},{10,6},{11,7},{12,8},{13,9},{1... | collective-permute-start | bytes 3145736 | tf_op jit(solution)/shard_map/ppermute | solution.py:38
  65.1 34.8 %collective-permute-start.37 = (bf16[256,2048]{1,0:T(8,128)(2,1)S(1)}, bf16[256,2048]{1,0:T(8,128)(2,1)S(1)}, u32[]{:S(2)}, u32[]{:S(2)}) collective-permute-start(bf16[256,2048]{1,0:T(8,128)(2,1)S(1)} %shard_map.84), channel_id=1, source_target_pairs={{16,0},{17,1},{18,2},{19,3},{20,4},{21,5},{22,6},{23,7},{24,8},{25... | collective-permute-start | bytes 3145736 | tf_op jit(solution)/shard_map/ppermute | solution.py:38
  66.5 19.8 %collective-permute-start.14 = (bf16[64,2048]{1,0:T(8,128)(2,1)S(1)}, bf16[64,2048]{1,0:T(8,128)(2,1)S(1)}, u32[]{:S(2)}, u32[]{:S(2)}) collective-permute-start(bf16[64,2048]{1,0:T(8,128)(2,1)S(1)} %pad_maximum_fusion.5), channel_id=1, source_target_pairs={{96,0},{97,1},{98,2},{99,3},{100,4},{101,5},{102,6},{103,7},{104,8... | collective-permute-start | bytes 786440 | tf_op jit(solution)/shard_map/ppermute | solution.py:38
  83.1 19.8 %collective-permute-start.25 = (bf16[256,2048]{1,0:T(8,128)(2,1)S(1)}, bf16[256,2048]{1,0:T(8,128)(2,1)S(1)}, u32[]{:S(2)}, u32[]{:S(2)}) collective-permute-start(bf16[256,2048]{1,0:T(8,128)(2,1)S(1)} %constant_dynamic-update-slice_fusion.2.refs_0_.refs_8_), channel_id=1, source_target_pairs={{3,0},{0,1},{1,2},{2,3},{7,4},{4,5},{5,6},{6,7},{11,8},{8,9},{9,10... | collective-permute-start | bytes 3145736 | tf_op jit(solution)/shard_map/ppermute | solution.py:38
  90.5 12.4 %collective-permute-start.27 = (bf16[256,2048]{1,0:T(8,128)(2,1)S(1)}, bf16[256,2048]{1,0:T(8,128)(2,1)S(1)}, u32[]{:S(2)}, u32[]{:S(2)}) collective-permute-start(bf16[256,2048]{1,0:T(8,128)(2,1)S(1)} %shard_map.81), channel_id=1, source_target_pairs={{16,0},{17,1},{18,2},{19,3},{20,4},{21,5},{22,6},{23,7},{24,8},{25... | collective-permute-start | bytes 3145736 | tf_op jit(solution)/shard_map/ppermute | solution.py:38
  93.0 19.0 %collective-permute-start.15 = (bf16[256,2048]{1,0:T(8,128)(2,1)S(1)}, bf16[256,2048]{1,0:T(8,128)(2,1)S(1)}, u32[]{:S(2)}, u32[]{:S(2)}) collective-permute-start(bf16[256,2048]{1,0:T(8,128)(2,1)S(1)} %constant_dynamic-update-slice_fusion.2.refs_0_.refs_8_), channel_id=1, source_target_pairs={{1,0},{2,1},{3,2},{0,3},{5,4},{6,5},{7,6},{4,7},{9,8},{10,9},{11,1... | collective-permute-start | bytes 3145736 | tf_op jit(solution)/shard_map/ppermute | solution.py:38
  99.8 12.2 %collective-permute-start.17 = (bf16[256,2048]{1,0:T(8,128)(2,1)S(1)}, bf16[256,2048]{1,0:T(8,128)(2,1)S(1)}, u32[]{:S(2)}, u32[]{:S(2)}) collective-permute-start(bf16[256,2048]{1,0:T(8,128)(2,1)S(1)} %shard_map.78), channel_id=1, source_target_pairs={{16,0},{17,1},{18,2},{19,3},{20,4},{21,5},{22,6},{23,7},{24,8},{25... | collective-permute-start | bytes 3145736 | tf_op jit(solution)/shard_map/ppermute | solution.py:38
  99.9 94.1 %collective-permute-start.49 = (bf16[256,2048]{1,0:T(8,128)(2,1)S(1)}, bf16[256,2048]{1,0:T(8,128)(2,1)S(1)}, u32[]{:S(2)}, u32[]{:S(2)}) collective-permute-start(bf16[256,2048]{1,0:T(8,128)(2,1)S(1)} %pad_maximum_fusion.refs_0_.refs_8_), channel_id=1, source_target_pairs={{16,0},{17,1},{18,2},{19,3},{20,4},{21,5},{22,6},{23,7},{24,8},{25... | collective-permute-start | bytes 3145736 | tf_op jit(solution)/shard_map/ppermute | solution.py:38
  102.9 14.9 %collective-permute-start.40 = (bf16[64,2048]{1,0:T(8,128)(2,1)S(1)}, bf16[64,2048]{1,0:T(8,128)(2,1)S(1)}, u32[]{:S(2)}, u32[]{:S(2)}) collective-permute-start(bf16[64,2048]{1,0:T(8,128)(2,1)S(1)} %get-tuple-element.25), channel_id=1, source_target_pairs={{32,0},{33,1},{34,2},{35,3},{36,4},{37,5},{38,6},{39,7},{40,8},{41... | collective-permute-start | bytes 786440 | tf_op jit(solution)/shard_map/ppermute | solution.py:38
  103.0 14.9 %collective-permute-start.39 = (bf16[64,2048]{1,0:T(8,128)(2,1)S(1)}, bf16[64,2048]{1,0:T(8,128)(2,1)S(1)}, u32[]{:S(2)}, u32[]{:S(2)}) collective-permute-start(bf16[64,2048]{1,0:T(8,128)(2,1)S(1)} %get-tuple-element.26), channel_id=1, source_target_pairs={{64,0},{65,1},{66,2},{67,3},{68,4},{69,5},{70,6},{71,7},{72,8},{73... | collective-permute-start | bytes 786440 | tf_op jit(solution)/shard_map/ppermute | solution.py:38
  112.0 14.9 %collective-permute-start.38 = (bf16[64,2048]{1,0:T(8,128)(2,1)S(1)}, bf16[64,2048]{1,0:T(8,128)(2,1)S(1)}, u32[]{:S(2)}, u32[]{:S(2)}) collective-permute-start(bf16[64,2048]{1,0:T(8,128)(2,1)S(1)} %get-tuple-element.24), channel_id=1, source_target_pairs={{96,0},{97,1},{98,2},{99,3},{100,4},{101,5},{102,6},{103,7},{104,8... | collective-permute-start | bytes 786440 | tf_op jit(solution)/shard_map/ppermute | solution.py:38
  112.0 15.5 %collective-permute-start.30 = (bf16[64,2048]{1,0:T(8,128)(2,1)S(1)}, bf16[64,2048]{1,0:T(8,128)(2,1)S(1)}, u32[]{:S(2)}, u32[]{:S(2)}) collective-permute-start(bf16[64,2048]{1,0:T(8,128)(2,1)S(1)} %get-tuple-element.22), channel_id=1, source_target_pairs={{32,0},{33,1},{34,2},{35,3},{36,4},{37,5},{38,6},{39,7},{40,8},{41... | collective-permute-start | bytes 786440 | tf_op jit(solution)/shard_map/ppermute | solution.py:38
  117.8 20.1 %collective-permute-start.28 = (bf16[64,2048]{1,0:T(8,128)(2,1)S(1)}, bf16[64,2048]{1,0:T(8,128)(2,1)S(1)}, u32[]{:S(2)}, u32[]{:S(2)}) collective-permute-start(bf16[64,2048]{1,0:T(8,128)(2,1)S(1)} %get-tuple-element.21), channel_id=1, source_target_pairs={{96,0},{97,1},{98,2},{99,3},{100,4},{101,5},{102,6},{103,7},{104,8... | collective-permute-start | bytes 786440 | tf_op jit(solution)/shard_map/ppermute | solution.py:38
  126.9 11.3 %collective-permute-start.20 = (bf16[64,2048]{1,0:T(8,128)(2,1)S(1)}, bf16[64,2048]{1,0:T(8,128)(2,1)S(1)}, u32[]{:S(2)}, u32[]{:S(2)}) collective-permute-start(bf16[64,2048]{1,0:T(8,128)(2,1)S(1)} %get-tuple-element.19), channel_id=1, source_target_pairs={{32,0},{33,1},{34,2},{35,3},{36,4},{37,5},{38,6},{39,7},{40,8},{41... | collective-permute-start | bytes 786440 | tf_op jit(solution)/shard_map/ppermute | solution.py:38
  127.5 11.9 %collective-permute-start.19 = (bf16[64,2048]{1,0:T(8,128)(2,1)S(1)}, bf16[64,2048]{1,0:T(8,128)(2,1)S(1)}, u32[]{:S(2)}, u32[]{:S(2)}) collective-permute-start(bf16[64,2048]{1,0:T(8,128)(2,1)S(1)} %get-tuple-element.20), channel_id=1, source_target_pairs={{64,0},{65,1},{66,2},{67,3},{68,4},{69,5},{70,6},{71,7},{72,8},{73... | collective-permute-start | bytes 786440 | tf_op jit(solution)/shard_map/ppermute | solution.py:38
  128.5 15.9 %collective-permute-start.18 = (bf16[64,2048]{1,0:T(8,128)(2,1)S(1)}, bf16[64,2048]{1,0:T(8,128)(2,1)S(1)}, u32[]{:S(2)}, u32[]{:S(2)}) collective-permute-start(bf16[64,2048]{1,0:T(8,128)(2,1)S(1)} %get-tuple-element.18), channel_id=1, source_target_pairs={{96,0},{97,1},{98,2},{99,3},{100,4},{101,5},{102,6},{103,7},{104,8... | collective-permute-start | bytes 786440 | tf_op jit(solution)/shard_map/ppermute | solution.py:38
  137.9 14.7 %collective-permute-start.43 = (bf16[64,2048]{1,0:T(8,128)(2,1)S(1)}, bf16[64,2048]{1,0:T(8,128)(2,1)S(1)}, u32[]{:S(2)}, u32[]{:S(2)}) collective-permute-start(bf16[64,2048]{1,0:T(8,128)(2,1)S(1)} %pad_maximum_fusion.8), channel_id=1, source_target_pairs={{96,0},{97,1},{98,2},{99,3},{100,4},{101,5},{102,6},{103,7},{104,8... | collective-permute-start | bytes 786440 | tf_op jit(solution)/shard_map/ppermute | solution.py:38
  138.2 14.4 %collective-permute-start.42 = (bf16[64,2048]{1,0:T(8,128)(2,1)S(1)}, bf16[64,2048]{1,0:T(8,128)(2,1)S(1)}, u32[]{:S(2)}, u32[]{:S(2)}) collective-permute-start(bf16[64,2048]{1,0:T(8,128)(2,1)S(1)} %pad_maximum_fusion.8), channel_id=1, source_target_pairs={{64,0},{65,1},{66,2},{67,3},{68,4},{69,5},{70,6},{71,7},{72,8},{73... | collective-permute-start | bytes 786440 | tf_op jit(solution)/shard_map/ppermute | solution.py:38
  139.3 15.9 %collective-permute-start.41 = (bf16[64,2048]{1,0:T(8,128)(2,1)S(1)}, bf16[64,2048]{1,0:T(8,128)(2,1)S(1)}, u32[]{:S(2)}, u32[]{:S(2)}) collective-permute-start(bf16[64,2048]{1,0:T(8,128)(2,1)S(1)} %pad_maximum_fusion.8), channel_id=1, source_target_pairs={{32,0},{33,1},{34,2},{35,3},{36,4},{37,5},{38,6},{39,7},{40,8},{41... | collective-permute-start | bytes 786440 | tf_op jit(solution)/shard_map/ppermute | solution.py:38
  144.4 21.7 %collective-permute-start.33 = (bf16[64,2048]{1,0:T(8,128)(2,1)S(1)}, bf16[64,2048]{1,0:T(8,128)(2,1)S(1)}, u32[]{:S(2)}, u32[]{:S(2)}) collective-permute-start(bf16[64,2048]{1,0:T(8,128)(2,1)S(1)} %pad_maximum_fusion.7), channel_id=1, source_target_pairs={{96,0},{97,1},{98,2},{99,3},{100,4},{101,5},{102,6},{103,7},{104,8... | collective-permute-start | bytes 786440 | tf_op jit(solution)/shard_map/ppermute | solution.py:38
  152.7 13.5 %collective-permute-start.32 = (bf16[64,2048]{1,0:T(8,128)(2,1)S(1)}, bf16[64,2048]{1,0:T(8,128)(2,1)S(1)}, u32[]{:S(2)}, u32[]{:S(2)}) collective-permute-start(bf16[64,2048]{1,0:T(8,128)(2,1)S(1)} %pad_maximum_fusion.7), channel_id=1, source_target_pairs={{64,0},{65,1},{66,2},{67,3},{68,4},{69,5},{70,6},{71,7},{72,8},{73... | collective-permute-start | bytes 786440 | tf_op jit(solution)/shard_map/ppermute | solution.py:38
  152.7 14.5 %collective-permute-start.31 = (bf16[64,2048]{1,0:T(8,128)(2,1)S(1)}, bf16[64,2048]{1,0:T(8,128)(2,1)S(1)}, u32[]{:S(2)}, u32[]{:S(2)}) collective-permute-start(bf16[64,2048]{1,0:T(8,128)(2,1)S(1)} %pad_maximum_fusion.7), channel_id=1, source_target_pairs={{32,0},{33,1},{34,2},{35,3},{36,4},{37,5},{38,6},{39,7},{40,8},{41... | collective-permute-start | bytes 786440 | tf_op jit(solution)/shard_map/ppermute | solution.py:38
  155.4 39.6 %collective-permute-start.54 = (bf16[256,2048]{1,0:T(8,128)(2,1)S(1)}, bf16[256,2048]{1,0:T(8,128)(2,1)S(1)}, u32[]{:S(2)}, u32[]{:S(2)}) collective-permute-start(bf16[256,2048]{1,0:T(8,128)(2,1)S(1)} %pad_maximum_fusion.3.refs_0_.refs_14_.refs_6_), channel_id=1, source_target_pairs={{16,0},{17,1},{18,2},{19,3},{20,4},{21,5},{22,6},{23,7},{24,8},{25... | collective-permute-start | bytes 3145736 | tf_op jit(solution)/shard_map/ppermute | solution.py:38
  176.5 30.1 %collective-permute-start.52 = (bf16[256,2048]{1,0:T(8,128)(2,1)}, bf16[256,2048]{1,0:T(8,128)(2,1)}, u32[]{:S(2)}, u32[]{:S(2)}) collective-permute-start(bf16[256,2048]{1,0:T(8,128)(2,1)} %pad_maximum_fusion.2.refs_0_.refs_12_.refs_4_), channel_id=1, source_target_pairs={{16,0},{17,1},{18,2},{19,3},{20,4},{21,5},{22,6},{23,7},{24,8},{25... | collective-permute-start | bytes 3145736 | tf_op jit(solution)/shard_map/ppermute | solution.py:38
  186.0 26.3 %collective-permute-start.50 = (bf16[256,2048]{1,0:T(8,128)(2,1)}, bf16[256,2048]{1,0:T(8,128)(2,1)}, u32[]{:S(2)}, u32[]{:S(2)}) collective-permute-start(bf16[256,2048]{1,0:T(8,128)(2,1)} %pad_maximum_fusion.1.refs_0_.refs_10_.refs_2_), channel_id=1, source_target_pairs={{16,0},{17,1},{18,2},{19,3},{20,4},{21,5},{22,6},{23,7},{24,8},{25... | collective-permute-start | bytes 3145736 | tf_op jit(solution)/shard_map/ppermute | solution.py:38
  186.0 32.0 %collective-permute-start.44 = (bf16[256,2048]{1,0:T(8,128)(2,1)}, bf16[256,2048]{1,0:T(8,128)(2,1)}, u32[]{:S(2)}, u32[]{:S(2)}) collective-permute-start(bf16[256,2048]{1,0:T(8,128)(2,1)} %shard_map.86), channel_id=1, source_target_pairs={{2,0},{3,1},{0,2},{1,3},{6,4},{7,5},{4,6},{5,7},{10,8},{11,9},{8,1... | collective-permute-start | bytes 3145736 | tf_op jit(solution)/shard_map/ppermute | solution.py:38
  195.0 31.7 %collective-permute-start.34 = (bf16[256,2048]{1,0:T(8,128)(2,1)}, bf16[256,2048]{1,0:T(8,128)(2,1)}, u32[]{:S(2)}, u32[]{:S(2)}) collective-permute-start(bf16[256,2048]{1,0:T(8,128)(2,1)} %shard_map.83), channel_id=1, source_target_pairs={{1,0},{2,1},{3,2},{0,3},{5,4},{6,5},{7,6},{4,7},{9,8},{10,9},{11,1... | collective-permute-start | bytes 3145736 | tf_op jit(solution)/shard_map/ppermute | solution.py:38
  196.0 30.7 %collective-permute-start.24 = (bf16[256,2048]{1,0:T(8,128)(2,1)}, bf16[256,2048]{1,0:T(8,128)(2,1)}, u32[]{:S(2)}, u32[]{:S(2)}) collective-permute-start(bf16[256,2048]{1,0:T(8,128)(2,1)} %shard_map.80), channel_id=1, source_target_pairs={{3,0},{0,1},{1,2},{2,3},{7,4},{4,5},{5,6},{6,7},{11,8},{8,9},{9,10... | collective-permute-start | bytes 3145736 | tf_op jit(solution)/shard_map/ppermute | solution.py:38
  206.6 39.7 %collective-permute-start.55 = (bf16[256,2048]{1,0:T(8,128)(2,1)S(1)}, bf16[256,2048]{1,0:T(8,128)(2,1)S(1)}, u32[]{:S(2)}, u32[]{:S(2)}) collective-permute-start(bf16[256,2048]{1,0:T(8,128)(2,1)S(1)} %shard_map.90), channel_id=1, source_target_pairs={{8,0},{9,1},{10,2},{11,3},{12,4},{13,5},{14,6},{15,7},{0,8},{1,9},... | collective-permute-start | bytes 3145736 | tf_op jit(solution)/shard_map/ppermute | solution.py:38
  212.3 36.8 %collective-permute-start.53 = (bf16[256,2048]{1,0:T(8,128)(2,1)S(1)}, bf16[256,2048]{1,0:T(8,128)(2,1)S(1)}, u32[]{:S(2)}, u32[]{:S(2)}) collective-permute-start(bf16[256,2048]{1,0:T(8,128)(2,1)S(1)} %shard_map.89), channel_id=1, source_target_pairs={{4,0},{5,1},{6,2},{7,3},{8,4},{9,5},{10,6},{11,7},{12,8},{13,9},{1... | collective-permute-start | bytes 3145736 | tf_op jit(solution)/shard_map/ppermute | solution.py:38
  218.1 31.8 %collective-permute-start.51 = (bf16[256,2048]{1,0:T(8,128)(2,1)S(1)}, bf16[256,2048]{1,0:T(8,128)(2,1)S(1)}, u32[]{:S(2)}, u32[]{:S(2)}) collective-permute-start(bf16[256,2048]{1,0:T(8,128)(2,1)S(1)} %shard_map.88), channel_id=1, source_target_pairs={{12,0},{13,1},{14,2},{15,3},{0,4},{1,5},{2,6},{3,7},{4,8},{5,9},{6... | collective-permute-start | bytes 3145736 | tf_op jit(solution)/shard_map/ppermute | solution.py:38
  229.6 24.0 %collective-permute-start.48 = (bf16[64,2048]{1,0:T(8,128)(2,1)S(1)}, bf16[64,2048]{1,0:T(8,128)(2,1)S(1)}, u32[]{:S(2)}, u32[]{:S(2)}) collective-permute-start(bf16[64,2048]{1,0:T(8,128)(2,1)S(1)} %get-tuple-element.8), channel_id=1, source_target_pairs={{4,0},{5,1},{6,2},{7,3},{8,4},{9,5},{10,6},{11,7},{12,8},{13,9},{1... | collective-permute-start | bytes 786440 | tf_op jit(solution)/shard_map/ppermute | solution.py:38
  236.3 24.2 %collective-permute-start.47 = (bf16[64,2048]{1,0:T(8,128)(2,1)S(1)}, bf16[64,2048]{1,0:T(8,128)(2,1)S(1)}, u32[]{:S(2)}, u32[]{:S(2)}) collective-permute-start(bf16[64,2048]{1,0:T(8,128)(2,1)S(1)} %get-tuple-element.9), channel_id=1, source_target_pairs={{8,0},{9,1},{10,2},{11,3},{12,4},{13,5},{14,6},{15,7},{0,8},{1,9},... | collective-permute-start | bytes 786440 | tf_op jit(solution)/shard_map/ppermute | solution.py:38
  246.3 16.2 %collective-permute-start.46 = (bf16[64,2048]{1,0:T(8,128)(2,1)S(1)}, bf16[64,2048]{1,0:T(8,128)(2,1)S(1)}, u32[]{:S(2)}, u32[]{:S(2)}) collective-permute-start(bf16[64,2048]{1,0:T(8,128)(2,1)S(1)} %get-tuple-element.10), channel_id=1, source_target_pairs={{12,0},{13,1},{14,2},{15,3},{0,4},{1,5},{2,6},{3,7},{4,8},{5,9},{6... | collective-permute-start | bytes 786440 | tf_op jit(solution)/shard_map/ppermute | solution.py:38
  249.1 22.7 %collective-permute-start.45 = (bf16[64,2048]{1,0:T(8,128)(2,1)S(1)}, bf16[64,2048]{1,0:T(8,128)(2,1)S(1)}, u32[]{:S(2)}, u32[]{:S(2)}) collective-permute-start(bf16[64,2048]{1,0:T(8,128)(2,1)S(1)} %get-tuple-element.7), channel_id=1, source_target_pairs={{0,0},{1,1},{2,2},{3,3},{4,4},{5,5},{6,6},{7,7},{8,8},{9,9},{10,10... | collective-permute-start | bytes 786440 | tf_op jit(solution)/shard_map/ppermute | solution.py:38
  250.7 21.1 %collective-permute-start.59 = (bf16[64,2048]{1,0:T(8,128)(2,1)S(1)}, bf16[64,2048]{1,0:T(8,128)(2,1)S(1)}, u32[]{:S(2)}, u32[]{:S(2)}) collective-permute-start(bf16[64,2048]{1,0:T(8,128)(2,1)S(1)} %get-tuple-element.12), channel_id=1, source_target_pairs={{3,0},{0,1},{1,2},{2,3},{7,4},{4,5},{5,6},{6,7},{11,8},{8,9},{9,10... | collective-permute-start | bytes 786440 | tf_op jit(solution)/shard_map/ppermute | solution.py:38
  253.6 18.2 %collective-permute-start.58 = (bf16[64,2048]{1,0:T(8,128)(2,1)S(1)}, bf16[64,2048]{1,0:T(8,128)(2,1)S(1)}, u32[]{:S(2)}, u32[]{:S(2)}) collective-permute-start(bf16[64,2048]{1,0:T(8,128)(2,1)S(1)} %get-tuple-element.13), channel_id=1, source_target_pairs={{2,0},{3,1},{0,2},{1,3},{6,4},{7,5},{4,6},{5,7},{10,8},{11,9},{8,1... | collective-permute-start | bytes 786440 | tf_op jit(solution)/shard_map/ppermute | solution.py:38
  (37 other events, 573.6 us)

commit v2 on v1

v2 whole, which is shorter than its diff:
```python
import functools
import math

import jax
import jax.numpy as jnp
from jax import lax
from jax.experimental import pallas as pl
from jax.experimental.pallas import tpu as pltpu
from jax.sharding import PartitionSpec as P

AXES = ("row", "col", "dp")
RING = 4
BF = jnp.bfloat16
F32 = jnp.float32
NN = (((1,), (0,)), ((), ()))
NT = (((1,), (1,)), ((), ()))
TN = (((0,), (0,)), ((), ()))


def gelu_parts(pre):
    cdf = 0.5 * (1.0 + jax.scipy.special.erf(pre * (1.0 / math.sqrt(2.0))))
    activated = pre * cdf
    slope = cdf + pre * jnp.exp(-0.5 * pre * pre) * (1.0 / math.sqrt(2.0 * math.pi))
    return (activated, slope)


def flat(z, c, x, y):
    return ((z * 2 + c) * RING + x) * RING + y


def exchange(array, partner):
    pairs = []
    for z in range(RING):
        for c in range(2):
            for x in range(RING):
                for y in range(RING):
                    pairs.append((flat(*partner(z, c, x, y)), flat(z, c, x, y)))
    return lax.ppermute(array, AXES, pairs)


NEAR = ((1, 3), (3, 1))
Z_PAIR = ((1, 3), (3, 1))
OWNER_SLOT = ((0, 2, 3, 1), (0, 1, 3, 2))


def along(keep, first, turn):
    def partner(z, c, x, y):
        half = c if keep else 1 - c
        step = NEAR[c][turn]
        if (half == 0) == first:
            return (z, c, x ^ step, y)
        return (z, c, x, y ^ step)

    return partner


def along_z(turn):
    return lambda z, c, x, y: (z ^ Z_PAIR[c][turn], c, x, y)


def other_core(z, c, x, y):
    return (z, 1 - c, x, y)


def slots_of(keep, z, core):
    def one(c):
        owner = c if keep else 1 - c
        table = jnp.array(OWNER_SLOT[owner], jnp.int32)
        near = NEAR[c]
        arrival = jnp.array([0, near[0], near[1], near[0] ^ near[1]], jnp.int32)
        return table[z ^ arrival]

    return jnp.where(core == 0, one(0), one(1))


def assemble_kernel(slot_ref, a_ref, b_ref, c_ref, out_ref):
    rows = a_ref.shape[0]

    def put(i, value):
        out_ref[pl.ds(pl.multiple_of(slot_ref[i] * rows, rows), rows), :] = value

    put(0, a_ref[...])
    put(1, b_ref[...])
    put(2, c_ref[:rows, :])
    put(3, c_ref[rows:, :])


def assemble(slots, a, b, c):
    rows, wide = a.shape
    tiles = 2
    spec = lambda n: pl.BlockSpec((n, wide // tiles), lambda i, slot: (0, i))
    return pl.pallas_call(
        assemble_kernel,
        grid_spec=pltpu.PrefetchScalarGridSpec(
            num_scalar_prefetch=1,
            grid=(tiles,),
            in_specs=[spec(rows), spec(rows), spec(2 * rows)],
            out_specs=spec(4 * rows),
        ),
        out_shape=jax.ShapeDtypeStruct((4 * rows, wide), BF),
        cost_estimate=pl.CostEstimate(flops=0, bytes_accessed=16 * rows * wide, transcendentals=0),
    )(slots, a, b, c)


def pair_kernel(pieces, added, split, ordered, block, slot_ref, *refs):
    a_refs, rest = refs[:pieces], refs[pieces:]
    left_ref, right_ref = rest[:2]
    rest = rest[2:]
    if added:
        more_ref, rest = rest[0], rest[1:]

    def rows_of():
        values = []
        for a_ref in a_refs:
            for i in range(a_ref.shape[0] // (4 * block)):
                if ordered:
                    for j in range(4):
                        first = pl.multiple_of(slot_ref[j] * block, block)
                        values.append(a_ref[pl.ds(i * 4 * block + first, block), :])
                else:
                    values.append(a_ref[i * 4 * block:(i + 1) * 4 * block, :])
        return values[0] if len(values) == 1 else jnp.concatenate(values, axis=0)

    def finish(total):
        if added:
            total = total + more_ref[...].astype(F32)
        total = total.astype(BF)
        if not split:
            rest[0][...] = total
            return
        two = 2 * block
        for i in range(total.shape[0] // (2 * two)):
            rest[0][i * two:(i + 1) * two, :] = total[2 * i * two:(2 * i + 1) * two]
            rest[1][i * two:(i + 1) * two, :] = total[(2 * i + 1) * two:(2 * i + 2) * two]

    @pl.when(pl.program_id(0) == 0)
    def _():
        finish(lax.dot_general(rows_of(), left_ref[...], NN, preferred_element_type=F32))

    @pl.when(pl.program_id(0) == 1)
    def _():
        finish(lax.dot_general(rows_of(), right_ref[...], NT, preferred_element_type=F32))


def pair_dot(pieces, left, right, slots, block, more=None, split=False, ordered=False, tile=512):
    rows = sum(a.shape[0] for a in pieces)
    depth, wide = left.shape
    tiles = wide // tile
    in_specs = [pl.BlockSpec((a.shape[0], depth), lambda h, n, slot: (0, h)) for a in pieces]
    in_specs += [
        pl.BlockSpec((depth, tile), lambda h, n, slot: (0, n * (1 - h) + (tiles - 1) * h)),
        pl.BlockSpec((tile, depth), lambda h, n, slot: (n * h, 0)),
    ]
    out_of = lambda n_rows: pl.BlockSpec((n_rows, tile), lambda h, n, slot: (0, h * tiles + n))
    args = [*pieces, left, right]
    if more is not None:
        in_specs.append(out_of(rows))
        args.append(more)
    outs = [rows // 2, rows // 2] if split else [rows]
    result = pl.pallas_call(
        functools.partial(pair_kernel, len(pieces), more is not None, split, ordered, block),
        grid_spec=pltpu.PrefetchScalarGridSpec(
            num_scalar_prefetch=1,
            grid=(2, tiles),
            in_specs=in_specs,
            out_specs=[out_of(n) for n in outs],
        ),
        out_shape=[jax.ShapeDtypeStruct((n, 2 * wide), BF) for n in outs],
        compiler_params=pltpu.CompilerParams(vmem_limit_bytes=24 * 2**20),
        cost_estimate=pl.CostEstimate(
            flops=4 * rows * depth * wide,
            bytes_accessed=4 * depth * wide + 8 * rows * wide,
            transcendentals=0,
        ),
    )(slots, *args)
    return result if split else result[0]


def grad_kernel(left_count, pairs, factor, *refs):
    lefts, rights, out_ref = refs[:left_count], refs[left_count:-1], refs[-1]
    total = None
    for i, first, j, second, rows in pairs:
        term = lax.dot_general(
            lefts[i][first:first + rows, :],
            rights[j][second:second + rows, :],
            TN,
            preferred_element_type=F32,
        )
        total = term if total is None else total + term
    out_ref[...] = total * factor


def grad_dot(lefts, left_part, rights, right_part, pairs, factor, tile=256):
    wide = lefts[0].shape[1] // 2
    tiles = wide // tile
    tokens = sum(a.shape[0] for a in lefts)
    return pl.pallas_call(
        functools.partial(grad_kernel, len(lefts), pairs, factor),
        grid=(tiles,),
        in_specs=[pl.BlockSpec((a.shape[0], wide), lambda n: (0, left_part)) for a in lefts]
        + [pl.BlockSpec((a.shape[0], tile), lambda n: (0, right_part * tiles + n)) for a in rights],
        out_specs=pl.BlockSpec((wide, tile), lambda n: (0, n)),
        out_shape=jax.ShapeDtypeStruct((wide, wide), F32),
        compiler_params=pltpu.CompilerParams(vmem_limit_bytes=40 * 2**20),
        cost_estimate=pl.CostEstimate(
            flops=2 * tokens * wide * wide,
            bytes_accessed=4 * tokens * wide + 4 * wide * wide,
            transcendentals=0,
        ),
    )(*lefts, *rights)


def blocks_of(array, count, block):
    pieces = array.shape[0] // (count * block)
    cut = array.reshape(pieces, count, block, array.shape[1])
    return [cut[:, i].reshape(pieces * block, array.shape[1]) for i in range(count)]


def shards(tokens, out_grad, weight_in, weight_out):
    core = lax.axis_index("row") % 2
    z = lax.axis_index("row") // 2
    dp = lax.axis_index("dp")
    rows, width = tokens.shape
    block = rows // 2
    inner = weight_in.shape[1] // 2
    factor = 1.0 / math.sqrt(rows * 16)
    both_ways = (True, False)

    both = jnp.concatenate([tokens, out_grad], axis=1)
    slots = {keep: slots_of(keep, z, core) for keep in both_ways}
    w_in = lax.dynamic_slice_in_dim(weight_in, dp * inner, inner, 1)
    w_out = lax.dynamic_slice_in_dim(weight_out, dp * inner, inner, 0)

    panel = {}
    one, two = {}, {}
    start = {
        True: lax.dynamic_slice_in_dim(both, core * block, block, 0),
        False: lax.dynamic_slice_in_dim(both, (1 - core) * block, block, 0),
    }
    for keep in both_ways:
        one[keep] = exchange(start[keep], along(keep, True, 0))
    for keep in both_ways:
        pair = jnp.concatenate([start[keep], one[keep]], axis=0)
        two[keep] = exchange(pair, along(keep, True, 1))
    for keep in both_ways:
        panel[keep, 0] = assemble(slots[keep], start[keep], one[keep], two[keep])
    for keep in both_ways:
        panel[keep, 1] = exchange(panel[keep, 0], along(keep, False, 0))
    for keep in both_ways:
        panel[keep, 2] = exchange(panel[keep, 0], along(keep, False, 1))
    for keep in both_ways:
        panel[keep, 3] = exchange(panel[keep, 1], along(keep, False, 1))

    batches = {True: ((0,), (1, 2), (3,)), False: ((0,), (2, 1), (3,))}
    hidden = {}
    summed = {}
    for b in range(3):
        sent = pair_dot(
            [panel[False, p] for p in batches[False][b]], w_in, w_out, slots[False], block
        )
        kept, passed = pair_dot(
            [panel[True, p] for p in batches[True][b]],
            w_in,
            w_out,
            slots[True],
            block,
            more=exchange(sent, other_core),
            split=True,
        )
        got = exchange(passed, along_z(0))
        kept, got = blocks_of(kept, 2, block), blocks_of(got, 2, block)
        halfway = [kept[i].astype(F32) + got[i].astype(F32) for i in range(2)]
        value = halfway[0] + exchange(halfway[1].astype(BF), along_z(1)).astype(F32)
        pre, back = value[:, :width], value[:, width:]
        activated, slope = gelu_parts(pre)
        mine = jnp.concatenate([activated.astype(BF), (back * slope).astype(BF)], axis=1)
        pair = jnp.concatenate([mine, exchange(mine, along_z(1))], axis=0)
        other = exchange(pair, along_z(0))
        count = len(batches[True][b])
        hidden[True, b] = jnp.concatenate(
            [a.reshape(2, count, block, 2 * width) for a in (pair, other)], axis=0
        ).transpose(1, 0, 2, 3).reshape(4 * count * block, 2 * width)
        hidden[False, b] = exchange(hidden[True, b], other_core)

        for keep in both_ways:
            kept, passed = pair_dot(
                [hidden[keep, b]], w_out, w_in, slots[keep], block, split=True, ordered=True
            )
            got = exchange(passed, along(keep, True, 1))
            kept, got = blocks_of(kept, 2, block), blocks_of(got, 2, block)
            halfway = [kept[i].astype(F32) + got[i].astype(F32) for i in range(2)]
            total = halfway[0] + exchange(
                halfway[1].astype(BF), along(keep, True, 0)
            ).astype(F32)
            for i, p in enumerate(batches[keep][b]):
                summed[keep, p] = total[i * block:(i + 1) * block]

    done = {}
    for keep in both_ways:
        passed = jnp.concatenate([summed[keep, 2], summed[keep, 3]], axis=0).astype(BF)
        got = exchange(passed, along(keep, False, 1)).astype(F32)
        last = (summed[keep, 1] + got[block:]).astype(BF)
        done[keep] = (
            summed[keep, 0] + got[:block] + exchange(last, along(keep, False, 0)).astype(F32)
        ).astype(BF)

    panels, hiddens, in_pairs, out_pairs = [], [], [], []
    for keep in both_ways:
        for b in range(3):
            for i, p in enumerate(batches[keep][b]):
                in_pairs.append((len(panels), 0, len(hiddens), i * 4 * block, 4 * block))
                out_pairs.append((len(hiddens), i * 4 * block, len(panels), 0, 4 * block))
                panels.append(panel[keep, p])
            hiddens.append(hidden[keep, b])
    grad_in = grad_dot(panels, 0, hiddens, 1, in_pairs, factor)
    grad_out = grad_dot(hiddens, 0, panels, 1, out_pairs, factor)

    low = jnp.where(core == 0, done[True], done[False])
    high = jnp.where(core == 0, done[False], done[True])
    result = jnp.concatenate([low, high], axis=0)
    return (result[:, :width], result[:, width:], grad_in, grad_out)


def solution(mesh):
    placed = (P(("col", "dp"), "row"), P(("col", "dp"), "row"), P("row", "col"), P("col", "row"))
    return jax.shard_map(
        shards,
        mesh=mesh,
        in_specs=placed,
        out_specs=(
            P(("col", "dp"), "row"),
            P(("col", "dp"), "row"),
            P("row", ("col", "dp")),
            P(("col", "dp"), "row"),
        ),
        check_vma=False,
    )
```

time: 276 us -> 256 us (0.928)
  starting transfers between devices: 117 us -> 52.3 us
  waiting for transfers between devices: 73.5 us -> 116 us
  Pallas kernels: 61.5 us -> 67.5 us
    ppermute x60 -> x44, starting transfers between devices: 117 us -> 52.3 us  [exchange(): return lax.ppermute(array, AXES, pairs)]
    ppermute x60 -> x44, waiting for transfers between devices: 73.5 us -> 116 us  [exchange(): return lax.ppermute(array, AXES, pairs)]
    pallas_call x18 -> x16, Pallas kernels: 61.5 us -> 67.5 us  [the longest x12 45 us: pair_dot(): pl.pallas_call(functools.partial(pair_kernel, len(pieces), more is not No...]
    unnamed x57 -> x33, local copies, waits for them, and re-layouts: 6.83 us -> 4.65 us
  transfers between devices with their start and end apart: 60 -> 44, of which waited for: 15 -> 18; matrix products, arithmetic and copies ran while one was open for 5% -> 4% of each run, Pallas kernels for 23% -> 25%
where the time goes in v2:
time: 256 us; the launch traced here: 255 us
  waiting for transfers between devices  116 us (45%)
  Pallas kernels  67.5 us (26%)
  starting transfers between devices  52.3 us (20%)
  local copies, waits for them, and re-layouts  11.3 us (4%)
  other arithmetic  7.07 us (3%)
    ppermute x44, waiting for transfers between devices, exchange(): return lax.ppermute(array, AXES, pairs)  116 us
    ppermute x44, starting transfers between devices, exchange(): return lax.ppermute(array, AXES, pairs)  52.3 us
    pallas_call x12, Pallas kernels, pair_dot(): pl.pallas_call(functools.partial(pair_kernel, len(pieces), more is not No...  45 us
    pallas_call x2, Pallas kernels, grad_dot(): pl.pallas_call(functools.partial(grad_kernel, len(lefts), pairs, factor),...  16.8 us
    pallas_call x2, Pallas kernels, assemble(): pl.pallas_call(assemble_kernel, grid_spec=pltpu.PrefetchScalarGridSpec(nu...  5.7 us
  transfers between devices with their start and end apart: 44, of which 18 were waited for; matrix products, arithmetic and copies ran while one was open for 4% of the time, Pallas kernels for 25%

profile of v2, /device:TPU:8, one launch (start us, length us, event | category | flops | bytes accessed | tf_op | source)
XLA Modules:
  0.0 255.1 jit_solution(12078137787453257270)
XLA Ops:
  3.2 6.0 %collective-permute-done.2.b_ref = bf16[64,2048]{1,0:T(8,128)(2,1)S(1)} collective-permute-done((bf16[64,2048]{1,0:T(8,128)(2,1)S(1)}, bf16[64,2048]{1,0:T(8,128)(2,1)S(1)}, u32[]{:S(2)}, u32[]{:S(2)}) %collective-permute-start.2) | collective-permute-done | bytes 262176 | tf_op jit(solution)/shard_map/ppermute | solution.py:38
  12.8 5.7 %collective-permute-done.3.c_ref = bf16[128,2048]{1,0:T(8,128)(2,1)S(1)} collective-permute-done((bf16[128,2048]{1,0:T(8,128)(2,1)S(1)}, bf16[128,2048]{1,0:T(8,128)(2,1)S(1)}, u32[]{:S(2)}, u32[]{:S(2)}) %collective-permute-start.3) | collective-permute-done | bytes 524320 | tf_op jit(solution)/shard_map/ppermute | solution.py:38
  19.3 2.8 %shard_map.148.refs_0_.refs_4_.refs_10_ = bf16[256,2048]{1,0:T(8,128)(2,1)} custom-call(s32[4]{0:T(128)} %broadcast_select_fusion.2.slot_ref, bf16[64,2048]{1,0:T(8,128)(2,1)} %copy-done.12, bf16[64,2048]{1,0:T(8,128)(2,1)} %copy-done.13, bf16[128,2048]{1,0:T(8,128)(2,1)} %copy-done.14), custom_call_target="tpu_custom_call" | custom-call | bytes 2097152 | tf_op jit(solution)/shard_map/pallas_call | solution.py:92
  23.5 2.1 collective-permute-start.13
  27.5 2.8 %constant_dynamic-slice_fusion.1 = (bf16[1024,1024]{1,0:T(8,128)(2,1)S(1)}, bf16[1024,1024]{1,0:T(8,128)(2,1)S(1)}) fusion(bf16[2048,1024]{1,0:T(8,128)(2,1)} %param.15, s32[]{:T(128)S(6)} %select_n.65, bf16[1024,2048]{1,0:T(8,128)(2,1)} %param.14), kind=kLoop, calls=%fused_computation.98 | loop fusion | bytes 8388612 | tf_op jit(solution)/shard_map/dynamic_slice | solution.py:232
  30.3 9.7 %collective-permute-done.b_ref = bf16[64,2048]{1,0:T(8,128)(2,1)} collective-permute-done((bf16[64,2048]{1,0:T(8,128)(2,1)S(1)}, bf16[64,2048]{1,0:T(8,128)(2,1)}, u32[]{:S(2)}, u32[]{:S(2)}) %collective-permute-start) | collective-permute-done | bytes 262176 | tf_op jit(solution)/shard_map/ppermute | solution.py:38
  41.0 2.8 %collective-permute-start.1 = (bf16[128,2048]{1,0:T(8,128)(2,1)S(1)}, bf16[128,2048]{1,0:T(8,128)(2,1)}, u32[]{:S(2)}, u32[]{:S(2)}) collective-permute-start(bf16[128,2048]{1,0:T(8,128)(2,1)S(1)} %pad_maximum_fusion.3), channel_id=1, source_target_pairs={{12,0},{13,1},{14,2},{15,3},{8,4},{9,5},{10,6},{11,7},{4,8},{5,9},... | collective-permute-start | bytes 1572872 | tf_op jit(solution)/shard_map/ppermute | solution.py:38
  43.8 3.7 %shard_map.149 = bf16[256,2048]{1,0:T(8,128)(2,1)} custom-call(s32[4]{0:T(128)S(1)} %copy-done.7, bf16[256,2048]{1,0:T(8,128)(2,1)S(1)} %copy-done.3, bf16[1024,1024]{1,0:T(8,128)(2,1)S(1)} %get-tuple-element.62.refs_1_.refs_2_, bf16[1024,1024]{1,0:T(8,128)(2,1)S(1)} %get-tuple-element.61.refs_2_.refs_1_.refs_3_), custom_call_target="tpu_custom_call" | custom-call | flops 1073741824 | bytes 6291456 | tf_op jit(solution)/shard_map/pallas_call | solution.py:160
  47.5 6.2 %shard_map.152 = bf16[512,2048]{1,0:T(8,128)(2,1)} custom-call(s32[4]{0:T(128)S(1)} %copy-done.7, bf16[256,2048]{1,0:T(8,128)(2,1)} %collective-permute-done.13.refs_0_.refs_5_.refs_11_, bf16[256,2048]{1,0:T(8,128)(2,1)} %collective-permute-done.14.refs_1_.refs_6_.refs_12_, bf16[1024,1024]{1,0:T(8,128)(2,1)S(1)} %get-tuple-element.62.refs_1_.refs_2_, ...), custom_call_target="tpu_custom_call" | custom-call | flops 2147483648 | bytes 8388608 | tf_op jit(solution)/shard_map/pallas_call | solution.py:160
  54.8 2.9 %shard_map.147.refs_0_.refs_6_ = bf16[256,2048]{1,0:T(8,128)(2,1)} custom-call(s32[4]{0:T(128)} %broadcast_select_fusion.3.slot_ref, bf16[64,2048]{1,0:T(8,128)(2,1)} %copy-done.11, bf16[64,2048]{1,0:T(8,128)(2,1)} %collective-permute-done.b_ref, bf16[128,2048]{1,0:T(8,128)(2,1)} %collective-permute-done.1.c_ref), custom_call_target="tpu_custom_call" | custom-call | bytes 2097152 | tf_op jit(solution)/shard_map/pallas_call | solution.py:92
  57.7 1.7 collective-permute-start.11
  59.8 2.5 collective-permute-start.12
  65.1 4.2 %shard_map.150 = (bf16[128,2048]{1,0:T(8,128)(2,1)S(1)}, bf16[128,2048]{1,0:T(8,128)(2,1)S(1)}) custom-call(s32[4]{0:T(128)S(1)} %copy-done.8, bf16[256,2048]{1,0:T(8,128)(2,1)S(1)} %copy-done.4, bf16[1024,1024]{1,0:T(8,128)(2,1)S(1)} %copy-done.1, bf16[1024,1024]{1,0:T(8,128)(2,1)S(1)} %get-tuple-element.61.refs_2_.refs_1_.refs_3_, ...), custom_call_target="tpu_custom_call" | custom-call | flops 1073741824 | bytes 6291456 | tf_op jit(solution)/shard_map/pallas_call | solution.py:160
  69.3 2.0 collective-permute-start.5
  71.3 11.9 %collective-permute-done.11.refs_0_.refs_1_.refs_7_ = bf16[256,2048]{1,0:T(8,128)(2,1)S(1)} collective-permute-done((bf16[256,2048]{1,0:T(8,128)(2,1)}, bf16[256,2048]{1,0:T(8,128)(2,1)S(1)}, u32[]{:S(2)}, u32[]{:S(2)}) %collective-permute-start.11) | collective-permute-done | bytes 1048608 | tf_op jit(solution)/shard_map/ppermute | solution.py:38
  83.2 2.3 collective-permute-start.22
  85.5 2.9 %shard_map.155 = bf16[256,2048]{1,0:T(8,128)(2,1)S(1)} custom-call(s32[4]{0:T(128)S(1)} %copy-done.7, bf16[256,2048]{1,0:T(8,128)(2,1)S(1)} %collective-permute-done.23.refs_0_.refs_7_.refs_13_, bf16[1024,1024]{1,0:T(8,128)(2,1)S(1)} %copy-done.1, bf16[1024,1024]{1,0:T(8,128)(2,1)S(1)} %get-tuple-element.61.refs_2_.refs_1_.refs_3_), custom_call_target="tpu_custom_call" | custom-call | flops 1073741824 | bytes 6291456 | tf_op jit(solution)/shard_map/pallas_call | solution.py:160
  88.6 4.1 %collective-permute-start.6 = (bf16[64,2048]{1,0:T(8,128)(2,1)S(1)}, bf16[64,2048]{1,0:T(8,128)(2,1)S(1)}, u32[]{:S(2)}, u32[]{:S(2)}) collective-permute-start(bf16[64,2048]{1,0:T(8,128)(2,1)S(1)} %fusion.26), channel_id=1, source_target_pairs={{96,0},{97,1},{98,2},{99,3},{100,4},{101,5},{102,6},{103,7},{104,8... | collective-permute-start | bytes 786440 | tf_op jit(solution)/shard_map/ppermute | solution.py:38
  92.7 5.3 %shard_map.153 = (bf16[256,2048]{1,0:T(8,128)(2,1)S(1)}, bf16[256,2048]{1,0:T(8,128)(2,1)S(1)}) custom-call(s32[4]{0:T(128)S(1)} %copy-done.8, bf16[256,2048]{1,0:T(8,128)(2,1)S(1)} %collective-permute-done.11.refs_0_.refs_1_.refs_7_, bf16[256,2048]{1,0:T(8,128)(2,1)S(1)} %collective-permute-done.12.refs_1_.refs_2_.refs_8_, ...), custom_call_target="tpu_custom_call" | custom-call | flops 2147483648 | bytes 8388608 | tf_op jit(solution)/shard_map/pallas_call | solution.py:160
  98.3 3.0 %shard_map.156 = (bf16[128,2048]{1,0:T(8,128)(2,1)S(1)}, bf16[128,2048]{1,0:T(8,128)(2,1)S(1)}) custom-call(s32[4]{0:T(128)S(1)} %copy-done.8, bf16[256,2048]{1,0:T(8,128)(2,1)S(1)} %collective-permute-done.22.refs_0_.refs_3_.refs_9_, bf16[1024,1024]{1,0:T(8,128)(2,1)S(1)} %copy-done.1, bf16[1024,1024]{1,0:T(8,128)(2,1)S(1)} %get-tuple-element.61.refs_2_.refs_1_.refs_3_, ...), custom_call_target="tpu_custom_call" | custom-call | flops 1073741824 | bytes 6291456 | tf_op jit(solution)/shard_map/pallas_call | solution.py:160
  101.3 2.0 collective-permute-start.25
  103.4 15.1 %collective-permute-done.25 = bf16[128,2048]{1,0:T(8,128)(2,1)S(1)} collective-permute-done((bf16[128,2048]{1,0:T(8,128)(2,1)S(1)}, bf16[128,2048]{1,0:T(8,128)(2,1)S(1)}, u32[]{:S(2)}, u32[]{:S(2)}) %collective-permute-start.25) | collective-permute-done | bytes 524320 | tf_op jit(solution)/shard_map/ppermute | solution.py:38
  119.1 3.5 %collective-permute-start.17 = (bf16[128,2048]{1,0:T(8,128)(2,1)S(1)}, bf16[128,2048]{1,0:T(8,128)(2,1)S(1)}, u32[]{:S(2)}, u32[]{:S(2)}) collective-permute-start(bf16[128,2048]{1,0:T(8,128)(2,1)S(1)} %bitcast.116), channel_id=1, source_target_pairs={{96,0},{97,1},{98,2},{99,3},{100,4},{101,5},{102,6},{103,7},{104,8... | collective-permute-start | bytes 1572872 | tf_op jit(solution)/shard_map/ppermute | solution.py:38
  122.5 3.7 %collective-permute-done.26 = bf16[64,2048]{1,0:T(8,128)(2,1)S(1)} collective-permute-done((bf16[64,2048]{1,0:T(8,128)(2,1)S(1)}, bf16[64,2048]{1,0:T(8,128)(2,1)S(1)}, u32[]{:S(2)}, u32[]{:S(2)}) %collective-permute-start.26) | collective-permute-done | bytes 262176 | tf_op jit(solution)/shard_map/ppermute | solution.py:38
  126.6 5.3 %collective-permute-done.17 = bf16[128,2048]{1,0:T(8,128)(2,1)S(1)} collective-permute-done((bf16[128,2048]{1,0:T(8,128)(2,1)S(1)}, bf16[128,2048]{1,0:T(8,128)(2,1)S(1)}, u32[]{:S(2)}, u32[]{:S(2)}) %collective-permute-start.17) | collective-permute-done | bytes 524320 | tf_op jit(solution)/shard_map/ppermute | solution.py:38
  133.6 2.3 collective-permute-start.7
  136.0 12.5 %collective-permute-done.18 = bf16[128,2048]{1,0:T(8,128)(2,1)S(1)} collective-permute-done((bf16[128,2048]{1,0:T(8,128)(2,1)S(1)}, bf16[128,2048]{1,0:T(8,128)(2,1)S(1)}, u32[]{:S(2)}, u32[]{:S(2)}) %collective-permute-start.18) | collective-permute-done | bytes 524320 | tf_op jit(solution)/shard_map/ppermute | solution.py:38
  148.7 5.4 %collective-permute-done.7 = bf16[64,2048]{1,0:T(8,128)(2,1)S(1)} collective-permute-done((bf16[64,2048]{1,0:T(8,128)(2,1)S(1)}, bf16[64,2048]{1,0:T(8,128)(2,1)S(1)}, u32[]{:S(2)}, u32[]{:S(2)}) %collective-permute-start.7) | collective-permute-done | bytes 262176 | tf_op jit(solution)/shard_map/ppermute | solution.py:38
  154.3 2.9 %shard_map.157 = (bf16[128,2048]{1,0:T(8,128)(2,1)S(1)}, bf16[128,2048]{1,0:T(8,128)(2,1)S(1)}) custom-call(s32[4]{0:T(128)S(1)} %copy-done.8, bf16[256,2048]{1,0:T(8,128)(2,1)S(1)} %bitcast.76, bf16[1024,1024]{1,0:T(8,128)(2,1)S(1)} %get-tuple-element.61.refs_2_.refs_1_.refs_3_, bf16[1024,1024]{1,0:T(8,128)(2,1)S(1)} %copy-done.1), custom_call_target="tpu_custom_call" | custom-call | flops 1073741824 | bytes 6291456 | tf_op jit(solution)/shard_map/pallas_call | solution.py:160
  157.3 11.7 %collective-permute-done.8 = bf16[128,2048]{1,0:T(8,128)(2,1)S(1)} collective-permute-done((bf16[128,2048]{1,0:T(8,128)(2,1)S(1)}, bf16[128,2048]{1,0:T(8,128)(2,1)S(1)}, u32[]{:S(2)}, u32[]{:S(2)}) %collective-permute-start.8) | collective-permute-done | bytes 524320 | tf_op jit(solution)/shard_map/ppermute | solution.py:38
  169.3 2.9 %shard_map.151 = (bf16[128,2048]{1,0:T(8,128)(2,1)S(1)}, bf16[128,2048]{1,0:T(8,128)(2,1)S(1)}) custom-call(s32[4]{0:T(128)S(1)} %copy-done.8, bf16[256,2048]{1,0:T(8,128)(2,1)S(1)} %bitcast.81, bf16[1024,1024]{1,0:T(8,128)(2,1)S(1)} %get-tuple-element.61.refs_2_.refs_1_.refs_3_, bf16[1024,1024]{1,0:T(8,128)(2,1)S(1)} %copy-done.1), custom_call_target="tpu_custom_call" | custom-call | flops 1073741824 | bytes 6291456 | tf_op jit(solution)/shard_map/pallas_call | solution.py:160
  172.2 2.6 %collective-permute-start.39 = (bf16[256,2048]{1,0:T(8,128)(2,1)S(1)}, bf16[256,2048]{1,0:T(8,128)(2,1)S(1)}, u32[]{:S(2)}, u32[]{:S(2)}) collective-permute-start(bf16[256,2048]{1,0:T(8,128)(2,1)S(1)} %bitcast.77), channel_id=1, source_target_pairs={{16,0},{17,1},{18,2},{19,3},{20,4},{21,5},{22,6},{23,7},{24,8},{25... | collective-permute-start | bytes 3145736 | tf_op jit(solution)/shard_map/ppermute | solution.py:38
  175.8 4.1 %shard_map.154 = (bf16[256,2048]{1,0:T(8,128)(2,1)S(1)}, bf16[256,2048]{1,0:T(8,128)(2,1)S(1)}) custom-call(s32[4]{0:T(128)S(1)} %copy-done.8, bf16[512,2048]{1,0:T(8,128)(2,1)S(1)} %bitcast.73, bf16[1024,1024]{1,0:T(8,128)(2,1)S(1)} %get-tuple-element.61.refs_2_.refs_1_.refs_3_, bf16[1024,1024]{1,0:T(8,128)(2,1)S(1)} %copy-done.1), custom_call_target="tpu_custom_call" | custom-call | flops 2147483648 | bytes 8388608 | tf_op jit(solution)/shard_map/pallas_call | solution.py:160
  179.9 2.7 %collective-permute-done.9 = bf16[128,2048]{1,0:T(8,128)(2,1)S(1)} collective-permute-done((bf16[128,2048]{1,0:T(8,128)(2,1)S(1)}, bf16[128,2048]{1,0:T(8,128)(2,1)S(1)}, u32[]{:S(2)}, u32[]{:S(2)}) %collective-permute-start.9) | collective-permute-done | bytes 524320 | tf_op jit(solution)/shard_map/ppermute | solution.py:38
  182.8 2.9 %shard_map.158 = (bf16[128,2048]{1,0:T(8,128)(2,1)S(1)}, bf16[128,2048]{1,0:T(8,128)(2,1)S(1)}) custom-call(s32[4]{0:T(128)S(1)} %copy-done.7, bf16[256,2048]{1,0:T(8,128)(2,1)S(1)} %collective-permute-done.33.refs_0_.refs_11_.refs_3_, bf16[1024,1024]{1,0:T(8,128)(2,1)S(1)} %get-tuple-element.61.refs_2_.refs_1_.refs_3_, bf16[1024,1024]{1,0:T(8,128)(2,1)S(1)} %copy-done.1), custom_call_target="tpu_custom_call" | custom-call | flops 1073741824 | bytes 6291456 | tf_op jit(solution)/shard_map/pallas_call | solution.py:160
  186.7 2.9 %shard_map.160 = (bf16[128,2048]{1,0:T(8,128)(2,1)S(1)}, bf16[128,2048]{1,0:T(8,128)(2,1)S(1)}) custom-call(s32[4]{0:T(128)S(1)} %copy-done.7, bf16[256,2048]{1,0:T(8,128)(2,1)S(1)} %collective-permute-done.39.refs_0_.refs_13_.refs_5_, bf16[1024,1024]{1,0:T(8,128)(2,1)S(1)} %get-tuple-element.61.refs_2_.refs_1_.refs_3_, bf16[1024,1024]{1,0:T(8,128)(2,1)S(1)} %copy-done.1), custom_call_target="tpu_custom_call" | custom-call | flops 1073741824 | bytes 6291456 | tf_op jit(solution)/shard_map/pallas_call | solution.py:160
  190.9 7.7 %collective-permute-done.20 = bf16[256,2048]{1,0:T(8,128)(2,1)S(1)} collective-permute-done((bf16[256,2048]{1,0:T(8,128)(2,1)S(1)}, bf16[256,2048]{1,0:T(8,128)(2,1)S(1)}, u32[]{:S(2)}, u32[]{:S(2)}) %collective-permute-start.20) | collective-permute-done | bytes 1048608 | tf_op jit(solution)/shard_map/ppermute | solution.py:38
  199.3 4.1 %shard_map.159 = (bf16[256,2048]{1,0:T(8,128)(2,1)S(1)}, bf16[256,2048]{1,0:T(8,128)(2,1)S(1)}) custom-call(s32[4]{0:T(128)S(1)} %copy-done.7, bf16[512,2048]{1,0:T(8,128)(2,1)S(1)} %collective-permute-done.36.refs_0_.refs_12_.refs_4_, bf16[1024,1024]{1,0:T(8,128)(2,1)S(1)} %get-tuple-element.61.refs_2_.refs_1_.refs_3_, bf16[1024,1024]{1,0:T(8,128)(2,1)S(1)} %copy-done.1), custom_call_target="tpu_custom_call" | custom-call | flops 2147483648 | bytes 8388608 | tf_op jit(solution)/shard_map/pallas_call | solution.py:160
  203.9 3.2 %collective-permute-start.41 = (bf16[64,2048]{1,0:T(8,128)(2,1)S(1)}, bf16[64,2048]{1,0:T(8,128)(2,1)S(1)}, u32[]{:S(2)}, u32[]{:S(2)}) collective-permute-start(bf16[64,2048]{1,0:T(8,128)(2,1)S(1)} %fusion.31), channel_id=1, source_target_pairs={{1,0},{0,1},{3,2},{2,3},{5,4},{4,5},{7,6},{6,7},{9,8},{8,9},{11,10... | collective-permute-start | bytes 786440 | tf_op jit(solution)/shard_map/ppermute | solution.py:38
  207.0 6.7 %collective-permute-done.21 = bf16[128,2048]{1,0:T(8,128)(2,1)S(1)} collective-permute-done((bf16[128,2048]{1,0:T(8,128)(2,1)S(1)}, bf16[128,2048]{1,0:T(8,128)(2,1)S(1)}, u32[]{:S(2)}, u32[]{:S(2)}) %collective-permute-start.21) | collective-permute-done | bytes 524320 | tf_op jit(solution)/shard_map/ppermute | solution.py:38
  214.0 4.3 %collective-permute-done.37 = bf16[256,2048]{1,0:T(8,128)(2,1)S(1)} collective-permute-done((bf16[256,2048]{1,0:T(8,128)(2,1)S(1)}, bf16[256,2048]{1,0:T(8,128)(2,1)S(1)}, u32[]{:S(2)}, u32[]{:S(2)}) %collective-permute-start.37) | collective-permute-done | bytes 1048608 | tf_op jit(solution)/shard_map/ppermute | solution.py:38
  218.7 3.6 %collective-permute-start.38 = (bf16[128,2048]{1,0:T(8,128)(2,1)S(1)}, bf16[128,2048]{1,0:T(8,128)(2,1)S(1)}, u32[]{:S(2)}, u32[]{:S(2)}) collective-permute-start(bf16[128,2048]{1,0:T(8,128)(2,1)S(1)} %bitcast.114), channel_id=1, source_target_pairs={{1,0},{0,1},{3,2},{2,3},{5,4},{4,5},{7,6},{6,7},{9,8},{8,9},{11,10... | collective-permute-start | bytes 1572872 | tf_op jit(solution)/shard_map/ppermute | solution.py:38
  224.0 5.4 %collective-permute-done.38 = bf16[128,2048]{1,0:T(8,128)(2,1)S(1)} collective-permute-done((bf16[128,2048]{1,0:T(8,128)(2,1)S(1)}, bf16[128,2048]{1,0:T(8,128)(2,1)S(1)}, u32[]{:S(2)}, u32[]{:S(2)}) %collective-permute-start.38) | collective-permute-done | bytes 524320 | tf_op jit(solution)/shard_map/ppermute | solution.py:38
  229.7 2.5 collective-permute-start.42
  232.2 2.1 collective-permute-start.32
  234.3 8.6 %shard_map.162 = f32[1024,1024]{1,0:T(8,128)} custom-call(bf16[256,2048]{1,0:T(8,128)(2,1)S(1)} %bitcast.82, bf16[512,2048]{1,0:T(8,128)(2,1)} %bitcast.74, bf16[256,2048]{1,0:T(8,128)(2,1)S(1)} %bitcast.78, bf16[256,2048]{1,0:T(8,128)(2,1)S(1)} %collective-permute-done.33.refs_0_.refs_11_.refs_3_, bf16[512,2048]{1,0:T(8,128)(2,1)} %copy-done.6, ...), custom_call_target="tpu_custom_call" | custom-call | flops 4294967296 | bytes 12582912 | tf_op jit(solution)/shard_map/pallas_call | solution.py:197
  243.1 2.4 collective-permute-start.43
  245.6 8.2 %shard_map.161 = f32[1024,1024]{1,0:T(8,128)} custom-call(bf16[256,2048]{1,0:T(8,128)(2,1)S(1)} %copy-done.5, bf16[256,2048]{1,0:T(8,128)(2,1)S(1)} %collective-permute-done.11.refs_0_.refs_1_.refs_7_, bf16[256,2048]{1,0:T(8,128)(2,1)S(1)} %collective-permute-done.12.refs_1_.refs_2_.refs_8_, ...), custom_call_target="tpu_custom_call" | custom-call | flops 4294967296 | bytes 12582912 | tf_op jit(solution)/shard_map/pallas_call | solution.py:197
  (143 shorter events, 28.0 us)
Async XLA Ops:
  2.7 37.3 %copy-start.11 = (bf16[64,2048]{1,0:T(8,128)(2,1)}, bf16[64,2048]{1,0:T(8,128)(2,1)S(1)}, u32[]{:S(2)}) copy-start(bf16[64,2048]{1,0:T(8,128)(2,1)S(1)} %get-tuple-element.58.a_ref) | copy-start | bytes 786436
  2.7 6.5 %collective-permute-start.2 = (bf16[64,2048]{1,0:T(8,128)(2,1)S(1)}, bf16[64,2048]{1,0:T(8,128)(2,1)S(1)}, u32[]{:S(2)}, u32[]{:S(2)}) collective-permute-start(bf16[64,2048]{1,0:T(8,128)(2,1)S(1)} %get-tuple-element.57.a_ref), channel_id=1, source_target_pairs={{1,0},{0,1},{3,2},{2,3},{5,4},{4,5},{7,6},{6,7},{9,8},{8,9},{11,10... | collective-permute-start | bytes 786440 | tf_op jit(solution)/shard_map/ppermute | solution.py:38
  9.2 9.3 %collective-permute-start.3 = (bf16[128,2048]{1,0:T(8,128)(2,1)S(1)}, bf16[128,2048]{1,0:T(8,128)(2,1)S(1)}, u32[]{:S(2)}, u32[]{:S(2)}) collective-permute-start(bf16[128,2048]{1,0:T(8,128)(2,1)S(1)} %pad_maximum_fusion.4), channel_id=1, source_target_pairs={{3,0},{2,1},{1,2},{0,3},{7,4},{6,5},{5,6},{4,7},{11,8},{10,9},{9,1... | collective-permute-start | bytes 1572872 | tf_op jit(solution)/shard_map/ppermute | solution.py:38
  22.1 25.5 %collective-permute-start.14 = (bf16[256,2048]{1,0:T(8,128)(2,1)}, bf16[256,2048]{1,0:T(8,128)(2,1)}, u32[]{:S(2)}, u32[]{:S(2)}) collective-permute-start(bf16[256,2048]{1,0:T(8,128)(2,1)} %shard_map.148.refs_0_.refs_4_.refs_10_), channel_id=1, source_target_pairs={{4,0},{5,1},{6,2},{7,3},{0,4},{1,5},{2,6},{3,7},{12,8},{13,9},{14,... | collective-permute-start | bytes 3145736 | tf_op jit(solution)/shard_map/ppermute | solution.py:38
  23.5 24.0 %collective-permute-start.13 = (bf16[256,2048]{1,0:T(8,128)(2,1)}, bf16[256,2048]{1,0:T(8,128)(2,1)}, u32[]{:S(2)}, u32[]{:S(2)}) collective-permute-start(bf16[256,2048]{1,0:T(8,128)(2,1)} %shard_map.148.refs_0_.refs_4_.refs_10_), channel_id=1, source_target_pairs={{12,0},{13,1},{14,2},{15,3},{8,4},{9,5},{10,6},{11,7},{4,8},{5,9},... | collective-permute-start | bytes 3145736 | tf_op jit(solution)/shard_map/ppermute | solution.py:38
  25.6 14.3 %collective-permute-start = (bf16[64,2048]{1,0:T(8,128)(2,1)S(1)}, bf16[64,2048]{1,0:T(8,128)(2,1)}, u32[]{:S(2)}, u32[]{:S(2)}) collective-permute-start(bf16[64,2048]{1,0:T(8,128)(2,1)S(1)} %get-tuple-element.58.a_ref), channel_id=1, source_target_pairs={{4,0},{5,1},{6,2},{7,3},{0,4},{1,5},{2,6},{3,7},{12,8},{13,9},{14,... | collective-permute-start | bytes 786440 | tf_op jit(solution)/shard_map/ppermute | solution.py:38
  27.5 16.3 %copy-start.3 = (bf16[256,2048]{1,0:T(8,128)(2,1)S(1)}, bf16[256,2048]{1,0:T(8,128)(2,1)}, u32[]{:S(2)}) copy-start(bf16[256,2048]{1,0:T(8,128)(2,1)} %shard_map.148.refs_0_.refs_4_.refs_10_) | copy-start | bytes 3145732
  27.5 16.3 %copy-start.7 = (s32[4]{0:T(128)S(1)}, s32[4]{0:T(128)}, u32[]{:S(2)}) copy-start(s32[4]{0:T(128)} %broadcast_select_fusion.2.slot_ref) | copy-start | bytes 52
  30.3 17.3 %copy-start = (bf16[1024,1024]{1,0:T(8,128)(2,1)}, bf16[1024,1024]{1,0:T(8,128)(2,1)S(1)}, u32[]{:S(2)}) copy-start(bf16[1024,1024]{1,0:T(8,128)(2,1)S(1)} %get-tuple-element.62.refs_1_.refs_2_) | copy-start | bytes 6291460
  41.0 13.8 %collective-permute-start.1 = (bf16[128,2048]{1,0:T(8,128)(2,1)S(1)}, bf16[128,2048]{1,0:T(8,128)(2,1)}, u32[]{:S(2)}, u32[]{:S(2)}) collective-permute-start(bf16[128,2048]{1,0:T(8,128)(2,1)S(1)} %pad_maximum_fusion.3), channel_id=1, source_target_pairs={{12,0},{13,1},{14,2},{15,3},{8,4},{9,5},{10,6},{11,7},{4,8},{5,9},... | collective-permute-start | bytes 1572872 | tf_op jit(solution)/shard_map/ppermute | solution.py:38
  47.5 14.8 %collective-permute-start.4 = (bf16[256,2048]{1,0:T(8,128)(2,1)}, bf16[256,2048]{1,0:T(8,128)(2,1)}, u32[]{:S(2)}, u32[]{:S(2)}) collective-permute-start(bf16[256,2048]{1,0:T(8,128)(2,1)} %shard_map.149), channel_id=1, source_target_pairs={{16,0},{17,1},{18,2},{19,3},{20,4},{21,5},{22,6},{23,7},{24,8},{25... | collective-permute-start | bytes 3145736 | tf_op jit(solution)/shard_map/ppermute | solution.py:38
  53.8 38.9 %collective-permute-start.15 = (bf16[512,2048]{1,0:T(8,128)(2,1)}, bf16[512,2048]{1,0:T(8,128)(2,1)}, u32[]{:S(2)}, u32[]{:S(2)}) collective-permute-start(bf16[512,2048]{1,0:T(8,128)(2,1)} %shard_map.152), channel_id=1, source_target_pairs={{16,0},{17,1},{18,2},{19,3},{20,4},{21,5},{22,6},{23,7},{24,8},{25... | collective-permute-start | bytes 6291464 | tf_op jit(solution)/shard_map/ppermute | solution.py:38
  57.7 25.5 %collective-permute-start.11 = (bf16[256,2048]{1,0:T(8,128)(2,1)}, bf16[256,2048]{1,0:T(8,128)(2,1)S(1)}, u32[]{:S(2)}, u32[]{:S(2)}) collective-permute-start(bf16[256,2048]{1,0:T(8,128)(2,1)} %shard_map.147.refs_0_.refs_6_), channel_id=1, source_target_pairs={{1,0},{0,1},{3,2},{2,3},{5,4},{4,5},{7,6},{6,7},{9,8},{8,9},{11,10... | collective-permute-start | bytes 3145736 | tf_op jit(solution)/shard_map/ppermute | solution.py:38
  59.4 26.2 %collective-permute-start.23 = (bf16[256,2048]{1,0:T(8,128)(2,1)}, bf16[256,2048]{1,0:T(8,128)(2,1)S(1)}, u32[]{:S(2)}, u32[]{:S(2)}) collective-permute-start(bf16[256,2048]{1,0:T(8,128)(2,1)} %collective-permute-done.14.refs_1_.refs_6_.refs_12_), channel_id=1, source_target_pairs={{12,0},{13,1},{14,2},{15,3},{8,4},{9,5},{10,6},{11,7},{4,8},{5,9},... | collective-permute-start | bytes 3145736 | tf_op jit(solution)/shard_map/ppermute | solution.py:38
  59.8 32.9 %collective-permute-start.12 = (bf16[256,2048]{1,0:T(8,128)(2,1)}, bf16[256,2048]{1,0:T(8,128)(2,1)S(1)}, u32[]{:S(2)}, u32[]{:S(2)}) collective-permute-start(bf16[256,2048]{1,0:T(8,128)(2,1)} %shard_map.147.refs_0_.refs_6_), channel_id=1, source_target_pairs={{3,0},{2,1},{1,2},{0,3},{7,4},{6,5},{5,6},{4,7},{11,8},{10,9},{9,1... | collective-permute-start | bytes 3145736 | tf_op jit(solution)/shard_map/ppermute | solution.py:38
  69.3 19.2 %collective-permute-start.5 = (bf16[128,2048]{1,0:T(8,128)(2,1)S(1)}, bf16[128,2048]{1,0:T(8,128)(2,1)S(1)}, u32[]{:S(2)}, u32[]{:S(2)}) collective-permute-start(bf16[128,2048]{1,0:T(8,128)(2,1)S(1)} %get-tuple-element.23), channel_id=1, source_target_pairs={{32,0},{33,1},{34,2},{35,3},{36,4},{37,5},{38,6},{39,7},{40,8},{41... | collective-permute-start | bytes 1572872 | tf_op jit(solution)/shard_map/ppermute | solution.py:38
  83.2 15.1 %collective-permute-start.22 = (bf16[256,2048]{1,0:T(8,128)(2,1)S(1)}, bf16[256,2048]{1,0:T(8,128)(2,1)S(1)}, u32[]{:S(2)}, u32[]{:S(2)}) collective-permute-start(bf16[256,2048]{1,0:T(8,128)(2,1)S(1)} %collective-permute-done.11.refs_0_.refs_1_.refs_7_), channel_id=1, source_target_pairs={{3,0},{2,1},{1,2},{0,3},{7,4},{6,5},{5,6},{4,7},{11,8},{10,9},{9,1... | collective-permute-start | bytes 3145736 | tf_op jit(solution)/shard_map/ppermute | solution.py:38
  88.4 9.9 %collective-permute-start.24 = (bf16[256,2048]{1,0:T(8,128)(2,1)S(1)}, bf16[256,2048]{1,0:T(8,128)(2,1)S(1)}, u32[]{:S(2)}, u32[]{:S(2)}) collective-permute-start(bf16[256,2048]{1,0:T(8,128)(2,1)S(1)} %shard_map.155), channel_id=1, source_target_pairs={{16,0},{17,1},{18,2},{19,3},{20,4},{21,5},{22,6},{23,7},{24,8},{25... | collective-permute-start | bytes 3145736 | tf_op jit(solution)/shard_map/ppermute | solution.py:38
  88.6 14.7 %collective-permute-start.6 = (bf16[64,2048]{1,0:T(8,128)(2,1)S(1)}, bf16[64,2048]{1,0:T(8,128)(2,1)S(1)}, u32[]{:S(2)}, u32[]{:S(2)}) collective-permute-start(bf16[64,2048]{1,0:T(8,128)(2,1)S(1)} %fusion.26), channel_id=1, source_target_pairs={{96,0},{97,1},{98,2},{99,3},{100,4},{101,5},{102,6},{103,7},{104,8... | collective-permute-start | bytes 786440 | tf_op jit(solution)/shard_map/ppermute | solution.py:38
  98.0 20.7 %collective-permute-start.16 = (bf16[256,2048]{1,0:T(8,128)(2,1)S(1)}, bf16[256,2048]{1,0:T(8,128)(2,1)S(1)}, u32[]{:S(2)}, u32[]{:S(2)}) collective-permute-start(bf16[256,2048]{1,0:T(8,128)(2,1)S(1)} %get-tuple-element.27), channel_id=1, source_target_pairs={{32,0},{33,1},{34,2},{35,3},{36,4},{37,5},{38,6},{39,7},{40,8},{41... | collective-permute-start | bytes 3145736 | tf_op jit(solution)/shard_map/ppermute | solution.py:38
  101.3 17.2 %collective-permute-start.25 = (bf16[128,2048]{1,0:T(8,128)(2,1)S(1)}, bf16[128,2048]{1,0:T(8,128)(2,1)S(1)}, u32[]{:S(2)}, u32[]{:S(2)}) collective-permute-start(bf16[128,2048]{1,0:T(8,128)(2,1)S(1)} %get-tuple-element.31), channel_id=1, source_target_pairs={{32,0},{33,1},{34,2},{35,3},{36,4},{37,5},{38,6},{39,7},{40,8},{41... | collective-permute-start | bytes 1572872 | tf_op jit(solution)/shard_map/ppermute | solution.py:38
  118.6 7.7 %collective-permute-start.26 = (bf16[64,2048]{1,0:T(8,128)(2,1)S(1)}, bf16[64,2048]{1,0:T(8,128)(2,1)S(1)}, u32[]{:S(2)}, u32[]{:S(2)}) collective-permute-start(bf16[64,2048]{1,0:T(8,128)(2,1)S(1)} %fusion.28), channel_id=1, source_target_pairs={{96,0},{97,1},{98,2},{99,3},{100,4},{101,5},{102,6},{103,7},{104,8... | collective-permute-start | bytes 786440 | tf_op jit(solution)/shard_map/ppermute | solution.py:38
  119.1 12.8 %collective-permute-start.17 = (bf16[128,2048]{1,0:T(8,128)(2,1)S(1)}, bf16[128,2048]{1,0:T(8,128)(2,1)S(1)}, u32[]{:S(2)}, u32[]{:S(2)}) collective-permute-start(bf16[128,2048]{1,0:T(8,128)(2,1)S(1)} %bitcast.116), channel_id=1, source_target_pairs={{96,0},{97,1},{98,2},{99,3},{100,4},{101,5},{102,6},{103,7},{104,8... | collective-permute-start | bytes 1572872 | tf_op jit(solution)/shard_map/ppermute | solution.py:38
  126.5 9.4 %collective-permute-start.27 = (bf16[64,2048]{1,0:T(8,128)(2,1)S(1)}, bf16[64,2048]{1,0:T(8,128)(2,1)S(1)}, u32[]{:S(2)}, u32[]{:S(2)}) collective-permute-start(bf16[64,2048]{1,0:T(8,128)(2,1)S(1)} %pad_maximum_fusion.12), channel_id=1, source_target_pairs={{96,0},{97,1},{98,2},{99,3},{100,4},{101,5},{102,6},{103,7},{104,8... | collective-permute-start | bytes 786440 | tf_op jit(solution)/shard_map/ppermute | solution.py:38
  132.3 16.2 %collective-permute-start.18 = (bf16[128,2048]{1,0:T(8,128)(2,1)S(1)}, bf16[128,2048]{1,0:T(8,128)(2,1)S(1)}, u32[]{:S(2)}, u32[]{:S(2)}) collective-permute-start(bf16[128,2048]{1,0:T(8,128)(2,1)S(1)} %pad_maximum_fusion.6), channel_id=1, source_target_pairs={{96,0},{97,1},{98,2},{99,3},{100,4},{101,5},{102,6},{103,7},{104,8... | collective-permute-start | bytes 1572872 | tf_op jit(solution)/shard_map/ppermute | solution.py:38
  133.6 20.5 %collective-permute-start.7 = (bf16[64,2048]{1,0:T(8,128)(2,1)S(1)}, bf16[64,2048]{1,0:T(8,128)(2,1)S(1)}, u32[]{:S(2)}, u32[]{:S(2)}) collective-permute-start(bf16[64,2048]{1,0:T(8,128)(2,1)S(1)} %pad_maximum_fusion.11), channel_id=1, source_target_pairs={{96,0},{97,1},{98,2},{99,3},{100,4},{101,5},{102,6},{103,7},{104,8... | collective-permute-start | bytes 786440 | tf_op jit(solution)/shard_map/ppermute | solution.py:38
  135.9 18.3 %collective-permute-start.28 = (bf16[128,2048]{1,0:T(8,128)(2,1)S(1)}, bf16[128,2048]{1,0:T(8,128)(2,1)S(1)}, u32[]{:S(2)}, u32[]{:S(2)}) collective-permute-start(bf16[128,2048]{1,0:T(8,128)(2,1)S(1)} %pad_maximum_fusion.7), channel_id=1, source_target_pairs={{32,0},{33,1},{34,2},{35,3},{36,4},{37,5},{38,6},{39,7},{40,8},{41... | collective-permute-start | bytes 1572872 | tf_op jit(solution)/shard_map/ppermute | solution.py:38
  148.6 26.2 %collective-permute-start.19 = (bf16[256,2048]{1,0:T(8,128)(2,1)S(1)}, bf16[256,2048]{1,0:T(8,128)(2,1)S(1)}, u32[]{:S(2)}, u32[]{:S(2)}) collective-permute-start(bf16[256,2048]{1,0:T(8,128)(2,1)S(1)} %pad_maximum_fusion.1), channel_id=1, source_target_pairs={{32,0},{33,1},{34,2},{35,3},{36,4},{37,5},{38,6},{39,7},{40,8},{41... | collective-permute-start | bytes 3145736 | tf_op jit(solution)/shard_map/ppermute | solution.py:38
  154.1 14.9 %collective-permute-start.8 = (bf16[128,2048]{1,0:T(8,128)(2,1)S(1)}, bf16[128,2048]{1,0:T(8,128)(2,1)S(1)}, u32[]{:S(2)}, u32[]{:S(2)}) collective-permute-start(bf16[128,2048]{1,0:T(8,128)(2,1)S(1)} %pad_maximum_fusion.5), channel_id=1, source_target_pairs={{32,0},{33,1},{34,2},{35,3},{36,4},{37,5},{38,6},{39,7},{40,8},{41... | collective-permute-start | bytes 1572872 | tf_op jit(solution)/shard_map/ppermute | solution.py:38
  157.2 18.1 %collective-permute-start.29 = (bf16[128,2048]{1,0:T(8,128)(2,1)S(1)}, bf16[128,2048]{1,0:T(8,128)(2,1)S(1)}, u32[]{:S(2)}, u32[]{:S(2)}) collective-permute-start(bf16[128,2048]{1,0:T(8,128)(2,1)S(1)} %get-tuple-element.33), channel_id=1, source_target_pairs={{12,0},{13,1},{14,2},{15,3},{8,4},{9,5},{10,6},{11,7},{4,8},{5,9},... | collective-permute-start | bytes 1572872 | tf_op jit(solution)/shard_map/ppermute | solution.py:38
  169.2 13.5 %collective-permute-start.33 = (bf16[256,2048]{1,0:T(8,128)(2,1)S(1)}, bf16[256,2048]{1,0:T(8,128)(2,1)S(1)}, u32[]{:S(2)}, u32[]{:S(2)}) collective-permute-start(bf16[256,2048]{1,0:T(8,128)(2,1)S(1)} %bitcast.80), channel_id=1, source_target_pairs={{16,0},{17,1},{18,2},{19,3},{20,4},{21,5},{22,6},{23,7},{24,8},{25... | collective-permute-start | bytes 3145736 | tf_op jit(solution)/shard_map/ppermute | solution.py:38
  172.2 10.5 %collective-permute-start.9 = (bf16[128,2048]{1,0:T(8,128)(2,1)S(1)}, bf16[128,2048]{1,0:T(8,128)(2,1)S(1)}, u32[]{:S(2)}, u32[]{:S(2)}) collective-permute-start(bf16[128,2048]{1,0:T(8,128)(2,1)S(1)} %get-tuple-element.25), channel_id=1, source_target_pairs={{12,0},{13,1},{14,2},{15,3},{8,4},{9,5},{10,6},{11,7},{4,8},{5,9},... | collective-permute-start | bytes 1572872 | tf_op jit(solution)/shard_map/ppermute | solution.py:38
  172.2 14.5 %collective-permute-start.39 = (bf16[256,2048]{1,0:T(8,128)(2,1)S(1)}, bf16[256,2048]{1,0:T(8,128)(2,1)S(1)}, u32[]{:S(2)}, u32[]{:S(2)}) collective-permute-start(bf16[256,2048]{1,0:T(8,128)(2,1)S(1)} %bitcast.77), channel_id=1, source_target_pairs={{16,0},{17,1},{18,2},{19,3},{20,4},{21,5},{22,6},{23,7},{24,8},{25... | collective-permute-start | bytes 3145736 | tf_op jit(solution)/shard_map/ppermute | solution.py:38
  175.2 24.1 %collective-permute-start.36 = (bf16[512,2048]{1,0:T(8,128)(2,1)S(1)}, bf16[512,2048]{1,0:T(8,128)(2,1)S(1)}, u32[]{:S(2)}, u32[]{:S(2)}) collective-permute-start(bf16[512,2048]{1,0:T(8,128)(2,1)S(1)} %bitcast.72), channel_id=1, source_target_pairs={{16,0},{17,1},{18,2},{19,3},{20,4},{21,5},{22,6},{23,7},{24,8},{25... | collective-permute-start | bytes 6291464 | tf_op jit(solution)/shard_map/ppermute | solution.py:38
  175.4 10.3 %collective-permute-start.30 = (bf16[64,2048]{1,0:T(8,128)(2,1)S(1)}, bf16[64,2048]{1,0:T(8,128)(2,1)S(1)}, u32[]{:S(2)}, u32[]{:S(2)}) collective-permute-start(bf16[64,2048]{1,0:T(8,128)(2,1)S(1)} %fusion.29), channel_id=1, source_target_pairs={{4,0},{5,1},{6,2},{7,3},{0,4},{1,5},{2,6},{3,7},{12,8},{13,9},{14,... | collective-permute-start | bytes 786440 | tf_op jit(solution)/shard_map/ppermute | solution.py:38
  182.6 16.0 %collective-permute-start.20 = (bf16[256,2048]{1,0:T(8,128)(2,1)S(1)}, bf16[256,2048]{1,0:T(8,128)(2,1)S(1)}, u32[]{:S(2)}, u32[]{:S(2)}) collective-permute-start(bf16[256,2048]{1,0:T(8,128)(2,1)S(1)} %get-tuple-element.29), channel_id=1, source_target_pairs={{12,0},{13,1},{14,2},{15,3},{8,4},{9,5},{10,6},{11,7},{4,8},{5,9},... | collective-permute-start | bytes 3145736 | tf_op jit(solution)/shard_map/ppermute | solution.py:38
  182.7 71.1 %collective-permute-start.10 = (bf16[64,2048]{1,0:T(8,128)(2,1)S(1)}, bf16[64,2048]{1,0:T(8,128)(2,1)S(1)}, u32[]{:S(2)}, u32[]{:S(2)}) collective-permute-start(bf16[64,2048]{1,0:T(8,128)(2,1)S(1)} %fusion.27), channel_id=1, source_target_pairs={{4,0},{5,1},{6,2},{7,3},{0,4},{1,5},{2,6},{3,7},{12,8},{13,9},{14,... | collective-permute-start | bytes 786440 | tf_op jit(solution)/shard_map/ppermute | solution.py:38
  185.7 36.6 %collective-permute-start.34 = (bf16[128,2048]{1,0:T(8,128)(2,1)S(1)}, bf16[128,2048]{1,0:T(8,128)(2,1)S(1)}, u32[]{:S(2)}, u32[]{:S(2)}) collective-permute-start(bf16[128,2048]{1,0:T(8,128)(2,1)S(1)} %get-tuple-element.35), channel_id=1, source_target_pairs={{3,0},{2,1},{1,2},{0,3},{7,4},{6,5},{5,6},{4,7},{11,8},{10,9},{9,1... | collective-permute-start | bytes 1572872 | tf_op jit(solution)/shard_map/ppermute | solution.py:38
  189.6 14.2 %collective-permute-start.40 = (bf16[128,2048]{1,0:T(8,128)(2,1)S(1)}, bf16[128,2048]{1,0:T(8,128)(2,1)S(1)}, u32[]{:S(2)}, u32[]{:S(2)}) collective-permute-start(bf16[128,2048]{1,0:T(8,128)(2,1)S(1)} %get-tuple-element.39), channel_id=1, source_target_pairs={{3,0},{2,1},{1,2},{0,3},{7,4},{6,5},{5,6},{4,7},{11,8},{10,9},{9,1... | collective-permute-start | bytes 1572872 | tf_op jit(solution)/shard_map/ppermute | solution.py:38
  199.0 14.8 %collective-permute-start.21 = (bf16[128,2048]{1,0:T(8,128)(2,1)S(1)}, bf16[128,2048]{1,0:T(8,128)(2,1)S(1)}, u32[]{:S(2)}, u32[]{:S(2)}) collective-permute-start(bf16[128,2048]{1,0:T(8,128)(2,1)S(1)} %bitcast.115), channel_id=1, source_target_pairs={{4,0},{5,1},{6,2},{7,3},{0,4},{1,5},{2,6},{3,7},{12,8},{13,9},{14,... | collective-permute-start | bytes 1572872 | tf_op jit(solution)/shard_map/ppermute | solution.py:38
  203.4 14.9 %collective-permute-start.37 = (bf16[256,2048]{1,0:T(8,128)(2,1)S(1)}, bf16[256,2048]{1,0:T(8,128)(2,1)S(1)}, u32[]{:S(2)}, u32[]{:S(2)}) collective-permute-start(bf16[256,2048]{1,0:T(8,128)(2,1)S(1)} %get-tuple-element.37), channel_id=1, source_target_pairs={{3,0},{2,1},{1,2},{0,3},{7,4},{6,5},{5,6},{4,7},{11,8},{10,9},{9,1... | collective-permute-start | bytes 3145736 | tf_op jit(solution)/shard_map/ppermute | solution.py:38
  203.9 18.6 %collective-permute-start.41 = (bf16[64,2048]{1,0:T(8,128)(2,1)S(1)}, bf16[64,2048]{1,0:T(8,128)(2,1)S(1)}, u32[]{:S(2)}, u32[]{:S(2)}) collective-permute-start(bf16[64,2048]{1,0:T(8,128)(2,1)S(1)} %fusion.31), channel_id=1, source_target_pairs={{1,0},{0,1},{3,2},{2,3},{5,4},{4,5},{7,6},{6,7},{9,8},{8,9},{11,10... | collective-permute-start | bytes 786440 | tf_op jit(solution)/shard_map/ppermute | solution.py:38
  213.9 10.0 %collective-permute-start.31 = (bf16[128,2048]{1,0:T(8,128)(2,1)S(1)}, bf16[128,2048]{1,0:T(8,128)(2,1)S(1)}, u32[]{:S(2)}, u32[]{:S(2)}) collective-permute-start(bf16[128,2048]{1,0:T(8,128)(2,1)S(1)} %pad_maximum_fusion.8), channel_id=1, source_target_pairs={{3,0},{2,1},{1,2},{0,3},{7,4},{6,5},{5,6},{4,7},{11,8},{10,9},{9,1... | collective-permute-start | bytes 1572872 | tf_op jit(solution)/shard_map/ppermute | solution.py:38
  218.7 10.8 %collective-permute-start.38 = (bf16[128,2048]{1,0:T(8,128)(2,1)S(1)}, bf16[128,2048]{1,0:T(8,128)(2,1)S(1)}, u32[]{:S(2)}, u32[]{:S(2)}) collective-permute-start(bf16[128,2048]{1,0:T(8,128)(2,1)S(1)} %bitcast.114), channel_id=1, source_target_pairs={{1,0},{0,1},{3,2},{2,3},{5,4},{4,5},{7,6},{6,7},{9,8},{8,9},{11,10... | collective-permute-start | bytes 1572872 | tf_op jit(solution)/shard_map/ppermute | solution.py:38
  222.4 31.4 %collective-permute-start.35 = (bf16[64,2048]{1,0:T(8,128)(2,1)S(1)}, bf16[64,2048]{1,0:T(8,128)(2,1)S(1)}, u32[]{:S(2)}, u32[]{:S(2)}) collective-permute-start(bf16[64,2048]{1,0:T(8,128)(2,1)S(1)} %fusion.30), channel_id=1, source_target_pairs={{1,0},{0,1},{3,2},{2,3},{5,4},{4,5},{7,6},{6,7},{9,8},{8,9},{11,10... | collective-permute-start | bytes 786440 | tf_op jit(solution)/shard_map/ppermute | solution.py:38
  229.7 13.3 %collective-permute-start.42 = (bf16[128,2048]{1,0:T(8,128)(2,1)S(1)}, bf16[128,2048]{1,0:T(8,128)(2,1)S(1)}, u32[]{:S(2)}, u32[]{:S(2)}) collective-permute-start(bf16[128,2048]{1,0:T(8,128)(2,1)S(1)} %pad_maximum_fusion.9), channel_id=1, source_target_pairs={{12,0},{13,1},{14,2},{15,3},{8,4},{9,5},{10,6},{11,7},{4,8},{5,9},... | collective-permute-start | bytes 1572872 | tf_op jit(solution)/shard_map/ppermute | solution.py:38
  232.2 21.6 %collective-permute-start.32 = (bf16[64,2048]{1,0:T(8,128)(2,1)S(1)}, bf16[64,2048]{1,0:T(8,128)(2,1)S(1)}, u32[]{:S(2)}, u32[]{:S(2)}) collective-permute-start(bf16[64,2048]{1,0:T(8,128)(2,1)S(1)} %fusion.9), channel_id=1, source_target_pairs={{1,0},{0,1},{3,2},{2,3},{5,4},{4,5},{7,6},{6,7},{9,8},{8,9},{11,10... | collective-permute-start | bytes 786440 | tf_op jit(solution)/shard_map/ppermute | solution.py:38
  243.1 10.7 %collective-permute-start.43 = (bf16[64,2048]{1,0:T(8,128)(2,1)S(1)}, bf16[64,2048]{1,0:T(8,128)(2,1)S(1)}, u32[]{:S(2)}, u32[]{:S(2)}) collective-permute-start(bf16[64,2048]{1,0:T(8,128)(2,1)S(1)} %fusion.6), channel_id=1, source_target_pairs={{4,0},{5,1},{6,2},{7,3},{0,4},{1,5},{2,6},{3,7},{12,8},{13,9},{14,... | collective-permute-start | bytes 786440 | tf_op jit(solution)/shard_map/ppermute | solution.py:38
  (12 other events, 81.1 us)

commit v3 on v2

v3 whole, which is shorter than its diff:
```python
import functools
import math

import jax
import jax.numpy as jnp
from jax import lax
from jax.experimental import pallas as pl
from jax.experimental.pallas import tpu as pltpu
from jax.sharding import PartitionSpec as P

AXES = ("row", "col", "dp")
RING = 4
BF = jnp.bfloat16
F32 = jnp.float32
NN = (((1,), (0,)), ((), ()))
NT = (((1,), (1,)), ((), ()))
TN = (((0,), (0,)), ((), ()))


def cost(flops, bytes_accessed, transcendentals):
    return pl.CostEstimate(
        flops=flops // 100, bytes_accessed=bytes_accessed // 100, transcendentals=transcendentals
    )


def gelu_parts(pre):
    cdf = 0.5 * (1.0 + jax.scipy.special.erf(pre * (1.0 / math.sqrt(2.0))))
    activated = pre * cdf
    slope = cdf + pre * jnp.exp(-0.5 * pre * pre) * (1.0 / math.sqrt(2.0 * math.pi))
    return (activated, slope)


def flat(z, c, x, y):
    return ((z * 2 + c) * RING + x) * RING + y


def exchange(array, partner):
    pairs = []
    for z in range(RING):
        for c in range(2):
            for x in range(RING):
                for y in range(RING):
                    pairs.append((flat(*partner(z, c, x, y)), flat(z, c, x, y)))
    return lax.ppermute(array, AXES, pairs)


NEAR = ((1, 3), (3, 1))
Z_PAIR = ((1, 3), (3, 1))
OWNER_SLOT = ((0, 2, 3, 1), (0, 1, 3, 2))


def along(keep, first, turn):
    def partner(z, c, x, y):
        half = c if keep else 1 - c
        step = NEAR[c][turn]
        if (half == 0) == first:
            return (z, c, x ^ step, y)
        return (z, c, x, y ^ step)

    return partner


def along_z(turn):
    return lambda z, c, x, y: (z ^ Z_PAIR[c][turn], c, x, y)


def other_core(z, c, x, y):
    return (z, 1 - c, x, y)


def slot_of(keep, place_ref, i):
    z, core = place_ref[0], place_ref[1]

    def one(c):
        near = NEAR[c]
        owned = z ^ (0, near[0], near[1], near[0] ^ near[1])[i]
        table = OWNER_SLOT[c if keep else 1 - c]
        slot = jnp.int32(table[0])
        for j in range(1, RING):
            slot = jnp.where(owned == j, table[j], slot)
        return slot

    return jnp.where(core == 0, one(0), one(1))


def cut_kernel(place_ref, tokens_ref, grad_ref, kept_ref, passed_ref):
    block, wide = kept_ref.shape[0], tokens_ref.shape[1]
    core = place_ref[1]
    for ref, which in ((kept_ref, core), (passed_ref, 1 - core)):
        rows = pl.ds(pl.multiple_of(which * block, block), block)
        ref[:, :wide] = tokens_ref[rows, :]
        ref[:, wide:] = grad_ref[rows, :]


def cut(place, tokens, out_grad):
    rows, wide = tokens.shape
    half = jax.ShapeDtypeStruct((rows // 2, 2 * wide), BF)
    return pl.pallas_call(
        cut_kernel,
        grid_spec=pltpu.PrefetchScalarGridSpec(
            num_scalar_prefetch=1,
            grid=(1,),
            in_specs=[pl.BlockSpec((rows, wide), lambda i, place: (0, 0))] * 2,
            out_specs=[pl.BlockSpec((rows // 2, 2 * wide), lambda i, place: (0, 0))] * 2,
        ),
        out_shape=[half, half],
        cost_estimate=cost(flops=0, bytes_accessed=8 * rows * wide, transcendentals=0),
    )(place, tokens, out_grad)


def assemble_kernel(keep, place_ref, a_ref, b_ref, c_ref, out_ref):
    rows = a_ref.shape[0]

    def put(i, value):
        out_ref[pl.ds(pl.multiple_of(slot_of(keep, place_ref, i) * rows, rows), rows), :] = value

    put(0, a_ref[...])
    put(1, b_ref[...])
    put(2, c_ref[:rows, :])
    put(3, c_ref[rows:, :])


def assemble(keep, place, a, b, c):
    rows, wide = a.shape
    tiles = 2
    spec = lambda n: pl.BlockSpec((n, wide // tiles), lambda i, place: (0, i))
    return pl.pallas_call(
        functools.partial(assemble_kernel, keep),
        grid_spec=pltpu.PrefetchScalarGridSpec(
            num_scalar_prefetch=1,
            grid=(tiles,),
            in_specs=[spec(rows), spec(rows), spec(2 * rows)],
            out_specs=spec(4 * rows),
        ),
        out_shape=jax.ShapeDtypeStruct((4 * rows, wide), BF),
        cost_estimate=cost(flops=0, bytes_accessed=16 * rows * wide, transcendentals=0),
    )(place, a, b, c)


def pair_kernel(pieces, added, split, keep, block, place_ref, *refs):
    a_refs, rest = refs[:pieces], refs[pieces:]
    left_ref, right_ref = rest[:2]
    rest = rest[2:]
    if added:
        more_ref, rest = rest[0], rest[1:]

    def rows_of():
        if keep is None:
            values = [a_ref[...] for a_ref in a_refs]
        else:
            size = a_refs[0].shape[0] // RING
            values = [
                a_refs[0][pl.ds(pl.multiple_of(slot_of(keep, place_ref, i) * size, size), size), :]
                for i in range(RING)
            ]
        return values[0] if len(values) == 1 else jnp.concatenate(values, axis=0)

    def finish(total):
        if added:
            total = total + more_ref[...].astype(F32)
        total = total.astype(BF)
        if not split:
            rest[0][...] = total
        elif keep is not None or pieces == 1:
            half = total.shape[0] // 2
            rest[0][...] = total[:half]
            rest[1][...] = total[half:]
        else:
            for i in range(RING):
                for j in range(pieces):
                    first = (j * RING + i) * block
                    at = ((i % 2) * pieces + j) * block
                    rest[i // 2][at:at + block, :] = total[first:first + block]

    @pl.when(pl.program_id(0) == 0)
    def _():
        finish(lax.dot_general(rows_of(), left_ref[...], NN, preferred_element_type=F32))

    @pl.when(pl.program_id(0) == 1)
    def _():
        finish(lax.dot_general(rows_of(), right_ref[...], NT, preferred_element_type=F32))


def pair_dot(pieces, left, right, place, block, more=None, split=False, keep=None, tile=512):
    rows = sum(a.shape[0] for a in pieces)
    depth, wide = left.shape
    tiles = wide // tile
    in_specs = [pl.BlockSpec((a.shape[0], depth), lambda h, n, place: (0, h)) for a in pieces]
    in_specs += [
        pl.BlockSpec((depth, tile), lambda h, n, place: (0, n * (1 - h) + (tiles - 1) * h)),
        pl.BlockSpec((tile, depth), lambda h, n, place: (n * h, 0)),
    ]
    out_of = lambda n_rows: pl.BlockSpec((n_rows, tile), lambda h, n, place: (0, h * tiles + n))
    args = [*pieces, left, right]
    if more is not None:
        in_specs.append(out_of(rows))
        args.append(more)
    outs = [rows // 2, rows // 2] if split else [rows]
    result = pl.pallas_call(
        functools.partial(pair_kernel, len(pieces), more is not None, split, keep, block),
        grid_spec=pltpu.PrefetchScalarGridSpec(
            num_scalar_prefetch=1,
            grid=(2, tiles),
            in_specs=in_specs,
            out_specs=[out_of(n) for n in outs],
        ),
        out_shape=[jax.ShapeDtypeStruct((n, 2 * wide), BF) for n in outs],
        compiler_params=pltpu.CompilerParams(vmem_limit_bytes=24 * 2**20),
        cost_estimate=cost(
            flops=4 * rows * depth * wide,
            bytes_accessed=4 * depth * wide + 8 * rows * wide,
            transcendentals=0,
        ),
    )(place, *args)
    return result if split else result[0]


def stacked(refs):
    if len(refs) == 1:
        return refs[0][...]
    block = refs[0].shape[0] // RING
    return jnp.concatenate(
        [ref[i * block:(i + 1) * block, :] for i in range(RING) for ref in refs], axis=0
    )


def grad_kernel(left_count, right_count, pairs, factor, *refs):
    lefts, rights, out_ref = refs[:left_count], refs[left_count:left_count + right_count], refs[-1]
    total = None
    for left, right in pairs:
        term = lax.dot_general(
            stacked([lefts[i] for i in left]),
            stacked([rights[i] for i in right]),
            TN,
            preferred_element_type=F32,
        )
        total = term if total is None else total + term
    out_ref[...] = total * factor


def grad_dot(lefts, left_part, rights, right_part, pairs, factor, begun=None, tile=256):
    wide = lefts[0].shape[1] // 2
    tiles = wide // tile // 2
    skip = 0 if begun is None else tiles
    base = right_part * 2 * tiles + skip
    tokens = sum(a.shape[0] for a in lefts)
    args = [*lefts, *rights]
    in_specs = [pl.BlockSpec((a.shape[0], wide), lambda n: (0, left_part)) for a in lefts]
    in_specs += [pl.BlockSpec((a.shape[0], tile), lambda n: (0, base + n)) for a in rights]
    aliases = {}
    if begun is not None:
        aliases = {len(args): 0}
        args.append(begun)
        in_specs.append(pl.BlockSpec(memory_space=pl.ANY))
    return pl.pallas_call(
        functools.partial(grad_kernel, len(lefts), len(rights), pairs, factor),
        grid=(tiles,),
        in_specs=in_specs,
        out_specs=pl.BlockSpec((wide, tile), lambda n: (0, skip + n)),
        out_shape=jax.ShapeDtypeStruct((wide, wide), F32),
        input_output_aliases=aliases,
        compiler_params=pltpu.CompilerParams(vmem_limit_bytes=40 * 2**20),
        cost_estimate=cost(
            flops=tokens * wide * wide,
            bytes_accessed=3 * tokens * wide + 2 * wide * wide,
            transcendentals=0,
        ),
    )(*args)


def after(value, *events):
    return lax.optimization_barrier((value, *events))[0]


def shards(tokens, out_grad, weight_in, weight_out):
    core = lax.axis_index("row") % 2
    z = lax.axis_index("row") // 2
    dp = lax.axis_index("dp")
    rows, width = tokens.shape
    block = rows // 2
    inner = weight_in.shape[1] // 2
    factor = 1.0 / math.sqrt(rows * 16)
    both_ways = (True, False)

    place = jnp.stack([z, core]).astype(jnp.int32)
    w_in = lax.dynamic_slice_in_dim(weight_in, dp * inner, inner, 1)
    w_out = lax.dynamic_slice_in_dim(weight_out, dp * inner, inner, 0)

    panel = {}
    start, one, two = {}, {}, {}
    start[True], start[False] = cut(place, tokens, out_grad)
    order = (False, True)
    for keep in order:
        one[keep] = exchange(start[keep], along(keep, True, 0))
    for keep in order:
        pair = jnp.concatenate([start[keep], one[keep]], axis=0)
        two[keep] = exchange(pair, along(keep, True, 1))
    for keep in order:
        panel[keep, 0] = assemble(keep, place, start[keep], one[keep], two[keep])
    panel[True, 0], panel[False, 0] = lax.optimization_barrier((panel[True, 0], panel[False, 0]))
    for keep in order:
        panel[keep, 1] = exchange(panel[keep, 0], along(keep, False, 0))
    for keep in order:
        panel[keep, 2] = exchange(panel[keep, 0], along(keep, False, 1))
    for keep in order:
        panel[keep, 3] = exchange(panel[keep, 1], along(keep, False, 1))

    batches = {True: ((0,), (1, 2), (3,)), False: ((0,), (2, 1), (3,))}

    def passed_dot(b, *events):
        pieces = [panel[False, p] for p in batches[False][b]]
        pieces[0] = after(pieces[0], *events)
        return pair_dot(pieces, w_in, w_out, place, block)

    def kept_dot(b, got, *events):
        pieces = [panel[True, p] for p in batches[True][b]]
        got = after(got, *events) if events else got
        return pair_dot(pieces, w_in, w_out, place, block, more=got, split=True)

    def halfway(kept, got):
        half = kept.shape[0] // 2
        sums = kept.astype(F32) + got.astype(F32)
        return [sums[:half], sums[half:]]

    def hidden_of(value):
        pre, back = value[:, :width], value[:, width:]
        activated, slope = gelu_parts(pre)
        return jnp.concatenate([activated.astype(BF), (back * slope).astype(BF)], axis=1)

    def joined(pair, other):
        return jnp.concatenate([pair, other], axis=0)

    def out_dot(keep, b, *events):
        value = hidden[keep, b]
        value = after(value, *events) if events else value
        return pair_dot([value], w_out, w_in, place, block, split=True, keep=keep)

    def first_half(keep, kept, passed):
        return halfway(kept, exchange(passed, along(keep, True, 1)))

    def first_sum(keep, sums, *events):
        passed = sums[1].astype(BF)
        passed = after(passed, *events) if events else passed
        return sums[0] + exchange(passed, along(keep, True, 0)).astype(F32)

    hidden, firsts, summed = {}, {}, {}

    sent0 = passed_dot(0)
    kept0, send0 = kept_dot(0, exchange(sent0, other_core))
    half0 = halfway(kept0, exchange(send0, along_z(0)))
    turned = after(half0[1].astype(BF), *(panel[keep, p] for keep in order for p in (1, 2)))
    mine0 = hidden_of(half0[0] + exchange(turned, along_z(1)).astype(F32))
    next0 = exchange(mine0, along_z(1))

    sent1 = passed_dot(1, turned)
    got1 = exchange(sent1, other_core)
    pair0 = jnp.concatenate([mine0, next0], axis=0)
    far0 = exchange(pair0, along_z(0))
    kept1, send1 = kept_dot(1, got1, pair0)
    send1 = after(send1, panel[True, 3], panel[False, 3])
    step1 = exchange(send1, along_z(0))

    hidden[True, 0] = joined(after(pair0, send1), far0)
    hidden[False, 0] = exchange(hidden[True, 0], other_core)
    sent2 = passed_dot(2, hidden[True, 0])
    got2 = exchange(sent2, other_core)
    out_kept0 = out_dot(True, 0, sent2)
    kept2, send2 = kept_dot(2, got2, out_kept0[0])
    step2 = exchange(send2, along_z(0))
    out_passed0 = out_dot(False, 0, send2)

    half1 = halfway(kept1, step1)
    turned1 = after(half1[1].astype(BF), out_passed0[0])
    value1 = half1[0] + exchange(turned1, along_z(1)).astype(F32)
    half2 = halfway(kept2, step2)
    mine1 = hidden_of(value1)
    own_kept = first_half(True, *out_kept0)
    own_passed = first_half(False, *out_passed0)
    next1 = exchange(after(mine1, own_kept[0], own_passed[0]), along_z(1))
    mine2 = hidden_of(half2[0] + exchange(half2[1].astype(BF), along_z(1)).astype(F32))
    next2 = exchange(mine2, along_z(1))
    firsts[True, 0] = first_sum(True, own_kept)
    firsts[False, 0] = first_sum(False, own_passed)
    pair1 = after(jnp.concatenate([mine1, next1], axis=0), firsts[True, 0], firsts[False, 0])
    far1 = exchange(pair1, along_z(0))
    pair2 = jnp.concatenate([mine2, next2], axis=0)
    far2 = exchange(pair2, along_z(0))

    hidden[True, 1] = joined(pair1, far1)
    hidden[False, 1] = exchange(hidden[True, 1], other_core)
    out_kept1 = out_dot(True, 1)
    hidden[True, 2] = joined(after(pair2, out_kept1[0]), far2)
    hidden[False, 2] = exchange(hidden[True, 2], other_core)
    out_passed1 = out_dot(False, 1, hidden[True, 2])
    half_kept1 = first_half(True, *out_kept1)
    out_kept2 = out_dot(True, 2, out_passed1[0])
    half_passed1 = first_half(False, *out_passed1)
    out_passed2 = out_dot(False, 2, out_kept2[0])

    panels, hiddens, in_pairs, out_pairs = [], [], [], []
    for keep in both_ways:
        for b in range(3):
            numbers = tuple(range(len(panels), len(panels) + len(batches[keep][b])))
            in_pairs.append((numbers, (len(hiddens),)))
            out_pairs.append(((len(hiddens),), numbers))
            panels += [panel[keep, p] for p in batches[keep][b]]
            hiddens.append(hidden[keep, b])

    def grads(which, begun, *events):
        if which == 0:
            lefts, rights, parts, pairs = panels, list(hiddens), (0, 1), in_pairs
        else:
            lefts, rights, parts, pairs = hiddens, list(panels), (0, 1), out_pairs
        rights[0] = after(rights[0], *events)
        return grad_dot(lefts, parts[0], rights, parts[1], pairs, factor, begun)

    firsts[True, 1] = first_sum(True, half_kept1)
    firsts[False, 1] = first_sum(False, half_passed1)
    grad_in = grads(0, None, out_passed2[0])
    half_kept2 = first_half(True, *out_kept2)
    half_passed2 = first_half(False, *out_passed2)
    firsts[True, 2] = first_sum(True, half_kept2, grad_in)
    firsts[False, 2] = first_sum(False, half_passed2, grad_in)
    grad_in = grads(0, grad_in, half_kept2[0], half_passed2[0])
    for keep in both_ways:
        for b in range(3):
            for i, p in enumerate(batches[keep][b]):
                summed[keep, p] = firsts[keep, b][i * block:(i + 1) * block]
    lasts, gots = {}, {}
    for keep in both_ways:
        passed = jnp.concatenate([summed[keep, 2], summed[keep, 3]], axis=0).astype(BF)
        passed = after(passed, grad_in)
        gots[keep] = exchange(passed, along(keep, False, 1))
    grad_out = grads(1, None, grad_in)
    done = {}
    for keep in both_ways:
        got = gots[keep].astype(F32)
        last = after((summed[keep, 1] + got[block:]).astype(BF), grad_out)
        lasts[keep] = exchange(last, along(keep, False, 0))
    grad_out = grads(1, grad_out, gots[True], gots[False])
    for keep in both_ways:
        got = gots[keep].astype(F32)
        got_last = after(lasts[keep], grad_out)
        done[keep] = (summed[keep, 0] + got[:block] + got_last.astype(F32)).astype(BF)

    low = jnp.where(core == 0, done[True], done[False])
    high = jnp.where(core == 0, done[False], done[True])
    result = jnp.concatenate([low, high], axis=0)
    return (result[:, :width], result[:, width:], grad_in, grad_out)


def solution(mesh):
    placed = (P(("col", "dp"), "row"), P(("col", "dp"), "row"), P("row", "col"), P("col", "row"))
    return jax.shard_map(
        shards,
        mesh=mesh,
        in_specs=placed,
        out_specs=(
            P(("col", "dp"), "row"),
            P(("col", "dp"), "row"),
            P("row", ("col", "dp")),
            P(("col", "dp"), "row"),
        ),
        check_vma=False,
    )
```

time: 256 us -> 269 us (1.051)
  waiting for transfers between devices: 116 us -> 94.5 us
  starting transfers between devices: 52.3 us -> 67.9 us
  local copies, waits for them, and re-layouts: 11.3 us -> 21.5 us
  other arithmetic: 7.07 us -> 12.9 us
    ppermute x44, waiting for transfers between devices: 116 us -> 94.5 us  [exchange(): return lax.ppermute(array, AXES, pairs)]
    ppermute x44, starting transfers between devices: 52.3 us -> 67.9 us  [exchange(): return lax.ppermute(array, AXES, pairs)]
    unnamed x33 -> x75, local copies, waits for them, and re-layouts: 4.65 us -> 16.9 us
    pallas_call x4 -> x7, Pallas kernels: 22.5 us -> 28.8 us  [the longest x4 20.7 us: grad_dot(): pl.pallas_call(functools.partial(grad_kernel, len(lefts), len(rights), pa...]
    pallas_call x12, Pallas kernels: 45 us -> 39.8 us  [pair_dot(): pl.pallas_call(functools.partial(pair_kernel, len(pieces), more is not No...]
    add x5 -> x16, other arithmetic: 0.53 us -> 3.94 us  [the longest x4 1.92 us: first_sum(): return sums[0] + exchange(passed, along(keep, True, 0)).astype(F32)]
    concatenate x2, other arithmetic: 1.03 us -> 3.75 us  [shards(): pair = jnp.concatenate([start[keep], one[keep]], axis=0)]
  transfers between devices with their start and end apart: 44 -> 44, of which waited for: 18 -> 19; matrix products, arithmetic and copies ran while one was open for 4% -> 6% of each run, Pallas kernels for 25% -> 20%
where the time goes in v3:
time: 269 us; the launch traced here: 267 us
  waiting for transfers between devices  94.5 us (35%)
  Pallas kernels  68.6 us (26%)
  starting transfers between devices  67.9 us (25%)
  local copies, waits for them, and re-layouts  21.5 us (8%)
  other arithmetic  12.9 us (5%)
    ppermute x44, waiting for transfers between devices, exchange(): return lax.ppermute(array, AXES, pairs)  94.5 us
    ppermute x44, starting transfers between devices, exchange(): return lax.ppermute(array, AXES, pairs)  67.9 us
    pallas_call x12, Pallas kernels, pair_dot(): pl.pallas_call(functools.partial(pair_kernel, len(pieces), more is not No...  39.8 us
    pallas_call x4, Pallas kernels, grad_dot(): pl.pallas_call(functools.partial(grad_kernel, len(lefts), len(rights), pa...  20.7 us
    unnamed x75, local copies, waits for them, and re-layouts  16.9 us
    pallas_call x2, Pallas kernels, assemble(): pl.pallas_call(functools.partial(assemble_kernel, keep), grid_spec=pltpu....  5.56 us
  transfers between devices with their start and end apart: 44, of which 19 were waited for; matrix products, arithmetic and copies ran while one was open for 6% of the time, Pallas kernels for 20%

profile of v3, /device:TPU:8, one launch (start us, length us, event | category | flops | bytes accessed | tf_op | source)
XLA Modules:
  0.0 266.8 jit_solution(228202182045245216)
XLA Ops:
  1.3 2.5 shard_map.75
  5.7 4.6 %collective-permute-done.b_ref = bf16[64,2048]{1,0:T(8,128)(2,1)S(1)} collective-permute-done((bf16[64,2048]{1,0:T(8,128)(2,1)}, bf16[64,2048]{1,0:T(8,128)(2,1)S(1)}, u32[]{:S(2)}, u32[]{:S(2)}) %collective-permute-start) | collective-permute-done | bytes 262176 | tf_op jit(solution)/shard_map/ppermute | solution.py:44
  12.2 2.8 %collective-permute-start.1 = (bf16[128,2048]{1,0:T(8,128)(2,1)}, bf16[128,2048]{1,0:T(8,128)(2,1)S(1)}, u32[]{:S(2)}, u32[]{:S(2)}) collective-permute-start(bf16[128,2048]{1,0:T(8,128)(2,1)} %pad_maximum_fusion.1), channel_id=1, source_target_pairs={{12,0},{13,1},{14,2},{15,3},{8,4},{9,5},{10,6},{11,7},{4,8},{5,9},... | collective-permute-start | bytes 1572872 | tf_op jit(solution)/shard_map/ppermute | solution.py:44
  18.4 4.0 %constant_dynamic-slice_fusion = (bf16[1024,1024]{1,0:T(8,128)(2,1)S(1)}, bf16[1024,1024]{1,0:T(8,128)(2,1)}) fusion(bf16[2048,1024]{1,0:T(8,128)(2,1)} %param.7, s32[]{:T(128)S(6)} %select_n.30, bf16[1024,2048]{1,0:T(8,128)(2,1)} %param.6), kind=kLoop, calls=%fused_computation.89 | loop fusion | bytes 8388612 | tf_op jit(solution)/shard_map/dynamic_slice | solution.py:287
  23.6 2.8 %shard_map.76.refs_0_.refs_6_ = bf16[256,2048]{1,0:T(8,128)(2,1)} custom-call(s32[2]{0:T(128)} %pad_add_fusion.place_ref, bf16[64,2048]{1,0:T(8,128)(2,1)} %get-tuple-element.54.a_ref, bf16[64,2048]{1,0:T(8,128)(2,1)} %copy-done.34, bf16[128,2048]{1,0:T(8,128)(2,1)} %copy-done.35), custom_call_target="tpu_custom_call" | custom-call | bytes 20971 | tf_op jit(solution)/shard_map/pallas_call | solution.py:127
  26.4 2.8 %shard_map.77.refs_0_.refs_4_.refs_10_ = bf16[256,2048]{1,0:T(8,128)(2,1)} custom-call(s32[2]{0:T(128)} %pad_add_fusion.place_ref, bf16[64,2048]{1,0:T(8,128)(2,1)} %get-tuple-element.55.a_ref, bf16[64,2048]{1,0:T(8,128)(2,1)} %copy-done.33, bf16[128,2048]{1,0:T(8,128)(2,1)} %collective-permute-done.3.c_ref), custom_call_target="tpu_custom_call" | custom-call | bytes 20971 | tf_op jit(solution)/shard_map/pallas_call | solution.py:127
  32.0 2.9 %shard_map.78 = bf16[256,2048]{1,0:T(8,128)(2,1)S(1)} custom-call(s32[2]{0:T(128)S(1)} %copy-done.26, bf16[256,2048]{1,0:T(8,128)(2,1)S(1)} %copy-done.4, bf16[1024,1024]{1,0:T(8,128)(2,1)S(1)} %copy-done, bf16[1024,1024]{1,0:T(8,128)(2,1)S(1)} %get-tuple-element.115.refs_2_.refs_3_.refs_1_), custom_call_target="tpu_custom_call" | custom-call | flops 10737418 | bytes 62914 | tf_op jit(solution)/shard_map/pallas_call | solution.py:199
  36.7 3.1 %collective-permute-start.8 = (bf16[256,2048]{1,0:T(8,128)(2,1)S(1)}, bf16[256,2048]{1,0:T(8,128)(2,1)S(1)}, u32[]{:S(2)}, u32[]{:S(2)}) collective-permute-start(bf16[256,2048]{1,0:T(8,128)(2,1)S(1)} %copy-done.3), channel_id=1, source_target_pairs={{1,0},{0,1},{3,2},{2,3},{5,4},{4,5},{7,6},{6,7},{9,8},{8,9},{11,10... | collective-permute-start | bytes 3145736 | tf_op jit(solution)/shard_map/ppermute | solution.py:44
  41.3 3.0 %shard_map.79 = (bf16[128,2048]{1,0:T(8,128)(2,1)S(1)}, bf16[128,2048]{1,0:T(8,128)(2,1)S(1)}) custom-call(s32[2]{0:T(128)S(1)} %copy-done.26, bf16[256,2048]{1,0:T(8,128)(2,1)S(1)} %copy-done.3, bf16[1024,1024]{1,0:T(8,128)(2,1)S(1)} %copy-done, bf16[1024,1024]{1,0:T(8,128)(2,1)S(1)} %get-tuple-element.115.refs_2_.refs_3_.refs_1_, ...), custom_call_target="tpu_custom_call" | custom-call | flops 10737418 | bytes 62914 | tf_op jit(solution)/shard_map/pallas_call | solution.py:199
  46.3 7.3 %collective-permute-done.5 = bf16[128,2048]{1,0:T(8,128)(2,1)S(1)} collective-permute-done((bf16[128,2048]{1,0:T(8,128)(2,1)S(1)}, bf16[128,2048]{1,0:T(8,128)(2,1)S(1)}, u32[]{:S(2)}, u32[]{:S(2)}) %collective-permute-start.5) | collective-permute-done | bytes 524320 | tf_op jit(solution)/shard_map/ppermute | solution.py:44
  53.7 4.6 %collective-permute-done.9.refs_1_.refs_2_.refs_8_ = bf16[256,2048]{1,0:T(8,128)(2,1)S(1)} collective-permute-done((bf16[256,2048]{1,0:T(8,128)(2,1)S(1)}, bf16[256,2048]{1,0:T(8,128)(2,1)S(1)}, u32[]{:S(2)}, u32[]{:S(2)}) %collective-permute-start.9) | collective-permute-done | bytes 1048608 | tf_op jit(solution)/shard_map/ppermute | solution.py:44
  58.3 4.8 %collective-permute-done.8.refs_0_.refs_1_.refs_7_ = bf16[256,2048]{1,0:T(8,128)(2,1)S(1)} collective-permute-done((bf16[256,2048]{1,0:T(8,128)(2,1)S(1)}, bf16[256,2048]{1,0:T(8,128)(2,1)S(1)}, u32[]{:S(2)}, u32[]{:S(2)}) %collective-permute-start.8) | collective-permute-done | bytes 1048608 | tf_op jit(solution)/shard_map/ppermute | solution.py:44
  63.1 4.1 %shard_map.80 = bf16[512,2048]{1,0:T(8,128)(2,1)S(1)} custom-call(s32[2]{0:T(128)S(1)} %copy-done.26, bf16[256,2048]{1,0:T(8,128)(2,1)S(1)} %collective-permute-done.7.refs_0_.refs_5_.refs_11_, bf16[256,2048]{1,0:T(8,128)(2,1)S(1)} %collective-permute-done.6.refs_1_.refs_6_.refs_12_, bf16[1024,1024]{1,0:T(8,128)(2,1)S(1)} %copy-done, ...), custom_call_target="tpu_custom_call" | custom-call | flops 21474836 | bytes 83886 | tf_op jit(solution)/shard_map/pallas_call | solution.py:199
  67.3 4.1 %collective-permute-start.10 = (bf16[64,2048]{1,0:T(8,128)(2,1)S(1)}, bf16[64,2048]{1,0:T(8,128)(2,1)S(1)}, u32[]{:S(2)}, u32[]{:S(2)}) collective-permute-start(bf16[64,2048]{1,0:T(8,128)(2,1)S(1)} %slice.259), channel_id=1, source_target_pairs={{96,0},{97,1},{98,2},{99,3},{100,4},{101,5},{102,6},{103,7},{104,8... | collective-permute-start | bytes 786440 | tf_op jit(solution)/shard_map/ppermute | solution.py:44
  71.7 2.7 %collective-permute-start.14 = (bf16[256,2048]{1,0:T(8,128)(2,1)S(1)}, bf16[256,2048]{1,0:T(8,128)(2,1)S(1)}, u32[]{:S(2)}, u32[]{:S(2)}) collective-permute-start(bf16[256,2048]{1,0:T(8,128)(2,1)S(1)} %collective-permute-done.6.refs_1_.refs_6_.refs_12_), channel_id=1, source_target_pairs={{12,0},{13,1},{14,2},{15,3},{8,4},{9,5},{10,6},{11,7},{4,8},{5,9},... | collective-permute-start | bytes 3145736 | tf_op jit(solution)/shard_map/ppermute | solution.py:44
  76.0 3.3 %collective-permute-start.11 = (bf16[64,2048]{1,0:T(8,128)(2,1)S(1)}, bf16[64,2048]{1,0:T(8,128)(2,1)S(1)}, u32[]{:S(2)}, u32[]{:S(2)}) collective-permute-start(bf16[64,2048]{1,0:T(8,128)(2,1)S(1)} %pad_maximum_fusion.9), channel_id=1, source_target_pairs={{96,0},{97,1},{98,2},{99,3},{100,4},{101,5},{102,6},{103,7},{104,8... | collective-permute-start | bytes 786440 | tf_op jit(solution)/shard_map/ppermute | solution.py:44
  79.3 4.4 %collective-permute-done.11 = bf16[64,2048]{1,0:T(8,128)(2,1)S(1)} collective-permute-done((bf16[64,2048]{1,0:T(8,128)(2,1)S(1)}, bf16[64,2048]{1,0:T(8,128)(2,1)S(1)}, u32[]{:S(2)}, u32[]{:S(2)}) %collective-permute-start.11) | collective-permute-done | bytes 262176 | tf_op jit(solution)/shard_map/ppermute | solution.py:44
  83.8 4.3 %shard_map.81 = (bf16[256,2048]{1,0:T(8,128)(2,1)S(1)}, bf16[256,2048]{1,0:T(8,128)(2,1)S(1)}) custom-call(s32[2]{0:T(128)S(1)} %copy-done.26, bf16[256,2048]{1,0:T(8,128)(2,1)S(1)} %collective-permute-done.8.refs_0_.refs_1_.refs_7_, bf16[256,2048]{1,0:T(8,128)(2,1)S(1)} %collective-permute-done.9.refs_1_.refs_2_.refs_8_, bf16[1024,1024]{1,0:T(8,128)(2,1)S(1)} %copy-done, ...), custom_call_target="tpu_custom_call" | custom-call | flops 21474836 | bytes 83886 | tf_op jit(solution)/shard_map/pallas_call | solution.py:199
  88.2 4.8 %collective-permute-done.15 = bf16[128,2048]{1,0:T(8,128)(2,1)S(1)} collective-permute-done((bf16[128,2048]{1,0:T(8,128)(2,1)S(1)}, bf16[128,2048]{1,0:T(8,128)(2,1)S(1)}, u32[]{:S(2)}, u32[]{:S(2)}) %collective-permute-start.15) | collective-permute-done | bytes 524320 | tf_op jit(solution)/shard_map/ppermute | solution.py:44
  93.0 2.9 %shard_map.82 = bf16[256,2048]{1,0:T(8,128)(2,1)S(1)} custom-call(s32[2]{0:T(128)S(1)} %copy-done.26, bf16[256,2048]{1,0:T(8,128)(2,1)S(1)} %collective-permute-done.14.refs_0_.refs_7_.refs_13_, bf16[1024,1024]{1,0:T(8,128)(2,1)S(1)} %copy-done, bf16[1024,1024]{1,0:T(8,128)(2,1)S(1)} %get-tuple-element.115.refs_2_.refs_3_.refs_1_), custom_call_target="tpu_custom_call" | custom-call | flops 10737418 | bytes 62914 | tf_op jit(solution)/shard_map/pallas_call | solution.py:199
  96.4 2.9 %shard_map.83 = (bf16[128,2048]{1,0:T(8,128)(2,1)S(1)}, bf16[128,2048]{1,0:T(8,128)(2,1)S(1)}) custom-call(s32[2]{0:T(128)S(1)} %copy-done.26, bf16[256,2048]{1,0:T(8,128)(2,1)S(1)} %constant_dynamic-update-slice_fusion.refs_0_.refs_8_, bf16[1024,1024]{1,0:T(8,128)(2,1)S(1)} %get-tuple-element.115.refs_2_.refs_3_.refs_1_, bf16[1024,1024]{1,0:T(8,128)(2,1)S(1)} %copy-done), custom_call_target="tpu_custom_call" | custom-call | flops 10737418 | bytes 62914 | tf_op jit(solution)/shard_map/pallas_call | solution.py:199
  100.9 8.9 %collective-permute-done.16 = bf16[128,2048]{1,0:T(8,128)(2,1)S(1)} collective-permute-done((bf16[128,2048]{1,0:T(8,128)(2,1)S(1)}, bf16[128,2048]{1,0:T(8,128)(2,1)S(1)}, u32[]{:S(2)}, u32[]{:S(2)}) %collective-permute-start.16) | collective-permute-done | bytes 524320 | tf_op jit(solution)/shard_map/ppermute | solution.py:44
  110.1 3.0 %shard_map.84 = (bf16[128,2048]{1,0:T(8,128)(2,1)S(1)}, bf16[128,2048]{1,0:T(8,128)(2,1)S(1)}) custom-call(s32[2]{0:T(128)S(1)} %copy-done.26, bf16[256,2048]{1,0:T(8,128)(2,1)S(1)} %collective-permute-done.13.refs_0_.refs_3_.refs_9_, bf16[1024,1024]{1,0:T(8,128)(2,1)S(1)} %copy-done, bf16[1024,1024]{1,0:T(8,128)(2,1)S(1)} %get-tuple-element.115.refs_2_.refs_3_.refs_1_, ...), custom_call_target="tpu_custom_call" | custom-call | flops 10737418 | bytes 62914 | tf_op jit(solution)/shard_map/pallas_call | solution.py:199
  113.1 2.9 %shard_map.85 = (bf16[128,2048]{1,0:T(8,128)(2,1)S(1)}, bf16[128,2048]{1,0:T(8,128)(2,1)S(1)}) custom-call(s32[2]{0:T(128)S(1)} %copy-done.26, bf16[256,2048]{1,0:T(8,128)(2,1)S(1)} %collective-permute-done.19.refs_0_.refs_11_.refs_3_, bf16[1024,1024]{1,0:T(8,128)(2,1)S(1)} %get-tuple-element.115.refs_2_.refs_3_.refs_1_, bf16[1024,1024]{1,0:T(8,128)(2,1)S(1)} %copy-done), custom_call_target="tpu_custom_call" | custom-call | flops 10737418 | bytes 62914 | tf_op jit(solution)/shard_map/pallas_call | solution.py:199
  116.8 3.3 %collective-permute-start.21 = (bf16[128,2048]{1,0:T(8,128)(2,1)S(1)}, bf16[128,2048]{1,0:T(8,128)(2,1)S(1)}, u32[]{:S(2)}, u32[]{:S(2)}) collective-permute-start(bf16[128,2048]{1,0:T(8,128)(2,1)S(1)} %slice.251), channel_id=1, source_target_pairs={{96,0},{97,1},{98,2},{99,3},{100,4},{101,5},{102,6},{103,7},{104,8... | collective-permute-start | bytes 1572872 | tf_op jit(solution)/shard_map/ppermute | solution.py:44
  122.4 2.9 %collective-permute-done.22 = bf16[128,2048]{1,0:T(8,128)(2,1)S(1)} collective-permute-done((bf16[128,2048]{1,0:T(8,128)(2,1)S(1)}, bf16[128,2048]{1,0:T(8,128)(2,1)S(1)}, u32[]{:S(2)}, u32[]{:S(2)}) %collective-permute-start.22) | collective-permute-done | bytes 524320 | tf_op jit(solution)/shard_map/ppermute | solution.py:44
  127.6 3.8 %collective-permute-done.21 = bf16[128,2048]{1,0:T(8,128)(2,1)S(1)} collective-permute-done((bf16[128,2048]{1,0:T(8,128)(2,1)S(1)}, bf16[128,2048]{1,0:T(8,128)(2,1)S(1)}, u32[]{:S(2)}, u32[]{:S(2)}) %collective-permute-start.21) | collective-permute-done | bytes 524320 | tf_op jit(solution)/shard_map/ppermute | solution.py:44
  131.8 3.5 %collective-permute-start.23 = (bf16[128,2048]{1,0:T(8,128)(2,1)S(1)}, bf16[128,2048]{1,0:T(8,128)(2,1)S(1)}, u32[]{:S(2)}, u32[]{:S(2)}) collective-permute-start(bf16[128,2048]{1,0:T(8,128)(2,1)S(1)} %pad_maximum_fusion.4), channel_id=1, source_target_pairs={{96,0},{97,1},{98,2},{99,3},{100,4},{101,5},{102,6},{103,7},{104,8... | collective-permute-start | bytes 1572872 | tf_op jit(solution)/shard_map/ppermute | solution.py:44
  136.4 8.8 %collective-permute-done.23 = bf16[128,2048]{1,0:T(8,128)(2,1)S(1)} collective-permute-done((bf16[128,2048]{1,0:T(8,128)(2,1)S(1)}, bf16[128,2048]{1,0:T(8,128)(2,1)S(1)}, u32[]{:S(2)}, u32[]{:S(2)}) %collective-permute-start.23) | collective-permute-done | bytes 524320 | tf_op jit(solution)/shard_map/ppermute | solution.py:44
  146.0 4.8 %collective-permute-done.29 = bf16[64,2048]{1,0:T(8,128)(2,1)S(1)} collective-permute-done((bf16[64,2048]{1,0:T(8,128)(2,1)S(1)}, bf16[64,2048]{1,0:T(8,128)(2,1)S(1)}, u32[]{:S(2)}, u32[]{:S(2)}) %collective-permute-start.29) | collective-permute-done | bytes 262176 | tf_op jit(solution)/shard_map/ppermute | solution.py:44
  151.0 3.8 %collective-permute-start.30 = (bf16[64,2048]{1,0:T(8,128)(2,1)S(1)}, bf16[64,2048]{1,0:T(8,128)(2,1)S(1)}, u32[]{:S(2)}, u32[]{:S(2)}) collective-permute-start(bf16[64,2048]{1,0:T(8,128)(2,1)S(1)} %pad_maximum_fusion.10), channel_id=1, source_target_pairs={{96,0},{97,1},{98,2},{99,3},{100,4},{101,5},{102,6},{103,7},{104,8... | collective-permute-start | bytes 786440 | tf_op jit(solution)/shard_map/ppermute | solution.py:44
  154.8 5.3 %collective-permute-done.25 = bf16[256,2048]{1,0:T(8,128)(2,1)S(1)} collective-permute-done((bf16[256,2048]{1,0:T(8,128)(2,1)S(1)}, bf16[256,2048]{1,0:T(8,128)(2,1)S(1)}, u32[]{:S(2)}, u32[]{:S(2)}) %collective-permute-start.25) | collective-permute-done | bytes 1048608 | tf_op jit(solution)/shard_map/ppermute | solution.py:44
  160.2 4.1 %shard_map.86 = (bf16[256,2048]{1,0:T(8,128)(2,1)S(1)}, bf16[256,2048]{1,0:T(8,128)(2,1)S(1)}) custom-call(s32[2]{0:T(128)S(1)} %copy-done.26, bf16[512,2048]{1,0:T(8,128)(2,1)S(1)} %constant_dynamic-update-slice_fusion.2.refs_0_.refs_9_.refs_1_, bf16[1024,1024]{1,0:T(8,128)(2,1)S(1)} %get-tuple-element.115.refs_2_.refs_3_.refs_1_, ...), custom_call_target="tpu_custom_call" | custom-call | flops 21474836 | bytes 83886 | tf_op jit(solution)/shard_map/pallas_call | solution.py:199
  164.4 3.3 %collective-permute-start.26 = (bf16[256,2048]{1,0:T(8,128)(2,1)S(1)}, bf16[256,2048]{1,0:T(8,128)(2,1)S(1)}, u32[]{:S(2)}, u32[]{:S(2)}) collective-permute-start(bf16[256,2048]{1,0:T(8,128)(2,1)S(1)} %get-tuple-element.80), channel_id=1, source_target_pairs={{12,0},{13,1},{14,2},{15,3},{8,4},{9,5},{10,6},{11,7},{4,8},{5,9},... | collective-permute-start | bytes 3145736 | tf_op jit(solution)/shard_map/ppermute | solution.py:44
  169.8 7.1 %collective-permute-done.31 = bf16[128,2048]{1,0:T(8,128)(2,1)S(1)} collective-permute-done((bf16[128,2048]{1,0:T(8,128)(2,1)S(1)}, bf16[128,2048]{1,0:T(8,128)(2,1)S(1)}, u32[]{:S(2)}, u32[]{:S(2)}) %collective-permute-start.31) | collective-permute-done | bytes 524320 | tf_op jit(solution)/shard_map/ppermute | solution.py:44
  183.1 4.1 %shard_map.87 = (bf16[256,2048]{1,0:T(8,128)(2,1)S(1)}, bf16[256,2048]{1,0:T(8,128)(2,1)S(1)}) custom-call(s32[2]{0:T(128)S(1)} %copy-done.26, bf16[512,2048]{1,0:T(8,128)(2,1)S(1)} %collective-permute-done.32.refs_0_.refs_12_.refs_4_, bf16[1024,1024]{1,0:T(8,128)(2,1)S(1)} %get-tuple-element.115.refs_2_.refs_3_.refs_1_, bf16[1024,1024]{1,0:T(8,128)(2,1)S(1)} %copy-done), custom_call_target="tpu_custom_call" | custom-call | flops 21474836 | bytes 83886 | tf_op jit(solution)/shard_map/pallas_call | solution.py:199
  187.2 2.9 %shard_map.88 = (bf16[128,2048]{1,0:T(8,128)(2,1)S(1)}, bf16[128,2048]{1,0:T(8,128)(2,1)S(1)}) custom-call(s32[2]{0:T(128)S(1)} %copy-done.26, bf16[256,2048]{1,0:T(8,128)(2,1)S(1)} %constant_dynamic-update-slice_fusion.4.refs_0_.refs_10_.refs_2_, bf16[1024,1024]{1,0:T(8,128)(2,1)S(1)} %get-tuple-element.115.refs_2_.refs_3_.refs_1_, ...), custom_call_target="tpu_custom_call" | custom-call | flops 10737418 | bytes 62914 | tf_op jit(solution)/shard_map/pallas_call | solution.py:199
  190.1 2.9 %collective-permute-start.33 = (bf16[128,2048]{1,0:T(8,128)(2,1)S(1)}, bf16[128,2048]{1,0:T(8,128)(2,1)S(1)}, u32[]{:S(2)}, u32[]{:S(2)}) collective-permute-start(bf16[128,2048]{1,0:T(8,128)(2,1)S(1)} %get-tuple-element.87), channel_id=1, source_target_pairs={{12,0},{13,1},{14,2},{15,3},{8,4},{9,5},{10,6},{11,7},{4,8},{5,9},... | collective-permute-start | bytes 1572872 | tf_op jit(solution)/shard_map/ppermute | solution.py:44
  193.0 2.9 %shard_map.89 = (bf16[128,2048]{1,0:T(8,128)(2,1)S(1)}, bf16[128,2048]{1,0:T(8,128)(2,1)S(1)}) custom-call(s32[2]{0:T(128)S(1)} %copy-done.26, bf16[256,2048]{1,0:T(8,128)(2,1)S(1)} %collective-permute-done.34.refs_0_.refs_13_.refs_5_, bf16[1024,1024]{1,0:T(8,128)(2,1)S(1)} %get-tuple-element.115.refs_2_.refs_3_.refs_1_, bf16[1024,1024]{1,0:T(8,128)(2,1)S(1)} %copy-done), custom_call_target="tpu_custom_call" | custom-call | flops 10737418 | bytes 62914 | tf_op jit(solution)/shard_map/pallas_call | solution.py:199
  198.2 4.8 %shard_map.90.refs_14_ = f32[1024,1024]{1,0:T(8,128)} custom-call(bf16[256,2048]{1,0:T(8,128)(2,1)S(1)} %copy-done.3, bf16[256,2048]{1,0:T(8,128)(2,1)S(1)} %collective-permute-done.8.refs_0_.refs_1_.refs_7_, bf16[256,2048]{1,0:T(8,128)(2,1)S(1)} %collective-permute-done.9.refs_1_.refs_2_.refs_8_, ...), custom_call_target="tpu_custom_call" | custom-call | flops 21474836 | bytes 83886 | tf_op jit(solution)/shard_map/pallas_call | solution.py:255
  203.3 4.7 %collective-permute-done.36 = bf16[128,2048]{1,0:T(8,128)(2,1)S(1)} collective-permute-done((bf16[128,2048]{1,0:T(8,128)(2,1)S(1)}, bf16[128,2048]{1,0:T(8,128)(2,1)S(1)}, u32[]{:S(2)}, u32[]{:S(2)}) %collective-permute-start.36) | collective-permute-done | bytes 524320 | tf_op jit(solution)/shard_map/ppermute | solution.py:44
  208.1 3.2 %collective-permute-start.41 = (bf16[64,2048]{1,0:T(8,128)(2,1)S(1)}, bf16[64,2048]{1,0:T(8,128)(2,1)S(1)}, u32[]{:S(2)}, u32[]{:S(2)}) collective-permute-start(bf16[64,2048]{1,0:T(8,128)(2,1)S(1)} %slice.252), channel_id=1, source_target_pairs={{1,0},{0,1},{3,2},{2,3},{5,4},{4,5},{7,6},{6,7},{9,8},{8,9},{11,10... | collective-permute-start | bytes 786440 | tf_op jit(solution)/shard_map/ppermute | solution.py:44
  211.3 4.8 %shard_map.91 = f32[1024,1024]{1,0:T(8,128)} custom-call(bf16[256,2048]{1,0:T(8,128)(2,1)S(1)} %copy-done.3, bf16[256,2048]{1,0:T(8,128)(2,1)S(1)} %collective-permute-done.8.refs_0_.refs_1_.refs_7_, bf16[256,2048]{1,0:T(8,128)(2,1)S(1)} %collective-permute-done.9.refs_1_.refs_2_.refs_8_, ...), custom_call_target="tpu_custom_call", output_to_operand_aliasing={{}: (14, {})} | custom-call | flops 21474836 | bytes 83886 | tf_op jit(solution)/shard_map/pallas_call | solution.py:255
  216.1 3.1 %collective-permute-done.39 = bf16[256,2048]{1,0:T(8,128)(2,1)S(1)} collective-permute-done((bf16[256,2048]{1,0:T(8,128)(2,1)S(1)}, bf16[256,2048]{1,0:T(8,128)(2,1)S(1)}, u32[]{:S(2)}, u32[]{:S(2)}) %collective-permute-start.39) | collective-permute-done | bytes 1048608 | tf_op jit(solution)/shard_map/ppermute | solution.py:44
  219.6 3.2 %collective-permute-start.40 = (bf16[128,2048]{1,0:T(8,128)(2,1)S(1)}, bf16[128,2048]{1,0:T(8,128)(2,1)S(1)}, u32[]{:S(2)}, u32[]{:S(2)}) collective-permute-start(bf16[128,2048]{1,0:T(8,128)(2,1)S(1)} %slice.249), channel_id=1, source_target_pairs={{1,0},{0,1},{3,2},{2,3},{5,4},{4,5},{7,6},{6,7},{9,8},{8,9},{11,10... | collective-permute-start | bytes 1572872 | tf_op jit(solution)/shard_map/ppermute | solution.py:44
  223.9 10.6 %collective-permute-done.40 = bf16[128,2048]{1,0:T(8,128)(2,1)S(1)} collective-permute-done((bf16[128,2048]{1,0:T(8,128)(2,1)S(1)}, bf16[128,2048]{1,0:T(8,128)(2,1)S(1)}, u32[]{:S(2)}, u32[]{:S(2)}) %collective-permute-start.40) | collective-permute-done | bytes 524320 | tf_op jit(solution)/shard_map/ppermute | solution.py:44
  236.3 5.5 %shard_map.92.refs_14_ = f32[1024,1024]{1,0:T(8,128)} custom-call(bf16[256,2048]{1,0:T(8,128)(2,1)S(1)} %constant_dynamic-update-slice_fusion.refs_0_.refs_8_, bf16[512,2048]{1,0:T(8,128)(2,1)} %copy-done.1, bf16[256,2048]{1,0:T(8,128)(2,1)S(1)} %constant_dynamic-update-slice_fusion.4.refs_0_.refs_10_.refs_2_, ...), custom_call_target="tpu_custom_call" | custom-call | flops 21474836 | bytes 83886 | tf_op jit(solution)/shard_map/pallas_call | solution.py:255
  259.1 5.6 %shard_map.93 = f32[1024,1024]{1,0:T(8,128)} custom-call(bf16[256,2048]{1,0:T(8,128)(2,1)S(1)} %copy-done.7, bf16[512,2048]{1,0:T(8,128)(2,1)} %copy-done.1, bf16[256,2048]{1,0:T(8,128)(2,1)S(1)} %copy-done.9, bf16[256,2048]{1,0:T(8,128)(2,1)S(1)} %copy-done.23, bf16[512,2048]{1,0:T(8,128)(2,1)} %copy-done.2, ...), custom_call_target="tpu_custom_call", output_to_operand_aliasing={{}: (14, {})} | custom-call | flops 21474836 | bytes 83886 | tf_op jit(solution)/shard_map/pallas_call | solution.py:255
  (188 shorter events, 63.6 us)
Async XLA Ops:
  3.8 6.6 %collective-permute-start = (bf16[64,2048]{1,0:T(8,128)(2,1)}, bf16[64,2048]{1,0:T(8,128)(2,1)S(1)}, u32[]{:S(2)}, u32[]{:S(2)}) collective-permute-start(bf16[64,2048]{1,0:T(8,128)(2,1)} %get-tuple-element.54.a_ref), channel_id=1, source_target_pairs={{4,0},{5,1},{6,2},{7,3},{0,4},{1,5},{2,6},{3,7},{12,8},{13,9},{14,... | collective-permute-start | bytes 786440 | tf_op jit(solution)/shard_map/ppermute | solution.py:44
  5.3 9.7 %collective-permute-start.2 = (bf16[64,2048]{1,0:T(8,128)(2,1)}, bf16[64,2048]{1,0:T(8,128)(2,1)S(1)}, u32[]{:S(2)}, u32[]{:S(2)}) collective-permute-start(bf16[64,2048]{1,0:T(8,128)(2,1)} %get-tuple-element.55.a_ref), channel_id=1, source_target_pairs={{1,0},{0,1},{3,2},{2,3},{5,4},{4,5},{7,6},{6,7},{9,8},{8,9},{11,10... | collective-permute-start | bytes 786440 | tf_op jit(solution)/shard_map/ppermute | solution.py:44
  12.2 10.6 %collective-permute-start.1 = (bf16[128,2048]{1,0:T(8,128)(2,1)}, bf16[128,2048]{1,0:T(8,128)(2,1)S(1)}, u32[]{:S(2)}, u32[]{:S(2)}) collective-permute-start(bf16[128,2048]{1,0:T(8,128)(2,1)} %pad_maximum_fusion.1), channel_id=1, source_target_pairs={{12,0},{13,1},{14,2},{15,3},{8,4},{9,5},{10,6},{11,7},{4,8},{5,9},... | collective-permute-start | bytes 1572872 | tf_op jit(solution)/shard_map/ppermute | solution.py:44
  16.9 9.5 %collective-permute-start.3 = (bf16[128,2048]{1,0:T(8,128)(2,1)}, bf16[128,2048]{1,0:T(8,128)(2,1)}, u32[]{:S(2)}, u32[]{:S(2)}) collective-permute-start(bf16[128,2048]{1,0:T(8,128)(2,1)} %pad_maximum_fusion.2), channel_id=1, source_target_pairs={{3,0},{2,1},{1,2},{0,3},{7,4},{6,5},{5,6},{4,7},{11,8},{10,9},{9,1... | collective-permute-start | bytes 1572872 | tf_op jit(solution)/shard_map/ppermute | solution.py:44
  34.9 6.4 %collective-permute-start.4 = (bf16[256,2048]{1,0:T(8,128)(2,1)S(1)}, bf16[256,2048]{1,0:T(8,128)(2,1)S(1)}, u32[]{:S(2)}, u32[]{:S(2)}) collective-permute-start(bf16[256,2048]{1,0:T(8,128)(2,1)S(1)} %shard_map.78), channel_id=1, source_target_pairs={{16,0},{17,1},{18,2},{19,3},{20,4},{21,5},{22,6},{23,7},{24,8},{25... | collective-permute-start | bytes 3145736 | tf_op jit(solution)/shard_map/ppermute | solution.py:44
  35.0 23.3 %collective-permute-start.9 = (bf16[256,2048]{1,0:T(8,128)(2,1)S(1)}, bf16[256,2048]{1,0:T(8,128)(2,1)S(1)}, u32[]{:S(2)}, u32[]{:S(2)}) collective-permute-start(bf16[256,2048]{1,0:T(8,128)(2,1)S(1)} %copy-done.3), channel_id=1, source_target_pairs={{3,0},{2,1},{1,2},{0,3},{7,4},{6,5},{5,6},{4,7},{11,8},{10,9},{9,1... | collective-permute-start | bytes 3145736 | tf_op jit(solution)/shard_map/ppermute | solution.py:44
  36.7 26.4 %collective-permute-start.8 = (bf16[256,2048]{1,0:T(8,128)(2,1)S(1)}, bf16[256,2048]{1,0:T(8,128)(2,1)S(1)}, u32[]{:S(2)}, u32[]{:S(2)}) collective-permute-start(bf16[256,2048]{1,0:T(8,128)(2,1)S(1)} %copy-done.3), channel_id=1, source_target_pairs={{1,0},{0,1},{3,2},{2,3},{5,4},{4,5},{7,6},{6,7},{9,8},{8,9},{11,10... | collective-permute-start | bytes 3145736 | tf_op jit(solution)/shard_map/ppermute | solution.py:44
  39.7 23.3 %collective-permute-start.7 = (bf16[256,2048]{1,0:T(8,128)(2,1)S(1)}, bf16[256,2048]{1,0:T(8,128)(2,1)S(1)}, u32[]{:S(2)}, u32[]{:S(2)}) collective-permute-start(bf16[256,2048]{1,0:T(8,128)(2,1)S(1)} %copy-done.4), channel_id=1, source_target_pairs={{12,0},{13,1},{14,2},{15,3},{8,4},{9,5},{10,6},{11,7},{4,8},{5,9},... | collective-permute-start | bytes 3145736 | tf_op jit(solution)/shard_map/ppermute | solution.py:44
  41.3 21.7 %collective-permute-start.6 = (bf16[256,2048]{1,0:T(8,128)(2,1)S(1)}, bf16[256,2048]{1,0:T(8,128)(2,1)S(1)}, u32[]{:S(2)}, u32[]{:S(2)}) collective-permute-start(bf16[256,2048]{1,0:T(8,128)(2,1)S(1)} %copy-done.4), channel_id=1, source_target_pairs={{4,0},{5,1},{6,2},{7,3},{0,4},{1,5},{2,6},{3,7},{12,8},{13,9},{14,... | collective-permute-start | bytes 3145736 | tf_op jit(solution)/shard_map/ppermute | solution.py:44
  44.3 9.3 %collective-permute-start.5 = (bf16[128,2048]{1,0:T(8,128)(2,1)S(1)}, bf16[128,2048]{1,0:T(8,128)(2,1)S(1)}, u32[]{:S(2)}, u32[]{:S(2)}) collective-permute-start(bf16[128,2048]{1,0:T(8,128)(2,1)S(1)} %get-tuple-element.59), channel_id=1, source_target_pairs={{32,0},{33,1},{34,2},{35,3},{36,4},{37,5},{38,6},{39,7},{40,8},{41... | collective-permute-start | bytes 1572872 | tf_op jit(solution)/shard_map/ppermute | solution.py:44
  58.3 178.0 %copy-start.10 = (bf16[256,2048]{1,0:T(8,128)(2,1)}, bf16[256,2048]{1,0:T(8,128)(2,1)S(1)}, u32[]{:S(2)}) copy-start(bf16[256,2048]{1,0:T(8,128)(2,1)S(1)} %collective-permute-done.9.refs_1_.refs_2_.refs_8_) | copy-start | bytes 3145732
  63.0 173.2 %copy-start.12 = (bf16[256,2048]{1,0:T(8,128)(2,1)}, bf16[256,2048]{1,0:T(8,128)(2,1)S(1)}, u32[]{:S(2)}) copy-start(bf16[256,2048]{1,0:T(8,128)(2,1)S(1)} %collective-permute-done.8.refs_0_.refs_1_.refs_7_) | copy-start | bytes 3145732
  63.0 173.2 %copy-start.14 = (bf16[256,2048]{1,0:T(8,128)(2,1)}, bf16[256,2048]{1,0:T(8,128)(2,1)S(1)}, u32[]{:S(2)}) copy-start(bf16[256,2048]{1,0:T(8,128)(2,1)S(1)} %collective-permute-done.7.refs_0_.refs_5_.refs_11_) | copy-start | bytes 3145732
  63.0 173.2 %copy-start.16 = (bf16[256,2048]{1,0:T(8,128)(2,1)}, bf16[256,2048]{1,0:T(8,128)(2,1)S(1)}, u32[]{:S(2)}) copy-start(bf16[256,2048]{1,0:T(8,128)(2,1)S(1)} %collective-permute-done.6.refs_1_.refs_6_.refs_12_) | copy-start | bytes 3145732
  67.2 16.6 %collective-permute-start.12 = (bf16[512,2048]{1,0:T(8,128)(2,1)S(1)}, bf16[512,2048]{1,0:T(8,128)(2,1)S(1)}, u32[]{:S(2)}, u32[]{:S(2)}) collective-permute-start(bf16[512,2048]{1,0:T(8,128)(2,1)S(1)} %shard_map.80), channel_id=1, source_target_pairs={{16,0},{17,1},{18,2},{19,3},{20,4},{21,5},{22,6},{23,7},{24,8},{25... | collective-permute-start | bytes 6291464 | tf_op jit(solution)/shard_map/ppermute | solution.py:44
  67.3 8.5 %collective-permute-start.10 = (bf16[64,2048]{1,0:T(8,128)(2,1)S(1)}, bf16[64,2048]{1,0:T(8,128)(2,1)S(1)}, u32[]{:S(2)}, u32[]{:S(2)}) collective-permute-start(bf16[64,2048]{1,0:T(8,128)(2,1)S(1)} %slice.259), channel_id=1, source_target_pairs={{96,0},{97,1},{98,2},{99,3},{100,4},{101,5},{102,6},{103,7},{104,8... | collective-permute-start | bytes 786440 | tf_op jit(solution)/shard_map/ppermute | solution.py:44
  71.4 16.7 %collective-permute-start.13 = (bf16[256,2048]{1,0:T(8,128)(2,1)S(1)}, bf16[256,2048]{1,0:T(8,128)(2,1)S(1)}, u32[]{:S(2)}, u32[]{:S(2)}) collective-permute-start(bf16[256,2048]{1,0:T(8,128)(2,1)S(1)} %collective-permute-done.8.refs_0_.refs_1_.refs_7_), channel_id=1, source_target_pairs={{3,0},{2,1},{1,2},{0,3},{7,4},{6,5},{5,6},{4,7},{11,8},{10,9},{9,1... | collective-permute-start | bytes 3145736 | tf_op jit(solution)/shard_map/ppermute | solution.py:44
  71.7 16.4 %collective-permute-start.14 = (bf16[256,2048]{1,0:T(8,128)(2,1)S(1)}, bf16[256,2048]{1,0:T(8,128)(2,1)S(1)}, u32[]{:S(2)}, u32[]{:S(2)}) collective-permute-start(bf16[256,2048]{1,0:T(8,128)(2,1)S(1)} %collective-permute-done.6.refs_1_.refs_6_.refs_12_), channel_id=1, source_target_pairs={{12,0},{13,1},{14,2},{15,3},{8,4},{9,5},{10,6},{11,7},{4,8},{5,9},... | collective-permute-start | bytes 3145736 | tf_op jit(solution)/shard_map/ppermute | solution.py:44
  76.0 7.7 %collective-permute-start.11 = (bf16[64,2048]{1,0:T(8,128)(2,1)S(1)}, bf16[64,2048]{1,0:T(8,128)(2,1)S(1)}, u32[]{:S(2)}, u32[]{:S(2)}) collective-permute-start(bf16[64,2048]{1,0:T(8,128)(2,1)S(1)} %pad_maximum_fusion.9), channel_id=1, source_target_pairs={{96,0},{97,1},{98,2},{99,3},{100,4},{101,5},{102,6},{103,7},{104,8... | collective-permute-start | bytes 786440 | tf_op jit(solution)/shard_map/ppermute | solution.py:44
  83.7 9.3 %collective-permute-start.15 = (bf16[128,2048]{1,0:T(8,128)(2,1)S(1)}, bf16[128,2048]{1,0:T(8,128)(2,1)S(1)}, u32[]{:S(2)}, u32[]{:S(2)}) collective-permute-start(bf16[128,2048]{1,0:T(8,128)(2,1)S(1)} %pad_maximum_fusion.3), channel_id=1, source_target_pairs={{32,0},{33,1},{34,2},{35,3},{36,4},{37,5},{38,6},{39,7},{40,8},{41... | collective-permute-start | bytes 1572872 | tf_op jit(solution)/shard_map/ppermute | solution.py:44
  95.8 14.2 %collective-permute-start.20 = (bf16[256,2048]{1,0:T(8,128)(2,1)S(1)}, bf16[256,2048]{1,0:T(8,128)(2,1)S(1)}, u32[]{:S(2)}, u32[]{:S(2)}) collective-permute-start(bf16[256,2048]{1,0:T(8,128)(2,1)S(1)} %shard_map.82), channel_id=1, source_target_pairs={{16,0},{17,1},{18,2},{19,3},{20,4},{21,5},{22,6},{23,7},{24,8},{25... | collective-permute-start | bytes 3145736 | tf_op jit(solution)/shard_map/ppermute | solution.py:44
  95.9 17.1 %collective-permute-start.19 = (bf16[256,2048]{1,0:T(8,128)(2,1)S(1)}, bf16[256,2048]{1,0:T(8,128)(2,1)S(1)}, u32[]{:S(2)}, u32[]{:S(2)}) collective-permute-start(bf16[256,2048]{1,0:T(8,128)(2,1)S(1)} %constant_dynamic-update-slice_fusion.refs_0_.refs_8_), channel_id=1, source_target_pairs={{16,0},{17,1},{18,2},{19,3},{20,4},{21,5},{22,6},{23,7},{24,8},{25... | collective-permute-start | bytes 3145736 | tf_op jit(solution)/shard_map/ppermute | solution.py:44
  96.4 19.9 %collective-permute-start.18 = (bf16[256,2048]{1,0:T(8,128)(2,1)S(1)}, bf16[256,2048]{1,0:T(8,128)(2,1)S(1)}, u32[]{:S(2)}, u32[]{:S(2)}) collective-permute-start(bf16[256,2048]{1,0:T(8,128)(2,1)S(1)} %get-tuple-element.64), channel_id=1, source_target_pairs={{32,0},{33,1},{34,2},{35,3},{36,4},{37,5},{38,6},{39,7},{40,8},{41... | collective-permute-start | bytes 3145736 | tf_op jit(solution)/shard_map/ppermute | solution.py:44
  99.3 10.5 %collective-permute-start.16 = (bf16[128,2048]{1,0:T(8,128)(2,1)S(1)}, bf16[128,2048]{1,0:T(8,128)(2,1)S(1)}, u32[]{:S(2)}, u32[]{:S(2)}) collective-permute-start(bf16[128,2048]{1,0:T(8,128)(2,1)S(1)} %get-tuple-element.69), channel_id=1, source_target_pairs={{12,0},{13,1},{14,2},{15,3},{8,4},{9,5},{10,6},{11,7},{4,8},{5,9},... | collective-permute-start | bytes 1572872 | tf_op jit(solution)/shard_map/ppermute | solution.py:44
  110.0 10.2 %collective-permute-start.17 = (bf16[64,2048]{1,0:T(8,128)(2,1)S(1)}, bf16[64,2048]{1,0:T(8,128)(2,1)S(1)}, u32[]{:S(2)}, u32[]{:S(2)}) collective-permute-start(bf16[64,2048]{1,0:T(8,128)(2,1)S(1)} %slice.258), channel_id=1, source_target_pairs={{4,0},{5,1},{6,2},{7,3},{0,4},{1,5},{2,6},{3,7},{12,8},{13,9},{14,... | collective-permute-start | bytes 786440 | tf_op jit(solution)/shard_map/ppermute | solution.py:44
  116.0 9.3 %collective-permute-start.22 = (bf16[128,2048]{1,0:T(8,128)(2,1)S(1)}, bf16[128,2048]{1,0:T(8,128)(2,1)S(1)}, u32[]{:S(2)}, u32[]{:S(2)}) collective-permute-start(bf16[128,2048]{1,0:T(8,128)(2,1)S(1)} %get-tuple-element.76), channel_id=1, source_target_pairs={{3,0},{2,1},{1,2},{0,3},{7,4},{6,5},{5,6},{4,7},{11,8},{10,9},{9,1... | collective-permute-start | bytes 1572872 | tf_op jit(solution)/shard_map/ppermute | solution.py:44
  116.8 14.5 %collective-permute-start.21 = (bf16[128,2048]{1,0:T(8,128)(2,1)S(1)}, bf16[128,2048]{1,0:T(8,128)(2,1)S(1)}, u32[]{:S(2)}, u32[]{:S(2)}) collective-permute-start(bf16[128,2048]{1,0:T(8,128)(2,1)S(1)} %slice.251), channel_id=1, source_target_pairs={{96,0},{97,1},{98,2},{99,3},{100,4},{101,5},{102,6},{103,7},{104,8... | collective-permute-start | bytes 1572872 | tf_op jit(solution)/shard_map/ppermute | solution.py:44
  121.0 14.3 %collective-permute-start.28 = (bf16[128,2048]{1,0:T(8,128)(2,1)S(1)}, bf16[128,2048]{1,0:T(8,128)(2,1)S(1)}, u32[]{:S(2)}, u32[]{:S(2)}) collective-permute-start(bf16[128,2048]{1,0:T(8,128)(2,1)S(1)} %get-tuple-element.72), channel_id=1, source_target_pairs={{32,0},{33,1},{34,2},{35,3},{36,4},{37,5},{38,6},{39,7},{40,8},{41... | collective-permute-start | bytes 1572872 | tf_op jit(solution)/shard_map/ppermute | solution.py:44
  125.4 10.1 %collective-permute-start.24 = (bf16[64,2048]{1,0:T(8,128)(2,1)S(1)}, bf16[64,2048]{1,0:T(8,128)(2,1)S(1)}, u32[]{:S(2)}, u32[]{:S(2)}) collective-permute-start(bf16[64,2048]{1,0:T(8,128)(2,1)S(1)} %slice.257), channel_id=1, source_target_pairs={{1,0},{0,1},{3,2},{2,3},{5,4},{4,5},{7,6},{6,7},{9,8},{8,9},{11,10... | collective-permute-start | bytes 786440 | tf_op jit(solution)/shard_map/ppermute | solution.py:44
  131.8 13.4 %collective-permute-start.23 = (bf16[128,2048]{1,0:T(8,128)(2,1)S(1)}, bf16[128,2048]{1,0:T(8,128)(2,1)S(1)}, u32[]{:S(2)}, u32[]{:S(2)}) collective-permute-start(bf16[128,2048]{1,0:T(8,128)(2,1)S(1)} %pad_maximum_fusion.4), channel_id=1, source_target_pairs={{96,0},{97,1},{98,2},{99,3},{100,4},{101,5},{102,6},{103,7},{104,8... | collective-permute-start | bytes 1572872 | tf_op jit(solution)/shard_map/ppermute | solution.py:44
  135.4 15.4 %collective-permute-start.29 = (bf16[64,2048]{1,0:T(8,128)(2,1)S(1)}, bf16[64,2048]{1,0:T(8,128)(2,1)S(1)}, u32[]{:S(2)}, u32[]{:S(2)}) collective-permute-start(bf16[64,2048]{1,0:T(8,128)(2,1)S(1)} %slice.255), channel_id=1, source_target_pairs={{96,0},{97,1},{98,2},{99,3},{100,4},{101,5},{102,6},{103,7},{104,8... | collective-permute-start | bytes 786440 | tf_op jit(solution)/shard_map/ppermute | solution.py:44
  145.2 14.9 %collective-permute-start.25 = (bf16[256,2048]{1,0:T(8,128)(2,1)S(1)}, bf16[256,2048]{1,0:T(8,128)(2,1)S(1)}, u32[]{:S(2)}, u32[]{:S(2)}) collective-permute-start(bf16[256,2048]{1,0:T(8,128)(2,1)S(1)} %pad_maximum_fusion), channel_id=1, source_target_pairs={{32,0},{33,1},{34,2},{35,3},{36,4},{37,5},{38,6},{39,7},{40,8},{41... | collective-permute-start | bytes 3145736 | tf_op jit(solution)/shard_map/ppermute | solution.py:44
  151.0 16.7 %collective-permute-start.30 = (bf16[64,2048]{1,0:T(8,128)(2,1)S(1)}, bf16[64,2048]{1,0:T(8,128)(2,1)S(1)}, u32[]{:S(2)}, u32[]{:S(2)}) collective-permute-start(bf16[64,2048]{1,0:T(8,128)(2,1)S(1)} %pad_maximum_fusion.10), channel_id=1, source_target_pairs={{96,0},{97,1},{98,2},{99,3},{100,4},{101,5},{102,6},{103,7},{104,8... | collective-permute-start | bytes 786440 | tf_op jit(solution)/shard_map/ppermute | solution.py:44
  164.4 16.1 %collective-permute-start.26 = (bf16[256,2048]{1,0:T(8,128)(2,1)S(1)}, bf16[256,2048]{1,0:T(8,128)(2,1)S(1)}, u32[]{:S(2)}, u32[]{:S(2)}) collective-permute-start(bf16[256,2048]{1,0:T(8,128)(2,1)S(1)} %get-tuple-element.80), channel_id=1, source_target_pairs={{12,0},{13,1},{14,2},{15,3},{8,4},{9,5},{10,6},{11,7},{4,8},{5,9},... | collective-permute-start | bytes 3145736 | tf_op jit(solution)/shard_map/ppermute | solution.py:44
  167.6 15.4 %collective-permute-start.32 = (bf16[512,2048]{1,0:T(8,128)(2,1)S(1)}, bf16[512,2048]{1,0:T(8,128)(2,1)S(1)}, u32[]{:S(2)}, u32[]{:S(2)}) collective-permute-start(bf16[512,2048]{1,0:T(8,128)(2,1)S(1)} %constant_dynamic-update-slice_fusion.2.refs_0_.refs_9_.refs_1_), channel_id=1, source_target_pairs={{16,0},{17,1},{18,2},{19,3},{20,4},{21,5},{22,6},{23,7},{24,8},{25... | collective-permute-start | bytes 6291464 | tf_op jit(solution)/shard_map/ppermute | solution.py:44
  167.7 9.3 %collective-permute-start.31 = (bf16[128,2048]{1,0:T(8,128)(2,1)S(1)}, bf16[128,2048]{1,0:T(8,128)(2,1)S(1)}, u32[]{:S(2)}, u32[]{:S(2)}) collective-permute-start(bf16[128,2048]{1,0:T(8,128)(2,1)S(1)} %pad_maximum_fusion.5), channel_id=1, source_target_pairs={{32,0},{33,1},{34,2},{35,3},{36,4},{37,5},{38,6},{39,7},{40,8},{41... | collective-permute-start | bytes 1572872 | tf_op jit(solution)/shard_map/ppermute | solution.py:44
  177.0 16.0 %collective-permute-start.34 = (bf16[256,2048]{1,0:T(8,128)(2,1)S(1)}, bf16[256,2048]{1,0:T(8,128)(2,1)S(1)}, u32[]{:S(2)}, u32[]{:S(2)}) collective-permute-start(bf16[256,2048]{1,0:T(8,128)(2,1)S(1)} %constant_dynamic-update-slice_fusion.4.refs_0_.refs_10_.refs_2_), channel_id=1, source_target_pairs={{16,0},{17,1},{18,2},{19,3},{20,4},{21,5},{22,6},{23,7},{24,8},{25... | collective-permute-start | bytes 3145736 | tf_op jit(solution)/shard_map/ppermute | solution.py:44
  180.9 15.6 %collective-permute-start.27 = (bf16[128,2048]{1,0:T(8,128)(2,1)S(1)}, bf16[128,2048]{1,0:T(8,128)(2,1)S(1)}, u32[]{:S(2)}, u32[]{:S(2)}) collective-permute-start(bf16[128,2048]{1,0:T(8,128)(2,1)S(1)} %slice.250), channel_id=1, source_target_pairs={{4,0},{5,1},{6,2},{7,3},{0,4},{1,5},{2,6},{3,7},{12,8},{13,9},{14,... | collective-permute-start | bytes 1572872 | tf_op jit(solution)/shard_map/ppermute | solution.py:44
  190.1 12.9 %collective-permute-start.33 = (bf16[128,2048]{1,0:T(8,128)(2,1)S(1)}, bf16[128,2048]{1,0:T(8,128)(2,1)S(1)}, u32[]{:S(2)}, u32[]{:S(2)}) collective-permute-start(bf16[128,2048]{1,0:T(8,128)(2,1)S(1)} %get-tuple-element.87), channel_id=1, source_target_pairs={{12,0},{13,1},{14,2},{15,3},{8,4},{9,5},{10,6},{11,7},{4,8},{5,9},... | collective-permute-start | bytes 1572872 | tf_op jit(solution)/shard_map/ppermute | solution.py:44
  195.9 12.1 %collective-permute-start.36 = (bf16[128,2048]{1,0:T(8,128)(2,1)S(1)}, bf16[128,2048]{1,0:T(8,128)(2,1)S(1)}, u32[]{:S(2)}, u32[]{:S(2)}) collective-permute-start(bf16[128,2048]{1,0:T(8,128)(2,1)S(1)} %get-tuple-element.92), channel_id=1, source_target_pairs={{3,0},{2,1},{1,2},{0,3},{7,4},{6,5},{5,6},{4,7},{11,8},{10,9},{9,1... | collective-permute-start | bytes 1572872 | tf_op jit(solution)/shard_map/ppermute | solution.py:44
  196.6 22.6 %collective-permute-start.39 = (bf16[256,2048]{1,0:T(8,128)(2,1)S(1)}, bf16[256,2048]{1,0:T(8,128)(2,1)S(1)}, u32[]{:S(2)}, u32[]{:S(2)}) collective-permute-start(bf16[256,2048]{1,0:T(8,128)(2,1)S(1)} %get-tuple-element.97), channel_id=1, source_target_pairs={{3,0},{2,1},{1,2},{0,3},{7,4},{6,5},{5,6},{4,7},{11,8},{10,9},{9,1... | collective-permute-start | bytes 3145736 | tf_op jit(solution)/shard_map/ppermute | solution.py:44
  203.2 12.9 %collective-permute-start.35 = (bf16[64,2048]{1,0:T(8,128)(2,1)S(1)}, bf16[64,2048]{1,0:T(8,128)(2,1)S(1)}, u32[]{:S(2)}, u32[]{:S(2)}) collective-permute-start(bf16[64,2048]{1,0:T(8,128)(2,1)S(1)} %slice.254), channel_id=1, source_target_pairs={{4,0},{5,1},{6,2},{7,3},{0,4},{1,5},{2,6},{3,7},{12,8},{13,9},{14,... | collective-permute-start | bytes 786440 | tf_op jit(solution)/shard_map/ppermute | solution.py:44
  208.1 15.7 %collective-permute-start.41 = (bf16[64,2048]{1,0:T(8,128)(2,1)S(1)}, bf16[64,2048]{1,0:T(8,128)(2,1)S(1)}, u32[]{:S(2)}, u32[]{:S(2)}) collective-permute-start(bf16[64,2048]{1,0:T(8,128)(2,1)S(1)} %slice.252), channel_id=1, source_target_pairs={{1,0},{0,1},{3,2},{2,3},{5,4},{4,5},{7,6},{6,7},{9,8},{8,9},{11,10... | collective-permute-start | bytes 786440 | tf_op jit(solution)/shard_map/ppermute | solution.py:44
  219.6 14.9 %collective-permute-start.40 = (bf16[128,2048]{1,0:T(8,128)(2,1)S(1)}, bf16[128,2048]{1,0:T(8,128)(2,1)S(1)}, u32[]{:S(2)}, u32[]{:S(2)}) collective-permute-start(bf16[128,2048]{1,0:T(8,128)(2,1)S(1)} %slice.249), channel_id=1, source_target_pairs={{1,0},{0,1},{3,2},{2,3},{5,4},{4,5},{7,6},{6,7},{9,8},{8,9},{11,10... | collective-permute-start | bytes 1572872 | tf_op jit(solution)/shard_map/ppermute | solution.py:44
  222.8 19.0 %collective-permute-start.37 = (bf16[128,2048]{1,0:T(8,128)(2,1)S(1)}, bf16[128,2048]{1,0:T(8,128)(2,1)S(1)}, u32[]{:S(2)}, u32[]{:S(2)}) collective-permute-start(bf16[128,2048]{1,0:T(8,128)(2,1)S(1)} %pad_maximum_fusion.6), channel_id=1, source_target_pairs={{3,0},{2,1},{1,2},{0,3},{7,4},{6,5},{5,6},{4,7},{11,8},{10,9},{9,1... | collective-permute-start | bytes 1572872 | tf_op jit(solution)/shard_map/ppermute | solution.py:44
  234.7 11.5 %collective-permute-start.42 = (bf16[128,2048]{1,0:T(8,128)(2,1)S(1)}, bf16[128,2048]{1,0:T(8,128)(2,1)S(1)}, u32[]{:S(2)}, u32[]{:S(2)}) collective-permute-start(bf16[128,2048]{1,0:T(8,128)(2,1)S(1)} %pad_maximum_fusion.7), channel_id=1, source_target_pairs={{12,0},{13,1},{14,2},{15,3},{8,4},{9,5},{10,6},{11,7},{4,8},{5,9},... | collective-permute-start | bytes 1572872 | tf_op jit(solution)/shard_map/ppermute | solution.py:44
  243.7 21.0 %collective-permute-start.38 = (bf16[64,2048]{1,0:T(8,128)(2,1)}, bf16[64,2048]{1,0:T(8,128)(2,1)S(1)}, u32[]{:S(2)}, u32[]{:S(2)}) collective-permute-start(bf16[64,2048]{1,0:T(8,128)(2,1)} %fusion.9), channel_id=1, source_target_pairs={{1,0},{0,1},{3,2},{2,3},{5,4},{4,5},{7,6},{6,7},{9,8},{8,9},{11,10... | collective-permute-start | bytes 786440 | tf_op jit(solution)/shard_map/ppermute | solution.py:44
  248.0 16.7 %collective-permute-start.43 = (bf16[64,2048]{1,0:T(8,128)(2,1)}, bf16[64,2048]{1,0:T(8,128)(2,1)}, u32[]{:S(2)}, u32[]{:S(2)}) collective-permute-start(bf16[64,2048]{1,0:T(8,128)(2,1)} %fusion.6), channel_id=1, source_target_pairs={{4,0},{5,1},{6,2},{7,3},{0,4},{1,5},{2,6},{3,7},{12,8},{13,9},{14,... | collective-permute-start | bytes 786440 | tf_op jit(solution)/shard_map/ppermute | solution.py:44
  (32 other events, 753.1 us)

commit v4 on v3

v4 whole, which is shorter than its diff:
```python
import functools
import math

import jax
import jax.numpy as jnp
from jax import lax
from jax.experimental import pallas as pl
from jax.experimental.pallas import tpu as pltpu
from jax.sharding import PartitionSpec as P

AXES = ("row", "col", "dp")
RING = 4
PARTS = 2
BF = jnp.bfloat16
F32 = jnp.float32
NN = (((1,), (0,)), ((), ()))
NT = (((1,), (1,)), ((), ()))
TN = (((0,), (0,)), ((), ()))


def cost(flops, bytes_accessed, transcendentals):
    return pl.CostEstimate(
        flops=flops // 100, bytes_accessed=bytes_accessed // 100, transcendentals=transcendentals
    )


def gelu_parts(pre):
    cdf = 0.5 * (1.0 + jax.scipy.special.erf(pre * (1.0 / math.sqrt(2.0))))
    activated = pre * cdf
    slope = cdf + pre * jnp.exp(-0.5 * pre * pre) * (1.0 / math.sqrt(2.0 * math.pi))
    return (activated, slope)


def flat(z, c, x, y):
    return ((z * 2 + c) * RING + x) * RING + y


def exchange(array, partner):
    pairs = []
    for z in range(RING):
        for c in range(2):
            for x in range(RING):
                for y in range(RING):
                    pairs.append((flat(*partner(z, c, x, y)), flat(z, c, x, y)))
    return lax.ppermute(array, AXES, pairs)


NEAR = ((1, 3), (3, 1))
Z_PAIR = ((1, 3), (3, 1))
OWNER_SLOT = ((0, 2, 3, 1), (0, 1, 3, 2))


def along(keep, first, turn):
    def partner(z, c, x, y):
        half = c if keep else 1 - c
        step = NEAR[c][turn]
        if (half == 0) == first:
            return (z, c, x ^ step, y)
        return (z, c, x, y ^ step)

    return partner


def along_z(turn):
    return lambda z, c, x, y: (z ^ Z_PAIR[c][turn], c, x, y)


def other_core(z, c, x, y):
    return (z, 1 - c, x, y)


def slot_of(keep, place_ref, i):
    z, core = place_ref[0], place_ref[1]

    def one(c):
        near = NEAR[c]
        owned = z ^ (0, near[0], near[1], near[0] ^ near[1])[i]
        table = OWNER_SLOT[c if keep else 1 - c]
        slot = jnp.int32(table[0])
        for j in range(1, RING):
            slot = jnp.where(owned == j, table[j], slot)
        return slot

    return jnp.where(core == 0, one(0), one(1))


def arrival_of(keep, place_ref, i):
    z, core = place_ref[0], place_ref[1]

    def one(c):
        near = NEAR[c]
        arrival = (0, near[0], near[1], near[0] ^ near[1])
        owned = z ^ OWNER_SLOT[c if keep else 1 - c].index(i)
        place = jnp.int32(arrival.index(0))
        for j in range(1, RING):
            place = jnp.where(owned == j, arrival.index(j), place)
        return place

    return jnp.where(core == 0, one(0), one(1))


def cut_kernel(place_ref, tokens_ref, grad_ref, kept_ref, passed_ref):
    block, wide = kept_ref.shape[0], tokens_ref.shape[1]
    core = place_ref[1]
    for ref, which in ((kept_ref, core), (passed_ref, 1 - core)):
        rows = pl.ds(pl.multiple_of(which * block, block), block)
        ref[:, :wide] = tokens_ref[rows, :]
        ref[:, wide:] = grad_ref[rows, :]


def cut(place, tokens, out_grad):
    rows, wide = tokens.shape
    half = jax.ShapeDtypeStruct((rows // 2, 2 * wide), BF)
    return pl.pallas_call(
        cut_kernel,
        grid_spec=pltpu.PrefetchScalarGridSpec(
            num_scalar_prefetch=1,
            grid=(1,),
            in_specs=[pl.BlockSpec((rows, wide), lambda i, place: (0, 0))] * 2,
            out_specs=[pl.BlockSpec((rows // 2, 2 * wide), lambda i, place: (0, 0))] * 2,
        ),
        out_shape=[half, half],
        cost_estimate=cost(flops=0, bytes_accessed=8 * rows * wide, transcendentals=0),
    )(place, tokens, out_grad)


def assemble_kernel(keep, place_ref, a_ref, b_ref, c_ref, *out_refs):
    rows = a_ref.shape[0]
    part = rows // PARTS

    def put(i, ref, first):
        at = pl.multiple_of(slot_of(keep, place_ref, i) * part, part)
        for j, out_ref in enumerate(out_refs):
            out_ref[pl.ds(at, part), :] = ref[first + j * part:first + (j + 1) * part, :]

    put(0, a_ref, 0)
    put(1, b_ref, 0)
    put(2, c_ref, 0)
    put(3, c_ref, rows)


def assemble(keep, place, a, b, c):
    rows, wide = a.shape
    tiles = 2
    spec = lambda n: pl.BlockSpec((n, wide // tiles), lambda i, place: (0, i))
    out_rows = RING * rows // PARTS
    return pl.pallas_call(
        functools.partial(assemble_kernel, keep),
        grid_spec=pltpu.PrefetchScalarGridSpec(
            num_scalar_prefetch=1,
            grid=(tiles,),
            in_specs=[spec(rows), spec(rows), spec(2 * rows)],
            out_specs=[spec(out_rows)] * PARTS,
        ),
        out_shape=[jax.ShapeDtypeStruct((out_rows, wide), BF)] * PARTS,
        cost_estimate=cost(flops=0, bytes_accessed=16 * rows * wide, transcendentals=0),
    )(place, a, b, c)


def order_of(keep):
    return (0, 1, 2, 3) if keep else (0, 2, 1, 3)


def panel_at(piece, slot):
    return piece // 2, (piece % 2) * RING + slot


def hidden_at(keep, piece, slot):
    return slot // 2, (slot % 2) * RING + order_of(keep).index(piece)


def pair_kernel(keep, hidden, added, split, block, place_ref, *refs):
    a_refs, (left_ref, right_ref), rest = refs[:2], refs[2:4], refs[4:]
    if added:
        more_ref, rest = rest[0], rest[1:]
    rows_ref = rest[-1]
    out_refs = rest[:-1]

    @pl.when(pl.program_id(1) == 0)
    def _():
        if hidden:
            size = RING * block
            for i in range(RING):
                at = pl.multiple_of(arrival_of(keep, place_ref, i) * size, size)
                first = (i % 2) * size
                rows_ref[pl.ds(at, size), :] = a_refs[i // 2][first:first + size, :]
        else:
            for i in range(RING):
                for j, piece in enumerate(order_of(keep)):
                    which, first = panel_at(piece, i)
                    at = (i * RING + j) * block
                    rows_ref[at:at + block, :] = a_refs[which][first * block:(first + 1) * block, :]

    def finish(total):
        if added:
            total = total + more_ref[...].astype(F32)
        total = total.astype(BF)
        if not split:
            out_refs[0][...] = total
        else:
            half = total.shape[0] // 2
            out_refs[0][...] = total[:half]
            out_refs[1][...] = total[half:]

    @pl.when(pl.program_id(0) == 0)
    def _():
        finish(lax.dot_general(rows_ref[...], left_ref[...], NN, preferred_element_type=F32))

    @pl.when(pl.program_id(0) == 1)
    def _():
        finish(lax.dot_general(rows_ref[...], right_ref[...], NT, preferred_element_type=F32))


def pair_dot(keep, hidden, pair, left, right, place, more=None, split=True, tile=512):
    rows = sum(a.shape[0] for a in pair)
    block = rows // RING // RING
    depth, wide = left.shape
    tiles = wide // tile
    in_specs = [pl.BlockSpec((a.shape[0], depth), lambda h, n, place: (0, h)) for a in pair]
    in_specs += [
        pl.BlockSpec((depth, tile), lambda h, n, place: (0, n * (1 - h) + (tiles - 1) * h)),
        pl.BlockSpec((tile, depth), lambda h, n, place: (n * h, 0)),
    ]
    out_of = lambda n_rows: pl.BlockSpec((n_rows, tile), lambda h, n, place: (0, h * tiles + n))
    args = [*pair, left, right]
    if more is not None:
        in_specs.append(out_of(rows))
        args.append(more)
    outs = [rows // 2, rows // 2] if split else [rows]
    result = pl.pallas_call(
        functools.partial(pair_kernel, keep, hidden, more is not None, split, block),
        grid_spec=pltpu.PrefetchScalarGridSpec(
            num_scalar_prefetch=1,
            grid=(2, tiles),
            in_specs=in_specs,
            out_specs=[out_of(n) for n in outs],
            scratch_shapes=[pltpu.VMEM((rows, depth), BF)],
        ),
        out_shape=[jax.ShapeDtypeStruct((n, 2 * wide), BF) for n in outs],
        compiler_params=pltpu.CompilerParams(vmem_limit_bytes=18 * 2**20),
        cost_estimate=cost(
            flops=4 * rows * depth * wide,
            bytes_accessed=4 * depth * wide + 8 * rows * wide,
            transcendentals=0,
        ),
    )(place, *args)
    return result if split else result[0]


def grad_kernel(pairs, block, factor, begun, *refs):
    lefts, rights, out_ref = refs[:4], refs[4:8], refs[-1]
    total = None
    for i, blocks in enumerate(pairs):
        right = jnp.concatenate(
            [rights[j][first * block:(first + 1) * block, :] for j, first in blocks], axis=0
        )
        term = lax.dot_general(lefts[i][...], right, TN, preferred_element_type=F32)
        total = term if total is None else total + term
    total = total * factor
    out_ref[...] = total + refs[8][...] if begun else total


def grad_dot(lefts, left_part, rights, right_part, pairs, factor, begun=None, tile=256):
    wide = lefts[0].shape[1] // 2
    tiles = wide // tile
    tokens = sum(a.shape[0] for a in lefts)
    args = [*lefts, *rights]
    in_specs = [pl.BlockSpec((a.shape[0], wide), lambda n: (0, left_part)) for a in lefts]
    in_specs += [
        pl.BlockSpec((a.shape[0], tile), lambda n: (0, right_part * tiles + n)) for a in rights
    ]
    out_spec = pl.BlockSpec((wide, tile), lambda n: (0, n))
    aliases = {}
    if begun is not None:
        aliases = {len(args): 0}
        args.append(begun)
        in_specs.append(out_spec)
    block = rights[0].shape[0] // (2 * RING)
    return pl.pallas_call(
        functools.partial(grad_kernel, pairs, block, factor, begun is not None),
        grid=(tiles,),
        in_specs=in_specs,
        out_specs=out_spec,
        out_shape=jax.ShapeDtypeStruct((wide, wide), F32),
        input_output_aliases=aliases,
        compiler_params=pltpu.CompilerParams(vmem_limit_bytes=24 * 2**20),
        cost_estimate=cost(
            flops=2 * tokens * wide * wide,
            bytes_accessed=3 * tokens * wide + 2 * wide * wide,
            transcendentals=0,
        ),
    )(*args)


def after(value, *events):
    return lax.optimization_barrier((value, *events))[0]


def shards(tokens, out_grad, weight_in, weight_out):
    core = lax.axis_index("row") % 2
    z = lax.axis_index("row") // 2
    dp = lax.axis_index("dp")
    rows, width = tokens.shape
    block = rows // 2
    inner = weight_in.shape[1] // 2
    factor = 1.0 / math.sqrt(rows * 16)
    both_ways = (True, False)

    place = jnp.stack([z, core]).astype(jnp.int32)
    w_in = lax.dynamic_slice_in_dim(weight_in, dp * inner, inner, 1)
    w_out = lax.dynamic_slice_in_dim(weight_out, dp * inner, inner, 0)

    order = (False, True)
    start, one, two, own_a, own_b = {}, {}, {}, {}, {}
    start[True], start[False] = cut(place, tokens, out_grad)
    for keep in order:
        one[keep] = exchange(start[keep], along(keep, True, 0))
    for keep in order:
        pair = jnp.concatenate([start[keep], one[keep]], axis=0)
        two[keep] = exchange(pair, along(keep, True, 1))
    for keep in order:
        own_a[keep], own_b[keep] = assemble(keep, place, start[keep], one[keep], two[keep])

    def every(values, *events):
        both = lax.optimization_barrier((values[True], values[False], *events))
        return {True: both[0], False: both[1]}

    def neighbours(own):
        near = {keep: exchange(own[keep], along(keep, False, 0)) for keep in order}
        return {keep: jnp.concatenate([own[keep], near[keep]], axis=0) for keep in order}

    def others(near):
        return {keep: exchange(near[keep], along(keep, False, 1)) for keep in order}

    def panel_dot(keep, near, rest, *events, more=None):
        pair = [near[keep], rest[keep]]
        pair[0] = after(pair[0], *events) if events else pair[0]
        return pair_dot(keep, False, pair, w_in, w_out, place, more=more, split=keep)

    def out_dot(keep, pair, *events):
        pair = list(pair)
        pair[1] = after(pair[1], *events) if events else pair[1]
        return pair_dot(keep, True, pair, w_out, w_in, place)

    def halfway(kept, got):
        half = kept.shape[0] // 2
        sums = kept.astype(F32) + got.astype(F32)
        return [sums[:half], sums[half:]]

    def hidden_of(value):
        pre, back = value[:, :width], value[:, width:]
        activated, slope = gelu_parts(pre)
        return jnp.concatenate([activated.astype(BF), (back * slope).astype(BF)], axis=1)

    near_a = neighbours(every(own_a))
    rest_a = others(near_a)
    near_b = neighbours(every(own_b, near_a[True], near_a[False]))
    sent_a = panel_dot(False, near_a, rest_a, near_b[True], near_b[False])
    kept_a, send_a = panel_dot(True, near_a, rest_a, more=exchange(sent_a, other_core))
    step_a = exchange(send_a, along_z(0))
    rest_b = others(near_b)
    sent_b = panel_dot(False, near_b, rest_b, send_a)
    kept_b, send_b = panel_dot(True, near_b, rest_b, more=exchange(sent_b, other_core))
    step_b = exchange(send_b, along_z(0))

    half_a = halfway(kept_a, step_a)
    turn_a = exchange(after(half_a[1].astype(BF), send_b), along_z(1))
    half_b = halfway(kept_b, step_b)
    mine_a = hidden_of(half_a[0] + turn_a.astype(F32))
    next_a = exchange(mine_a, along_z(1))
    turn_b = exchange(after(half_b[1].astype(BF), mine_a), along_z(1))
    pair_a = jnp.concatenate([mine_a, next_a], axis=0)
    far_a = exchange(pair_a, along_z(0))
    mine_b = hidden_of(half_b[0] + turn_b.astype(F32))
    next_b = exchange(mine_b, along_z(1))
    pair_b = jnp.concatenate([mine_b, next_b], axis=0)
    far_b = exchange(pair_b, along_z(0))
    far_a = after(far_a, pair_b)
    hid_a = {True: (pair_a, far_a)}
    hid_a[False] = (exchange(pair_a, other_core), exchange(far_a, other_core))
    hid_b = {True: (pair_b, far_b)}
    hid_b[False] = (exchange(pair_b, other_core), exchange(far_b, other_core))

    in_pairs, out_pairs = [], []
    for base, keep in ((0, True), (2, False)):
        for i in range(2):
            in_pairs.append(
                tuple(
                    (base + hidden_at(keep, 2 * i + p, slot)[0], hidden_at(keep, 2 * i + p, slot)[1])
                    for p in range(2)
                    for slot in range(RING)
                )
            )
            out_pairs.append(
                tuple(
                    (base + panel_at(piece, 2 * i + s)[0], panel_at(piece, 2 * i + s)[1])
                    for s in range(2)
                    for piece in order_of(keep)
                )
            )

    def grads(which, near, rest, hid, begun, *events):
        panels = [near[True], rest[True], near[False], rest[False]]
        hiddens = [*hid[True], *hid[False]]
        lefts, rights, pairs = (
            (panels, hiddens, in_pairs) if which == 0 else (hiddens, panels, out_pairs)
        )
        lefts[0] = after(lefts[0], *events)
        return grad_dot(lefts, 0, rights, 1, pairs, factor, begun)

    def first_half(keep, kept, passed):
        return halfway(kept, exchange(passed, along(keep, True, 1)))

    def first_sum(keep, sums, *events):
        passed = sums[1].astype(BF)
        passed = after(passed, *events) if events else passed
        return sums[0] + exchange(passed, along(keep, True, 0)).astype(F32)

    out_a, out_b, sums_a, sums_b, total_a, total_b = {}, {}, {}, {}, {}, {}
    out_a[True] = out_dot(True, hid_a[True])
    out_a[False] = out_dot(False, hid_a[False], out_a[True][0])
    grad_in = grads(0, near_a, rest_a, hid_a, None, out_a[False][0])
    for keep in both_ways:
        sums_a[keep] = first_half(keep, *out_a[keep])
    out_b[True] = out_dot(True, hid_b[True], grad_in, sums_a[True][0], sums_a[False][0])
    out_b[False] = out_dot(False, hid_b[False], out_b[True][0])
    for keep in both_ways:
        total_a[keep] = first_sum(keep, sums_a[keep])
    grad_out = grads(1, near_a, rest_a, hid_a, None, out_b[False][0])
    for keep in both_ways:
        sums_b[keep] = first_half(keep, *out_b[keep])
    for keep in both_ways:
        total_b[keep] = first_sum(keep, sums_b[keep], grad_out, total_a[True], total_a[False])
    grad_in = grads(0, near_b, rest_b, hid_b, grad_in, sums_b[True][0], sums_b[False][0])

    part = block // PARTS
    pick = lambda keep, piece: jnp.concatenate(
        [
            total[keep][order_of(keep).index(piece) * part:(order_of(keep).index(piece) + 1) * part]
            for total in (total_a, total_b)
        ],
        axis=0,
    )
    gots, done = {}, {}
    for keep in both_ways:
        passed = jnp.concatenate([pick(keep, 2), pick(keep, 3)], axis=0).astype(BF)
        gots[keep] = exchange(after(passed, grad_in), along(keep, False, 1))
    grad_out = grads(1, near_b, rest_b, hid_b, grad_out, grad_in)
    for keep in both_ways:
        got = gots[keep].astype(F32)
        last = after((pick(keep, 1) + got[block:]).astype(BF), grad_out)
        done[keep] = (
            pick(keep, 0) + got[:block] + exchange(last, along(keep, False, 0)).astype(F32)
        ).astype(BF)

    low = jnp.where(core == 0, done[True], done[False])
    high = jnp.where(core == 0, done[False], done[True])
    result = jnp.concatenate([low, high], axis=0)
    return (result[:, :width], result[:, width:], grad_in, grad_out)


def solution(mesh):
    placed = (P(("col", "dp"), "row"), P(("col", "dp"), "row"), P("row", "col"), P("col", "row"))
    return jax.shard_map(
        shards,
        mesh=mesh,
        in_specs=placed,
        out_specs=(
            P(("col", "dp"), "row"),
            P(("col", "dp"), "row"),
            P("row", ("col", "dp")),
            P(("col", "dp"), "row"),
        ),
        check_vma=False,
    )
```

time: 269 us -> 288 us (1.071)
  waiting for transfers between devices: 94.5 us -> 146 us
  local copies, waits for them, and re-layouts: 21.5 us -> 6.75 us
  starting transfers between devices: 67.9 us -> 57.2 us
  Pallas kernels: 68.6 us -> 65.3 us
    ppermute x44 -> x38, waiting for transfers between devices: 94.5 us -> 146 us  [exchange(): return lax.ppermute(array, AXES, pairs)]
    unnamed x75 -> x20, local copies, waits for them, and re-layouts: 16.9 us -> 3.85 us
    ppermute x44 -> x38, starting transfers between devices: 67.9 us -> 57.2 us  [exchange(): return lax.ppermute(array, AXES, pairs)]
    pallas_call x16 -> x12, Pallas kernels: 60.5 us -> 57.1 us  [the longest x8 34.7 us: pair_dot(): pl.pallas_call(functools.partial(pair_kernel, keep, hidden, more is not N...]
  transfers between devices with their start and end apart: 44 -> 38, of which waited for: 19 -> 22; matrix products, arithmetic and copies ran while one was open for 6% -> 4% of each run, Pallas kernels for 20% -> 15%
where the time goes in v4:
time: 288 us; the launch traced here: 287 us
  waiting for transfers between devices  146 us (51%)
  Pallas kernels  65.3 us (23%)
  starting transfers between devices  57.2 us (20%)
  other arithmetic  10.3 us (4%)
  local copies, waits for them, and re-layouts  6.75 us (2%)
    ppermute x38, waiting for transfers between devices, exchange(): return lax.ppermute(array, AXES, pairs)  146 us
    ppermute x38, starting transfers between devices, exchange(): return lax.ppermute(array, AXES, pairs)  57.2 us
    pallas_call x8, Pallas kernels, pair_dot(): pl.pallas_call(functools.partial(pair_kernel, keep, hidden, more is not N...  34.7 us
    pallas_call x4, Pallas kernels, grad_dot(): pl.pallas_call(functools.partial(grad_kernel, pairs, block, factor, begun...  22.4 us
  transfers between devices with their start and end apart: 38, of which 22 were waited for; matrix products, arithmetic and copies ran while one was open for 4% of the time, Pallas kernels for 15%

profile of v4, /device:TPU:8, one launch (start us, length us, event | category | flops | bytes accessed | tf_op | source)
XLA Modules:
  0.0 287.0 jit_solution(4403639351244056029)
XLA Ops:
  1.2 2.5 shard_map.75
  5.7 4.6 %collective-permute-done.2.b_ref = bf16[64,2048]{1,0:T(8,128)(2,1)S(1)} collective-permute-done((bf16[64,2048]{1,0:T(8,128)(2,1)}, bf16[64,2048]{1,0:T(8,128)(2,1)S(1)}, u32[]{:S(2)}, u32[]{:S(2)}) %collective-permute-start.2) | collective-permute-done | bytes 262176 | tf_op jit(solution)/shard_map/ppermute | solution.py:45
  14.2 2.8 collective-permute-start.1
  17.0 3.7 %collective-permute-done.3.c_ref = bf16[128,2048]{1,0:T(8,128)(2,1)S(1)} collective-permute-done((bf16[128,2048]{1,0:T(8,128)(2,1)S(1)}, bf16[128,2048]{1,0:T(8,128)(2,1)S(1)}, u32[]{:S(2)}, u32[]{:S(2)}) %collective-permute-start.3) | collective-permute-done | bytes 524320 | tf_op jit(solution)/shard_map/ppermute | solution.py:45
  21.5 2.8 shard_map.77
  25.5 2.9 %shard_map.76 = (bf16[128,2048]{1,0:T(8,128)(2,1)}, bf16[128,2048]{1,0:T(8,128)(2,1)}) custom-call(s32[2]{0:T(128)} %pad_add_fusion.place_ref, bf16[64,2048]{1,0:T(8,128)(2,1)} %get-tuple-element.44.a_ref, bf16[64,2048]{1,0:T(8,128)(2,1)} %copy-done.2, bf16[128,2048]{1,0:T(8,128)(2,1)} %copy-done.6), custom_call_target="tpu_custom_call" | custom-call | bytes 20971 | tf_op jit(solution)/shard_map/pallas_call | solution.py:147
  33.3 4.4 %collective-permute-done.6 = bf16[128,2048]{1,0:T(8,128)(2,1)S(1)} collective-permute-done((bf16[128,2048]{1,0:T(8,128)(2,1)}, bf16[128,2048]{1,0:T(8,128)(2,1)S(1)}, u32[]{:S(2)}, u32[]{:S(2)}) %collective-permute-start.6) | collective-permute-done | bytes 524320 | tf_op jit(solution)/shard_map/ppermute | solution.py:45
  37.8 2.8 collective-permute-start.9
  40.8 2.1 constant_dynamic-slice_fusion
  43.0 2.4 collective-permute-start.7
  45.4 4.5 %collective-permute-done.8 = bf16[128,2048]{1,0:T(8,128)(2,1)S(1)} collective-permute-done((bf16[128,2048]{1,0:T(8,128)(2,1)S(1)}, bf16[128,2048]{1,0:T(8,128)(2,1)S(1)}, u32[]{:S(2)}, u32[]{:S(2)}) %collective-permute-start.8) | collective-permute-done | bytes 524320 | tf_op jit(solution)/shard_map/ppermute | solution.py:45
  50.0 5.7 %collective-permute-done.7 = bf16[128,2048]{1,0:T(8,128)(2,1)S(1)} collective-permute-done((bf16[128,2048]{1,0:T(8,128)(2,1)S(1)}, bf16[128,2048]{1,0:T(8,128)(2,1)S(1)}, u32[]{:S(2)}, u32[]{:S(2)}) %collective-permute-start.7) | collective-permute-done | bytes 524320 | tf_op jit(solution)/shard_map/ppermute | solution.py:45
  55.8 3.7 %collective-permute-done.9.refs_1_.refs_3_.refs_7_ = bf16[256,2048]{1,0:T(8,128)(2,1)S(1)} collective-permute-done((bf16[256,2048]{1,0:T(8,128)(2,1)S(1)}, bf16[256,2048]{1,0:T(8,128)(2,1)S(1)}, u32[]{:S(2)}, u32[]{:S(2)}) %collective-permute-start.9) | collective-permute-done | bytes 1048608 | tf_op jit(solution)/shard_map/ppermute | solution.py:45
  59.5 4.3 %shard_map.78 = bf16[512,2048]{1,0:T(8,128)(2,1)S(1)} custom-call(s32[2]{0:T(128)S(1)} %copy-done, bf16[256,2048]{1,0:T(8,128)(2,1)S(1)} %constant_dynamic-update-slice_fusion.2.refs_0_.refs_2_.refs_6_, bf16[256,2048]{1,0:T(8,128)(2,1)S(1)} %collective-permute-done.9.refs_1_.refs_3_.refs_7_, bf16[1024,1024]{1,0:T(8,128)(2,1)S(1)} %get-tuple-element.118.refs_2_.refs_3_, ...), custom_call_target="tpu_custom_call" | custom-call | flops 21474836 | bytes 83886 | tf_op jit(solution)/shard_map/pallas_call | solution.py:230
  65.1 2.8 collective-permute-start.13
  67.9 10.8 %collective-permute-done.5.refs_1_.refs_5_ = bf16[256,2048]{1,0:T(8,128)(2,1)S(1)} collective-permute-done((bf16[256,2048]{1,0:T(8,128)(2,1)S(1)}, bf16[256,2048]{1,0:T(8,128)(2,1)S(1)}, u32[]{:S(2)}, u32[]{:S(2)}) %collective-permute-start.5) | collective-permute-done | bytes 1048608 | tf_op jit(solution)/shard_map/ppermute | solution.py:45
  78.7 4.4 %shard_map.79 = (bf16[256,2048]{1,0:T(8,128)(2,1)S(1)}, bf16[256,2048]{1,0:T(8,128)(2,1)S(1)}) custom-call(s32[2]{0:T(128)S(1)} %copy-done, bf16[256,2048]{1,0:T(8,128)(2,1)S(1)} %constant_dynamic-update-slice_fusion.refs_0_.refs_4_, bf16[256,2048]{1,0:T(8,128)(2,1)S(1)} %collective-permute-done.5.refs_1_.refs_5_, ...), custom_call_target="tpu_custom_call" | custom-call | flops 21474836 | bytes 83886 | tf_op jit(solution)/shard_map/pallas_call | solution.py:230
  83.2 4.3 %shard_map.80 = bf16[512,2048]{1,0:T(8,128)(2,1)S(1)} custom-call(s32[2]{0:T(128)S(1)} %copy-done, bf16[256,2048]{1,0:T(8,128)(2,1)S(1)} %constant_dynamic-update-slice_fusion.6.refs_0_.refs_2_.refs_6_, bf16[256,2048]{1,0:T(8,128)(2,1)S(1)} %collective-permute-done.13.refs_1_.refs_3_.refs_7_, bf16[1024,1024]{1,0:T(8,128)(2,1)S(1)} %get-tuple-element.118.refs_2_.refs_3_, ...), custom_call_target="tpu_custom_call" | custom-call | flops 21474836 | bytes 83886 | tf_op jit(solution)/shard_map/pallas_call | solution.py:230
  87.6 2.0 collective-permute-start.11
  90.8 11.7 %collective-permute-done.11 = bf16[256,2048]{1,0:T(8,128)(2,1)S(1)} collective-permute-done((bf16[256,2048]{1,0:T(8,128)(2,1)S(1)}, bf16[256,2048]{1,0:T(8,128)(2,1)S(1)}, u32[]{:S(2)}, u32[]{:S(2)}) %collective-permute-start.11) | collective-permute-done | bytes 1048608 | tf_op jit(solution)/shard_map/ppermute | solution.py:45
  104.4 4.5 %shard_map.81 = (bf16[256,2048]{1,0:T(8,128)(2,1)S(1)}, bf16[256,2048]{1,0:T(8,128)(2,1)S(1)}) custom-call(s32[2]{0:T(128)S(1)} %copy-done, bf16[256,2048]{1,0:T(8,128)(2,1)S(1)} %constant_dynamic-update-slice_fusion.4.refs_0_.refs_4_, bf16[256,2048]{1,0:T(8,128)(2,1)S(1)} %collective-permute-done.12.refs_1_.refs_5_, ...), custom_call_target="tpu_custom_call" | custom-call | flops 21474836 | bytes 83886 | tf_op jit(solution)/shard_map/pallas_call | solution.py:230
  108.8 2.7 collective-permute-start.15
  112.5 12.2 %collective-permute-done.15 = bf16[128,2048]{1,0:T(8,128)(2,1)S(1)} collective-permute-done((bf16[128,2048]{1,0:T(8,128)(2,1)S(1)}, bf16[128,2048]{1,0:T(8,128)(2,1)S(1)}, u32[]{:S(2)}, u32[]{:S(2)}) %collective-permute-start.15) | collective-permute-done | bytes 524320 | tf_op jit(solution)/shard_map/ppermute | solution.py:45
  125.1 3.0 %collective-permute-start.16 = (bf16[128,2048]{1,0:T(8,128)(2,1)S(1)}, bf16[128,2048]{1,0:T(8,128)(2,1)S(1)}, u32[]{:S(2)}, u32[]{:S(2)}) collective-permute-start(bf16[128,2048]{1,0:T(8,128)(2,1)S(1)} %pad_maximum_fusion.4), channel_id=1, source_target_pairs={{96,0},{97,1},{98,2},{99,3},{100,4},{101,5},{102,6},{103,7},{104,8... | collective-permute-start | bytes 1572872 | tf_op jit(solution)/shard_map/ppermute | solution.py:45
  128.1 6.1 %collective-permute-done.18 = bf16[256,2048]{1,0:T(8,128)(2,1)S(1)} collective-permute-done((bf16[256,2048]{1,0:T(8,128)(2,1)S(1)}, bf16[256,2048]{1,0:T(8,128)(2,1)S(1)}, u32[]{:S(2)}, u32[]{:S(2)}) %collective-permute-start.18) | collective-permute-done | bytes 1048608 | tf_op jit(solution)/shard_map/ppermute | solution.py:45
  136.7 14.0 %collective-permute-done.19 = bf16[128,2048]{1,0:T(8,128)(2,1)S(1)} collective-permute-done((bf16[128,2048]{1,0:T(8,128)(2,1)S(1)}, bf16[128,2048]{1,0:T(8,128)(2,1)S(1)}, u32[]{:S(2)}, u32[]{:S(2)}) %collective-permute-start.19) | collective-permute-done | bytes 524320 | tf_op jit(solution)/shard_map/ppermute | solution.py:45
  151.2 10.5 %collective-permute-done.20 = bf16[128,2048]{1,0:T(8,128)(2,1)S(1)} collective-permute-done((bf16[128,2048]{1,0:T(8,128)(2,1)S(1)}, bf16[128,2048]{1,0:T(8,128)(2,1)S(1)}, u32[]{:S(2)}, u32[]{:S(2)}) %collective-permute-start.20) | collective-permute-done | bytes 524320 | tf_op jit(solution)/shard_map/ppermute | solution.py:45
  161.8 4.3 %shard_map.82 = (bf16[256,2048]{1,0:T(8,128)(2,1)S(1)}, bf16[256,2048]{1,0:T(8,128)(2,1)S(1)}) custom-call(s32[2]{0:T(128)S(1)} %copy-done, bf16[256,2048]{1,0:T(8,128)(2,1)S(1)} %pad_maximum_fusion.refs_0_.refs_4_, bf16[256,2048]{1,0:T(8,128)(2,1)S(1)} %collective-permute-done.17.refs_1_.refs_5_, bf16[1024,1024]{1,0:T(8,128)(2,1)S(1)} %get-tuple-element.117.refs_3_.refs_2_, ...), custom_call_target="tpu_custom_call" | custom-call | flops 21474836 | bytes 83886 | tf_op jit(solution)/shard_map/pallas_call | solution.py:230
  166.1 2.8 collective-permute-start.21
  169.5 12.7 %collective-permute-done.21 = bf16[256,2048]{1,0:T(8,128)(2,1)S(1)} collective-permute-done((bf16[256,2048]{1,0:T(8,128)(2,1)S(1)}, bf16[256,2048]{1,0:T(8,128)(2,1)S(1)}, u32[]{:S(2)}, u32[]{:S(2)}) %collective-permute-start.21) | collective-permute-done | bytes 1048608 | tf_op jit(solution)/shard_map/ppermute | solution.py:45
  182.8 4.3 %shard_map.83 = (bf16[256,2048]{1,0:T(8,128)(2,1)S(1)}, bf16[256,2048]{1,0:T(8,128)(2,1)S(1)}) custom-call(s32[2]{0:T(128)S(1)} %copy-done, bf16[256,2048]{1,0:T(8,128)(2,1)S(1)} %collective-permute-done.24.refs_0_.refs_6_.refs_2_, bf16[256,2048]{1,0:T(8,128)(2,1)S(1)} %collective-permute-done.25.refs_1_.refs_7_.refs_3_, ...), custom_call_target="tpu_custom_call" | custom-call | flops 21474836 | bytes 83886 | tf_op jit(solution)/shard_map/pallas_call | solution.py:230
  188.4 4.7 %shard_map.84.refs_8_ = f32[1024,1024]{1,0:T(8,128)} custom-call(bf16[256,2048]{1,0:T(8,128)(2,1)S(1)} %constant_dynamic-update-slice_fusion.refs_0_.refs_4_, bf16[256,2048]{1,0:T(8,128)(2,1)S(1)} %collective-permute-done.5.refs_1_.refs_5_, bf16[256,2048]{1,0:T(8,128)(2,1)S(1)} %constant_dynamic-update-slice_fusion.2.refs_0_.refs_2_.refs_6_, ...), custom_call_target="tpu_custom_call" | custom-call | flops 21474836 | bytes 52428 | tf_op jit(solution)/shard_map/pallas_call | solution.py:279
  193.2 4.3 %shard_map.85 = (bf16[256,2048]{1,0:T(8,128)(2,1)S(1)}, bf16[256,2048]{1,0:T(8,128)(2,1)S(1)}) custom-call(s32[2]{0:T(128)S(1)} %copy-done, bf16[256,2048]{1,0:T(8,128)(2,1)S(1)} %pad_maximum_fusion.1.refs_0_.refs_4_, bf16[256,2048]{1,0:T(8,128)(2,1)S(1)} %collective-permute-done.23.refs_1_.refs_5_, ...), custom_call_target="tpu_custom_call" | custom-call | flops 21474836 | bytes 83886 | tf_op jit(solution)/shard_map/pallas_call | solution.py:230
  197.5 2.8 collective-permute-start.27
  200.3 2.1 collective-permute-start.29
  203.1 5.1 %collective-permute-start.30 = (bf16[128,2048]{1,0:T(8,128)(2,1)S(1)}, bf16[128,2048]{1,0:T(8,128)(2,1)S(1)}, u32[]{:S(2)}, u32[]{:S(2)}) collective-permute-start(bf16[128,2048]{1,0:T(8,128)(2,1)S(1)} %slice.255), channel_id=1, source_target_pairs={{1,0},{0,1},{3,2},{2,3},{5,4},{4,5},{7,6},{6,7},{9,8},{8,9},{11,10... | collective-permute-start | bytes 1572872 | tf_op jit(solution)/shard_map/ppermute | solution.py:45
  208.2 4.3 %shard_map.86 = (bf16[256,2048]{1,0:T(8,128)(2,1)S(1)}, bf16[256,2048]{1,0:T(8,128)(2,1)S(1)}) custom-call(s32[2]{0:T(128)S(1)} %copy-done, bf16[256,2048]{1,0:T(8,128)(2,1)S(1)} %collective-permute-done.28.refs_0_.refs_6_.refs_2_, bf16[256,2048]{1,0:T(8,128)(2,1)S(1)} %collective-permute-done.29.refs_1_.refs_7_.refs_3_, ...), custom_call_target="tpu_custom_call" | custom-call | flops 21474836 | bytes 83886 | tf_op jit(solution)/shard_map/pallas_call | solution.py:230
  212.5 6.7 %collective-permute-done.27 = bf16[256,2048]{1,0:T(8,128)(2,1)S(1)} collective-permute-done((bf16[256,2048]{1,0:T(8,128)(2,1)S(1)}, bf16[256,2048]{1,0:T(8,128)(2,1)S(1)}, u32[]{:S(2)}, u32[]{:S(2)}) %collective-permute-start.27) | collective-permute-done | bytes 1048608 | tf_op jit(solution)/shard_map/ppermute | solution.py:45
  219.6 6.5 %shard_map.88 = f32[1024,1024]{1,0:T(8,128)} custom-call(bf16[256,2048]{1,0:T(8,128)(2,1)S(1)} %constant_dynamic-update-slice_fusion.4.refs_0_.refs_4_, bf16[256,2048]{1,0:T(8,128)(2,1)S(1)} %collective-permute-done.12.refs_1_.refs_5_, ...), custom_call_target="tpu_custom_call", output_to_operand_aliasing={{}: (8, {})} | custom-call | flops 21474836 | bytes 52428 | tf_op jit(solution)/shard_map/pallas_call | solution.py:279
  226.6 4.7 %shard_map.87.refs_8_ = f32[1024,1024]{1,0:T(8,128)} custom-call(bf16[256,2048]{1,0:T(8,128)(2,1)S(1)} %pad_maximum_fusion.refs_0_.refs_4_, bf16[256,2048]{1,0:T(8,128)(2,1)S(1)} %collective-permute-done.17.refs_1_.refs_5_, bf16[256,2048]{1,0:T(8,128)(2,1)S(1)} %collective-permute-done.24.refs_0_.refs_6_.refs_2_, ...), custom_call_target="tpu_custom_call" | custom-call | flops 21474836 | bytes 52428 | tf_op jit(solution)/shard_map/pallas_call | solution.py:279
  232.8 13.7 %collective-permute-done.32 = bf16[256,2048]{1,0:T(8,128)(2,1)S(1)} collective-permute-done((bf16[256,2048]{1,0:T(8,128)(2,1)S(1)}, bf16[256,2048]{1,0:T(8,128)(2,1)S(1)}, u32[]{:S(2)}, u32[]{:S(2)}) %collective-permute-start.32) | collective-permute-done | bytes 1048608 | tf_op jit(solution)/shard_map/ppermute | solution.py:45
  246.9 6.7 %collective-permute-start.35 = (bf16[128,2048]{1,0:T(8,128)(2,1)S(1)}, bf16[128,2048]{1,0:T(8,128)(2,1)S(1)}, u32[]{:S(2)}, u32[]{:S(2)}) collective-permute-start(bf16[128,2048]{1,0:T(8,128)(2,1)S(1)} %slice.254), channel_id=1, source_target_pairs={{1,0},{0,1},{3,2},{2,3},{5,4},{4,5},{7,6},{6,7},{9,8},{8,9},{11,10... | collective-permute-start | bytes 1572872 | tf_op jit(solution)/shard_map/ppermute | solution.py:45
  253.6 6.5 %shard_map.89 = f32[1024,1024]{1,0:T(8,128)} custom-call(bf16[256,2048]{1,0:T(8,128)(2,1)S(1)} %pad_maximum_fusion.1.refs_0_.refs_4_, bf16[256,2048]{1,0:T(8,128)(2,1)S(1)} %collective-permute-done.23.refs_1_.refs_5_, bf16[256,2048]{1,0:T(8,128)(2,1)S(1)} %collective-permute-done.28.refs_0_.refs_6_.refs_2_, ...), custom_call_target="tpu_custom_call", output_to_operand_aliasing={{}: (8, {})} | custom-call | flops 21474836 | bytes 52428 | tf_op jit(solution)/shard_map/pallas_call | solution.py:279
  260.5 3.5 %collective-permute-done.35 = bf16[128,2048]{1,0:T(8,128)(2,1)S(1)} collective-permute-done((bf16[128,2048]{1,0:T(8,128)(2,1)S(1)}, bf16[128,2048]{1,0:T(8,128)(2,1)S(1)}, u32[]{:S(2)}, u32[]{:S(2)}) %collective-permute-start.35) | collective-permute-done | bytes 524320 | tf_op jit(solution)/shard_map/ppermute | solution.py:45
  264.2 2.9 %collective-permute-start.36 = (bf16[128,2048]{1,0:T(8,128)(2,1)S(1)}, bf16[128,2048]{1,0:T(8,128)(2,1)S(1)}, u32[]{:S(2)}, u32[]{:S(2)}) collective-permute-start(bf16[128,2048]{1,0:T(8,128)(2,1)S(1)} %pad_maximum_fusion.7), channel_id=1, source_target_pairs={{12,0},{13,1},{14,2},{15,3},{8,4},{9,5},{10,6},{11,7},{4,8},{5,9},... | collective-permute-start | bytes 1572872 | tf_op jit(solution)/shard_map/ppermute | solution.py:45
  267.2 2.4 collective-permute-done.33
  271.7 5.8 %collective-permute-done.36 = bf16[128,2048]{1,0:T(8,128)(2,1)S(1)} collective-permute-done((bf16[128,2048]{1,0:T(8,128)(2,1)S(1)}, bf16[128,2048]{1,0:T(8,128)(2,1)S(1)}, u32[]{:S(2)}, u32[]{:S(2)}) %collective-permute-start.36) | collective-permute-done | bytes 524320 | tf_op jit(solution)/shard_map/ppermute | solution.py:45
  278.3 6.7 %collective-permute-done.37 = bf16[64,2048]{1,0:T(8,128)(2,1)} collective-permute-done((bf16[64,2048]{1,0:T(8,128)(2,1)}, bf16[64,2048]{1,0:T(8,128)(2,1)}, u32[]{:S(2)}, u32[]{:S(2)}) %collective-permute-start.37) | collective-permute-done | bytes 262176 | tf_op jit(solution)/shard_map/ppermute | solution.py:45
  (112 shorter events, 34.0 us)
Async XLA Ops:
  3.8 6.6 %collective-permute-start.2 = (bf16[64,2048]{1,0:T(8,128)(2,1)}, bf16[64,2048]{1,0:T(8,128)(2,1)S(1)}, u32[]{:S(2)}, u32[]{:S(2)}) collective-permute-start(bf16[64,2048]{1,0:T(8,128)(2,1)} %get-tuple-element.46.a_ref), channel_id=1, source_target_pairs={{1,0},{0,1},{3,2},{2,3},{5,4},{4,5},{7,6},{6,7},{9,8},{8,9},{11,10... | collective-permute-start | bytes 786440 | tf_op jit(solution)/shard_map/ppermute | solution.py:45
  4.1 9.0 %collective-permute-start = (bf16[64,2048]{1,0:T(8,128)(2,1)}, bf16[64,2048]{1,0:T(8,128)(2,1)S(1)}, u32[]{:S(2)}, u32[]{:S(2)}) collective-permute-start(bf16[64,2048]{1,0:T(8,128)(2,1)} %get-tuple-element.44.a_ref), channel_id=1, source_target_pairs={{4,0},{5,1},{6,2},{7,3},{0,4},{1,5},{2,6},{3,7},{12,8},{13,9},{14,... | collective-permute-start | bytes 786440 | tf_op jit(solution)/shard_map/ppermute | solution.py:45
  10.3 10.3 %copy-start.3 = (bf16[64,2048]{1,0:T(8,128)(2,1)}, bf16[64,2048]{1,0:T(8,128)(2,1)S(1)}, u32[]{:S(2)}) copy-start(bf16[64,2048]{1,0:T(8,128)(2,1)S(1)} %collective-permute-done.2.b_ref) | copy-start | bytes 786436
  11.4 9.3 %collective-permute-start.3 = (bf16[128,2048]{1,0:T(8,128)(2,1)S(1)}, bf16[128,2048]{1,0:T(8,128)(2,1)S(1)}, u32[]{:S(2)}, u32[]{:S(2)}) collective-permute-start(bf16[128,2048]{1,0:T(8,128)(2,1)S(1)} %pad_maximum_fusion.3), channel_id=1, source_target_pairs={{3,0},{2,1},{1,2},{0,3},{7,4},{6,5},{5,6},{4,7},{11,8},{10,9},{9,1... | collective-permute-start | bytes 1572872 | tf_op jit(solution)/shard_map/ppermute | solution.py:45
  13.1 11.6 %copy-start.2 = (bf16[64,2048]{1,0:T(8,128)(2,1)}, bf16[64,2048]{1,0:T(8,128)(2,1)S(1)}, u32[]{:S(2)}) copy-start(bf16[64,2048]{1,0:T(8,128)(2,1)S(1)} %collective-permute-done.b_ref) | copy-start | bytes 786436
  14.2 10.5 %collective-permute-start.1 = (bf16[128,2048]{1,0:T(8,128)(2,1)S(1)}, bf16[128,2048]{1,0:T(8,128)(2,1)S(1)}, u32[]{:S(2)}, u32[]{:S(2)}) collective-permute-start(bf16[128,2048]{1,0:T(8,128)(2,1)S(1)} %pad_maximum_fusion.2), channel_id=1, source_target_pairs={{12,0},{13,1},{14,2},{15,3},{8,4},{9,5},{10,6},{11,7},{4,8},{5,9},... | collective-permute-start | bytes 1572872 | tf_op jit(solution)/shard_map/ppermute | solution.py:45
  20.7 0.8 copy-start.7
  24.7 0.8 copy-start.6
  25.4 15.2 %copy-start.4 = (bf16[128,2048]{1,0:T(8,128)(2,1)S(1)}, bf16[128,2048]{1,0:T(8,128)(2,1)}, u32[]{:S(2)}) copy-start(bf16[128,2048]{1,0:T(8,128)(2,1)} %get-tuple-element.53) | copy-start | bytes 1572868
  28.3 9.4 %collective-permute-start.6 = (bf16[128,2048]{1,0:T(8,128)(2,1)}, bf16[128,2048]{1,0:T(8,128)(2,1)S(1)}, u32[]{:S(2)}, u32[]{:S(2)}) collective-permute-start(bf16[128,2048]{1,0:T(8,128)(2,1)} %get-tuple-element.49), channel_id=1, source_target_pairs={{4,0},{5,1},{6,2},{7,3},{0,4},{1,5},{2,6},{3,7},{12,8},{13,9},{14,... | collective-permute-start | bytes 1572872 | tf_op jit(solution)/shard_map/ppermute | solution.py:45
  29.5 11.3 %copy-start.1 = (bf16[2048,1024]{1,0:T(8,128)(2,1)S(1)}, bf16[2048,1024]{1,0:T(8,128)(2,1)}, u32[]{:S(2)}) copy-start(bf16[2048,1024]{1,0:T(8,128)(2,1)} %param.7) | copy-start | bytes 12582916
  29.5 11.1 %collective-permute-start.4 = (bf16[128,2048]{1,0:T(8,128)(2,1)}, bf16[128,2048]{1,0:T(8,128)(2,1)S(1)}, u32[]{:S(2)}, u32[]{:S(2)}) collective-permute-start(bf16[128,2048]{1,0:T(8,128)(2,1)} %get-tuple-element.48), channel_id=1, source_target_pairs={{1,0},{0,1},{3,2},{2,3},{5,4},{4,5},{7,6},{6,7},{9,8},{8,9},{11,10... | collective-permute-start | bytes 1572872 | tf_op jit(solution)/shard_map/ppermute | solution.py:45
  37.8 21.7 %collective-permute-start.9 = (bf16[256,2048]{1,0:T(8,128)(2,1)S(1)}, bf16[256,2048]{1,0:T(8,128)(2,1)S(1)}, u32[]{:S(2)}, u32[]{:S(2)}) collective-permute-start(bf16[256,2048]{1,0:T(8,128)(2,1)S(1)} %constant_dynamic-update-slice_fusion.2.refs_0_.refs_2_.refs_6_), channel_id=1, source_target_pairs={{12,0},{13,1},{14,2},{15,3},{8,4},{9,5},{10,6},{11,7},{4,8},{5,9},... | collective-permute-start | bytes 3145736 | tf_op jit(solution)/shard_map/ppermute | solution.py:45
  40.7 2.3 copy-start.5
  40.7 9.3 %collective-permute-start.8 = (bf16[128,2048]{1,0:T(8,128)(2,1)S(1)}, bf16[128,2048]{1,0:T(8,128)(2,1)S(1)}, u32[]{:S(2)}, u32[]{:S(2)}) collective-permute-start(bf16[128,2048]{1,0:T(8,128)(2,1)S(1)} %copy-done.4), channel_id=1, source_target_pairs={{4,0},{5,1},{6,2},{7,3},{0,4},{1,5},{2,6},{3,7},{12,8},{13,9},{14,... | collective-permute-start | bytes 1572872 | tf_op jit(solution)/shard_map/ppermute | solution.py:45
  43.0 16.5 %copy-start = (s32[2]{0:T(128)S(1)}, s32[2]{0:T(128)}, u32[]{:S(2)}) copy-start(s32[2]{0:T(128)} %pad_add_fusion.place_ref) | copy-start | bytes 28
  43.0 12.8 %collective-permute-start.7 = (bf16[128,2048]{1,0:T(8,128)(2,1)S(1)}, bf16[128,2048]{1,0:T(8,128)(2,1)S(1)}, u32[]{:S(2)}, u32[]{:S(2)}) collective-permute-start(bf16[128,2048]{1,0:T(8,128)(2,1)S(1)} %copy-done.5), channel_id=1, source_target_pairs={{1,0},{0,1},{3,2},{2,3},{5,4},{4,5},{7,6},{6,7},{9,8},{8,9},{11,10... | collective-permute-start | bytes 1572872 | tf_op jit(solution)/shard_map/ppermute | solution.py:45
  63.8 15.0 %collective-permute-start.10 = (bf16[512,2048]{1,0:T(8,128)(2,1)S(1)}, bf16[512,2048]{1,0:T(8,128)(2,1)S(1)}, u32[]{:S(2)}, u32[]{:S(2)}) collective-permute-start(bf16[512,2048]{1,0:T(8,128)(2,1)S(1)} %shard_map.78), channel_id=1, source_target_pairs={{16,0},{17,1},{18,2},{19,3},{20,4},{21,5},{22,6},{23,7},{24,8},{25... | collective-permute-start | bytes 6291464 | tf_op jit(solution)/shard_map/ppermute | solution.py:45
  63.9 14.9 %collective-permute-start.5 = (bf16[256,2048]{1,0:T(8,128)(2,1)S(1)}, bf16[256,2048]{1,0:T(8,128)(2,1)S(1)}, u32[]{:S(2)}, u32[]{:S(2)}) collective-permute-start(bf16[256,2048]{1,0:T(8,128)(2,1)S(1)} %constant_dynamic-update-slice_fusion.refs_0_.refs_4_), channel_id=1, source_target_pairs={{3,0},{2,1},{1,2},{0,3},{7,4},{6,5},{5,6},{4,7},{11,8},{10,9},{9,1... | collective-permute-start | bytes 3145736 | tf_op jit(solution)/shard_map/ppermute | solution.py:45
  65.1 18.0 %collective-permute-start.13 = (bf16[256,2048]{1,0:T(8,128)(2,1)S(1)}, bf16[256,2048]{1,0:T(8,128)(2,1)S(1)}, u32[]{:S(2)}, u32[]{:S(2)}) collective-permute-start(bf16[256,2048]{1,0:T(8,128)(2,1)S(1)} %constant_dynamic-update-slice_fusion.6.refs_0_.refs_2_.refs_6_), channel_id=1, source_target_pairs={{12,0},{13,1},{14,2},{15,3},{8,4},{9,5},{10,6},{11,7},{4,8},{5,9},... | collective-permute-start | bytes 3145736 | tf_op jit(solution)/shard_map/ppermute | solution.py:45
  87.5 16.9 %collective-permute-start.14 = (bf16[512,2048]{1,0:T(8,128)(2,1)S(1)}, bf16[512,2048]{1,0:T(8,128)(2,1)S(1)}, u32[]{:S(2)}, u32[]{:S(2)}) collective-permute-start(bf16[512,2048]{1,0:T(8,128)(2,1)S(1)} %shard_map.80), channel_id=1, source_target_pairs={{16,0},{17,1},{18,2},{19,3},{20,4},{21,5},{22,6},{23,7},{24,8},{25... | collective-permute-start | bytes 6291464 | tf_op jit(solution)/shard_map/ppermute | solution.py:45
  87.6 14.9 %collective-permute-start.11 = (bf16[256,2048]{1,0:T(8,128)(2,1)S(1)}, bf16[256,2048]{1,0:T(8,128)(2,1)S(1)}, u32[]{:S(2)}, u32[]{:S(2)}) collective-permute-start(bf16[256,2048]{1,0:T(8,128)(2,1)S(1)} %get-tuple-element.56), channel_id=1, source_target_pairs={{32,0},{33,1},{34,2},{35,3},{36,4},{37,5},{38,6},{39,7},{40,8},{41... | collective-permute-start | bytes 3145736 | tf_op jit(solution)/shard_map/ppermute | solution.py:45
  89.6 14.8 %collective-permute-start.12 = (bf16[256,2048]{1,0:T(8,128)(2,1)S(1)}, bf16[256,2048]{1,0:T(8,128)(2,1)S(1)}, u32[]{:S(2)}, u32[]{:S(2)}) collective-permute-start(bf16[256,2048]{1,0:T(8,128)(2,1)S(1)} %constant_dynamic-update-slice_fusion.4.refs_0_.refs_4_), channel_id=1, source_target_pairs={{3,0},{2,1},{1,2},{0,3},{7,4},{6,5},{5,6},{4,7},{11,8},{10,9},{9,1... | collective-permute-start | bytes 3145736 | tf_op jit(solution)/shard_map/ppermute | solution.py:45
  108.8 15.8 %collective-permute-start.15 = (bf16[128,2048]{1,0:T(8,128)(2,1)S(1)}, bf16[128,2048]{1,0:T(8,128)(2,1)S(1)}, u32[]{:S(2)}, u32[]{:S(2)}) collective-permute-start(bf16[128,2048]{1,0:T(8,128)(2,1)S(1)} %slice.259), channel_id=1, source_target_pairs={{96,0},{97,1},{98,2},{99,3},{100,4},{101,5},{102,6},{103,7},{104,8... | collective-permute-start | bytes 1572872 | tf_op jit(solution)/shard_map/ppermute | solution.py:45
  111.5 22.6 %collective-permute-start.18 = (bf16[256,2048]{1,0:T(8,128)(2,1)S(1)}, bf16[256,2048]{1,0:T(8,128)(2,1)S(1)}, u32[]{:S(2)}, u32[]{:S(2)}) collective-permute-start(bf16[256,2048]{1,0:T(8,128)(2,1)S(1)} %get-tuple-element.58), channel_id=1, source_target_pairs={{32,0},{33,1},{34,2},{35,3},{36,4},{37,5},{38,6},{39,7},{40,8},{41... | collective-permute-start | bytes 3145736 | tf_op jit(solution)/shard_map/ppermute | solution.py:45
  125.1 11.1 %collective-permute-start.16 = (bf16[128,2048]{1,0:T(8,128)(2,1)S(1)}, bf16[128,2048]{1,0:T(8,128)(2,1)S(1)}, u32[]{:S(2)}, u32[]{:S(2)}) collective-permute-start(bf16[128,2048]{1,0:T(8,128)(2,1)S(1)} %pad_maximum_fusion.4), channel_id=1, source_target_pairs={{96,0},{97,1},{98,2},{99,3},{100,4},{101,5},{102,6},{103,7},{104,8... | collective-permute-start | bytes 1572872 | tf_op jit(solution)/shard_map/ppermute | solution.py:45
  134.6 16.1 %collective-permute-start.19 = (bf16[128,2048]{1,0:T(8,128)(2,1)S(1)}, bf16[128,2048]{1,0:T(8,128)(2,1)S(1)}, u32[]{:S(2)}, u32[]{:S(2)}) collective-permute-start(bf16[128,2048]{1,0:T(8,128)(2,1)S(1)} %slice.258), channel_id=1, source_target_pairs={{96,0},{97,1},{98,2},{99,3},{100,4},{101,5},{102,6},{103,7},{104,8... | collective-permute-start | bytes 1572872 | tf_op jit(solution)/shard_map/ppermute | solution.py:45
  136.3 25.5 %collective-permute-start.17 = (bf16[256,2048]{1,0:T(8,128)(2,1)S(1)}, bf16[256,2048]{1,0:T(8,128)(2,1)S(1)}, u32[]{:S(2)}, u32[]{:S(2)}) collective-permute-start(bf16[256,2048]{1,0:T(8,128)(2,1)S(1)} %pad_maximum_fusion.refs_0_.refs_4_), channel_id=1, source_target_pairs={{32,0},{33,1},{34,2},{35,3},{36,4},{37,5},{38,6},{39,7},{40,8},{41... | collective-permute-start | bytes 3145736 | tf_op jit(solution)/shard_map/ppermute | solution.py:45
  151.1 10.6 %collective-permute-start.20 = (bf16[128,2048]{1,0:T(8,128)(2,1)S(1)}, bf16[128,2048]{1,0:T(8,128)(2,1)S(1)}, u32[]{:S(2)}, u32[]{:S(2)}) collective-permute-start(bf16[128,2048]{1,0:T(8,128)(2,1)S(1)} %pad_maximum_fusion.5), channel_id=1, source_target_pairs={{96,0},{97,1},{98,2},{99,3},{100,4},{101,5},{102,6},{103,7},{104,8... | collective-permute-start | bytes 1572872 | tf_op jit(solution)/shard_map/ppermute | solution.py:45
  166.1 16.1 %collective-permute-start.21 = (bf16[256,2048]{1,0:T(8,128)(2,1)S(1)}, bf16[256,2048]{1,0:T(8,128)(2,1)S(1)}, u32[]{:S(2)}, u32[]{:S(2)}) collective-permute-start(bf16[256,2048]{1,0:T(8,128)(2,1)S(1)} %get-tuple-element.64), channel_id=1, source_target_pairs={{12,0},{13,1},{14,2},{15,3},{8,4},{9,5},{10,6},{11,7},{4,8},{5,9},... | collective-permute-start | bytes 3145736 | tf_op jit(solution)/shard_map/ppermute | solution.py:45
  168.9 13.9 %collective-permute-start.24 = (bf16[256,2048]{1,0:T(8,128)(2,1)S(1)}, bf16[256,2048]{1,0:T(8,128)(2,1)S(1)}, u32[]{:S(2)}, u32[]{:S(2)}) collective-permute-start(bf16[256,2048]{1,0:T(8,128)(2,1)S(1)} %pad_maximum_fusion.refs_0_.refs_4_), channel_id=1, source_target_pairs={{16,0},{17,1},{18,2},{19,3},{20,4},{21,5},{22,6},{23,7},{24,8},{25... | collective-permute-start | bytes 3145736 | tf_op jit(solution)/shard_map/ppermute | solution.py:45
  168.9 13.9 %collective-permute-start.25 = (bf16[256,2048]{1,0:T(8,128)(2,1)S(1)}, bf16[256,2048]{1,0:T(8,128)(2,1)S(1)}, u32[]{:S(2)}, u32[]{:S(2)}) collective-permute-start(bf16[256,2048]{1,0:T(8,128)(2,1)S(1)} %collective-permute-done.17.refs_1_.refs_5_), channel_id=1, source_target_pairs={{16,0},{17,1},{18,2},{19,3},{20,4},{21,5},{22,6},{23,7},{24,8},{25... | collective-permute-start | bytes 3145736 | tf_op jit(solution)/shard_map/ppermute | solution.py:45
  169.4 23.7 %collective-permute-start.23 = (bf16[256,2048]{1,0:T(8,128)(2,1)S(1)}, bf16[256,2048]{1,0:T(8,128)(2,1)S(1)}, u32[]{:S(2)}, u32[]{:S(2)}) collective-permute-start(bf16[256,2048]{1,0:T(8,128)(2,1)S(1)} %pad_maximum_fusion.1.refs_0_.refs_4_), channel_id=1, source_target_pairs={{32,0},{33,1},{34,2},{35,3},{36,4},{37,5},{38,6},{39,7},{40,8},{41... | collective-permute-start | bytes 3145736 | tf_op jit(solution)/shard_map/ppermute | solution.py:45
  182.6 19.8 %collective-permute-start.22 = (bf16[128,2048]{1,0:T(8,128)(2,1)S(1)}, bf16[128,2048]{1,0:T(8,128)(2,1)S(1)}, u32[]{:S(2)}, u32[]{:S(2)}) collective-permute-start(bf16[128,2048]{1,0:T(8,128)(2,1)S(1)} %slice.257), channel_id=1, source_target_pairs={{4,0},{5,1},{6,2},{7,3},{0,4},{1,5},{2,6},{3,7},{12,8},{13,9},{14,... | collective-permute-start | bytes 1572872 | tf_op jit(solution)/shard_map/ppermute | solution.py:45
  182.7 25.4 %collective-permute-start.28 = (bf16[256,2048]{1,0:T(8,128)(2,1)S(1)}, bf16[256,2048]{1,0:T(8,128)(2,1)S(1)}, u32[]{:S(2)}, u32[]{:S(2)}) collective-permute-start(bf16[256,2048]{1,0:T(8,128)(2,1)S(1)} %pad_maximum_fusion.1.refs_0_.refs_4_), channel_id=1, source_target_pairs={{16,0},{17,1},{18,2},{19,3},{20,4},{21,5},{22,6},{23,7},{24,8},{25... | collective-permute-start | bytes 3145736 | tf_op jit(solution)/shard_map/ppermute | solution.py:45
  187.2 15.5 %collective-permute-start.26 = (bf16[256,2048]{1,0:T(8,128)(2,1)S(1)}, bf16[256,2048]{1,0:T(8,128)(2,1)S(1)}, u32[]{:S(2)}, u32[]{:S(2)}) collective-permute-start(bf16[256,2048]{1,0:T(8,128)(2,1)S(1)} %get-tuple-element.68), channel_id=1, source_target_pairs={{3,0},{2,1},{1,2},{0,3},{7,4},{6,5},{5,6},{4,7},{11,8},{10,9},{9,1... | collective-permute-start | bytes 3145736 | tf_op jit(solution)/shard_map/ppermute | solution.py:45
  197.5 21.7 %collective-permute-start.27 = (bf16[256,2048]{1,0:T(8,128)(2,1)S(1)}, bf16[256,2048]{1,0:T(8,128)(2,1)S(1)}, u32[]{:S(2)}, u32[]{:S(2)}) collective-permute-start(bf16[256,2048]{1,0:T(8,128)(2,1)S(1)} %get-tuple-element.71), channel_id=1, source_target_pairs={{12,0},{13,1},{14,2},{15,3},{8,4},{9,5},{10,6},{11,7},{4,8},{5,9},... | collective-permute-start | bytes 3145736 | tf_op jit(solution)/shard_map/ppermute | solution.py:45
  200.3 7.8 %collective-permute-start.29 = (bf16[256,2048]{1,0:T(8,128)(2,1)S(1)}, bf16[256,2048]{1,0:T(8,128)(2,1)S(1)}, u32[]{:S(2)}, u32[]{:S(2)}) collective-permute-start(bf16[256,2048]{1,0:T(8,128)(2,1)S(1)} %collective-permute-done.23.refs_1_.refs_5_), channel_id=1, source_target_pairs={{16,0},{17,1},{18,2},{19,3},{20,4},{21,5},{22,6},{23,7},{24,8},{25... | collective-permute-start | bytes 3145736 | tf_op jit(solution)/shard_map/ppermute | solution.py:45
  203.1 28.3 %collective-permute-start.30 = (bf16[128,2048]{1,0:T(8,128)(2,1)S(1)}, bf16[128,2048]{1,0:T(8,128)(2,1)S(1)}, u32[]{:S(2)}, u32[]{:S(2)}) collective-permute-start(bf16[128,2048]{1,0:T(8,128)(2,1)S(1)} %slice.255), channel_id=1, source_target_pairs={{1,0},{0,1},{3,2},{2,3},{5,4},{4,5},{7,6},{6,7},{9,8},{8,9},{11,10... | collective-permute-start | bytes 1572872 | tf_op jit(solution)/shard_map/ppermute | solution.py:45
  226.1 20.4 %collective-permute-start.32 = (bf16[256,2048]{1,0:T(8,128)(2,1)S(1)}, bf16[256,2048]{1,0:T(8,128)(2,1)S(1)}, u32[]{:S(2)}, u32[]{:S(2)}) collective-permute-start(bf16[256,2048]{1,0:T(8,128)(2,1)S(1)} %get-tuple-element.76), channel_id=1, source_target_pairs={{3,0},{2,1},{1,2},{0,3},{7,4},{6,5},{5,6},{4,7},{11,8},{10,9},{9,1... | collective-permute-start | bytes 3145736 | tf_op jit(solution)/shard_map/ppermute | solution.py:45
  231.5 28.5 %collective-permute-start.31 = (bf16[128,2048]{1,0:T(8,128)(2,1)S(1)}, bf16[128,2048]{1,0:T(8,128)(2,1)S(1)}, u32[]{:S(2)}, u32[]{:S(2)}) collective-permute-start(bf16[128,2048]{1,0:T(8,128)(2,1)S(1)} %slice.256), channel_id=1, source_target_pairs={{4,0},{5,1},{6,2},{7,3},{0,4},{1,5},{2,6},{3,7},{12,8},{13,9},{14,... | collective-permute-start | bytes 1572872 | tf_op jit(solution)/shard_map/ppermute | solution.py:45
  246.9 17.0 %collective-permute-start.35 = (bf16[128,2048]{1,0:T(8,128)(2,1)S(1)}, bf16[128,2048]{1,0:T(8,128)(2,1)S(1)}, u32[]{:S(2)}, u32[]{:S(2)}) collective-permute-start(bf16[128,2048]{1,0:T(8,128)(2,1)S(1)} %slice.254), channel_id=1, source_target_pairs={{1,0},{0,1},{3,2},{2,3},{5,4},{4,5},{7,6},{6,7},{9,8},{8,9},{11,10... | collective-permute-start | bytes 1572872 | tf_op jit(solution)/shard_map/ppermute | solution.py:45
  260.3 9.3 %collective-permute-start.33 = (bf16[128,2048]{1,0:T(8,128)(2,1)S(1)}, bf16[128,2048]{1,0:T(8,128)(2,1)S(1)}, u32[]{:S(2)}, u32[]{:S(2)}) collective-permute-start(bf16[128,2048]{1,0:T(8,128)(2,1)S(1)} %pad_maximum_fusion.6), channel_id=1, source_target_pairs={{3,0},{2,1},{1,2},{0,3},{7,4},{6,5},{5,6},{4,7},{11,8},{10,9},{9,1... | collective-permute-start | bytes 1572872 | tf_op jit(solution)/shard_map/ppermute | solution.py:45
  264.2 13.3 %collective-permute-start.36 = (bf16[128,2048]{1,0:T(8,128)(2,1)S(1)}, bf16[128,2048]{1,0:T(8,128)(2,1)S(1)}, u32[]{:S(2)}, u32[]{:S(2)}) collective-permute-start(bf16[128,2048]{1,0:T(8,128)(2,1)S(1)} %pad_maximum_fusion.7), channel_id=1, source_target_pairs={{12,0},{13,1},{14,2},{15,3},{8,4},{9,5},{10,6},{11,7},{4,8},{5,9},... | collective-permute-start | bytes 1572872 | tf_op jit(solution)/shard_map/ppermute | solution.py:45
  270.5 7.9 %collective-permute-start.34 = (bf16[64,2048]{1,0:T(8,128)(2,1)}, bf16[64,2048]{1,0:T(8,128)(2,1)S(1)}, u32[]{:S(2)}, u32[]{:S(2)}) collective-permute-start(bf16[64,2048]{1,0:T(8,128)(2,1)} %fusion.15), channel_id=1, source_target_pairs={{1,0},{0,1},{3,2},{2,3},{5,4},{4,5},{7,6},{6,7},{9,8},{8,9},{11,10... | collective-permute-start | bytes 786440 | tf_op jit(solution)/shard_map/ppermute | solution.py:45
  278.3 6.7 %collective-permute-start.37 = (bf16[64,2048]{1,0:T(8,128)(2,1)}, bf16[64,2048]{1,0:T(8,128)(2,1)}, u32[]{:S(2)}, u32[]{:S(2)}) collective-permute-start(bf16[64,2048]{1,0:T(8,128)(2,1)} %fusion.12), channel_id=1, source_target_pairs={{4,0},{5,1},{6,2},{7,3},{0,4},{1,5},{2,6},{3,7},{12,8},{13,9},{14,... | collective-permute-start | bytes 786440 | tf_op jit(solution)/shard_map/ppermute | solution.py:45

commit v5 on v4

--- a/solution.py
+++ b/solution.py
@@ -20,7 +20,7 @@
 
 def cost(flops, bytes_accessed, transcendentals):
     return pl.CostEstimate(
-        flops=flops // 100, bytes_accessed=bytes_accessed // 100, transcendentals=transcendentals
+        flops=flops // 1000, bytes_accessed=bytes_accessed // 1000, transcendentals=transcendentals
     )
 
 
@@ -108,20 +108,31 @@
         ref[:, wide:] = grad_ref[rows, :]
 
 
+def whole(kernel, place, arrays, shapes):
+    return pl.pallas_call(
+        kernel,
+        in_specs=[pl.BlockSpec(memory_space=pltpu.SMEM)]
+        + [pl.BlockSpec(memory_space=pltpu.VMEM)] * len(arrays),
+        out_specs=[pl.BlockSpec(memory_space=pltpu.VMEM)] * len(shapes),
+        out_shape=[jax.ShapeDtypeStruct(shape, BF) for shape in shapes],
+        compiler_params=pltpu.CompilerParams(vmem_limit_bytes=8 * 2**20),
+        cost_estimate=cost(flops=0, bytes_accessed=0, transcendentals=0),
+    )(place, *arrays)
+
+
 def cut(place, tokens, out_grad):
     rows, wide = tokens.shape
-    half = jax.ShapeDtypeStruct((rows // 2, 2 * wide), BF)
-    return pl.pallas_call(
-        cut_kernel,
-        grid_spec=pltpu.PrefetchScalarGridSpec(
-            num_scalar_prefetch=1,
-            grid=(1,),
-            in_specs=[pl.BlockSpec((rows, wide), lambda i, place: (0, 0))] * 2,
-            out_specs=[pl.BlockSpec((rows // 2, 2 * wide), lambda i, place: (0, 0))] * 2,
-        ),
-        out_shape=[half, half],
-        cost_estimate=cost(flops=0, bytes_accessed=8 * rows * wide, transcendentals=0),
-    )(place, tokens, out_grad)
+    return whole(cut_kernel, place, [tokens, out_grad], [(rows // 2, 2 * wide)] * 2)
+
+
+def join_kernel(place_ref, a_ref, b_ref, out_ref):
+    rows = a_ref.shape[0]
+    out_ref[:rows, :] = a_ref[...]
+    out_ref[rows:, :] = b_ref[...]
+
+
+def join(place, a, b):
+    return whole(join_kernel, place, [a, b], [(2 * a.shape[0], a.shape[1])])[0]
 
 
 def assemble_kernel(keep, place_ref, a_ref, b_ref, c_ref, *out_refs):
@@ -141,20 +152,8 @@
 
 def assemble(keep, place, a, b, c):
     rows, wide = a.shape
-    tiles = 2
-    spec = lambda n: pl.BlockSpec((n, wide // tiles), lambda i, place: (0, i))
-    out_rows = RING * rows // PARTS
-    return pl.pallas_call(
-        functools.partial(assemble_kernel, keep),
-        grid_spec=pltpu.PrefetchScalarGridSpec(
-            num_scalar_prefetch=1,
-            grid=(tiles,),
-            in_specs=[spec(rows), spec(rows), spec(2 * rows)],
-            out_specs=[spec(out_rows)] * PARTS,
-        ),
-        out_shape=[jax.ShapeDtypeStruct((out_rows, wide), BF)] * PARTS,
-        cost_estimate=cost(flops=0, bytes_accessed=16 * rows * wide, transcendentals=0),
-    )(place, a, b, c)
+    kernel = functools.partial(assemble_kernel, keep)
+    return whole(kernel, place, [a, b, c], [(RING * rows // PARTS, wide)] * PARTS)
 
 
 def order_of(keep):
@@ -316,25 +315,21 @@
     for keep in order:
         one[keep] = exchange(start[keep], along(keep, True, 0))
     for keep in order:
-        pair = jnp.concatenate([start[keep], one[keep]], axis=0)
-        two[keep] = exchange(pair, along(keep, True, 1))
+        two[keep] = exchange(join(place, start[keep], one[keep]), along(keep, True, 1))
     for keep in order:
         own_a[keep], own_b[keep] = assemble(keep, place, start[keep], one[keep], two[keep])
 
-    def every(values, *events):
-        both = lax.optimization_barrier((values[True], values[False], *events))
-        return {True: both[0], False: both[1]}
-
     def neighbours(own):
-        near = {keep: exchange(own[keep], along(keep, False, 0)) for keep in order}
-        return {keep: jnp.concatenate([own[keep], near[keep]], axis=0) for keep in order}
+        return {keep: exchange(own[keep], along(keep, False, 0)) for keep in order}
+
+    def joined(own, near):
+        return {keep: join(place, own[keep], near[keep]) for keep in order}
 
     def others(near):
         return {keep: exchange(near[keep], along(keep, False, 1)) for keep in order}
 
     def panel_dot(keep, near, rest, *events, more=None):
-        pair = [near[keep], rest[keep]]
-        pair[0] = after(pair[0], *events) if events else pair[0]
+        pair = [near[keep], after(rest[keep], *events) if events else rest[keep]]
         return pair_dot(keep, False, pair, w_in, w_out, place, more=more, split=keep)
 
     def out_dot(keep, pair, *events):
@@ -352,23 +347,27 @@
         activated, slope = gelu_parts(pre)
         return jnp.concatenate([activated.astype(BF), (back * slope).astype(BF)], axis=1)
 
-    near_a = neighbours(every(own_a))
+    both = lax.optimization_barrier((own_a[True], own_a[False]))
+    own_a = {True: both[0], False: both[1]}
+    near_a = joined(own_a, neighbours(own_a))
     rest_a = others(near_a)
-    near_b = neighbours(every(own_b, near_a[True], near_a[False]))
-    sent_a = panel_dot(False, near_a, rest_a, near_b[True], near_b[False])
-    kept_a, send_a = panel_dot(True, near_a, rest_a, more=exchange(sent_a, other_core))
+    step_b = neighbours(own_b)
+    sent_a = panel_dot(False, near_a, rest_a, rest_a[True])
+    got_a = after(exchange(sent_a, other_core), step_b[True], step_b[False])
+    kept_a, send_a = panel_dot(True, near_a, rest_a, more=got_a)
     step_a = exchange(send_a, along_z(0))
+    near_b = joined(own_b, step_b)
     rest_b = others(near_b)
-    sent_b = panel_dot(False, near_b, rest_b, send_a)
-    kept_b, send_b = panel_dot(True, near_b, rest_b, more=exchange(sent_b, other_core))
+    sent_b = panel_dot(False, near_b, rest_b, rest_b[True], send_a)
+    half_a = halfway(kept_a, step_a)
+    turn_a = exchange(half_a[1].astype(BF), along_z(1))
+    got_b = after(exchange(sent_b, other_core), turn_a)
+    kept_b, send_b = panel_dot(True, near_b, rest_b, more=got_b)
     step_b = exchange(send_b, along_z(0))
-
-    half_a = halfway(kept_a, step_a)
-    turn_a = exchange(after(half_a[1].astype(BF), send_b), along_z(1))
     half_b = halfway(kept_b, step_b)
     mine_a = hidden_of(half_a[0] + turn_a.astype(F32))
     next_a = exchange(mine_a, along_z(1))
-    turn_b = exchange(after(half_b[1].astype(BF), mine_a), along_z(1))
+    turn_b = exchange(half_b[1].astype(BF), along_z(1))
     pair_a = jnp.concatenate([mine_a, next_a], axis=0)
     far_a = exchange(pair_a, along_z(0))
     mine_b = hidden_of(half_b[0] + turn_b.astype(F32))
@@ -408,30 +407,32 @@
         lefts[0] = after(lefts[0], *events)
         return grad_dot(lefts, 0, rights, 1, pairs, factor, begun)
 
-    def first_half(keep, kept, passed):
-        return halfway(kept, exchange(passed, along(keep, True, 1)))
-
-    def first_sum(keep, sums, *events):
-        passed = sums[1].astype(BF)
-        passed = after(passed, *events) if events else passed
-        return sums[0] + exchange(passed, along(keep, True, 0)).astype(F32)
-
-    out_a, out_b, sums_a, sums_b, total_a, total_b = {}, {}, {}, {}, {}, {}
+    def second_half(keep, kept, got):
+        sums = halfway(kept, got)
+        return sums[0], exchange(sums[1].astype(BF), along(keep, True, 0))
+
+    out_a, out_b, got_a, got_b = {}, {}, {}, {}
+    sums_a, sums_b, last_a, last_b, total_a, total_b = {}, {}, {}, {}, {}, {}
     out_a[True] = out_dot(True, hid_a[True])
     out_a[False] = out_dot(False, hid_a[False], out_a[True][0])
+    for keep in both_ways:
+        got_a[keep] = exchange(out_a[keep][1], along(keep, True, 1))
     grad_in = grads(0, near_a, rest_a, hid_a, None, out_a[False][0])
     for keep in both_ways:
-        sums_a[keep] = first_half(keep, *out_a[keep])
-    out_b[True] = out_dot(True, hid_b[True], grad_in, sums_a[True][0], sums_a[False][0])
+        got = after(got_a[keep], grad_in, got_a[not keep])
+        sums_a[keep], last_a[keep] = second_half(keep, out_a[keep][0], got)
+    out_b[True] = out_dot(True, hid_b[True], got_a[True], got_a[False], grad_in)
     out_b[False] = out_dot(False, hid_b[False], out_b[True][0])
     for keep in both_ways:
-        total_a[keep] = first_sum(keep, sums_a[keep])
-    grad_out = grads(1, near_a, rest_a, hid_a, None, out_b[False][0])
-    for keep in both_ways:
-        sums_b[keep] = first_half(keep, *out_b[keep])
-    for keep in both_ways:
-        total_b[keep] = first_sum(keep, sums_b[keep], grad_out, total_a[True], total_a[False])
-    grad_in = grads(0, near_b, rest_b, hid_b, grad_in, sums_b[True][0], sums_b[False][0])
+        got_b[keep] = exchange(out_b[keep][1], along(keep, True, 1))
+    grad_out = grads(1, near_a, rest_a, hid_a, None, out_b[False][0], last_a[True], last_a[False])
+    for keep in both_ways:
+        got = after(got_b[keep], grad_out, got_b[not keep])
+        sums_b[keep], last_b[keep] = second_half(keep, out_b[keep][0], got)
+    grad_in = grads(0, near_b, rest_b, hid_b, grad_in, got_b[True], got_b[False], grad_out)
+    for keep in both_ways:
+        total_a[keep] = sums_a[keep] + last_a[keep].astype(F32)
+        total_b[keep] = sums_b[keep] + after(last_b[keep], grad_in).astype(F32)
 
     part = block // PARTS
     pick = lambda keep, piece: jnp.concatenate(
@@ -444,11 +445,11 @@
     gots, done = {}, {}
     for keep in both_ways:
         passed = jnp.concatenate([pick(keep, 2), pick(keep, 3)], axis=0).astype(BF)
-        gots[keep] = exchange(after(passed, grad_in), along(keep, False, 1))
-    grad_out = grads(1, near_b, rest_b, hid_b, grad_out, grad_in)
-    for keep in both_ways:
-        got = gots[keep].astype(F32)
-        last = after((pick(keep, 1) + got[block:]).astype(BF), grad_out)
+        gots[keep] = exchange(passed, along(keep, False, 1))
+    grad_out = grads(1, near_b, rest_b, hid_b, grad_out, last_b[True], last_b[False], grad_in)
+    for keep in both_ways:
+        got = after(gots[keep], grad_out).astype(F32)
+        last = (pick(keep, 1) + got[block:]).astype(BF)
         done[keep] = (
             pick(keep, 0) + got[:block] + exchange(last, along(keep, False, 0)).astype(F32)
         ).astype(BF)

time: 288 us -> 255 us (0.89)
  the two profiles are of different devices: /device:TPU:8 before, /device:TPU:32 now
where the time goes in v5:
time: 255 us; the launch traced here: 254 us
  waiting for transfers between devices  118 us (46%)
  Pallas kernels  65 us (25%)
  starting transfers between devices  55.3 us (22%)
  other arithmetic  7.58 us (3%)
  local copies, waits for them, and re-layouts  6.76 us (3%)
    ppermute x38, waiting for transfers between devices, exchange(): return lax.ppermute(array, AXES, pairs)  118 us
    ppermute x38, starting transfers between devices, exchange(): return lax.ppermute(array, AXES, pairs)  55.3 us
    pallas_call x8, Pallas kernels, pair_dot(): pl.pallas_call(functools.partial(pair_kernel, keep, hidden, more is not N...  35.5 us
    pallas_call x4, Pallas kernels, grad_dot(): pl.pallas_call(functools.partial(grad_kernel, pairs, block, factor, begun...  24.1 us
    pallas_call x9, Pallas kernels, whole(): pl.pallas_call(kernel, in_specs=[pl.BlockSpec(memory_space=pltpu.SMEM)] +...  5.4 us
  transfers between devices with their start and end apart: 38, of which 25 were waited for; matrix products, arithmetic and copies ran while one was open for 3% of the time, Pallas kernels for 22%

profile of v5, /device:TPU:32, one launch (start us, length us, event | category | flops | bytes accessed | tf_op | source)
XLA Modules:
  0.0 254.4 jit_solution(13154385643840920210)
XLA Ops:
  6.4 3.3 %collective-permute-done.b_ref = bf16[64,2048]{1,0:T(8,128)(2,1)S(1)} collective-permute-done((bf16[64,2048]{1,0:T(8,128)(2,1)S(1)}, bf16[64,2048]{1,0:T(8,128)(2,1)S(1)}, u32[]{:S(2)}, u32[]{:S(2)}) %collective-permute-start) | collective-permute-done | bytes 262176 | tf_op jit(solution)/shard_map/ppermute | solution.py:45
  10.2 2.8 %collective-permute-start.1 = (bf16[128,2048]{1,0:T(8,128)(2,1)S(1)}, bf16[128,2048]{1,0:T(8,128)(2,1)S(1)}, u32[]{:S(2)}, u32[]{:S(2)}) collective-permute-start(bf16[128,2048]{1,0:T(8,128)(2,1)S(1)} %shard_map.76), channel_id=1, source_target_pairs={{12,0},{13,1},{14,2},{15,3},{8,4},{9,5},{10,6},{11,7},{4,8},{5,9},... | collective-permute-start | bytes 1572872 | tf_op jit(solution)/shard_map/ppermute | solution.py:45
  13.7 3.1 %collective-permute-start.3 = (bf16[128,2048]{1,0:T(8,128)(2,1)S(1)}, bf16[128,2048]{1,0:T(8,128)(2,1)S(1)}, u32[]{:S(2)}, u32[]{:S(2)}) collective-permute-start(bf16[128,2048]{1,0:T(8,128)(2,1)S(1)} %shard_map.78), channel_id=1, source_target_pairs={{3,0},{2,1},{1,2},{0,3},{7,4},{6,5},{5,6},{4,7},{11,8},{10,9},{9,1... | collective-permute-start | bytes 1572872 | tf_op jit(solution)/shard_map/ppermute | solution.py:45
  16.8 4.0 %collective-permute-done.1.c_ref = bf16[128,2048]{1,0:T(8,128)(2,1)S(1)} collective-permute-done((bf16[128,2048]{1,0:T(8,128)(2,1)S(1)}, bf16[128,2048]{1,0:T(8,128)(2,1)S(1)}, u32[]{:S(2)}, u32[]{:S(2)}) %collective-permute-start.1) | collective-permute-done | bytes 524320 | tf_op jit(solution)/shard_map/ppermute | solution.py:45
  22.1 2.0 collective-permute-done.3.c_ref
  26.2 8.6 %collective-permute-done.6.b_ref = bf16[128,2048]{1,0:T(8,128)(2,1)S(1)} collective-permute-done((bf16[128,2048]{1,0:T(8,128)(2,1)S(1)}, bf16[128,2048]{1,0:T(8,128)(2,1)S(1)}, u32[]{:S(2)}, u32[]{:S(2)}) %collective-permute-start.6) | collective-permute-done | bytes 524320 | tf_op jit(solution)/shard_map/ppermute | solution.py:45
  36.8 3.1 %collective-permute-start.5 = (bf16[256,2048]{1,0:T(8,128)(2,1)S(1)}, bf16[256,2048]{1,0:T(8,128)(2,1)}, u32[]{:S(2)}, u32[]{:S(2)}) collective-permute-start(bf16[256,2048]{1,0:T(8,128)(2,1)S(1)} %shard_map.80.refs_0_.refs_4_), channel_id=1, source_target_pairs={{3,0},{2,1},{1,2},{0,3},{7,4},{6,5},{5,6},{4,7},{11,8},{10,9},{9,1... | collective-permute-start | bytes 3145736 | tf_op jit(solution)/shard_map/ppermute | solution.py:45
  39.9 2.7 %constant_dynamic-slice_fusion = (bf16[1024,1024]{1,0:T(8,128)(2,1)S(1)}, bf16[1024,1024]{1,0:T(8,128)(2,1)S(1)}) fusion(bf16[2048,1024]{1,0:T(8,128)(2,1)} %param.7, s32[]{:T(128)S(6)} %select_n.30, bf16[1024,2048]{1,0:T(8,128)(2,1)} %param.6), kind=kLoop, calls=%fused_computation.59 | loop fusion | bytes 8388612 | tf_op jit(solution)/shard_map/dynamic_slice | solution.py:310
  42.6 8.9 %collective-permute-done.7.refs_1_.refs_3_.refs_7_ = bf16[256,2048]{1,0:T(8,128)(2,1)S(1)} collective-permute-done((bf16[256,2048]{1,0:T(8,128)(2,1)S(1)}, bf16[256,2048]{1,0:T(8,128)(2,1)S(1)}, u32[]{:S(2)}, u32[]{:S(2)}) %collective-permute-start.7) | collective-permute-done | bytes 1048608 | tf_op jit(solution)/shard_map/ppermute | solution.py:45
  53.0 4.3 %shard_map.82 = bf16[512,2048]{1,0:T(8,128)(2,1)S(1)} custom-call(s32[2]{0:T(128)S(1)} %pad_add_fusion.place_ref, bf16[256,2048]{1,0:T(8,128)(2,1)S(1)} %shard_map.81.refs_0_.refs_2_.refs_6_, bf16[256,2048]{1,0:T(8,128)(2,1)S(1)} %collective-permute-done.7.refs_1_.refs_3_.refs_7_, bf16[1024,1024]{1,0:T(8,128)(2,1)S(1)} %get-tuple-element.118.refs_2_.refs_3_, ...), custom_call_target="tpu_custom_call" | custom-call | flops 2147483 | bytes 8388 | tf_op jit(solution)/shard_map/pallas_call | solution.py:229
  57.4 1.8 collective-permute-start.10
  59.2 7.4 %collective-permute-done.10.b_ref = bf16[128,2048]{1,0:T(8,128)(2,1)S(1)} collective-permute-done((bf16[128,2048]{1,0:T(8,128)(2,1)S(1)}, bf16[128,2048]{1,0:T(8,128)(2,1)S(1)}, u32[]{:S(2)}, u32[]{:S(2)}) %collective-permute-start.10) | collective-permute-done | bytes 524320 | tf_op jit(solution)/shard_map/ppermute | solution.py:45
  67.3 2.6 %collective-permute-start.16 = (bf16[256,2048]{1,0:T(8,128)(2,1)S(1)}, bf16[256,2048]{1,0:T(8,128)(2,1)S(1)}, u32[]{:S(2)}, u32[]{:S(2)}) collective-permute-start(bf16[256,2048]{1,0:T(8,128)(2,1)S(1)} %shard_map.85.refs_0_.refs_2_.refs_6_), channel_id=1, source_target_pairs={{12,0},{13,1},{14,2},{15,3},{8,4},{9,5},{10,6},{11,7},{4,8},{5,9},... | collective-permute-start | bytes 3145736 | tf_op jit(solution)/shard_map/ppermute | solution.py:45
  70.5 3.1 %collective-permute-start.15 = (bf16[256,2048]{1,0:T(8,128)(2,1)S(1)}, bf16[256,2048]{1,0:T(8,128)(2,1)S(1)}, u32[]{:S(2)}, u32[]{:S(2)}) collective-permute-start(bf16[256,2048]{1,0:T(8,128)(2,1)S(1)} %shard_map.84.refs_0_.refs_4_), channel_id=1, source_target_pairs={{3,0},{2,1},{1,2},{0,3},{7,4},{6,5},{5,6},{4,7},{11,8},{10,9},{9,1... | collective-permute-start | bytes 3145736 | tf_op jit(solution)/shard_map/ppermute | solution.py:45
  73.5 5.3 %shard_map.83 = (bf16[256,2048]{1,0:T(8,128)(2,1)S(1)}, bf16[256,2048]{1,0:T(8,128)(2,1)S(1)}) custom-call(s32[2]{0:T(128)S(1)} %pad_add_fusion.place_ref, bf16[256,2048]{1,0:T(8,128)(2,1)S(1)} %shard_map.80.refs_0_.refs_4_, bf16[256,2048]{1,0:T(8,128)(2,1)} %collective-permute-done.5.refs_1_.refs_5_, ...), custom_call_target="tpu_custom_call" | custom-call | flops 2147483 | bytes 8388 | tf_op jit(solution)/shard_map/pallas_call | solution.py:229
  79.1 4.3 %collective-permute-done.16.refs_1_.refs_3_.refs_7_ = bf16[256,2048]{1,0:T(8,128)(2,1)S(1)} collective-permute-done((bf16[256,2048]{1,0:T(8,128)(2,1)S(1)}, bf16[256,2048]{1,0:T(8,128)(2,1)S(1)}, u32[]{:S(2)}, u32[]{:S(2)}) %collective-permute-start.16) | collective-permute-done | bytes 1048608 | tf_op jit(solution)/shard_map/ppermute | solution.py:45
  83.4 3.2 %collective-permute-done.15.refs_1_.refs_5_ = bf16[256,2048]{1,0:T(8,128)(2,1)S(1)} collective-permute-done((bf16[256,2048]{1,0:T(8,128)(2,1)S(1)}, bf16[256,2048]{1,0:T(8,128)(2,1)S(1)}, u32[]{:S(2)}, u32[]{:S(2)}) %collective-permute-start.15) | collective-permute-done | bytes 1048608 | tf_op jit(solution)/shard_map/ppermute | solution.py:45
  86.5 4.3 %shard_map.86 = bf16[512,2048]{1,0:T(8,128)(2,1)S(1)} custom-call(s32[2]{0:T(128)S(1)} %pad_add_fusion.place_ref, bf16[256,2048]{1,0:T(8,128)(2,1)S(1)} %shard_map.85.refs_0_.refs_2_.refs_6_, bf16[256,2048]{1,0:T(8,128)(2,1)S(1)} %collective-permute-done.16.refs_1_.refs_3_.refs_7_, bf16[1024,1024]{1,0:T(8,128)(2,1)S(1)} %get-tuple-element.118.refs_2_.refs_3_, ...), custom_call_target="tpu_custom_call" | custom-call | flops 2147483 | bytes 8388 | tf_op jit(solution)/shard_map/pallas_call | solution.py:229
  90.9 2.8 %collective-permute-done.11 = bf16[256,2048]{1,0:T(8,128)(2,1)S(1)} collective-permute-done((bf16[256,2048]{1,0:T(8,128)(2,1)S(1)}, bf16[256,2048]{1,0:T(8,128)(2,1)S(1)}, u32[]{:S(2)}, u32[]{:S(2)}) %collective-permute-start.11) | collective-permute-done | bytes 1048608 | tf_op jit(solution)/shard_map/ppermute | solution.py:45
  94.2 2.0 collective-permute-start.12
  96.2 7.2 %collective-permute-done.12 = bf16[128,2048]{1,0:T(8,128)(2,1)S(1)} collective-permute-done((bf16[128,2048]{1,0:T(8,128)(2,1)S(1)}, bf16[128,2048]{1,0:T(8,128)(2,1)S(1)}, u32[]{:S(2)}, u32[]{:S(2)}) %collective-permute-start.12) | collective-permute-done | bytes 524320 | tf_op jit(solution)/shard_map/ppermute | solution.py:45
  103.4 4.5 %shard_map.87 = (bf16[256,2048]{1,0:T(8,128)(2,1)S(1)}, bf16[256,2048]{1,0:T(8,128)(2,1)S(1)}) custom-call(s32[2]{0:T(128)S(1)} %pad_add_fusion.place_ref, bf16[256,2048]{1,0:T(8,128)(2,1)S(1)} %shard_map.84.refs_0_.refs_4_, bf16[256,2048]{1,0:T(8,128)(2,1)S(1)} %collective-permute-done.15.refs_1_.refs_5_, ...), custom_call_target="tpu_custom_call" | custom-call | flops 2147483 | bytes 8388 | tf_op jit(solution)/shard_map/pallas_call | solution.py:229
  107.9 2.2 collective-permute-start.18
  110.5 2.9 %collective-permute-start.13 = (bf16[128,2048]{1,0:T(8,128)(2,1)S(1)}, bf16[128,2048]{1,0:T(8,128)(2,1)S(1)}, u32[]{:S(2)}, u32[]{:S(2)}) collective-permute-start(bf16[128,2048]{1,0:T(8,128)(2,1)S(1)} %pad_maximum_fusion.2), channel_id=1, source_target_pairs={{96,0},{97,1},{98,2},{99,3},{100,4},{101,5},{102,6},{103,7},{104,8... | collective-permute-start | bytes 1572872 | tf_op jit(solution)/shard_map/ppermute | solution.py:45
  113.4 13.6 %collective-permute-done.18 = bf16[256,2048]{1,0:T(8,128)(2,1)S(1)} collective-permute-done((bf16[256,2048]{1,0:T(8,128)(2,1)S(1)}, bf16[256,2048]{1,0:T(8,128)(2,1)S(1)}, u32[]{:S(2)}, u32[]{:S(2)}) %collective-permute-start.18) | collective-permute-done | bytes 1048608 | tf_op jit(solution)/shard_map/ppermute | solution.py:45
  127.7 2.1 collective-permute-start.14
  129.8 12.6 %collective-permute-done.19 = bf16[128,2048]{1,0:T(8,128)(2,1)S(1)} collective-permute-done((bf16[128,2048]{1,0:T(8,128)(2,1)S(1)}, bf16[128,2048]{1,0:T(8,128)(2,1)S(1)}, u32[]{:S(2)}, u32[]{:S(2)}) %collective-permute-start.19) | collective-permute-done | bytes 524320 | tf_op jit(solution)/shard_map/ppermute | solution.py:45
  142.9 9.5 %collective-permute-done.20 = bf16[128,2048]{1,0:T(8,128)(2,1)S(1)} collective-permute-done((bf16[128,2048]{1,0:T(8,128)(2,1)S(1)}, bf16[128,2048]{1,0:T(8,128)(2,1)S(1)}, u32[]{:S(2)}, u32[]{:S(2)}) %collective-permute-start.20) | collective-permute-done | bytes 524320 | tf_op jit(solution)/shard_map/ppermute | solution.py:45
  153.0 3.9 %collective-permute-start.26 = (bf16[256,2048]{1,0:T(8,128)(2,1)S(1)}, bf16[256,2048]{1,0:T(8,128)(2,1)S(1)}, u32[]{:S(2)}, u32[]{:S(2)}) collective-permute-start(bf16[256,2048]{1,0:T(8,128)(2,1)S(1)} %pad_maximum_fusion.1.refs_0_.refs_4_), channel_id=1, source_target_pairs={{32,0},{33,1},{34,2},{35,3},{36,4},{37,5},{38,6},{39,7},{40,8},{41... | collective-permute-start | bytes 3145736 | tf_op jit(solution)/shard_map/ppermute | solution.py:45
  156.9 4.3 %shard_map.88 = (bf16[256,2048]{1,0:T(8,128)(2,1)S(1)}, bf16[256,2048]{1,0:T(8,128)(2,1)S(1)}) custom-call(s32[2]{0:T(128)S(1)} %pad_add_fusion.place_ref, bf16[256,2048]{1,0:T(8,128)(2,1)S(1)} %pad_maximum_fusion.refs_0_.refs_4_, bf16[256,2048]{1,0:T(8,128)(2,1)S(1)} %collective-permute-done.14.refs_1_.refs_5_, ...), custom_call_target="tpu_custom_call" | custom-call | flops 2147483 | bytes 8388 | tf_op jit(solution)/shard_map/pallas_call | solution.py:229
  161.3 2.0 collective-permute-start.21
  163.3 4.3 %shard_map.89 = (bf16[256,2048]{1,0:T(8,128)(2,1)S(1)}, bf16[256,2048]{1,0:T(8,128)(2,1)S(1)}) custom-call(s32[2]{0:T(128)S(1)} %pad_add_fusion.place_ref, bf16[256,2048]{1,0:T(8,128)(2,1)S(1)} %collective-permute-done.22.refs_0_.refs_6_.refs_2_, bf16[256,2048]{1,0:T(8,128)(2,1)S(1)} %collective-permute-done.23.refs_1_.refs_7_.refs_3_, ...), custom_call_target="tpu_custom_call" | custom-call | flops 2147483 | bytes 8388 | tf_op jit(solution)/shard_map/pallas_call | solution.py:229
  169.7 5.6 %shard_map.90.refs_8_ = f32[1024,1024]{1,0:T(8,128)} custom-call(bf16[256,2048]{1,0:T(8,128)(2,1)S(1)} %shard_map.80.refs_0_.refs_4_, bf16[256,2048]{1,0:T(8,128)(2,1)} %collective-permute-done.5.refs_1_.refs_5_, bf16[256,2048]{1,0:T(8,128)(2,1)S(1)} %shard_map.81.refs_0_.refs_2_.refs_6_, ...), custom_call_target="tpu_custom_call" | custom-call | flops 2147483 | bytes 5242 | tf_op jit(solution)/shard_map/pallas_call | solution.py:278
  175.3 2.0 collective-permute-done.21
  177.3 8.6 %collective-permute-done.24 = bf16[256,2048]{1,0:T(8,128)(2,1)S(1)} collective-permute-done((bf16[256,2048]{1,0:T(8,128)(2,1)S(1)}, bf16[256,2048]{1,0:T(8,128)(2,1)S(1)}, u32[]{:S(2)}, u32[]{:S(2)}) %collective-permute-start.24) | collective-permute-done | bytes 1048608 | tf_op jit(solution)/shard_map/ppermute | solution.py:45
  188.5 4.3 %shard_map.91 = (bf16[256,2048]{1,0:T(8,128)(2,1)S(1)}, bf16[256,2048]{1,0:T(8,128)(2,1)S(1)}) custom-call(s32[2]{0:T(128)S(1)} %pad_add_fusion.place_ref, bf16[256,2048]{1,0:T(8,128)(2,1)S(1)} %pad_maximum_fusion.1.refs_0_.refs_4_, bf16[256,2048]{1,0:T(8,128)(2,1)S(1)} %collective-permute-done.26.refs_1_.refs_5_, ...), custom_call_target="tpu_custom_call" | custom-call | flops 2147483 | bytes 8388 | tf_op jit(solution)/shard_map/pallas_call | solution.py:229
  192.8 4.3 %shard_map.92 = (bf16[256,2048]{1,0:T(8,128)(2,1)S(1)}, bf16[256,2048]{1,0:T(8,128)(2,1)S(1)}) custom-call(s32[2]{0:T(128)S(1)} %pad_add_fusion.place_ref, bf16[256,2048]{1,0:T(8,128)(2,1)S(1)} %collective-permute-done.28.refs_0_.refs_6_.refs_2_, bf16[256,2048]{1,0:T(8,128)(2,1)S(1)} %collective-permute-done.29.refs_1_.refs_7_.refs_3_, ...), custom_call_target="tpu_custom_call" | custom-call | flops 2147483 | bytes 8388 | tf_op jit(solution)/shard_map/pallas_call | solution.py:229
  198.7 3.6 %collective-permute-done.30 = bf16[128,2048]{1,0:T(8,128)(2,1)S(1)} collective-permute-done((bf16[128,2048]{1,0:T(8,128)(2,1)S(1)}, bf16[128,2048]{1,0:T(8,128)(2,1)S(1)}, u32[]{:S(2)}, u32[]{:S(2)}) %collective-permute-start.30) | collective-permute-done | bytes 524320 | tf_op jit(solution)/shard_map/ppermute | solution.py:45
  202.5 5.6 %shard_map.93.refs_8_ = f32[1024,1024]{1,0:T(8,128)} custom-call(bf16[256,2048]{1,0:T(8,128)(2,1)S(1)} %pad_maximum_fusion.refs_0_.refs_4_, bf16[256,2048]{1,0:T(8,128)(2,1)S(1)} %collective-permute-done.14.refs_1_.refs_5_, bf16[256,2048]{1,0:T(8,128)(2,1)S(1)} %collective-permute-done.22.refs_0_.refs_6_.refs_2_, ...), custom_call_target="tpu_custom_call" | custom-call | flops 2147483 | bytes 5242 | tf_op jit(solution)/shard_map/pallas_call | solution.py:278
  208.1 5.1 %collective-permute-done.31 = bf16[256,2048]{1,0:T(8,128)(2,1)S(1)} collective-permute-done((bf16[256,2048]{1,0:T(8,128)(2,1)S(1)}, bf16[256,2048]{1,0:T(8,128)(2,1)S(1)}, u32[]{:S(2)}, u32[]{:S(2)}) %collective-permute-start.31) | collective-permute-done | bytes 1048608 | tf_op jit(solution)/shard_map/ppermute | solution.py:45
  214.7 3.5 %collective-permute-start.34 = (bf16[128,2048]{1,0:T(8,128)(2,1)S(1)}, bf16[128,2048]{1,0:T(8,128)(2,1)S(1)}, u32[]{:S(2)}, u32[]{:S(2)}) collective-permute-start(bf16[128,2048]{1,0:T(8,128)(2,1)S(1)} %slice.254), channel_id=1, source_target_pairs={{1,0},{0,1},{3,2},{2,3},{5,4},{4,5},{7,6},{6,7},{9,8},{8,9},{11,10... | collective-permute-start | bytes 1572872 | tf_op jit(solution)/shard_map/ppermute | solution.py:45
  218.2 6.5 %shard_map.94 = f32[1024,1024]{1,0:T(8,128)} custom-call(bf16[256,2048]{1,0:T(8,128)(2,1)S(1)} %shard_map.84.refs_0_.refs_4_, bf16[256,2048]{1,0:T(8,128)(2,1)S(1)} %collective-permute-done.15.refs_1_.refs_5_, bf16[256,2048]{1,0:T(8,128)(2,1)S(1)} %shard_map.85.refs_0_.refs_2_.refs_6_, ...), custom_call_target="tpu_custom_call", output_to_operand_aliasing={{}: (8, {})} | custom-call | flops 2147483 | bytes 5242 | tf_op jit(solution)/shard_map/pallas_call | solution.py:278
  225.0 5.2 %collective-permute-start.33 = (bf16[128,2048]{1,0:T(8,128)(2,1)S(1)}, bf16[128,2048]{1,0:T(8,128)(2,1)S(1)}, u32[]{:S(2)}, u32[]{:S(2)}) collective-permute-start(bf16[128,2048]{1,0:T(8,128)(2,1)S(1)} %pad_maximum_fusion.4), channel_id=1, source_target_pairs={{3,0},{2,1},{1,2},{0,3},{7,4},{6,5},{5,6},{4,7},{11,8},{10,9},{9,1... | collective-permute-start | bytes 1572872 | tf_op jit(solution)/shard_map/ppermute | solution.py:45
  230.6 6.5 %shard_map.95 = f32[1024,1024]{1,0:T(8,128)} custom-call(bf16[256,2048]{1,0:T(8,128)(2,1)S(1)} %pad_maximum_fusion.1.refs_0_.refs_4_, bf16[256,2048]{1,0:T(8,128)(2,1)S(1)} %collective-permute-done.26.refs_1_.refs_5_, bf16[256,2048]{1,0:T(8,128)(2,1)S(1)} %collective-permute-done.28.refs_0_.refs_6_.refs_2_, ...), custom_call_target="tpu_custom_call", output_to_operand_aliasing={{}: (8, {})} | custom-call | flops 2147483 | bytes 5242 | tf_op jit(solution)/shard_map/pallas_call | solution.py:278
  237.1 2.3 collective-permute-done.33
  240.2 4.6 %collective-permute-start.35 = (bf16[64,2048]{1,0:T(8,128)(2,1)}, bf16[64,2048]{1,0:T(8,128)(2,1)S(1)}, u32[]{:S(2)}, u32[]{:S(2)}) collective-permute-start(bf16[64,2048]{1,0:T(8,128)(2,1)} %fusion.15), channel_id=1, source_target_pairs={{1,0},{0,1},{3,2},{2,3},{5,4},{4,5},{7,6},{6,7},{9,8},{8,9},{11,10... | collective-permute-start | bytes 786440 | tf_op jit(solution)/shard_map/ppermute | solution.py:45
  246.1 3.2 %collective-permute-done.35 = bf16[64,2048]{1,0:T(8,128)(2,1)S(1)} collective-permute-done((bf16[64,2048]{1,0:T(8,128)(2,1)}, bf16[64,2048]{1,0:T(8,128)(2,1)S(1)}, u32[]{:S(2)}, u32[]{:S(2)}) %collective-permute-start.35) | collective-permute-done | bytes 262176 | tf_op jit(solution)/shard_map/ppermute | solution.py:45
  249.3 3.0 %collective-permute-done.37 = bf16[64,2048]{1,0:T(8,128)(2,1)} collective-permute-done((bf16[64,2048]{1,0:T(8,128)(2,1)}, bf16[64,2048]{1,0:T(8,128)(2,1)}, u32[]{:S(2)}, u32[]{:S(2)}) %collective-permute-start.37) | collective-permute-done | bytes 262176 | tf_op jit(solution)/shard_map/ppermute | solution.py:45
  (104 shorter events, 30.8 us)
Async XLA Ops:
  0.7 1.0 copy-start.4
  1.7 0.9 copy-start.5
  3.2 6.5 %collective-permute-start = (bf16[64,2048]{1,0:T(8,128)(2,1)S(1)}, bf16[64,2048]{1,0:T(8,128)(2,1)S(1)}, u32[]{:S(2)}, u32[]{:S(2)}) collective-permute-start(bf16[64,2048]{1,0:T(8,128)(2,1)S(1)} %get-tuple-element.44.a_ref), channel_id=1, source_target_pairs={{4,0},{5,1},{6,2},{7,3},{0,4},{1,5},{2,6},{3,7},{12,8},{13,9},{14,... | collective-permute-start | bytes 786440 | tf_op jit(solution)/shard_map/ppermute | solution.py:45
  4.8 8.3 %collective-permute-start.2 = (bf16[64,2048]{1,0:T(8,128)(2,1)S(1)}, bf16[64,2048]{1,0:T(8,128)(2,1)S(1)}, u32[]{:S(2)}, u32[]{:S(2)}) collective-permute-start(bf16[64,2048]{1,0:T(8,128)(2,1)S(1)} %get-tuple-element.46.a_ref), channel_id=1, source_target_pairs={{1,0},{0,1},{3,2},{2,3},{5,4},{4,5},{7,6},{6,7},{9,8},{8,9},{11,10... | collective-permute-start | bytes 786440 | tf_op jit(solution)/shard_map/ppermute | solution.py:45
  10.2 10.5 %collective-permute-start.1 = (bf16[128,2048]{1,0:T(8,128)(2,1)S(1)}, bf16[128,2048]{1,0:T(8,128)(2,1)S(1)}, u32[]{:S(2)}, u32[]{:S(2)}) collective-permute-start(bf16[128,2048]{1,0:T(8,128)(2,1)S(1)} %shard_map.76), channel_id=1, source_target_pairs={{12,0},{13,1},{14,2},{15,3},{8,4},{9,5},{10,6},{11,7},{4,8},{5,9},... | collective-permute-start | bytes 1572872 | tf_op jit(solution)/shard_map/ppermute | solution.py:45
  13.7 10.5 %collective-permute-start.3 = (bf16[128,2048]{1,0:T(8,128)(2,1)S(1)}, bf16[128,2048]{1,0:T(8,128)(2,1)S(1)}, u32[]{:S(2)}, u32[]{:S(2)}) collective-permute-start(bf16[128,2048]{1,0:T(8,128)(2,1)S(1)} %shard_map.78), channel_id=1, source_target_pairs={{3,0},{2,1},{1,2},{0,3},{7,4},{6,5},{5,6},{4,7},{11,8},{10,9},{9,1... | collective-permute-start | bytes 1572872 | tf_op jit(solution)/shard_map/ppermute | solution.py:45
  21.3 0.8 copy-start
  24.8 0.8 copy-start.2
  25.6 9.2 %collective-permute-start.6 = (bf16[128,2048]{1,0:T(8,128)(2,1)S(1)}, bf16[128,2048]{1,0:T(8,128)(2,1)S(1)}, u32[]{:S(2)}, u32[]{:S(2)}) collective-permute-start(bf16[128,2048]{1,0:T(8,128)(2,1)S(1)} %get-tuple-element.49.a_ref), channel_id=1, source_target_pairs={{4,0},{5,1},{6,2},{7,3},{0,4},{1,5},{2,6},{3,7},{12,8},{13,9},{14,... | collective-permute-start | bytes 1572872 | tf_op jit(solution)/shard_map/ppermute | solution.py:45
  25.8 10.4 %collective-permute-start.4 = (bf16[128,2048]{1,0:T(8,128)(2,1)S(1)}, bf16[128,2048]{1,0:T(8,128)(2,1)S(1)}, u32[]{:S(2)}, u32[]{:S(2)}) collective-permute-start(bf16[128,2048]{1,0:T(8,128)(2,1)S(1)} %get-tuple-element.48.a_ref), channel_id=1, source_target_pairs={{1,0},{0,1},{3,2},{2,3},{5,4},{4,5},{7,6},{6,7},{9,8},{8,9},{11,10... | collective-permute-start | bytes 1572872 | tf_op jit(solution)/shard_map/ppermute | solution.py:45
  35.4 16.1 %collective-permute-start.7 = (bf16[256,2048]{1,0:T(8,128)(2,1)S(1)}, bf16[256,2048]{1,0:T(8,128)(2,1)S(1)}, u32[]{:S(2)}, u32[]{:S(2)}) collective-permute-start(bf16[256,2048]{1,0:T(8,128)(2,1)S(1)} %shard_map.81.refs_0_.refs_2_.refs_6_), channel_id=1, source_target_pairs={{12,0},{13,1},{14,2},{15,3},{8,4},{9,5},{10,6},{11,7},{4,8},{5,9},... | collective-permute-start | bytes 3145736 | tf_op jit(solution)/shard_map/ppermute | solution.py:45
  36.8 16.2 %collective-permute-start.5 = (bf16[256,2048]{1,0:T(8,128)(2,1)S(1)}, bf16[256,2048]{1,0:T(8,128)(2,1)}, u32[]{:S(2)}, u32[]{:S(2)}) collective-permute-start(bf16[256,2048]{1,0:T(8,128)(2,1)S(1)} %shard_map.80.refs_0_.refs_4_), channel_id=1, source_target_pairs={{3,0},{2,1},{1,2},{0,3},{7,4},{6,5},{5,6},{4,7},{11,8},{10,9},{9,1... | collective-permute-start | bytes 3145736 | tf_op jit(solution)/shard_map/ppermute | solution.py:45
  53.0 4.4 %copy-start.3 = (bf16[128,2048]{1,0:T(8,128)(2,1)S(1)}, bf16[128,2048]{1,0:T(8,128)(2,1)}, u32[]{:S(2)}) copy-start(bf16[128,2048]{1,0:T(8,128)(2,1)} %copy-done.2) | copy-start | bytes 1572868
  53.0 6.2 %copy-start.1 = (bf16[128,2048]{1,0:T(8,128)(2,1)S(1)}, bf16[128,2048]{1,0:T(8,128)(2,1)}, u32[]{:S(2)}) copy-start(bf16[128,2048]{1,0:T(8,128)(2,1)} %copy-done) | copy-start | bytes 1572868
  57.3 16.2 %collective-permute-start.8 = (bf16[512,2048]{1,0:T(8,128)(2,1)S(1)}, bf16[512,2048]{1,0:T(8,128)(2,1)S(1)}, u32[]{:S(2)}, u32[]{:S(2)}) collective-permute-start(bf16[512,2048]{1,0:T(8,128)(2,1)S(1)} %shard_map.82), channel_id=1, source_target_pairs={{16,0},{17,1},{18,2},{19,3},{20,4},{21,5},{22,6},{23,7},{24,8},{25... | collective-permute-start | bytes 6291464 | tf_op jit(solution)/shard_map/ppermute | solution.py:45
  57.4 9.3 %collective-permute-start.10 = (bf16[128,2048]{1,0:T(8,128)(2,1)S(1)}, bf16[128,2048]{1,0:T(8,128)(2,1)S(1)}, u32[]{:S(2)}, u32[]{:S(2)}) collective-permute-start(bf16[128,2048]{1,0:T(8,128)(2,1)S(1)} %copy-done.3), channel_id=1, source_target_pairs={{4,0},{5,1},{6,2},{7,3},{0,4},{1,5},{2,6},{3,7},{12,8},{13,9},{14,... | collective-permute-start | bytes 1572872 | tf_op jit(solution)/shard_map/ppermute | solution.py:45
  59.2 10.6 %collective-permute-start.9 = (bf16[128,2048]{1,0:T(8,128)(2,1)S(1)}, bf16[128,2048]{1,0:T(8,128)(2,1)S(1)}, u32[]{:S(2)}, u32[]{:S(2)}) collective-permute-start(bf16[128,2048]{1,0:T(8,128)(2,1)S(1)} %copy-done.1), channel_id=1, source_target_pairs={{1,0},{0,1},{3,2},{2,3},{5,4},{4,5},{7,6},{6,7},{9,8},{8,9},{11,10... | collective-permute-start | bytes 1572872 | tf_op jit(solution)/shard_map/ppermute | solution.py:45
  67.3 16.1 %collective-permute-start.16 = (bf16[256,2048]{1,0:T(8,128)(2,1)S(1)}, bf16[256,2048]{1,0:T(8,128)(2,1)S(1)}, u32[]{:S(2)}, u32[]{:S(2)}) collective-permute-start(bf16[256,2048]{1,0:T(8,128)(2,1)S(1)} %shard_map.85.refs_0_.refs_2_.refs_6_), channel_id=1, source_target_pairs={{12,0},{13,1},{14,2},{15,3},{8,4},{9,5},{10,6},{11,7},{4,8},{5,9},... | collective-permute-start | bytes 3145736 | tf_op jit(solution)/shard_map/ppermute | solution.py:45
  70.5 16.1 %collective-permute-start.15 = (bf16[256,2048]{1,0:T(8,128)(2,1)S(1)}, bf16[256,2048]{1,0:T(8,128)(2,1)S(1)}, u32[]{:S(2)}, u32[]{:S(2)}) collective-permute-start(bf16[256,2048]{1,0:T(8,128)(2,1)S(1)} %shard_map.84.refs_0_.refs_4_), channel_id=1, source_target_pairs={{3,0},{2,1},{1,2},{0,3},{7,4},{6,5},{5,6},{4,7},{11,8},{10,9},{9,1... | collective-permute-start | bytes 3145736 | tf_op jit(solution)/shard_map/ppermute | solution.py:45
  78.9 14.9 %collective-permute-start.11 = (bf16[256,2048]{1,0:T(8,128)(2,1)S(1)}, bf16[256,2048]{1,0:T(8,128)(2,1)S(1)}, u32[]{:S(2)}, u32[]{:S(2)}) collective-permute-start(bf16[256,2048]{1,0:T(8,128)(2,1)S(1)} %get-tuple-element.55), channel_id=1, source_target_pairs={{32,0},{33,1},{34,2},{35,3},{36,4},{37,5},{38,6},{39,7},{40,8},{41... | collective-permute-start | bytes 3145736 | tf_op jit(solution)/shard_map/ppermute | solution.py:45
  90.8 12.6 %collective-permute-start.17 = (bf16[512,2048]{1,0:T(8,128)(2,1)S(1)}, bf16[512,2048]{1,0:T(8,128)(2,1)S(1)}, u32[]{:S(2)}, u32[]{:S(2)}) collective-permute-start(bf16[512,2048]{1,0:T(8,128)(2,1)S(1)} %shard_map.86), channel_id=1, source_target_pairs={{16,0},{17,1},{18,2},{19,3},{20,4},{21,5},{22,6},{23,7},{24,8},{25... | collective-permute-start | bytes 6291464 | tf_op jit(solution)/shard_map/ppermute | solution.py:45
  94.2 9.3 %collective-permute-start.12 = (bf16[128,2048]{1,0:T(8,128)(2,1)S(1)}, bf16[128,2048]{1,0:T(8,128)(2,1)S(1)}, u32[]{:S(2)}, u32[]{:S(2)}) collective-permute-start(bf16[128,2048]{1,0:T(8,128)(2,1)S(1)} %slice.259), channel_id=1, source_target_pairs={{96,0},{97,1},{98,2},{99,3},{100,4},{101,5},{102,6},{103,7},{104,8... | collective-permute-start | bytes 1572872 | tf_op jit(solution)/shard_map/ppermute | solution.py:45
  107.9 19.1 %collective-permute-start.18 = (bf16[256,2048]{1,0:T(8,128)(2,1)S(1)}, bf16[256,2048]{1,0:T(8,128)(2,1)S(1)}, u32[]{:S(2)}, u32[]{:S(2)}) collective-permute-start(bf16[256,2048]{1,0:T(8,128)(2,1)S(1)} %get-tuple-element.59), channel_id=1, source_target_pairs={{32,0},{33,1},{34,2},{35,3},{36,4},{37,5},{38,6},{39,7},{40,8},{41... | collective-permute-start | bytes 3145736 | tf_op jit(solution)/shard_map/ppermute | solution.py:45
  110.5 17.0 %collective-permute-start.13 = (bf16[128,2048]{1,0:T(8,128)(2,1)S(1)}, bf16[128,2048]{1,0:T(8,128)(2,1)S(1)}, u32[]{:S(2)}, u32[]{:S(2)}) collective-permute-start(bf16[128,2048]{1,0:T(8,128)(2,1)S(1)} %pad_maximum_fusion.2), channel_id=1, source_target_pairs={{96,0},{97,1},{98,2},{99,3},{100,4},{101,5},{102,6},{103,7},{104,8... | collective-permute-start | bytes 1572872 | tf_op jit(solution)/shard_map/ppermute | solution.py:45
  127.5 14.9 %collective-permute-start.19 = (bf16[128,2048]{1,0:T(8,128)(2,1)S(1)}, bf16[128,2048]{1,0:T(8,128)(2,1)S(1)}, u32[]{:S(2)}, u32[]{:S(2)}) collective-permute-start(bf16[128,2048]{1,0:T(8,128)(2,1)S(1)} %slice.258), channel_id=1, source_target_pairs={{96,0},{97,1},{98,2},{99,3},{100,4},{101,5},{102,6},{103,7},{104,8... | collective-permute-start | bytes 1572872 | tf_op jit(solution)/shard_map/ppermute | solution.py:45
  127.7 24.8 %collective-permute-start.14 = (bf16[256,2048]{1,0:T(8,128)(2,1)S(1)}, bf16[256,2048]{1,0:T(8,128)(2,1)S(1)}, u32[]{:S(2)}, u32[]{:S(2)}) collective-permute-start(bf16[256,2048]{1,0:T(8,128)(2,1)S(1)} %pad_maximum_fusion.refs_0_.refs_4_), channel_id=1, source_target_pairs={{32,0},{33,1},{34,2},{35,3},{36,4},{37,5},{38,6},{39,7},{40,8},{41... | collective-permute-start | bytes 3145736 | tf_op jit(solution)/shard_map/ppermute | solution.py:45
  142.8 9.6 %collective-permute-start.20 = (bf16[128,2048]{1,0:T(8,128)(2,1)S(1)}, bf16[128,2048]{1,0:T(8,128)(2,1)S(1)}, u32[]{:S(2)}, u32[]{:S(2)}) collective-permute-start(bf16[128,2048]{1,0:T(8,128)(2,1)S(1)} %pad_maximum_fusion.3), channel_id=1, source_target_pairs={{96,0},{97,1},{98,2},{99,3},{100,4},{101,5},{102,6},{103,7},{104,8... | collective-permute-start | bytes 1572872 | tf_op jit(solution)/shard_map/ppermute | solution.py:45
  152.4 10.8 %collective-permute-start.23 = (bf16[256,2048]{1,0:T(8,128)(2,1)S(1)}, bf16[256,2048]{1,0:T(8,128)(2,1)S(1)}, u32[]{:S(2)}, u32[]{:S(2)}) collective-permute-start(bf16[256,2048]{1,0:T(8,128)(2,1)S(1)} %collective-permute-done.14.refs_1_.refs_5_), channel_id=1, source_target_pairs={{16,0},{17,1},{18,2},{19,3},{20,4},{21,5},{22,6},{23,7},{24,8},{25... | collective-permute-start | bytes 3145736 | tf_op jit(solution)/shard_map/ppermute | solution.py:45
  152.5 10.7 %collective-permute-start.22 = (bf16[256,2048]{1,0:T(8,128)(2,1)S(1)}, bf16[256,2048]{1,0:T(8,128)(2,1)S(1)}, u32[]{:S(2)}, u32[]{:S(2)}) collective-permute-start(bf16[256,2048]{1,0:T(8,128)(2,1)S(1)} %pad_maximum_fusion.refs_0_.refs_4_), channel_id=1, source_target_pairs={{16,0},{17,1},{18,2},{19,3},{20,4},{21,5},{22,6},{23,7},{24,8},{25... | collective-permute-start | bytes 3145736 | tf_op jit(solution)/shard_map/ppermute | solution.py:45
  153.0 16.7 %collective-permute-start.26 = (bf16[256,2048]{1,0:T(8,128)(2,1)S(1)}, bf16[256,2048]{1,0:T(8,128)(2,1)S(1)}, u32[]{:S(2)}, u32[]{:S(2)}) collective-permute-start(bf16[256,2048]{1,0:T(8,128)(2,1)S(1)} %pad_maximum_fusion.1.refs_0_.refs_4_), channel_id=1, source_target_pairs={{32,0},{33,1},{34,2},{35,3},{36,4},{37,5},{38,6},{39,7},{40,8},{41... | collective-permute-start | bytes 3145736 | tf_op jit(solution)/shard_map/ppermute | solution.py:45
  161.3 16.1 %collective-permute-start.21 = (bf16[256,2048]{1,0:T(8,128)(2,1)S(1)}, bf16[256,2048]{1,0:T(8,128)(2,1)S(1)}, u32[]{:S(2)}, u32[]{:S(2)}) collective-permute-start(bf16[256,2048]{1,0:T(8,128)(2,1)S(1)} %get-tuple-element.62), channel_id=1, source_target_pairs={{12,0},{13,1},{14,2},{15,3},{8,4},{9,5},{10,6},{11,7},{4,8},{5,9},... | collective-permute-start | bytes 3145736 | tf_op jit(solution)/shard_map/ppermute | solution.py:45
  167.6 18.4 %collective-permute-start.24 = (bf16[256,2048]{1,0:T(8,128)(2,1)S(1)}, bf16[256,2048]{1,0:T(8,128)(2,1)S(1)}, u32[]{:S(2)}, u32[]{:S(2)}) collective-permute-start(bf16[256,2048]{1,0:T(8,128)(2,1)S(1)} %get-tuple-element.66), channel_id=1, source_target_pairs={{3,0},{2,1},{1,2},{0,3},{7,4},{6,5},{5,6},{4,7},{11,8},{10,9},{9,1... | collective-permute-start | bytes 3145736 | tf_op jit(solution)/shard_map/ppermute | solution.py:45
  168.5 24.3 %collective-permute-start.28 = (bf16[256,2048]{1,0:T(8,128)(2,1)S(1)}, bf16[256,2048]{1,0:T(8,128)(2,1)S(1)}, u32[]{:S(2)}, u32[]{:S(2)}) collective-permute-start(bf16[256,2048]{1,0:T(8,128)(2,1)S(1)} %pad_maximum_fusion.1.refs_0_.refs_4_), channel_id=1, source_target_pairs={{16,0},{17,1},{18,2},{19,3},{20,4},{21,5},{22,6},{23,7},{24,8},{25... | collective-permute-start | bytes 3145736 | tf_op jit(solution)/shard_map/ppermute | solution.py:45
  169.7 23.1 %collective-permute-start.29 = (bf16[256,2048]{1,0:T(8,128)(2,1)S(1)}, bf16[256,2048]{1,0:T(8,128)(2,1)S(1)}, u32[]{:S(2)}, u32[]{:S(2)}) collective-permute-start(bf16[256,2048]{1,0:T(8,128)(2,1)S(1)} %collective-permute-done.26.refs_1_.refs_5_), channel_id=1, source_target_pairs={{16,0},{17,1},{18,2},{19,3},{20,4},{21,5},{22,6},{23,7},{24,8},{25... | collective-permute-start | bytes 3145736 | tf_op jit(solution)/shard_map/ppermute | solution.py:45
  186.4 12.1 %collective-permute-start.25 = (bf16[128,2048]{1,0:T(8,128)(2,1)S(1)}, bf16[128,2048]{1,0:T(8,128)(2,1)S(1)}, u32[]{:S(2)}, u32[]{:S(2)}) collective-permute-start(bf16[128,2048]{1,0:T(8,128)(2,1)S(1)} %slice.257), channel_id=1, source_target_pairs={{4,0},{5,1},{6,2},{7,3},{0,4},{1,5},{2,6},{3,7},{12,8},{13,9},{14,... | collective-permute-start | bytes 1572872 | tf_op jit(solution)/shard_map/ppermute | solution.py:45
  188.4 13.9 %collective-permute-start.30 = (bf16[128,2048]{1,0:T(8,128)(2,1)S(1)}, bf16[128,2048]{1,0:T(8,128)(2,1)S(1)}, u32[]{:S(2)}, u32[]{:S(2)}) collective-permute-start(bf16[128,2048]{1,0:T(8,128)(2,1)S(1)} %slice.256), channel_id=1, source_target_pairs={{1,0},{0,1},{3,2},{2,3},{5,4},{4,5},{7,6},{6,7},{9,8},{8,9},{11,10... | collective-permute-start | bytes 1572872 | tf_op jit(solution)/shard_map/ppermute | solution.py:45
  197.1 16.1 %collective-permute-start.31 = (bf16[256,2048]{1,0:T(8,128)(2,1)S(1)}, bf16[256,2048]{1,0:T(8,128)(2,1)S(1)}, u32[]{:S(2)}, u32[]{:S(2)}) collective-permute-start(bf16[256,2048]{1,0:T(8,128)(2,1)S(1)} %get-tuple-element.75), channel_id=1, source_target_pairs={{3,0},{2,1},{1,2},{0,3},{7,4},{6,5},{5,6},{4,7},{11,8},{10,9},{9,1... | collective-permute-start | bytes 3145736 | tf_op jit(solution)/shard_map/ppermute | solution.py:45
  197.2 16.3 %collective-permute-start.27 = (bf16[256,2048]{1,0:T(8,128)(2,1)S(1)}, bf16[256,2048]{1,0:T(8,128)(2,1)S(1)}, u32[]{:S(2)}, u32[]{:S(2)}) collective-permute-start(bf16[256,2048]{1,0:T(8,128)(2,1)S(1)} %get-tuple-element.70), channel_id=1, source_target_pairs={{12,0},{13,1},{14,2},{15,3},{8,4},{9,5},{10,6},{11,7},{4,8},{5,9},... | collective-permute-start | bytes 3145736 | tf_op jit(solution)/shard_map/ppermute | solution.py:45
  214.0 10.8 %collective-permute-start.32 = (bf16[128,2048]{1,0:T(8,128)(2,1)S(1)}, bf16[128,2048]{1,0:T(8,128)(2,1)S(1)}, u32[]{:S(2)}, u32[]{:S(2)}) collective-permute-start(bf16[128,2048]{1,0:T(8,128)(2,1)S(1)} %slice.255), channel_id=1, source_target_pairs={{4,0},{5,1},{6,2},{7,3},{0,4},{1,5},{2,6},{3,7},{12,8},{13,9},{14,... | collective-permute-start | bytes 1572872 | tf_op jit(solution)/shard_map/ppermute | solution.py:45
  214.7 15.5 %collective-permute-start.34 = (bf16[128,2048]{1,0:T(8,128)(2,1)S(1)}, bf16[128,2048]{1,0:T(8,128)(2,1)S(1)}, u32[]{:S(2)}, u32[]{:S(2)}) collective-permute-start(bf16[128,2048]{1,0:T(8,128)(2,1)S(1)} %slice.254), channel_id=1, source_target_pairs={{1,0},{0,1},{3,2},{2,3},{5,4},{4,5},{7,6},{6,7},{9,8},{8,9},{11,10... | collective-permute-start | bytes 1572872 | tf_op jit(solution)/shard_map/ppermute | solution.py:45
  225.0 14.4 %collective-permute-start.33 = (bf16[128,2048]{1,0:T(8,128)(2,1)S(1)}, bf16[128,2048]{1,0:T(8,128)(2,1)S(1)}, u32[]{:S(2)}, u32[]{:S(2)}) collective-permute-start(bf16[128,2048]{1,0:T(8,128)(2,1)S(1)} %pad_maximum_fusion.4), channel_id=1, source_target_pairs={{3,0},{2,1},{1,2},{0,3},{7,4},{6,5},{5,6},{4,7},{11,8},{10,9},{9,1... | collective-permute-start | bytes 1572872 | tf_op jit(solution)/shard_map/ppermute | solution.py:45
  230.4 14.3 %collective-permute-start.36 = (bf16[128,2048]{1,0:T(8,128)(2,1)S(1)}, bf16[128,2048]{1,0:T(8,128)(2,1)S(1)}, u32[]{:S(2)}, u32[]{:S(2)}) collective-permute-start(bf16[128,2048]{1,0:T(8,128)(2,1)S(1)} %pad_maximum_fusion.5), channel_id=1, source_target_pairs={{12,0},{13,1},{14,2},{15,3},{8,4},{9,5},{10,6},{11,7},{4,8},{5,9},... | collective-permute-start | bytes 1572872 | tf_op jit(solution)/shard_map/ppermute | solution.py:45
  240.2 9.1 %collective-permute-start.35 = (bf16[64,2048]{1,0:T(8,128)(2,1)}, bf16[64,2048]{1,0:T(8,128)(2,1)S(1)}, u32[]{:S(2)}, u32[]{:S(2)}) collective-permute-start(bf16[64,2048]{1,0:T(8,128)(2,1)} %fusion.15), channel_id=1, source_target_pairs={{1,0},{0,1},{3,2},{2,3},{5,4},{4,5},{7,6},{6,7},{9,8},{8,9},{11,10... | collective-permute-start | bytes 786440 | tf_op jit(solution)/shard_map/ppermute | solution.py:45
  245.6 6.7 %collective-permute-start.37 = (bf16[64,2048]{1,0:T(8,128)(2,1)}, bf16[64,2048]{1,0:T(8,128)(2,1)}, u32[]{:S(2)}, u32[]{:S(2)}) collective-permute-start(bf16[64,2048]{1,0:T(8,128)(2,1)} %fusion.12), channel_id=1, source_target_pairs={{4,0},{5,1},{6,2},{7,3},{0,4},{1,5},{2,6},{3,7},{12,8},{13,9},{14,... | collective-permute-start | bytes 786440 | tf_op jit(solution)/shard_map/ppermute | solution.py:45

commit v6 on v5

--- a/solution.py
+++ b/solution.py
@@ -351,34 +351,24 @@
     own_a = {True: both[0], False: both[1]}
     near_a = joined(own_a, neighbours(own_a))
     rest_a = others(near_a)
-    step_b = neighbours(own_b)
+    near_of_b = neighbours(own_b)
     sent_a = panel_dot(False, near_a, rest_a, rest_a[True])
-    got_a = after(exchange(sent_a, other_core), step_b[True], step_b[False])
-    kept_a, send_a = panel_dot(True, near_a, rest_a, more=got_a)
-    step_a = exchange(send_a, along_z(0))
-    near_b = joined(own_b, step_b)
+    kept_a, send_a = panel_dot(True, near_a, rest_a, more=exchange(sent_a, other_core))
+    step_a = after(exchange(send_a, along_z(0)), near_of_b[True], near_of_b[False])
+    near_b = joined(own_b, near_of_b)
     rest_b = others(near_b)
-    sent_b = panel_dot(False, near_b, rest_b, rest_b[True], send_a)
     half_a = halfway(kept_a, step_a)
     turn_a = exchange(half_a[1].astype(BF), along_z(1))
-    got_b = after(exchange(sent_b, other_core), turn_a)
-    kept_b, send_b = panel_dot(True, near_b, rest_b, more=got_b)
+    mine_a = hidden_of(half_a[0] + turn_a.astype(F32))
+    sent_b = panel_dot(False, near_b, rest_b, rest_b[True], mine_a)
+    next_a = exchange(mine_a, along_z(1))
+    got_b = after(exchange(sent_b, other_core), next_a)
+    pair_a = join(place, mine_a, next_a)
+    far_a = exchange(pair_a, along_z(0))
+    kept_b, send_b = panel_dot(True, near_b, rest_b, pair_a, more=got_b)
     step_b = exchange(send_b, along_z(0))
-    half_b = halfway(kept_b, step_b)
-    mine_a = hidden_of(half_a[0] + turn_a.astype(F32))
-    next_a = exchange(mine_a, along_z(1))
-    turn_b = exchange(half_b[1].astype(BF), along_z(1))
-    pair_a = jnp.concatenate([mine_a, next_a], axis=0)
-    far_a = exchange(pair_a, along_z(0))
-    mine_b = hidden_of(half_b[0] + turn_b.astype(F32))
-    next_b = exchange(mine_b, along_z(1))
-    pair_b = jnp.concatenate([mine_b, next_b], axis=0)
-    far_b = exchange(pair_b, along_z(0))
-    far_a = after(far_a, pair_b)
     hid_a = {True: (pair_a, far_a)}
     hid_a[False] = (exchange(pair_a, other_core), exchange(far_a, other_core))
-    hid_b = {True: (pair_b, far_b)}
-    hid_b[False] = (exchange(pair_b, other_core), exchange(far_b, other_core))
 
     in_pairs, out_pairs = [], []
     for base, keep in ((0, True), (2, False)):
@@ -414,25 +404,38 @@
     out_a, out_b, got_a, got_b = {}, {}, {}, {}
     sums_a, sums_b, last_a, last_b, total_a, total_b = {}, {}, {}, {}, {}, {}
     out_a[True] = out_dot(True, hid_a[True])
-    out_a[False] = out_dot(False, hid_a[False], out_a[True][0])
+    half_b = halfway(kept_b, after(step_b, out_a[True][0]))
+    turn_b = exchange(half_b[1].astype(BF), along_z(1))
+    out_a[False] = out_dot(False, hid_a[False], out_a[True][0], step_b)
+    mine_b = hidden_of(half_b[0] + after(turn_b, out_a[False][0]).astype(F32))
+    next_b = exchange(mine_b, along_z(1))
     for keep in both_ways:
         got_a[keep] = exchange(out_a[keep][1], along(keep, True, 1))
-    grad_in = grads(0, near_a, rest_a, hid_a, None, out_a[False][0])
+    grad_in = grads(0, near_a, rest_a, hid_a, None, out_a[False][0], turn_b)
+    pair_b = join(place, mine_b, after(next_b, grad_in))
+    far_b = exchange(pair_b, along_z(0))
+    grad_out = grads(1, near_a, rest_a, hid_a, None, next_b, got_a[True], got_a[False], grad_in)
     for keep in both_ways:
         got = after(got_a[keep], grad_in, got_a[not keep])
         sums_a[keep], last_a[keep] = second_half(keep, out_a[keep][0], got)
-    out_b[True] = out_dot(True, hid_b[True], got_a[True], got_a[False], grad_in)
+    far_b = after(far_b, grad_out)
+    hid_b = {True: (pair_b, far_b)}
+    hid_b[False] = (exchange(pair_b, other_core), exchange(far_b, other_core))
+
+    out_b[True] = out_dot(True, hid_b[True])
     out_b[False] = out_dot(False, hid_b[False], out_b[True][0])
     for keep in both_ways:
         got_b[keep] = exchange(out_b[keep][1], along(keep, True, 1))
-    grad_out = grads(1, near_a, rest_a, hid_a, None, out_b[False][0], last_a[True], last_a[False])
-    for keep in both_ways:
-        got = after(got_b[keep], grad_out, got_b[not keep])
+    grad_in = grads(
+        0, near_b, rest_b, hid_b, grad_in, out_b[False][0], last_a[True], last_a[False]
+    )
+    for keep in both_ways:
+        got = after(got_b[keep], grad_in, got_b[not keep])
         sums_b[keep], last_b[keep] = second_half(keep, out_b[keep][0], got)
-    grad_in = grads(0, near_b, rest_b, hid_b, grad_in, got_b[True], got_b[False], grad_out)
+    grad_out = grads(1, near_b, rest_b, hid_b, grad_out, got_b[True], got_b[False], grad_in)
     for keep in both_ways:
         total_a[keep] = sums_a[keep] + last_a[keep].astype(F32)
-        total_b[keep] = sums_b[keep] + after(last_b[keep], grad_in).astype(F32)
+        total_b[keep] = sums_b[keep] + after(last_b[keep], grad_out, last_b[not keep]).astype(F32)
 
     part = block // PARTS
     pick = lambda keep, piece: jnp.concatenate(
@@ -446,9 +449,8 @@
     for keep in both_ways:
         passed = jnp.concatenate([pick(keep, 2), pick(keep, 3)], axis=0).astype(BF)
         gots[keep] = exchange(passed, along(keep, False, 1))
-    grad_out = grads(1, near_b, rest_b, hid_b, grad_out, last_b[True], last_b[False], grad_in)
-    for keep in both_ways:
-        got = after(gots[keep], grad_out).astype(F32)
+    for keep in both_ways:
+        got = after(gots[keep], gots[not keep]).astype(F32)
         last = (pick(keep, 1) + got[block:]).astype(BF)
         done[keep] = (
             pick(keep, 0) + got[:block] + exchange(last, along(keep, False, 0)).astype(F32)

time: 255 us -> 249 us (0.976)
  the two profiles are of different devices: /device:TPU:32 before, /device:TPU:8 now
where the time goes in v6:
time: 249 us
  waiting for transfers between devices  120 us (48%)
  Pallas kernels  66.4 us (27%)
  starting transfers between devices  47.1 us (19%)
  other arithmetic  7.52 us (3%)
  local copies, waits for them, and re-layouts  6.77 us (3%)
    ppermute x38, waiting for transfers between devices, exchange(): return lax.ppermute(array, AXES, pairs)  120 us
    ppermute x38, starting transfers between devices, exchange(): return lax.ppermute(array, AXES, pairs)  47.1 us
    pallas_call x8, Pallas kernels, pair_dot(): pl.pallas_call(functools.partial(pair_kernel, keep, hidden, more is not N...  35.6 us
    pallas_call x4, Pallas kernels, grad_dot(): pl.pallas_call(functools.partial(grad_kernel, pairs, block, factor, begun...  24.1 us
    pallas_call x11, Pallas kernels, whole(): pl.pallas_call(kernel, in_specs=[pl.BlockSpec(memory_space=pltpu.SMEM)] +...  6.61 us
  transfers between devices with their start and end apart: 38, of which 27 were waited for; matrix products, arithmetic and copies ran while one was open for 3% of the time, Pallas kernels for 21%

profile of v6, /device:TPU:8, one launch (start us, length us, event | category | flops | bytes accessed | tf_op | source)
XLA Modules:
  0.0 248.7 jit_solution(18091080317757770921)
XLA Ops:
  5.2 4.4 %collective-permute-done.b_ref = bf16[64,2048]{1,0:T(8,128)(2,1)S(1)} collective-permute-done((bf16[64,2048]{1,0:T(8,128)(2,1)S(1)}, bf16[64,2048]{1,0:T(8,128)(2,1)S(1)}, u32[]{:S(2)}, u32[]{:S(2)}) %collective-permute-start) | collective-permute-done | bytes 262176 | tf_op jit(solution)/shard_map/ppermute | solution.py:45
  10.2 2.8 %collective-permute-start.1 = (bf16[128,2048]{1,0:T(8,128)(2,1)S(1)}, bf16[128,2048]{1,0:T(8,128)(2,1)S(1)}, u32[]{:S(2)}, u32[]{:S(2)}) collective-permute-start(bf16[128,2048]{1,0:T(8,128)(2,1)S(1)} %shard_map.76), channel_id=1, source_target_pairs={{12,0},{13,1},{14,2},{15,3},{8,4},{9,5},{10,6},{11,7},{4,8},{5,9},... | collective-permute-start | bytes 1572872 | tf_op jit(solution)/shard_map/ppermute | solution.py:45
  15.3 5.4 %collective-permute-done.1.c_ref = bf16[128,2048]{1,0:T(8,128)(2,1)S(1)} collective-permute-done((bf16[128,2048]{1,0:T(8,128)(2,1)S(1)}, bf16[128,2048]{1,0:T(8,128)(2,1)S(1)}, u32[]{:S(2)}, u32[]{:S(2)}) %collective-permute-start.1) | collective-permute-done | bytes 524320 | tf_op jit(solution)/shard_map/ppermute | solution.py:45
  26.2 7.3 %collective-permute-done.6.b_ref = bf16[128,2048]{1,0:T(8,128)(2,1)S(1)} collective-permute-done((bf16[128,2048]{1,0:T(8,128)(2,1)S(1)}, bf16[128,2048]{1,0:T(8,128)(2,1)S(1)}, u32[]{:S(2)}, u32[]{:S(2)}) %collective-permute-start.6) | collective-permute-done | bytes 524320 | tf_op jit(solution)/shard_map/ppermute | solution.py:45
  34.2 2.0 collective-permute-start.7
  38.5 2.7 %constant_dynamic-slice_fusion = (bf16[1024,1024]{1,0:T(8,128)(2,1)S(1)}, bf16[1024,1024]{1,0:T(8,128)(2,1)S(1)}) fusion(bf16[2048,1024]{1,0:T(8,128)(2,1)} %param.7, s32[]{:T(128)S(6)} %select_n.30, bf16[1024,2048]{1,0:T(8,128)(2,1)} %param.6), kind=kLoop, calls=%fused_computation.57 | loop fusion | bytes 8388612 | tf_op jit(solution)/shard_map/dynamic_slice | solution.py:310
  41.2 9.1 %collective-permute-done.7.refs_1_.refs_3_.refs_7_ = bf16[256,2048]{1,0:T(8,128)(2,1)S(1)} collective-permute-done((bf16[256,2048]{1,0:T(8,128)(2,1)S(1)}, bf16[256,2048]{1,0:T(8,128)(2,1)S(1)}, u32[]{:S(2)}, u32[]{:S(2)}) %collective-permute-start.7) | collective-permute-done | bytes 1048608 | tf_op jit(solution)/shard_map/ppermute | solution.py:45
  51.8 4.3 %shard_map.82 = bf16[512,2048]{1,0:T(8,128)(2,1)S(1)} custom-call(s32[2]{0:T(128)S(1)} %pad_add_fusion.place_ref, bf16[256,2048]{1,0:T(8,128)(2,1)S(1)} %shard_map.81.refs_0_.refs_2_.refs_6_, bf16[256,2048]{1,0:T(8,128)(2,1)S(1)} %collective-permute-done.7.refs_1_.refs_3_.refs_7_, bf16[1024,1024]{1,0:T(8,128)(2,1)S(1)} %get-tuple-element.124.refs_2_.refs_3_, ...), custom_call_target="tpu_custom_call" | custom-call | flops 2147483 | bytes 8388 | tf_op jit(solution)/shard_map/pallas_call | solution.py:229
  56.2 4.1 %collective-permute-done.8.refs_4_ = bf16[512,2048]{1,0:T(8,128)(2,1)S(1)} collective-permute-done((bf16[512,2048]{1,0:T(8,128)(2,1)S(1)}, bf16[512,2048]{1,0:T(8,128)(2,1)S(1)}, u32[]{:S(2)}, u32[]{:S(2)}) %collective-permute-start.8) | collective-permute-done | bytes 2097184 | tf_op jit(solution)/shard_map/ppermute | solution.py:45
  60.4 5.3 %shard_map.83 = (bf16[256,2048]{1,0:T(8,128)(2,1)S(1)}, bf16[256,2048]{1,0:T(8,128)(2,1)S(1)}) custom-call(s32[2]{0:T(128)S(1)} %pad_add_fusion.place_ref, bf16[256,2048]{1,0:T(8,128)(2,1)S(1)} %shard_map.80.refs_0_.refs_4_, bf16[256,2048]{1,0:T(8,128)(2,1)} %collective-permute-done.5.refs_1_.refs_5_, ...), custom_call_target="tpu_custom_call" | custom-call | flops 2147483 | bytes 8388 | tf_op jit(solution)/shard_map/pallas_call | solution.py:229
  65.7 2.0 collective-permute-start.9
  67.7 1.7 collective-permute-start.10
  69.4 1.7 collective-permute-start.11
  71.1 5.8 %collective-permute-done.10.b_ref = bf16[128,2048]{1,0:T(8,128)(2,1)S(1)} collective-permute-done((bf16[128,2048]{1,0:T(8,128)(2,1)S(1)}, bf16[128,2048]{1,0:T(8,128)(2,1)S(1)}, u32[]{:S(2)}, u32[]{:S(2)}) %collective-permute-start.10) | collective-permute-done | bytes 524320 | tf_op jit(solution)/shard_map/ppermute | solution.py:45
  76.9 1.7 collective-permute-done.11.b_ref
  78.5 2.0 collective-permute-done.9
  81.0 4.1 %collective-permute-start.12 = (bf16[128,2048]{1,0:T(8,128)(2,1)S(1)}, bf16[128,2048]{1,0:T(8,128)(2,1)S(1)}, u32[]{:S(2)}, u32[]{:S(2)}) collective-permute-start(bf16[128,2048]{1,0:T(8,128)(2,1)S(1)} %slice.259), channel_id=1, source_target_pairs={{96,0},{97,1},{98,2},{99,3},{100,4},{101,5},{102,6},{103,7},{104,8... | collective-permute-start | bytes 1572872 | tf_op jit(solution)/shard_map/ppermute | solution.py:45
  89.3 2.9 %collective-permute-done.12 = bf16[128,2048]{1,0:T(8,128)(2,1)S(1)} collective-permute-done((bf16[128,2048]{1,0:T(8,128)(2,1)S(1)}, bf16[128,2048]{1,0:T(8,128)(2,1)S(1)}, u32[]{:S(2)}, u32[]{:S(2)}) %collective-permute-start.12) | collective-permute-done | bytes 524320 | tf_op jit(solution)/shard_map/ppermute | solution.py:45
  92.7 9.1 %collective-permute-done.19.refs_1_.refs_3_.refs_7_ = bf16[256,2048]{1,0:T(8,128)(2,1)S(1)} collective-permute-done((bf16[256,2048]{1,0:T(8,128)(2,1)S(1)}, bf16[256,2048]{1,0:T(8,128)(2,1)S(1)}, u32[]{:S(2)}, u32[]{:S(2)}) %collective-permute-start.19) | collective-permute-done | bytes 1048608 | tf_op jit(solution)/shard_map/ppermute | solution.py:45
  102.6 4.3 %shard_map.88 = bf16[512,2048]{1,0:T(8,128)(2,1)S(1)} custom-call(s32[2]{0:T(128)S(1)} %pad_add_fusion.place_ref, bf16[256,2048]{1,0:T(8,128)(2,1)S(1)} %shard_map.87.refs_0_.refs_2_.refs_6_, bf16[256,2048]{1,0:T(8,128)(2,1)S(1)} %collective-permute-done.19.refs_1_.refs_3_.refs_7_, bf16[1024,1024]{1,0:T(8,128)(2,1)S(1)} %get-tuple-element.124.refs_2_.refs_3_, ...), custom_call_target="tpu_custom_call" | custom-call | flops 2147483 | bytes 8388 | tf_op jit(solution)/shard_map/pallas_call | solution.py:229
  107.0 10.4 %collective-permute-done.13.b_ref = bf16[128,2048]{1,0:T(8,128)(2,1)S(1)} collective-permute-done((bf16[128,2048]{1,0:T(8,128)(2,1)S(1)}, bf16[128,2048]{1,0:T(8,128)(2,1)S(1)}, u32[]{:S(2)}, u32[]{:S(2)}) %collective-permute-start.13) | collective-permute-done | bytes 524320 | tf_op jit(solution)/shard_map/ppermute | solution.py:45
  118.3 4.5 %shard_map.89 = (bf16[256,2048]{1,0:T(8,128)(2,1)S(1)}, bf16[256,2048]{1,0:T(8,128)(2,1)S(1)}) custom-call(s32[2]{0:T(128)S(1)} %pad_add_fusion.place_ref, bf16[256,2048]{1,0:T(8,128)(2,1)S(1)} %shard_map.86.refs_0_.refs_4_, bf16[256,2048]{1,0:T(8,128)(2,1)S(1)} %collective-permute-done.18.refs_1_.refs_5_, ...), custom_call_target="tpu_custom_call" | custom-call | flops 2147483 | bytes 8388 | tf_op jit(solution)/shard_map/pallas_call | solution.py:229
  122.8 2.1 collective-permute-start.21
  124.9 8.2 %collective-permute-done.14.refs_1_.refs_5_ = bf16[256,2048]{1,0:T(8,128)(2,1)S(1)} collective-permute-done((bf16[256,2048]{1,0:T(8,128)(2,1)S(1)}, bf16[256,2048]{1,0:T(8,128)(2,1)S(1)}, u32[]{:S(2)}, u32[]{:S(2)}) %collective-permute-start.14) | collective-permute-done | bytes 1048608 | tf_op jit(solution)/shard_map/ppermute | solution.py:45
  133.1 4.3 %shard_map.85 = (bf16[256,2048]{1,0:T(8,128)(2,1)S(1)}, bf16[256,2048]{1,0:T(8,128)(2,1)S(1)}) custom-call(s32[2]{0:T(128)S(1)} %pad_add_fusion.place_ref, bf16[256,2048]{1,0:T(8,128)(2,1)S(1)} %shard_map.84.refs_0_.refs_4_, bf16[256,2048]{1,0:T(8,128)(2,1)S(1)} %collective-permute-done.14.refs_1_.refs_5_, ...), custom_call_target="tpu_custom_call" | custom-call | flops 2147483 | bytes 8388 | tf_op jit(solution)/shard_map/pallas_call | solution.py:229
  137.4 6.9 %collective-permute-done.21 = bf16[256,2048]{1,0:T(8,128)(2,1)S(1)} collective-permute-done((bf16[256,2048]{1,0:T(8,128)(2,1)S(1)}, bf16[256,2048]{1,0:T(8,128)(2,1)S(1)}, u32[]{:S(2)}, u32[]{:S(2)}) %collective-permute-start.21) | collective-permute-done | bytes 1048608 | tf_op jit(solution)/shard_map/ppermute | solution.py:45
  144.9 2.0 collective-permute-start.15
  146.9 4.3 %shard_map.90 = (bf16[256,2048]{1,0:T(8,128)(2,1)S(1)}, bf16[256,2048]{1,0:T(8,128)(2,1)S(1)}) custom-call(s32[2]{0:T(128)S(1)} %pad_add_fusion.place_ref, bf16[256,2048]{1,0:T(8,128)(2,1)S(1)} %collective-permute-done.16.refs_0_.refs_6_.refs_2_, bf16[256,2048]{1,0:T(8,128)(2,1)S(1)} %collective-permute-done.17.refs_1_.refs_7_.refs_3_, ...), custom_call_target="tpu_custom_call" | custom-call | flops 2147483 | bytes 8388 | tf_op jit(solution)/shard_map/pallas_call | solution.py:229
  151.2 2.0 collective-permute-start.23
  153.2 2.0 collective-permute-done.22
  156.5 5.6 %shard_map.91.refs_8_ = f32[1024,1024]{1,0:T(8,128)} custom-call(bf16[256,2048]{1,0:T(8,128)(2,1)S(1)} %shard_map.80.refs_0_.refs_4_, bf16[256,2048]{1,0:T(8,128)(2,1)} %collective-permute-done.5.refs_1_.refs_5_, bf16[256,2048]{1,0:T(8,128)(2,1)S(1)} %shard_map.81.refs_0_.refs_2_.refs_6_, ...), custom_call_target="tpu_custom_call" | custom-call | flops 2147483 | bytes 5242 | tf_op jit(solution)/shard_map/pallas_call | solution.py:278
  162.1 5.2 %collective-permute-done.25.b_ref = bf16[128,2048]{1,0:T(8,128)(2,1)S(1)} collective-permute-done((bf16[128,2048]{1,0:T(8,128)(2,1)S(1)}, bf16[128,2048]{1,0:T(8,128)(2,1)S(1)}, u32[]{:S(2)}, u32[]{:S(2)}) %collective-permute-start.25) | collective-permute-done | bytes 524320 | tf_op jit(solution)/shard_map/ppermute | solution.py:45
  168.6 5.6 %shard_map.93.refs_8_ = f32[1024,1024]{1,0:T(8,128)} custom-call(bf16[256,2048]{1,0:T(8,128)(2,1)S(1)} %shard_map.84.refs_0_.refs_4_, bf16[256,2048]{1,0:T(8,128)(2,1)S(1)} %collective-permute-done.14.refs_1_.refs_5_, bf16[256,2048]{1,0:T(8,128)(2,1)S(1)} %collective-permute-done.16.refs_0_.refs_6_.refs_2_, ...), custom_call_target="tpu_custom_call" | custom-call | flops 2147483 | bytes 5242 | tf_op jit(solution)/shard_map/pallas_call | solution.py:278
  174.2 8.6 %collective-permute-done.26.refs_1_.refs_5_ = bf16[256,2048]{1,0:T(8,128)(2,1)S(1)} collective-permute-done((bf16[256,2048]{1,0:T(8,128)(2,1)S(1)}, bf16[256,2048]{1,0:T(8,128)(2,1)S(1)}, u32[]{:S(2)}, u32[]{:S(2)}) %collective-permute-start.26) | collective-permute-done | bytes 1048608 | tf_op jit(solution)/shard_map/ppermute | solution.py:45
  183.2 4.2 %collective-permute-start.30 = (bf16[128,2048]{1,0:T(8,128)(2,1)S(1)}, bf16[128,2048]{1,0:T(8,128)(2,1)S(1)}, u32[]{:S(2)}, u32[]{:S(2)}) collective-permute-start(bf16[128,2048]{1,0:T(8,128)(2,1)S(1)} %slice.256), channel_id=1, source_target_pairs={{1,0},{0,1},{3,2},{2,3},{5,4},{4,5},{7,6},{6,7},{9,8},{8,9},{11,10... | collective-permute-start | bytes 1572872 | tf_op jit(solution)/shard_map/ppermute | solution.py:45
  187.6 4.3 %shard_map.94 = (bf16[256,2048]{1,0:T(8,128)(2,1)S(1)}, bf16[256,2048]{1,0:T(8,128)(2,1)S(1)}) custom-call(s32[2]{0:T(128)S(1)} %pad_add_fusion.place_ref, bf16[256,2048]{1,0:T(8,128)(2,1)S(1)} %shard_map.92.refs_0_.refs_4_, bf16[256,2048]{1,0:T(8,128)(2,1)S(1)} %collective-permute-done.26.refs_1_.refs_5_, ...), custom_call_target="tpu_custom_call" | custom-call | flops 2147483 | bytes 8388 | tf_op jit(solution)/shard_map/pallas_call | solution.py:229
  191.9 2.6 %collective-permute-start.27 = (bf16[256,2048]{1,0:T(8,128)(2,1)S(1)}, bf16[256,2048]{1,0:T(8,128)(2,1)S(1)}, u32[]{:S(2)}, u32[]{:S(2)}) collective-permute-start(bf16[256,2048]{1,0:T(8,128)(2,1)S(1)} %get-tuple-element.77), channel_id=1, source_target_pairs={{12,0},{13,1},{14,2},{15,3},{8,4},{9,5},{10,6},{11,7},{4,8},{5,9},... | collective-permute-start | bytes 3145736 | tf_op jit(solution)/shard_map/ppermute | solution.py:45
  194.5 4.3 %shard_map.95 = (bf16[256,2048]{1,0:T(8,128)(2,1)S(1)}, bf16[256,2048]{1,0:T(8,128)(2,1)S(1)}) custom-call(s32[2]{0:T(128)S(1)} %pad_add_fusion.place_ref, bf16[256,2048]{1,0:T(8,128)(2,1)S(1)} %collective-permute-done.28.refs_0_.refs_6_.refs_2_, bf16[256,2048]{1,0:T(8,128)(2,1)S(1)} %collective-permute-done.29.refs_1_.refs_7_.refs_3_, ...), custom_call_target="tpu_custom_call" | custom-call | flops 2147483 | bytes 8388 | tf_op jit(solution)/shard_map/pallas_call | solution.py:229
  200.0 6.5 %shard_map.96 = f32[1024,1024]{1,0:T(8,128)} custom-call(bf16[256,2048]{1,0:T(8,128)(2,1)S(1)} %shard_map.86.refs_0_.refs_4_, bf16[256,2048]{1,0:T(8,128)(2,1)S(1)} %collective-permute-done.18.refs_1_.refs_5_, bf16[256,2048]{1,0:T(8,128)(2,1)S(1)} %shard_map.87.refs_0_.refs_2_.refs_6_, ...), custom_call_target="tpu_custom_call", output_to_operand_aliasing={{}: (8, {})} | custom-call | flops 2147483 | bytes 5242 | tf_op jit(solution)/shard_map/pallas_call | solution.py:278
  206.5 1.7 collective-permute-done.27
  208.2 5.5 %collective-permute-done.31 = bf16[256,2048]{1,0:T(8,128)(2,1)S(1)} collective-permute-done((bf16[256,2048]{1,0:T(8,128)(2,1)S(1)}, bf16[256,2048]{1,0:T(8,128)(2,1)S(1)}, u32[]{:S(2)}, u32[]{:S(2)}) %collective-permute-start.31) | collective-permute-done | bytes 1048608 | tf_op jit(solution)/shard_map/ppermute | solution.py:45
  216.0 6.5 %shard_map.97 = f32[1024,1024]{1,0:T(8,128)} custom-call(bf16[256,2048]{1,0:T(8,128)(2,1)S(1)} %shard_map.92.refs_0_.refs_4_, bf16[256,2048]{1,0:T(8,128)(2,1)S(1)} %collective-permute-done.26.refs_1_.refs_5_, bf16[256,2048]{1,0:T(8,128)(2,1)S(1)} %collective-permute-done.28.refs_0_.refs_6_.refs_2_, ...), custom_call_target="tpu_custom_call", output_to_operand_aliasing={{}: (8, {})} | custom-call | flops 2147483 | bytes 5242 | tf_op jit(solution)/shard_map/pallas_call | solution.py:278
  226.0 1.9 collective-permute-start.35
  228.0 5.6 %collective-permute-done.34 = bf16[128,2048]{1,0:T(8,128)(2,1)S(1)} collective-permute-done((bf16[128,2048]{1,0:T(8,128)(2,1)S(1)}, bf16[128,2048]{1,0:T(8,128)(2,1)S(1)}, u32[]{:S(2)}, u32[]{:S(2)}) %collective-permute-start.34) | collective-permute-done | bytes 524320 | tf_op jit(solution)/shard_map/ppermute | solution.py:45
  233.6 2.9 %collective-permute-done.35 = bf16[128,2048]{1,0:T(8,128)(2,1)S(1)} collective-permute-done((bf16[128,2048]{1,0:T(8,128)(2,1)S(1)}, bf16[128,2048]{1,0:T(8,128)(2,1)S(1)}, u32[]{:S(2)}, u32[]{:S(2)}) %collective-permute-start.35) | collective-permute-done | bytes 524320 | tf_op jit(solution)/shard_map/ppermute | solution.py:45
  237.3 1.8 collective-permute-start.36
  240.2 3.7 %collective-permute-done.36 = bf16[64,2048]{1,0:T(8,128)(2,1)S(1)} collective-permute-done((bf16[64,2048]{1,0:T(8,128)(2,1)}, bf16[64,2048]{1,0:T(8,128)(2,1)S(1)}, u32[]{:S(2)}, u32[]{:S(2)}) %collective-permute-start.36) | collective-permute-done | bytes 262176 | tf_op jit(solution)/shard_map/ppermute | solution.py:45
  243.9 2.8 %collective-permute-done.37 = bf16[64,2048]{1,0:T(8,128)(2,1)} collective-permute-done((bf16[64,2048]{1,0:T(8,128)(2,1)}, bf16[64,2048]{1,0:T(8,128)(2,1)}, u32[]{:S(2)}, u32[]{:S(2)}) %collective-permute-start.37) | collective-permute-done | bytes 262176 | tf_op jit(solution)/shard_map/ppermute | solution.py:45
  (104 shorter events, 38.9 us)
Async XLA Ops:
  0.7 1.0 copy-start.4
  1.7 0.9 copy-start.5
  3.2 6.5 %collective-permute-start = (bf16[64,2048]{1,0:T(8,128)(2,1)S(1)}, bf16[64,2048]{1,0:T(8,128)(2,1)S(1)}, u32[]{:S(2)}, u32[]{:S(2)}) collective-permute-start(bf16[64,2048]{1,0:T(8,128)(2,1)S(1)} %get-tuple-element.47.a_ref), channel_id=1, source_target_pairs={{4,0},{5,1},{6,2},{7,3},{0,4},{1,5},{2,6},{3,7},{12,8},{13,9},{14,... | collective-permute-start | bytes 786440 | tf_op jit(solution)/shard_map/ppermute | solution.py:45
  4.8 8.3 %collective-permute-start.2 = (bf16[64,2048]{1,0:T(8,128)(2,1)S(1)}, bf16[64,2048]{1,0:T(8,128)(2,1)S(1)}, u32[]{:S(2)}, u32[]{:S(2)}) collective-permute-start(bf16[64,2048]{1,0:T(8,128)(2,1)S(1)} %get-tuple-element.49.a_ref), channel_id=1, source_target_pairs={{1,0},{0,1},{3,2},{2,3},{5,4},{4,5},{7,6},{6,7},{9,8},{8,9},{11,10... | collective-permute-start | bytes 786440 | tf_op jit(solution)/shard_map/ppermute | solution.py:45
  10.2 10.5 %collective-permute-start.1 = (bf16[128,2048]{1,0:T(8,128)(2,1)S(1)}, bf16[128,2048]{1,0:T(8,128)(2,1)S(1)}, u32[]{:S(2)}, u32[]{:S(2)}) collective-permute-start(bf16[128,2048]{1,0:T(8,128)(2,1)S(1)} %shard_map.76), channel_id=1, source_target_pairs={{12,0},{13,1},{14,2},{15,3},{8,4},{9,5},{10,6},{11,7},{4,8},{5,9},... | collective-permute-start | bytes 1572872 | tf_op jit(solution)/shard_map/ppermute | solution.py:45
  13.7 9.3 %collective-permute-start.3 = (bf16[128,2048]{1,0:T(8,128)(2,1)S(1)}, bf16[128,2048]{1,0:T(8,128)(2,1)S(1)}, u32[]{:S(2)}, u32[]{:S(2)}) collective-permute-start(bf16[128,2048]{1,0:T(8,128)(2,1)S(1)} %shard_map.78), channel_id=1, source_target_pairs={{3,0},{2,1},{1,2},{0,3},{7,4},{6,5},{5,6},{4,7},{11,8},{10,9},{9,1... | collective-permute-start | bytes 1572872 | tf_op jit(solution)/shard_map/ppermute | solution.py:45
  21.3 0.8 copy-start
  23.6 0.8 copy-start.2
  24.4 9.2 %collective-permute-start.6 = (bf16[128,2048]{1,0:T(8,128)(2,1)S(1)}, bf16[128,2048]{1,0:T(8,128)(2,1)S(1)}, u32[]{:S(2)}, u32[]{:S(2)}) collective-permute-start(bf16[128,2048]{1,0:T(8,128)(2,1)S(1)} %get-tuple-element.52.a_ref), channel_id=1, source_target_pairs={{4,0},{5,1},{6,2},{7,3},{0,4},{1,5},{2,6},{3,7},{12,8},{13,9},{14,... | collective-permute-start | bytes 1572872 | tf_op jit(solution)/shard_map/ppermute | solution.py:45
  24.6 11.6 %collective-permute-start.4 = (bf16[128,2048]{1,0:T(8,128)(2,1)S(1)}, bf16[128,2048]{1,0:T(8,128)(2,1)S(1)}, u32[]{:S(2)}, u32[]{:S(2)}) collective-permute-start(bf16[128,2048]{1,0:T(8,128)(2,1)S(1)} %get-tuple-element.51.a_ref), channel_id=1, source_target_pairs={{1,0},{0,1},{3,2},{2,3},{5,4},{4,5},{7,6},{6,7},{9,8},{8,9},{11,10... | collective-permute-start | bytes 1572872 | tf_op jit(solution)/shard_map/ppermute | solution.py:45
  34.2 16.1 %collective-permute-start.7 = (bf16[256,2048]{1,0:T(8,128)(2,1)S(1)}, bf16[256,2048]{1,0:T(8,128)(2,1)S(1)}, u32[]{:S(2)}, u32[]{:S(2)}) collective-permute-start(bf16[256,2048]{1,0:T(8,128)(2,1)S(1)} %shard_map.81.refs_0_.refs_2_.refs_6_), channel_id=1, source_target_pairs={{12,0},{13,1},{14,2},{15,3},{8,4},{9,5},{10,6},{11,7},{4,8},{5,9},... | collective-permute-start | bytes 3145736 | tf_op jit(solution)/shard_map/ppermute | solution.py:45
  36.8 15.0 %collective-permute-start.5 = (bf16[256,2048]{1,0:T(8,128)(2,1)S(1)}, bf16[256,2048]{1,0:T(8,128)(2,1)}, u32[]{:S(2)}, u32[]{:S(2)}) collective-permute-start(bf16[256,2048]{1,0:T(8,128)(2,1)S(1)} %shard_map.80.refs_0_.refs_4_), channel_id=1, source_target_pairs={{3,0},{2,1},{1,2},{0,3},{7,4},{6,5},{5,6},{4,7},{11,8},{10,9},{9,1... | collective-permute-start | bytes 3145736 | tf_op jit(solution)/shard_map/ppermute | solution.py:45
  56.1 11.6 %copy-start.1 = (bf16[128,2048]{1,0:T(8,128)(2,1)S(1)}, bf16[128,2048]{1,0:T(8,128)(2,1)}, u32[]{:S(2)}) copy-start(bf16[128,2048]{1,0:T(8,128)(2,1)} %copy-done) | copy-start | bytes 1572868
  56.1 13.2 %copy-start.3 = (bf16[128,2048]{1,0:T(8,128)(2,1)S(1)}, bf16[128,2048]{1,0:T(8,128)(2,1)}, u32[]{:S(2)}) copy-start(bf16[128,2048]{1,0:T(8,128)(2,1)} %copy-done.2) | copy-start | bytes 1572868
  56.1 4.2 %collective-permute-start.8 = (bf16[512,2048]{1,0:T(8,128)(2,1)S(1)}, bf16[512,2048]{1,0:T(8,128)(2,1)S(1)}, u32[]{:S(2)}, u32[]{:S(2)}) collective-permute-start(bf16[512,2048]{1,0:T(8,128)(2,1)S(1)} %shard_map.82), channel_id=1, source_target_pairs={{16,0},{17,1},{18,2},{19,3},{20,4},{21,5},{22,6},{23,7},{24,8},{25... | collective-permute-start | bytes 6291464 | tf_op jit(solution)/shard_map/ppermute | solution.py:45
  65.7 14.9 %collective-permute-start.9 = (bf16[256,2048]{1,0:T(8,128)(2,1)S(1)}, bf16[256,2048]{1,0:T(8,128)(2,1)S(1)}, u32[]{:S(2)}, u32[]{:S(2)}) collective-permute-start(bf16[256,2048]{1,0:T(8,128)(2,1)S(1)} %get-tuple-element.55), channel_id=1, source_target_pairs={{32,0},{33,1},{34,2},{35,3},{36,4},{37,5},{38,6},{39,7},{40,8},{41... | collective-permute-start | bytes 3145736 | tf_op jit(solution)/shard_map/ppermute | solution.py:45
  67.7 9.2 %collective-permute-start.10 = (bf16[128,2048]{1,0:T(8,128)(2,1)S(1)}, bf16[128,2048]{1,0:T(8,128)(2,1)S(1)}, u32[]{:S(2)}, u32[]{:S(2)}) collective-permute-start(bf16[128,2048]{1,0:T(8,128)(2,1)S(1)} %copy-done.1), channel_id=1, source_target_pairs={{1,0},{0,1},{3,2},{2,3},{5,4},{4,5},{7,6},{6,7},{9,8},{8,9},{11,10... | collective-permute-start | bytes 1572872 | tf_op jit(solution)/shard_map/ppermute | solution.py:45
  69.4 9.2 %collective-permute-start.11 = (bf16[128,2048]{1,0:T(8,128)(2,1)S(1)}, bf16[128,2048]{1,0:T(8,128)(2,1)S(1)}, u32[]{:S(2)}, u32[]{:S(2)}) collective-permute-start(bf16[128,2048]{1,0:T(8,128)(2,1)S(1)} %copy-done.3), channel_id=1, source_target_pairs={{4,0},{5,1},{6,2},{7,3},{0,4},{1,5},{2,6},{3,7},{12,8},{13,9},{14,... | collective-permute-start | bytes 1572872 | tf_op jit(solution)/shard_map/ppermute | solution.py:45
  81.0 11.3 %collective-permute-start.12 = (bf16[128,2048]{1,0:T(8,128)(2,1)S(1)}, bf16[128,2048]{1,0:T(8,128)(2,1)S(1)}, u32[]{:S(2)}, u32[]{:S(2)}) collective-permute-start(bf16[128,2048]{1,0:T(8,128)(2,1)S(1)} %slice.259), channel_id=1, source_target_pairs={{96,0},{97,1},{98,2},{99,3},{100,4},{101,5},{102,6},{103,7},{104,8... | collective-permute-start | bytes 1572872 | tf_op jit(solution)/shard_map/ppermute | solution.py:45
  85.7 16.1 %collective-permute-start.19 = (bf16[256,2048]{1,0:T(8,128)(2,1)S(1)}, bf16[256,2048]{1,0:T(8,128)(2,1)S(1)}, u32[]{:S(2)}, u32[]{:S(2)}) collective-permute-start(bf16[256,2048]{1,0:T(8,128)(2,1)S(1)} %shard_map.87.refs_0_.refs_2_.refs_6_), channel_id=1, source_target_pairs={{12,0},{13,1},{14,2},{15,3},{8,4},{9,5},{10,6},{11,7},{4,8},{5,9},... | collective-permute-start | bytes 3145736 | tf_op jit(solution)/shard_map/ppermute | solution.py:45
  87.7 14.9 %collective-permute-start.18 = (bf16[256,2048]{1,0:T(8,128)(2,1)S(1)}, bf16[256,2048]{1,0:T(8,128)(2,1)S(1)}, u32[]{:S(2)}, u32[]{:S(2)}) collective-permute-start(bf16[256,2048]{1,0:T(8,128)(2,1)S(1)} %shard_map.86.refs_0_.refs_4_), channel_id=1, source_target_pairs={{3,0},{2,1},{1,2},{0,3},{7,4},{6,5},{5,6},{4,7},{11,8},{10,9},{9,1... | collective-permute-start | bytes 3145736 | tf_op jit(solution)/shard_map/ppermute | solution.py:45
  106.8 11.5 %collective-permute-start.20 = (bf16[512,2048]{1,0:T(8,128)(2,1)S(1)}, bf16[512,2048]{1,0:T(8,128)(2,1)S(1)}, u32[]{:S(2)}, u32[]{:S(2)}) collective-permute-start(bf16[512,2048]{1,0:T(8,128)(2,1)S(1)} %shard_map.88), channel_id=1, source_target_pairs={{16,0},{17,1},{18,2},{19,3},{20,4},{21,5},{22,6},{23,7},{24,8},{25... | collective-permute-start | bytes 6291464 | tf_op jit(solution)/shard_map/ppermute | solution.py:45
  106.9 10.5 %collective-permute-start.13 = (bf16[128,2048]{1,0:T(8,128)(2,1)S(1)}, bf16[128,2048]{1,0:T(8,128)(2,1)S(1)}, u32[]{:S(2)}, u32[]{:S(2)}) collective-permute-start(bf16[128,2048]{1,0:T(8,128)(2,1)S(1)} %pad_maximum_fusion.a_ref), channel_id=1, source_target_pairs={{96,0},{97,1},{98,2},{99,3},{100,4},{101,5},{102,6},{103,7},{104,8... | collective-permute-start | bytes 1572872 | tf_op jit(solution)/shard_map/ppermute | solution.py:45
  118.0 15.1 %collective-permute-start.14 = (bf16[256,2048]{1,0:T(8,128)(2,1)S(1)}, bf16[256,2048]{1,0:T(8,128)(2,1)S(1)}, u32[]{:S(2)}, u32[]{:S(2)}) collective-permute-start(bf16[256,2048]{1,0:T(8,128)(2,1)S(1)} %shard_map.84.refs_0_.refs_4_), channel_id=1, source_target_pairs={{32,0},{33,1},{34,2},{35,3},{36,4},{37,5},{38,6},{39,7},{40,8},{41... | collective-permute-start | bytes 3145736 | tf_op jit(solution)/shard_map/ppermute | solution.py:45
  122.8 21.5 %collective-permute-start.21 = (bf16[256,2048]{1,0:T(8,128)(2,1)S(1)}, bf16[256,2048]{1,0:T(8,128)(2,1)S(1)}, u32[]{:S(2)}, u32[]{:S(2)}) collective-permute-start(bf16[256,2048]{1,0:T(8,128)(2,1)S(1)} %get-tuple-element.64), channel_id=1, source_target_pairs={{32,0},{33,1},{34,2},{35,3},{36,4},{37,5},{38,6},{39,7},{40,8},{41... | collective-permute-start | bytes 3145736 | tf_op jit(solution)/shard_map/ppermute | solution.py:45
  124.9 22.0 %collective-permute-start.16 = (bf16[256,2048]{1,0:T(8,128)(2,1)S(1)}, bf16[256,2048]{1,0:T(8,128)(2,1)S(1)}, u32[]{:S(2)}, u32[]{:S(2)}) collective-permute-start(bf16[256,2048]{1,0:T(8,128)(2,1)S(1)} %shard_map.84.refs_0_.refs_4_), channel_id=1, source_target_pairs={{16,0},{17,1},{18,2},{19,3},{20,4},{21,5},{22,6},{23,7},{24,8},{25... | collective-permute-start | bytes 3145736 | tf_op jit(solution)/shard_map/ppermute | solution.py:45
  133.1 13.8 %collective-permute-start.17 = (bf16[256,2048]{1,0:T(8,128)(2,1)S(1)}, bf16[256,2048]{1,0:T(8,128)(2,1)S(1)}, u32[]{:S(2)}, u32[]{:S(2)}) collective-permute-start(bf16[256,2048]{1,0:T(8,128)(2,1)S(1)} %collective-permute-done.14.refs_1_.refs_5_), channel_id=1, source_target_pairs={{16,0},{17,1},{18,2},{19,3},{20,4},{21,5},{22,6},{23,7},{24,8},{25... | collective-permute-start | bytes 3145736 | tf_op jit(solution)/shard_map/ppermute | solution.py:45
  144.8 10.5 %collective-permute-start.22 = (bf16[128,2048]{1,0:T(8,128)(2,1)S(1)}, bf16[128,2048]{1,0:T(8,128)(2,1)S(1)}, u32[]{:S(2)}, u32[]{:S(2)}) collective-permute-start(bf16[128,2048]{1,0:T(8,128)(2,1)S(1)} %slice.258), channel_id=1, source_target_pairs={{96,0},{97,1},{98,2},{99,3},{100,4},{101,5},{102,6},{103,7},{104,8... | collective-permute-start | bytes 1572872 | tf_op jit(solution)/shard_map/ppermute | solution.py:45
  144.9 23.1 %collective-permute-start.15 = (bf16[256,2048]{1,0:T(8,128)(2,1)S(1)}, bf16[256,2048]{1,0:T(8,128)(2,1)S(1)}, u32[]{:S(2)}, u32[]{:S(2)}) collective-permute-start(bf16[256,2048]{1,0:T(8,128)(2,1)S(1)} %get-tuple-element.60), channel_id=1, source_target_pairs={{12,0},{13,1},{14,2},{15,3},{8,4},{9,5},{10,6},{11,7},{4,8},{5,9},... | collective-permute-start | bytes 3145736 | tf_op jit(solution)/shard_map/ppermute | solution.py:45
  151.2 16.8 %collective-permute-start.23 = (bf16[256,2048]{1,0:T(8,128)(2,1)S(1)}, bf16[256,2048]{1,0:T(8,128)(2,1)S(1)}, u32[]{:S(2)}, u32[]{:S(2)}) collective-permute-start(bf16[256,2048]{1,0:T(8,128)(2,1)S(1)} %get-tuple-element.70), channel_id=1, source_target_pairs={{3,0},{2,1},{1,2},{0,3},{7,4},{6,5},{5,6},{4,7},{11,8},{10,9},{9,1... | collective-permute-start | bytes 3145736 | tf_op jit(solution)/shard_map/ppermute | solution.py:45
  155.7 11.6 %collective-permute-start.25 = (bf16[128,2048]{1,0:T(8,128)(2,1)S(1)}, bf16[128,2048]{1,0:T(8,128)(2,1)S(1)}, u32[]{:S(2)}, u32[]{:S(2)}) collective-permute-start(bf16[128,2048]{1,0:T(8,128)(2,1)S(1)} %pad_maximum_fusion.1.a_ref), channel_id=1, source_target_pairs={{96,0},{97,1},{98,2},{99,3},{100,4},{101,5},{102,6},{103,7},{104,8... | collective-permute-start | bytes 1572872 | tf_op jit(solution)/shard_map/ppermute | solution.py:45
  167.9 14.9 %collective-permute-start.26 = (bf16[256,2048]{1,0:T(8,128)(2,1)S(1)}, bf16[256,2048]{1,0:T(8,128)(2,1)S(1)}, u32[]{:S(2)}, u32[]{:S(2)}) collective-permute-start(bf16[256,2048]{1,0:T(8,128)(2,1)S(1)} %shard_map.92.refs_0_.refs_4_), channel_id=1, source_target_pairs={{32,0},{33,1},{34,2},{35,3},{36,4},{37,5},{38,6},{39,7},{40,8},{41... | collective-permute-start | bytes 3145736 | tf_op jit(solution)/shard_map/ppermute | solution.py:45
  168.5 18.9 %collective-permute-start.24 = (bf16[128,2048]{1,0:T(8,128)(2,1)S(1)}, bf16[128,2048]{1,0:T(8,128)(2,1)S(1)}, u32[]{:S(2)}, u32[]{:S(2)}) collective-permute-start(bf16[128,2048]{1,0:T(8,128)(2,1)S(1)} %slice.257), channel_id=1, source_target_pairs={{4,0},{5,1},{6,2},{7,3},{0,4},{1,5},{2,6},{3,7},{12,8},{13,9},{14,... | collective-permute-start | bytes 1572872 | tf_op jit(solution)/shard_map/ppermute | solution.py:45
  168.6 25.9 %collective-permute-start.28 = (bf16[256,2048]{1,0:T(8,128)(2,1)S(1)}, bf16[256,2048]{1,0:T(8,128)(2,1)S(1)}, u32[]{:S(2)}, u32[]{:S(2)}) collective-permute-start(bf16[256,2048]{1,0:T(8,128)(2,1)S(1)} %shard_map.92.refs_0_.refs_4_), channel_id=1, source_target_pairs={{16,0},{17,1},{18,2},{19,3},{20,4},{21,5},{22,6},{23,7},{24,8},{25... | collective-permute-start | bytes 3145736 | tf_op jit(solution)/shard_map/ppermute | solution.py:45
  182.8 11.7 %collective-permute-start.29 = (bf16[256,2048]{1,0:T(8,128)(2,1)S(1)}, bf16[256,2048]{1,0:T(8,128)(2,1)S(1)}, u32[]{:S(2)}, u32[]{:S(2)}) collective-permute-start(bf16[256,2048]{1,0:T(8,128)(2,1)S(1)} %collective-permute-done.26.refs_1_.refs_5_), channel_id=1, source_target_pairs={{16,0},{17,1},{18,2},{19,3},{20,4},{21,5},{22,6},{23,7},{24,8},{25... | collective-permute-start | bytes 3145736 | tf_op jit(solution)/shard_map/ppermute | solution.py:45
  183.2 16.6 %collective-permute-start.30 = (bf16[128,2048]{1,0:T(8,128)(2,1)S(1)}, bf16[128,2048]{1,0:T(8,128)(2,1)S(1)}, u32[]{:S(2)}, u32[]{:S(2)}) collective-permute-start(bf16[128,2048]{1,0:T(8,128)(2,1)S(1)} %slice.256), channel_id=1, source_target_pairs={{1,0},{0,1},{3,2},{2,3},{5,4},{4,5},{7,6},{6,7},{9,8},{8,9},{11,10... | collective-permute-start | bytes 1572872 | tf_op jit(solution)/shard_map/ppermute | solution.py:45
  191.9 16.3 %collective-permute-start.27 = (bf16[256,2048]{1,0:T(8,128)(2,1)S(1)}, bf16[256,2048]{1,0:T(8,128)(2,1)S(1)}, u32[]{:S(2)}, u32[]{:S(2)}) collective-permute-start(bf16[256,2048]{1,0:T(8,128)(2,1)S(1)} %get-tuple-element.77), channel_id=1, source_target_pairs={{12,0},{13,1},{14,2},{15,3},{8,4},{9,5},{10,6},{11,7},{4,8},{5,9},... | collective-permute-start | bytes 3145736 | tf_op jit(solution)/shard_map/ppermute | solution.py:45
  198.8 14.9 %collective-permute-start.31 = (bf16[256,2048]{1,0:T(8,128)(2,1)S(1)}, bf16[256,2048]{1,0:T(8,128)(2,1)S(1)}, u32[]{:S(2)}, u32[]{:S(2)}) collective-permute-start(bf16[256,2048]{1,0:T(8,128)(2,1)S(1)} %get-tuple-element.82), channel_id=1, source_target_pairs={{3,0},{2,1},{1,2},{0,3},{7,4},{6,5},{5,6},{4,7},{11,8},{10,9},{9,1... | collective-permute-start | bytes 3145736 | tf_op jit(solution)/shard_map/ppermute | solution.py:45
  214.1 9.3 %collective-permute-start.32 = (bf16[128,2048]{1,0:T(8,128)(2,1)S(1)}, bf16[128,2048]{1,0:T(8,128)(2,1)S(1)}, u32[]{:S(2)}, u32[]{:S(2)}) collective-permute-start(bf16[128,2048]{1,0:T(8,128)(2,1)S(1)} %slice.255), channel_id=1, source_target_pairs={{4,0},{5,1},{6,2},{7,3},{0,4},{1,5},{2,6},{3,7},{12,8},{13,9},{14,... | collective-permute-start | bytes 1572872 | tf_op jit(solution)/shard_map/ppermute | solution.py:45
  214.6 9.3 %collective-permute-start.33 = (bf16[128,2048]{1,0:T(8,128)(2,1)S(1)}, bf16[128,2048]{1,0:T(8,128)(2,1)S(1)}, u32[]{:S(2)}, u32[]{:S(2)}) collective-permute-start(bf16[128,2048]{1,0:T(8,128)(2,1)S(1)} %slice.254), channel_id=1, source_target_pairs={{1,0},{0,1},{3,2},{2,3},{5,4},{4,5},{7,6},{6,7},{9,8},{8,9},{11,10... | collective-permute-start | bytes 1572872 | tf_op jit(solution)/shard_map/ppermute | solution.py:45
  224.4 9.3 %collective-permute-start.34 = (bf16[128,2048]{1,0:T(8,128)(2,1)S(1)}, bf16[128,2048]{1,0:T(8,128)(2,1)S(1)}, u32[]{:S(2)}, u32[]{:S(2)}) collective-permute-start(bf16[128,2048]{1,0:T(8,128)(2,1)S(1)} %pad_maximum_fusion.2), channel_id=1, source_target_pairs={{3,0},{2,1},{1,2},{0,3},{7,4},{6,5},{5,6},{4,7},{11,8},{10,9},{9,1... | collective-permute-start | bytes 1572872 | tf_op jit(solution)/shard_map/ppermute | solution.py:45
  226.0 10.5 %collective-permute-start.35 = (bf16[128,2048]{1,0:T(8,128)(2,1)S(1)}, bf16[128,2048]{1,0:T(8,128)(2,1)S(1)}, u32[]{:S(2)}, u32[]{:S(2)}) collective-permute-start(bf16[128,2048]{1,0:T(8,128)(2,1)S(1)} %pad_maximum_fusion.3), channel_id=1, source_target_pairs={{12,0},{13,1},{14,2},{15,3},{8,4},{9,5},{10,6},{11,7},{4,8},{5,9},... | collective-permute-start | bytes 1572872 | tf_op jit(solution)/shard_map/ppermute | solution.py:45
  237.3 6.6 %collective-permute-start.36 = (bf16[64,2048]{1,0:T(8,128)(2,1)}, bf16[64,2048]{1,0:T(8,128)(2,1)S(1)}, u32[]{:S(2)}, u32[]{:S(2)}) collective-permute-start(bf16[64,2048]{1,0:T(8,128)(2,1)} %fusion.15), channel_id=1, source_target_pairs={{1,0},{0,1},{3,2},{2,3},{5,4},{4,5},{7,6},{6,7},{9,8},{8,9},{11,10... | collective-permute-start | bytes 786440 | tf_op jit(solution)/shard_map/ppermute | solution.py:45
  240.0 6.7 %collective-permute-start.37 = (bf16[64,2048]{1,0:T(8,128)(2,1)}, bf16[64,2048]{1,0:T(8,128)(2,1)}, u32[]{:S(2)}, u32[]{:S(2)}) collective-permute-start(bf16[64,2048]{1,0:T(8,128)(2,1)} %fusion.12), channel_id=1, source_target_pairs={{4,0},{5,1},{6,2},{7,3},{0,4},{1,5},{2,6},{3,7},{12,8},{13,9},{14,... | collective-permute-start | bytes 786440 | tf_op jit(solution)/shard_map/ppermute | solution.py:45

commit v7 on v6

--- a/solution.py
+++ b/solution.py
@@ -135,13 +135,13 @@
     return whole(join_kernel, place, [a, b], [(2 * a.shape[0], a.shape[1])])[0]
 
 
-def assemble_kernel(keep, place_ref, a_ref, b_ref, c_ref, *out_refs):
+def assemble_kernel(keep, place_ref, a_ref, b_ref, c_ref, out_ref):
     rows = a_ref.shape[0]
     part = rows // PARTS
 
     def put(i, ref, first):
-        at = pl.multiple_of(slot_of(keep, place_ref, i) * part, part)
-        for j, out_ref in enumerate(out_refs):
+        for j in range(PARTS):
+            at = pl.multiple_of((j * RING + slot_of(keep, place_ref, i)) * part, part)
             out_ref[pl.ds(at, part), :] = ref[first + j * part:first + (j + 1) * part, :]
 
     put(0, a_ref, 0)
@@ -153,7 +153,18 @@
 def assemble(keep, place, a, b, c):
     rows, wide = a.shape
     kernel = functools.partial(assemble_kernel, keep)
-    return whole(kernel, place, [a, b, c], [(RING * rows // PARTS, wide)] * PARTS)
+    return whole(kernel, place, [a, b, c], [(RING * rows, wide)])[0]
+
+
+def regroup_kernel(place_ref, own_ref, near_ref, a_ref, b_ref):
+    half = own_ref.shape[0] // 2
+    for i, out_ref in enumerate((a_ref, b_ref)):
+        out_ref[:half, :] = own_ref[i * half:(i + 1) * half, :]
+        out_ref[half:, :] = near_ref[i * half:(i + 1) * half, :]
+
+
+def regroup(place, own, near):
+    return whole(regroup_kernel, place, [own, near], [own.shape] * 2)
 
 
 def order_of(keep):
@@ -310,20 +321,14 @@
     w_out = lax.dynamic_slice_in_dim(weight_out, dp * inner, inner, 0)
 
     order = (False, True)
-    start, one, two, own_a, own_b = {}, {}, {}, {}, {}
+    start, one, two, own, near_a, near_b = {}, {}, {}, {}, {}, {}
     start[True], start[False] = cut(place, tokens, out_grad)
     for keep in order:
         one[keep] = exchange(start[keep], along(keep, True, 0))
     for keep in order:
         two[keep] = exchange(join(place, start[keep], one[keep]), along(keep, True, 1))
     for keep in order:
-        own_a[keep], own_b[keep] = assemble(keep, place, start[keep], one[keep], two[keep])
-
-    def neighbours(own):
-        return {keep: exchange(own[keep], along(keep, False, 0)) for keep in order}
-
-    def joined(own, near):
-        return {keep: join(place, own[keep], near[keep]) for keep in order}
+        own[keep] = assemble(keep, place, start[keep], one[keep], two[keep])
 
     def others(near):
         return {keep: exchange(near[keep], along(keep, False, 1)) for keep in order}
@@ -347,26 +352,27 @@
         activated, slope = gelu_parts(pre)
         return jnp.concatenate([activated.astype(BF), (back * slope).astype(BF)], axis=1)
 
-    both = lax.optimization_barrier((own_a[True], own_a[False]))
-    own_a = {True: both[0], False: both[1]}
-    near_a = joined(own_a, neighbours(own_a))
+    both = lax.optimization_barrier((own[True], own[False]))
+    own = {True: both[0], False: both[1]}
+    near = {keep: exchange(own[keep], along(keep, False, 0)) for keep in order}
+    for keep in order:
+        near_a[keep], near_b[keep] = regroup(place, own[keep], near[keep])
     rest_a = others(near_a)
-    near_of_b = neighbours(own_b)
+    rest_b = others(near_b)
     sent_a = panel_dot(False, near_a, rest_a, rest_a[True])
     kept_a, send_a = panel_dot(True, near_a, rest_a, more=exchange(sent_a, other_core))
-    step_a = after(exchange(send_a, along_z(0)), near_of_b[True], near_of_b[False])
-    near_b = joined(own_b, near_of_b)
-    rest_b = others(near_b)
+    sent_b = panel_dot(False, near_b, rest_b, rest_b[True], send_a)
+    step_a = after(exchange(send_a, along_z(0)), sent_b)
     half_a = halfway(kept_a, step_a)
     turn_a = exchange(half_a[1].astype(BF), along_z(1))
-    mine_a = hidden_of(half_a[0] + turn_a.astype(F32))
-    sent_b = panel_dot(False, near_b, rest_b, rest_b[True], mine_a)
+    kept_b, send_b = panel_dot(
+        True, near_b, rest_b, step_a, more=exchange(sent_b, other_core)
+    )
+    mine_a = hidden_of(half_a[0] + after(turn_a, send_b).astype(F32))
     next_a = exchange(mine_a, along_z(1))
-    got_b = after(exchange(sent_b, other_core), next_a)
+    step_b = exchange(after(send_b, next_a), along_z(0))
     pair_a = join(place, mine_a, next_a)
     far_a = exchange(pair_a, along_z(0))
-    kept_b, send_b = panel_dot(True, near_b, rest_b, pair_a, more=got_b)
-    step_b = exchange(send_b, along_z(0))
     hid_a = {True: (pair_a, far_a)}
     hid_a[False] = (exchange(pair_a, other_core), exchange(far_a, other_core))
 

time: 249 us -> 242 us (0.972)
  waiting for transfers between devices: 120 us -> 111 us
    ppermute x38 -> x36, waiting for transfers between devices: 120 us -> 111 us  [exchange(): return lax.ppermute(array, AXES, pairs)]
    ppermute x38 -> x36, starting transfers between devices: 47.1 us -> 48.8 us  [exchange(): return lax.ppermute(array, AXES, pairs)]
    pallas_call x11 -> x9, Pallas kernels: 6.61 us -> 6.56 us  [whole(): pl.pallas_call(kernel, in_specs=[pl.BlockSpec(memory_space=pltpu.SMEM)] +...]
  transfers between devices with their start and end apart: 38 -> 36, of which waited for: 27 -> 25; matrix products, arithmetic and copies ran while one was open for 3% -> 2% of each run, Pallas kernels for 21% -> 25%
where the time goes in v7:
time: 242 us; the launch traced here: 241 us
  waiting for transfers between devices  111 us (46%)
  Pallas kernels  68.2 us (28%)
  starting transfers between devices  48.8 us (20%)
  other arithmetic  6.78 us (3%)
  local copies, waits for them, and re-layouts  5.18 us (2%)
    ppermute x36, waiting for transfers between devices, exchange(): return lax.ppermute(array, AXES, pairs)  111 us
    ppermute x36, starting transfers between devices, exchange(): return lax.ppermute(array, AXES, pairs)  48.8 us
    pallas_call x8, Pallas kernels, pair_dot(): pl.pallas_call(functools.partial(pair_kernel, keep, hidden, more is not N...  36.8 us
    pallas_call x4, Pallas kernels, grad_dot(): pl.pallas_call(functools.partial(grad_kernel, pairs, block, factor, begun...  24.9 us
    pallas_call x9, Pallas kernels, whole(): pl.pallas_call(kernel, in_specs=[pl.BlockSpec(memory_space=pltpu.SMEM)] +...  6.56 us
  transfers between devices with their start and end apart: 36, of which 25 were waited for; matrix products, arithmetic and copies ran while one was open for 2% of the time, Pallas kernels for 25%

profile of v7, /device:TPU:8, one launch (start us, length us, event | category | flops | bytes accessed | tf_op | source)
XLA Modules:
  0.0 240.9 jit_solution(17838741367900393277)
XLA Ops:
  5.2 4.4 %collective-permute-done.b_ref = bf16[64,2048]{1,0:T(8,128)(2,1)S(1)} collective-permute-done((bf16[64,2048]{1,0:T(8,128)(2,1)S(1)}, bf16[64,2048]{1,0:T(8,128)(2,1)S(1)}, u32[]{:S(2)}, u32[]{:S(2)}) %collective-permute-start) | collective-permute-done | bytes 262176 | tf_op jit(solution)/shard_map/ppermute | solution.py:45
  10.2 2.8 %collective-permute-start.1 = (bf16[128,2048]{1,0:T(8,128)(2,1)S(1)}, bf16[128,2048]{1,0:T(8,128)(2,1)S(1)}, u32[]{:S(2)}, u32[]{:S(2)}) collective-permute-start(bf16[128,2048]{1,0:T(8,128)(2,1)S(1)} %shard_map.76), channel_id=1, source_target_pairs={{12,0},{13,1},{14,2},{15,3},{8,4},{9,5},{10,6},{11,7},{4,8},{5,9},... | collective-permute-start | bytes 1572872 | tf_op jit(solution)/shard_map/ppermute | solution.py:45
  13.7 1.7 collective-permute-start.3
  15.3 5.4 %collective-permute-done.1.c_ref = bf16[128,2048]{1,0:T(8,128)(2,1)S(1)} collective-permute-done((bf16[128,2048]{1,0:T(8,128)(2,1)S(1)}, bf16[128,2048]{1,0:T(8,128)(2,1)S(1)}, u32[]{:S(2)}, u32[]{:S(2)}) %collective-permute-start.1) | collective-permute-done | bytes 524320 | tf_op jit(solution)/shard_map/ppermute | solution.py:45
  23.6 1.7 collective-permute-start.4
  25.5 12.9 %collective-permute-done.4.near_ref = bf16[256,2048]{1,0:T(8,128)(2,1)S(1)} collective-permute-done((bf16[256,2048]{1,0:T(8,128)(2,1)S(1)}, bf16[256,2048]{1,0:T(8,128)(2,1)S(1)}, u32[]{:S(2)}, u32[]{:S(2)}) %collective-permute-start.4) | collective-permute-done | bytes 1048608 | tf_op jit(solution)/shard_map/ppermute | solution.py:45
  39.1 2.1 collective-permute-start.5
  41.4 1.7 shard_map.81
  43.7 2.7 %constant_dynamic-slice_fusion = (bf16[1024,1024]{1,0:T(8,128)(2,1)S(1)}, bf16[1024,1024]{1,0:T(8,128)(2,1)S(1)}) fusion(bf16[2048,1024]{1,0:T(8,128)(2,1)} %param.7, s32[]{:T(128)S(6)} %select_n.30, bf16[1024,2048]{1,0:T(8,128)(2,1)} %param.6), kind=kLoop, calls=%fused_computation.57 | loop fusion | bytes 8388612 | tf_op jit(solution)/shard_map/dynamic_slice | solution.py:321
  46.4 7.8 %collective-permute-done.5.refs_1_.refs_5_ = bf16[256,2048]{1,0:T(8,128)(2,1)} collective-permute-done((bf16[256,2048]{1,0:T(8,128)(2,1)S(1)}, bf16[256,2048]{1,0:T(8,128)(2,1)}, u32[]{:S(2)}, u32[]{:S(2)}) %collective-permute-start.5) | collective-permute-done | bytes 1048608 | tf_op jit(solution)/shard_map/ppermute | solution.py:45
  54.1 5.3 %collective-permute-done.7.refs_1_.refs_3_.refs_7_ = bf16[256,2048]{1,0:T(8,128)(2,1)} collective-permute-done((bf16[256,2048]{1,0:T(8,128)(2,1)}, bf16[256,2048]{1,0:T(8,128)(2,1)}, u32[]{:S(2)}, u32[]{:S(2)}) %collective-permute-start.7) | collective-permute-done | bytes 1048608 | tf_op jit(solution)/shard_map/ppermute | solution.py:45
  59.4 5.5 %shard_map.82 = bf16[512,2048]{1,0:T(8,128)(2,1)S(1)} custom-call(s32[2]{0:T(128)S(1)} %pad_add_fusion.place_ref, bf16[256,2048]{1,0:T(8,128)(2,1)} %get-tuple-element.53.refs_0_.refs_2_.refs_6_, bf16[256,2048]{1,0:T(8,128)(2,1)} %collective-permute-done.7.refs_1_.refs_3_.refs_7_, bf16[1024,1024]{1,0:T(8,128)(2,1)S(1)} %get-tuple-element.126.refs_2_.refs_3_, ...), custom_call_target="tpu_custom_call" | custom-call | flops 2147483 | bytes 8388 | tf_op jit(solution)/shard_map/pallas_call | solution.py:240
  65.0 3.0 %collective-permute-start.11 = (bf16[256,2048]{1,0:T(8,128)(2,1)S(1)}, bf16[256,2048]{1,0:T(8,128)(2,1)S(1)}, u32[]{:S(2)}, u32[]{:S(2)}) collective-permute-start(bf16[256,2048]{1,0:T(8,128)(2,1)S(1)} %get-tuple-element.83.refs_0_.refs_4_), channel_id=1, source_target_pairs={{3,0},{2,1},{1,2},{0,3},{7,4},{6,5},{5,6},{4,7},{11,8},{10,9},{9,1... | collective-permute-start | bytes 3145736 | tf_op jit(solution)/shard_map/ppermute | solution.py:45
  69.2 5.3 %shard_map.83 = (bf16[256,2048]{1,0:T(8,128)(2,1)S(1)}, bf16[256,2048]{1,0:T(8,128)(2,1)S(1)}) custom-call(s32[2]{0:T(128)S(1)} %pad_add_fusion.place_ref, bf16[256,2048]{1,0:T(8,128)(2,1)S(1)} %get-tuple-element.71.refs_0_.refs_4_, bf16[256,2048]{1,0:T(8,128)(2,1)} %collective-permute-done.5.refs_1_.refs_5_, ...), custom_call_target="tpu_custom_call" | custom-call | flops 2147483 | bytes 8388 | tf_op jit(solution)/shard_map/pallas_call | solution.py:240
  74.5 2.0 collective-permute-start.9
  76.5 4.3 %collective-permute-done.11.refs_1_.refs_5_ = bf16[256,2048]{1,0:T(8,128)(2,1)S(1)} collective-permute-done((bf16[256,2048]{1,0:T(8,128)(2,1)S(1)}, bf16[256,2048]{1,0:T(8,128)(2,1)S(1)}, u32[]{:S(2)}, u32[]{:S(2)}) %collective-permute-start.11) | collective-permute-done | bytes 1048608 | tf_op jit(solution)/shard_map/ppermute | solution.py:45
  80.8 3.2 %collective-permute-done.10.refs_1_.refs_3_.refs_7_ = bf16[256,2048]{1,0:T(8,128)(2,1)S(1)} collective-permute-done((bf16[256,2048]{1,0:T(8,128)(2,1)S(1)}, bf16[256,2048]{1,0:T(8,128)(2,1)S(1)}, u32[]{:S(2)}, u32[]{:S(2)}) %collective-permute-start.10) | collective-permute-done | bytes 1048608 | tf_op jit(solution)/shard_map/ppermute | solution.py:45
  84.0 4.3 %shard_map.84 = bf16[512,2048]{1,0:T(8,128)(2,1)S(1)} custom-call(s32[2]{0:T(128)S(1)} %pad_add_fusion.place_ref, bf16[256,2048]{1,0:T(8,128)(2,1)S(1)} %get-tuple-element.57.refs_0_.refs_2_.refs_6_, bf16[256,2048]{1,0:T(8,128)(2,1)S(1)} %collective-permute-done.10.refs_1_.refs_3_.refs_7_, bf16[1024,1024]{1,0:T(8,128)(2,1)S(1)} %get-tuple-element.126.refs_2_.refs_3_, ...), custom_call_target="tpu_custom_call" | custom-call | flops 2147483 | bytes 8388 | tf_op jit(solution)/shard_map/pallas_call | solution.py:240
  89.8 4.1 %collective-permute-start.12 = (bf16[128,2048]{1,0:T(8,128)(2,1)S(1)}, bf16[128,2048]{1,0:T(8,128)(2,1)S(1)}, u32[]{:S(2)}, u32[]{:S(2)}) collective-permute-start(bf16[128,2048]{1,0:T(8,128)(2,1)S(1)} %slice.259), channel_id=1, source_target_pairs={{96,0},{97,1},{98,2},{99,3},{100,4},{101,5},{102,6},{103,7},{104,8... | collective-permute-start | bytes 1572872 | tf_op jit(solution)/shard_map/ppermute | solution.py:45
  93.9 4.5 %shard_map.85 = (bf16[256,2048]{1,0:T(8,128)(2,1)S(1)}, bf16[256,2048]{1,0:T(8,128)(2,1)S(1)}) custom-call(s32[2]{0:T(128)S(1)} %pad_add_fusion.place_ref, bf16[256,2048]{1,0:T(8,128)(2,1)S(1)} %get-tuple-element.83.refs_0_.refs_4_, bf16[256,2048]{1,0:T(8,128)(2,1)S(1)} %collective-permute-done.11.refs_1_.refs_5_, ...), custom_call_target="tpu_custom_call" | custom-call | flops 2147483 | bytes 8388 | tf_op jit(solution)/shard_map/pallas_call | solution.py:240
  98.4 2.7 %collective-permute-done.12 = bf16[128,2048]{1,0:T(8,128)(2,1)S(1)} collective-permute-done((bf16[128,2048]{1,0:T(8,128)(2,1)S(1)}, bf16[128,2048]{1,0:T(8,128)(2,1)S(1)}, u32[]{:S(2)}, u32[]{:S(2)}) %collective-permute-start.12) | collective-permute-done | bytes 524320 | tf_op jit(solution)/shard_map/ppermute | solution.py:45
  101.5 3.3 %collective-permute-start.14 = (bf16[128,2048]{1,0:T(8,128)(2,1)S(1)}, bf16[128,2048]{1,0:T(8,128)(2,1)S(1)}, u32[]{:S(2)}, u32[]{:S(2)}) collective-permute-start(bf16[128,2048]{1,0:T(8,128)(2,1)S(1)} %pad_maximum_fusion.a_ref), channel_id=1, source_target_pairs={{96,0},{97,1},{98,2},{99,3},{100,4},{101,5},{102,6},{103,7},{104,8... | collective-permute-start | bytes 1572872 | tf_op jit(solution)/shard_map/ppermute | solution.py:45
  104.8 7.2 %collective-permute-done.14.b_ref = bf16[128,2048]{1,0:T(8,128)(2,1)S(1)} collective-permute-done((bf16[128,2048]{1,0:T(8,128)(2,1)S(1)}, bf16[128,2048]{1,0:T(8,128)(2,1)S(1)}, u32[]{:S(2)}, u32[]{:S(2)}) %collective-permute-start.14) | collective-permute-done | bytes 524320 | tf_op jit(solution)/shard_map/ppermute | solution.py:45
  112.7 2.0 collective-permute-start.19
  114.7 12.8 %collective-permute-done.15.refs_1_.refs_5_ = bf16[256,2048]{1,0:T(8,128)(2,1)S(1)} collective-permute-done((bf16[256,2048]{1,0:T(8,128)(2,1)S(1)}, bf16[256,2048]{1,0:T(8,128)(2,1)S(1)}, u32[]{:S(2)}, u32[]{:S(2)}) %collective-permute-start.15) | collective-permute-done | bytes 1048608 | tf_op jit(solution)/shard_map/ppermute | solution.py:45
  127.5 4.3 %shard_map.87 = (bf16[256,2048]{1,0:T(8,128)(2,1)S(1)}, bf16[256,2048]{1,0:T(8,128)(2,1)S(1)}) custom-call(s32[2]{0:T(128)S(1)} %pad_add_fusion.place_ref, bf16[256,2048]{1,0:T(8,128)(2,1)S(1)} %shard_map.86.refs_0_.refs_4_, bf16[256,2048]{1,0:T(8,128)(2,1)S(1)} %collective-permute-done.15.refs_1_.refs_5_, ...), custom_call_target="tpu_custom_call" | custom-call | flops 2147483 | bytes 8388 | tf_op jit(solution)/shard_map/pallas_call | solution.py:240
  131.8 6.9 %collective-permute-done.19 = bf16[256,2048]{1,0:T(8,128)(2,1)S(1)} collective-permute-done((bf16[256,2048]{1,0:T(8,128)(2,1)S(1)}, bf16[256,2048]{1,0:T(8,128)(2,1)S(1)}, u32[]{:S(2)}, u32[]{:S(2)}) %collective-permute-start.19) | collective-permute-done | bytes 1048608 | tf_op jit(solution)/shard_map/ppermute | solution.py:45
  139.1 3.3 %collective-permute-start.20 = (bf16[128,2048]{1,0:T(8,128)(2,1)S(1)}, bf16[128,2048]{1,0:T(8,128)(2,1)S(1)}, u32[]{:S(2)}, u32[]{:S(2)}) collective-permute-start(bf16[128,2048]{1,0:T(8,128)(2,1)S(1)} %slice.258), channel_id=1, source_target_pairs={{96,0},{97,1},{98,2},{99,3},{100,4},{101,5},{102,6},{103,7},{104,8... | collective-permute-start | bytes 1572872 | tf_op jit(solution)/shard_map/ppermute | solution.py:45
  142.4 2.8 %collective-permute-start.16 = (bf16[256,2048]{1,0:T(8,128)(2,1)S(1)}, bf16[256,2048]{1,0:T(8,128)(2,1)S(1)}, u32[]{:S(2)}, u32[]{:S(2)}) collective-permute-start(bf16[256,2048]{1,0:T(8,128)(2,1)S(1)} %get-tuple-element.65), channel_id=1, source_target_pairs={{12,0},{13,1},{14,2},{15,3},{8,4},{9,5},{10,6},{11,7},{4,8},{5,9},... | collective-permute-start | bytes 3145736 | tf_op jit(solution)/shard_map/ppermute | solution.py:45
  145.3 4.3 %shard_map.88 = (bf16[256,2048]{1,0:T(8,128)(2,1)S(1)}, bf16[256,2048]{1,0:T(8,128)(2,1)S(1)}) custom-call(s32[2]{0:T(128)S(1)} %pad_add_fusion.place_ref, bf16[256,2048]{1,0:T(8,128)(2,1)S(1)} %collective-permute-done.17.refs_0_.refs_6_.refs_2_, bf16[256,2048]{1,0:T(8,128)(2,1)S(1)} %collective-permute-done.18.refs_1_.refs_7_.refs_3_, ...), custom_call_target="tpu_custom_call" | custom-call | flops 2147483 | bytes 8388 | tf_op jit(solution)/shard_map/pallas_call | solution.py:240
  150.0 2.9 %collective-permute-start.21 = (bf16[256,2048]{1,0:T(8,128)(2,1)S(1)}, bf16[256,2048]{1,0:T(8,128)(2,1)S(1)}, u32[]{:S(2)}, u32[]{:S(2)}) collective-permute-start(bf16[256,2048]{1,0:T(8,128)(2,1)S(1)} %get-tuple-element.72), channel_id=1, source_target_pairs={{3,0},{2,1},{1,2},{0,3},{7,4},{6,5},{5,6},{4,7},{11,8},{10,9},{9,1... | collective-permute-start | bytes 3145736 | tf_op jit(solution)/shard_map/ppermute | solution.py:45
  153.0 3.3 %collective-permute-start.23 = (bf16[128,2048]{1,0:T(8,128)(2,1)S(1)}, bf16[128,2048]{1,0:T(8,128)(2,1)S(1)}, u32[]{:S(2)}, u32[]{:S(2)}) collective-permute-start(bf16[128,2048]{1,0:T(8,128)(2,1)S(1)} %pad_maximum_fusion.1.a_ref), channel_id=1, source_target_pairs={{96,0},{97,1},{98,2},{99,3},{100,4},{101,5},{102,6},{103,7},{104,8... | collective-permute-start | bytes 1572872 | tf_op jit(solution)/shard_map/ppermute | solution.py:45
  156.3 5.9 %shard_map.89.refs_8_ = f32[1024,1024]{1,0:T(8,128)} custom-call(bf16[256,2048]{1,0:T(8,128)(2,1)S(1)} %get-tuple-element.71.refs_0_.refs_4_, bf16[256,2048]{1,0:T(8,128)(2,1)} %collective-permute-done.5.refs_1_.refs_5_, bf16[256,2048]{1,0:T(8,128)(2,1)} %get-tuple-element.53.refs_0_.refs_2_.refs_6_, ...), custom_call_target="tpu_custom_call" | custom-call | flops 2147483 | bytes 5242 | tf_op jit(solution)/shard_map/pallas_call | solution.py:289
  162.2 2.9 %collective-permute-done.23.b_ref = bf16[128,2048]{1,0:T(8,128)(2,1)S(1)} collective-permute-done((bf16[128,2048]{1,0:T(8,128)(2,1)S(1)}, bf16[128,2048]{1,0:T(8,128)(2,1)S(1)}, u32[]{:S(2)}, u32[]{:S(2)}) %collective-permute-start.23) | collective-permute-done | bytes 524320 | tf_op jit(solution)/shard_map/ppermute | solution.py:45
  166.4 6.0 %shard_map.91.refs_8_ = f32[1024,1024]{1,0:T(8,128)} custom-call(bf16[256,2048]{1,0:T(8,128)(2,1)S(1)} %shard_map.86.refs_0_.refs_4_, bf16[256,2048]{1,0:T(8,128)(2,1)S(1)} %collective-permute-done.15.refs_1_.refs_5_, bf16[256,2048]{1,0:T(8,128)(2,1)S(1)} %collective-permute-done.17.refs_0_.refs_6_.refs_2_, ...), custom_call_target="tpu_custom_call" | custom-call | flops 2147483 | bytes 5242 | tf_op jit(solution)/shard_map/pallas_call | solution.py:289
  172.4 8.2 %collective-permute-done.24.refs_1_.refs_5_ = bf16[256,2048]{1,0:T(8,128)(2,1)S(1)} collective-permute-done((bf16[256,2048]{1,0:T(8,128)(2,1)S(1)}, bf16[256,2048]{1,0:T(8,128)(2,1)S(1)}, u32[]{:S(2)}, u32[]{:S(2)}) %collective-permute-start.24) | collective-permute-done | bytes 1048608 | tf_op jit(solution)/shard_map/ppermute | solution.py:45
  181.1 4.3 %shard_map.92 = (bf16[256,2048]{1,0:T(8,128)(2,1)S(1)}, bf16[256,2048]{1,0:T(8,128)(2,1)S(1)}) custom-call(s32[2]{0:T(128)S(1)} %pad_add_fusion.place_ref, bf16[256,2048]{1,0:T(8,128)(2,1)S(1)} %shard_map.90.refs_0_.refs_4_, bf16[256,2048]{1,0:T(8,128)(2,1)S(1)} %collective-permute-done.24.refs_1_.refs_5_, ...), custom_call_target="tpu_custom_call" | custom-call | flops 2147483 | bytes 8388 | tf_op jit(solution)/shard_map/pallas_call | solution.py:240
  185.4 3.0 %collective-permute-start.25 = (bf16[256,2048]{1,0:T(8,128)(2,1)S(1)}, bf16[256,2048]{1,0:T(8,128)(2,1)S(1)}, u32[]{:S(2)}, u32[]{:S(2)}) collective-permute-start(bf16[256,2048]{1,0:T(8,128)(2,1)S(1)} %get-tuple-element.79), channel_id=1, source_target_pairs={{12,0},{13,1},{14,2},{15,3},{8,4},{9,5},{10,6},{11,7},{4,8},{5,9},... | collective-permute-start | bytes 3145736 | tf_op jit(solution)/shard_map/ppermute | solution.py:45
  188.6 4.3 %shard_map.93 = (bf16[256,2048]{1,0:T(8,128)(2,1)S(1)}, bf16[256,2048]{1,0:T(8,128)(2,1)S(1)}) custom-call(s32[2]{0:T(128)S(1)} %pad_add_fusion.place_ref, bf16[256,2048]{1,0:T(8,128)(2,1)S(1)} %collective-permute-done.26.refs_0_.refs_6_.refs_2_, bf16[256,2048]{1,0:T(8,128)(2,1)S(1)} %collective-permute-done.27.refs_1_.refs_7_.refs_3_, ...), custom_call_target="tpu_custom_call" | custom-call | flops 2147483 | bytes 8388 | tf_op jit(solution)/shard_map/pallas_call | solution.py:240
  193.5 6.5 %shard_map.94 = f32[1024,1024]{1,0:T(8,128)} custom-call(bf16[256,2048]{1,0:T(8,128)(2,1)S(1)} %get-tuple-element.83.refs_0_.refs_4_, bf16[256,2048]{1,0:T(8,128)(2,1)S(1)} %collective-permute-done.11.refs_1_.refs_5_, bf16[256,2048]{1,0:T(8,128)(2,1)S(1)} %get-tuple-element.57.refs_0_.refs_2_.refs_6_, ...), custom_call_target="tpu_custom_call", output_to_operand_aliasing={{}: (8, {})} | custom-call | flops 2147483 | bytes 5242 | tf_op jit(solution)/shard_map/pallas_call | solution.py:289
  200.0 2.2 collective-permute-done.25
  202.2 5.8 %collective-permute-done.29 = bf16[256,2048]{1,0:T(8,128)(2,1)S(1)} collective-permute-done((bf16[256,2048]{1,0:T(8,128)(2,1)S(1)}, bf16[256,2048]{1,0:T(8,128)(2,1)S(1)}, u32[]{:S(2)}, u32[]{:S(2)}) %collective-permute-start.29) | collective-permute-done | bytes 1048608 | tf_op jit(solution)/shard_map/ppermute | solution.py:45
  210.4 6.5 %shard_map.95 = f32[1024,1024]{1,0:T(8,128)} custom-call(bf16[256,2048]{1,0:T(8,128)(2,1)S(1)} %shard_map.90.refs_0_.refs_4_, bf16[256,2048]{1,0:T(8,128)(2,1)S(1)} %collective-permute-done.24.refs_1_.refs_5_, bf16[256,2048]{1,0:T(8,128)(2,1)S(1)} %collective-permute-done.26.refs_0_.refs_6_.refs_2_, ...), custom_call_target="tpu_custom_call", output_to_operand_aliasing={{}: (8, {})} | custom-call | flops 2147483 | bytes 5242 | tf_op jit(solution)/shard_map/pallas_call | solution.py:289
  218.8 2.1 collective-permute-start.33
  221.1 6.9 %collective-permute-done.32 = bf16[128,2048]{1,0:T(8,128)(2,1)S(1)} collective-permute-done((bf16[128,2048]{1,0:T(8,128)(2,1)S(1)}, bf16[128,2048]{1,0:T(8,128)(2,1)S(1)}, u32[]{:S(2)}, u32[]{:S(2)}) %collective-permute-start.32) | collective-permute-done | bytes 524320 | tf_op jit(solution)/shard_map/ppermute | solution.py:45
  230.2 2.0 collective-permute-start.34
  233.5 3.3 %collective-permute-done.34 = bf16[64,2048]{1,0:T(8,128)(2,1)} collective-permute-done((bf16[64,2048]{1,0:T(8,128)(2,1)}, bf16[64,2048]{1,0:T(8,128)(2,1)}, u32[]{:S(2)}, u32[]{:S(2)}) %collective-permute-start.34) | collective-permute-done | bytes 262176 | tf_op jit(solution)/shard_map/ppermute | solution.py:45
  236.9 2.0 collective-permute-done.35
  (90 shorter events, 27.3 us)
Async XLA Ops:
  0.7 1.0 copy-start
  1.7 0.9 copy-start.1
  3.2 6.5 %collective-permute-start = (bf16[64,2048]{1,0:T(8,128)(2,1)S(1)}, bf16[64,2048]{1,0:T(8,128)(2,1)S(1)}, u32[]{:S(2)}, u32[]{:S(2)}) collective-permute-start(bf16[64,2048]{1,0:T(8,128)(2,1)S(1)} %get-tuple-element.48.a_ref), channel_id=1, source_target_pairs={{4,0},{5,1},{6,2},{7,3},{0,4},{1,5},{2,6},{3,7},{12,8},{13,9},{14,... | collective-permute-start | bytes 786440 | tf_op jit(solution)/shard_map/ppermute | solution.py:45
  4.8 8.3 %collective-permute-start.2 = (bf16[64,2048]{1,0:T(8,128)(2,1)S(1)}, bf16[64,2048]{1,0:T(8,128)(2,1)S(1)}, u32[]{:S(2)}, u32[]{:S(2)}) collective-permute-start(bf16[64,2048]{1,0:T(8,128)(2,1)S(1)} %get-tuple-element.49.a_ref), channel_id=1, source_target_pairs={{1,0},{0,1},{3,2},{2,3},{5,4},{4,5},{7,6},{6,7},{9,8},{8,9},{11,10... | collective-permute-start | bytes 786440 | tf_op jit(solution)/shard_map/ppermute | solution.py:45
  10.2 10.5 %collective-permute-start.1 = (bf16[128,2048]{1,0:T(8,128)(2,1)S(1)}, bf16[128,2048]{1,0:T(8,128)(2,1)S(1)}, u32[]{:S(2)}, u32[]{:S(2)}) collective-permute-start(bf16[128,2048]{1,0:T(8,128)(2,1)S(1)} %shard_map.76), channel_id=1, source_target_pairs={{12,0},{13,1},{14,2},{15,3},{8,4},{9,5},{10,6},{11,7},{4,8},{5,9},... | collective-permute-start | bytes 1572872 | tf_op jit(solution)/shard_map/ppermute | solution.py:45
  13.7 9.3 %collective-permute-start.3 = (bf16[128,2048]{1,0:T(8,128)(2,1)S(1)}, bf16[128,2048]{1,0:T(8,128)(2,1)S(1)}, u32[]{:S(2)}, u32[]{:S(2)}) collective-permute-start(bf16[128,2048]{1,0:T(8,128)(2,1)S(1)} %shard_map.78), channel_id=1, source_target_pairs={{3,0},{2,1},{1,2},{0,3},{7,4},{6,5},{5,6},{4,7},{11,8},{10,9},{9,1... | collective-permute-start | bytes 1572872 | tf_op jit(solution)/shard_map/ppermute | solution.py:45
  23.6 14.9 %collective-permute-start.4 = (bf16[256,2048]{1,0:T(8,128)(2,1)S(1)}, bf16[256,2048]{1,0:T(8,128)(2,1)S(1)}, u32[]{:S(2)}, u32[]{:S(2)}) collective-permute-start(bf16[256,2048]{1,0:T(8,128)(2,1)S(1)} %shard_map.77.own_ref), channel_id=1, source_target_pairs={{1,0},{0,1},{3,2},{2,3},{5,4},{4,5},{7,6},{6,7},{9,8},{8,9},{11,10... | collective-permute-start | bytes 3145736 | tf_op jit(solution)/shard_map/ppermute | solution.py:45
  25.3 16.1 %collective-permute-start.6 = (bf16[256,2048]{1,0:T(8,128)(2,1)S(1)}, bf16[256,2048]{1,0:T(8,128)(2,1)S(1)}, u32[]{:S(2)}, u32[]{:S(2)}) collective-permute-start(bf16[256,2048]{1,0:T(8,128)(2,1)S(1)} %shard_map.79.own_ref), channel_id=1, source_target_pairs={{4,0},{5,1},{6,2},{7,3},{0,4},{1,5},{2,6},{3,7},{12,8},{13,9},{14,... | collective-permute-start | bytes 3145736 | tf_op jit(solution)/shard_map/ppermute | solution.py:45
  39.1 15.0 %collective-permute-start.5 = (bf16[256,2048]{1,0:T(8,128)(2,1)S(1)}, bf16[256,2048]{1,0:T(8,128)(2,1)}, u32[]{:S(2)}, u32[]{:S(2)}) collective-permute-start(bf16[256,2048]{1,0:T(8,128)(2,1)S(1)} %get-tuple-element.71.refs_0_.refs_4_), channel_id=1, source_target_pairs={{3,0},{2,1},{1,2},{0,3},{7,4},{6,5},{5,6},{4,7},{11,8},{10,9},{9,1... | collective-permute-start | bytes 3145736 | tf_op jit(solution)/shard_map/ppermute | solution.py:45
  43.1 16.3 %collective-permute-start.7 = (bf16[256,2048]{1,0:T(8,128)(2,1)}, bf16[256,2048]{1,0:T(8,128)(2,1)}, u32[]{:S(2)}, u32[]{:S(2)}) collective-permute-start(bf16[256,2048]{1,0:T(8,128)(2,1)} %get-tuple-element.53.refs_0_.refs_2_.refs_6_), channel_id=1, source_target_pairs={{12,0},{13,1},{14,2},{15,3},{8,4},{9,5},{10,6},{11,7},{4,8},{5,9},... | collective-permute-start | bytes 3145736 | tf_op jit(solution)/shard_map/ppermute | solution.py:45
  64.9 4.2 %collective-permute-start.8 = (bf16[512,2048]{1,0:T(8,128)(2,1)S(1)}, bf16[512,2048]{1,0:T(8,128)(2,1)S(1)}, u32[]{:S(2)}, u32[]{:S(2)}) collective-permute-start(bf16[512,2048]{1,0:T(8,128)(2,1)S(1)} %shard_map.82), channel_id=1, source_target_pairs={{16,0},{17,1},{18,2},{19,3},{20,4},{21,5},{22,6},{23,7},{24,8},{25... | collective-permute-start | bytes 6291464 | tf_op jit(solution)/shard_map/ppermute | solution.py:45
  65.0 15.7 %collective-permute-start.11 = (bf16[256,2048]{1,0:T(8,128)(2,1)S(1)}, bf16[256,2048]{1,0:T(8,128)(2,1)S(1)}, u32[]{:S(2)}, u32[]{:S(2)}) collective-permute-start(bf16[256,2048]{1,0:T(8,128)(2,1)S(1)} %get-tuple-element.83.refs_0_.refs_4_), channel_id=1, source_target_pairs={{3,0},{2,1},{1,2},{0,3},{7,4},{6,5},{5,6},{4,7},{11,8},{10,9},{9,1... | collective-permute-start | bytes 3145736 | tf_op jit(solution)/shard_map/ppermute | solution.py:45
  68.0 16.0 %collective-permute-start.10 = (bf16[256,2048]{1,0:T(8,128)(2,1)S(1)}, bf16[256,2048]{1,0:T(8,128)(2,1)S(1)}, u32[]{:S(2)}, u32[]{:S(2)}) collective-permute-start(bf16[256,2048]{1,0:T(8,128)(2,1)S(1)} %get-tuple-element.57.refs_0_.refs_2_.refs_6_), channel_id=1, source_target_pairs={{12,0},{13,1},{14,2},{15,3},{8,4},{9,5},{10,6},{11,7},{4,8},{5,9},... | collective-permute-start | bytes 3145736 | tf_op jit(solution)/shard_map/ppermute | solution.py:45
  74.5 14.9 %collective-permute-start.9 = (bf16[256,2048]{1,0:T(8,128)(2,1)S(1)}, bf16[256,2048]{1,0:T(8,128)(2,1)S(1)}, u32[]{:S(2)}, u32[]{:S(2)}) collective-permute-start(bf16[256,2048]{1,0:T(8,128)(2,1)S(1)} %get-tuple-element.56), channel_id=1, source_target_pairs={{32,0},{33,1},{34,2},{35,3},{36,4},{37,5},{38,6},{39,7},{40,8},{41... | collective-permute-start | bytes 3145736 | tf_op jit(solution)/shard_map/ppermute | solution.py:45
  88.3 5.7 %collective-permute-start.13 = (bf16[512,2048]{1,0:T(8,128)(2,1)S(1)}, bf16[512,2048]{1,0:T(8,128)(2,1)S(1)}, u32[]{:S(2)}, u32[]{:S(2)}) collective-permute-start(bf16[512,2048]{1,0:T(8,128)(2,1)S(1)} %shard_map.84), channel_id=1, source_target_pairs={{16,0},{17,1},{18,2},{19,3},{20,4},{21,5},{22,6},{23,7},{24,8},{25... | collective-permute-start | bytes 6291464 | tf_op jit(solution)/shard_map/ppermute | solution.py:45
  89.8 11.3 %collective-permute-start.12 = (bf16[128,2048]{1,0:T(8,128)(2,1)S(1)}, bf16[128,2048]{1,0:T(8,128)(2,1)S(1)}, u32[]{:S(2)}, u32[]{:S(2)}) collective-permute-start(bf16[128,2048]{1,0:T(8,128)(2,1)S(1)} %slice.259), channel_id=1, source_target_pairs={{96,0},{97,1},{98,2},{99,3},{100,4},{101,5},{102,6},{103,7},{104,8... | collective-permute-start | bytes 1572872 | tf_op jit(solution)/shard_map/ppermute | solution.py:45
  101.5 10.5 %collective-permute-start.14 = (bf16[128,2048]{1,0:T(8,128)(2,1)S(1)}, bf16[128,2048]{1,0:T(8,128)(2,1)S(1)}, u32[]{:S(2)}, u32[]{:S(2)}) collective-permute-start(bf16[128,2048]{1,0:T(8,128)(2,1)S(1)} %pad_maximum_fusion.a_ref), channel_id=1, source_target_pairs={{96,0},{97,1},{98,2},{99,3},{100,4},{101,5},{102,6},{103,7},{104,8... | collective-permute-start | bytes 1572872 | tf_op jit(solution)/shard_map/ppermute | solution.py:45
  112.6 14.9 %collective-permute-start.15 = (bf16[256,2048]{1,0:T(8,128)(2,1)S(1)}, bf16[256,2048]{1,0:T(8,128)(2,1)S(1)}, u32[]{:S(2)}, u32[]{:S(2)}) collective-permute-start(bf16[256,2048]{1,0:T(8,128)(2,1)S(1)} %shard_map.86.refs_0_.refs_4_), channel_id=1, source_target_pairs={{32,0},{33,1},{34,2},{35,3},{36,4},{37,5},{38,6},{39,7},{40,8},{41... | collective-permute-start | bytes 3145736 | tf_op jit(solution)/shard_map/ppermute | solution.py:45
  112.7 26.0 %collective-permute-start.19 = (bf16[256,2048]{1,0:T(8,128)(2,1)S(1)}, bf16[256,2048]{1,0:T(8,128)(2,1)S(1)}, u32[]{:S(2)}, u32[]{:S(2)}) collective-permute-start(bf16[256,2048]{1,0:T(8,128)(2,1)S(1)} %get-tuple-element.66), channel_id=1, source_target_pairs={{32,0},{33,1},{34,2},{35,3},{36,4},{37,5},{38,6},{39,7},{40,8},{41... | collective-permute-start | bytes 3145736 | tf_op jit(solution)/shard_map/ppermute | solution.py:45
  114.7 30.6 %collective-permute-start.17 = (bf16[256,2048]{1,0:T(8,128)(2,1)S(1)}, bf16[256,2048]{1,0:T(8,128)(2,1)S(1)}, u32[]{:S(2)}, u32[]{:S(2)}) collective-permute-start(bf16[256,2048]{1,0:T(8,128)(2,1)S(1)} %shard_map.86.refs_0_.refs_4_), channel_id=1, source_target_pairs={{16,0},{17,1},{18,2},{19,3},{20,4},{21,5},{22,6},{23,7},{24,8},{25... | collective-permute-start | bytes 3145736 | tf_op jit(solution)/shard_map/ppermute | solution.py:45
  138.7 6.6 %collective-permute-start.18 = (bf16[256,2048]{1,0:T(8,128)(2,1)S(1)}, bf16[256,2048]{1,0:T(8,128)(2,1)S(1)}, u32[]{:S(2)}, u32[]{:S(2)}) collective-permute-start(bf16[256,2048]{1,0:T(8,128)(2,1)S(1)} %collective-permute-done.15.refs_1_.refs_5_), channel_id=1, source_target_pairs={{16,0},{17,1},{18,2},{19,3},{20,4},{21,5},{22,6},{23,7},{24,8},{25... | collective-permute-start | bytes 3145736 | tf_op jit(solution)/shard_map/ppermute | solution.py:45
  139.1 10.5 %collective-permute-start.20 = (bf16[128,2048]{1,0:T(8,128)(2,1)S(1)}, bf16[128,2048]{1,0:T(8,128)(2,1)S(1)}, u32[]{:S(2)}, u32[]{:S(2)}) collective-permute-start(bf16[128,2048]{1,0:T(8,128)(2,1)S(1)} %slice.258), channel_id=1, source_target_pairs={{96,0},{97,1},{98,2},{99,3},{100,4},{101,5},{102,6},{103,7},{104,8... | collective-permute-start | bytes 1572872 | tf_op jit(solution)/shard_map/ppermute | solution.py:45
  142.4 23.4 %collective-permute-start.16 = (bf16[256,2048]{1,0:T(8,128)(2,1)S(1)}, bf16[256,2048]{1,0:T(8,128)(2,1)S(1)}, u32[]{:S(2)}, u32[]{:S(2)}) collective-permute-start(bf16[256,2048]{1,0:T(8,128)(2,1)S(1)} %get-tuple-element.65), channel_id=1, source_target_pairs={{12,0},{13,1},{14,2},{15,3},{8,4},{9,5},{10,6},{11,7},{4,8},{5,9},... | collective-permute-start | bytes 3145736 | tf_op jit(solution)/shard_map/ppermute | solution.py:45
  150.0 15.9 %collective-permute-start.21 = (bf16[256,2048]{1,0:T(8,128)(2,1)S(1)}, bf16[256,2048]{1,0:T(8,128)(2,1)S(1)}, u32[]{:S(2)}, u32[]{:S(2)}) collective-permute-start(bf16[256,2048]{1,0:T(8,128)(2,1)S(1)} %get-tuple-element.72), channel_id=1, source_target_pairs={{3,0},{2,1},{1,2},{0,3},{7,4},{6,5},{5,6},{4,7},{11,8},{10,9},{9,1... | collective-permute-start | bytes 3145736 | tf_op jit(solution)/shard_map/ppermute | solution.py:45
  153.0 12.1 %collective-permute-start.23 = (bf16[128,2048]{1,0:T(8,128)(2,1)S(1)}, bf16[128,2048]{1,0:T(8,128)(2,1)S(1)}, u32[]{:S(2)}, u32[]{:S(2)}) collective-permute-start(bf16[128,2048]{1,0:T(8,128)(2,1)S(1)} %pad_maximum_fusion.1.a_ref), channel_id=1, source_target_pairs={{96,0},{97,1},{98,2},{99,3},{100,4},{101,5},{102,6},{103,7},{104,8... | collective-permute-start | bytes 1572872 | tf_op jit(solution)/shard_map/ppermute | solution.py:45
  165.7 14.9 %collective-permute-start.24 = (bf16[256,2048]{1,0:T(8,128)(2,1)S(1)}, bf16[256,2048]{1,0:T(8,128)(2,1)S(1)}, u32[]{:S(2)}, u32[]{:S(2)}) collective-permute-start(bf16[256,2048]{1,0:T(8,128)(2,1)S(1)} %shard_map.90.refs_0_.refs_4_), channel_id=1, source_target_pairs={{32,0},{33,1},{34,2},{35,3},{36,4},{37,5},{38,6},{39,7},{40,8},{41... | collective-permute-start | bytes 3145736 | tf_op jit(solution)/shard_map/ppermute | solution.py:45
  165.8 22.9 %collective-permute-start.26 = (bf16[256,2048]{1,0:T(8,128)(2,1)S(1)}, bf16[256,2048]{1,0:T(8,128)(2,1)S(1)}, u32[]{:S(2)}, u32[]{:S(2)}) collective-permute-start(bf16[256,2048]{1,0:T(8,128)(2,1)S(1)} %shard_map.90.refs_0_.refs_4_), channel_id=1, source_target_pairs={{16,0},{17,1},{18,2},{19,3},{20,4},{21,5},{22,6},{23,7},{24,8},{25... | collective-permute-start | bytes 3145736 | tf_op jit(solution)/shard_map/ppermute | solution.py:45
  166.3 22.1 %collective-permute-start.22 = (bf16[128,2048]{1,0:T(8,128)(2,1)S(1)}, bf16[128,2048]{1,0:T(8,128)(2,1)S(1)}, u32[]{:S(2)}, u32[]{:S(2)}) collective-permute-start(bf16[128,2048]{1,0:T(8,128)(2,1)S(1)} %slice.257), channel_id=1, source_target_pairs={{4,0},{5,1},{6,2},{7,3},{0,4},{1,5},{2,6},{3,7},{12,8},{13,9},{14,... | collective-permute-start | bytes 1572872 | tf_op jit(solution)/shard_map/ppermute | solution.py:45
  180.6 8.1 %collective-permute-start.27 = (bf16[256,2048]{1,0:T(8,128)(2,1)S(1)}, bf16[256,2048]{1,0:T(8,128)(2,1)S(1)}, u32[]{:S(2)}, u32[]{:S(2)}) collective-permute-start(bf16[256,2048]{1,0:T(8,128)(2,1)S(1)} %collective-permute-done.24.refs_1_.refs_5_), channel_id=1, source_target_pairs={{16,0},{17,1},{18,2},{19,3},{20,4},{21,5},{22,6},{23,7},{24,8},{25... | collective-permute-start | bytes 3145736 | tf_op jit(solution)/shard_map/ppermute | solution.py:45
  181.0 12.3 %collective-permute-start.28 = (bf16[128,2048]{1,0:T(8,128)(2,1)S(1)}, bf16[128,2048]{1,0:T(8,128)(2,1)S(1)}, u32[]{:S(2)}, u32[]{:S(2)}) collective-permute-start(bf16[128,2048]{1,0:T(8,128)(2,1)S(1)} %slice.256), channel_id=1, source_target_pairs={{1,0},{0,1},{3,2},{2,3},{5,4},{4,5},{7,6},{6,7},{9,8},{8,9},{11,10... | collective-permute-start | bytes 1572872 | tf_op jit(solution)/shard_map/ppermute | solution.py:45
  185.4 16.8 %collective-permute-start.25 = (bf16[256,2048]{1,0:T(8,128)(2,1)S(1)}, bf16[256,2048]{1,0:T(8,128)(2,1)S(1)}, u32[]{:S(2)}, u32[]{:S(2)}) collective-permute-start(bf16[256,2048]{1,0:T(8,128)(2,1)S(1)} %get-tuple-element.79), channel_id=1, source_target_pairs={{12,0},{13,1},{14,2},{15,3},{8,4},{9,5},{10,6},{11,7},{4,8},{5,9},... | collective-permute-start | bytes 3145736 | tf_op jit(solution)/shard_map/ppermute | solution.py:45
  193.0 15.1 %collective-permute-start.29 = (bf16[256,2048]{1,0:T(8,128)(2,1)S(1)}, bf16[256,2048]{1,0:T(8,128)(2,1)S(1)}, u32[]{:S(2)}, u32[]{:S(2)}) collective-permute-start(bf16[256,2048]{1,0:T(8,128)(2,1)S(1)} %get-tuple-element.84), channel_id=1, source_target_pairs={{3,0},{2,1},{1,2},{0,3},{7,4},{6,5},{5,6},{4,7},{11,8},{10,9},{9,1... | collective-permute-start | bytes 3145736 | tf_op jit(solution)/shard_map/ppermute | solution.py:45
  208.5 9.3 %collective-permute-start.30 = (bf16[128,2048]{1,0:T(8,128)(2,1)S(1)}, bf16[128,2048]{1,0:T(8,128)(2,1)S(1)}, u32[]{:S(2)}, u32[]{:S(2)}) collective-permute-start(bf16[128,2048]{1,0:T(8,128)(2,1)S(1)} %slice.255), channel_id=1, source_target_pairs={{4,0},{5,1},{6,2},{7,3},{0,4},{1,5},{2,6},{3,7},{12,8},{13,9},{14,... | collective-permute-start | bytes 1572872 | tf_op jit(solution)/shard_map/ppermute | solution.py:45
  209.0 9.3 %collective-permute-start.31 = (bf16[128,2048]{1,0:T(8,128)(2,1)S(1)}, bf16[128,2048]{1,0:T(8,128)(2,1)S(1)}, u32[]{:S(2)}, u32[]{:S(2)}) collective-permute-start(bf16[128,2048]{1,0:T(8,128)(2,1)S(1)} %slice.254), channel_id=1, source_target_pairs={{1,0},{0,1},{3,2},{2,3},{5,4},{4,5},{7,6},{6,7},{9,8},{8,9},{11,10... | collective-permute-start | bytes 1572872 | tf_op jit(solution)/shard_map/ppermute | solution.py:45
  218.7 9.3 %collective-permute-start.32 = (bf16[128,2048]{1,0:T(8,128)(2,1)S(1)}, bf16[128,2048]{1,0:T(8,128)(2,1)S(1)}, u32[]{:S(2)}, u32[]{:S(2)}) collective-permute-start(bf16[128,2048]{1,0:T(8,128)(2,1)S(1)} %pad_maximum_fusion.2), channel_id=1, source_target_pairs={{3,0},{2,1},{1,2},{0,3},{7,4},{6,5},{5,6},{4,7},{11,8},{10,9},{9,1... | collective-permute-start | bytes 1572872 | tf_op jit(solution)/shard_map/ppermute | solution.py:45
  218.8 10.5 %collective-permute-start.33 = (bf16[128,2048]{1,0:T(8,128)(2,1)S(1)}, bf16[128,2048]{1,0:T(8,128)(2,1)S(1)}, u32[]{:S(2)}, u32[]{:S(2)}) collective-permute-start(bf16[128,2048]{1,0:T(8,128)(2,1)S(1)} %pad_maximum_fusion.3), channel_id=1, source_target_pairs={{12,0},{13,1},{14,2},{15,3},{8,4},{9,5},{10,6},{11,7},{4,8},{5,9},... | collective-permute-start | bytes 1572872 | tf_op jit(solution)/shard_map/ppermute | solution.py:45
  230.2 6.7 %collective-permute-start.34 = (bf16[64,2048]{1,0:T(8,128)(2,1)}, bf16[64,2048]{1,0:T(8,128)(2,1)}, u32[]{:S(2)}, u32[]{:S(2)}) collective-permute-start(bf16[64,2048]{1,0:T(8,128)(2,1)} %fusion.15), channel_id=1, source_target_pairs={{1,0},{0,1},{3,2},{2,3},{5,4},{4,5},{7,6},{6,7},{9,8},{8,9},{11,10... | collective-permute-start | bytes 786440 | tf_op jit(solution)/shard_map/ppermute | solution.py:45
  232.3 6.6 %collective-permute-start.35 = (bf16[64,2048]{1,0:T(8,128)(2,1)S(1)}, bf16[64,2048]{1,0:T(8,128)(2,1)}, u32[]{:S(2)}, u32[]{:S(2)}) collective-permute-start(bf16[64,2048]{1,0:T(8,128)(2,1)S(1)} %fusion.12), channel_id=1, source_target_pairs={{4,0},{5,1},{6,2},{7,3},{0,4},{1,5},{2,6},{3,7},{12,8},{13,9},{14,... | collective-permute-start | bytes 786440 | tf_op jit(solution)/shard_map/ppermute | solution.py:45

commit v8 on v7

--- a/solution.py
+++ b/solution.py
@@ -347,7 +347,13 @@
         sums = kept.astype(F32) + got.astype(F32)
         return [sums[:half], sums[half:]]
 
-    def hidden_of(value):
+    def half_sum(kept, got):
+        return (kept.astype(F32) + got.astype(F32)).astype(BF)
+
+    def hidden_of(half, got):
+        rows = half.shape[0] // 2
+        other = jnp.concatenate([got[rows:], got[:rows]], axis=0)
+        value = half.astype(F32) + other.astype(F32)
         pre, back = value[:, :width], value[:, width:]
         activated, slope = gelu_parts(pre)
         return jnp.concatenate([activated.astype(BF), (back * slope).astype(BF)], axis=1)
@@ -363,15 +369,13 @@
     kept_a, send_a = panel_dot(True, near_a, rest_a, more=exchange(sent_a, other_core))
     sent_b = panel_dot(False, near_b, rest_b, rest_b[True], send_a)
     step_a = after(exchange(send_a, along_z(0)), sent_b)
-    half_a = halfway(kept_a, step_a)
-    turn_a = exchange(half_a[1].astype(BF), along_z(1))
+    half_a = half_sum(kept_a, step_a)
+    turn_a = exchange(half_a, along_z(1))
     kept_b, send_b = panel_dot(
         True, near_b, rest_b, step_a, more=exchange(sent_b, other_core)
     )
-    mine_a = hidden_of(half_a[0] + after(turn_a, send_b).astype(F32))
-    next_a = exchange(mine_a, along_z(1))
-    step_b = exchange(after(send_b, next_a), along_z(0))
-    pair_a = join(place, mine_a, next_a)
+    pair_a = hidden_of(half_a, after(turn_a, send_b))
+    step_b = exchange(after(send_b, turn_a), along_z(0))
     far_a = exchange(pair_a, along_z(0))
     hid_a = {True: (pair_a, far_a)}
     hid_a[False] = (exchange(pair_a, other_core), exchange(far_a, other_core))
@@ -410,21 +414,19 @@
     out_a, out_b, got_a, got_b = {}, {}, {}, {}
     sums_a, sums_b, last_a, last_b, total_a, total_b = {}, {}, {}, {}, {}, {}
     out_a[True] = out_dot(True, hid_a[True])
-    half_b = halfway(kept_b, after(step_b, out_a[True][0]))
-    turn_b = exchange(half_b[1].astype(BF), along_z(1))
+    half_b = half_sum(kept_b, after(step_b, out_a[True][0]))
+    turn_b = exchange(half_b, along_z(1))
     out_a[False] = out_dot(False, hid_a[False], out_a[True][0], step_b)
-    mine_b = hidden_of(half_b[0] + after(turn_b, out_a[False][0]).astype(F32))
-    next_b = exchange(mine_b, along_z(1))
     for keep in both_ways:
         got_a[keep] = exchange(out_a[keep][1], along(keep, True, 1))
-    grad_in = grads(0, near_a, rest_a, hid_a, None, out_a[False][0], turn_b)
-    pair_b = join(place, mine_b, after(next_b, grad_in))
+    grad_in = grads(0, near_a, rest_a, hid_a, None, out_a[False][0])
+    pair_b = hidden_of(half_b, after(turn_b, grad_in))
     far_b = exchange(pair_b, along_z(0))
-    grad_out = grads(1, near_a, rest_a, hid_a, None, next_b, got_a[True], got_a[False], grad_in)
+    grad_out = grads(1, near_a, rest_a, hid_a, None, turn_b, got_a[True], got_a[False], grad_in)
     for keep in both_ways:
         got = after(got_a[keep], grad_in, got_a[not keep])
         sums_a[keep], last_a[keep] = second_half(keep, out_a[keep][0], got)
-    far_b = after(far_b, grad_out)
+    far_b = after(far_b, grad_out, last_a[True], last_a[False])
     hid_b = {True: (pair_b, far_b)}
     hid_b[False] = (exchange(pair_b, other_core), exchange(far_b, other_core))
 
@@ -433,7 +435,7 @@
     for keep in both_ways:
         got_b[keep] = exchange(out_b[keep][1], along(keep, True, 1))
     grad_in = grads(
-        0, near_b, rest_b, hid_b, grad_in, out_b[False][0], last_a[True], last_a[False]
+        0, near_b, rest_b, hid_b, grad_in, out_b[False][0]
     )
     for keep in both_ways:
         got = after(got_b[keep], grad_in, got_b[not keep])

time: 242 us -> 240 us (level)
    ppermute x36 -> x34, waiting for transfers between devices: 111 us -> 109 us  [exchange(): return lax.ppermute(array, AXES, pairs)]
    ppermute x36 -> x34, starting transfers between devices: 48.8 us -> 47.5 us  [exchange(): return lax.ppermute(array, AXES, pairs)]
    pallas_call x9 -> x7, Pallas kernels: 6.56 us -> 5.35 us  [whole(): pl.pallas_call(kernel, in_specs=[pl.BlockSpec(memory_space=pltpu.SMEM)] +...]
  transfers between devices with their start and end apart: 36 -> 34, of which waited for: 25 -> 24; matrix products, arithmetic and copies ran while one was open for 2% -> 3% of each run, Pallas kernels for 25% -> 25%
where the time goes in v8:
time: 240 us; the launch traced here: 237 us
  waiting for transfers between devices  109 us (45%)
  Pallas kernels  66.9 us (28%)
  starting transfers between devices  47.5 us (20%)
  other arithmetic  7.89 us (3%)
  local copies, waits for them, and re-layouts  5.25 us (2%)
    ppermute x34, waiting for transfers between devices, exchange(): return lax.ppermute(array, AXES, pairs)  109 us
    ppermute x34, starting transfers between devices, exchange(): return lax.ppermute(array, AXES, pairs)  47.5 us
    pallas_call x8, Pallas kernels, pair_dot(): pl.pallas_call(functools.partial(pair_kernel, keep, hidden, more is not N...  36.8 us
    pallas_call x4, Pallas kernels, grad_dot(): pl.pallas_call(functools.partial(grad_kernel, pairs, block, factor, begun...  24.8 us
    pallas_call x7, Pallas kernels, whole(): pl.pallas_call(kernel, in_specs=[pl.BlockSpec(memory_space=pltpu.SMEM)] +...  5.35 us
  transfers between devices with their start and end apart: 34, of which 24 were waited for; matrix products, arithmetic and copies ran while one was open for 3% of the time, Pallas kernels for 25%

profile of v8, /device:TPU:8, one launch (start us, length us, event | category | flops | bytes accessed | tf_op | source)
XLA Modules:
  0.0 237.4 jit_solution(11443596294502428732)
XLA Ops:
  3.2 1.6 collective-permute-start
  5.2 4.4 %collective-permute-done.b_ref = bf16[64,2048]{1,0:T(8,128)(2,1)S(1)} collective-permute-done((bf16[64,2048]{1,0:T(8,128)(2,1)S(1)}, bf16[64,2048]{1,0:T(8,128)(2,1)S(1)}, u32[]{:S(2)}, u32[]{:S(2)}) %collective-permute-start) | collective-permute-done | bytes 262176 | tf_op jit(solution)/shard_map/ppermute | solution.py:45
  10.2 2.8 %collective-permute-start.1 = (bf16[128,2048]{1,0:T(8,128)(2,1)S(1)}, bf16[128,2048]{1,0:T(8,128)(2,1)S(1)}, u32[]{:S(2)}, u32[]{:S(2)}) collective-permute-start(bf16[128,2048]{1,0:T(8,128)(2,1)S(1)} %shard_map.76), channel_id=1, source_target_pairs={{12,0},{13,1},{14,2},{15,3},{8,4},{9,5},{10,6},{11,7},{4,8},{5,9},... | collective-permute-start | bytes 1572872 | tf_op jit(solution)/shard_map/ppermute | solution.py:45
  13.7 1.7 collective-permute-start.3
  15.3 5.4 %collective-permute-done.1.c_ref = bf16[128,2048]{1,0:T(8,128)(2,1)S(1)} collective-permute-done((bf16[128,2048]{1,0:T(8,128)(2,1)S(1)}, bf16[128,2048]{1,0:T(8,128)(2,1)S(1)}, u32[]{:S(2)}, u32[]{:S(2)}) %collective-permute-start.1) | collective-permute-done | bytes 524320 | tf_op jit(solution)/shard_map/ppermute | solution.py:45
  21.3 1.6 collective-permute-done.3.c_ref
  23.6 1.7 collective-permute-start.4
  25.5 12.9 %collective-permute-done.4.near_ref = bf16[256,2048]{1,0:T(8,128)(2,1)S(1)} collective-permute-done((bf16[256,2048]{1,0:T(8,128)(2,1)S(1)}, bf16[256,2048]{1,0:T(8,128)(2,1)S(1)}, u32[]{:S(2)}, u32[]{:S(2)}) %collective-permute-start.4) | collective-permute-done | bytes 1048608 | tf_op jit(solution)/shard_map/ppermute | solution.py:45
  39.1 2.1 collective-permute-start.5
  41.4 1.7 shard_map.81
  43.7 2.7 %constant_dynamic-slice_fusion = (bf16[1024,1024]{1,0:T(8,128)(2,1)S(1)}, bf16[1024,1024]{1,0:T(8,128)(2,1)S(1)}) fusion(bf16[2048,1024]{1,0:T(8,128)(2,1)} %param.7, s32[]{:T(128)S(6)} %select_n.30, bf16[1024,2048]{1,0:T(8,128)(2,1)} %param.6), kind=kLoop, calls=%fused_computation.55 | loop fusion | bytes 8388612 | tf_op jit(solution)/shard_map/dynamic_slice | solution.py:321
  46.4 7.8 %collective-permute-done.5.refs_1_.refs_5_ = bf16[256,2048]{1,0:T(8,128)(2,1)} collective-permute-done((bf16[256,2048]{1,0:T(8,128)(2,1)S(1)}, bf16[256,2048]{1,0:T(8,128)(2,1)}, u32[]{:S(2)}, u32[]{:S(2)}) %collective-permute-start.5) | collective-permute-done | bytes 1048608 | tf_op jit(solution)/shard_map/ppermute | solution.py:45
  54.1 5.3 %collective-permute-done.7.refs_1_.refs_3_.refs_7_ = bf16[256,2048]{1,0:T(8,128)(2,1)} collective-permute-done((bf16[256,2048]{1,0:T(8,128)(2,1)}, bf16[256,2048]{1,0:T(8,128)(2,1)}, u32[]{:S(2)}, u32[]{:S(2)}) %collective-permute-start.7) | collective-permute-done | bytes 1048608 | tf_op jit(solution)/shard_map/ppermute | solution.py:45
  59.4 5.5 %shard_map.82 = bf16[512,2048]{1,0:T(8,128)(2,1)S(1)} custom-call(s32[2]{0:T(128)S(1)} %pad_add_fusion.place_ref, bf16[256,2048]{1,0:T(8,128)(2,1)} %get-tuple-element.52.refs_0_.refs_2_.refs_6_, bf16[256,2048]{1,0:T(8,128)(2,1)} %collective-permute-done.7.refs_1_.refs_3_.refs_7_, bf16[1024,1024]{1,0:T(8,128)(2,1)S(1)} %get-tuple-element.128.refs_2_.refs_3_, ...), custom_call_target="tpu_custom_call" | custom-call | flops 2147483 | bytes 8388 | tf_op jit(solution)/shard_map/pallas_call | solution.py:240
  65.0 3.0 %collective-permute-start.11 = (bf16[256,2048]{1,0:T(8,128)(2,1)S(1)}, bf16[256,2048]{1,0:T(8,128)(2,1)S(1)}, u32[]{:S(2)}, u32[]{:S(2)}) collective-permute-start(bf16[256,2048]{1,0:T(8,128)(2,1)S(1)} %get-tuple-element.81.refs_0_.refs_4_), channel_id=1, source_target_pairs={{3,0},{2,1},{1,2},{0,3},{7,4},{6,5},{5,6},{4,7},{11,8},{10,9},{9,1... | collective-permute-start | bytes 3145736 | tf_op jit(solution)/shard_map/ppermute | solution.py:45
  69.2 5.3 %shard_map.83 = (bf16[256,2048]{1,0:T(8,128)(2,1)S(1)}, bf16[256,2048]{1,0:T(8,128)(2,1)S(1)}) custom-call(s32[2]{0:T(128)S(1)} %pad_add_fusion.place_ref, bf16[256,2048]{1,0:T(8,128)(2,1)S(1)} %get-tuple-element.68.refs_0_.refs_4_, bf16[256,2048]{1,0:T(8,128)(2,1)} %collective-permute-done.5.refs_1_.refs_5_, ...), custom_call_target="tpu_custom_call" | custom-call | flops 2147483 | bytes 8388 | tf_op jit(solution)/shard_map/pallas_call | solution.py:240
  74.5 2.0 collective-permute-start.9
  76.5 4.3 %collective-permute-done.11.refs_1_.refs_5_ = bf16[256,2048]{1,0:T(8,128)(2,1)S(1)} collective-permute-done((bf16[256,2048]{1,0:T(8,128)(2,1)S(1)}, bf16[256,2048]{1,0:T(8,128)(2,1)S(1)}, u32[]{:S(2)}, u32[]{:S(2)}) %collective-permute-start.11) | collective-permute-done | bytes 1048608 | tf_op jit(solution)/shard_map/ppermute | solution.py:45
  80.8 3.2 %collective-permute-done.10.refs_1_.refs_3_.refs_7_ = bf16[256,2048]{1,0:T(8,128)(2,1)S(1)} collective-permute-done((bf16[256,2048]{1,0:T(8,128)(2,1)S(1)}, bf16[256,2048]{1,0:T(8,128)(2,1)S(1)}, u32[]{:S(2)}, u32[]{:S(2)}) %collective-permute-start.10) | collective-permute-done | bytes 1048608 | tf_op jit(solution)/shard_map/ppermute | solution.py:45
  84.0 4.3 %shard_map.84 = bf16[512,2048]{1,0:T(8,128)(2,1)S(1)} custom-call(s32[2]{0:T(128)S(1)} %pad_add_fusion.place_ref, bf16[256,2048]{1,0:T(8,128)(2,1)S(1)} %get-tuple-element.56.refs_0_.refs_2_.refs_6_, bf16[256,2048]{1,0:T(8,128)(2,1)S(1)} %collective-permute-done.10.refs_1_.refs_3_.refs_7_, bf16[1024,1024]{1,0:T(8,128)(2,1)S(1)} %get-tuple-element.128.refs_2_.refs_3_, ...), custom_call_target="tpu_custom_call" | custom-call | flops 2147483 | bytes 8388 | tf_op jit(solution)/shard_map/pallas_call | solution.py:240
  89.8 4.1 %collective-permute-start.12 = (bf16[256,2048]{1,0:T(8,128)(2,1)S(1)}, bf16[256,2048]{1,0:T(8,128)(2,1)S(1)}, u32[]{:S(2)}, u32[]{:S(2)}) collective-permute-start(bf16[256,2048]{1,0:T(8,128)(2,1)S(1)} %add_convert_fusion.1), channel_id=1, source_target_pairs={{96,0},{97,1},{98,2},{99,3},{100,4},{101,5},{102,6},{103,7},{104,8... | collective-permute-start | bytes 3145736 | tf_op jit(solution)/shard_map/ppermute | solution.py:45
  93.9 4.5 %shard_map.85 = (bf16[256,2048]{1,0:T(8,128)(2,1)S(1)}, bf16[256,2048]{1,0:T(8,128)(2,1)S(1)}) custom-call(s32[2]{0:T(128)S(1)} %pad_add_fusion.place_ref, bf16[256,2048]{1,0:T(8,128)(2,1)S(1)} %get-tuple-element.81.refs_0_.refs_4_, bf16[256,2048]{1,0:T(8,128)(2,1)S(1)} %collective-permute-done.11.refs_1_.refs_5_, ...), custom_call_target="tpu_custom_call" | custom-call | flops 2147483 | bytes 8388 | tf_op jit(solution)/shard_map/pallas_call | solution.py:240
  98.4 8.3 %collective-permute-done.12 = bf16[256,2048]{1,0:T(8,128)(2,1)S(1)} collective-permute-done((bf16[256,2048]{1,0:T(8,128)(2,1)S(1)}, bf16[256,2048]{1,0:T(8,128)(2,1)S(1)}, u32[]{:S(2)}, u32[]{:S(2)}) %collective-permute-start.12) | collective-permute-done | bytes 1048608 | tf_op jit(solution)/shard_map/ppermute | solution.py:45
  107.8 2.0 collective-permute-start.18
  109.8 12.8 %collective-permute-done.14.refs_1_.refs_5_ = bf16[256,2048]{1,0:T(8,128)(2,1)S(1)} collective-permute-done((bf16[256,2048]{1,0:T(8,128)(2,1)S(1)}, bf16[256,2048]{1,0:T(8,128)(2,1)S(1)}, u32[]{:S(2)}, u32[]{:S(2)}) %collective-permute-start.14) | collective-permute-done | bytes 1048608 | tf_op jit(solution)/shard_map/ppermute | solution.py:45
  122.6 4.3 %shard_map.86 = (bf16[256,2048]{1,0:T(8,128)(2,1)S(1)}, bf16[256,2048]{1,0:T(8,128)(2,1)S(1)}) custom-call(s32[2]{0:T(128)S(1)} %pad_add_fusion.place_ref, bf16[256,2048]{1,0:T(8,128)(2,1)S(1)} %pad_maximum_fusion.refs_0_.refs_4_, bf16[256,2048]{1,0:T(8,128)(2,1)S(1)} %collective-permute-done.14.refs_1_.refs_5_, ...), custom_call_target="tpu_custom_call" | custom-call | flops 2147483 | bytes 8388 | tf_op jit(solution)/shard_map/pallas_call | solution.py:240
  126.9 6.9 %collective-permute-done.18 = bf16[256,2048]{1,0:T(8,128)(2,1)S(1)} collective-permute-done((bf16[256,2048]{1,0:T(8,128)(2,1)S(1)}, bf16[256,2048]{1,0:T(8,128)(2,1)S(1)}, u32[]{:S(2)}, u32[]{:S(2)}) %collective-permute-start.18) | collective-permute-done | bytes 1048608 | tf_op jit(solution)/shard_map/ppermute | solution.py:45
  134.2 3.3 %collective-permute-start.21 = (bf16[256,2048]{1,0:T(8,128)(2,1)S(1)}, bf16[256,2048]{1,0:T(8,128)(2,1)S(1)}, u32[]{:S(2)}, u32[]{:S(2)}) collective-permute-start(bf16[256,2048]{1,0:T(8,128)(2,1)S(1)} %add_convert_fusion), channel_id=1, source_target_pairs={{96,0},{97,1},{98,2},{99,3},{100,4},{101,5},{102,6},{103,7},{104,8... | collective-permute-start | bytes 3145736 | tf_op jit(solution)/shard_map/ppermute | solution.py:45
  137.5 2.0 collective-permute-start.15
  139.6 4.3 %shard_map.87 = (bf16[256,2048]{1,0:T(8,128)(2,1)S(1)}, bf16[256,2048]{1,0:T(8,128)(2,1)S(1)}) custom-call(s32[2]{0:T(128)S(1)} %pad_add_fusion.place_ref, bf16[256,2048]{1,0:T(8,128)(2,1)S(1)} %collective-permute-done.16.refs_0_.refs_6_.refs_2_, bf16[256,2048]{1,0:T(8,128)(2,1)S(1)} %collective-permute-done.17.refs_1_.refs_7_.refs_3_, ...), custom_call_target="tpu_custom_call" | custom-call | flops 2147483 | bytes 8388 | tf_op jit(solution)/shard_map/pallas_call | solution.py:240
  144.8 5.9 %shard_map.88.refs_8_ = f32[1024,1024]{1,0:T(8,128)} custom-call(bf16[256,2048]{1,0:T(8,128)(2,1)S(1)} %get-tuple-element.68.refs_0_.refs_4_, bf16[256,2048]{1,0:T(8,128)(2,1)} %collective-permute-done.5.refs_1_.refs_5_, bf16[256,2048]{1,0:T(8,128)(2,1)} %get-tuple-element.52.refs_0_.refs_2_.refs_6_, ...), custom_call_target="tpu_custom_call" | custom-call | flops 2147483 | bytes 5242 | tf_op jit(solution)/shard_map/pallas_call | solution.py:289
  151.9 1.7 collective-permute-done.15
  153.6 5.2 %collective-permute-done.19 = bf16[256,2048]{1,0:T(8,128)(2,1)S(1)} collective-permute-done((bf16[256,2048]{1,0:T(8,128)(2,1)S(1)}, bf16[256,2048]{1,0:T(8,128)(2,1)S(1)}, u32[]{:S(2)}, u32[]{:S(2)}) %collective-permute-start.19) | collective-permute-done | bytes 1048608 | tf_op jit(solution)/shard_map/ppermute | solution.py:45
  159.7 2.3 collective-permute-start.23
  162.0 5.9 %shard_map.89.refs_8_ = f32[1024,1024]{1,0:T(8,128)} custom-call(bf16[256,2048]{1,0:T(8,128)(2,1)S(1)} %pad_maximum_fusion.refs_0_.refs_4_, bf16[256,2048]{1,0:T(8,128)(2,1)S(1)} %collective-permute-done.14.refs_1_.refs_5_, bf16[256,2048]{1,0:T(8,128)(2,1)S(1)} %collective-permute-done.16.refs_0_.refs_6_.refs_2_, ...), custom_call_target="tpu_custom_call" | custom-call | flops 2147483 | bytes 5242 | tf_op jit(solution)/shard_map/pallas_call | solution.py:289
  169.7 4.3 %shard_map.90 = (bf16[256,2048]{1,0:T(8,128)(2,1)S(1)}, bf16[256,2048]{1,0:T(8,128)(2,1)S(1)}) custom-call(s32[2]{0:T(128)S(1)} %pad_add_fusion.place_ref, bf16[256,2048]{1,0:T(8,128)(2,1)S(1)} %pad_maximum_fusion.1.refs_0_.refs_4_, bf16[256,2048]{1,0:T(8,128)(2,1)S(1)} %collective-permute-done.22.refs_1_.refs_5_, ...), custom_call_target="tpu_custom_call" | custom-call | flops 2147483 | bytes 8388 | tf_op jit(solution)/shard_map/pallas_call | solution.py:240
  174.0 4.2 %collective-permute-start.24 = (bf16[256,2048]{1,0:T(8,128)(2,1)S(1)}, bf16[256,2048]{1,0:T(8,128)(2,1)S(1)}, u32[]{:S(2)}, u32[]{:S(2)}) collective-permute-start(bf16[256,2048]{1,0:T(8,128)(2,1)S(1)} %get-tuple-element.78), channel_id=1, source_target_pairs={{12,0},{13,1},{14,2},{15,3},{8,4},{9,5},{10,6},{11,7},{4,8},{5,9},... | collective-permute-start | bytes 3145736 | tf_op jit(solution)/shard_map/ppermute | solution.py:45
  178.4 4.3 %shard_map.91 = (bf16[256,2048]{1,0:T(8,128)(2,1)S(1)}, bf16[256,2048]{1,0:T(8,128)(2,1)S(1)}) custom-call(s32[2]{0:T(128)S(1)} %pad_add_fusion.place_ref, bf16[256,2048]{1,0:T(8,128)(2,1)S(1)} %collective-permute-done.25.refs_0_.refs_6_.refs_2_, bf16[256,2048]{1,0:T(8,128)(2,1)S(1)} %collective-permute-done.26.refs_1_.refs_7_.refs_3_, ...), custom_call_target="tpu_custom_call" | custom-call | flops 2147483 | bytes 8388 | tf_op jit(solution)/shard_map/pallas_call | solution.py:240
  182.7 1.9 collective-permute-start.27
  184.8 6.5 %shard_map.92 = f32[1024,1024]{1,0:T(8,128)} custom-call(bf16[256,2048]{1,0:T(8,128)(2,1)S(1)} %get-tuple-element.81.refs_0_.refs_4_, bf16[256,2048]{1,0:T(8,128)(2,1)S(1)} %collective-permute-done.11.refs_1_.refs_5_, bf16[256,2048]{1,0:T(8,128)(2,1)S(1)} %get-tuple-element.56.refs_0_.refs_2_.refs_6_, ...), custom_call_target="tpu_custom_call", output_to_operand_aliasing={{}: (8, {})} | custom-call | flops 2147483 | bytes 5242 | tf_op jit(solution)/shard_map/pallas_call | solution.py:289
  191.3 6.5 %collective-permute-done.27 = bf16[256,2048]{1,0:T(8,128)(2,1)S(1)} collective-permute-done((bf16[256,2048]{1,0:T(8,128)(2,1)S(1)}, bf16[256,2048]{1,0:T(8,128)(2,1)S(1)}, u32[]{:S(2)}, u32[]{:S(2)}) %collective-permute-start.27) | collective-permute-done | bytes 1048608 | tf_op jit(solution)/shard_map/ppermute | solution.py:45
  200.1 4.5 %collective-permute-start.29 = (bf16[128,2048]{1,0:T(8,128)(2,1)S(1)}, bf16[128,2048]{1,0:T(8,128)(2,1)S(1)}, u32[]{:S(2)}, u32[]{:S(2)}) collective-permute-start(bf16[128,2048]{1,0:T(8,128)(2,1)S(1)} %slice.244), channel_id=1, source_target_pairs={{1,0},{0,1},{3,2},{2,3},{5,4},{4,5},{7,6},{6,7},{9,8},{8,9},{11,10... | collective-permute-start | bytes 1572872 | tf_op jit(solution)/shard_map/ppermute | solution.py:45
  204.7 6.5 %shard_map.93 = f32[1024,1024]{1,0:T(8,128)} custom-call(bf16[256,2048]{1,0:T(8,128)(2,1)S(1)} %pad_maximum_fusion.1.refs_0_.refs_4_, bf16[256,2048]{1,0:T(8,128)(2,1)S(1)} %collective-permute-done.22.refs_1_.refs_5_, bf16[256,2048]{1,0:T(8,128)(2,1)S(1)} %collective-permute-done.25.refs_0_.refs_6_.refs_2_, ...), custom_call_target="tpu_custom_call", output_to_operand_aliasing={{}: (8, {})} | custom-call | flops 2147483 | bytes 5242 | tf_op jit(solution)/shard_map/pallas_call | solution.py:289
  213.4 8.9 %collective-permute-done.30 = bf16[128,2048]{1,0:T(8,128)(2,1)S(1)} collective-permute-done((bf16[128,2048]{1,0:T(8,128)(2,1)S(1)}, bf16[128,2048]{1,0:T(8,128)(2,1)S(1)}, u32[]{:S(2)}, u32[]{:S(2)}) %collective-permute-start.30) | collective-permute-done | bytes 524320 | tf_op jit(solution)/shard_map/ppermute | solution.py:45
  222.3 2.6 %collective-permute-done.31 = bf16[128,2048]{1,0:T(8,128)(2,1)S(1)} collective-permute-done((bf16[128,2048]{1,0:T(8,128)(2,1)S(1)}, bf16[128,2048]{1,0:T(8,128)(2,1)S(1)}, u32[]{:S(2)}, u32[]{:S(2)}) %collective-permute-start.31) | collective-permute-done | bytes 524320 | tf_op jit(solution)/shard_map/ppermute | solution.py:45
  225.7 2.9 %collective-permute-start.32 = (bf16[64,2048]{1,0:T(8,128)(2,1)}, bf16[64,2048]{1,0:T(8,128)(2,1)}, u32[]{:S(2)}, u32[]{:S(2)}) collective-permute-start(bf16[64,2048]{1,0:T(8,128)(2,1)} %fusion.15), channel_id=1, source_target_pairs={{1,0},{0,1},{3,2},{2,3},{5,4},{4,5},{7,6},{6,7},{9,8},{8,9},{11,10... | collective-permute-start | bytes 786440 | tf_op jit(solution)/shard_map/ppermute | solution.py:45
  229.4 3.9 %collective-permute-done.32 = bf16[64,2048]{1,0:T(8,128)(2,1)} collective-permute-done((bf16[64,2048]{1,0:T(8,128)(2,1)}, bf16[64,2048]{1,0:T(8,128)(2,1)}, u32[]{:S(2)}, u32[]{:S(2)}) %collective-permute-start.32) | collective-permute-done | bytes 262176 | tf_op jit(solution)/shard_map/ppermute | solution.py:45
  233.3 2.1 collective-permute-done.33
  (84 shorter events, 24.6 us)
Async XLA Ops:
  0.7 1.0 copy-start
  1.7 0.9 copy-start.1
  3.2 6.5 %collective-permute-start = (bf16[64,2048]{1,0:T(8,128)(2,1)S(1)}, bf16[64,2048]{1,0:T(8,128)(2,1)S(1)}, u32[]{:S(2)}, u32[]{:S(2)}) collective-permute-start(bf16[64,2048]{1,0:T(8,128)(2,1)S(1)} %get-tuple-element.47.a_ref), channel_id=1, source_target_pairs={{4,0},{5,1},{6,2},{7,3},{0,4},{1,5},{2,6},{3,7},{12,8},{13,9},{14,... | collective-permute-start | bytes 786440 | tf_op jit(solution)/shard_map/ppermute | solution.py:45
  4.8 8.3 %collective-permute-start.2 = (bf16[64,2048]{1,0:T(8,128)(2,1)S(1)}, bf16[64,2048]{1,0:T(8,128)(2,1)S(1)}, u32[]{:S(2)}, u32[]{:S(2)}) collective-permute-start(bf16[64,2048]{1,0:T(8,128)(2,1)S(1)} %get-tuple-element.48.a_ref), channel_id=1, source_target_pairs={{1,0},{0,1},{3,2},{2,3},{5,4},{4,5},{7,6},{6,7},{9,8},{8,9},{11,10... | collective-permute-start | bytes 786440 | tf_op jit(solution)/shard_map/ppermute | solution.py:45
  10.2 10.5 %collective-permute-start.1 = (bf16[128,2048]{1,0:T(8,128)(2,1)S(1)}, bf16[128,2048]{1,0:T(8,128)(2,1)S(1)}, u32[]{:S(2)}, u32[]{:S(2)}) collective-permute-start(bf16[128,2048]{1,0:T(8,128)(2,1)S(1)} %shard_map.76), channel_id=1, source_target_pairs={{12,0},{13,1},{14,2},{15,3},{8,4},{9,5},{10,6},{11,7},{4,8},{5,9},... | collective-permute-start | bytes 1572872 | tf_op jit(solution)/shard_map/ppermute | solution.py:45
  13.7 9.3 %collective-permute-start.3 = (bf16[128,2048]{1,0:T(8,128)(2,1)S(1)}, bf16[128,2048]{1,0:T(8,128)(2,1)S(1)}, u32[]{:S(2)}, u32[]{:S(2)}) collective-permute-start(bf16[128,2048]{1,0:T(8,128)(2,1)S(1)} %shard_map.78), channel_id=1, source_target_pairs={{3,0},{2,1},{1,2},{0,3},{7,4},{6,5},{5,6},{4,7},{11,8},{10,9},{9,1... | collective-permute-start | bytes 1572872 | tf_op jit(solution)/shard_map/ppermute | solution.py:45
  23.6 14.9 %collective-permute-start.4 = (bf16[256,2048]{1,0:T(8,128)(2,1)S(1)}, bf16[256,2048]{1,0:T(8,128)(2,1)S(1)}, u32[]{:S(2)}, u32[]{:S(2)}) collective-permute-start(bf16[256,2048]{1,0:T(8,128)(2,1)S(1)} %shard_map.77.own_ref), channel_id=1, source_target_pairs={{1,0},{0,1},{3,2},{2,3},{5,4},{4,5},{7,6},{6,7},{9,8},{8,9},{11,10... | collective-permute-start | bytes 3145736 | tf_op jit(solution)/shard_map/ppermute | solution.py:45
  25.3 16.1 %collective-permute-start.6 = (bf16[256,2048]{1,0:T(8,128)(2,1)S(1)}, bf16[256,2048]{1,0:T(8,128)(2,1)S(1)}, u32[]{:S(2)}, u32[]{:S(2)}) collective-permute-start(bf16[256,2048]{1,0:T(8,128)(2,1)S(1)} %shard_map.79.own_ref), channel_id=1, source_target_pairs={{4,0},{5,1},{6,2},{7,3},{0,4},{1,5},{2,6},{3,7},{12,8},{13,9},{14,... | collective-permute-start | bytes 3145736 | tf_op jit(solution)/shard_map/ppermute | solution.py:45
  39.1 15.0 %collective-permute-start.5 = (bf16[256,2048]{1,0:T(8,128)(2,1)S(1)}, bf16[256,2048]{1,0:T(8,128)(2,1)}, u32[]{:S(2)}, u32[]{:S(2)}) collective-permute-start(bf16[256,2048]{1,0:T(8,128)(2,1)S(1)} %get-tuple-element.68.refs_0_.refs_4_), channel_id=1, source_target_pairs={{3,0},{2,1},{1,2},{0,3},{7,4},{6,5},{5,6},{4,7},{11,8},{10,9},{9,1... | collective-permute-start | bytes 3145736 | tf_op jit(solution)/shard_map/ppermute | solution.py:45
  43.1 16.3 %collective-permute-start.7 = (bf16[256,2048]{1,0:T(8,128)(2,1)}, bf16[256,2048]{1,0:T(8,128)(2,1)}, u32[]{:S(2)}, u32[]{:S(2)}) collective-permute-start(bf16[256,2048]{1,0:T(8,128)(2,1)} %get-tuple-element.52.refs_0_.refs_2_.refs_6_), channel_id=1, source_target_pairs={{12,0},{13,1},{14,2},{15,3},{8,4},{9,5},{10,6},{11,7},{4,8},{5,9},... | collective-permute-start | bytes 3145736 | tf_op jit(solution)/shard_map/ppermute | solution.py:45
  64.9 4.2 %collective-permute-start.8 = (bf16[512,2048]{1,0:T(8,128)(2,1)S(1)}, bf16[512,2048]{1,0:T(8,128)(2,1)S(1)}, u32[]{:S(2)}, u32[]{:S(2)}) collective-permute-start(bf16[512,2048]{1,0:T(8,128)(2,1)S(1)} %shard_map.82), channel_id=1, source_target_pairs={{16,0},{17,1},{18,2},{19,3},{20,4},{21,5},{22,6},{23,7},{24,8},{25... | collective-permute-start | bytes 6291464 | tf_op jit(solution)/shard_map/ppermute | solution.py:45
  65.0 15.7 %collective-permute-start.11 = (bf16[256,2048]{1,0:T(8,128)(2,1)S(1)}, bf16[256,2048]{1,0:T(8,128)(2,1)S(1)}, u32[]{:S(2)}, u32[]{:S(2)}) collective-permute-start(bf16[256,2048]{1,0:T(8,128)(2,1)S(1)} %get-tuple-element.81.refs_0_.refs_4_), channel_id=1, source_target_pairs={{3,0},{2,1},{1,2},{0,3},{7,4},{6,5},{5,6},{4,7},{11,8},{10,9},{9,1... | collective-permute-start | bytes 3145736 | tf_op jit(solution)/shard_map/ppermute | solution.py:45
  68.0 16.0 %collective-permute-start.10 = (bf16[256,2048]{1,0:T(8,128)(2,1)S(1)}, bf16[256,2048]{1,0:T(8,128)(2,1)S(1)}, u32[]{:S(2)}, u32[]{:S(2)}) collective-permute-start(bf16[256,2048]{1,0:T(8,128)(2,1)S(1)} %get-tuple-element.56.refs_0_.refs_2_.refs_6_), channel_id=1, source_target_pairs={{12,0},{13,1},{14,2},{15,3},{8,4},{9,5},{10,6},{11,7},{4,8},{5,9},... | collective-permute-start | bytes 3145736 | tf_op jit(solution)/shard_map/ppermute | solution.py:45
  74.5 14.9 %collective-permute-start.9 = (bf16[256,2048]{1,0:T(8,128)(2,1)S(1)}, bf16[256,2048]{1,0:T(8,128)(2,1)S(1)}, u32[]{:S(2)}, u32[]{:S(2)}) collective-permute-start(bf16[256,2048]{1,0:T(8,128)(2,1)S(1)} %get-tuple-element.55), channel_id=1, source_target_pairs={{32,0},{33,1},{34,2},{35,3},{36,4},{37,5},{38,6},{39,7},{40,8},{41... | collective-permute-start | bytes 3145736 | tf_op jit(solution)/shard_map/ppermute | solution.py:45
  88.3 5.6 %collective-permute-start.13 = (bf16[512,2048]{1,0:T(8,128)(2,1)S(1)}, bf16[512,2048]{1,0:T(8,128)(2,1)S(1)}, u32[]{:S(2)}, u32[]{:S(2)}) collective-permute-start(bf16[512,2048]{1,0:T(8,128)(2,1)S(1)} %shard_map.84), channel_id=1, source_target_pairs={{16,0},{17,1},{18,2},{19,3},{20,4},{21,5},{22,6},{23,7},{24,8},{25... | collective-permute-start | bytes 6291464 | tf_op jit(solution)/shard_map/ppermute | solution.py:45
  89.8 16.9 %collective-permute-start.12 = (bf16[256,2048]{1,0:T(8,128)(2,1)S(1)}, bf16[256,2048]{1,0:T(8,128)(2,1)S(1)}, u32[]{:S(2)}, u32[]{:S(2)}) collective-permute-start(bf16[256,2048]{1,0:T(8,128)(2,1)S(1)} %add_convert_fusion.1), channel_id=1, source_target_pairs={{96,0},{97,1},{98,2},{99,3},{100,4},{101,5},{102,6},{103,7},{104,8... | collective-permute-start | bytes 3145736 | tf_op jit(solution)/shard_map/ppermute | solution.py:45
  107.7 14.9 %collective-permute-start.14 = (bf16[256,2048]{1,0:T(8,128)(2,1)S(1)}, bf16[256,2048]{1,0:T(8,128)(2,1)S(1)}, u32[]{:S(2)}, u32[]{:S(2)}) collective-permute-start(bf16[256,2048]{1,0:T(8,128)(2,1)S(1)} %pad_maximum_fusion.refs_0_.refs_4_), channel_id=1, source_target_pairs={{32,0},{33,1},{34,2},{35,3},{36,4},{37,5},{38,6},{39,7},{40,8},{41... | collective-permute-start | bytes 3145736 | tf_op jit(solution)/shard_map/ppermute | solution.py:45
  107.8 26.0 %collective-permute-start.18 = (bf16[256,2048]{1,0:T(8,128)(2,1)S(1)}, bf16[256,2048]{1,0:T(8,128)(2,1)S(1)}, u32[]{:S(2)}, u32[]{:S(2)}) collective-permute-start(bf16[256,2048]{1,0:T(8,128)(2,1)S(1)} %get-tuple-element.65), channel_id=1, source_target_pairs={{32,0},{33,1},{34,2},{35,3},{36,4},{37,5},{38,6},{39,7},{40,8},{41... | collective-permute-start | bytes 3145736 | tf_op jit(solution)/shard_map/ppermute | solution.py:45
  109.8 29.8 %collective-permute-start.16 = (bf16[256,2048]{1,0:T(8,128)(2,1)S(1)}, bf16[256,2048]{1,0:T(8,128)(2,1)S(1)}, u32[]{:S(2)}, u32[]{:S(2)}) collective-permute-start(bf16[256,2048]{1,0:T(8,128)(2,1)S(1)} %pad_maximum_fusion.refs_0_.refs_4_), channel_id=1, source_target_pairs={{16,0},{17,1},{18,2},{19,3},{20,4},{21,5},{22,6},{23,7},{24,8},{25... | collective-permute-start | bytes 3145736 | tf_op jit(solution)/shard_map/ppermute | solution.py:45
  133.8 5.7 %collective-permute-start.17 = (bf16[256,2048]{1,0:T(8,128)(2,1)S(1)}, bf16[256,2048]{1,0:T(8,128)(2,1)S(1)}, u32[]{:S(2)}, u32[]{:S(2)}) collective-permute-start(bf16[256,2048]{1,0:T(8,128)(2,1)S(1)} %collective-permute-done.14.refs_1_.refs_5_), channel_id=1, source_target_pairs={{16,0},{17,1},{18,2},{19,3},{20,4},{21,5},{22,6},{23,7},{24,8},{25... | collective-permute-start | bytes 3145736 | tf_op jit(solution)/shard_map/ppermute | solution.py:45
  134.2 16.5 %collective-permute-start.21 = (bf16[256,2048]{1,0:T(8,128)(2,1)S(1)}, bf16[256,2048]{1,0:T(8,128)(2,1)S(1)}, u32[]{:S(2)}, u32[]{:S(2)}) collective-permute-start(bf16[256,2048]{1,0:T(8,128)(2,1)S(1)} %add_convert_fusion), channel_id=1, source_target_pairs={{96,0},{97,1},{98,2},{99,3},{100,4},{101,5},{102,6},{103,7},{104,8... | collective-permute-start | bytes 3145736 | tf_op jit(solution)/shard_map/ppermute | solution.py:45
  137.5 16.0 %collective-permute-start.15 = (bf16[256,2048]{1,0:T(8,128)(2,1)S(1)}, bf16[256,2048]{1,0:T(8,128)(2,1)S(1)}, u32[]{:S(2)}, u32[]{:S(2)}) collective-permute-start(bf16[256,2048]{1,0:T(8,128)(2,1)S(1)} %get-tuple-element.64), channel_id=1, source_target_pairs={{12,0},{13,1},{14,2},{15,3},{8,4},{9,5},{10,6},{11,7},{4,8},{5,9},... | collective-permute-start | bytes 3145736 | tf_op jit(solution)/shard_map/ppermute | solution.py:45
  143.9 14.9 %collective-permute-start.19 = (bf16[256,2048]{1,0:T(8,128)(2,1)S(1)}, bf16[256,2048]{1,0:T(8,128)(2,1)S(1)}, u32[]{:S(2)}, u32[]{:S(2)}) collective-permute-start(bf16[256,2048]{1,0:T(8,128)(2,1)S(1)} %get-tuple-element.69), channel_id=1, source_target_pairs={{3,0},{2,1},{1,2},{0,3},{7,4},{6,5},{5,6},{4,7},{11,8},{10,9},{9,1... | collective-permute-start | bytes 3145736 | tf_op jit(solution)/shard_map/ppermute | solution.py:45
  151.8 16.1 %collective-permute-start.22 = (bf16[256,2048]{1,0:T(8,128)(2,1)S(1)}, bf16[256,2048]{1,0:T(8,128)(2,1)S(1)}, u32[]{:S(2)}, u32[]{:S(2)}) collective-permute-start(bf16[256,2048]{1,0:T(8,128)(2,1)S(1)} %pad_maximum_fusion.1.refs_0_.refs_4_), channel_id=1, source_target_pairs={{32,0},{33,1},{34,2},{35,3},{36,4},{37,5},{38,6},{39,7},{40,8},{41... | collective-permute-start | bytes 3145736 | tf_op jit(solution)/shard_map/ppermute | solution.py:45
  159.2 9.3 %collective-permute-start.20 = (bf16[128,2048]{1,0:T(8,128)(2,1)S(1)}, bf16[128,2048]{1,0:T(8,128)(2,1)S(1)}, u32[]{:S(2)}, u32[]{:S(2)}) collective-permute-start(bf16[128,2048]{1,0:T(8,128)(2,1)S(1)} %slice.247), channel_id=1, source_target_pairs={{4,0},{5,1},{6,2},{7,3},{0,4},{1,5},{2,6},{3,7},{12,8},{13,9},{14,... | collective-permute-start | bytes 1572872 | tf_op jit(solution)/shard_map/ppermute | solution.py:45
  159.7 9.4 %collective-permute-start.23 = (bf16[128,2048]{1,0:T(8,128)(2,1)S(1)}, bf16[128,2048]{1,0:T(8,128)(2,1)S(1)}, u32[]{:S(2)}, u32[]{:S(2)}) collective-permute-start(bf16[128,2048]{1,0:T(8,128)(2,1)S(1)} %slice.246), channel_id=1, source_target_pairs={{1,0},{0,1},{3,2},{2,3},{5,4},{4,5},{7,6},{6,7},{9,8},{8,9},{11,10... | collective-permute-start | bytes 1572872 | tf_op jit(solution)/shard_map/ppermute | solution.py:45
  169.2 9.2 %collective-permute-start.26 = (bf16[256,2048]{1,0:T(8,128)(2,1)S(1)}, bf16[256,2048]{1,0:T(8,128)(2,1)S(1)}, u32[]{:S(2)}, u32[]{:S(2)}) collective-permute-start(bf16[256,2048]{1,0:T(8,128)(2,1)S(1)} %collective-permute-done.22.refs_1_.refs_5_), channel_id=1, source_target_pairs={{16,0},{17,1},{18,2},{19,3},{20,4},{21,5},{22,6},{23,7},{24,8},{25... | collective-permute-start | bytes 3145736 | tf_op jit(solution)/shard_map/ppermute | solution.py:45
  169.2 9.2 %collective-permute-start.25 = (bf16[256,2048]{1,0:T(8,128)(2,1)S(1)}, bf16[256,2048]{1,0:T(8,128)(2,1)S(1)}, u32[]{:S(2)}, u32[]{:S(2)}) collective-permute-start(bf16[256,2048]{1,0:T(8,128)(2,1)S(1)} %pad_maximum_fusion.1.refs_0_.refs_4_), channel_id=1, source_target_pairs={{16,0},{17,1},{18,2},{19,3},{20,4},{21,5},{22,6},{23,7},{24,8},{25... | collective-permute-start | bytes 3145736 | tf_op jit(solution)/shard_map/ppermute | solution.py:45
  174.0 17.3 %collective-permute-start.24 = (bf16[256,2048]{1,0:T(8,128)(2,1)S(1)}, bf16[256,2048]{1,0:T(8,128)(2,1)S(1)}, u32[]{:S(2)}, u32[]{:S(2)}) collective-permute-start(bf16[256,2048]{1,0:T(8,128)(2,1)S(1)} %get-tuple-element.78), channel_id=1, source_target_pairs={{12,0},{13,1},{14,2},{15,3},{8,4},{9,5},{10,6},{11,7},{4,8},{5,9},... | collective-permute-start | bytes 3145736 | tf_op jit(solution)/shard_map/ppermute | solution.py:45
  182.7 15.1 %collective-permute-start.27 = (bf16[256,2048]{1,0:T(8,128)(2,1)S(1)}, bf16[256,2048]{1,0:T(8,128)(2,1)S(1)}, u32[]{:S(2)}, u32[]{:S(2)}) collective-permute-start(bf16[256,2048]{1,0:T(8,128)(2,1)S(1)} %get-tuple-element.82), channel_id=1, source_target_pairs={{3,0},{2,1},{1,2},{0,3},{7,4},{6,5},{5,6},{4,7},{11,8},{10,9},{9,1... | collective-permute-start | bytes 3145736 | tf_op jit(solution)/shard_map/ppermute | solution.py:45
  198.2 13.0 %collective-permute-start.28 = (bf16[128,2048]{1,0:T(8,128)(2,1)S(1)}, bf16[128,2048]{1,0:T(8,128)(2,1)S(1)}, u32[]{:S(2)}, u32[]{:S(2)}) collective-permute-start(bf16[128,2048]{1,0:T(8,128)(2,1)S(1)} %slice.245), channel_id=1, source_target_pairs={{4,0},{5,1},{6,2},{7,3},{0,4},{1,5},{2,6},{3,7},{12,8},{13,9},{14,... | collective-permute-start | bytes 1572872 | tf_op jit(solution)/shard_map/ppermute | solution.py:45
  200.1 12.5 %collective-permute-start.29 = (bf16[128,2048]{1,0:T(8,128)(2,1)S(1)}, bf16[128,2048]{1,0:T(8,128)(2,1)S(1)}, u32[]{:S(2)}, u32[]{:S(2)}) collective-permute-start(bf16[128,2048]{1,0:T(8,128)(2,1)S(1)} %slice.244), channel_id=1, source_target_pairs={{1,0},{0,1},{3,2},{2,3},{5,4},{4,5},{7,6},{6,7},{9,8},{8,9},{11,10... | collective-permute-start | bytes 1572872 | tf_op jit(solution)/shard_map/ppermute | solution.py:45
  213.1 9.3 %collective-permute-start.30 = (bf16[128,2048]{1,0:T(8,128)(2,1)S(1)}, bf16[128,2048]{1,0:T(8,128)(2,1)S(1)}, u32[]{:S(2)}, u32[]{:S(2)}) collective-permute-start(bf16[128,2048]{1,0:T(8,128)(2,1)S(1)} %pad_maximum_fusion.2), channel_id=1, source_target_pairs={{3,0},{2,1},{1,2},{0,3},{7,4},{6,5},{5,6},{4,7},{11,8},{10,9},{9,1... | collective-permute-start | bytes 1572872 | tf_op jit(solution)/shard_map/ppermute | solution.py:45
  213.2 11.7 %collective-permute-start.31 = (bf16[128,2048]{1,0:T(8,128)(2,1)S(1)}, bf16[128,2048]{1,0:T(8,128)(2,1)S(1)}, u32[]{:S(2)}, u32[]{:S(2)}) collective-permute-start(bf16[128,2048]{1,0:T(8,128)(2,1)S(1)} %pad_maximum_fusion.3), channel_id=1, source_target_pairs={{12,0},{13,1},{14,2},{15,3},{8,4},{9,5},{10,6},{11,7},{4,8},{5,9},... | collective-permute-start | bytes 1572872 | tf_op jit(solution)/shard_map/ppermute | solution.py:45
  225.7 7.5 %collective-permute-start.32 = (bf16[64,2048]{1,0:T(8,128)(2,1)}, bf16[64,2048]{1,0:T(8,128)(2,1)}, u32[]{:S(2)}, u32[]{:S(2)}) collective-permute-start(bf16[64,2048]{1,0:T(8,128)(2,1)} %fusion.15), channel_id=1, source_target_pairs={{1,0},{0,1},{3,2},{2,3},{5,4},{4,5},{7,6},{6,7},{9,8},{8,9},{11,10... | collective-permute-start | bytes 786440 | tf_op jit(solution)/shard_map/ppermute | solution.py:45
  228.8 6.6 %collective-permute-start.33 = (bf16[64,2048]{1,0:T(8,128)(2,1)S(1)}, bf16[64,2048]{1,0:T(8,128)(2,1)}, u32[]{:S(2)}, u32[]{:S(2)}) collective-permute-start(bf16[64,2048]{1,0:T(8,128)(2,1)S(1)} %fusion.12), channel_id=1, source_target_pairs={{4,0},{5,1},{6,2},{7,3},{0,4},{1,5},{2,6},{3,7},{12,8},{13,9},{14,... | collective-permute-start | bytes 786440 | tf_op jit(solution)/shard_map/ppermute | solution.py:45

commit v9 on v8

--- a/solution.py
+++ b/solution.py
@@ -135,13 +135,13 @@
     return whole(join_kernel, place, [a, b], [(2 * a.shape[0], a.shape[1])])[0]
 
 
-def assemble_kernel(keep, place_ref, a_ref, b_ref, c_ref, out_ref):
+def assemble_kernel(keep, place_ref, a_ref, b_ref, c_ref, *out_refs):
     rows = a_ref.shape[0]
     part = rows // PARTS
 
     def put(i, ref, first):
-        for j in range(PARTS):
-            at = pl.multiple_of((j * RING + slot_of(keep, place_ref, i)) * part, part)
+        at = pl.multiple_of(slot_of(keep, place_ref, i) * part, part)
+        for j, out_ref in enumerate(out_refs):
             out_ref[pl.ds(at, part), :] = ref[first + j * part:first + (j + 1) * part, :]
 
     put(0, a_ref, 0)
@@ -153,18 +153,7 @@
 def assemble(keep, place, a, b, c):
     rows, wide = a.shape
     kernel = functools.partial(assemble_kernel, keep)
-    return whole(kernel, place, [a, b, c], [(RING * rows, wide)])[0]
-
-
-def regroup_kernel(place_ref, own_ref, near_ref, a_ref, b_ref):
-    half = own_ref.shape[0] // 2
-    for i, out_ref in enumerate((a_ref, b_ref)):
-        out_ref[:half, :] = own_ref[i * half:(i + 1) * half, :]
-        out_ref[half:, :] = near_ref[i * half:(i + 1) * half, :]
-
-
-def regroup(place, own, near):
-    return whole(regroup_kernel, place, [own, near], [own.shape] * 2)
+    return whole(kernel, place, [a, b, c], [(RING * rows // PARTS, wide)] * PARTS)
 
 
 def order_of(keep):
@@ -321,14 +310,14 @@
     w_out = lax.dynamic_slice_in_dim(weight_out, dp * inner, inner, 0)
 
     order = (False, True)
-    start, one, two, own, near_a, near_b = {}, {}, {}, {}, {}, {}
+    start, one, two, own_a, own_b = {}, {}, {}, {}, {}
     start[True], start[False] = cut(place, tokens, out_grad)
     for keep in order:
         one[keep] = exchange(start[keep], along(keep, True, 0))
     for keep in order:
         two[keep] = exchange(join(place, start[keep], one[keep]), along(keep, True, 1))
     for keep in order:
-        own[keep] = assemble(keep, place, start[keep], one[keep], two[keep])
+        own_a[keep], own_b[keep] = assemble(keep, place, start[keep], one[keep], two[keep])
 
     def others(near):
         return {keep: exchange(near[keep], along(keep, False, 1)) for keep in order}
@@ -358,21 +347,27 @@
         activated, slope = gelu_parts(pre)
         return jnp.concatenate([activated.astype(BF), (back * slope).astype(BF)], axis=1)
 
-    both = lax.optimization_barrier((own[True], own[False]))
-    own = {True: both[0], False: both[1]}
-    near = {keep: exchange(own[keep], along(keep, False, 0)) for keep in order}
-    for keep in order:
-        near_a[keep], near_b[keep] = regroup(place, own[keep], near[keep])
+    def neighbours(own):
+        return {keep: exchange(own[keep], along(keep, False, 0)) for keep in order}
+
+    def joined(own, near):
+        return {keep: join(place, own[keep], near[keep]) for keep in order}
+
+    both = lax.optimization_barrier((own_a[True], own_a[False]))
+    own_a = {True: both[0], False: both[1]}
+    near_a = joined(own_a, neighbours(own_a))
     rest_a = others(near_a)
-    rest_b = others(near_b)
+    near_of_b = neighbours(own_b)
     sent_a = panel_dot(False, near_a, rest_a, rest_a[True])
     kept_a, send_a = panel_dot(True, near_a, rest_a, more=exchange(sent_a, other_core))
-    sent_b = panel_dot(False, near_b, rest_b, rest_b[True], send_a)
-    step_a = after(exchange(send_a, along_z(0)), sent_b)
+    near_b = joined(own_b, {keep: after(near_of_b[keep], send_a) for keep in order})
+    rest_b = others(near_b)
+    step_a = after(exchange(send_a, along_z(0)), rest_b[True], rest_b[False])
+    sent_b = panel_dot(False, near_b, rest_b, step_a)
     half_a = half_sum(kept_a, step_a)
     turn_a = exchange(half_a, along_z(1))
     kept_b, send_b = panel_dot(
-        True, near_b, rest_b, step_a, more=exchange(sent_b, other_core)
+        True, near_b, rest_b, more=exchange(sent_b, other_core)
     )
     pair_a = hidden_of(half_a, after(turn_a, send_b))
     step_b = exchange(after(send_b, turn_a), along_z(0))
@@ -430,7 +425,7 @@
     hid_b = {True: (pair_b, far_b)}
     hid_b[False] = (exchange(pair_b, other_core), exchange(far_b, other_core))
 
-    out_b[True] = out_dot(True, hid_b[True])
+    out_b[True] = out_dot(True, hid_b[True], hid_b[False][0])
     out_b[False] = out_dot(False, hid_b[False], out_b[True][0])
     for keep in both_ways:
         got_b[keep] = exchange(out_b[keep][1], along(keep, True, 1))

time: 240 us -> 237 us (0.988)
  waiting for transfers between devices: 109 us -> 104 us
    ppermute x34 -> x36, waiting for transfers between devices: 109 us -> 104 us  [exchange(): return lax.ppermute(array, AXES, pairs)]
    ppermute x34 -> x36, starting transfers between devices: 47.5 us -> 48.5 us  [exchange(): return lax.ppermute(array, AXES, pairs)]
    pallas_call x7 -> x9, Pallas kernels: 5.35 us -> 5.4 us  [whole(): pl.pallas_call(kernel, in_specs=[pl.BlockSpec(memory_space=pltpu.SMEM)] +...]
  transfers between devices with their start and end apart: 34 -> 36, of which waited for: 24 -> 24; matrix products, arithmetic and copies ran while one was open for 3% -> 3% of each run, Pallas kernels for 25% -> 23%
where the time goes in v9:
time: 237 us; the launch traced here: 234 us
  waiting for transfers between devices  104 us (44%)
  Pallas kernels  65 us (27%)
  starting transfers between devices  48.5 us (20%)
  other arithmetic  8.66 us (4%)
  local copies, waits for them, and re-layouts  6.83 us (3%)
    ppermute x36, waiting for transfers between devices, exchange(): return lax.ppermute(array, AXES, pairs)  104 us
    ppermute x36, starting transfers between devices, exchange(): return lax.ppermute(array, AXES, pairs)  48.5 us
    pallas_call x8, Pallas kernels, pair_dot(): pl.pallas_call(functools.partial(pair_kernel, keep, hidden, more is not N...  35.5 us
    pallas_call x4, Pallas kernels, grad_dot(): pl.pallas_call(functools.partial(grad_kernel, pairs, block, factor, begun...  24.1 us
    pallas_call x9, Pallas kernels, whole(): pl.pallas_call(kernel, in_specs=[pl.BlockSpec(memory_space=pltpu.SMEM)] +...  5.4 us
  transfers between devices with their start and end apart: 36, of which 24 were waited for; matrix products, arithmetic and copies ran while one was open for 3% of the time, Pallas kernels for 23%

profile of v9, /device:TPU:8, one launch (start us, length us, event | category | flops | bytes accessed | tf_op | source)
XLA Modules:
  0.0 233.9 jit_solution(1936327075169439930)
XLA Ops:
  3.2 1.6 collective-permute-start
  5.2 4.4 %collective-permute-done.b_ref = bf16[64,2048]{1,0:T(8,128)(2,1)S(1)} collective-permute-done((bf16[64,2048]{1,0:T(8,128)(2,1)S(1)}, bf16[64,2048]{1,0:T(8,128)(2,1)S(1)}, u32[]{:S(2)}, u32[]{:S(2)}) %collective-permute-start) | collective-permute-done | bytes 262176 | tf_op jit(solution)/shard_map/ppermute | solution.py:45
  10.2 2.8 %collective-permute-start.1 = (bf16[128,2048]{1,0:T(8,128)(2,1)S(1)}, bf16[128,2048]{1,0:T(8,128)(2,1)S(1)}, u32[]{:S(2)}, u32[]{:S(2)}) collective-permute-start(bf16[128,2048]{1,0:T(8,128)(2,1)S(1)} %shard_map.76), channel_id=1, source_target_pairs={{12,0},{13,1},{14,2},{15,3},{8,4},{9,5},{10,6},{11,7},{4,8},{5,9},... | collective-permute-start | bytes 1572872 | tf_op jit(solution)/shard_map/ppermute | solution.py:45
  13.7 1.7 collective-permute-start.3
  15.3 5.4 %collective-permute-done.1.c_ref = bf16[128,2048]{1,0:T(8,128)(2,1)S(1)} collective-permute-done((bf16[128,2048]{1,0:T(8,128)(2,1)S(1)}, bf16[128,2048]{1,0:T(8,128)(2,1)S(1)}, u32[]{:S(2)}, u32[]{:S(2)}) %collective-permute-start.1) | collective-permute-done | bytes 524320 | tf_op jit(solution)/shard_map/ppermute | solution.py:45
  24.6 1.7 collective-permute-start.4
  26.2 7.3 %collective-permute-done.6.b_ref = bf16[128,2048]{1,0:T(8,128)(2,1)S(1)} collective-permute-done((bf16[128,2048]{1,0:T(8,128)(2,1)S(1)}, bf16[128,2048]{1,0:T(8,128)(2,1)S(1)}, u32[]{:S(2)}, u32[]{:S(2)}) %collective-permute-start.6) | collective-permute-done | bytes 524320 | tf_op jit(solution)/shard_map/ppermute | solution.py:45
  34.2 2.0 collective-permute-start.7
  36.8 1.7 collective-permute-start.5
  38.5 2.7 %constant_dynamic-slice_fusion = (bf16[1024,1024]{1,0:T(8,128)(2,1)S(1)}, bf16[1024,1024]{1,0:T(8,128)(2,1)S(1)}) fusion(bf16[2048,1024]{1,0:T(8,128)(2,1)} %param.7, s32[]{:T(128)S(6)} %select_n.30, bf16[1024,2048]{1,0:T(8,128)(2,1)} %param.6), kind=kLoop, calls=%fused_computation.55 | loop fusion | bytes 8388612 | tf_op jit(solution)/shard_map/dynamic_slice | solution.py:310
  41.2 9.1 %collective-permute-done.7.refs_1_.refs_3_.refs_7_ = bf16[256,2048]{1,0:T(8,128)(2,1)S(1)} collective-permute-done((bf16[256,2048]{1,0:T(8,128)(2,1)S(1)}, bf16[256,2048]{1,0:T(8,128)(2,1)S(1)}, u32[]{:S(2)}, u32[]{:S(2)}) %collective-permute-start.7) | collective-permute-done | bytes 1048608 | tf_op jit(solution)/shard_map/ppermute | solution.py:45
  50.2 1.6 collective-permute-done.5.refs_1_.refs_5_
  51.8 4.3 %shard_map.82 = bf16[512,2048]{1,0:T(8,128)(2,1)S(1)} custom-call(s32[2]{0:T(128)S(1)} %pad_add_fusion.place_ref, bf16[256,2048]{1,0:T(8,128)(2,1)S(1)} %shard_map.81.refs_0_.refs_2_.refs_6_, bf16[256,2048]{1,0:T(8,128)(2,1)S(1)} %collective-permute-done.7.refs_1_.refs_3_.refs_7_, bf16[1024,1024]{1,0:T(8,128)(2,1)S(1)} %get-tuple-element.132.refs_2_.refs_3_, ...), custom_call_target="tpu_custom_call" | custom-call | flops 2147483 | bytes 8388 | tf_op jit(solution)/shard_map/pallas_call | solution.py:229
  56.7 3.0 %collective-permute-start.10 = (bf16[128,2048]{1,0:T(8,128)(2,1)S(1)}, bf16[128,2048]{1,0:T(8,128)(2,1)S(1)}, u32[]{:S(2)}, u32[]{:S(2)}) collective-permute-start(bf16[128,2048]{1,0:T(8,128)(2,1)S(1)} %copy-done.1), channel_id=1, source_target_pairs={{1,0},{0,1},{3,2},{2,3},{5,4},{4,5},{7,6},{6,7},{9,8},{8,9},{11,10... | collective-permute-start | bytes 1572872 | tf_op jit(solution)/shard_map/ppermute | solution.py:45
  60.3 5.3 %shard_map.83 = (bf16[256,2048]{1,0:T(8,128)(2,1)S(1)}, bf16[256,2048]{1,0:T(8,128)(2,1)S(1)}) custom-call(s32[2]{0:T(128)S(1)} %pad_add_fusion.place_ref, bf16[256,2048]{1,0:T(8,128)(2,1)S(1)} %shard_map.80.refs_0_.refs_4_, bf16[256,2048]{1,0:T(8,128)(2,1)} %collective-permute-done.5.refs_1_.refs_5_, ...), custom_call_target="tpu_custom_call" | custom-call | flops 2147483 | bytes 8388 | tf_op jit(solution)/shard_map/pallas_call | solution.py:229
  67.4 2.6 %collective-permute-start.11 = (bf16[256,2048]{1,0:T(8,128)(2,1)S(1)}, bf16[256,2048]{1,0:T(8,128)(2,1)S(1)}, u32[]{:S(2)}, u32[]{:S(2)}) collective-permute-start(bf16[256,2048]{1,0:T(8,128)(2,1)S(1)} %shard_map.84.refs_0_.refs_4_), channel_id=1, source_target_pairs={{3,0},{2,1},{1,2},{0,3},{7,4},{6,5},{5,6},{4,7},{11,8},{10,9},{9,1... | collective-permute-start | bytes 3145736 | tf_op jit(solution)/shard_map/ppermute | solution.py:45
  70.8 1.9 collective-permute-start.9
  72.7 10.1 %collective-permute-done.11.refs_1_.refs_5_ = bf16[256,2048]{1,0:T(8,128)(2,1)S(1)} collective-permute-done((bf16[256,2048]{1,0:T(8,128)(2,1)S(1)}, bf16[256,2048]{1,0:T(8,128)(2,1)S(1)}, u32[]{:S(2)}, u32[]{:S(2)}) %collective-permute-start.11) | collective-permute-done | bytes 1048608 | tf_op jit(solution)/shard_map/ppermute | solution.py:45
  82.8 3.2 %collective-permute-done.13.refs_1_.refs_3_.refs_7_ = bf16[256,2048]{1,0:T(8,128)(2,1)S(1)} collective-permute-done((bf16[256,2048]{1,0:T(8,128)(2,1)S(1)}, bf16[256,2048]{1,0:T(8,128)(2,1)S(1)}, u32[]{:S(2)}, u32[]{:S(2)}) %collective-permute-start.13) | collective-permute-done | bytes 1048608 | tf_op jit(solution)/shard_map/ppermute | solution.py:45
  86.1 4.3 %shard_map.86 = bf16[512,2048]{1,0:T(8,128)(2,1)S(1)} custom-call(s32[2]{0:T(128)S(1)} %pad_add_fusion.place_ref, bf16[256,2048]{1,0:T(8,128)(2,1)S(1)} %shard_map.85.refs_0_.refs_2_.refs_6_, bf16[256,2048]{1,0:T(8,128)(2,1)S(1)} %collective-permute-done.13.refs_1_.refs_3_.refs_7_, bf16[1024,1024]{1,0:T(8,128)(2,1)S(1)} %get-tuple-element.132.refs_2_.refs_3_, ...), custom_call_target="tpu_custom_call" | custom-call | flops 2147483 | bytes 8388 | tf_op jit(solution)/shard_map/pallas_call | solution.py:229
  91.8 3.4 %collective-permute-start.14 = (bf16[256,2048]{1,0:T(8,128)(2,1)S(1)}, bf16[256,2048]{1,0:T(8,128)(2,1)S(1)}, u32[]{:S(2)}, u32[]{:S(2)}) collective-permute-start(bf16[256,2048]{1,0:T(8,128)(2,1)S(1)} %add_convert_fusion.1), channel_id=1, source_target_pairs={{96,0},{97,1},{98,2},{99,3},{100,4},{101,5},{102,6},{103,7},{104,8... | collective-permute-start | bytes 3145736 | tf_op jit(solution)/shard_map/ppermute | solution.py:45
  95.2 4.5 %shard_map.87 = (bf16[256,2048]{1,0:T(8,128)(2,1)S(1)}, bf16[256,2048]{1,0:T(8,128)(2,1)S(1)}) custom-call(s32[2]{0:T(128)S(1)} %pad_add_fusion.place_ref, bf16[256,2048]{1,0:T(8,128)(2,1)S(1)} %shard_map.84.refs_0_.refs_4_, bf16[256,2048]{1,0:T(8,128)(2,1)S(1)} %collective-permute-done.11.refs_1_.refs_5_, ...), custom_call_target="tpu_custom_call" | custom-call | flops 2147483 | bytes 8388 | tf_op jit(solution)/shard_map/pallas_call | solution.py:229
  99.7 8.4 %collective-permute-done.14 = bf16[256,2048]{1,0:T(8,128)(2,1)S(1)} collective-permute-done((bf16[256,2048]{1,0:T(8,128)(2,1)S(1)}, bf16[256,2048]{1,0:T(8,128)(2,1)S(1)}, u32[]{:S(2)}, u32[]{:S(2)}) %collective-permute-start.14) | collective-permute-done | bytes 1048608 | tf_op jit(solution)/shard_map/ppermute | solution.py:45
  109.2 2.0 collective-permute-start.20
  111.2 12.8 %collective-permute-done.16.refs_1_.refs_5_ = bf16[256,2048]{1,0:T(8,128)(2,1)S(1)} collective-permute-done((bf16[256,2048]{1,0:T(8,128)(2,1)S(1)}, bf16[256,2048]{1,0:T(8,128)(2,1)S(1)}, u32[]{:S(2)}, u32[]{:S(2)}) %collective-permute-start.16) | collective-permute-done | bytes 1048608 | tf_op jit(solution)/shard_map/ppermute | solution.py:45
  124.0 4.3 %shard_map.88 = (bf16[256,2048]{1,0:T(8,128)(2,1)S(1)}, bf16[256,2048]{1,0:T(8,128)(2,1)S(1)}) custom-call(s32[2]{0:T(128)S(1)} %pad_add_fusion.place_ref, bf16[256,2048]{1,0:T(8,128)(2,1)S(1)} %pad_maximum_fusion.refs_0_.refs_4_, bf16[256,2048]{1,0:T(8,128)(2,1)S(1)} %collective-permute-done.16.refs_1_.refs_5_, ...), custom_call_target="tpu_custom_call" | custom-call | flops 2147483 | bytes 8388 | tf_op jit(solution)/shard_map/pallas_call | solution.py:229
  128.3 6.9 %collective-permute-done.20 = bf16[256,2048]{1,0:T(8,128)(2,1)S(1)} collective-permute-done((bf16[256,2048]{1,0:T(8,128)(2,1)S(1)}, bf16[256,2048]{1,0:T(8,128)(2,1)S(1)}, u32[]{:S(2)}, u32[]{:S(2)}) %collective-permute-start.20) | collective-permute-done | bytes 1048608 | tf_op jit(solution)/shard_map/ppermute | solution.py:45
  135.6 3.3 %collective-permute-start.23 = (bf16[256,2048]{1,0:T(8,128)(2,1)S(1)}, bf16[256,2048]{1,0:T(8,128)(2,1)S(1)}, u32[]{:S(2)}, u32[]{:S(2)}) collective-permute-start(bf16[256,2048]{1,0:T(8,128)(2,1)S(1)} %add_convert_fusion), channel_id=1, source_target_pairs={{96,0},{97,1},{98,2},{99,3},{100,4},{101,5},{102,6},{103,7},{104,8... | collective-permute-start | bytes 3145736 | tf_op jit(solution)/shard_map/ppermute | solution.py:45
  138.9 2.0 collective-permute-start.17
  140.9 4.3 %shard_map.89 = (bf16[256,2048]{1,0:T(8,128)(2,1)S(1)}, bf16[256,2048]{1,0:T(8,128)(2,1)S(1)}) custom-call(s32[2]{0:T(128)S(1)} %pad_add_fusion.place_ref, bf16[256,2048]{1,0:T(8,128)(2,1)S(1)} %collective-permute-done.18.refs_0_.refs_6_.refs_2_, bf16[256,2048]{1,0:T(8,128)(2,1)S(1)} %collective-permute-done.19.refs_1_.refs_7_.refs_3_, ...), custom_call_target="tpu_custom_call" | custom-call | flops 2147483 | bytes 8388 | tf_op jit(solution)/shard_map/pallas_call | solution.py:229
  145.6 5.6 %shard_map.90.refs_8_ = f32[1024,1024]{1,0:T(8,128)} custom-call(bf16[256,2048]{1,0:T(8,128)(2,1)S(1)} %shard_map.80.refs_0_.refs_4_, bf16[256,2048]{1,0:T(8,128)(2,1)} %collective-permute-done.5.refs_1_.refs_5_, bf16[256,2048]{1,0:T(8,128)(2,1)S(1)} %shard_map.81.refs_0_.refs_2_.refs_6_, ...), custom_call_target="tpu_custom_call" | custom-call | flops 2147483 | bytes 5242 | tf_op jit(solution)/shard_map/pallas_call | solution.py:278
  153.0 1.9 collective-permute-done.17
  154.9 5.2 %collective-permute-done.21 = bf16[256,2048]{1,0:T(8,128)(2,1)S(1)} collective-permute-done((bf16[256,2048]{1,0:T(8,128)(2,1)S(1)}, bf16[256,2048]{1,0:T(8,128)(2,1)S(1)}, u32[]{:S(2)}, u32[]{:S(2)}) %collective-permute-start.21) | collective-permute-done | bytes 1048608 | tf_op jit(solution)/shard_map/ppermute | solution.py:45
  162.3 3.0 %collective-permute-start.25 = (bf16[128,2048]{1,0:T(8,128)(2,1)S(1)}, bf16[128,2048]{1,0:T(8,128)(2,1)S(1)}, u32[]{:S(2)}, u32[]{:S(2)}) collective-permute-start(bf16[128,2048]{1,0:T(8,128)(2,1)S(1)} %slice.246), channel_id=1, source_target_pairs={{1,0},{0,1},{3,2},{2,3},{5,4},{4,5},{7,6},{6,7},{9,8},{8,9},{11,10... | collective-permute-start | bytes 1572872 | tf_op jit(solution)/shard_map/ppermute | solution.py:45
  165.3 5.5 %shard_map.91.refs_8_ = f32[1024,1024]{1,0:T(8,128)} custom-call(bf16[256,2048]{1,0:T(8,128)(2,1)S(1)} %pad_maximum_fusion.refs_0_.refs_4_, bf16[256,2048]{1,0:T(8,128)(2,1)S(1)} %collective-permute-done.16.refs_1_.refs_5_, bf16[256,2048]{1,0:T(8,128)(2,1)S(1)} %collective-permute-done.18.refs_0_.refs_6_.refs_2_, ...), custom_call_target="tpu_custom_call" | custom-call | flops 2147483 | bytes 5242 | tf_op jit(solution)/shard_map/pallas_call | solution.py:278
  170.8 1.6 collective-permute-done.25
  172.5 4.3 %shard_map.92 = (bf16[256,2048]{1,0:T(8,128)(2,1)S(1)}, bf16[256,2048]{1,0:T(8,128)(2,1)S(1)}) custom-call(s32[2]{0:T(128)S(1)} %pad_add_fusion.place_ref, bf16[256,2048]{1,0:T(8,128)(2,1)S(1)} %pad_maximum_fusion.1.refs_0_.refs_4_, bf16[256,2048]{1,0:T(8,128)(2,1)S(1)} %collective-permute-done.24.refs_1_.refs_5_, ...), custom_call_target="tpu_custom_call" | custom-call | flops 2147483 | bytes 8388 | tf_op jit(solution)/shard_map/pallas_call | solution.py:229
  178.2 4.3 %shard_map.93 = (bf16[256,2048]{1,0:T(8,128)(2,1)S(1)}, bf16[256,2048]{1,0:T(8,128)(2,1)S(1)}) custom-call(s32[2]{0:T(128)S(1)} %pad_add_fusion.place_ref, bf16[256,2048]{1,0:T(8,128)(2,1)S(1)} %collective-permute-done.26.refs_0_.refs_6_.refs_2_, bf16[256,2048]{1,0:T(8,128)(2,1)S(1)} %collective-permute-done.28.refs_1_.refs_7_.refs_3_, ...), custom_call_target="tpu_custom_call" | custom-call | flops 2147483 | bytes 8388 | tf_op jit(solution)/shard_map/pallas_call | solution.py:229
  182.9 6.5 %shard_map.94 = f32[1024,1024]{1,0:T(8,128)} custom-call(bf16[256,2048]{1,0:T(8,128)(2,1)S(1)} %shard_map.84.refs_0_.refs_4_, bf16[256,2048]{1,0:T(8,128)(2,1)S(1)} %collective-permute-done.11.refs_1_.refs_5_, bf16[256,2048]{1,0:T(8,128)(2,1)S(1)} %shard_map.85.refs_0_.refs_2_.refs_6_, ...), custom_call_target="tpu_custom_call", output_to_operand_aliasing={{}: (8, {})} | custom-call | flops 2147483 | bytes 5242 | tf_op jit(solution)/shard_map/pallas_call | solution.py:278
  189.4 3.5 %collective-permute-done.27 = bf16[256,2048]{1,0:T(8,128)(2,1)S(1)} collective-permute-done((bf16[256,2048]{1,0:T(8,128)(2,1)S(1)}, bf16[256,2048]{1,0:T(8,128)(2,1)S(1)}, u32[]{:S(2)}, u32[]{:S(2)}) %collective-permute-start.27) | collective-permute-done | bytes 1048608 | tf_op jit(solution)/shard_map/ppermute | solution.py:45
  192.9 4.5 %collective-permute-done.29 = bf16[256,2048]{1,0:T(8,128)(2,1)S(1)} collective-permute-done((bf16[256,2048]{1,0:T(8,128)(2,1)S(1)}, bf16[256,2048]{1,0:T(8,128)(2,1)S(1)}, u32[]{:S(2)}, u32[]{:S(2)}) %collective-permute-start.29) | collective-permute-done | bytes 1048608 | tf_op jit(solution)/shard_map/ppermute | solution.py:45
  199.7 3.3 %collective-permute-start.31 = (bf16[128,2048]{1,0:T(8,128)(2,1)S(1)}, bf16[128,2048]{1,0:T(8,128)(2,1)S(1)}, u32[]{:S(2)}, u32[]{:S(2)}) collective-permute-start(bf16[128,2048]{1,0:T(8,128)(2,1)S(1)} %slice.244), channel_id=1, source_target_pairs={{1,0},{0,1},{3,2},{2,3},{5,4},{4,5},{7,6},{6,7},{9,8},{8,9},{11,10... | collective-permute-start | bytes 1572872 | tf_op jit(solution)/shard_map/ppermute | solution.py:45
  203.1 6.5 %shard_map.95 = f32[1024,1024]{1,0:T(8,128)} custom-call(bf16[256,2048]{1,0:T(8,128)(2,1)S(1)} %pad_maximum_fusion.1.refs_0_.refs_4_, bf16[256,2048]{1,0:T(8,128)(2,1)S(1)} %collective-permute-done.24.refs_1_.refs_5_, bf16[256,2048]{1,0:T(8,128)(2,1)S(1)} %collective-permute-done.26.refs_0_.refs_6_.refs_2_, ...), custom_call_target="tpu_custom_call", output_to_operand_aliasing={{}: (8, {})} | custom-call | flops 2147483 | bytes 5242 | tf_op jit(solution)/shard_map/pallas_call | solution.py:278
  210.8 2.2 collective-permute-start.33
  213.1 6.9 %collective-permute-done.32 = bf16[128,2048]{1,0:T(8,128)(2,1)S(1)} collective-permute-done((bf16[128,2048]{1,0:T(8,128)(2,1)S(1)}, bf16[128,2048]{1,0:T(8,128)(2,1)S(1)}, u32[]{:S(2)}, u32[]{:S(2)}) %collective-permute-start.32) | collective-permute-done | bytes 524320 | tf_op jit(solution)/shard_map/ppermute | solution.py:45
  222.1 2.2 collective-permute-start.34
  225.5 3.4 %collective-permute-done.34 = bf16[64,2048]{1,0:T(8,128)(2,1)S(1)} collective-permute-done((bf16[64,2048]{1,0:T(8,128)(2,1)}, bf16[64,2048]{1,0:T(8,128)(2,1)S(1)}, u32[]{:S(2)}, u32[]{:S(2)}) %collective-permute-start.34) | collective-permute-done | bytes 262176 | tf_op jit(solution)/shard_map/ppermute | solution.py:45
  228.9 3.0 %collective-permute-done.35 = bf16[64,2048]{1,0:T(8,128)(2,1)} collective-permute-done((bf16[64,2048]{1,0:T(8,128)(2,1)}, bf16[64,2048]{1,0:T(8,128)(2,1)}, u32[]{:S(2)}, u32[]{:S(2)}) %collective-permute-start.35) | collective-permute-done | bytes 262176 | tf_op jit(solution)/shard_map/ppermute | solution.py:45
  (98 shorter events, 30.9 us)
Async XLA Ops:
  0.7 1.0 copy-start.4
  1.7 0.9 copy-start.5
  3.2 6.5 %collective-permute-start = (bf16[64,2048]{1,0:T(8,128)(2,1)S(1)}, bf16[64,2048]{1,0:T(8,128)(2,1)S(1)}, u32[]{:S(2)}, u32[]{:S(2)}) collective-permute-start(bf16[64,2048]{1,0:T(8,128)(2,1)S(1)} %get-tuple-element.49.a_ref), channel_id=1, source_target_pairs={{4,0},{5,1},{6,2},{7,3},{0,4},{1,5},{2,6},{3,7},{12,8},{13,9},{14,... | collective-permute-start | bytes 786440 | tf_op jit(solution)/shard_map/ppermute | solution.py:45
  4.8 8.3 %collective-permute-start.2 = (bf16[64,2048]{1,0:T(8,128)(2,1)S(1)}, bf16[64,2048]{1,0:T(8,128)(2,1)S(1)}, u32[]{:S(2)}, u32[]{:S(2)}) collective-permute-start(bf16[64,2048]{1,0:T(8,128)(2,1)S(1)} %get-tuple-element.51.a_ref), channel_id=1, source_target_pairs={{1,0},{0,1},{3,2},{2,3},{5,4},{4,5},{7,6},{6,7},{9,8},{8,9},{11,10... | collective-permute-start | bytes 786440 | tf_op jit(solution)/shard_map/ppermute | solution.py:45
  10.2 10.5 %collective-permute-start.1 = (bf16[128,2048]{1,0:T(8,128)(2,1)S(1)}, bf16[128,2048]{1,0:T(8,128)(2,1)S(1)}, u32[]{:S(2)}, u32[]{:S(2)}) collective-permute-start(bf16[128,2048]{1,0:T(8,128)(2,1)S(1)} %shard_map.76), channel_id=1, source_target_pairs={{12,0},{13,1},{14,2},{15,3},{8,4},{9,5},{10,6},{11,7},{4,8},{5,9},... | collective-permute-start | bytes 1572872 | tf_op jit(solution)/shard_map/ppermute | solution.py:45
  13.7 9.3 %collective-permute-start.3 = (bf16[128,2048]{1,0:T(8,128)(2,1)S(1)}, bf16[128,2048]{1,0:T(8,128)(2,1)S(1)}, u32[]{:S(2)}, u32[]{:S(2)}) collective-permute-start(bf16[128,2048]{1,0:T(8,128)(2,1)S(1)} %shard_map.78), channel_id=1, source_target_pairs={{3,0},{2,1},{1,2},{0,3},{7,4},{6,5},{5,6},{4,7},{11,8},{10,9},{9,1... | collective-permute-start | bytes 1572872 | tf_op jit(solution)/shard_map/ppermute | solution.py:45
  21.3 0.8 copy-start
  23.6 0.8 copy-start.2
  24.4 9.2 %collective-permute-start.6 = (bf16[128,2048]{1,0:T(8,128)(2,1)S(1)}, bf16[128,2048]{1,0:T(8,128)(2,1)S(1)}, u32[]{:S(2)}, u32[]{:S(2)}) collective-permute-start(bf16[128,2048]{1,0:T(8,128)(2,1)S(1)} %get-tuple-element.54.a_ref), channel_id=1, source_target_pairs={{4,0},{5,1},{6,2},{7,3},{0,4},{1,5},{2,6},{3,7},{12,8},{13,9},{14,... | collective-permute-start | bytes 1572872 | tf_op jit(solution)/shard_map/ppermute | solution.py:45
  24.6 11.6 %collective-permute-start.4 = (bf16[128,2048]{1,0:T(8,128)(2,1)S(1)}, bf16[128,2048]{1,0:T(8,128)(2,1)S(1)}, u32[]{:S(2)}, u32[]{:S(2)}) collective-permute-start(bf16[128,2048]{1,0:T(8,128)(2,1)S(1)} %get-tuple-element.53.a_ref), channel_id=1, source_target_pairs={{1,0},{0,1},{3,2},{2,3},{5,4},{4,5},{7,6},{6,7},{9,8},{8,9},{11,10... | collective-permute-start | bytes 1572872 | tf_op jit(solution)/shard_map/ppermute | solution.py:45
  34.2 16.1 %collective-permute-start.7 = (bf16[256,2048]{1,0:T(8,128)(2,1)S(1)}, bf16[256,2048]{1,0:T(8,128)(2,1)S(1)}, u32[]{:S(2)}, u32[]{:S(2)}) collective-permute-start(bf16[256,2048]{1,0:T(8,128)(2,1)S(1)} %shard_map.81.refs_0_.refs_2_.refs_6_), channel_id=1, source_target_pairs={{12,0},{13,1},{14,2},{15,3},{8,4},{9,5},{10,6},{11,7},{4,8},{5,9},... | collective-permute-start | bytes 3145736 | tf_op jit(solution)/shard_map/ppermute | solution.py:45
  36.8 15.0 %collective-permute-start.5 = (bf16[256,2048]{1,0:T(8,128)(2,1)S(1)}, bf16[256,2048]{1,0:T(8,128)(2,1)}, u32[]{:S(2)}, u32[]{:S(2)}) collective-permute-start(bf16[256,2048]{1,0:T(8,128)(2,1)S(1)} %shard_map.80.refs_0_.refs_4_), channel_id=1, source_target_pairs={{3,0},{2,1},{1,2},{0,3},{7,4},{6,5},{5,6},{4,7},{11,8},{10,9},{9,1... | collective-permute-start | bytes 3145736 | tf_op jit(solution)/shard_map/ppermute | solution.py:45
  51.8 4.4 %copy-start.3 = (bf16[128,2048]{1,0:T(8,128)(2,1)S(1)}, bf16[128,2048]{1,0:T(8,128)(2,1)}, u32[]{:S(2)}) copy-start(bf16[128,2048]{1,0:T(8,128)(2,1)} %copy-done.2) | copy-start | bytes 1572868
  51.8 4.9 %copy-start.1 = (bf16[128,2048]{1,0:T(8,128)(2,1)S(1)}, bf16[128,2048]{1,0:T(8,128)(2,1)}, u32[]{:S(2)}) copy-start(bf16[128,2048]{1,0:T(8,128)(2,1)} %copy-done) | copy-start | bytes 1572868
  56.1 4.2 %collective-permute-start.8 = (bf16[512,2048]{1,0:T(8,128)(2,1)S(1)}, bf16[512,2048]{1,0:T(8,128)(2,1)S(1)}, u32[]{:S(2)}, u32[]{:S(2)}) collective-permute-start(bf16[512,2048]{1,0:T(8,128)(2,1)S(1)} %shard_map.82), channel_id=1, source_target_pairs={{16,0},{17,1},{18,2},{19,3},{20,4},{21,5},{22,6},{23,7},{24,8},{25... | collective-permute-start | bytes 6291464 | tf_op jit(solution)/shard_map/ppermute | solution.py:45
  56.2 9.4 %collective-permute-start.12 = (bf16[128,2048]{1,0:T(8,128)(2,1)S(1)}, bf16[128,2048]{1,0:T(8,128)(2,1)S(1)}, u32[]{:S(2)}, u32[]{:S(2)}) collective-permute-start(bf16[128,2048]{1,0:T(8,128)(2,1)S(1)} %copy-done.3), channel_id=1, source_target_pairs={{4,0},{5,1},{6,2},{7,3},{0,4},{1,5},{2,6},{3,7},{12,8},{13,9},{14,... | collective-permute-start | bytes 1572872 | tf_op jit(solution)/shard_map/ppermute | solution.py:45
  56.7 10.2 %collective-permute-start.10 = (bf16[128,2048]{1,0:T(8,128)(2,1)S(1)}, bf16[128,2048]{1,0:T(8,128)(2,1)S(1)}, u32[]{:S(2)}, u32[]{:S(2)}) collective-permute-start(bf16[128,2048]{1,0:T(8,128)(2,1)S(1)} %copy-done.1), channel_id=1, source_target_pairs={{1,0},{0,1},{3,2},{2,3},{5,4},{4,5},{7,6},{6,7},{9,8},{8,9},{11,10... | collective-permute-start | bytes 1572872 | tf_op jit(solution)/shard_map/ppermute | solution.py:45
  67.4 15.4 %collective-permute-start.11 = (bf16[256,2048]{1,0:T(8,128)(2,1)S(1)}, bf16[256,2048]{1,0:T(8,128)(2,1)S(1)}, u32[]{:S(2)}, u32[]{:S(2)}) collective-permute-start(bf16[256,2048]{1,0:T(8,128)(2,1)S(1)} %shard_map.84.refs_0_.refs_4_), channel_id=1, source_target_pairs={{3,0},{2,1},{1,2},{0,3},{7,4},{6,5},{5,6},{4,7},{11,8},{10,9},{9,1... | collective-permute-start | bytes 3145736 | tf_op jit(solution)/shard_map/ppermute | solution.py:45
  70.0 16.0 %collective-permute-start.13 = (bf16[256,2048]{1,0:T(8,128)(2,1)S(1)}, bf16[256,2048]{1,0:T(8,128)(2,1)S(1)}, u32[]{:S(2)}, u32[]{:S(2)}) collective-permute-start(bf16[256,2048]{1,0:T(8,128)(2,1)S(1)} %shard_map.85.refs_0_.refs_2_.refs_6_), channel_id=1, source_target_pairs={{12,0},{13,1},{14,2},{15,3},{8,4},{9,5},{10,6},{11,7},{4,8},{5,9},... | collective-permute-start | bytes 3145736 | tf_op jit(solution)/shard_map/ppermute | solution.py:45
  70.8 15.3 %collective-permute-start.9 = (bf16[256,2048]{1,0:T(8,128)(2,1)S(1)}, bf16[256,2048]{1,0:T(8,128)(2,1)S(1)}, u32[]{:S(2)}, u32[]{:S(2)}) collective-permute-start(bf16[256,2048]{1,0:T(8,128)(2,1)S(1)} %get-tuple-element.57), channel_id=1, source_target_pairs={{32,0},{33,1},{34,2},{35,3},{36,4},{37,5},{38,6},{39,7},{40,8},{41... | collective-permute-start | bytes 3145736 | tf_op jit(solution)/shard_map/ppermute | solution.py:45
  90.3 4.9 %collective-permute-start.15 = (bf16[512,2048]{1,0:T(8,128)(2,1)S(1)}, bf16[512,2048]{1,0:T(8,128)(2,1)S(1)}, u32[]{:S(2)}, u32[]{:S(2)}) collective-permute-start(bf16[512,2048]{1,0:T(8,128)(2,1)S(1)} %shard_map.86), channel_id=1, source_target_pairs={{16,0},{17,1},{18,2},{19,3},{20,4},{21,5},{22,6},{23,7},{24,8},{25... | collective-permute-start | bytes 6291464 | tf_op jit(solution)/shard_map/ppermute | solution.py:45
  91.8 16.3 %collective-permute-start.14 = (bf16[256,2048]{1,0:T(8,128)(2,1)S(1)}, bf16[256,2048]{1,0:T(8,128)(2,1)S(1)}, u32[]{:S(2)}, u32[]{:S(2)}) collective-permute-start(bf16[256,2048]{1,0:T(8,128)(2,1)S(1)} %add_convert_fusion.1), channel_id=1, source_target_pairs={{96,0},{97,1},{98,2},{99,3},{100,4},{101,5},{102,6},{103,7},{104,8... | collective-permute-start | bytes 3145736 | tf_op jit(solution)/shard_map/ppermute | solution.py:45
  109.1 14.9 %collective-permute-start.16 = (bf16[256,2048]{1,0:T(8,128)(2,1)S(1)}, bf16[256,2048]{1,0:T(8,128)(2,1)S(1)}, u32[]{:S(2)}, u32[]{:S(2)}) collective-permute-start(bf16[256,2048]{1,0:T(8,128)(2,1)S(1)} %pad_maximum_fusion.refs_0_.refs_4_), channel_id=1, source_target_pairs={{32,0},{33,1},{34,2},{35,3},{36,4},{37,5},{38,6},{39,7},{40,8},{41... | collective-permute-start | bytes 3145736 | tf_op jit(solution)/shard_map/ppermute | solution.py:45
  109.2 26.0 %collective-permute-start.20 = (bf16[256,2048]{1,0:T(8,128)(2,1)S(1)}, bf16[256,2048]{1,0:T(8,128)(2,1)S(1)}, u32[]{:S(2)}, u32[]{:S(2)}) collective-permute-start(bf16[256,2048]{1,0:T(8,128)(2,1)S(1)} %get-tuple-element.68), channel_id=1, source_target_pairs={{32,0},{33,1},{34,2},{35,3},{36,4},{37,5},{38,6},{39,7},{40,8},{41... | collective-permute-start | bytes 3145736 | tf_op jit(solution)/shard_map/ppermute | solution.py:45
  111.2 29.7 %collective-permute-start.18 = (bf16[256,2048]{1,0:T(8,128)(2,1)S(1)}, bf16[256,2048]{1,0:T(8,128)(2,1)S(1)}, u32[]{:S(2)}, u32[]{:S(2)}) collective-permute-start(bf16[256,2048]{1,0:T(8,128)(2,1)S(1)} %pad_maximum_fusion.refs_0_.refs_4_), channel_id=1, source_target_pairs={{16,0},{17,1},{18,2},{19,3},{20,4},{21,5},{22,6},{23,7},{24,8},{25... | collective-permute-start | bytes 3145736 | tf_op jit(solution)/shard_map/ppermute | solution.py:45
  135.2 5.7 %collective-permute-start.19 = (bf16[256,2048]{1,0:T(8,128)(2,1)S(1)}, bf16[256,2048]{1,0:T(8,128)(2,1)S(1)}, u32[]{:S(2)}, u32[]{:S(2)}) collective-permute-start(bf16[256,2048]{1,0:T(8,128)(2,1)S(1)} %collective-permute-done.16.refs_1_.refs_5_), channel_id=1, source_target_pairs={{16,0},{17,1},{18,2},{19,3},{20,4},{21,5},{22,6},{23,7},{24,8},{25... | collective-permute-start | bytes 3145736 | tf_op jit(solution)/shard_map/ppermute | solution.py:45
  135.6 16.1 %collective-permute-start.23 = (bf16[256,2048]{1,0:T(8,128)(2,1)S(1)}, bf16[256,2048]{1,0:T(8,128)(2,1)S(1)}, u32[]{:S(2)}, u32[]{:S(2)}) collective-permute-start(bf16[256,2048]{1,0:T(8,128)(2,1)S(1)} %add_convert_fusion), channel_id=1, source_target_pairs={{96,0},{97,1},{98,2},{99,3},{100,4},{101,5},{102,6},{103,7},{104,8... | collective-permute-start | bytes 3145736 | tf_op jit(solution)/shard_map/ppermute | solution.py:45
  138.9 16.0 %collective-permute-start.17 = (bf16[256,2048]{1,0:T(8,128)(2,1)S(1)}, bf16[256,2048]{1,0:T(8,128)(2,1)S(1)}, u32[]{:S(2)}, u32[]{:S(2)}) collective-permute-start(bf16[256,2048]{1,0:T(8,128)(2,1)S(1)} %get-tuple-element.67), channel_id=1, source_target_pairs={{12,0},{13,1},{14,2},{15,3},{8,4},{9,5},{10,6},{11,7},{4,8},{5,9},... | collective-permute-start | bytes 3145736 | tf_op jit(solution)/shard_map/ppermute | solution.py:45
  145.2 14.9 %collective-permute-start.21 = (bf16[256,2048]{1,0:T(8,128)(2,1)S(1)}, bf16[256,2048]{1,0:T(8,128)(2,1)S(1)}, u32[]{:S(2)}, u32[]{:S(2)}) collective-permute-start(bf16[256,2048]{1,0:T(8,128)(2,1)S(1)} %get-tuple-element.72), channel_id=1, source_target_pairs={{3,0},{2,1},{1,2},{0,3},{7,4},{6,5},{5,6},{4,7},{11,8},{10,9},{9,1... | collective-permute-start | bytes 3145736 | tf_op jit(solution)/shard_map/ppermute | solution.py:45
  152.8 19.7 %collective-permute-start.26 = (bf16[256,2048]{1,0:T(8,128)(2,1)S(1)}, bf16[256,2048]{1,0:T(8,128)(2,1)S(1)}, u32[]{:S(2)}, u32[]{:S(2)}) collective-permute-start(bf16[256,2048]{1,0:T(8,128)(2,1)S(1)} %pad_maximum_fusion.1.refs_0_.refs_4_), channel_id=1, source_target_pairs={{16,0},{17,1},{18,2},{19,3},{20,4},{21,5},{22,6},{23,7},{24,8},{25... | collective-permute-start | bytes 3145736 | tf_op jit(solution)/shard_map/ppermute | solution.py:45
  152.9 17.9 %collective-permute-start.24 = (bf16[256,2048]{1,0:T(8,128)(2,1)S(1)}, bf16[256,2048]{1,0:T(8,128)(2,1)S(1)}, u32[]{:S(2)}, u32[]{:S(2)}) collective-permute-start(bf16[256,2048]{1,0:T(8,128)(2,1)S(1)} %pad_maximum_fusion.1.refs_0_.refs_4_), channel_id=1, source_target_pairs={{32,0},{33,1},{34,2},{35,3},{36,4},{37,5},{38,6},{39,7},{40,8},{41... | collective-permute-start | bytes 3145736 | tf_op jit(solution)/shard_map/ppermute | solution.py:45
  160.5 10.3 %collective-permute-start.22 = (bf16[128,2048]{1,0:T(8,128)(2,1)S(1)}, bf16[128,2048]{1,0:T(8,128)(2,1)S(1)}, u32[]{:S(2)}, u32[]{:S(2)}) collective-permute-start(bf16[128,2048]{1,0:T(8,128)(2,1)S(1)} %slice.247), channel_id=1, source_target_pairs={{4,0},{5,1},{6,2},{7,3},{0,4},{1,5},{2,6},{3,7},{12,8},{13,9},{14,... | collective-permute-start | bytes 1572872 | tf_op jit(solution)/shard_map/ppermute | solution.py:45
  162.3 10.1 %collective-permute-start.25 = (bf16[128,2048]{1,0:T(8,128)(2,1)S(1)}, bf16[128,2048]{1,0:T(8,128)(2,1)S(1)}, u32[]{:S(2)}, u32[]{:S(2)}) collective-permute-start(bf16[128,2048]{1,0:T(8,128)(2,1)S(1)} %slice.246), channel_id=1, source_target_pairs={{1,0},{0,1},{3,2},{2,3},{5,4},{4,5},{7,6},{6,7},{9,8},{8,9},{11,10... | collective-permute-start | bytes 1572872 | tf_op jit(solution)/shard_map/ppermute | solution.py:45
  172.5 5.7 %collective-permute-start.28 = (bf16[256,2048]{1,0:T(8,128)(2,1)S(1)}, bf16[256,2048]{1,0:T(8,128)(2,1)S(1)}, u32[]{:S(2)}, u32[]{:S(2)}) collective-permute-start(bf16[256,2048]{1,0:T(8,128)(2,1)S(1)} %collective-permute-done.24.refs_1_.refs_5_), channel_id=1, source_target_pairs={{16,0},{17,1},{18,2},{19,3},{20,4},{21,5},{22,6},{23,7},{24,8},{25... | collective-permute-start | bytes 3145736 | tf_op jit(solution)/shard_map/ppermute | solution.py:45
  176.8 16.1 %collective-permute-start.27 = (bf16[256,2048]{1,0:T(8,128)(2,1)S(1)}, bf16[256,2048]{1,0:T(8,128)(2,1)S(1)}, u32[]{:S(2)}, u32[]{:S(2)}) collective-permute-start(bf16[256,2048]{1,0:T(8,128)(2,1)S(1)} %get-tuple-element.82), channel_id=1, source_target_pairs={{12,0},{13,1},{14,2},{15,3},{8,4},{9,5},{10,6},{11,7},{4,8},{5,9},... | collective-permute-start | bytes 3145736 | tf_op jit(solution)/shard_map/ppermute | solution.py:45
  182.5 14.9 %collective-permute-start.29 = (bf16[256,2048]{1,0:T(8,128)(2,1)S(1)}, bf16[256,2048]{1,0:T(8,128)(2,1)S(1)}, u32[]{:S(2)}, u32[]{:S(2)}) collective-permute-start(bf16[256,2048]{1,0:T(8,128)(2,1)S(1)} %get-tuple-element.86), channel_id=1, source_target_pairs={{3,0},{2,1},{1,2},{0,3},{7,4},{6,5},{5,6},{4,7},{11,8},{10,9},{9,1... | collective-permute-start | bytes 3145736 | tf_op jit(solution)/shard_map/ppermute | solution.py:45
  197.8 11.8 %collective-permute-start.30 = (bf16[128,2048]{1,0:T(8,128)(2,1)S(1)}, bf16[128,2048]{1,0:T(8,128)(2,1)S(1)}, u32[]{:S(2)}, u32[]{:S(2)}) collective-permute-start(bf16[128,2048]{1,0:T(8,128)(2,1)S(1)} %slice.245), channel_id=1, source_target_pairs={{4,0},{5,1},{6,2},{7,3},{0,4},{1,5},{2,6},{3,7},{12,8},{13,9},{14,... | collective-permute-start | bytes 1572872 | tf_op jit(solution)/shard_map/ppermute | solution.py:45
  199.7 10.5 %collective-permute-start.31 = (bf16[128,2048]{1,0:T(8,128)(2,1)S(1)}, bf16[128,2048]{1,0:T(8,128)(2,1)S(1)}, u32[]{:S(2)}, u32[]{:S(2)}) collective-permute-start(bf16[128,2048]{1,0:T(8,128)(2,1)S(1)} %slice.244), channel_id=1, source_target_pairs={{1,0},{0,1},{3,2},{2,3},{5,4},{4,5},{7,6},{6,7},{9,8},{8,9},{11,10... | collective-permute-start | bytes 1572872 | tf_op jit(solution)/shard_map/ppermute | solution.py:45
  210.7 9.3 %collective-permute-start.32 = (bf16[128,2048]{1,0:T(8,128)(2,1)S(1)}, bf16[128,2048]{1,0:T(8,128)(2,1)S(1)}, u32[]{:S(2)}, u32[]{:S(2)}) collective-permute-start(bf16[128,2048]{1,0:T(8,128)(2,1)S(1)} %pad_maximum_fusion.2), channel_id=1, source_target_pairs={{3,0},{2,1},{1,2},{0,3},{7,4},{6,5},{5,6},{4,7},{11,8},{10,9},{9,1... | collective-permute-start | bytes 1572872 | tf_op jit(solution)/shard_map/ppermute | solution.py:45
  210.8 10.5 %collective-permute-start.33 = (bf16[128,2048]{1,0:T(8,128)(2,1)S(1)}, bf16[128,2048]{1,0:T(8,128)(2,1)S(1)}, u32[]{:S(2)}, u32[]{:S(2)}) collective-permute-start(bf16[128,2048]{1,0:T(8,128)(2,1)S(1)} %pad_maximum_fusion.3), channel_id=1, source_target_pairs={{12,0},{13,1},{14,2},{15,3},{8,4},{9,5},{10,6},{11,7},{4,8},{5,9},... | collective-permute-start | bytes 1572872 | tf_op jit(solution)/shard_map/ppermute | solution.py:45
  222.1 6.8 %collective-permute-start.34 = (bf16[64,2048]{1,0:T(8,128)(2,1)}, bf16[64,2048]{1,0:T(8,128)(2,1)S(1)}, u32[]{:S(2)}, u32[]{:S(2)}) collective-permute-start(bf16[64,2048]{1,0:T(8,128)(2,1)} %fusion.15), channel_id=1, source_target_pairs={{1,0},{0,1},{3,2},{2,3},{5,4},{4,5},{7,6},{6,7},{9,8},{8,9},{11,10... | collective-permute-start | bytes 786440 | tf_op jit(solution)/shard_map/ppermute | solution.py:45
  225.2 6.7 %collective-permute-start.35 = (bf16[64,2048]{1,0:T(8,128)(2,1)}, bf16[64,2048]{1,0:T(8,128)(2,1)}, u32[]{:S(2)}, u32[]{:S(2)}) collective-permute-start(bf16[64,2048]{1,0:T(8,128)(2,1)} %fusion.12), channel_id=1, source_target_pairs={{4,0},{5,1},{6,2},{7,3},{0,4},{1,5},{2,6},{3,7},{12,8},{13,9},{14,... | collective-permute-start | bytes 786440 | tf_op jit(solution)/shard_map/ppermute | solution.py:45

commit v10 on v9

--- a/solution.py
+++ b/solution.py
@@ -99,13 +99,24 @@
     return jnp.where(core == 0, one(0), one(1))
 
 
-def cut_kernel(place_ref, tokens_ref, grad_ref, kept_ref, passed_ref):
+def cut_kernel(place_ref, tokens_ref, grad_ref, kept_ref, passed_ref, sems):
     block, wide = kept_ref.shape[0], tokens_ref.shape[1]
     core = place_ref[1]
+    copies = []
     for ref, which in ((kept_ref, core), (passed_ref, 1 - core)):
         rows = pl.ds(pl.multiple_of(which * block, block), block)
-        ref[:, :wide] = tokens_ref[rows, :]
-        ref[:, wide:] = grad_ref[rows, :]
+        for i, source in enumerate((tokens_ref, grad_ref)):
+            copies.append(
+                pltpu.make_async_copy(
+                    source.at[rows, :],
+                    ref.at[:, i * wide:(i + 1) * wide],
+                    sems.at[len(copies)],
+                )
+            )
+    for copy in copies:
+        copy.start()
+    for copy in copies:
+        copy.wait()
 
 
 def whole(kernel, place, arrays, shapes):
@@ -122,7 +133,17 @@
 
 def cut(place, tokens, out_grad):
     rows, wide = tokens.shape
-    return whole(cut_kernel, place, [tokens, out_grad], [(rows // 2, 2 * wide)] * 2)
+    half = jax.ShapeDtypeStruct((rows // 2, 2 * wide), BF)
+    return pl.pallas_call(
+        cut_kernel,
+        in_specs=[pl.BlockSpec(memory_space=pltpu.SMEM)]
+        + [pl.BlockSpec(memory_space=pltpu.HBM)] * 2,
+        out_specs=[pl.BlockSpec(memory_space=pltpu.VMEM)] * 2,
+        out_shape=[half, half],
+        scratch_shapes=[pltpu.SemaphoreType.DMA((4,))],
+        compiler_params=pltpu.CompilerParams(vmem_limit_bytes=8 * 2**20),
+        cost_estimate=cost(flops=0, bytes_accessed=0, transcendentals=0),
+    )(place, tokens, out_grad)
 
 
 def join_kernel(place_ref, a_ref, b_ref, out_ref):
@@ -168,7 +189,7 @@
     return slot // 2, (slot % 2) * RING + order_of(keep).index(piece)
 
 
-def pair_kernel(keep, hidden, added, split, block, place_ref, *refs):
+def pair_kernel(keep, hidden, added, split, side, block, place_ref, *refs):
     a_refs, (left_ref, right_ref), rest = refs[:2], refs[2:4], refs[4:]
     if added:
         more_ref, rest = rest[0], rest[1:]
@@ -190,6 +211,12 @@
                     at = (i * RING + j) * block
                     rows_ref[at:at + block, :] = a_refs[which][first * block:(first + 1) * block, :]
 
+    def rows():
+        if side is None:
+            return rows_ref[...]
+        half = rows_ref.shape[0] // 2
+        return rows_ref[side * half:(side + 1) * half, :]
+
     def finish(total):
         if added:
             total = total + more_ref[...].astype(F32)
@@ -203,14 +230,14 @@
 
     @pl.when(pl.program_id(0) == 0)
     def _():
-        finish(lax.dot_general(rows_ref[...], left_ref[...], NN, preferred_element_type=F32))
+        finish(lax.dot_general(rows(), left_ref[...], NN, preferred_element_type=F32))
 
     @pl.when(pl.program_id(0) == 1)
     def _():
-        finish(lax.dot_general(rows_ref[...], right_ref[...], NT, preferred_element_type=F32))
-
-
-def pair_dot(keep, hidden, pair, left, right, place, more=None, split=True, tile=512):
+        finish(lax.dot_general(rows(), right_ref[...], NT, preferred_element_type=F32))
+
+
+def pair_dot(keep, hidden, pair, left, right, place, more=None, split=True, side=None, tile=512):
     rows = sum(a.shape[0] for a in pair)
     block = rows // RING // RING
     depth, wide = left.shape
@@ -225,9 +252,9 @@
     if more is not None:
         in_specs.append(out_of(rows))
         args.append(more)
-    outs = [rows // 2, rows // 2] if split else [rows]
+    outs = [rows // 2, rows // 2] if split else [rows if side is None else rows // 2]
     result = pl.pallas_call(
-        functools.partial(pair_kernel, keep, hidden, more is not None, split, block),
+        functools.partial(pair_kernel, keep, hidden, more is not None, split, side, block),
         grid_spec=pltpu.PrefetchScalarGridSpec(
             num_scalar_prefetch=1,
             grid=(2, tiles),
@@ -326,10 +353,12 @@
         pair = [near[keep], after(rest[keep], *events) if events else rest[keep]]
         return pair_dot(keep, False, pair, w_in, w_out, place, more=more, split=keep)
 
-    def out_dot(keep, pair, *events):
+    def out_dot(keep, pair, *events, side=None):
         pair = list(pair)
         pair[1] = after(pair[1], *events) if events else pair[1]
-        return pair_dot(keep, True, pair, w_out, w_in, place)
+        return pair_dot(
+            keep, True, pair, w_out, w_in, place, split=side is None, side=side
+        )
 
     def halfway(kept, got):
         half = kept.shape[0] // 2
@@ -366,11 +395,11 @@
     sent_b = panel_dot(False, near_b, rest_b, step_a)
     half_a = half_sum(kept_a, step_a)
     turn_a = exchange(half_a, along_z(1))
+    pair_a = hidden_of(half_a, turn_a)
     kept_b, send_b = panel_dot(
-        True, near_b, rest_b, more=exchange(sent_b, other_core)
+        True, near_b, rest_b, pair_a, more=exchange(sent_b, other_core)
     )
-    pair_a = hidden_of(half_a, after(turn_a, send_b))
-    step_b = exchange(after(send_b, turn_a), along_z(0))
+    step_b = exchange(send_b, along_z(0))
     far_a = exchange(pair_a, along_z(0))
     hid_a = {True: (pair_a, far_a)}
     hid_a[False] = (exchange(pair_a, other_core), exchange(far_a, other_core))
@@ -409,9 +438,9 @@
     out_a, out_b, got_a, got_b = {}, {}, {}, {}
     sums_a, sums_b, last_a, last_b, total_a, total_b = {}, {}, {}, {}, {}, {}
     out_a[True] = out_dot(True, hid_a[True])
-    half_b = half_sum(kept_b, after(step_b, out_a[True][0]))
+    out_a[False] = out_dot(False, hid_a[False], out_a[True][0])
+    half_b = half_sum(kept_b, after(step_b, out_a[True][0], out_a[False][0]))
     turn_b = exchange(half_b, along_z(1))
-    out_a[False] = out_dot(False, hid_a[False], out_a[True][0], step_b)
     for keep in both_ways:
         got_a[keep] = exchange(out_a[keep][1], along(keep, True, 1))
     grad_in = grads(0, near_a, rest_a, hid_a, None, out_a[False][0])
@@ -425,8 +454,12 @@
     hid_b = {True: (pair_b, far_b)}
     hid_b[False] = (exchange(pair_b, other_core), exchange(far_b, other_core))
 
-    out_b[True] = out_dot(True, hid_b[True], hid_b[False][0])
-    out_b[False] = out_dot(False, hid_b[False], out_b[True][0])
+    leaves, stays = {}, {}
+    leaves[True] = out_dot(True, hid_b[True], hid_b[False][0], side=1)
+    leaves[False] = out_dot(False, hid_b[False], leaves[True], side=1)
+    stays[True] = out_dot(True, hid_b[True], leaves[False], side=0)
+    stays[False] = out_dot(False, hid_b[False], stays[True], side=0)
+    out_b = {keep: (stays[keep], leaves[keep]) for keep in both_ways}
     for keep in both_ways:
         got_b[keep] = exchange(out_b[keep][1], along(keep, True, 1))
     grad_in = grads(

time: 237 us -> 236 us (level)
  waiting for transfers between devices: 104 us -> 99.5 us
  Pallas kernels: 65 us -> 69.2 us
    ppermute x36, waiting for transfers between devices: 104 us -> 99.5 us  [exchange(): return lax.ppermute(array, AXES, pairs)]
    pallas_call x8 -> x10, Pallas kernels: 35.5 us -> 39.6 us  [pair_dot(): pl.pallas_call(functools.partial(pair_kernel, keep, hidden, more is not N...]
    pallas_call x9 -> x8, Pallas kernels: 5.4 us -> 4.82 us  [whole(): pl.pallas_call(kernel, in_specs=[pl.BlockSpec(memory_space=pltpu.SMEM)] +...]
  transfers between devices with their start and end apart: 36 -> 36, of which waited for: 24 -> 23; matrix products, arithmetic and copies ran while one was open for 3% -> 3% of each run, Pallas kernels for 23% -> 27%
where the time goes in v10:
time: 236 us; the launch traced here: 234 us
  waiting for transfers between devices  99.5 us (42%)
  Pallas kernels  69.2 us (29%)
  starting transfers between devices  48.4 us (21%)
  other arithmetic  8.61 us (4%)
  local copies, waits for them, and re-layouts  6.8 us (3%)
    ppermute x36, waiting for transfers between devices, exchange(): return lax.ppermute(array, AXES, pairs)  99.5 us
    ppermute x36, starting transfers between devices, exchange(): return lax.ppermute(array, AXES, pairs)  48.4 us
    pallas_call x10, Pallas kernels, pair_dot(): pl.pallas_call(functools.partial(pair_kernel, keep, hidden, more is not N...  39.6 us
    pallas_call x4, Pallas kernels, grad_dot(): pl.pallas_call(functools.partial(grad_kernel, pairs, block, factor, begun...  24.1 us
    pallas_call x8, Pallas kernels, whole(): pl.pallas_call(kernel, in_specs=[pl.BlockSpec(memory_space=pltpu.SMEM)] +...  4.82 us
  transfers between devices with their start and end apart: 36, of which 23 were waited for; matrix products, arithmetic and copies ran while one was open for 3% of the time, Pallas kernels for 27%

profile of v10, /device:TPU:8, one launch (start us, length us, event | category | flops | bytes accessed | tf_op | source)
XLA Modules:
  0.0 233.7 jit_solution(4793152095991527707)
XLA Ops:
  3.3 1.6 collective-permute-start
  5.3 4.4 %collective-permute-done.b_ref = bf16[64,2048]{1,0:T(8,128)(2,1)S(1)} collective-permute-done((bf16[64,2048]{1,0:T(8,128)(2,1)S(1)}, bf16[64,2048]{1,0:T(8,128)(2,1)S(1)}, u32[]{:S(2)}, u32[]{:S(2)}) %collective-permute-start) | collective-permute-done | bytes 262176 | tf_op jit(solution)/shard_map/ppermute | solution.py:45
  10.3 2.8 %collective-permute-start.1 = (bf16[128,2048]{1,0:T(8,128)(2,1)S(1)}, bf16[128,2048]{1,0:T(8,128)(2,1)S(1)}, u32[]{:S(2)}, u32[]{:S(2)}) collective-permute-start(bf16[128,2048]{1,0:T(8,128)(2,1)S(1)} %shard_map.76), channel_id=1, source_target_pairs={{12,0},{13,1},{14,2},{15,3},{8,4},{9,5},{10,6},{11,7},{4,8},{5,9},... | collective-permute-start | bytes 1572872 | tf_op jit(solution)/shard_map/ppermute | solution.py:45
  13.8 1.7 collective-permute-start.3
  15.4 5.4 %collective-permute-done.1.c_ref = bf16[128,2048]{1,0:T(8,128)(2,1)S(1)} collective-permute-done((bf16[128,2048]{1,0:T(8,128)(2,1)S(1)}, bf16[128,2048]{1,0:T(8,128)(2,1)S(1)}, u32[]{:S(2)}, u32[]{:S(2)}) %collective-permute-start.1) | collective-permute-done | bytes 524320 | tf_op jit(solution)/shard_map/ppermute | solution.py:45
  24.7 1.7 collective-permute-start.4
  26.3 7.3 %collective-permute-done.6.b_ref = bf16[128,2048]{1,0:T(8,128)(2,1)S(1)} collective-permute-done((bf16[128,2048]{1,0:T(8,128)(2,1)S(1)}, bf16[128,2048]{1,0:T(8,128)(2,1)S(1)}, u32[]{:S(2)}, u32[]{:S(2)}) %collective-permute-start.6) | collective-permute-done | bytes 524320 | tf_op jit(solution)/shard_map/ppermute | solution.py:45
  34.3 2.0 collective-permute-start.7
  36.9 1.7 collective-permute-start.5
  38.6 2.7 %constant_dynamic-slice_fusion = (bf16[1024,1024]{1,0:T(8,128)(2,1)S(1)}, bf16[1024,1024]{1,0:T(8,128)(2,1)S(1)}) fusion(bf16[2048,1024]{1,0:T(8,128)(2,1)} %param.7, s32[]{:T(128)S(6)} %select_n.30, bf16[1024,2048]{1,0:T(8,128)(2,1)} %param.6), kind=kLoop, calls=%fused_computation.55 | loop fusion | bytes 8388612 | tf_op jit(solution)/shard_map/dynamic_slice | solution.py:337
  41.3 9.1 %collective-permute-done.7.refs_1_.refs_3_.refs_7_ = bf16[256,2048]{1,0:T(8,128)(2,1)S(1)} collective-permute-done((bf16[256,2048]{1,0:T(8,128)(2,1)S(1)}, bf16[256,2048]{1,0:T(8,128)(2,1)S(1)}, u32[]{:S(2)}, u32[]{:S(2)}) %collective-permute-start.7) | collective-permute-done | bytes 1048608 | tf_op jit(solution)/shard_map/ppermute | solution.py:45
  50.3 1.6 collective-permute-done.5.refs_1_.refs_5_
  51.9 4.3 %shard_map.82 = bf16[512,2048]{1,0:T(8,128)(2,1)S(1)} custom-call(s32[2]{0:T(128)S(1)} %pad_add_fusion.place_ref, bf16[256,2048]{1,0:T(8,128)(2,1)S(1)} %shard_map.81.refs_0_.refs_2_.refs_6_, bf16[256,2048]{1,0:T(8,128)(2,1)S(1)} %collective-permute-done.7.refs_1_.refs_3_.refs_7_, bf16[1024,1024]{1,0:T(8,128)(2,1)S(1)} %get-tuple-element.126.refs_2_.refs_3_, ...), custom_call_target="tpu_custom_call" | custom-call | flops 2147483 | bytes 8388 | tf_op jit(solution)/shard_map/pallas_call | solution.py:256
  56.8 3.0 %collective-permute-start.10 = (bf16[128,2048]{1,0:T(8,128)(2,1)S(1)}, bf16[128,2048]{1,0:T(8,128)(2,1)S(1)}, u32[]{:S(2)}, u32[]{:S(2)}) collective-permute-start(bf16[128,2048]{1,0:T(8,128)(2,1)S(1)} %copy-done.1), channel_id=1, source_target_pairs={{1,0},{0,1},{3,2},{2,3},{5,4},{4,5},{7,6},{6,7},{9,8},{8,9},{11,10... | collective-permute-start | bytes 1572872 | tf_op jit(solution)/shard_map/ppermute | solution.py:45
  60.4 5.3 %shard_map.83 = (bf16[256,2048]{1,0:T(8,128)(2,1)S(1)}, bf16[256,2048]{1,0:T(8,128)(2,1)S(1)}) custom-call(s32[2]{0:T(128)S(1)} %pad_add_fusion.place_ref, bf16[256,2048]{1,0:T(8,128)(2,1)S(1)} %shard_map.80.refs_0_.refs_4_, bf16[256,2048]{1,0:T(8,128)(2,1)} %collective-permute-done.5.refs_1_.refs_5_, ...), custom_call_target="tpu_custom_call" | custom-call | flops 2147483 | bytes 8388 | tf_op jit(solution)/shard_map/pallas_call | solution.py:256
  67.6 2.6 %collective-permute-start.11 = (bf16[256,2048]{1,0:T(8,128)(2,1)S(1)}, bf16[256,2048]{1,0:T(8,128)(2,1)S(1)}, u32[]{:S(2)}, u32[]{:S(2)}) collective-permute-start(bf16[256,2048]{1,0:T(8,128)(2,1)S(1)} %shard_map.84.refs_0_.refs_4_), channel_id=1, source_target_pairs={{3,0},{2,1},{1,2},{0,3},{7,4},{6,5},{5,6},{4,7},{11,8},{10,9},{9,1... | collective-permute-start | bytes 3145736 | tf_op jit(solution)/shard_map/ppermute | solution.py:45
  70.9 1.9 collective-permute-start.9
  72.8 10.1 %collective-permute-done.11.refs_1_.refs_5_ = bf16[256,2048]{1,0:T(8,128)(2,1)S(1)} collective-permute-done((bf16[256,2048]{1,0:T(8,128)(2,1)S(1)}, bf16[256,2048]{1,0:T(8,128)(2,1)S(1)}, u32[]{:S(2)}, u32[]{:S(2)}) %collective-permute-start.11) | collective-permute-done | bytes 1048608 | tf_op jit(solution)/shard_map/ppermute | solution.py:45
  82.9 3.2 %collective-permute-done.13.refs_1_.refs_3_.refs_7_ = bf16[256,2048]{1,0:T(8,128)(2,1)S(1)} collective-permute-done((bf16[256,2048]{1,0:T(8,128)(2,1)S(1)}, bf16[256,2048]{1,0:T(8,128)(2,1)S(1)}, u32[]{:S(2)}, u32[]{:S(2)}) %collective-permute-start.13) | collective-permute-done | bytes 1048608 | tf_op jit(solution)/shard_map/ppermute | solution.py:45
  86.6 4.1 %collective-permute-start.14 = (bf16[256,2048]{1,0:T(8,128)(2,1)S(1)}, bf16[256,2048]{1,0:T(8,128)(2,1)S(1)}, u32[]{:S(2)}, u32[]{:S(2)}) collective-permute-start(bf16[256,2048]{1,0:T(8,128)(2,1)S(1)} %add_convert_fusion.1), channel_id=1, source_target_pairs={{96,0},{97,1},{98,2},{99,3},{100,4},{101,5},{102,6},{103,7},{104,8... | collective-permute-start | bytes 3145736 | tf_op jit(solution)/shard_map/ppermute | solution.py:45
  90.7 4.3 %shard_map.89 = bf16[512,2048]{1,0:T(8,128)(2,1)S(1)} custom-call(s32[2]{0:T(128)S(1)} %pad_add_fusion.place_ref, bf16[256,2048]{1,0:T(8,128)(2,1)S(1)} %shard_map.85.refs_0_.refs_2_.refs_6_, bf16[256,2048]{1,0:T(8,128)(2,1)S(1)} %collective-permute-done.13.refs_1_.refs_3_.refs_7_, bf16[1024,1024]{1,0:T(8,128)(2,1)S(1)} %get-tuple-element.126.refs_2_.refs_3_, ...), custom_call_target="tpu_custom_call" | custom-call | flops 2147483 | bytes 8388 | tf_op jit(solution)/shard_map/pallas_call | solution.py:256
  95.1 8.4 %collective-permute-done.14 = bf16[256,2048]{1,0:T(8,128)(2,1)S(1)} collective-permute-done((bf16[256,2048]{1,0:T(8,128)(2,1)S(1)}, bf16[256,2048]{1,0:T(8,128)(2,1)S(1)}, u32[]{:S(2)}, u32[]{:S(2)}) %collective-permute-start.14) | collective-permute-done | bytes 1048608 | tf_op jit(solution)/shard_map/ppermute | solution.py:45
  104.6 14.8 %collective-permute-done.15.refs_1_.refs_5_ = bf16[256,2048]{1,0:T(8,128)(2,1)S(1)} collective-permute-done((bf16[256,2048]{1,0:T(8,128)(2,1)S(1)}, bf16[256,2048]{1,0:T(8,128)(2,1)S(1)}, u32[]{:S(2)}, u32[]{:S(2)}) %collective-permute-start.15) | collective-permute-done | bytes 1048608 | tf_op jit(solution)/shard_map/ppermute | solution.py:45
  119.9 4.5 %shard_map.90 = (bf16[256,2048]{1,0:T(8,128)(2,1)S(1)}, bf16[256,2048]{1,0:T(8,128)(2,1)S(1)}) custom-call(s32[2]{0:T(128)S(1)} %pad_add_fusion.place_ref, bf16[256,2048]{1,0:T(8,128)(2,1)S(1)} %shard_map.84.refs_0_.refs_4_, bf16[256,2048]{1,0:T(8,128)(2,1)S(1)} %collective-permute-done.11.refs_1_.refs_5_, ...), custom_call_target="tpu_custom_call" | custom-call | flops 2147483 | bytes 8388 | tf_op jit(solution)/shard_map/pallas_call | solution.py:256
  124.4 4.3 %shard_map.86 = (bf16[256,2048]{1,0:T(8,128)(2,1)S(1)}, bf16[256,2048]{1,0:T(8,128)(2,1)S(1)}) custom-call(s32[2]{0:T(128)S(1)} %pad_add_fusion.place_ref, bf16[256,2048]{1,0:T(8,128)(2,1)S(1)} %pad_maximum_fusion.refs_0_.refs_4_, bf16[256,2048]{1,0:T(8,128)(2,1)S(1)} %collective-permute-done.15.refs_1_.refs_5_, ...), custom_call_target="tpu_custom_call" | custom-call | flops 2147483 | bytes 8388 | tf_op jit(solution)/shard_map/pallas_call | solution.py:256
  128.7 2.1 collective-permute-start.16
  130.9 4.3 %shard_map.87 = (bf16[256,2048]{1,0:T(8,128)(2,1)S(1)}, bf16[256,2048]{1,0:T(8,128)(2,1)S(1)}) custom-call(s32[2]{0:T(128)S(1)} %pad_add_fusion.place_ref, bf16[256,2048]{1,0:T(8,128)(2,1)S(1)} %collective-permute-done.17.refs_0_.refs_6_.refs_2_, bf16[256,2048]{1,0:T(8,128)(2,1)S(1)} %collective-permute-done.18.refs_1_.refs_7_.refs_3_, ...), custom_call_target="tpu_custom_call" | custom-call | flops 2147483 | bytes 8388 | tf_op jit(solution)/shard_map/pallas_call | solution.py:256
  135.4 3.9 %collective-permute-done.22 = bf16[256,2048]{1,0:T(8,128)(2,1)S(1)} collective-permute-done((bf16[256,2048]{1,0:T(8,128)(2,1)S(1)}, bf16[256,2048]{1,0:T(8,128)(2,1)S(1)}, u32[]{:S(2)}, u32[]{:S(2)}) %collective-permute-start.22) | collective-permute-done | bytes 1048608 | tf_op jit(solution)/shard_map/ppermute | solution.py:45
  139.6 3.3 %collective-permute-start.23 = (bf16[256,2048]{1,0:T(8,128)(2,1)S(1)}, bf16[256,2048]{1,0:T(8,128)(2,1)S(1)}, u32[]{:S(2)}, u32[]{:S(2)}) collective-permute-start(bf16[256,2048]{1,0:T(8,128)(2,1)S(1)} %add_convert_fusion), channel_id=1, source_target_pairs={{96,0},{97,1},{98,2},{99,3},{100,4},{101,5},{102,6},{103,7},{104,8... | collective-permute-start | bytes 3145736 | tf_op jit(solution)/shard_map/ppermute | solution.py:45
  142.9 5.6 %shard_map.88.refs_8_ = f32[1024,1024]{1,0:T(8,128)} custom-call(bf16[256,2048]{1,0:T(8,128)(2,1)S(1)} %shard_map.80.refs_0_.refs_4_, bf16[256,2048]{1,0:T(8,128)(2,1)} %collective-permute-done.5.refs_1_.refs_5_, bf16[256,2048]{1,0:T(8,128)(2,1)S(1)} %shard_map.81.refs_0_.refs_2_.refs_6_, ...), custom_call_target="tpu_custom_call" | custom-call | flops 2147483 | bytes 5242 | tf_op jit(solution)/shard_map/pallas_call | solution.py:305
  148.5 1.6 collective-permute-done.19
  150.1 5.6 %collective-permute-done.23 = bf16[256,2048]{1,0:T(8,128)(2,1)S(1)} collective-permute-done((bf16[256,2048]{1,0:T(8,128)(2,1)S(1)}, bf16[256,2048]{1,0:T(8,128)(2,1)S(1)}, u32[]{:S(2)}, u32[]{:S(2)}) %collective-permute-start.23) | collective-permute-done | bytes 1048608 | tf_op jit(solution)/shard_map/ppermute | solution.py:45
  158.7 2.7 %collective-permute-start.25 = (bf16[128,2048]{1,0:T(8,128)(2,1)S(1)}, bf16[128,2048]{1,0:T(8,128)(2,1)S(1)}, u32[]{:S(2)}, u32[]{:S(2)}) collective-permute-start(bf16[128,2048]{1,0:T(8,128)(2,1)S(1)} %slice.248), channel_id=1, source_target_pairs={{1,0},{0,1},{3,2},{2,3},{5,4},{4,5},{7,6},{6,7},{9,8},{8,9},{11,10... | collective-permute-start | bytes 1572872 | tf_op jit(solution)/shard_map/ppermute | solution.py:45
  161.4 5.5 %shard_map.91.refs_8_ = f32[1024,1024]{1,0:T(8,128)} custom-call(bf16[256,2048]{1,0:T(8,128)(2,1)S(1)} %pad_maximum_fusion.refs_0_.refs_4_, bf16[256,2048]{1,0:T(8,128)(2,1)S(1)} %collective-permute-done.15.refs_1_.refs_5_, bf16[256,2048]{1,0:T(8,128)(2,1)S(1)} %collective-permute-done.17.refs_0_.refs_6_.refs_2_, ...), custom_call_target="tpu_custom_call" | custom-call | flops 2147483 | bytes 5242 | tf_op jit(solution)/shard_map/pallas_call | solution.py:305
  166.9 1.6 collective-permute-done.25
  168.5 4.5 %collective-permute-done.24.refs_1_.refs_5_ = bf16[256,2048]{1,0:T(8,128)(2,1)S(1)} collective-permute-done((bf16[256,2048]{1,0:T(8,128)(2,1)S(1)}, bf16[256,2048]{1,0:T(8,128)(2,1)S(1)}, u32[]{:S(2)}, u32[]{:S(2)}) %collective-permute-start.24) | collective-permute-done | bytes 1048608 | tf_op jit(solution)/shard_map/ppermute | solution.py:45
  173.2 3.1 %shard_map.92 = bf16[256,2048]{1,0:T(8,128)(2,1)S(1)} custom-call(s32[2]{0:T(128)S(1)} %pad_add_fusion.place_ref, bf16[256,2048]{1,0:T(8,128)(2,1)S(1)} %pad_maximum_fusion.1.refs_0_.refs_4_, bf16[256,2048]{1,0:T(8,128)(2,1)S(1)} %collective-permute-done.24.refs_1_.refs_5_, bf16[1024,1024]{1,0:T(8,128)(2,1)S(1)} %get-tuple-element.125.refs_3_.refs_2_, ...), custom_call_target="tpu_custom_call" | custom-call | flops 2147483 | bytes 8388 | tf_op jit(solution)/shard_map/pallas_call | solution.py:256
  177.8 3.1 %shard_map.93 = bf16[256,2048]{1,0:T(8,128)(2,1)S(1)} custom-call(s32[2]{0:T(128)S(1)} %pad_add_fusion.place_ref, bf16[256,2048]{1,0:T(8,128)(2,1)S(1)} %collective-permute-done.26.refs_0_.refs_6_.refs_2_, bf16[256,2048]{1,0:T(8,128)(2,1)S(1)} %collective-permute-done.27.refs_1_.refs_7_.refs_3_, bf16[1024,1024]{1,0:T(8,128)(2,1)S(1)} %get-tuple-element.125.refs_3_.refs_2_, ...), custom_call_target="tpu_custom_call" | custom-call | flops 2147483 | bytes 8388 | tf_op jit(solution)/shard_map/pallas_call | solution.py:256
  181.7 3.2 %shard_map.94 = bf16[256,2048]{1,0:T(8,128)(2,1)S(1)} custom-call(s32[2]{0:T(128)S(1)} %pad_add_fusion.place_ref, bf16[256,2048]{1,0:T(8,128)(2,1)S(1)} %pad_maximum_fusion.1.refs_0_.refs_4_, bf16[256,2048]{1,0:T(8,128)(2,1)S(1)} %collective-permute-done.24.refs_1_.refs_5_, bf16[1024,1024]{1,0:T(8,128)(2,1)S(1)} %get-tuple-element.125.refs_3_.refs_2_, ...), custom_call_target="tpu_custom_call" | custom-call | flops 2147483 | bytes 8388 | tf_op jit(solution)/shard_map/pallas_call | solution.py:256
  184.8 3.1 %shard_map.95 = bf16[256,2048]{1,0:T(8,128)(2,1)S(1)} custom-call(s32[2]{0:T(128)S(1)} %pad_add_fusion.place_ref, bf16[256,2048]{1,0:T(8,128)(2,1)S(1)} %collective-permute-done.26.refs_0_.refs_6_.refs_2_, bf16[256,2048]{1,0:T(8,128)(2,1)S(1)} %collective-permute-done.27.refs_1_.refs_7_.refs_3_, bf16[1024,1024]{1,0:T(8,128)(2,1)S(1)} %get-tuple-element.125.refs_3_.refs_2_, ...), custom_call_target="tpu_custom_call" | custom-call | flops 2147483 | bytes 8388 | tf_op jit(solution)/shard_map/pallas_call | solution.py:256
  188.0 6.5 %shard_map.96 = f32[1024,1024]{1,0:T(8,128)} custom-call(bf16[256,2048]{1,0:T(8,128)(2,1)S(1)} %shard_map.84.refs_0_.refs_4_, bf16[256,2048]{1,0:T(8,128)(2,1)S(1)} %collective-permute-done.11.refs_1_.refs_5_, bf16[256,2048]{1,0:T(8,128)(2,1)S(1)} %shard_map.85.refs_0_.refs_2_.refs_6_, ...), custom_call_target="tpu_custom_call", output_to_operand_aliasing={{}: (8, {})} | custom-call | flops 2147483 | bytes 5242 | tf_op jit(solution)/shard_map/pallas_call | solution.py:305
  198.2 3.9 %collective-permute-start.31 = (bf16[128,2048]{1,0:T(8,128)(2,1)S(1)}, bf16[128,2048]{1,0:T(8,128)(2,1)S(1)}, u32[]{:S(2)}, u32[]{:S(2)}) collective-permute-start(bf16[128,2048]{1,0:T(8,128)(2,1)S(1)} %slice.246), channel_id=1, source_target_pairs={{1,0},{0,1},{3,2},{2,3},{5,4},{4,5},{7,6},{6,7},{9,8},{8,9},{11,10... | collective-permute-start | bytes 1572872 | tf_op jit(solution)/shard_map/ppermute | solution.py:45
  202.2 6.5 %shard_map.97 = f32[1024,1024]{1,0:T(8,128)} custom-call(bf16[256,2048]{1,0:T(8,128)(2,1)S(1)} %pad_maximum_fusion.1.refs_0_.refs_4_, bf16[256,2048]{1,0:T(8,128)(2,1)S(1)} %collective-permute-done.24.refs_1_.refs_5_, bf16[256,2048]{1,0:T(8,128)(2,1)S(1)} %collective-permute-done.26.refs_0_.refs_6_.refs_2_, ...), custom_call_target="tpu_custom_call", output_to_operand_aliasing={{}: (8, {})} | custom-call | flops 2147483 | bytes 5242 | tf_op jit(solution)/shard_map/pallas_call | solution.py:305
  209.9 1.5 collective-permute-start.33
  211.5 7.5 %collective-permute-done.32 = bf16[128,2048]{1,0:T(8,128)(2,1)S(1)} collective-permute-done((bf16[128,2048]{1,0:T(8,128)(2,1)S(1)}, bf16[128,2048]{1,0:T(8,128)(2,1)S(1)}, u32[]{:S(2)}, u32[]{:S(2)}) %collective-permute-start.32) | collective-permute-done | bytes 524320 | tf_op jit(solution)/shard_map/ppermute | solution.py:45
  221.2 2.9 %collective-permute-start.34 = (bf16[64,2048]{1,0:T(8,128)(2,1)}, bf16[64,2048]{1,0:T(8,128)(2,1)S(1)}, u32[]{:S(2)}, u32[]{:S(2)}) collective-permute-start(bf16[64,2048]{1,0:T(8,128)(2,1)} %fusion.15), channel_id=1, source_target_pairs={{1,0},{0,1},{3,2},{2,3},{5,4},{4,5},{7,6},{6,7},{9,8},{8,9},{11,10... | collective-permute-start | bytes 786440 | tf_op jit(solution)/shard_map/ppermute | solution.py:45
  226.4 2.2 collective-permute-done.34
  228.7 3.0 %collective-permute-done.35 = bf16[64,2048]{1,0:T(8,128)(2,1)} collective-permute-done((bf16[64,2048]{1,0:T(8,128)(2,1)}, bf16[64,2048]{1,0:T(8,128)(2,1)}, u32[]{:S(2)}, u32[]{:S(2)}) %collective-permute-start.35) | collective-permute-done | bytes 262176 | tf_op jit(solution)/shard_map/ppermute | solution.py:45
  (100 shorter events, 32.5 us)
Async XLA Ops:
  0.7 1.0 copy-start.4
  1.7 0.9 copy-start.5
  3.3 6.5 %collective-permute-start = (bf16[64,2048]{1,0:T(8,128)(2,1)S(1)}, bf16[64,2048]{1,0:T(8,128)(2,1)S(1)}, u32[]{:S(2)}, u32[]{:S(2)}) collective-permute-start(bf16[64,2048]{1,0:T(8,128)(2,1)S(1)} %get-tuple-element.46.a_ref), channel_id=1, source_target_pairs={{4,0},{5,1},{6,2},{7,3},{0,4},{1,5},{2,6},{3,7},{12,8},{13,9},{14,... | collective-permute-start | bytes 786440 | tf_op jit(solution)/shard_map/ppermute | solution.py:45
  4.9 8.3 %collective-permute-start.2 = (bf16[64,2048]{1,0:T(8,128)(2,1)S(1)}, bf16[64,2048]{1,0:T(8,128)(2,1)S(1)}, u32[]{:S(2)}, u32[]{:S(2)}) collective-permute-start(bf16[64,2048]{1,0:T(8,128)(2,1)S(1)} %get-tuple-element.48.a_ref), channel_id=1, source_target_pairs={{1,0},{0,1},{3,2},{2,3},{5,4},{4,5},{7,6},{6,7},{9,8},{8,9},{11,10... | collective-permute-start | bytes 786440 | tf_op jit(solution)/shard_map/ppermute | solution.py:45
  10.3 10.5 %collective-permute-start.1 = (bf16[128,2048]{1,0:T(8,128)(2,1)S(1)}, bf16[128,2048]{1,0:T(8,128)(2,1)S(1)}, u32[]{:S(2)}, u32[]{:S(2)}) collective-permute-start(bf16[128,2048]{1,0:T(8,128)(2,1)S(1)} %shard_map.76), channel_id=1, source_target_pairs={{12,0},{13,1},{14,2},{15,3},{8,4},{9,5},{10,6},{11,7},{4,8},{5,9},... | collective-permute-start | bytes 1572872 | tf_op jit(solution)/shard_map/ppermute | solution.py:45
  13.8 9.3 %collective-permute-start.3 = (bf16[128,2048]{1,0:T(8,128)(2,1)S(1)}, bf16[128,2048]{1,0:T(8,128)(2,1)S(1)}, u32[]{:S(2)}, u32[]{:S(2)}) collective-permute-start(bf16[128,2048]{1,0:T(8,128)(2,1)S(1)} %shard_map.78), channel_id=1, source_target_pairs={{3,0},{2,1},{1,2},{0,3},{7,4},{6,5},{5,6},{4,7},{11,8},{10,9},{9,1... | collective-permute-start | bytes 1572872 | tf_op jit(solution)/shard_map/ppermute | solution.py:45
  21.4 0.8 copy-start
  23.7 0.8 copy-start.2
  24.5 9.2 %collective-permute-start.6 = (bf16[128,2048]{1,0:T(8,128)(2,1)S(1)}, bf16[128,2048]{1,0:T(8,128)(2,1)S(1)}, u32[]{:S(2)}, u32[]{:S(2)}) collective-permute-start(bf16[128,2048]{1,0:T(8,128)(2,1)S(1)} %get-tuple-element.51.a_ref), channel_id=1, source_target_pairs={{4,0},{5,1},{6,2},{7,3},{0,4},{1,5},{2,6},{3,7},{12,8},{13,9},{14,... | collective-permute-start | bytes 1572872 | tf_op jit(solution)/shard_map/ppermute | solution.py:45
  24.7 11.6 %collective-permute-start.4 = (bf16[128,2048]{1,0:T(8,128)(2,1)S(1)}, bf16[128,2048]{1,0:T(8,128)(2,1)S(1)}, u32[]{:S(2)}, u32[]{:S(2)}) collective-permute-start(bf16[128,2048]{1,0:T(8,128)(2,1)S(1)} %get-tuple-element.50.a_ref), channel_id=1, source_target_pairs={{1,0},{0,1},{3,2},{2,3},{5,4},{4,5},{7,6},{6,7},{9,8},{8,9},{11,10... | collective-permute-start | bytes 1572872 | tf_op jit(solution)/shard_map/ppermute | solution.py:45
  34.3 16.1 %collective-permute-start.7 = (bf16[256,2048]{1,0:T(8,128)(2,1)S(1)}, bf16[256,2048]{1,0:T(8,128)(2,1)S(1)}, u32[]{:S(2)}, u32[]{:S(2)}) collective-permute-start(bf16[256,2048]{1,0:T(8,128)(2,1)S(1)} %shard_map.81.refs_0_.refs_2_.refs_6_), channel_id=1, source_target_pairs={{12,0},{13,1},{14,2},{15,3},{8,4},{9,5},{10,6},{11,7},{4,8},{5,9},... | collective-permute-start | bytes 3145736 | tf_op jit(solution)/shard_map/ppermute | solution.py:45
  36.9 15.0 %collective-permute-start.5 = (bf16[256,2048]{1,0:T(8,128)(2,1)S(1)}, bf16[256,2048]{1,0:T(8,128)(2,1)}, u32[]{:S(2)}, u32[]{:S(2)}) collective-permute-start(bf16[256,2048]{1,0:T(8,128)(2,1)S(1)} %shard_map.80.refs_0_.refs_4_), channel_id=1, source_target_pairs={{3,0},{2,1},{1,2},{0,3},{7,4},{6,5},{5,6},{4,7},{11,8},{10,9},{9,1... | collective-permute-start | bytes 3145736 | tf_op jit(solution)/shard_map/ppermute | solution.py:45
  51.9 4.4 %copy-start.3 = (bf16[128,2048]{1,0:T(8,128)(2,1)S(1)}, bf16[128,2048]{1,0:T(8,128)(2,1)}, u32[]{:S(2)}) copy-start(bf16[128,2048]{1,0:T(8,128)(2,1)} %copy-done.2) | copy-start | bytes 1572868
  51.9 4.9 %copy-start.1 = (bf16[128,2048]{1,0:T(8,128)(2,1)S(1)}, bf16[128,2048]{1,0:T(8,128)(2,1)}, u32[]{:S(2)}) copy-start(bf16[128,2048]{1,0:T(8,128)(2,1)} %copy-done) | copy-start | bytes 1572868
  56.2 4.2 %collective-permute-start.8 = (bf16[512,2048]{1,0:T(8,128)(2,1)S(1)}, bf16[512,2048]{1,0:T(8,128)(2,1)S(1)}, u32[]{:S(2)}, u32[]{:S(2)}) collective-permute-start(bf16[512,2048]{1,0:T(8,128)(2,1)S(1)} %shard_map.82), channel_id=1, source_target_pairs={{16,0},{17,1},{18,2},{19,3},{20,4},{21,5},{22,6},{23,7},{24,8},{25... | collective-permute-start | bytes 6291464 | tf_op jit(solution)/shard_map/ppermute | solution.py:45
  56.3 9.5 %collective-permute-start.12 = (bf16[128,2048]{1,0:T(8,128)(2,1)S(1)}, bf16[128,2048]{1,0:T(8,128)(2,1)S(1)}, u32[]{:S(2)}, u32[]{:S(2)}) collective-permute-start(bf16[128,2048]{1,0:T(8,128)(2,1)S(1)} %copy-done.3), channel_id=1, source_target_pairs={{4,0},{5,1},{6,2},{7,3},{0,4},{1,5},{2,6},{3,7},{12,8},{13,9},{14,... | collective-permute-start | bytes 1572872 | tf_op jit(solution)/shard_map/ppermute | solution.py:45
  56.8 10.2 %collective-permute-start.10 = (bf16[128,2048]{1,0:T(8,128)(2,1)S(1)}, bf16[128,2048]{1,0:T(8,128)(2,1)S(1)}, u32[]{:S(2)}, u32[]{:S(2)}) collective-permute-start(bf16[128,2048]{1,0:T(8,128)(2,1)S(1)} %copy-done.1), channel_id=1, source_target_pairs={{1,0},{0,1},{3,2},{2,3},{5,4},{4,5},{7,6},{6,7},{9,8},{8,9},{11,10... | collective-permute-start | bytes 1572872 | tf_op jit(solution)/shard_map/ppermute | solution.py:45
  67.6 15.4 %collective-permute-start.11 = (bf16[256,2048]{1,0:T(8,128)(2,1)S(1)}, bf16[256,2048]{1,0:T(8,128)(2,1)S(1)}, u32[]{:S(2)}, u32[]{:S(2)}) collective-permute-start(bf16[256,2048]{1,0:T(8,128)(2,1)S(1)} %shard_map.84.refs_0_.refs_4_), channel_id=1, source_target_pairs={{3,0},{2,1},{1,2},{0,3},{7,4},{6,5},{5,6},{4,7},{11,8},{10,9},{9,1... | collective-permute-start | bytes 3145736 | tf_op jit(solution)/shard_map/ppermute | solution.py:45
  70.2 16.0 %collective-permute-start.13 = (bf16[256,2048]{1,0:T(8,128)(2,1)S(1)}, bf16[256,2048]{1,0:T(8,128)(2,1)S(1)}, u32[]{:S(2)}, u32[]{:S(2)}) collective-permute-start(bf16[256,2048]{1,0:T(8,128)(2,1)S(1)} %shard_map.85.refs_0_.refs_2_.refs_6_), channel_id=1, source_target_pairs={{12,0},{13,1},{14,2},{15,3},{8,4},{9,5},{10,6},{11,7},{4,8},{5,9},... | collective-permute-start | bytes 3145736 | tf_op jit(solution)/shard_map/ppermute | solution.py:45
  70.9 15.3 %collective-permute-start.9 = (bf16[256,2048]{1,0:T(8,128)(2,1)S(1)}, bf16[256,2048]{1,0:T(8,128)(2,1)S(1)}, u32[]{:S(2)}, u32[]{:S(2)}) collective-permute-start(bf16[256,2048]{1,0:T(8,128)(2,1)S(1)} %get-tuple-element.54), channel_id=1, source_target_pairs={{32,0},{33,1},{34,2},{35,3},{36,4},{37,5},{38,6},{39,7},{40,8},{41... | collective-permute-start | bytes 3145736 | tf_op jit(solution)/shard_map/ppermute | solution.py:45
  86.6 16.9 %collective-permute-start.14 = (bf16[256,2048]{1,0:T(8,128)(2,1)S(1)}, bf16[256,2048]{1,0:T(8,128)(2,1)S(1)}, u32[]{:S(2)}, u32[]{:S(2)}) collective-permute-start(bf16[256,2048]{1,0:T(8,128)(2,1)S(1)} %add_convert_fusion.1), channel_id=1, source_target_pairs={{96,0},{97,1},{98,2},{99,3},{100,4},{101,5},{102,6},{103,7},{104,8... | collective-permute-start | bytes 3145736 | tf_op jit(solution)/shard_map/ppermute | solution.py:45
  95.0 24.9 %collective-permute-start.21 = (bf16[512,2048]{1,0:T(8,128)(2,1)S(1)}, bf16[512,2048]{1,0:T(8,128)(2,1)S(1)}, u32[]{:S(2)}, u32[]{:S(2)}) collective-permute-start(bf16[512,2048]{1,0:T(8,128)(2,1)S(1)} %shard_map.89), channel_id=1, source_target_pairs={{16,0},{17,1},{18,2},{19,3},{20,4},{21,5},{22,6},{23,7},{24,8},{25... | collective-permute-start | bytes 6291464 | tf_op jit(solution)/shard_map/ppermute | solution.py:45
  104.5 14.9 %collective-permute-start.15 = (bf16[256,2048]{1,0:T(8,128)(2,1)S(1)}, bf16[256,2048]{1,0:T(8,128)(2,1)S(1)}, u32[]{:S(2)}, u32[]{:S(2)}) collective-permute-start(bf16[256,2048]{1,0:T(8,128)(2,1)S(1)} %pad_maximum_fusion.refs_0_.refs_4_), channel_id=1, source_target_pairs={{32,0},{33,1},{34,2},{35,3},{36,4},{37,5},{38,6},{39,7},{40,8},{41... | collective-permute-start | bytes 3145736 | tf_op jit(solution)/shard_map/ppermute | solution.py:45
  119.3 11.5 %collective-permute-start.18 = (bf16[256,2048]{1,0:T(8,128)(2,1)S(1)}, bf16[256,2048]{1,0:T(8,128)(2,1)S(1)}, u32[]{:S(2)}, u32[]{:S(2)}) collective-permute-start(bf16[256,2048]{1,0:T(8,128)(2,1)S(1)} %collective-permute-done.15.refs_1_.refs_5_), channel_id=1, source_target_pairs={{16,0},{17,1},{18,2},{19,3},{20,4},{21,5},{22,6},{23,7},{24,8},{25... | collective-permute-start | bytes 3145736 | tf_op jit(solution)/shard_map/ppermute | solution.py:45
  119.4 11.5 %collective-permute-start.17 = (bf16[256,2048]{1,0:T(8,128)(2,1)S(1)}, bf16[256,2048]{1,0:T(8,128)(2,1)S(1)}, u32[]{:S(2)}, u32[]{:S(2)}) collective-permute-start(bf16[256,2048]{1,0:T(8,128)(2,1)S(1)} %pad_maximum_fusion.refs_0_.refs_4_), channel_id=1, source_target_pairs={{16,0},{17,1},{18,2},{19,3},{20,4},{21,5},{22,6},{23,7},{24,8},{25... | collective-permute-start | bytes 3145736 | tf_op jit(solution)/shard_map/ppermute | solution.py:45
  124.3 14.9 %collective-permute-start.22 = (bf16[256,2048]{1,0:T(8,128)(2,1)S(1)}, bf16[256,2048]{1,0:T(8,128)(2,1)S(1)}, u32[]{:S(2)}, u32[]{:S(2)}) collective-permute-start(bf16[256,2048]{1,0:T(8,128)(2,1)S(1)} %get-tuple-element.70), channel_id=1, source_target_pairs={{32,0},{33,1},{34,2},{35,3},{36,4},{37,5},{38,6},{39,7},{40,8},{41... | collective-permute-start | bytes 3145736 | tf_op jit(solution)/shard_map/ppermute | solution.py:45
  128.7 19.8 %collective-permute-start.16 = (bf16[256,2048]{1,0:T(8,128)(2,1)S(1)}, bf16[256,2048]{1,0:T(8,128)(2,1)S(1)}, u32[]{:S(2)}, u32[]{:S(2)}) collective-permute-start(bf16[256,2048]{1,0:T(8,128)(2,1)S(1)} %get-tuple-element.61), channel_id=1, source_target_pairs={{12,0},{13,1},{14,2},{15,3},{8,4},{9,5},{10,6},{11,7},{4,8},{5,9},... | collective-permute-start | bytes 3145736 | tf_op jit(solution)/shard_map/ppermute | solution.py:45
  135.2 14.9 %collective-permute-start.19 = (bf16[256,2048]{1,0:T(8,128)(2,1)S(1)}, bf16[256,2048]{1,0:T(8,128)(2,1)S(1)}, u32[]{:S(2)}, u32[]{:S(2)}) collective-permute-start(bf16[256,2048]{1,0:T(8,128)(2,1)S(1)} %get-tuple-element.65), channel_id=1, source_target_pairs={{3,0},{2,1},{1,2},{0,3},{7,4},{6,5},{5,6},{4,7},{11,8},{10,9},{9,1... | collective-permute-start | bytes 3145736 | tf_op jit(solution)/shard_map/ppermute | solution.py:45
  139.6 16.1 %collective-permute-start.23 = (bf16[256,2048]{1,0:T(8,128)(2,1)S(1)}, bf16[256,2048]{1,0:T(8,128)(2,1)S(1)}, u32[]{:S(2)}, u32[]{:S(2)}) collective-permute-start(bf16[256,2048]{1,0:T(8,128)(2,1)S(1)} %add_convert_fusion), channel_id=1, source_target_pairs={{96,0},{97,1},{98,2},{99,3},{100,4},{101,5},{102,6},{103,7},{104,8... | collective-permute-start | bytes 3145736 | tf_op jit(solution)/shard_map/ppermute | solution.py:45
  157.1 9.8 %collective-permute-start.20 = (bf16[128,2048]{1,0:T(8,128)(2,1)S(1)}, bf16[128,2048]{1,0:T(8,128)(2,1)S(1)}, u32[]{:S(2)}, u32[]{:S(2)}) collective-permute-start(bf16[128,2048]{1,0:T(8,128)(2,1)S(1)} %slice.249), channel_id=1, source_target_pairs={{4,0},{5,1},{6,2},{7,3},{0,4},{1,5},{2,6},{3,7},{12,8},{13,9},{14,... | collective-permute-start | bytes 1572872 | tf_op jit(solution)/shard_map/ppermute | solution.py:45
  158.1 14.9 %collective-permute-start.24 = (bf16[256,2048]{1,0:T(8,128)(2,1)S(1)}, bf16[256,2048]{1,0:T(8,128)(2,1)S(1)}, u32[]{:S(2)}, u32[]{:S(2)}) collective-permute-start(bf16[256,2048]{1,0:T(8,128)(2,1)S(1)} %pad_maximum_fusion.1.refs_0_.refs_4_), channel_id=1, source_target_pairs={{32,0},{33,1},{34,2},{35,3},{36,4},{37,5},{38,6},{39,7},{40,8},{41... | collective-permute-start | bytes 3145736 | tf_op jit(solution)/shard_map/ppermute | solution.py:45
  158.7 9.9 %collective-permute-start.25 = (bf16[128,2048]{1,0:T(8,128)(2,1)S(1)}, bf16[128,2048]{1,0:T(8,128)(2,1)S(1)}, u32[]{:S(2)}, u32[]{:S(2)}) collective-permute-start(bf16[128,2048]{1,0:T(8,128)(2,1)S(1)} %slice.248), channel_id=1, source_target_pairs={{1,0},{0,1},{3,2},{2,3},{5,4},{4,5},{7,6},{6,7},{9,8},{8,9},{11,10... | collective-permute-start | bytes 1572872 | tf_op jit(solution)/shard_map/ppermute | solution.py:45
  161.3 11.8 %collective-permute-start.26 = (bf16[256,2048]{1,0:T(8,128)(2,1)S(1)}, bf16[256,2048]{1,0:T(8,128)(2,1)S(1)}, u32[]{:S(2)}, u32[]{:S(2)}) collective-permute-start(bf16[256,2048]{1,0:T(8,128)(2,1)S(1)} %pad_maximum_fusion.1.refs_0_.refs_4_), channel_id=1, source_target_pairs={{16,0},{17,1},{18,2},{19,3},{20,4},{21,5},{22,6},{23,7},{24,8},{25... | collective-permute-start | bytes 3145736 | tf_op jit(solution)/shard_map/ppermute | solution.py:45
  173.0 4.8 %collective-permute-start.27 = (bf16[256,2048]{1,0:T(8,128)(2,1)S(1)}, bf16[256,2048]{1,0:T(8,128)(2,1)S(1)}, u32[]{:S(2)}, u32[]{:S(2)}) collective-permute-start(bf16[256,2048]{1,0:T(8,128)(2,1)S(1)} %collective-permute-done.24.refs_1_.refs_5_), channel_id=1, source_target_pairs={{16,0},{17,1},{18,2},{19,3},{20,4},{21,5},{22,6},{23,7},{24,8},{25... | collective-permute-start | bytes 3145736 | tf_op jit(solution)/shard_map/ppermute | solution.py:45
  176.3 18.1 %collective-permute-start.28 = (bf16[256,2048]{1,0:T(8,128)(2,1)S(1)}, bf16[256,2048]{1,0:T(8,128)(2,1)S(1)}, u32[]{:S(2)}, u32[]{:S(2)}) collective-permute-start(bf16[256,2048]{1,0:T(8,128)(2,1)S(1)} %shard_map.92), channel_id=1, source_target_pairs={{12,0},{13,1},{14,2},{15,3},{8,4},{9,5},{10,6},{11,7},{4,8},{5,9},... | collective-permute-start | bytes 3145736 | tf_op jit(solution)/shard_map/ppermute | solution.py:45
  181.0 14.9 %collective-permute-start.29 = (bf16[256,2048]{1,0:T(8,128)(2,1)S(1)}, bf16[256,2048]{1,0:T(8,128)(2,1)S(1)}, u32[]{:S(2)}, u32[]{:S(2)}) collective-permute-start(bf16[256,2048]{1,0:T(8,128)(2,1)S(1)} %shard_map.93), channel_id=1, source_target_pairs={{3,0},{2,1},{1,2},{0,3},{7,4},{6,5},{5,6},{4,7},{11,8},{10,9},{9,1... | collective-permute-start | bytes 3145736 | tf_op jit(solution)/shard_map/ppermute | solution.py:45
  196.3 12.4 %collective-permute-start.30 = (bf16[128,2048]{1,0:T(8,128)(2,1)S(1)}, bf16[128,2048]{1,0:T(8,128)(2,1)S(1)}, u32[]{:S(2)}, u32[]{:S(2)}) collective-permute-start(bf16[128,2048]{1,0:T(8,128)(2,1)S(1)} %slice.247), channel_id=1, source_target_pairs={{4,0},{5,1},{6,2},{7,3},{0,4},{1,5},{2,6},{3,7},{12,8},{13,9},{14,... | collective-permute-start | bytes 1572872 | tf_op jit(solution)/shard_map/ppermute | solution.py:45
  198.2 11.1 %collective-permute-start.31 = (bf16[128,2048]{1,0:T(8,128)(2,1)S(1)}, bf16[128,2048]{1,0:T(8,128)(2,1)S(1)}, u32[]{:S(2)}, u32[]{:S(2)}) collective-permute-start(bf16[128,2048]{1,0:T(8,128)(2,1)S(1)} %slice.246), channel_id=1, source_target_pairs={{1,0},{0,1},{3,2},{2,3},{5,4},{4,5},{7,6},{6,7},{9,8},{8,9},{11,10... | collective-permute-start | bytes 1572872 | tf_op jit(solution)/shard_map/ppermute | solution.py:45
  209.7 9.3 %collective-permute-start.32 = (bf16[128,2048]{1,0:T(8,128)(2,1)S(1)}, bf16[128,2048]{1,0:T(8,128)(2,1)S(1)}, u32[]{:S(2)}, u32[]{:S(2)}) collective-permute-start(bf16[128,2048]{1,0:T(8,128)(2,1)S(1)} %pad_maximum_fusion.2), channel_id=1, source_target_pairs={{3,0},{2,1},{1,2},{0,3},{7,4},{6,5},{5,6},{4,7},{11,8},{10,9},{9,1... | collective-permute-start | bytes 1572872 | tf_op jit(solution)/shard_map/ppermute | solution.py:45
  209.9 10.5 %collective-permute-start.33 = (bf16[128,2048]{1,0:T(8,128)(2,1)S(1)}, bf16[128,2048]{1,0:T(8,128)(2,1)S(1)}, u32[]{:S(2)}, u32[]{:S(2)}) collective-permute-start(bf16[128,2048]{1,0:T(8,128)(2,1)S(1)} %pad_maximum_fusion.3), channel_id=1, source_target_pairs={{12,0},{13,1},{14,2},{15,3},{8,4},{9,5},{10,6},{11,7},{4,8},{5,9},... | collective-permute-start | bytes 1572872 | tf_op jit(solution)/shard_map/ppermute | solution.py:45
  221.2 7.4 %collective-permute-start.34 = (bf16[64,2048]{1,0:T(8,128)(2,1)}, bf16[64,2048]{1,0:T(8,128)(2,1)S(1)}, u32[]{:S(2)}, u32[]{:S(2)}) collective-permute-start(bf16[64,2048]{1,0:T(8,128)(2,1)} %fusion.15), channel_id=1, source_target_pairs={{1,0},{0,1},{3,2},{2,3},{5,4},{4,5},{7,6},{6,7},{9,8},{8,9},{11,10... | collective-permute-start | bytes 786440 | tf_op jit(solution)/shard_map/ppermute | solution.py:45
  225.0 6.7 %collective-permute-start.35 = (bf16[64,2048]{1,0:T(8,128)(2,1)}, bf16[64,2048]{1,0:T(8,128)(2,1)}, u32[]{:S(2)}, u32[]{:S(2)}) collective-permute-start(bf16[64,2048]{1,0:T(8,128)(2,1)} %fusion.12), channel_id=1, source_target_pairs={{4,0},{5,1},{6,2},{7,3},{0,4},{1,5},{2,6},{3,7},{12,8},{13,9},{14,... | collective-permute-start | bytes 786440 | tf_op jit(solution)/shard_map/ppermute | solution.py:45

commit v11 on v10

--- a/solution.py
+++ b/solution.py
@@ -391,15 +391,15 @@
     kept_a, send_a = panel_dot(True, near_a, rest_a, more=exchange(sent_a, other_core))
     near_b = joined(own_b, {keep: after(near_of_b[keep], send_a) for keep in order})
     rest_b = others(near_b)
-    step_a = after(exchange(send_a, along_z(0)), rest_b[True], rest_b[False])
-    sent_b = panel_dot(False, near_b, rest_b, step_a)
+    sent_b = panel_dot(False, near_b, rest_b, rest_b[True], send_a)
+    step_a = after(exchange(send_a, along_z(0)), sent_b)
     half_a = half_sum(kept_a, step_a)
     turn_a = exchange(half_a, along_z(1))
-    pair_a = hidden_of(half_a, turn_a)
     kept_b, send_b = panel_dot(
-        True, near_b, rest_b, pair_a, more=exchange(sent_b, other_core)
+        True, near_b, rest_b, more=exchange(sent_b, other_core)
     )
-    step_b = exchange(send_b, along_z(0))
+    pair_a = hidden_of(half_a, after(turn_a, send_b))
+    step_b = exchange(after(send_b, turn_a), along_z(0))
     far_a = exchange(pair_a, along_z(0))
     hid_a = {True: (pair_a, far_a)}
     hid_a[False] = (exchange(pair_a, other_core), exchange(far_a, other_core))
@@ -438,9 +438,9 @@
     out_a, out_b, got_a, got_b = {}, {}, {}, {}
     sums_a, sums_b, last_a, last_b, total_a, total_b = {}, {}, {}, {}, {}, {}
     out_a[True] = out_dot(True, hid_a[True])
-    out_a[False] = out_dot(False, hid_a[False], out_a[True][0])
-    half_b = half_sum(kept_b, after(step_b, out_a[True][0], out_a[False][0]))
+    half_b = half_sum(kept_b, after(step_b, out_a[True][0]))
     turn_b = exchange(half_b, along_z(1))
+    out_a[False] = out_dot(False, hid_a[False], out_a[True][0], step_b)
     for keep in both_ways:
         got_a[keep] = exchange(out_a[keep][1], along(keep, True, 1))
     grad_in = grads(0, near_a, rest_a, hid_a, None, out_a[False][0])

time: 236 us -> 238 us (level)
  starting transfers between devices: 48.4 us -> 56.8 us
  waiting for transfers between devices: 99.5 us -> 95.2 us
    ppermute x36, starting transfers between devices: 48.4 us -> 56.8 us  [exchange(): return lax.ppermute(array, AXES, pairs)]
    ppermute x36, waiting for transfers between devices: 99.5 us -> 95.2 us  [exchange(): return lax.ppermute(array, AXES, pairs)]
  transfers between devices with their start and end apart: 36 -> 36, of which waited for: 23 -> 22; matrix products, arithmetic and copies ran while one was open for 3% -> 3% of each run, Pallas kernels for 27% -> 26%
where the time goes in v11:
time: 238 us
  waiting for transfers between devices  95.2 us (40%)
  Pallas kernels  69.2 us (29%)
  starting transfers between devices  56.8 us (24%)
  other arithmetic  8.63 us (4%)
  local copies, waits for them, and re-layouts  6.83 us (3%)
    ppermute x36, waiting for transfers between devices, exchange(): return lax.ppermute(array, AXES, pairs)  95.2 us
    ppermute x36, starting transfers between devices, exchange(): return lax.ppermute(array, AXES, pairs)  56.8 us
    pallas_call x10, Pallas kernels, pair_dot(): pl.pallas_call(functools.partial(pair_kernel, keep, hidden, more is not N...  39.5 us
    pallas_call x4, Pallas kernels, grad_dot(): pl.pallas_call(functools.partial(grad_kernel, pairs, block, factor, begun...  24.1 us
    pallas_call x8, Pallas kernels, whole(): pl.pallas_call(kernel, in_specs=[pl.BlockSpec(memory_space=pltpu.SMEM)] +...  4.82 us
  transfers between devices with their start and end apart: 36, of which 22 were waited for; matrix products, arithmetic and copies ran while one was open for 3% of the time, Pallas kernels for 26%

profile of v11, /device:TPU:8, one launch (start us, length us, event | category | flops | bytes accessed | tf_op | source)
XLA Modules:
  0.0 237.8 jit_solution(7822038604766266260)
XLA Ops:
  5.3 4.4 %collective-permute-done.b_ref = bf16[64,2048]{1,0:T(8,128)(2,1)S(1)} collective-permute-done((bf16[64,2048]{1,0:T(8,128)(2,1)S(1)}, bf16[64,2048]{1,0:T(8,128)(2,1)S(1)}, u32[]{:S(2)}, u32[]{:S(2)}) %collective-permute-start) | collective-permute-done | bytes 262176 | tf_op jit(solution)/shard_map/ppermute | solution.py:45
  10.3 2.8 %collective-permute-start.1 = (bf16[128,2048]{1,0:T(8,128)(2,1)S(1)}, bf16[128,2048]{1,0:T(8,128)(2,1)S(1)}, u32[]{:S(2)}, u32[]{:S(2)}) collective-permute-start(bf16[128,2048]{1,0:T(8,128)(2,1)S(1)} %shard_map.76), channel_id=1, source_target_pairs={{12,0},{13,1},{14,2},{15,3},{8,4},{9,5},{10,6},{11,7},{4,8},{5,9},... | collective-permute-start | bytes 1572872 | tf_op jit(solution)/shard_map/ppermute | solution.py:45
  13.8 1.7 collective-permute-start.3
  15.4 5.4 %collective-permute-done.1.c_ref = bf16[128,2048]{1,0:T(8,128)(2,1)S(1)} collective-permute-done((bf16[128,2048]{1,0:T(8,128)(2,1)S(1)}, bf16[128,2048]{1,0:T(8,128)(2,1)S(1)}, u32[]{:S(2)}, u32[]{:S(2)}) %collective-permute-start.1) | collective-permute-done | bytes 524320 | tf_op jit(solution)/shard_map/ppermute | solution.py:45
  24.7 1.7 collective-permute-start.4
  26.3 7.3 %collective-permute-done.6.b_ref = bf16[128,2048]{1,0:T(8,128)(2,1)S(1)} collective-permute-done((bf16[128,2048]{1,0:T(8,128)(2,1)S(1)}, bf16[128,2048]{1,0:T(8,128)(2,1)S(1)}, u32[]{:S(2)}, u32[]{:S(2)}) %collective-permute-start.6) | collective-permute-done | bytes 524320 | tf_op jit(solution)/shard_map/ppermute | solution.py:45
  34.3 2.0 collective-permute-start.7
  36.9 1.7 collective-permute-start.5
  38.6 2.7 %constant_dynamic-slice_fusion = (bf16[1024,1024]{1,0:T(8,128)(2,1)S(1)}, bf16[1024,1024]{1,0:T(8,128)(2,1)S(1)}) fusion(bf16[2048,1024]{1,0:T(8,128)(2,1)} %param.7, s32[]{:T(128)S(6)} %select_n.30, bf16[1024,2048]{1,0:T(8,128)(2,1)} %param.6), kind=kLoop, calls=%fused_computation.55 | loop fusion | bytes 8388612 | tf_op jit(solution)/shard_map/dynamic_slice | solution.py:337
  41.3 9.1 %collective-permute-done.7.refs_1_.refs_3_.refs_7_ = bf16[256,2048]{1,0:T(8,128)(2,1)S(1)} collective-permute-done((bf16[256,2048]{1,0:T(8,128)(2,1)S(1)}, bf16[256,2048]{1,0:T(8,128)(2,1)S(1)}, u32[]{:S(2)}, u32[]{:S(2)}) %collective-permute-start.7) | collective-permute-done | bytes 1048608 | tf_op jit(solution)/shard_map/ppermute | solution.py:45
  51.9 4.3 %shard_map.82 = bf16[512,2048]{1,0:T(8,128)(2,1)S(1)} custom-call(s32[2]{0:T(128)S(1)} %pad_add_fusion.place_ref, bf16[256,2048]{1,0:T(8,128)(2,1)S(1)} %shard_map.81.refs_0_.refs_2_.refs_6_, bf16[256,2048]{1,0:T(8,128)(2,1)S(1)} %collective-permute-done.7.refs_1_.refs_3_.refs_7_, bf16[1024,1024]{1,0:T(8,128)(2,1)S(1)} %get-tuple-element.128.refs_2_.refs_3_, ...), custom_call_target="tpu_custom_call" | custom-call | flops 2147483 | bytes 8388 | tf_op jit(solution)/shard_map/pallas_call | solution.py:256
  56.3 1.7 collective-permute-start.12
  58.0 1.7 collective-permute-start.10
  60.4 5.3 %shard_map.83 = (bf16[256,2048]{1,0:T(8,128)(2,1)S(1)}, bf16[256,2048]{1,0:T(8,128)(2,1)S(1)}) custom-call(s32[2]{0:T(128)S(1)} %pad_add_fusion.place_ref, bf16[256,2048]{1,0:T(8,128)(2,1)S(1)} %shard_map.80.refs_0_.refs_4_, bf16[256,2048]{1,0:T(8,128)(2,1)} %collective-permute-done.5.refs_1_.refs_5_, ...), custom_call_target="tpu_custom_call" | custom-call | flops 2147483 | bytes 8388 | tf_op jit(solution)/shard_map/pallas_call | solution.py:256
  67.8 2.6 %collective-permute-start.11 = (bf16[256,2048]{1,0:T(8,128)(2,1)S(1)}, bf16[256,2048]{1,0:T(8,128)(2,1)S(1)}, u32[]{:S(2)}, u32[]{:S(2)}) collective-permute-start(bf16[256,2048]{1,0:T(8,128)(2,1)S(1)} %shard_map.84.refs_0_.refs_2_.refs_6_), channel_id=1, source_target_pairs={{12,0},{13,1},{14,2},{15,3},{8,4},{9,5},{10,6},{11,7},{4,8},{5,9},... | collective-permute-start | bytes 3145736 | tf_op jit(solution)/shard_map/ppermute | solution.py:45
  70.4 2.4 %collective-permute-start.13 = (bf16[256,2048]{1,0:T(8,128)(2,1)S(1)}, bf16[256,2048]{1,0:T(8,128)(2,1)S(1)}, u32[]{:S(2)}, u32[]{:S(2)}) collective-permute-start(bf16[256,2048]{1,0:T(8,128)(2,1)S(1)} %shard_map.85.refs_0_.refs_4_), channel_id=1, source_target_pairs={{3,0},{2,1},{1,2},{0,3},{7,4},{6,5},{5,6},{4,7},{11,8},{10,9},{9,1... | collective-permute-start | bytes 3145736 | tf_op jit(solution)/shard_map/ppermute | solution.py:45
  72.8 1.9 collective-permute-start.9
  74.7 9.2 %collective-permute-done.11.refs_1_.refs_3_.refs_7_ = bf16[256,2048]{1,0:T(8,128)(2,1)S(1)} collective-permute-done((bf16[256,2048]{1,0:T(8,128)(2,1)S(1)}, bf16[256,2048]{1,0:T(8,128)(2,1)S(1)}, u32[]{:S(2)}, u32[]{:S(2)}) %collective-permute-start.11) | collective-permute-done | bytes 1048608 | tf_op jit(solution)/shard_map/ppermute | solution.py:45
  85.6 4.3 %shard_map.86 = bf16[512,2048]{1,0:T(8,128)(2,1)S(1)} custom-call(s32[2]{0:T(128)S(1)} %pad_add_fusion.place_ref, bf16[256,2048]{1,0:T(8,128)(2,1)S(1)} %shard_map.84.refs_0_.refs_2_.refs_6_, bf16[256,2048]{1,0:T(8,128)(2,1)S(1)} %collective-permute-done.11.refs_1_.refs_3_.refs_7_, bf16[1024,1024]{1,0:T(8,128)(2,1)S(1)} %get-tuple-element.128.refs_2_.refs_3_, ...), custom_call_target="tpu_custom_call" | custom-call | flops 2147483 | bytes 8388 | tf_op jit(solution)/shard_map/pallas_call | solution.py:256
  90.4 4.3 %collective-permute-start.14 = (bf16[256,2048]{1,0:T(8,128)(2,1)S(1)}, bf16[256,2048]{1,0:T(8,128)(2,1)S(1)}, u32[]{:S(2)}, u32[]{:S(2)}) collective-permute-start(bf16[256,2048]{1,0:T(8,128)(2,1)S(1)} %add_convert_fusion.1), channel_id=1, source_target_pairs={{96,0},{97,1},{98,2},{99,3},{100,4},{101,5},{102,6},{103,7},{104,8... | collective-permute-start | bytes 3145736 | tf_op jit(solution)/shard_map/ppermute | solution.py:45
  94.7 4.5 %shard_map.87 = (bf16[256,2048]{1,0:T(8,128)(2,1)S(1)}, bf16[256,2048]{1,0:T(8,128)(2,1)S(1)}) custom-call(s32[2]{0:T(128)S(1)} %pad_add_fusion.place_ref, bf16[256,2048]{1,0:T(8,128)(2,1)S(1)} %shard_map.85.refs_0_.refs_4_, bf16[256,2048]{1,0:T(8,128)(2,1)S(1)} %collective-permute-done.13.refs_1_.refs_5_, ...), custom_call_target="tpu_custom_call" | custom-call | flops 2147483 | bytes 8388 | tf_op jit(solution)/shard_map/pallas_call | solution.py:256
  99.1 8.3 %collective-permute-done.14 = bf16[256,2048]{1,0:T(8,128)(2,1)S(1)} collective-permute-done((bf16[256,2048]{1,0:T(8,128)(2,1)S(1)}, bf16[256,2048]{1,0:T(8,128)(2,1)S(1)}, u32[]{:S(2)}, u32[]{:S(2)}) %collective-permute-start.14) | collective-permute-done | bytes 1048608 | tf_op jit(solution)/shard_map/ppermute | solution.py:45
  108.6 2.0 collective-permute-start.20
  110.6 12.8 %collective-permute-done.16.refs_1_.refs_5_ = bf16[256,2048]{1,0:T(8,128)(2,1)S(1)} collective-permute-done((bf16[256,2048]{1,0:T(8,128)(2,1)S(1)}, bf16[256,2048]{1,0:T(8,128)(2,1)S(1)}, u32[]{:S(2)}, u32[]{:S(2)}) %collective-permute-start.16) | collective-permute-done | bytes 1048608 | tf_op jit(solution)/shard_map/ppermute | solution.py:45
  123.4 4.3 %shard_map.88 = (bf16[256,2048]{1,0:T(8,128)(2,1)S(1)}, bf16[256,2048]{1,0:T(8,128)(2,1)S(1)}) custom-call(s32[2]{0:T(128)S(1)} %pad_add_fusion.place_ref, bf16[256,2048]{1,0:T(8,128)(2,1)S(1)} %pad_maximum_fusion.refs_0_.refs_4_, bf16[256,2048]{1,0:T(8,128)(2,1)S(1)} %collective-permute-done.16.refs_1_.refs_5_, ...), custom_call_target="tpu_custom_call" | custom-call | flops 2147483 | bytes 8388 | tf_op jit(solution)/shard_map/pallas_call | solution.py:256
  127.7 6.9 %collective-permute-done.20 = bf16[256,2048]{1,0:T(8,128)(2,1)S(1)} collective-permute-done((bf16[256,2048]{1,0:T(8,128)(2,1)S(1)}, bf16[256,2048]{1,0:T(8,128)(2,1)S(1)}, u32[]{:S(2)}, u32[]{:S(2)}) %collective-permute-start.20) | collective-permute-done | bytes 1048608 | tf_op jit(solution)/shard_map/ppermute | solution.py:45
  135.0 3.3 %collective-permute-start.23 = (bf16[256,2048]{1,0:T(8,128)(2,1)S(1)}, bf16[256,2048]{1,0:T(8,128)(2,1)S(1)}, u32[]{:S(2)}, u32[]{:S(2)}) collective-permute-start(bf16[256,2048]{1,0:T(8,128)(2,1)S(1)} %add_convert_fusion), channel_id=1, source_target_pairs={{96,0},{97,1},{98,2},{99,3},{100,4},{101,5},{102,6},{103,7},{104,8... | collective-permute-start | bytes 3145736 | tf_op jit(solution)/shard_map/ppermute | solution.py:45
  139.2 4.3 %shard_map.89 = (bf16[256,2048]{1,0:T(8,128)(2,1)S(1)}, bf16[256,2048]{1,0:T(8,128)(2,1)S(1)}) custom-call(s32[2]{0:T(128)S(1)} %pad_add_fusion.place_ref, bf16[256,2048]{1,0:T(8,128)(2,1)S(1)} %collective-permute-done.18.refs_0_.refs_6_.refs_2_, bf16[256,2048]{1,0:T(8,128)(2,1)S(1)} %collective-permute-done.19.refs_1_.refs_7_.refs_3_, ...), custom_call_target="tpu_custom_call" | custom-call | flops 2147483 | bytes 8388 | tf_op jit(solution)/shard_map/pallas_call | solution.py:256
  143.5 2.5 %collective-permute-start.21 = (bf16[256,2048]{1,0:T(8,128)(2,1)S(1)}, bf16[256,2048]{1,0:T(8,128)(2,1)S(1)}, u32[]{:S(2)}, u32[]{:S(2)}) collective-permute-start(bf16[256,2048]{1,0:T(8,128)(2,1)S(1)} %get-tuple-element.70), channel_id=1, source_target_pairs={{3,0},{2,1},{1,2},{0,3},{7,4},{6,5},{5,6},{4,7},{11,8},{10,9},{9,1... | collective-permute-start | bytes 3145736 | tf_op jit(solution)/shard_map/ppermute | solution.py:45
  146.0 5.6 %shard_map.90.refs_8_ = f32[1024,1024]{1,0:T(8,128)} custom-call(bf16[256,2048]{1,0:T(8,128)(2,1)S(1)} %shard_map.80.refs_0_.refs_4_, bf16[256,2048]{1,0:T(8,128)(2,1)} %collective-permute-done.5.refs_1_.refs_5_, bf16[256,2048]{1,0:T(8,128)(2,1)S(1)} %shard_map.81.refs_0_.refs_2_.refs_6_, ...), custom_call_target="tpu_custom_call" | custom-call | flops 2147483 | bytes 5242 | tf_op jit(solution)/shard_map/pallas_call | solution.py:305
  154.3 4.4 %collective-permute-done.21 = bf16[256,2048]{1,0:T(8,128)(2,1)S(1)} collective-permute-done((bf16[256,2048]{1,0:T(8,128)(2,1)S(1)}, bf16[256,2048]{1,0:T(8,128)(2,1)S(1)}, u32[]{:S(2)}, u32[]{:S(2)}) %collective-permute-start.21) | collective-permute-done | bytes 1048608 | tf_op jit(solution)/shard_map/ppermute | solution.py:45
  159.9 2.9 %collective-permute-start.25 = (bf16[128,2048]{1,0:T(8,128)(2,1)S(1)}, bf16[128,2048]{1,0:T(8,128)(2,1)S(1)}, u32[]{:S(2)}, u32[]{:S(2)}) collective-permute-start(bf16[128,2048]{1,0:T(8,128)(2,1)S(1)} %slice.246), channel_id=1, source_target_pairs={{1,0},{0,1},{3,2},{2,3},{5,4},{4,5},{7,6},{6,7},{9,8},{8,9},{11,10... | collective-permute-start | bytes 1572872 | tf_op jit(solution)/shard_map/ppermute | solution.py:45
  162.8 5.5 %shard_map.91.refs_8_ = f32[1024,1024]{1,0:T(8,128)} custom-call(bf16[256,2048]{1,0:T(8,128)(2,1)S(1)} %pad_maximum_fusion.refs_0_.refs_4_, bf16[256,2048]{1,0:T(8,128)(2,1)S(1)} %collective-permute-done.16.refs_1_.refs_5_, bf16[256,2048]{1,0:T(8,128)(2,1)S(1)} %collective-permute-done.18.refs_0_.refs_6_.refs_2_, ...), custom_call_target="tpu_custom_call" | custom-call | flops 2147483 | bytes 5242 | tf_op jit(solution)/shard_map/pallas_call | solution.py:305
  169.9 3.1 %shard_map.92 = bf16[256,2048]{1,0:T(8,128)(2,1)S(1)} custom-call(s32[2]{0:T(128)S(1)} %pad_add_fusion.place_ref, bf16[256,2048]{1,0:T(8,128)(2,1)S(1)} %pad_maximum_fusion.1.refs_0_.refs_4_, bf16[256,2048]{1,0:T(8,128)(2,1)S(1)} %collective-permute-done.24.refs_1_.refs_5_, bf16[1024,1024]{1,0:T(8,128)(2,1)S(1)} %get-tuple-element.127.refs_3_.refs_2_, ...), custom_call_target="tpu_custom_call" | custom-call | flops 2147483 | bytes 8388 | tf_op jit(solution)/shard_map/pallas_call | solution.py:256
  173.1 3.0 %collective-permute-start.28 = (bf16[256,2048]{1,0:T(8,128)(2,1)S(1)}, bf16[256,2048]{1,0:T(8,128)(2,1)S(1)}, u32[]{:S(2)}, u32[]{:S(2)}) collective-permute-start(bf16[256,2048]{1,0:T(8,128)(2,1)S(1)} %shard_map.92), channel_id=1, source_target_pairs={{12,0},{13,1},{14,2},{15,3},{8,4},{9,5},{10,6},{11,7},{4,8},{5,9},... | collective-permute-start | bytes 3145736 | tf_op jit(solution)/shard_map/ppermute | solution.py:45
  176.3 3.1 %shard_map.93 = bf16[256,2048]{1,0:T(8,128)(2,1)S(1)} custom-call(s32[2]{0:T(128)S(1)} %pad_add_fusion.place_ref, bf16[256,2048]{1,0:T(8,128)(2,1)S(1)} %collective-permute-done.26.refs_0_.refs_6_.refs_2_, bf16[256,2048]{1,0:T(8,128)(2,1)S(1)} %collective-permute-done.27.refs_1_.refs_7_.refs_3_, bf16[1024,1024]{1,0:T(8,128)(2,1)S(1)} %get-tuple-element.127.refs_3_.refs_2_, ...), custom_call_target="tpu_custom_call" | custom-call | flops 2147483 | bytes 8388 | tf_op jit(solution)/shard_map/pallas_call | solution.py:256
  179.4 2.5 %collective-permute-start.29 = (bf16[256,2048]{1,0:T(8,128)(2,1)S(1)}, bf16[256,2048]{1,0:T(8,128)(2,1)S(1)}, u32[]{:S(2)}, u32[]{:S(2)}) collective-permute-start(bf16[256,2048]{1,0:T(8,128)(2,1)S(1)} %shard_map.93), channel_id=1, source_target_pairs={{3,0},{2,1},{1,2},{0,3},{7,4},{6,5},{5,6},{4,7},{11,8},{10,9},{9,1... | collective-permute-start | bytes 3145736 | tf_op jit(solution)/shard_map/ppermute | solution.py:45
  182.2 3.2 %shard_map.94 = bf16[256,2048]{1,0:T(8,128)(2,1)S(1)} custom-call(s32[2]{0:T(128)S(1)} %pad_add_fusion.place_ref, bf16[256,2048]{1,0:T(8,128)(2,1)S(1)} %pad_maximum_fusion.1.refs_0_.refs_4_, bf16[256,2048]{1,0:T(8,128)(2,1)S(1)} %collective-permute-done.24.refs_1_.refs_5_, bf16[1024,1024]{1,0:T(8,128)(2,1)S(1)} %get-tuple-element.127.refs_3_.refs_2_, ...), custom_call_target="tpu_custom_call" | custom-call | flops 2147483 | bytes 8388 | tf_op jit(solution)/shard_map/pallas_call | solution.py:256
  185.3 3.1 %shard_map.95 = bf16[256,2048]{1,0:T(8,128)(2,1)S(1)} custom-call(s32[2]{0:T(128)S(1)} %pad_add_fusion.place_ref, bf16[256,2048]{1,0:T(8,128)(2,1)S(1)} %collective-permute-done.26.refs_0_.refs_6_.refs_2_, bf16[256,2048]{1,0:T(8,128)(2,1)S(1)} %collective-permute-done.27.refs_1_.refs_7_.refs_3_, bf16[1024,1024]{1,0:T(8,128)(2,1)S(1)} %get-tuple-element.127.refs_3_.refs_2_, ...), custom_call_target="tpu_custom_call" | custom-call | flops 2147483 | bytes 8388 | tf_op jit(solution)/shard_map/pallas_call | solution.py:256
  188.5 6.5 %shard_map.96 = f32[1024,1024]{1,0:T(8,128)} custom-call(bf16[256,2048]{1,0:T(8,128)(2,1)S(1)} %shard_map.85.refs_0_.refs_4_, bf16[256,2048]{1,0:T(8,128)(2,1)S(1)} %collective-permute-done.13.refs_1_.refs_5_, bf16[256,2048]{1,0:T(8,128)(2,1)S(1)} %shard_map.84.refs_0_.refs_2_.refs_6_, ...), custom_call_target="tpu_custom_call", output_to_operand_aliasing={{}: (8, {})} | custom-call | flops 2147483 | bytes 5242 | tf_op jit(solution)/shard_map/pallas_call | solution.py:305
  197.4 2.7 %collective-permute-start.31 = (bf16[128,2048]{1,0:T(8,128)(2,1)S(1)}, bf16[128,2048]{1,0:T(8,128)(2,1)S(1)}, u32[]{:S(2)}, u32[]{:S(2)}) collective-permute-start(bf16[128,2048]{1,0:T(8,128)(2,1)S(1)} %slice.244), channel_id=1, source_target_pairs={{1,0},{0,1},{3,2},{2,3},{5,4},{4,5},{7,6},{6,7},{9,8},{8,9},{11,10... | collective-permute-start | bytes 1572872 | tf_op jit(solution)/shard_map/ppermute | solution.py:45
  200.1 6.5 %shard_map.97 = f32[1024,1024]{1,0:T(8,128)} custom-call(bf16[256,2048]{1,0:T(8,128)(2,1)S(1)} %pad_maximum_fusion.1.refs_0_.refs_4_, bf16[256,2048]{1,0:T(8,128)(2,1)S(1)} %collective-permute-done.24.refs_1_.refs_5_, bf16[256,2048]{1,0:T(8,128)(2,1)S(1)} %collective-permute-done.26.refs_0_.refs_6_.refs_2_, ...), custom_call_target="tpu_custom_call", output_to_operand_aliasing={{}: (8, {})} | custom-call | flops 2147483 | bytes 5242 | tf_op jit(solution)/shard_map/pallas_call | solution.py:305
  207.7 3.2 %collective-permute-start.32 = (bf16[128,2048]{1,0:T(8,128)(2,1)S(1)}, bf16[128,2048]{1,0:T(8,128)(2,1)S(1)}, u32[]{:S(2)}, u32[]{:S(2)}) collective-permute-start(bf16[128,2048]{1,0:T(8,128)(2,1)S(1)} %pad_maximum_fusion.2), channel_id=1, source_target_pairs={{3,0},{2,1},{1,2},{0,3},{7,4},{6,5},{5,6},{4,7},{11,8},{10,9},{9,1... | collective-permute-start | bytes 1572872 | tf_op jit(solution)/shard_map/ppermute | solution.py:45
  211.1 6.9 %collective-permute-done.32 = bf16[128,2048]{1,0:T(8,128)(2,1)S(1)} collective-permute-done((bf16[128,2048]{1,0:T(8,128)(2,1)S(1)}, bf16[128,2048]{1,0:T(8,128)(2,1)S(1)}, u32[]{:S(2)}, u32[]{:S(2)}) %collective-permute-start.32) | collective-permute-done | bytes 524320 | tf_op jit(solution)/shard_map/ppermute | solution.py:45
  218.1 4.5 %collective-permute-done.33 = bf16[128,2048]{1,0:T(8,128)(2,1)S(1)} collective-permute-done((bf16[128,2048]{1,0:T(8,128)(2,1)S(1)}, bf16[128,2048]{1,0:T(8,128)(2,1)S(1)}, u32[]{:S(2)}, u32[]{:S(2)}) %collective-permute-start.33) | collective-permute-done | bytes 524320 | tf_op jit(solution)/shard_map/ppermute | solution.py:45
  223.4 4.8 %collective-permute-start.34 = (bf16[64,2048]{1,0:T(8,128)(2,1)}, bf16[64,2048]{1,0:T(8,128)(2,1)S(1)}, u32[]{:S(2)}, u32[]{:S(2)}) collective-permute-start(bf16[64,2048]{1,0:T(8,128)(2,1)} %fusion.15), channel_id=1, source_target_pairs={{1,0},{0,1},{3,2},{2,3},{5,4},{4,5},{7,6},{6,7},{9,8},{8,9},{11,10... | collective-permute-start | bytes 786440 | tf_op jit(solution)/shard_map/ppermute | solution.py:45
  229.1 3.7 %collective-permute-done.34 = bf16[64,2048]{1,0:T(8,128)(2,1)S(1)} collective-permute-done((bf16[64,2048]{1,0:T(8,128)(2,1)}, bf16[64,2048]{1,0:T(8,128)(2,1)S(1)}, u32[]{:S(2)}, u32[]{:S(2)}) %collective-permute-start.34) | collective-permute-done | bytes 262176 | tf_op jit(solution)/shard_map/ppermute | solution.py:45
  232.8 3.0 %collective-permute-done.35 = bf16[64,2048]{1,0:T(8,128)(2,1)} collective-permute-done((bf16[64,2048]{1,0:T(8,128)(2,1)}, bf16[64,2048]{1,0:T(8,128)(2,1)}, u32[]{:S(2)}, u32[]{:S(2)}) %collective-permute-start.35) | collective-permute-done | bytes 262176 | tf_op jit(solution)/shard_map/ppermute | solution.py:45
  (100 shorter events, 32.9 us)
Async XLA Ops:
  0.7 1.0 copy-start.4
  1.7 0.9 copy-start.5
  3.3 6.5 %collective-permute-start = (bf16[64,2048]{1,0:T(8,128)(2,1)S(1)}, bf16[64,2048]{1,0:T(8,128)(2,1)S(1)}, u32[]{:S(2)}, u32[]{:S(2)}) collective-permute-start(bf16[64,2048]{1,0:T(8,128)(2,1)S(1)} %get-tuple-element.47.a_ref), channel_id=1, source_target_pairs={{4,0},{5,1},{6,2},{7,3},{0,4},{1,5},{2,6},{3,7},{12,8},{13,9},{14,... | collective-permute-start | bytes 786440 | tf_op jit(solution)/shard_map/ppermute | solution.py:45
  4.9 8.3 %collective-permute-start.2 = (bf16[64,2048]{1,0:T(8,128)(2,1)S(1)}, bf16[64,2048]{1,0:T(8,128)(2,1)S(1)}, u32[]{:S(2)}, u32[]{:S(2)}) collective-permute-start(bf16[64,2048]{1,0:T(8,128)(2,1)S(1)} %get-tuple-element.49.a_ref), channel_id=1, source_target_pairs={{1,0},{0,1},{3,2},{2,3},{5,4},{4,5},{7,6},{6,7},{9,8},{8,9},{11,10... | collective-permute-start | bytes 786440 | tf_op jit(solution)/shard_map/ppermute | solution.py:45
  10.3 10.5 %collective-permute-start.1 = (bf16[128,2048]{1,0:T(8,128)(2,1)S(1)}, bf16[128,2048]{1,0:T(8,128)(2,1)S(1)}, u32[]{:S(2)}, u32[]{:S(2)}) collective-permute-start(bf16[128,2048]{1,0:T(8,128)(2,1)S(1)} %shard_map.76), channel_id=1, source_target_pairs={{12,0},{13,1},{14,2},{15,3},{8,4},{9,5},{10,6},{11,7},{4,8},{5,9},... | collective-permute-start | bytes 1572872 | tf_op jit(solution)/shard_map/ppermute | solution.py:45
  13.8 9.3 %collective-permute-start.3 = (bf16[128,2048]{1,0:T(8,128)(2,1)S(1)}, bf16[128,2048]{1,0:T(8,128)(2,1)S(1)}, u32[]{:S(2)}, u32[]{:S(2)}) collective-permute-start(bf16[128,2048]{1,0:T(8,128)(2,1)S(1)} %shard_map.78), channel_id=1, source_target_pairs={{3,0},{2,1},{1,2},{0,3},{7,4},{6,5},{5,6},{4,7},{11,8},{10,9},{9,1... | collective-permute-start | bytes 1572872 | tf_op jit(solution)/shard_map/ppermute | solution.py:45
  21.4 0.8 copy-start
  23.7 0.8 copy-start.2
  24.5 9.2 %collective-permute-start.6 = (bf16[128,2048]{1,0:T(8,128)(2,1)S(1)}, bf16[128,2048]{1,0:T(8,128)(2,1)S(1)}, u32[]{:S(2)}, u32[]{:S(2)}) collective-permute-start(bf16[128,2048]{1,0:T(8,128)(2,1)S(1)} %get-tuple-element.52.a_ref), channel_id=1, source_target_pairs={{4,0},{5,1},{6,2},{7,3},{0,4},{1,5},{2,6},{3,7},{12,8},{13,9},{14,... | collective-permute-start | bytes 1572872 | tf_op jit(solution)/shard_map/ppermute | solution.py:45
  24.7 11.6 %collective-permute-start.4 = (bf16[128,2048]{1,0:T(8,128)(2,1)S(1)}, bf16[128,2048]{1,0:T(8,128)(2,1)S(1)}, u32[]{:S(2)}, u32[]{:S(2)}) collective-permute-start(bf16[128,2048]{1,0:T(8,128)(2,1)S(1)} %get-tuple-element.51.a_ref), channel_id=1, source_target_pairs={{1,0},{0,1},{3,2},{2,3},{5,4},{4,5},{7,6},{6,7},{9,8},{8,9},{11,10... | collective-permute-start | bytes 1572872 | tf_op jit(solution)/shard_map/ppermute | solution.py:45
  34.3 16.1 %collective-permute-start.7 = (bf16[256,2048]{1,0:T(8,128)(2,1)S(1)}, bf16[256,2048]{1,0:T(8,128)(2,1)S(1)}, u32[]{:S(2)}, u32[]{:S(2)}) collective-permute-start(bf16[256,2048]{1,0:T(8,128)(2,1)S(1)} %shard_map.81.refs_0_.refs_2_.refs_6_), channel_id=1, source_target_pairs={{12,0},{13,1},{14,2},{15,3},{8,4},{9,5},{10,6},{11,7},{4,8},{5,9},... | collective-permute-start | bytes 3145736 | tf_op jit(solution)/shard_map/ppermute | solution.py:45
  36.9 15.0 %collective-permute-start.5 = (bf16[256,2048]{1,0:T(8,128)(2,1)S(1)}, bf16[256,2048]{1,0:T(8,128)(2,1)}, u32[]{:S(2)}, u32[]{:S(2)}) collective-permute-start(bf16[256,2048]{1,0:T(8,128)(2,1)S(1)} %shard_map.80.refs_0_.refs_4_), channel_id=1, source_target_pairs={{3,0},{2,1},{1,2},{0,3},{7,4},{6,5},{5,6},{4,7},{11,8},{10,9},{9,1... | collective-permute-start | bytes 3145736 | tf_op jit(solution)/shard_map/ppermute | solution.py:45
  51.9 4.4 %copy-start.1 = (bf16[128,2048]{1,0:T(8,128)(2,1)S(1)}, bf16[128,2048]{1,0:T(8,128)(2,1)}, u32[]{:S(2)}) copy-start(bf16[128,2048]{1,0:T(8,128)(2,1)} %copy-done) | copy-start | bytes 1572868
  51.9 6.1 %copy-start.3 = (bf16[128,2048]{1,0:T(8,128)(2,1)S(1)}, bf16[128,2048]{1,0:T(8,128)(2,1)}, u32[]{:S(2)}) copy-start(bf16[128,2048]{1,0:T(8,128)(2,1)} %copy-done.2) | copy-start | bytes 1572868
  56.2 4.2 %collective-permute-start.8 = (bf16[512,2048]{1,0:T(8,128)(2,1)S(1)}, bf16[512,2048]{1,0:T(8,128)(2,1)S(1)}, u32[]{:S(2)}, u32[]{:S(2)}) collective-permute-start(bf16[512,2048]{1,0:T(8,128)(2,1)S(1)} %shard_map.82), channel_id=1, source_target_pairs={{16,0},{17,1},{18,2},{19,3},{20,4},{21,5},{22,6},{23,7},{24,8},{25... | collective-permute-start | bytes 6291464 | tf_op jit(solution)/shard_map/ppermute | solution.py:45
  56.3 9.5 %collective-permute-start.12 = (bf16[128,2048]{1,0:T(8,128)(2,1)S(1)}, bf16[128,2048]{1,0:T(8,128)(2,1)S(1)}, u32[]{:S(2)}, u32[]{:S(2)}) collective-permute-start(bf16[128,2048]{1,0:T(8,128)(2,1)S(1)} %copy-done.1), channel_id=1, source_target_pairs={{1,0},{0,1},{3,2},{2,3},{5,4},{4,5},{7,6},{6,7},{9,8},{8,9},{11,10... | collective-permute-start | bytes 1572872 | tf_op jit(solution)/shard_map/ppermute | solution.py:45
  58.0 9.2 %collective-permute-start.10 = (bf16[128,2048]{1,0:T(8,128)(2,1)S(1)}, bf16[128,2048]{1,0:T(8,128)(2,1)S(1)}, u32[]{:S(2)}, u32[]{:S(2)}) collective-permute-start(bf16[128,2048]{1,0:T(8,128)(2,1)S(1)} %copy-done.3), channel_id=1, source_target_pairs={{4,0},{5,1},{6,2},{7,3},{0,4},{1,5},{2,6},{3,7},{12,8},{13,9},{14,... | collective-permute-start | bytes 1572872 | tf_op jit(solution)/shard_map/ppermute | solution.py:45
  67.8 16.1 %collective-permute-start.11 = (bf16[256,2048]{1,0:T(8,128)(2,1)S(1)}, bf16[256,2048]{1,0:T(8,128)(2,1)S(1)}, u32[]{:S(2)}, u32[]{:S(2)}) collective-permute-start(bf16[256,2048]{1,0:T(8,128)(2,1)S(1)} %shard_map.84.refs_0_.refs_2_.refs_6_), channel_id=1, source_target_pairs={{12,0},{13,1},{14,2},{15,3},{8,4},{9,5},{10,6},{11,7},{4,8},{5,9},... | collective-permute-start | bytes 3145736 | tf_op jit(solution)/shard_map/ppermute | solution.py:45
  70.4 15.2 %collective-permute-start.13 = (bf16[256,2048]{1,0:T(8,128)(2,1)S(1)}, bf16[256,2048]{1,0:T(8,128)(2,1)S(1)}, u32[]{:S(2)}, u32[]{:S(2)}) collective-permute-start(bf16[256,2048]{1,0:T(8,128)(2,1)S(1)} %shard_map.85.refs_0_.refs_4_), channel_id=1, source_target_pairs={{3,0},{2,1},{1,2},{0,3},{7,4},{6,5},{5,6},{4,7},{11,8},{10,9},{9,1... | collective-permute-start | bytes 3145736 | tf_op jit(solution)/shard_map/ppermute | solution.py:45
  72.8 17.2 %collective-permute-start.9 = (bf16[256,2048]{1,0:T(8,128)(2,1)S(1)}, bf16[256,2048]{1,0:T(8,128)(2,1)S(1)}, u32[]{:S(2)}, u32[]{:S(2)}) collective-permute-start(bf16[256,2048]{1,0:T(8,128)(2,1)S(1)} %get-tuple-element.55), channel_id=1, source_target_pairs={{32,0},{33,1},{34,2},{35,3},{36,4},{37,5},{38,6},{39,7},{40,8},{41... | collective-permute-start | bytes 3145736 | tf_op jit(solution)/shard_map/ppermute | solution.py:45
  89.9 4.8 %collective-permute-start.15 = (bf16[512,2048]{1,0:T(8,128)(2,1)S(1)}, bf16[512,2048]{1,0:T(8,128)(2,1)S(1)}, u32[]{:S(2)}, u32[]{:S(2)}) collective-permute-start(bf16[512,2048]{1,0:T(8,128)(2,1)S(1)} %shard_map.86), channel_id=1, source_target_pairs={{16,0},{17,1},{18,2},{19,3},{20,4},{21,5},{22,6},{23,7},{24,8},{25... | collective-permute-start | bytes 6291464 | tf_op jit(solution)/shard_map/ppermute | solution.py:45
  90.4 17.1 %collective-permute-start.14 = (bf16[256,2048]{1,0:T(8,128)(2,1)S(1)}, bf16[256,2048]{1,0:T(8,128)(2,1)S(1)}, u32[]{:S(2)}, u32[]{:S(2)}) collective-permute-start(bf16[256,2048]{1,0:T(8,128)(2,1)S(1)} %add_convert_fusion.1), channel_id=1, source_target_pairs={{96,0},{97,1},{98,2},{99,3},{100,4},{101,5},{102,6},{103,7},{104,8... | collective-permute-start | bytes 3145736 | tf_op jit(solution)/shard_map/ppermute | solution.py:45
  108.5 14.9 %collective-permute-start.16 = (bf16[256,2048]{1,0:T(8,128)(2,1)S(1)}, bf16[256,2048]{1,0:T(8,128)(2,1)S(1)}, u32[]{:S(2)}, u32[]{:S(2)}) collective-permute-start(bf16[256,2048]{1,0:T(8,128)(2,1)S(1)} %pad_maximum_fusion.refs_0_.refs_4_), channel_id=1, source_target_pairs={{32,0},{33,1},{34,2},{35,3},{36,4},{37,5},{38,6},{39,7},{40,8},{41... | collective-permute-start | bytes 3145736 | tf_op jit(solution)/shard_map/ppermute | solution.py:45
  108.6 26.0 %collective-permute-start.20 = (bf16[256,2048]{1,0:T(8,128)(2,1)S(1)}, bf16[256,2048]{1,0:T(8,128)(2,1)S(1)}, u32[]{:S(2)}, u32[]{:S(2)}) collective-permute-start(bf16[256,2048]{1,0:T(8,128)(2,1)S(1)} %get-tuple-element.66), channel_id=1, source_target_pairs={{32,0},{33,1},{34,2},{35,3},{36,4},{37,5},{38,6},{39,7},{40,8},{41... | collective-permute-start | bytes 3145736 | tf_op jit(solution)/shard_map/ppermute | solution.py:45
  110.6 28.6 %collective-permute-start.18 = (bf16[256,2048]{1,0:T(8,128)(2,1)S(1)}, bf16[256,2048]{1,0:T(8,128)(2,1)S(1)}, u32[]{:S(2)}, u32[]{:S(2)}) collective-permute-start(bf16[256,2048]{1,0:T(8,128)(2,1)S(1)} %pad_maximum_fusion.refs_0_.refs_4_), channel_id=1, source_target_pairs={{16,0},{17,1},{18,2},{19,3},{20,4},{21,5},{22,6},{23,7},{24,8},{25... | collective-permute-start | bytes 3145736 | tf_op jit(solution)/shard_map/ppermute | solution.py:45
  134.6 4.6 %collective-permute-start.19 = (bf16[256,2048]{1,0:T(8,128)(2,1)S(1)}, bf16[256,2048]{1,0:T(8,128)(2,1)S(1)}, u32[]{:S(2)}, u32[]{:S(2)}) collective-permute-start(bf16[256,2048]{1,0:T(8,128)(2,1)S(1)} %collective-permute-done.16.refs_1_.refs_5_), channel_id=1, source_target_pairs={{16,0},{17,1},{18,2},{19,3},{20,4},{21,5},{22,6},{23,7},{24,8},{25... | collective-permute-start | bytes 3145736 | tf_op jit(solution)/shard_map/ppermute | solution.py:45
  135.0 16.6 %collective-permute-start.23 = (bf16[256,2048]{1,0:T(8,128)(2,1)S(1)}, bf16[256,2048]{1,0:T(8,128)(2,1)S(1)}, u32[]{:S(2)}, u32[]{:S(2)}) collective-permute-start(bf16[256,2048]{1,0:T(8,128)(2,1)S(1)} %add_convert_fusion), channel_id=1, source_target_pairs={{96,0},{97,1},{98,2},{99,3},{100,4},{101,5},{102,6},{103,7},{104,8... | collective-permute-start | bytes 3145736 | tf_op jit(solution)/shard_map/ppermute | solution.py:45
  138.3 16.0 %collective-permute-start.17 = (bf16[256,2048]{1,0:T(8,128)(2,1)S(1)}, bf16[256,2048]{1,0:T(8,128)(2,1)S(1)}, u32[]{:S(2)}, u32[]{:S(2)}) collective-permute-start(bf16[256,2048]{1,0:T(8,128)(2,1)S(1)} %get-tuple-element.65), channel_id=1, source_target_pairs={{12,0},{13,1},{14,2},{15,3},{8,4},{9,5},{10,6},{11,7},{4,8},{5,9},... | collective-permute-start | bytes 3145736 | tf_op jit(solution)/shard_map/ppermute | solution.py:45
  143.5 15.3 %collective-permute-start.21 = (bf16[256,2048]{1,0:T(8,128)(2,1)S(1)}, bf16[256,2048]{1,0:T(8,128)(2,1)S(1)}, u32[]{:S(2)}, u32[]{:S(2)}) collective-permute-start(bf16[256,2048]{1,0:T(8,128)(2,1)S(1)} %get-tuple-element.70), channel_id=1, source_target_pairs={{3,0},{2,1},{1,2},{0,3},{7,4},{6,5},{5,6},{4,7},{11,8},{10,9},{9,1... | collective-permute-start | bytes 3145736 | tf_op jit(solution)/shard_map/ppermute | solution.py:45
  152.6 17.3 %collective-permute-start.26 = (bf16[256,2048]{1,0:T(8,128)(2,1)S(1)}, bf16[256,2048]{1,0:T(8,128)(2,1)S(1)}, u32[]{:S(2)}, u32[]{:S(2)}) collective-permute-start(bf16[256,2048]{1,0:T(8,128)(2,1)S(1)} %pad_maximum_fusion.1.refs_0_.refs_4_), channel_id=1, source_target_pairs={{16,0},{17,1},{18,2},{19,3},{20,4},{21,5},{22,6},{23,7},{24,8},{25... | collective-permute-start | bytes 3145736 | tf_op jit(solution)/shard_map/ppermute | solution.py:45
  152.7 15.6 %collective-permute-start.24 = (bf16[256,2048]{1,0:T(8,128)(2,1)S(1)}, bf16[256,2048]{1,0:T(8,128)(2,1)S(1)}, u32[]{:S(2)}, u32[]{:S(2)}) collective-permute-start(bf16[256,2048]{1,0:T(8,128)(2,1)S(1)} %pad_maximum_fusion.1.refs_0_.refs_4_), channel_id=1, source_target_pairs={{32,0},{33,1},{34,2},{35,3},{36,4},{37,5},{38,6},{39,7},{40,8},{41... | collective-permute-start | bytes 3145736 | tf_op jit(solution)/shard_map/ppermute | solution.py:45
  159.2 9.3 %collective-permute-start.22 = (bf16[128,2048]{1,0:T(8,128)(2,1)S(1)}, bf16[128,2048]{1,0:T(8,128)(2,1)S(1)}, u32[]{:S(2)}, u32[]{:S(2)}) collective-permute-start(bf16[128,2048]{1,0:T(8,128)(2,1)S(1)} %slice.247), channel_id=1, source_target_pairs={{4,0},{5,1},{6,2},{7,3},{0,4},{1,5},{2,6},{3,7},{12,8},{13,9},{14,... | collective-permute-start | bytes 1572872 | tf_op jit(solution)/shard_map/ppermute | solution.py:45
  159.9 10.0 %collective-permute-start.25 = (bf16[128,2048]{1,0:T(8,128)(2,1)S(1)}, bf16[128,2048]{1,0:T(8,128)(2,1)S(1)}, u32[]{:S(2)}, u32[]{:S(2)}) collective-permute-start(bf16[128,2048]{1,0:T(8,128)(2,1)S(1)} %slice.246), channel_id=1, source_target_pairs={{1,0},{0,1},{3,2},{2,3},{5,4},{4,5},{7,6},{6,7},{9,8},{8,9},{11,10... | collective-permute-start | bytes 1572872 | tf_op jit(solution)/shard_map/ppermute | solution.py:45
  169.9 6.3 %collective-permute-start.27 = (bf16[256,2048]{1,0:T(8,128)(2,1)S(1)}, bf16[256,2048]{1,0:T(8,128)(2,1)S(1)}, u32[]{:S(2)}, u32[]{:S(2)}) collective-permute-start(bf16[256,2048]{1,0:T(8,128)(2,1)S(1)} %collective-permute-done.24.refs_1_.refs_5_), channel_id=1, source_target_pairs={{16,0},{17,1},{18,2},{19,3},{20,4},{21,5},{22,6},{23,7},{24,8},{25... | collective-permute-start | bytes 3145736 | tf_op jit(solution)/shard_map/ppermute | solution.py:45
  173.1 21.9 %collective-permute-start.28 = (bf16[256,2048]{1,0:T(8,128)(2,1)S(1)}, bf16[256,2048]{1,0:T(8,128)(2,1)S(1)}, u32[]{:S(2)}, u32[]{:S(2)}) collective-permute-start(bf16[256,2048]{1,0:T(8,128)(2,1)S(1)} %shard_map.92), channel_id=1, source_target_pairs={{12,0},{13,1},{14,2},{15,3},{8,4},{9,5},{10,6},{11,7},{4,8},{5,9},... | collective-permute-start | bytes 3145736 | tf_op jit(solution)/shard_map/ppermute | solution.py:45
  179.4 15.6 %collective-permute-start.29 = (bf16[256,2048]{1,0:T(8,128)(2,1)S(1)}, bf16[256,2048]{1,0:T(8,128)(2,1)S(1)}, u32[]{:S(2)}, u32[]{:S(2)}) collective-permute-start(bf16[256,2048]{1,0:T(8,128)(2,1)S(1)} %shard_map.93), channel_id=1, source_target_pairs={{3,0},{2,1},{1,2},{0,3},{7,4},{6,5},{5,6},{4,7},{11,8},{10,9},{9,1... | collective-permute-start | bytes 3145736 | tf_op jit(solution)/shard_map/ppermute | solution.py:45
  195.4 11.2 %collective-permute-start.30 = (bf16[128,2048]{1,0:T(8,128)(2,1)S(1)}, bf16[128,2048]{1,0:T(8,128)(2,1)S(1)}, u32[]{:S(2)}, u32[]{:S(2)}) collective-permute-start(bf16[128,2048]{1,0:T(8,128)(2,1)S(1)} %slice.245), channel_id=1, source_target_pairs={{4,0},{5,1},{6,2},{7,3},{0,4},{1,5},{2,6},{3,7},{12,8},{13,9},{14,... | collective-permute-start | bytes 1572872 | tf_op jit(solution)/shard_map/ppermute | solution.py:45
  197.4 9.9 %collective-permute-start.31 = (bf16[128,2048]{1,0:T(8,128)(2,1)S(1)}, bf16[128,2048]{1,0:T(8,128)(2,1)S(1)}, u32[]{:S(2)}, u32[]{:S(2)}) collective-permute-start(bf16[128,2048]{1,0:T(8,128)(2,1)S(1)} %slice.244), channel_id=1, source_target_pairs={{1,0},{0,1},{3,2},{2,3},{5,4},{4,5},{7,6},{6,7},{9,8},{8,9},{11,10... | collective-permute-start | bytes 1572872 | tf_op jit(solution)/shard_map/ppermute | solution.py:45
  207.7 10.4 %collective-permute-start.32 = (bf16[128,2048]{1,0:T(8,128)(2,1)S(1)}, bf16[128,2048]{1,0:T(8,128)(2,1)S(1)}, u32[]{:S(2)}, u32[]{:S(2)}) collective-permute-start(bf16[128,2048]{1,0:T(8,128)(2,1)S(1)} %pad_maximum_fusion.2), channel_id=1, source_target_pairs={{3,0},{2,1},{1,2},{0,3},{7,4},{6,5},{5,6},{4,7},{11,8},{10,9},{9,1... | collective-permute-start | bytes 1572872 | tf_op jit(solution)/shard_map/ppermute | solution.py:45
  211.0 11.6 %collective-permute-start.33 = (bf16[128,2048]{1,0:T(8,128)(2,1)S(1)}, bf16[128,2048]{1,0:T(8,128)(2,1)S(1)}, u32[]{:S(2)}, u32[]{:S(2)}) collective-permute-start(bf16[128,2048]{1,0:T(8,128)(2,1)S(1)} %pad_maximum_fusion.3), channel_id=1, source_target_pairs={{12,0},{13,1},{14,2},{15,3},{8,4},{9,5},{10,6},{11,7},{4,8},{5,9},... | collective-permute-start | bytes 1572872 | tf_op jit(solution)/shard_map/ppermute | solution.py:45
  223.4 9.3 %collective-permute-start.34 = (bf16[64,2048]{1,0:T(8,128)(2,1)}, bf16[64,2048]{1,0:T(8,128)(2,1)S(1)}, u32[]{:S(2)}, u32[]{:S(2)}) collective-permute-start(bf16[64,2048]{1,0:T(8,128)(2,1)} %fusion.15), channel_id=1, source_target_pairs={{1,0},{0,1},{3,2},{2,3},{5,4},{4,5},{7,6},{6,7},{9,8},{8,9},{11,10... | collective-permute-start | bytes 786440 | tf_op jit(solution)/shard_map/ppermute | solution.py:45
  229.1 6.7 %collective-permute-start.35 = (bf16[64,2048]{1,0:T(8,128)(2,1)}, bf16[64,2048]{1,0:T(8,128)(2,1)}, u32[]{:S(2)}, u32[]{:S(2)}) collective-permute-start(bf16[64,2048]{1,0:T(8,128)(2,1)} %fusion.12), channel_id=1, source_target_pairs={{4,0},{5,1},{6,2},{7,3},{0,4},{1,5},{2,6},{3,7},{12,8},{13,9},{14,... | collective-permute-start | bytes 786440 | tf_op jit(solution)/shard_map/ppermute | solution.py:45

commit v12 on v11

--- a/solution.py
+++ b/solution.py
@@ -471,7 +471,7 @@
     grad_out = grads(1, near_b, rest_b, hid_b, grad_out, got_b[True], got_b[False], grad_in)
     for keep in both_ways:
         total_a[keep] = sums_a[keep] + last_a[keep].astype(F32)
-        total_b[keep] = sums_b[keep] + after(last_b[keep], grad_out, last_b[not keep]).astype(F32)
+        total_b[keep] = sums_b[keep] + after(last_b[keep], grad_out).astype(F32)
 
     part = block // PARTS
     pick = lambda keep, piece: jnp.concatenate(
@@ -486,7 +486,7 @@
         passed = jnp.concatenate([pick(keep, 2), pick(keep, 3)], axis=0).astype(BF)
         gots[keep] = exchange(passed, along(keep, False, 1))
     for keep in both_ways:
-        got = after(gots[keep], gots[not keep]).astype(F32)
+        got = gots[keep].astype(F32)
         last = (pick(keep, 1) + got[block:]).astype(BF)
         done[keep] = (
             pick(keep, 0) + got[:block] + exchange(last, along(keep, False, 0)).astype(F32)

time: 238 us -> 234 us (0.983); the launches traced: 238 us -> 231 us
  waiting for transfers between devices: 95.2 us -> 89.9 us
  starting transfers between devices: 56.8 us -> 54.1 us
    ppermute x36, waiting for transfers between devices: 95.2 us -> 89.9 us  [exchange(): return lax.ppermute(array, AXES, pairs)]
    ppermute x36, starting transfers between devices: 56.8 us -> 54.1 us  [exchange(): return lax.ppermute(array, AXES, pairs)]
  transfers between devices with their start and end apart: 36 -> 36, of which waited for: 22 -> 21; matrix products, arithmetic and copies ran while one was open for 3% -> 4% of each run, Pallas kernels for 26% -> 27%
where the time goes in v12:
time: 234 us; the launch traced here: 231 us
  waiting for transfers between devices  89.9 us (38%)
  Pallas kernels  69.1 us (30%)
  starting transfers between devices  54.1 us (23%)
  other arithmetic  8.64 us (4%)
  local copies, waits for them, and re-layouts  7.54 us (3%)
    ppermute x36, waiting for transfers between devices, exchange(): return lax.ppermute(array, AXES, pairs)  89.9 us
    ppermute x36, starting transfers between devices, exchange(): return lax.ppermute(array, AXES, pairs)  54.1 us
    pallas_call x10, Pallas kernels, pair_dot(): pl.pallas_call(functools.partial(pair_kernel, keep, hidden, more is not N...  39.6 us
    pallas_call x4, Pallas kernels, grad_dot(): pl.pallas_call(functools.partial(grad_kernel, pairs, block, factor, begun...  24.1 us
    pallas_call x8, Pallas kernels, whole(): pl.pallas_call(kernel, in_specs=[pl.BlockSpec(memory_space=pltpu.SMEM)] +...  4.82 us
  transfers between devices with their start and end apart: 36, of which 21 were waited for; matrix products, arithmetic and copies ran while one was open for 4% of the time, Pallas kernels for 27%

profile of v12, /device:TPU:8, one launch (start us, length us, event | category | flops | bytes accessed | tf_op | source)
XLA Modules:
  0.0 230.5 jit_solution(9720569869262301926)
XLA Ops:
  5.3 4.4 %collective-permute-done.b_ref = bf16[64,2048]{1,0:T(8,128)(2,1)S(1)} collective-permute-done((bf16[64,2048]{1,0:T(8,128)(2,1)S(1)}, bf16[64,2048]{1,0:T(8,128)(2,1)S(1)}, u32[]{:S(2)}, u32[]{:S(2)}) %collective-permute-start) | collective-permute-done | bytes 262176 | tf_op jit(solution)/shard_map/ppermute | solution.py:45
  10.3 2.8 %collective-permute-start.1 = (bf16[128,2048]{1,0:T(8,128)(2,1)S(1)}, bf16[128,2048]{1,0:T(8,128)(2,1)S(1)}, u32[]{:S(2)}, u32[]{:S(2)}) collective-permute-start(bf16[128,2048]{1,0:T(8,128)(2,1)S(1)} %shard_map.76), channel_id=1, source_target_pairs={{12,0},{13,1},{14,2},{15,3},{8,4},{9,5},{10,6},{11,7},{4,8},{5,9},... | collective-permute-start | bytes 1572872 | tf_op jit(solution)/shard_map/ppermute | solution.py:45
  13.8 1.7 collective-permute-start.3
  15.4 5.4 %collective-permute-done.1.c_ref = bf16[128,2048]{1,0:T(8,128)(2,1)S(1)} collective-permute-done((bf16[128,2048]{1,0:T(8,128)(2,1)S(1)}, bf16[128,2048]{1,0:T(8,128)(2,1)S(1)}, u32[]{:S(2)}, u32[]{:S(2)}) %collective-permute-start.1) | collective-permute-done | bytes 524320 | tf_op jit(solution)/shard_map/ppermute | solution.py:45
  24.7 1.7 collective-permute-start.4
  26.3 7.3 %collective-permute-done.6.b_ref = bf16[128,2048]{1,0:T(8,128)(2,1)S(1)} collective-permute-done((bf16[128,2048]{1,0:T(8,128)(2,1)S(1)}, bf16[128,2048]{1,0:T(8,128)(2,1)S(1)}, u32[]{:S(2)}, u32[]{:S(2)}) %collective-permute-start.6) | collective-permute-done | bytes 524320 | tf_op jit(solution)/shard_map/ppermute | solution.py:45
  34.3 2.0 collective-permute-start.7
  36.9 1.7 collective-permute-start.5
  38.6 2.7 %constant_dynamic-slice_fusion = (bf16[1024,1024]{1,0:T(8,128)(2,1)S(1)}, bf16[1024,1024]{1,0:T(8,128)(2,1)S(1)}) fusion(bf16[2048,1024]{1,0:T(8,128)(2,1)} %param.7, s32[]{:T(128)S(6)} %select_n.30, bf16[1024,2048]{1,0:T(8,128)(2,1)} %param.6), kind=kLoop, calls=%fused_computation.55 | loop fusion | bytes 8388612 | tf_op jit(solution)/shard_map/dynamic_slice | solution.py:337
  41.3 9.1 %collective-permute-done.7.refs_1_.refs_3_.refs_7_ = bf16[256,2048]{1,0:T(8,128)(2,1)S(1)} collective-permute-done((bf16[256,2048]{1,0:T(8,128)(2,1)S(1)}, bf16[256,2048]{1,0:T(8,128)(2,1)S(1)}, u32[]{:S(2)}, u32[]{:S(2)}) %collective-permute-start.7) | collective-permute-done | bytes 1048608 | tf_op jit(solution)/shard_map/ppermute | solution.py:45
  51.9 4.3 %shard_map.82 = bf16[512,2048]{1,0:T(8,128)(2,1)S(1)} custom-call(s32[2]{0:T(128)S(1)} %pad_add_fusion.place_ref, bf16[256,2048]{1,0:T(8,128)(2,1)S(1)} %shard_map.81.refs_0_.refs_2_.refs_6_, bf16[256,2048]{1,0:T(8,128)(2,1)S(1)} %collective-permute-done.7.refs_1_.refs_3_.refs_7_, bf16[1024,1024]{1,0:T(8,128)(2,1)S(1)} %get-tuple-element.124.refs_2_.refs_3_, ...), custom_call_target="tpu_custom_call" | custom-call | flops 2147483 | bytes 8388 | tf_op jit(solution)/shard_map/pallas_call | solution.py:256
  56.3 1.7 collective-permute-start.12
  58.0 1.7 collective-permute-start.10
  60.4 5.3 %shard_map.83 = (bf16[256,2048]{1,0:T(8,128)(2,1)S(1)}, bf16[256,2048]{1,0:T(8,128)(2,1)S(1)}) custom-call(s32[2]{0:T(128)S(1)} %pad_add_fusion.place_ref, bf16[256,2048]{1,0:T(8,128)(2,1)S(1)} %shard_map.80.refs_0_.refs_4_, bf16[256,2048]{1,0:T(8,128)(2,1)} %collective-permute-done.5.refs_1_.refs_5_, ...), custom_call_target="tpu_custom_call" | custom-call | flops 2147483 | bytes 8388 | tf_op jit(solution)/shard_map/pallas_call | solution.py:256
  67.8 2.6 %collective-permute-start.11 = (bf16[256,2048]{1,0:T(8,128)(2,1)S(1)}, bf16[256,2048]{1,0:T(8,128)(2,1)S(1)}, u32[]{:S(2)}, u32[]{:S(2)}) collective-permute-start(bf16[256,2048]{1,0:T(8,128)(2,1)S(1)} %shard_map.84.refs_0_.refs_2_.refs_6_), channel_id=1, source_target_pairs={{12,0},{13,1},{14,2},{15,3},{8,4},{9,5},{10,6},{11,7},{4,8},{5,9},... | collective-permute-start | bytes 3145736 | tf_op jit(solution)/shard_map/ppermute | solution.py:45
  70.4 2.4 %collective-permute-start.13 = (bf16[256,2048]{1,0:T(8,128)(2,1)S(1)}, bf16[256,2048]{1,0:T(8,128)(2,1)S(1)}, u32[]{:S(2)}, u32[]{:S(2)}) collective-permute-start(bf16[256,2048]{1,0:T(8,128)(2,1)S(1)} %shard_map.85.refs_0_.refs_4_), channel_id=1, source_target_pairs={{3,0},{2,1},{1,2},{0,3},{7,4},{6,5},{5,6},{4,7},{11,8},{10,9},{9,1... | collective-permute-start | bytes 3145736 | tf_op jit(solution)/shard_map/ppermute | solution.py:45
  72.8 1.9 collective-permute-start.9
  74.7 9.2 %collective-permute-done.11.refs_1_.refs_3_.refs_7_ = bf16[256,2048]{1,0:T(8,128)(2,1)S(1)} collective-permute-done((bf16[256,2048]{1,0:T(8,128)(2,1)S(1)}, bf16[256,2048]{1,0:T(8,128)(2,1)S(1)}, u32[]{:S(2)}, u32[]{:S(2)}) %collective-permute-start.11) | collective-permute-done | bytes 1048608 | tf_op jit(solution)/shard_map/ppermute | solution.py:45
  83.9 1.7 collective-permute-done.13.refs_1_.refs_5_
  85.6 4.3 %shard_map.86 = bf16[512,2048]{1,0:T(8,128)(2,1)S(1)} custom-call(s32[2]{0:T(128)S(1)} %pad_add_fusion.place_ref, bf16[256,2048]{1,0:T(8,128)(2,1)S(1)} %shard_map.84.refs_0_.refs_2_.refs_6_, bf16[256,2048]{1,0:T(8,128)(2,1)S(1)} %collective-permute-done.11.refs_1_.refs_3_.refs_7_, bf16[1024,1024]{1,0:T(8,128)(2,1)S(1)} %get-tuple-element.124.refs_2_.refs_3_, ...), custom_call_target="tpu_custom_call" | custom-call | flops 2147483 | bytes 8388 | tf_op jit(solution)/shard_map/pallas_call | solution.py:256
  90.4 4.3 %collective-permute-start.14 = (bf16[256,2048]{1,0:T(8,128)(2,1)S(1)}, bf16[256,2048]{1,0:T(8,128)(2,1)S(1)}, u32[]{:S(2)}, u32[]{:S(2)}) collective-permute-start(bf16[256,2048]{1,0:T(8,128)(2,1)S(1)} %add_convert_fusion.1), channel_id=1, source_target_pairs={{96,0},{97,1},{98,2},{99,3},{100,4},{101,5},{102,6},{103,7},{104,8... | collective-permute-start | bytes 3145736 | tf_op jit(solution)/shard_map/ppermute | solution.py:45
  94.7 4.5 %shard_map.87 = (bf16[256,2048]{1,0:T(8,128)(2,1)S(1)}, bf16[256,2048]{1,0:T(8,128)(2,1)S(1)}) custom-call(s32[2]{0:T(128)S(1)} %pad_add_fusion.place_ref, bf16[256,2048]{1,0:T(8,128)(2,1)S(1)} %shard_map.85.refs_0_.refs_4_, bf16[256,2048]{1,0:T(8,128)(2,1)S(1)} %collective-permute-done.13.refs_1_.refs_5_, ...), custom_call_target="tpu_custom_call" | custom-call | flops 2147483 | bytes 8388 | tf_op jit(solution)/shard_map/pallas_call | solution.py:256
  99.1 8.3 %collective-permute-done.14 = bf16[256,2048]{1,0:T(8,128)(2,1)S(1)} collective-permute-done((bf16[256,2048]{1,0:T(8,128)(2,1)S(1)}, bf16[256,2048]{1,0:T(8,128)(2,1)S(1)}, u32[]{:S(2)}, u32[]{:S(2)}) %collective-permute-start.14) | collective-permute-done | bytes 1048608 | tf_op jit(solution)/shard_map/ppermute | solution.py:45
  108.6 2.0 collective-permute-start.20
  110.6 12.8 %collective-permute-done.16.refs_1_.refs_5_ = bf16[256,2048]{1,0:T(8,128)(2,1)S(1)} collective-permute-done((bf16[256,2048]{1,0:T(8,128)(2,1)S(1)}, bf16[256,2048]{1,0:T(8,128)(2,1)S(1)}, u32[]{:S(2)}, u32[]{:S(2)}) %collective-permute-start.16) | collective-permute-done | bytes 1048608 | tf_op jit(solution)/shard_map/ppermute | solution.py:45
  123.4 4.3 %shard_map.88 = (bf16[256,2048]{1,0:T(8,128)(2,1)S(1)}, bf16[256,2048]{1,0:T(8,128)(2,1)S(1)}) custom-call(s32[2]{0:T(128)S(1)} %pad_add_fusion.place_ref, bf16[256,2048]{1,0:T(8,128)(2,1)S(1)} %pad_maximum_fusion.refs_0_.refs_4_, bf16[256,2048]{1,0:T(8,128)(2,1)S(1)} %collective-permute-done.16.refs_1_.refs_5_, ...), custom_call_target="tpu_custom_call" | custom-call | flops 2147483 | bytes 8388 | tf_op jit(solution)/shard_map/pallas_call | solution.py:256
  127.7 6.9 %collective-permute-done.20 = bf16[256,2048]{1,0:T(8,128)(2,1)S(1)} collective-permute-done((bf16[256,2048]{1,0:T(8,128)(2,1)S(1)}, bf16[256,2048]{1,0:T(8,128)(2,1)S(1)}, u32[]{:S(2)}, u32[]{:S(2)}) %collective-permute-start.20) | collective-permute-done | bytes 1048608 | tf_op jit(solution)/shard_map/ppermute | solution.py:45
  135.0 3.3 %collective-permute-start.23 = (bf16[256,2048]{1,0:T(8,128)(2,1)S(1)}, bf16[256,2048]{1,0:T(8,128)(2,1)S(1)}, u32[]{:S(2)}, u32[]{:S(2)}) collective-permute-start(bf16[256,2048]{1,0:T(8,128)(2,1)S(1)} %add_convert_fusion), channel_id=1, source_target_pairs={{96,0},{97,1},{98,2},{99,3},{100,4},{101,5},{102,6},{103,7},{104,8... | collective-permute-start | bytes 3145736 | tf_op jit(solution)/shard_map/ppermute | solution.py:45
  139.1 4.3 %shard_map.89 = (bf16[256,2048]{1,0:T(8,128)(2,1)S(1)}, bf16[256,2048]{1,0:T(8,128)(2,1)S(1)}) custom-call(s32[2]{0:T(128)S(1)} %pad_add_fusion.place_ref, bf16[256,2048]{1,0:T(8,128)(2,1)S(1)} %collective-permute-done.18.refs_0_.refs_6_.refs_2_, bf16[256,2048]{1,0:T(8,128)(2,1)S(1)} %collective-permute-done.19.refs_1_.refs_7_.refs_3_, ...), custom_call_target="tpu_custom_call" | custom-call | flops 2147483 | bytes 8388 | tf_op jit(solution)/shard_map/pallas_call | solution.py:256
  143.5 2.5 %collective-permute-start.21 = (bf16[256,2048]{1,0:T(8,128)(2,1)S(1)}, bf16[256,2048]{1,0:T(8,128)(2,1)S(1)}, u32[]{:S(2)}, u32[]{:S(2)}) collective-permute-start(bf16[256,2048]{1,0:T(8,128)(2,1)S(1)} %get-tuple-element.68), channel_id=1, source_target_pairs={{3,0},{2,1},{1,2},{0,3},{7,4},{6,5},{5,6},{4,7},{11,8},{10,9},{9,1... | collective-permute-start | bytes 3145736 | tf_op jit(solution)/shard_map/ppermute | solution.py:45
  145.9 5.6 %shard_map.90.refs_8_ = f32[1024,1024]{1,0:T(8,128)} custom-call(bf16[256,2048]{1,0:T(8,128)(2,1)S(1)} %shard_map.80.refs_0_.refs_4_, bf16[256,2048]{1,0:T(8,128)(2,1)} %collective-permute-done.5.refs_1_.refs_5_, bf16[256,2048]{1,0:T(8,128)(2,1)S(1)} %shard_map.81.refs_0_.refs_2_.refs_6_, ...), custom_call_target="tpu_custom_call" | custom-call | flops 2147483 | bytes 5242 | tf_op jit(solution)/shard_map/pallas_call | solution.py:305
  154.3 4.4 %collective-permute-done.21 = bf16[256,2048]{1,0:T(8,128)(2,1)S(1)} collective-permute-done((bf16[256,2048]{1,0:T(8,128)(2,1)S(1)}, bf16[256,2048]{1,0:T(8,128)(2,1)S(1)}, u32[]{:S(2)}, u32[]{:S(2)}) %collective-permute-start.21) | collective-permute-done | bytes 1048608 | tf_op jit(solution)/shard_map/ppermute | solution.py:45
  159.9 2.9 %collective-permute-start.25 = (bf16[128,2048]{1,0:T(8,128)(2,1)S(1)}, bf16[128,2048]{1,0:T(8,128)(2,1)S(1)}, u32[]{:S(2)}, u32[]{:S(2)}) collective-permute-start(bf16[128,2048]{1,0:T(8,128)(2,1)S(1)} %slice.246), channel_id=1, source_target_pairs={{1,0},{0,1},{3,2},{2,3},{5,4},{4,5},{7,6},{6,7},{9,8},{8,9},{11,10... | collective-permute-start | bytes 1572872 | tf_op jit(solution)/shard_map/ppermute | solution.py:45
  162.7 5.5 %shard_map.91.refs_8_ = f32[1024,1024]{1,0:T(8,128)} custom-call(bf16[256,2048]{1,0:T(8,128)(2,1)S(1)} %pad_maximum_fusion.refs_0_.refs_4_, bf16[256,2048]{1,0:T(8,128)(2,1)S(1)} %collective-permute-done.16.refs_1_.refs_5_, bf16[256,2048]{1,0:T(8,128)(2,1)S(1)} %collective-permute-done.18.refs_0_.refs_6_.refs_2_, ...), custom_call_target="tpu_custom_call" | custom-call | flops 2147483 | bytes 5242 | tf_op jit(solution)/shard_map/pallas_call | solution.py:305
  169.9 3.1 %shard_map.92 = bf16[256,2048]{1,0:T(8,128)(2,1)S(1)} custom-call(s32[2]{0:T(128)S(1)} %pad_add_fusion.place_ref, bf16[256,2048]{1,0:T(8,128)(2,1)S(1)} %pad_maximum_fusion.1.refs_0_.refs_4_, bf16[256,2048]{1,0:T(8,128)(2,1)S(1)} %collective-permute-done.24.refs_1_.refs_5_, bf16[1024,1024]{1,0:T(8,128)(2,1)S(1)} %get-tuple-element.123.refs_3_.refs_2_, ...), custom_call_target="tpu_custom_call" | custom-call | flops 2147483 | bytes 8388 | tf_op jit(solution)/shard_map/pallas_call | solution.py:256
  173.1 3.0 %collective-permute-start.28 = (bf16[256,2048]{1,0:T(8,128)(2,1)S(1)}, bf16[256,2048]{1,0:T(8,128)(2,1)S(1)}, u32[]{:S(2)}, u32[]{:S(2)}) collective-permute-start(bf16[256,2048]{1,0:T(8,128)(2,1)S(1)} %shard_map.92), channel_id=1, source_target_pairs={{12,0},{13,1},{14,2},{15,3},{8,4},{9,5},{10,6},{11,7},{4,8},{5,9},... | collective-permute-start | bytes 3145736 | tf_op jit(solution)/shard_map/ppermute | solution.py:45
  176.4 3.1 %shard_map.93 = bf16[256,2048]{1,0:T(8,128)(2,1)S(1)} custom-call(s32[2]{0:T(128)S(1)} %pad_add_fusion.place_ref, bf16[256,2048]{1,0:T(8,128)(2,1)S(1)} %collective-permute-done.26.refs_0_.refs_6_.refs_2_, bf16[256,2048]{1,0:T(8,128)(2,1)S(1)} %collective-permute-done.27.refs_1_.refs_7_.refs_3_, bf16[1024,1024]{1,0:T(8,128)(2,1)S(1)} %get-tuple-element.123.refs_3_.refs_2_, ...), custom_call_target="tpu_custom_call" | custom-call | flops 2147483 | bytes 8388 | tf_op jit(solution)/shard_map/pallas_call | solution.py:256
  179.6 2.6 %collective-permute-start.29 = (bf16[256,2048]{1,0:T(8,128)(2,1)S(1)}, bf16[256,2048]{1,0:T(8,128)(2,1)S(1)}, u32[]{:S(2)}, u32[]{:S(2)}) collective-permute-start(bf16[256,2048]{1,0:T(8,128)(2,1)S(1)} %shard_map.93), channel_id=1, source_target_pairs={{3,0},{2,1},{1,2},{0,3},{7,4},{6,5},{5,6},{4,7},{11,8},{10,9},{9,1... | collective-permute-start | bytes 3145736 | tf_op jit(solution)/shard_map/ppermute | solution.py:45
  182.3 3.1 %shard_map.94 = bf16[256,2048]{1,0:T(8,128)(2,1)S(1)} custom-call(s32[2]{0:T(128)S(1)} %pad_add_fusion.place_ref, bf16[256,2048]{1,0:T(8,128)(2,1)S(1)} %pad_maximum_fusion.1.refs_0_.refs_4_, bf16[256,2048]{1,0:T(8,128)(2,1)S(1)} %collective-permute-done.24.refs_1_.refs_5_, bf16[1024,1024]{1,0:T(8,128)(2,1)S(1)} %get-tuple-element.123.refs_3_.refs_2_, ...), custom_call_target="tpu_custom_call" | custom-call | flops 2147483 | bytes 8388 | tf_op jit(solution)/shard_map/pallas_call | solution.py:256
  185.4 3.1 %shard_map.95 = bf16[256,2048]{1,0:T(8,128)(2,1)S(1)} custom-call(s32[2]{0:T(128)S(1)} %pad_add_fusion.place_ref, bf16[256,2048]{1,0:T(8,128)(2,1)S(1)} %collective-permute-done.26.refs_0_.refs_6_.refs_2_, bf16[256,2048]{1,0:T(8,128)(2,1)S(1)} %collective-permute-done.27.refs_1_.refs_7_.refs_3_, bf16[1024,1024]{1,0:T(8,128)(2,1)S(1)} %get-tuple-element.123.refs_3_.refs_2_, ...), custom_call_target="tpu_custom_call" | custom-call | flops 2147483 | bytes 8388 | tf_op jit(solution)/shard_map/pallas_call | solution.py:256
  188.6 6.5 %shard_map.96 = f32[1024,1024]{1,0:T(8,128)} custom-call(bf16[256,2048]{1,0:T(8,128)(2,1)S(1)} %shard_map.85.refs_0_.refs_4_, bf16[256,2048]{1,0:T(8,128)(2,1)S(1)} %collective-permute-done.13.refs_1_.refs_5_, bf16[256,2048]{1,0:T(8,128)(2,1)S(1)} %shard_map.84.refs_0_.refs_2_.refs_6_, ...), custom_call_target="tpu_custom_call", output_to_operand_aliasing={{}: (8, {})} | custom-call | flops 2147483 | bytes 5242 | tf_op jit(solution)/shard_map/pallas_call | solution.py:305
  197.4 2.7 %collective-permute-start.33 = (bf16[128,2048]{1,0:T(8,128)(2,1)S(1)}, bf16[128,2048]{1,0:T(8,128)(2,1)S(1)}, u32[]{:S(2)}, u32[]{:S(2)}) collective-permute-start(bf16[128,2048]{1,0:T(8,128)(2,1)S(1)} %slice.244), channel_id=1, source_target_pairs={{1,0},{0,1},{3,2},{2,3},{5,4},{4,5},{7,6},{6,7},{9,8},{8,9},{11,10... | collective-permute-start | bytes 1572872 | tf_op jit(solution)/shard_map/ppermute | solution.py:45
  200.1 6.5 %shard_map.97 = f32[1024,1024]{1,0:T(8,128)} custom-call(bf16[256,2048]{1,0:T(8,128)(2,1)S(1)} %pad_maximum_fusion.1.refs_0_.refs_4_, bf16[256,2048]{1,0:T(8,128)(2,1)S(1)} %collective-permute-done.24.refs_1_.refs_5_, bf16[256,2048]{1,0:T(8,128)(2,1)S(1)} %collective-permute-done.26.refs_0_.refs_6_.refs_2_, ...), custom_call_target="tpu_custom_call", output_to_operand_aliasing={{}: (8, {})} | custom-call | flops 2147483 | bytes 5242 | tf_op jit(solution)/shard_map/pallas_call | solution.py:305
  206.9 2.6 %collective-permute-start.31 = (bf16[128,2048]{1,0:T(8,128)(2,1)S(1)}, bf16[128,2048]{1,0:T(8,128)(2,1)S(1)}, u32[]{:S(2)}, u32[]{:S(2)}) collective-permute-start(bf16[128,2048]{1,0:T(8,128)(2,1)S(1)} %pad_maximum_fusion.2), channel_id=1, source_target_pairs={{3,0},{2,1},{1,2},{0,3},{7,4},{6,5},{5,6},{4,7},{11,8},{10,9},{9,1... | collective-permute-start | bytes 1572872 | tf_op jit(solution)/shard_map/ppermute | solution.py:45
  211.2 5.5 %collective-permute-done.31 = bf16[128,2048]{1,0:T(8,128)(2,1)S(1)} collective-permute-done((bf16[128,2048]{1,0:T(8,128)(2,1)S(1)}, bf16[128,2048]{1,0:T(8,128)(2,1)S(1)}, u32[]{:S(2)}, u32[]{:S(2)}) %collective-permute-start.31) | collective-permute-done | bytes 524320 | tf_op jit(solution)/shard_map/ppermute | solution.py:45
  219.2 1.7 collective-permute-done.34
  222.3 1.8 collective-permute-done.32
  224.1 4.4 %collective-permute-done.35 = bf16[64,2048]{1,0:T(8,128)(2,1)} collective-permute-done((bf16[64,2048]{1,0:T(8,128)(2,1)}, bf16[64,2048]{1,0:T(8,128)(2,1)}, u32[]{:S(2)}, u32[]{:S(2)}) %collective-permute-start.35) | collective-permute-done | bytes 262176 | tf_op jit(solution)/shard_map/ppermute | solution.py:45
  (102 shorter events, 34.1 us)
Async XLA Ops:
  0.7 1.0 copy-start.4
  1.7 0.9 copy-start.5
  3.3 6.5 %collective-permute-start = (bf16[64,2048]{1,0:T(8,128)(2,1)S(1)}, bf16[64,2048]{1,0:T(8,128)(2,1)S(1)}, u32[]{:S(2)}, u32[]{:S(2)}) collective-permute-start(bf16[64,2048]{1,0:T(8,128)(2,1)S(1)} %get-tuple-element.45.a_ref), channel_id=1, source_target_pairs={{4,0},{5,1},{6,2},{7,3},{0,4},{1,5},{2,6},{3,7},{12,8},{13,9},{14,... | collective-permute-start | bytes 786440 | tf_op jit(solution)/shard_map/ppermute | solution.py:45
  4.9 8.3 %collective-permute-start.2 = (bf16[64,2048]{1,0:T(8,128)(2,1)S(1)}, bf16[64,2048]{1,0:T(8,128)(2,1)S(1)}, u32[]{:S(2)}, u32[]{:S(2)}) collective-permute-start(bf16[64,2048]{1,0:T(8,128)(2,1)S(1)} %get-tuple-element.47.a_ref), channel_id=1, source_target_pairs={{1,0},{0,1},{3,2},{2,3},{5,4},{4,5},{7,6},{6,7},{9,8},{8,9},{11,10... | collective-permute-start | bytes 786440 | tf_op jit(solution)/shard_map/ppermute | solution.py:45
  10.3 10.5 %collective-permute-start.1 = (bf16[128,2048]{1,0:T(8,128)(2,1)S(1)}, bf16[128,2048]{1,0:T(8,128)(2,1)S(1)}, u32[]{:S(2)}, u32[]{:S(2)}) collective-permute-start(bf16[128,2048]{1,0:T(8,128)(2,1)S(1)} %shard_map.76), channel_id=1, source_target_pairs={{12,0},{13,1},{14,2},{15,3},{8,4},{9,5},{10,6},{11,7},{4,8},{5,9},... | collective-permute-start | bytes 1572872 | tf_op jit(solution)/shard_map/ppermute | solution.py:45
  13.8 9.3 %collective-permute-start.3 = (bf16[128,2048]{1,0:T(8,128)(2,1)S(1)}, bf16[128,2048]{1,0:T(8,128)(2,1)S(1)}, u32[]{:S(2)}, u32[]{:S(2)}) collective-permute-start(bf16[128,2048]{1,0:T(8,128)(2,1)S(1)} %shard_map.78), channel_id=1, source_target_pairs={{3,0},{2,1},{1,2},{0,3},{7,4},{6,5},{5,6},{4,7},{11,8},{10,9},{9,1... | collective-permute-start | bytes 1572872 | tf_op jit(solution)/shard_map/ppermute | solution.py:45
  21.4 0.8 copy-start
  23.7 0.8 copy-start.2
  24.5 9.2 %collective-permute-start.6 = (bf16[128,2048]{1,0:T(8,128)(2,1)S(1)}, bf16[128,2048]{1,0:T(8,128)(2,1)S(1)}, u32[]{:S(2)}, u32[]{:S(2)}) collective-permute-start(bf16[128,2048]{1,0:T(8,128)(2,1)S(1)} %get-tuple-element.50.a_ref), channel_id=1, source_target_pairs={{4,0},{5,1},{6,2},{7,3},{0,4},{1,5},{2,6},{3,7},{12,8},{13,9},{14,... | collective-permute-start | bytes 1572872 | tf_op jit(solution)/shard_map/ppermute | solution.py:45
  24.7 11.6 %collective-permute-start.4 = (bf16[128,2048]{1,0:T(8,128)(2,1)S(1)}, bf16[128,2048]{1,0:T(8,128)(2,1)S(1)}, u32[]{:S(2)}, u32[]{:S(2)}) collective-permute-start(bf16[128,2048]{1,0:T(8,128)(2,1)S(1)} %get-tuple-element.49.a_ref), channel_id=1, source_target_pairs={{1,0},{0,1},{3,2},{2,3},{5,4},{4,5},{7,6},{6,7},{9,8},{8,9},{11,10... | collective-permute-start | bytes 1572872 | tf_op jit(solution)/shard_map/ppermute | solution.py:45
  34.3 16.1 %collective-permute-start.7 = (bf16[256,2048]{1,0:T(8,128)(2,1)S(1)}, bf16[256,2048]{1,0:T(8,128)(2,1)S(1)}, u32[]{:S(2)}, u32[]{:S(2)}) collective-permute-start(bf16[256,2048]{1,0:T(8,128)(2,1)S(1)} %shard_map.81.refs_0_.refs_2_.refs_6_), channel_id=1, source_target_pairs={{12,0},{13,1},{14,2},{15,3},{8,4},{9,5},{10,6},{11,7},{4,8},{5,9},... | collective-permute-start | bytes 3145736 | tf_op jit(solution)/shard_map/ppermute | solution.py:45
  36.9 15.0 %collective-permute-start.5 = (bf16[256,2048]{1,0:T(8,128)(2,1)S(1)}, bf16[256,2048]{1,0:T(8,128)(2,1)}, u32[]{:S(2)}, u32[]{:S(2)}) collective-permute-start(bf16[256,2048]{1,0:T(8,128)(2,1)S(1)} %shard_map.80.refs_0_.refs_4_), channel_id=1, source_target_pairs={{3,0},{2,1},{1,2},{0,3},{7,4},{6,5},{5,6},{4,7},{11,8},{10,9},{9,1... | collective-permute-start | bytes 3145736 | tf_op jit(solution)/shard_map/ppermute | solution.py:45
  51.9 4.4 %copy-start.1 = (bf16[128,2048]{1,0:T(8,128)(2,1)S(1)}, bf16[128,2048]{1,0:T(8,128)(2,1)}, u32[]{:S(2)}) copy-start(bf16[128,2048]{1,0:T(8,128)(2,1)} %copy-done) | copy-start | bytes 1572868
  51.9 6.1 %copy-start.3 = (bf16[128,2048]{1,0:T(8,128)(2,1)S(1)}, bf16[128,2048]{1,0:T(8,128)(2,1)}, u32[]{:S(2)}) copy-start(bf16[128,2048]{1,0:T(8,128)(2,1)} %copy-done.2) | copy-start | bytes 1572868
  56.2 4.2 %collective-permute-start.8 = (bf16[512,2048]{1,0:T(8,128)(2,1)S(1)}, bf16[512,2048]{1,0:T(8,128)(2,1)S(1)}, u32[]{:S(2)}, u32[]{:S(2)}) collective-permute-start(bf16[512,2048]{1,0:T(8,128)(2,1)S(1)} %shard_map.82), channel_id=1, source_target_pairs={{16,0},{17,1},{18,2},{19,3},{20,4},{21,5},{22,6},{23,7},{24,8},{25... | collective-permute-start | bytes 6291464 | tf_op jit(solution)/shard_map/ppermute | solution.py:45
  56.3 9.5 %collective-permute-start.12 = (bf16[128,2048]{1,0:T(8,128)(2,1)S(1)}, bf16[128,2048]{1,0:T(8,128)(2,1)S(1)}, u32[]{:S(2)}, u32[]{:S(2)}) collective-permute-start(bf16[128,2048]{1,0:T(8,128)(2,1)S(1)} %copy-done.1), channel_id=1, source_target_pairs={{1,0},{0,1},{3,2},{2,3},{5,4},{4,5},{7,6},{6,7},{9,8},{8,9},{11,10... | collective-permute-start | bytes 1572872 | tf_op jit(solution)/shard_map/ppermute | solution.py:45
  58.0 9.2 %collective-permute-start.10 = (bf16[128,2048]{1,0:T(8,128)(2,1)S(1)}, bf16[128,2048]{1,0:T(8,128)(2,1)S(1)}, u32[]{:S(2)}, u32[]{:S(2)}) collective-permute-start(bf16[128,2048]{1,0:T(8,128)(2,1)S(1)} %copy-done.3), channel_id=1, source_target_pairs={{4,0},{5,1},{6,2},{7,3},{0,4},{1,5},{2,6},{3,7},{12,8},{13,9},{14,... | collective-permute-start | bytes 1572872 | tf_op jit(solution)/shard_map/ppermute | solution.py:45
  67.8 16.1 %collective-permute-start.11 = (bf16[256,2048]{1,0:T(8,128)(2,1)S(1)}, bf16[256,2048]{1,0:T(8,128)(2,1)S(1)}, u32[]{:S(2)}, u32[]{:S(2)}) collective-permute-start(bf16[256,2048]{1,0:T(8,128)(2,1)S(1)} %shard_map.84.refs_0_.refs_2_.refs_6_), channel_id=1, source_target_pairs={{12,0},{13,1},{14,2},{15,3},{8,4},{9,5},{10,6},{11,7},{4,8},{5,9},... | collective-permute-start | bytes 3145736 | tf_op jit(solution)/shard_map/ppermute | solution.py:45
  70.4 15.2 %collective-permute-start.13 = (bf16[256,2048]{1,0:T(8,128)(2,1)S(1)}, bf16[256,2048]{1,0:T(8,128)(2,1)S(1)}, u32[]{:S(2)}, u32[]{:S(2)}) collective-permute-start(bf16[256,2048]{1,0:T(8,128)(2,1)S(1)} %shard_map.85.refs_0_.refs_4_), channel_id=1, source_target_pairs={{3,0},{2,1},{1,2},{0,3},{7,4},{6,5},{5,6},{4,7},{11,8},{10,9},{9,1... | collective-permute-start | bytes 3145736 | tf_op jit(solution)/shard_map/ppermute | solution.py:45
  72.8 17.2 %collective-permute-start.9 = (bf16[256,2048]{1,0:T(8,128)(2,1)S(1)}, bf16[256,2048]{1,0:T(8,128)(2,1)S(1)}, u32[]{:S(2)}, u32[]{:S(2)}) collective-permute-start(bf16[256,2048]{1,0:T(8,128)(2,1)S(1)} %get-tuple-element.53), channel_id=1, source_target_pairs={{32,0},{33,1},{34,2},{35,3},{36,4},{37,5},{38,6},{39,7},{40,8},{41... | collective-permute-start | bytes 3145736 | tf_op jit(solution)/shard_map/ppermute | solution.py:45
  89.9 4.8 %collective-permute-start.15 = (bf16[512,2048]{1,0:T(8,128)(2,1)S(1)}, bf16[512,2048]{1,0:T(8,128)(2,1)S(1)}, u32[]{:S(2)}, u32[]{:S(2)}) collective-permute-start(bf16[512,2048]{1,0:T(8,128)(2,1)S(1)} %shard_map.86), channel_id=1, source_target_pairs={{16,0},{17,1},{18,2},{19,3},{20,4},{21,5},{22,6},{23,7},{24,8},{25... | collective-permute-start | bytes 6291464 | tf_op jit(solution)/shard_map/ppermute | solution.py:45
  90.4 17.1 %collective-permute-start.14 = (bf16[256,2048]{1,0:T(8,128)(2,1)S(1)}, bf16[256,2048]{1,0:T(8,128)(2,1)S(1)}, u32[]{:S(2)}, u32[]{:S(2)}) collective-permute-start(bf16[256,2048]{1,0:T(8,128)(2,1)S(1)} %add_convert_fusion.1), channel_id=1, source_target_pairs={{96,0},{97,1},{98,2},{99,3},{100,4},{101,5},{102,6},{103,7},{104,8... | collective-permute-start | bytes 3145736 | tf_op jit(solution)/shard_map/ppermute | solution.py:45
  108.5 14.9 %collective-permute-start.16 = (bf16[256,2048]{1,0:T(8,128)(2,1)S(1)}, bf16[256,2048]{1,0:T(8,128)(2,1)S(1)}, u32[]{:S(2)}, u32[]{:S(2)}) collective-permute-start(bf16[256,2048]{1,0:T(8,128)(2,1)S(1)} %pad_maximum_fusion.refs_0_.refs_4_), channel_id=1, source_target_pairs={{32,0},{33,1},{34,2},{35,3},{36,4},{37,5},{38,6},{39,7},{40,8},{41... | collective-permute-start | bytes 3145736 | tf_op jit(solution)/shard_map/ppermute | solution.py:45
  108.6 26.0 %collective-permute-start.20 = (bf16[256,2048]{1,0:T(8,128)(2,1)S(1)}, bf16[256,2048]{1,0:T(8,128)(2,1)S(1)}, u32[]{:S(2)}, u32[]{:S(2)}) collective-permute-start(bf16[256,2048]{1,0:T(8,128)(2,1)S(1)} %get-tuple-element.64), channel_id=1, source_target_pairs={{32,0},{33,1},{34,2},{35,3},{36,4},{37,5},{38,6},{39,7},{40,8},{41... | collective-permute-start | bytes 3145736 | tf_op jit(solution)/shard_map/ppermute | solution.py:45
  110.6 28.5 %collective-permute-start.18 = (bf16[256,2048]{1,0:T(8,128)(2,1)S(1)}, bf16[256,2048]{1,0:T(8,128)(2,1)S(1)}, u32[]{:S(2)}, u32[]{:S(2)}) collective-permute-start(bf16[256,2048]{1,0:T(8,128)(2,1)S(1)} %pad_maximum_fusion.refs_0_.refs_4_), channel_id=1, source_target_pairs={{16,0},{17,1},{18,2},{19,3},{20,4},{21,5},{22,6},{23,7},{24,8},{25... | collective-permute-start | bytes 3145736 | tf_op jit(solution)/shard_map/ppermute | solution.py:45
  134.6 4.5 %collective-permute-start.19 = (bf16[256,2048]{1,0:T(8,128)(2,1)S(1)}, bf16[256,2048]{1,0:T(8,128)(2,1)S(1)}, u32[]{:S(2)}, u32[]{:S(2)}) collective-permute-start(bf16[256,2048]{1,0:T(8,128)(2,1)S(1)} %collective-permute-done.16.refs_1_.refs_5_), channel_id=1, source_target_pairs={{16,0},{17,1},{18,2},{19,3},{20,4},{21,5},{22,6},{23,7},{24,8},{25... | collective-permute-start | bytes 3145736 | tf_op jit(solution)/shard_map/ppermute | solution.py:45
  135.0 16.6 %collective-permute-start.23 = (bf16[256,2048]{1,0:T(8,128)(2,1)S(1)}, bf16[256,2048]{1,0:T(8,128)(2,1)S(1)}, u32[]{:S(2)}, u32[]{:S(2)}) collective-permute-start(bf16[256,2048]{1,0:T(8,128)(2,1)S(1)} %add_convert_fusion), channel_id=1, source_target_pairs={{96,0},{97,1},{98,2},{99,3},{100,4},{101,5},{102,6},{103,7},{104,8... | collective-permute-start | bytes 3145736 | tf_op jit(solution)/shard_map/ppermute | solution.py:45
  138.3 16.0 %collective-permute-start.17 = (bf16[256,2048]{1,0:T(8,128)(2,1)S(1)}, bf16[256,2048]{1,0:T(8,128)(2,1)S(1)}, u32[]{:S(2)}, u32[]{:S(2)}) collective-permute-start(bf16[256,2048]{1,0:T(8,128)(2,1)S(1)} %get-tuple-element.63), channel_id=1, source_target_pairs={{12,0},{13,1},{14,2},{15,3},{8,4},{9,5},{10,6},{11,7},{4,8},{5,9},... | collective-permute-start | bytes 3145736 | tf_op jit(solution)/shard_map/ppermute | solution.py:45
  143.5 15.3 %collective-permute-start.21 = (bf16[256,2048]{1,0:T(8,128)(2,1)S(1)}, bf16[256,2048]{1,0:T(8,128)(2,1)S(1)}, u32[]{:S(2)}, u32[]{:S(2)}) collective-permute-start(bf16[256,2048]{1,0:T(8,128)(2,1)S(1)} %get-tuple-element.68), channel_id=1, source_target_pairs={{3,0},{2,1},{1,2},{0,3},{7,4},{6,5},{5,6},{4,7},{11,8},{10,9},{9,1... | collective-permute-start | bytes 3145736 | tf_op jit(solution)/shard_map/ppermute | solution.py:45
  152.6 17.3 %collective-permute-start.26 = (bf16[256,2048]{1,0:T(8,128)(2,1)S(1)}, bf16[256,2048]{1,0:T(8,128)(2,1)S(1)}, u32[]{:S(2)}, u32[]{:S(2)}) collective-permute-start(bf16[256,2048]{1,0:T(8,128)(2,1)S(1)} %pad_maximum_fusion.1.refs_0_.refs_4_), channel_id=1, source_target_pairs={{16,0},{17,1},{18,2},{19,3},{20,4},{21,5},{22,6},{23,7},{24,8},{25... | collective-permute-start | bytes 3145736 | tf_op jit(solution)/shard_map/ppermute | solution.py:45
  152.7 15.6 %collective-permute-start.24 = (bf16[256,2048]{1,0:T(8,128)(2,1)S(1)}, bf16[256,2048]{1,0:T(8,128)(2,1)S(1)}, u32[]{:S(2)}, u32[]{:S(2)}) collective-permute-start(bf16[256,2048]{1,0:T(8,128)(2,1)S(1)} %pad_maximum_fusion.1.refs_0_.refs_4_), channel_id=1, source_target_pairs={{32,0},{33,1},{34,2},{35,3},{36,4},{37,5},{38,6},{39,7},{40,8},{41... | collective-permute-start | bytes 3145736 | tf_op jit(solution)/shard_map/ppermute | solution.py:45
  159.2 9.3 %collective-permute-start.22 = (bf16[128,2048]{1,0:T(8,128)(2,1)S(1)}, bf16[128,2048]{1,0:T(8,128)(2,1)S(1)}, u32[]{:S(2)}, u32[]{:S(2)}) collective-permute-start(bf16[128,2048]{1,0:T(8,128)(2,1)S(1)} %slice.247), channel_id=1, source_target_pairs={{4,0},{5,1},{6,2},{7,3},{0,4},{1,5},{2,6},{3,7},{12,8},{13,9},{14,... | collective-permute-start | bytes 1572872 | tf_op jit(solution)/shard_map/ppermute | solution.py:45
  159.9 10.0 %collective-permute-start.25 = (bf16[128,2048]{1,0:T(8,128)(2,1)S(1)}, bf16[128,2048]{1,0:T(8,128)(2,1)S(1)}, u32[]{:S(2)}, u32[]{:S(2)}) collective-permute-start(bf16[128,2048]{1,0:T(8,128)(2,1)S(1)} %slice.246), channel_id=1, source_target_pairs={{1,0},{0,1},{3,2},{2,3},{5,4},{4,5},{7,6},{6,7},{9,8},{8,9},{11,10... | collective-permute-start | bytes 1572872 | tf_op jit(solution)/shard_map/ppermute | solution.py:45
  169.9 6.5 %collective-permute-start.27 = (bf16[256,2048]{1,0:T(8,128)(2,1)S(1)}, bf16[256,2048]{1,0:T(8,128)(2,1)S(1)}, u32[]{:S(2)}, u32[]{:S(2)}) collective-permute-start(bf16[256,2048]{1,0:T(8,128)(2,1)S(1)} %collective-permute-done.24.refs_1_.refs_5_), channel_id=1, source_target_pairs={{16,0},{17,1},{18,2},{19,3},{20,4},{21,5},{22,6},{23,7},{24,8},{25... | collective-permute-start | bytes 3145736 | tf_op jit(solution)/shard_map/ppermute | solution.py:45
  173.1 22.0 %collective-permute-start.28 = (bf16[256,2048]{1,0:T(8,128)(2,1)S(1)}, bf16[256,2048]{1,0:T(8,128)(2,1)S(1)}, u32[]{:S(2)}, u32[]{:S(2)}) collective-permute-start(bf16[256,2048]{1,0:T(8,128)(2,1)S(1)} %shard_map.92), channel_id=1, source_target_pairs={{12,0},{13,1},{14,2},{15,3},{8,4},{9,5},{10,6},{11,7},{4,8},{5,9},... | collective-permute-start | bytes 3145736 | tf_op jit(solution)/shard_map/ppermute | solution.py:45
  179.6 15.5 %collective-permute-start.29 = (bf16[256,2048]{1,0:T(8,128)(2,1)S(1)}, bf16[256,2048]{1,0:T(8,128)(2,1)S(1)}, u32[]{:S(2)}, u32[]{:S(2)}) collective-permute-start(bf16[256,2048]{1,0:T(8,128)(2,1)S(1)} %shard_map.93), channel_id=1, source_target_pairs={{3,0},{2,1},{1,2},{0,3},{7,4},{6,5},{5,6},{4,7},{11,8},{10,9},{9,1... | collective-permute-start | bytes 3145736 | tf_op jit(solution)/shard_map/ppermute | solution.py:45
  195.5 11.1 %collective-permute-start.30 = (bf16[128,2048]{1,0:T(8,128)(2,1)S(1)}, bf16[128,2048]{1,0:T(8,128)(2,1)S(1)}, u32[]{:S(2)}, u32[]{:S(2)}) collective-permute-start(bf16[128,2048]{1,0:T(8,128)(2,1)S(1)} %slice.245), channel_id=1, source_target_pairs={{4,0},{5,1},{6,2},{7,3},{0,4},{1,5},{2,6},{3,7},{12,8},{13,9},{14,... | collective-permute-start | bytes 1572872 | tf_op jit(solution)/shard_map/ppermute | solution.py:45
  197.4 12.1 %collective-permute-start.33 = (bf16[128,2048]{1,0:T(8,128)(2,1)S(1)}, bf16[128,2048]{1,0:T(8,128)(2,1)S(1)}, u32[]{:S(2)}, u32[]{:S(2)}) collective-permute-start(bf16[128,2048]{1,0:T(8,128)(2,1)S(1)} %slice.244), channel_id=1, source_target_pairs={{1,0},{0,1},{3,2},{2,3},{5,4},{4,5},{7,6},{6,7},{9,8},{8,9},{11,10... | collective-permute-start | bytes 1572872 | tf_op jit(solution)/shard_map/ppermute | solution.py:45
  206.9 9.8 %collective-permute-start.31 = (bf16[128,2048]{1,0:T(8,128)(2,1)S(1)}, bf16[128,2048]{1,0:T(8,128)(2,1)S(1)}, u32[]{:S(2)}, u32[]{:S(2)}) collective-permute-start(bf16[128,2048]{1,0:T(8,128)(2,1)S(1)} %pad_maximum_fusion.2), channel_id=1, source_target_pairs={{3,0},{2,1},{1,2},{0,3},{7,4},{6,5},{5,6},{4,7},{11,8},{10,9},{9,1... | collective-permute-start | bytes 1572872 | tf_op jit(solution)/shard_map/ppermute | solution.py:45
  209.8 11.1 %collective-permute-start.34 = (bf16[128,2048]{1,0:T(8,128)(2,1)S(1)}, bf16[128,2048]{1,0:T(8,128)(2,1)S(1)}, u32[]{:S(2)}, u32[]{:S(2)}) collective-permute-start(bf16[128,2048]{1,0:T(8,128)(2,1)S(1)} %pad_maximum_fusion.3), channel_id=1, source_target_pairs={{12,0},{13,1},{14,2},{15,3},{8,4},{9,5},{10,6},{11,7},{4,8},{5,9},... | collective-permute-start | bytes 1572872 | tf_op jit(solution)/shard_map/ppermute | solution.py:45
  217.6 10.9 %copy-start.6 = (f32[32,2048]{1,0:T(8,128)S(1)}, f32[32,2048]{1,0:T(8,128)}, u32[]{:S(2)}) copy-start(f32[32,2048]{1,0:T(8,128)} %get-tuple-element.107) | copy-start | bytes 786436
  217.6 6.6 %collective-permute-start.32 = (bf16[64,2048]{1,0:T(8,128)(2,1)}, bf16[64,2048]{1,0:T(8,128)(2,1)S(1)}, u32[]{:S(2)}, u32[]{:S(2)}) collective-permute-start(bf16[64,2048]{1,0:T(8,128)(2,1)} %fusion.15), channel_id=1, source_target_pairs={{1,0},{0,1},{3,2},{2,3},{5,4},{4,5},{7,6},{6,7},{9,8},{8,9},{11,10... | collective-permute-start | bytes 786440 | tf_op jit(solution)/shard_map/ppermute | solution.py:45
  221.8 6.7 %collective-permute-start.35 = (bf16[64,2048]{1,0:T(8,128)(2,1)}, bf16[64,2048]{1,0:T(8,128)(2,1)}, u32[]{:S(2)}, u32[]{:S(2)}) collective-permute-start(bf16[64,2048]{1,0:T(8,128)(2,1)} %fusion.12), channel_id=1, source_target_pairs={{4,0},{5,1},{6,2},{7,3},{0,4},{1,5},{2,6},{3,7},{12,8},{13,9},{14,... | collective-permute-start | bytes 786440 | tf_op jit(solution)/shard_map/ppermute | solution.py:45

commit v13 on v12

--- a/solution.py
+++ b/solution.py
@@ -144,6 +144,41 @@
         compiler_params=pltpu.CompilerParams(vmem_limit_bytes=8 * 2**20),
         cost_estimate=cost(flops=0, bytes_accessed=0, transcendentals=0),
     )(place, tokens, out_grad)
+
+
+def put_back_kernel(place_ref, kept_ref, passed_ref, mixed_ref, grad_ref, sems):
+    block, wide = kept_ref.shape[0], mixed_ref.shape[1]
+    core = place_ref[1]
+    copies = []
+    for ref, which in ((kept_ref, core), (passed_ref, 1 - core)):
+        rows = pl.ds(pl.multiple_of(which * block, block), block)
+        for i, target in enumerate((mixed_ref, grad_ref)):
+            copies.append(
+                pltpu.make_async_copy(
+                    ref.at[:, i * wide:(i + 1) * wide],
+                    target.at[rows, :],
+                    sems.at[len(copies)],
+                )
+            )
+    for copy in copies:
+        copy.start()
+    for copy in copies:
+        copy.wait()
+
+
+def put_back(place, kept, passed):
+    rows, wide = kept.shape
+    out = jax.ShapeDtypeStruct((2 * rows, wide // 2), BF)
+    return pl.pallas_call(
+        put_back_kernel,
+        in_specs=[pl.BlockSpec(memory_space=pltpu.SMEM)]
+        + [pl.BlockSpec(memory_space=pltpu.VMEM)] * 2,
+        out_specs=[pl.BlockSpec(memory_space=pltpu.HBM)] * 2,
+        out_shape=[out, out],
+        scratch_shapes=[pltpu.SemaphoreType.DMA((4,))],
+        compiler_params=pltpu.CompilerParams(vmem_limit_bytes=8 * 2**20),
+        cost_estimate=cost(flops=0, bytes_accessed=0, transcendentals=0),
+    )(place, kept, passed)
 
 
 def join_kernel(place_ref, a_ref, b_ref, out_ref):
@@ -438,7 +473,7 @@
     out_a, out_b, got_a, got_b = {}, {}, {}, {}
     sums_a, sums_b, last_a, last_b, total_a, total_b = {}, {}, {}, {}, {}, {}
     out_a[True] = out_dot(True, hid_a[True])
-    half_b = half_sum(kept_b, after(step_b, out_a[True][0]))
+    half_b = half_sum(kept_b, after(step_b, out_a[True][0], *hid_a[False]))
     turn_b = exchange(half_b, along_z(1))
     out_a[False] = out_dot(False, hid_a[False], out_a[True][0], step_b)
     for keep in both_ways:
@@ -448,7 +483,7 @@
     far_b = exchange(pair_b, along_z(0))
     grad_out = grads(1, near_a, rest_a, hid_a, None, turn_b, got_a[True], got_a[False], grad_in)
     for keep in both_ways:
-        got = after(got_a[keep], grad_in, got_a[not keep])
+        got = after(got_a[keep], grad_in, got_a[not keep], pair_b)
         sums_a[keep], last_a[keep] = second_half(keep, out_a[keep][0], got)
     far_b = after(far_b, grad_out, last_a[True], last_a[False])
     hid_b = {True: (pair_b, far_b)}
@@ -492,10 +527,8 @@
             pick(keep, 0) + got[:block] + exchange(last, along(keep, False, 0)).astype(F32)
         ).astype(BF)
 
-    low = jnp.where(core == 0, done[True], done[False])
-    high = jnp.where(core == 0, done[False], done[True])
-    result = jnp.concatenate([low, high], axis=0)
-    return (result[:, :width], result[:, width:], grad_in, grad_out)
+    mixed, token_grad = put_back(place, done[True], done[False])
+    return (mixed, token_grad, grad_in, grad_out)
 
 
 def solution(mesh):

time: 234 us -> 232 us (level)
  waiting for transfers between devices: 89.9 us -> 99.7 us
  starting transfers between devices: 54.1 us -> 46.3 us
  other arithmetic: 8.64 us -> 5.39 us
    ppermute x36, waiting for transfers between devices: 89.9 us -> 99.7 us  [exchange(): return lax.ppermute(array, AXES, pairs)]
    ppermute x36, starting transfers between devices: 54.1 us -> 46.3 us  [exchange(): return lax.ppermute(array, AXES, pairs)]
  transfers between devices with their start and end apart: 36 -> 36, of which waited for: 21 -> 23; matrix products, arithmetic and copies ran while one was open for 4% -> 3% of each run, Pallas kernels for 27% -> 28%
where the time goes in v13:
time: 232 us; the launch traced here: 230 us
  waiting for transfers between devices  99.7 us (43%)
  Pallas kernels  70.5 us (30%)
  starting transfers between devices  46.3 us (20%)
  local copies, waits for them, and re-layouts  6.8 us (3%)
  other arithmetic  5.39 us (2%)
    ppermute x36, waiting for transfers between devices, exchange(): return lax.ppermute(array, AXES, pairs)  99.7 us
    ppermute x36, starting transfers between devices, exchange(): return lax.ppermute(array, AXES, pairs)  46.3 us
    pallas_call x10, Pallas kernels, pair_dot(): pl.pallas_call(functools.partial(pair_kernel, keep, hidden, more is not N...  39.5 us
    pallas_call x4, Pallas kernels, grad_dot(): pl.pallas_call(functools.partial(grad_kernel, pairs, block, factor, begun...  24.1 us
    pallas_call x8, Pallas kernels, whole(): pl.pallas_call(kernel, in_specs=[pl.BlockSpec(memory_space=pltpu.SMEM)] +...  4.82 us
  transfers between devices with their start and end apart: 36, of which 23 were waited for; matrix products, arithmetic and copies ran while one was open for 3% of the time, Pallas kernels for 28%

profile of v13, /device:TPU:8, one launch (start us, length us, event | category | flops | bytes accessed | tf_op | source)
XLA Modules:
  0.0 230.1 jit_solution(4897453816407121665)
XLA Ops:
  3.8 1.6 collective-permute-start
  5.3 4.4 %collective-permute-done.2.b_ref = bf16[64,2048]{1,0:T(8,128)(2,1)S(1)} collective-permute-done((bf16[64,2048]{1,0:T(8,128)(2,1)S(1)}, bf16[64,2048]{1,0:T(8,128)(2,1)S(1)}, u32[]{:S(2)}, u32[]{:S(2)}) %collective-permute-start.2) | collective-permute-done | bytes 262176 | tf_op jit(solution)/shard_map/ppermute | solution.py:45
  10.3 1.7 collective-permute-start.3
  12.6 2.8 %collective-permute-start.1 = (bf16[128,2048]{1,0:T(8,128)(2,1)S(1)}, bf16[128,2048]{1,0:T(8,128)(2,1)S(1)}, u32[]{:S(2)}, u32[]{:S(2)}) collective-permute-start(bf16[128,2048]{1,0:T(8,128)(2,1)S(1)} %shard_map.76), channel_id=1, source_target_pairs={{12,0},{13,1},{14,2},{15,3},{8,4},{9,5},{10,6},{11,7},{4,8},{5,9},... | collective-permute-start | bytes 1572872 | tf_op jit(solution)/shard_map/ppermute | solution.py:45
  15.4 4.2 %collective-permute-done.3.c_ref = bf16[128,2048]{1,0:T(8,128)(2,1)S(1)} collective-permute-done((bf16[128,2048]{1,0:T(8,128)(2,1)S(1)}, bf16[128,2048]{1,0:T(8,128)(2,1)S(1)}, u32[]{:S(2)}, u32[]{:S(2)}) %collective-permute-start.3) | collective-permute-done | bytes 524320 | tf_op jit(solution)/shard_map/ppermute | solution.py:45
  21.0 2.0 collective-permute-done.1.c_ref
  24.8 1.9 collective-permute-start.4
  26.7 7.0 %collective-permute-done.6.b_ref = bf16[128,2048]{1,0:T(8,128)(2,1)S(1)} collective-permute-done((bf16[128,2048]{1,0:T(8,128)(2,1)S(1)}, bf16[128,2048]{1,0:T(8,128)(2,1)S(1)}, u32[]{:S(2)}, u32[]{:S(2)}) %collective-permute-start.6) | collective-permute-done | bytes 524320 | tf_op jit(solution)/shard_map/ppermute | solution.py:45
  34.3 2.8 %collective-permute-start.7 = (bf16[256,2048]{1,0:T(8,128)(2,1)S(1)}, bf16[256,2048]{1,0:T(8,128)(2,1)S(1)}, u32[]{:S(2)}, u32[]{:S(2)}) collective-permute-start(bf16[256,2048]{1,0:T(8,128)(2,1)S(1)} %shard_map.81.refs_0_.refs_2_.refs_6_), channel_id=1, source_target_pairs={{12,0},{13,1},{14,2},{15,3},{8,4},{9,5},{10,6},{11,7},{4,8},{5,9},... | collective-permute-start | bytes 3145736 | tf_op jit(solution)/shard_map/ppermute | solution.py:45
  38.4 2.7 %constant_dynamic-slice_fusion = (bf16[1024,1024]{1,0:T(8,128)(2,1)S(1)}, bf16[1024,1024]{1,0:T(8,128)(2,1)S(1)}) fusion(bf16[2048,1024]{1,0:T(8,128)(2,1)} %param.7, s32[]{:T(128)S(6)} %select_n.17, bf16[1024,2048]{1,0:T(8,128)(2,1)} %param.6), kind=kLoop, calls=%fused_computation.49 | loop fusion | bytes 8388612 | tf_op jit(solution)/shard_map/dynamic_slice | solution.py:372
  41.1 9.3 %collective-permute-done.7.refs_1_.refs_3_.refs_7_ = bf16[256,2048]{1,0:T(8,128)(2,1)S(1)} collective-permute-done((bf16[256,2048]{1,0:T(8,128)(2,1)S(1)}, bf16[256,2048]{1,0:T(8,128)(2,1)S(1)}, u32[]{:S(2)}, u32[]{:S(2)}) %collective-permute-start.7) | collective-permute-done | bytes 1048608 | tf_op jit(solution)/shard_map/ppermute | solution.py:45
  50.4 2.4 %collective-permute-done.5.refs_1_.refs_5_ = bf16[256,2048]{1,0:T(8,128)(2,1)} collective-permute-done((bf16[256,2048]{1,0:T(8,128)(2,1)S(1)}, bf16[256,2048]{1,0:T(8,128)(2,1)}, u32[]{:S(2)}, u32[]{:S(2)}) %collective-permute-start.5) | collective-permute-done | bytes 1048608 | tf_op jit(solution)/shard_map/ppermute | solution.py:45
  52.7 4.3 %shard_map.82 = bf16[512,2048]{1,0:T(8,128)(2,1)S(1)} custom-call(s32[2]{0:T(128)S(1)} %pad_add_fusion.place_ref, bf16[256,2048]{1,0:T(8,128)(2,1)S(1)} %shard_map.81.refs_0_.refs_2_.refs_6_, bf16[256,2048]{1,0:T(8,128)(2,1)S(1)} %collective-permute-done.7.refs_1_.refs_3_.refs_7_, bf16[1024,1024]{1,0:T(8,128)(2,1)S(1)} %get-tuple-element.123.refs_2_.refs_3_, ...), custom_call_target="tpu_custom_call" | custom-call | flops 2147483 | bytes 8388 | tf_op jit(solution)/shard_map/pallas_call | solution.py:291
  57.3 3.3 %collective-permute-start.12 = (bf16[128,2048]{1,0:T(8,128)(2,1)S(1)}, bf16[128,2048]{1,0:T(8,128)(2,1)S(1)}, u32[]{:S(2)}, u32[]{:S(2)}) collective-permute-start(bf16[128,2048]{1,0:T(8,128)(2,1)S(1)} %copy-done.3), channel_id=1, source_target_pairs={{1,0},{0,1},{3,2},{2,3},{5,4},{4,5},{7,6},{6,7},{9,8},{8,9},{11,10... | collective-permute-start | bytes 1572872 | tf_op jit(solution)/shard_map/ppermute | solution.py:45
  61.2 5.3 %shard_map.83 = (bf16[256,2048]{1,0:T(8,128)(2,1)S(1)}, bf16[256,2048]{1,0:T(8,128)(2,1)S(1)}) custom-call(s32[2]{0:T(128)S(1)} %pad_add_fusion.place_ref, bf16[256,2048]{1,0:T(8,128)(2,1)S(1)} %shard_map.80.refs_0_.refs_4_, bf16[256,2048]{1,0:T(8,128)(2,1)} %collective-permute-done.5.refs_1_.refs_5_, ...), custom_call_target="tpu_custom_call" | custom-call | flops 2147483 | bytes 8388 | tf_op jit(solution)/shard_map/pallas_call | solution.py:291
  67.2 2.4 %collective-permute-start.11 = (bf16[256,2048]{1,0:T(8,128)(2,1)S(1)}, bf16[256,2048]{1,0:T(8,128)(2,1)S(1)}, u32[]{:S(2)}, u32[]{:S(2)}) collective-permute-start(bf16[256,2048]{1,0:T(8,128)(2,1)S(1)} %shard_map.84.refs_0_.refs_2_.refs_6_), channel_id=1, source_target_pairs={{12,0},{13,1},{14,2},{15,3},{8,4},{9,5},{10,6},{11,7},{4,8},{5,9},... | collective-permute-start | bytes 3145736 | tf_op jit(solution)/shard_map/ppermute | solution.py:45
  70.3 2.0 collective-permute-start.9
  72.3 10.9 %collective-permute-done.11.refs_1_.refs_3_.refs_7_ = bf16[256,2048]{1,0:T(8,128)(2,1)S(1)} collective-permute-done((bf16[256,2048]{1,0:T(8,128)(2,1)S(1)}, bf16[256,2048]{1,0:T(8,128)(2,1)S(1)}, u32[]{:S(2)}, u32[]{:S(2)}) %collective-permute-start.11) | collective-permute-done | bytes 1048608 | tf_op jit(solution)/shard_map/ppermute | solution.py:45
  83.3 1.9 collective-permute-done.13.refs_1_.refs_5_
  85.1 4.3 %shard_map.86 = bf16[512,2048]{1,0:T(8,128)(2,1)S(1)} custom-call(s32[2]{0:T(128)S(1)} %pad_add_fusion.place_ref, bf16[256,2048]{1,0:T(8,128)(2,1)S(1)} %shard_map.84.refs_0_.refs_2_.refs_6_, bf16[256,2048]{1,0:T(8,128)(2,1)S(1)} %collective-permute-done.11.refs_1_.refs_3_.refs_7_, bf16[1024,1024]{1,0:T(8,128)(2,1)S(1)} %get-tuple-element.123.refs_2_.refs_3_, ...), custom_call_target="tpu_custom_call" | custom-call | flops 2147483 | bytes 8388 | tf_op jit(solution)/shard_map/pallas_call | solution.py:291
  89.9 4.3 %collective-permute-start.14 = (bf16[256,2048]{1,0:T(8,128)(2,1)S(1)}, bf16[256,2048]{1,0:T(8,128)(2,1)S(1)}, u32[]{:S(2)}, u32[]{:S(2)}) collective-permute-start(bf16[256,2048]{1,0:T(8,128)(2,1)S(1)} %add_convert_fusion.1), channel_id=1, source_target_pairs={{96,0},{97,1},{98,2},{99,3},{100,4},{101,5},{102,6},{103,7},{104,8... | collective-permute-start | bytes 3145736 | tf_op jit(solution)/shard_map/ppermute | solution.py:45
  94.2 4.5 %shard_map.87 = (bf16[256,2048]{1,0:T(8,128)(2,1)S(1)}, bf16[256,2048]{1,0:T(8,128)(2,1)S(1)}) custom-call(s32[2]{0:T(128)S(1)} %pad_add_fusion.place_ref, bf16[256,2048]{1,0:T(8,128)(2,1)S(1)} %shard_map.85.refs_0_.refs_4_, bf16[256,2048]{1,0:T(8,128)(2,1)S(1)} %collective-permute-done.13.refs_1_.refs_5_, ...), custom_call_target="tpu_custom_call" | custom-call | flops 2147483 | bytes 8388 | tf_op jit(solution)/shard_map/pallas_call | solution.py:291
  98.6 8.3 %collective-permute-done.14 = bf16[256,2048]{1,0:T(8,128)(2,1)S(1)} collective-permute-done((bf16[256,2048]{1,0:T(8,128)(2,1)S(1)}, bf16[256,2048]{1,0:T(8,128)(2,1)S(1)}, u32[]{:S(2)}, u32[]{:S(2)}) %collective-permute-start.14) | collective-permute-done | bytes 1048608 | tf_op jit(solution)/shard_map/ppermute | solution.py:45
  110.1 12.8 %collective-permute-done.16.refs_1_.refs_5_ = bf16[256,2048]{1,0:T(8,128)(2,1)S(1)} collective-permute-done((bf16[256,2048]{1,0:T(8,128)(2,1)S(1)}, bf16[256,2048]{1,0:T(8,128)(2,1)S(1)}, u32[]{:S(2)}, u32[]{:S(2)}) %collective-permute-start.16) | collective-permute-done | bytes 1048608 | tf_op jit(solution)/shard_map/ppermute | solution.py:45
  122.9 4.3 %shard_map.88 = (bf16[256,2048]{1,0:T(8,128)(2,1)S(1)}, bf16[256,2048]{1,0:T(8,128)(2,1)S(1)}) custom-call(s32[2]{0:T(128)S(1)} %pad_add_fusion.place_ref, bf16[256,2048]{1,0:T(8,128)(2,1)S(1)} %pad_maximum_fusion.refs_0_.refs_4_, bf16[256,2048]{1,0:T(8,128)(2,1)S(1)} %collective-permute-done.16.refs_1_.refs_5_, ...), custom_call_target="tpu_custom_call" | custom-call | flops 2147483 | bytes 8388 | tf_op jit(solution)/shard_map/pallas_call | solution.py:291
  127.2 6.9 %collective-permute-done.20 = bf16[256,2048]{1,0:T(8,128)(2,1)S(1)} collective-permute-done((bf16[256,2048]{1,0:T(8,128)(2,1)S(1)}, bf16[256,2048]{1,0:T(8,128)(2,1)S(1)}, u32[]{:S(2)}, u32[]{:S(2)}) %collective-permute-start.20) | collective-permute-done | bytes 1048608 | tf_op jit(solution)/shard_map/ppermute | solution.py:45
  134.6 3.3 %collective-permute-start.22 = (bf16[256,2048]{1,0:T(8,128)(2,1)S(1)}, bf16[256,2048]{1,0:T(8,128)(2,1)S(1)}, u32[]{:S(2)}, u32[]{:S(2)}) collective-permute-start(bf16[256,2048]{1,0:T(8,128)(2,1)S(1)} %add_convert_fusion), channel_id=1, source_target_pairs={{96,0},{97,1},{98,2},{99,3},{100,4},{101,5},{102,6},{103,7},{104,8... | collective-permute-start | bytes 3145736 | tf_op jit(solution)/shard_map/ppermute | solution.py:45
  137.9 1.4 collective-permute-start.17
  139.3 4.3 %shard_map.89 = (bf16[256,2048]{1,0:T(8,128)(2,1)S(1)}, bf16[256,2048]{1,0:T(8,128)(2,1)S(1)}) custom-call(s32[2]{0:T(128)S(1)} %pad_add_fusion.place_ref, bf16[256,2048]{1,0:T(8,128)(2,1)S(1)} %collective-permute-done.18.refs_0_.refs_6_.refs_2_, bf16[256,2048]{1,0:T(8,128)(2,1)S(1)} %collective-permute-done.19.refs_1_.refs_7_.refs_3_, ...), custom_call_target="tpu_custom_call" | custom-call | flops 2147483 | bytes 8388 | tf_op jit(solution)/shard_map/pallas_call | solution.py:291
  143.8 5.6 %shard_map.90.refs_8_ = f32[1024,1024]{1,0:T(8,128)} custom-call(bf16[256,2048]{1,0:T(8,128)(2,1)S(1)} %shard_map.80.refs_0_.refs_4_, bf16[256,2048]{1,0:T(8,128)(2,1)} %collective-permute-done.5.refs_1_.refs_5_, bf16[256,2048]{1,0:T(8,128)(2,1)S(1)} %shard_map.81.refs_0_.refs_2_.refs_6_, ...), custom_call_target="tpu_custom_call" | custom-call | flops 2147483 | bytes 5242 | tf_op jit(solution)/shard_map/pallas_call | solution.py:340
  151.7 2.1 collective-permute-done.17
  153.9 4.6 %collective-permute-done.21 = bf16[256,2048]{1,0:T(8,128)(2,1)S(1)} collective-permute-done((bf16[256,2048]{1,0:T(8,128)(2,1)S(1)}, bf16[256,2048]{1,0:T(8,128)(2,1)S(1)}, u32[]{:S(2)}, u32[]{:S(2)}) %collective-permute-start.21) | collective-permute-done | bytes 1048608 | tf_op jit(solution)/shard_map/ppermute | solution.py:45
  158.9 6.8 %collective-permute-start.25 = (bf16[128,2048]{1,0:T(8,128)(2,1)S(1)}, bf16[128,2048]{1,0:T(8,128)(2,1)S(1)}, u32[]{:S(2)}, u32[]{:S(2)}) collective-permute-start(bf16[128,2048]{1,0:T(8,128)(2,1)S(1)} %slice.230), channel_id=1, source_target_pairs={{1,0},{0,1},{3,2},{2,3},{5,4},{4,5},{7,6},{6,7},{9,8},{8,9},{11,10... | collective-permute-start | bytes 1572872 | tf_op jit(solution)/shard_map/ppermute | solution.py:45
  166.4 5.6 %shard_map.91.refs_8_ = f32[1024,1024]{1,0:T(8,128)} custom-call(bf16[256,2048]{1,0:T(8,128)(2,1)S(1)} %pad_maximum_fusion.refs_0_.refs_4_, bf16[256,2048]{1,0:T(8,128)(2,1)S(1)} %collective-permute-done.16.refs_1_.refs_5_, bf16[256,2048]{1,0:T(8,128)(2,1)S(1)} %collective-permute-done.18.refs_0_.refs_6_.refs_2_, ...), custom_call_target="tpu_custom_call" | custom-call | flops 2147483 | bytes 5242 | tf_op jit(solution)/shard_map/pallas_call | solution.py:340
  172.9 2.5 %collective-permute-done.23 = bf16[128,2048]{1,0:T(8,128)(2,1)S(1)} collective-permute-done((bf16[128,2048]{1,0:T(8,128)(2,1)S(1)}, bf16[128,2048]{1,0:T(8,128)(2,1)S(1)}, u32[]{:S(2)}, u32[]{:S(2)}) %collective-permute-start.23) | collective-permute-done | bytes 524320 | tf_op jit(solution)/shard_map/ppermute | solution.py:45
  175.9 3.1 %shard_map.92 = bf16[256,2048]{1,0:T(8,128)(2,1)S(1)} custom-call(s32[2]{0:T(128)S(1)} %pad_add_fusion.place_ref, bf16[256,2048]{1,0:T(8,128)(2,1)S(1)} %pad_maximum_fusion.1.refs_0_.refs_4_, bf16[256,2048]{1,0:T(8,128)(2,1)S(1)} %collective-permute-done.24.refs_1_.refs_5_, bf16[1024,1024]{1,0:T(8,128)(2,1)S(1)} %get-tuple-element.122.refs_3_.refs_2_, ...), custom_call_target="tpu_custom_call" | custom-call | flops 2147483 | bytes 8388 | tf_op jit(solution)/shard_map/pallas_call | solution.py:291
  180.2 3.1 %shard_map.93 = bf16[256,2048]{1,0:T(8,128)(2,1)S(1)} custom-call(s32[2]{0:T(128)S(1)} %pad_add_fusion.place_ref, bf16[256,2048]{1,0:T(8,128)(2,1)S(1)} %collective-permute-done.26.refs_0_.refs_6_.refs_2_, bf16[256,2048]{1,0:T(8,128)(2,1)S(1)} %collective-permute-done.27.refs_1_.refs_7_.refs_3_, bf16[1024,1024]{1,0:T(8,128)(2,1)S(1)} %get-tuple-element.122.refs_3_.refs_2_, ...), custom_call_target="tpu_custom_call" | custom-call | flops 2147483 | bytes 8388 | tf_op jit(solution)/shard_map/pallas_call | solution.py:291
  183.6 3.2 %shard_map.94 = bf16[256,2048]{1,0:T(8,128)(2,1)S(1)} custom-call(s32[2]{0:T(128)S(1)} %pad_add_fusion.place_ref, bf16[256,2048]{1,0:T(8,128)(2,1)S(1)} %pad_maximum_fusion.1.refs_0_.refs_4_, bf16[256,2048]{1,0:T(8,128)(2,1)S(1)} %collective-permute-done.24.refs_1_.refs_5_, bf16[1024,1024]{1,0:T(8,128)(2,1)S(1)} %get-tuple-element.122.refs_3_.refs_2_, ...), custom_call_target="tpu_custom_call" | custom-call | flops 2147483 | bytes 8388 | tf_op jit(solution)/shard_map/pallas_call | solution.py:291
  186.7 3.1 %shard_map.95 = bf16[256,2048]{1,0:T(8,128)(2,1)S(1)} custom-call(s32[2]{0:T(128)S(1)} %pad_add_fusion.place_ref, bf16[256,2048]{1,0:T(8,128)(2,1)S(1)} %collective-permute-done.26.refs_0_.refs_6_.refs_2_, bf16[256,2048]{1,0:T(8,128)(2,1)S(1)} %collective-permute-done.27.refs_1_.refs_7_.refs_3_, bf16[1024,1024]{1,0:T(8,128)(2,1)S(1)} %get-tuple-element.122.refs_3_.refs_2_, ...), custom_call_target="tpu_custom_call" | custom-call | flops 2147483 | bytes 8388 | tf_op jit(solution)/shard_map/pallas_call | solution.py:291
  189.9 6.5 %shard_map.96 = f32[1024,1024]{1,0:T(8,128)} custom-call(bf16[256,2048]{1,0:T(8,128)(2,1)S(1)} %shard_map.85.refs_0_.refs_4_, bf16[256,2048]{1,0:T(8,128)(2,1)S(1)} %collective-permute-done.13.refs_1_.refs_5_, bf16[256,2048]{1,0:T(8,128)(2,1)S(1)} %shard_map.84.refs_0_.refs_2_.refs_6_, ...), custom_call_target="tpu_custom_call", output_to_operand_aliasing={{}: (8, {})} | custom-call | flops 2147483 | bytes 5242 | tf_op jit(solution)/shard_map/pallas_call | solution.py:340
  196.4 1.9 collective-permute-done.29
  200.9 6.5 %shard_map.97 = f32[1024,1024]{1,0:T(8,128)} custom-call(bf16[256,2048]{1,0:T(8,128)(2,1)S(1)} %pad_maximum_fusion.1.refs_0_.refs_4_, bf16[256,2048]{1,0:T(8,128)(2,1)S(1)} %collective-permute-done.24.refs_1_.refs_5_, bf16[256,2048]{1,0:T(8,128)(2,1)S(1)} %collective-permute-done.26.refs_0_.refs_6_.refs_2_, ...), custom_call_target="tpu_custom_call", output_to_operand_aliasing={{}: (8, {})} | custom-call | flops 2147483 | bytes 5242 | tf_op jit(solution)/shard_map/pallas_call | solution.py:340
  208.2 2.2 collective-permute-start.34
  211.0 7.7 %collective-permute-done.34 = bf16[128,2048]{1,0:T(8,128)(2,1)S(1)} collective-permute-done((bf16[128,2048]{1,0:T(8,128)(2,1)S(1)}, bf16[128,2048]{1,0:T(8,128)(2,1)S(1)}, u32[]{:S(2)}, u32[]{:S(2)}) %collective-permute-start.34) | collective-permute-done | bytes 524320 | tf_op jit(solution)/shard_map/ppermute | solution.py:45
  218.9 2.9 %collective-permute-done.31 = bf16[128,2048]{1,0:T(8,128)(2,1)S(1)} collective-permute-done((bf16[128,2048]{1,0:T(8,128)(2,1)S(1)}, bf16[128,2048]{1,0:T(8,128)(2,1)S(1)}, u32[]{:S(2)}, u32[]{:S(2)}) %collective-permute-start.31) | collective-permute-done | bytes 524320 | tf_op jit(solution)/shard_map/ppermute | solution.py:45
  222.0 2.0 collective-permute-start.32
  225.3 3.1 %collective-permute-done.32 = bf16[64,2048]{1,0:T(8,128)(2,1)S(1)} collective-permute-done((bf16[64,2048]{1,0:T(8,128)(2,1)S(1)}, bf16[64,2048]{1,0:T(8,128)(2,1)S(1)}, u32[]{:S(2)}, u32[]{:S(2)}) %collective-permute-start.32) | collective-permute-done | bytes 262176 | tf_op jit(solution)/shard_map/ppermute | solution.py:45
  228.5 1.4 shard_map.98
  (100 shorter events, 27.5 us)
Async XLA Ops:
  0.7 1.0 copy-start.4
  1.7 0.9 copy-start.5
  3.3 6.5 %collective-permute-start.2 = (bf16[64,2048]{1,0:T(8,128)(2,1)S(1)}, bf16[64,2048]{1,0:T(8,128)(2,1)S(1)}, u32[]{:S(2)}, u32[]{:S(2)}) collective-permute-start(bf16[64,2048]{1,0:T(8,128)(2,1)S(1)} %get-tuple-element.49.a_ref), channel_id=1, source_target_pairs={{1,0},{0,1},{3,2},{2,3},{5,4},{4,5},{7,6},{6,7},{9,8},{8,9},{11,10... | collective-permute-start | bytes 786440 | tf_op jit(solution)/shard_map/ppermute | solution.py:45
  3.8 8.2 %collective-permute-start = (bf16[64,2048]{1,0:T(8,128)(2,1)S(1)}, bf16[64,2048]{1,0:T(8,128)(2,1)S(1)}, u32[]{:S(2)}, u32[]{:S(2)}) collective-permute-start(bf16[64,2048]{1,0:T(8,128)(2,1)S(1)} %get-tuple-element.47.a_ref), channel_id=1, source_target_pairs={{4,0},{5,1},{6,2},{7,3},{0,4},{1,5},{2,6},{3,7},{12,8},{13,9},{14,... | collective-permute-start | bytes 786440 | tf_op jit(solution)/shard_map/ppermute | solution.py:45
  10.3 9.3 %collective-permute-start.3 = (bf16[128,2048]{1,0:T(8,128)(2,1)S(1)}, bf16[128,2048]{1,0:T(8,128)(2,1)S(1)}, u32[]{:S(2)}, u32[]{:S(2)}) collective-permute-start(bf16[128,2048]{1,0:T(8,128)(2,1)S(1)} %shard_map.78), channel_id=1, source_target_pairs={{3,0},{2,1},{1,2},{0,3},{7,4},{6,5},{5,6},{4,7},{11,8},{10,9},{9,1... | collective-permute-start | bytes 1572872 | tf_op jit(solution)/shard_map/ppermute | solution.py:45
  12.6 10.5 %collective-permute-start.1 = (bf16[128,2048]{1,0:T(8,128)(2,1)S(1)}, bf16[128,2048]{1,0:T(8,128)(2,1)S(1)}, u32[]{:S(2)}, u32[]{:S(2)}) collective-permute-start(bf16[128,2048]{1,0:T(8,128)(2,1)S(1)} %shard_map.76), channel_id=1, source_target_pairs={{12,0},{13,1},{14,2},{15,3},{8,4},{9,5},{10,6},{11,7},{4,8},{5,9},... | collective-permute-start | bytes 1572872 | tf_op jit(solution)/shard_map/ppermute | solution.py:45
  20.2 0.8 copy-start
  23.7 0.8 copy-start.2
  24.5 9.2 %collective-permute-start.6 = (bf16[128,2048]{1,0:T(8,128)(2,1)S(1)}, bf16[128,2048]{1,0:T(8,128)(2,1)S(1)}, u32[]{:S(2)}, u32[]{:S(2)}) collective-permute-start(bf16[128,2048]{1,0:T(8,128)(2,1)S(1)} %get-tuple-element.52.a_ref), channel_id=1, source_target_pairs={{4,0},{5,1},{6,2},{7,3},{0,4},{1,5},{2,6},{3,7},{12,8},{13,9},{14,... | collective-permute-start | bytes 1572872 | tf_op jit(solution)/shard_map/ppermute | solution.py:45
  24.8 12.4 %collective-permute-start.4 = (bf16[128,2048]{1,0:T(8,128)(2,1)S(1)}, bf16[128,2048]{1,0:T(8,128)(2,1)S(1)}, u32[]{:S(2)}, u32[]{:S(2)}) collective-permute-start(bf16[128,2048]{1,0:T(8,128)(2,1)S(1)} %get-tuple-element.51.a_ref), channel_id=1, source_target_pairs={{1,0},{0,1},{3,2},{2,3},{5,4},{4,5},{7,6},{6,7},{9,8},{8,9},{11,10... | collective-permute-start | bytes 1572872 | tf_op jit(solution)/shard_map/ppermute | solution.py:45
  34.3 16.1 %collective-permute-start.7 = (bf16[256,2048]{1,0:T(8,128)(2,1)S(1)}, bf16[256,2048]{1,0:T(8,128)(2,1)S(1)}, u32[]{:S(2)}, u32[]{:S(2)}) collective-permute-start(bf16[256,2048]{1,0:T(8,128)(2,1)S(1)} %shard_map.81.refs_0_.refs_2_.refs_6_), channel_id=1, source_target_pairs={{12,0},{13,1},{14,2},{15,3},{8,4},{9,5},{10,6},{11,7},{4,8},{5,9},... | collective-permute-start | bytes 3145736 | tf_op jit(solution)/shard_map/ppermute | solution.py:45
  37.7 15.0 %collective-permute-start.5 = (bf16[256,2048]{1,0:T(8,128)(2,1)S(1)}, bf16[256,2048]{1,0:T(8,128)(2,1)}, u32[]{:S(2)}, u32[]{:S(2)}) collective-permute-start(bf16[256,2048]{1,0:T(8,128)(2,1)S(1)} %shard_map.80.refs_0_.refs_4_), channel_id=1, source_target_pairs={{3,0},{2,1},{1,2},{0,3},{7,4},{6,5},{5,6},{4,7},{11,8},{10,9},{9,1... | collective-permute-start | bytes 3145736 | tf_op jit(solution)/shard_map/ppermute | solution.py:45
  52.7 4.4 %copy-start.1 = (bf16[128,2048]{1,0:T(8,128)(2,1)S(1)}, bf16[128,2048]{1,0:T(8,128)(2,1)}, u32[]{:S(2)}) copy-start(bf16[128,2048]{1,0:T(8,128)(2,1)} %copy-done) | copy-start | bytes 1572868
  52.7 4.6 %copy-start.3 = (bf16[128,2048]{1,0:T(8,128)(2,1)S(1)}, bf16[128,2048]{1,0:T(8,128)(2,1)}, u32[]{:S(2)}) copy-start(bf16[128,2048]{1,0:T(8,128)(2,1)} %copy-done.2) | copy-start | bytes 1572868
  57.0 4.2 %collective-permute-start.8 = (bf16[512,2048]{1,0:T(8,128)(2,1)S(1)}, bf16[512,2048]{1,0:T(8,128)(2,1)S(1)}, u32[]{:S(2)}, u32[]{:S(2)}) collective-permute-start(bf16[512,2048]{1,0:T(8,128)(2,1)S(1)} %shard_map.82), channel_id=1, source_target_pairs={{16,0},{17,1},{18,2},{19,3},{20,4},{21,5},{22,6},{23,7},{24,8},{25... | collective-permute-start | bytes 6291464 | tf_op jit(solution)/shard_map/ppermute | solution.py:45
  57.1 9.4 %collective-permute-start.10 = (bf16[128,2048]{1,0:T(8,128)(2,1)S(1)}, bf16[128,2048]{1,0:T(8,128)(2,1)S(1)}, u32[]{:S(2)}, u32[]{:S(2)}) collective-permute-start(bf16[128,2048]{1,0:T(8,128)(2,1)S(1)} %copy-done.1), channel_id=1, source_target_pairs={{4,0},{5,1},{6,2},{7,3},{0,4},{1,5},{2,6},{3,7},{12,8},{13,9},{14,... | collective-permute-start | bytes 1572872 | tf_op jit(solution)/shard_map/ppermute | solution.py:45
  57.3 12.3 %collective-permute-start.12 = (bf16[128,2048]{1,0:T(8,128)(2,1)S(1)}, bf16[128,2048]{1,0:T(8,128)(2,1)S(1)}, u32[]{:S(2)}, u32[]{:S(2)}) collective-permute-start(bf16[128,2048]{1,0:T(8,128)(2,1)S(1)} %copy-done.3), channel_id=1, source_target_pairs={{1,0},{0,1},{3,2},{2,3},{5,4},{4,5},{7,6},{6,7},{9,8},{8,9},{11,10... | collective-permute-start | bytes 1572872 | tf_op jit(solution)/shard_map/ppermute | solution.py:45
  67.2 16.1 %collective-permute-start.11 = (bf16[256,2048]{1,0:T(8,128)(2,1)S(1)}, bf16[256,2048]{1,0:T(8,128)(2,1)S(1)}, u32[]{:S(2)}, u32[]{:S(2)}) collective-permute-start(bf16[256,2048]{1,0:T(8,128)(2,1)S(1)} %shard_map.84.refs_0_.refs_2_.refs_6_), channel_id=1, source_target_pairs={{12,0},{13,1},{14,2},{15,3},{8,4},{9,5},{10,6},{11,7},{4,8},{5,9},... | collective-permute-start | bytes 3145736 | tf_op jit(solution)/shard_map/ppermute | solution.py:45
  70.2 14.9 %collective-permute-start.13 = (bf16[256,2048]{1,0:T(8,128)(2,1)S(1)}, bf16[256,2048]{1,0:T(8,128)(2,1)S(1)}, u32[]{:S(2)}, u32[]{:S(2)}) collective-permute-start(bf16[256,2048]{1,0:T(8,128)(2,1)S(1)} %shard_map.85.refs_0_.refs_4_), channel_id=1, source_target_pairs={{3,0},{2,1},{1,2},{0,3},{7,4},{6,5},{5,6},{4,7},{11,8},{10,9},{9,1... | collective-permute-start | bytes 3145736 | tf_op jit(solution)/shard_map/ppermute | solution.py:45
  70.3 19.2 %collective-permute-start.9 = (bf16[256,2048]{1,0:T(8,128)(2,1)S(1)}, bf16[256,2048]{1,0:T(8,128)(2,1)S(1)}, u32[]{:S(2)}, u32[]{:S(2)}) collective-permute-start(bf16[256,2048]{1,0:T(8,128)(2,1)S(1)} %get-tuple-element.55), channel_id=1, source_target_pairs={{32,0},{33,1},{34,2},{35,3},{36,4},{37,5},{38,6},{39,7},{40,8},{41... | collective-permute-start | bytes 3145736 | tf_op jit(solution)/shard_map/ppermute | solution.py:45
  89.4 4.8 %collective-permute-start.15 = (bf16[512,2048]{1,0:T(8,128)(2,1)S(1)}, bf16[512,2048]{1,0:T(8,128)(2,1)S(1)}, u32[]{:S(2)}, u32[]{:S(2)}) collective-permute-start(bf16[512,2048]{1,0:T(8,128)(2,1)S(1)} %shard_map.86), channel_id=1, source_target_pairs={{16,0},{17,1},{18,2},{19,3},{20,4},{21,5},{22,6},{23,7},{24,8},{25... | collective-permute-start | bytes 6291464 | tf_op jit(solution)/shard_map/ppermute | solution.py:45
  89.9 17.1 %collective-permute-start.14 = (bf16[256,2048]{1,0:T(8,128)(2,1)S(1)}, bf16[256,2048]{1,0:T(8,128)(2,1)S(1)}, u32[]{:S(2)}, u32[]{:S(2)}) collective-permute-start(bf16[256,2048]{1,0:T(8,128)(2,1)S(1)} %add_convert_fusion.1), channel_id=1, source_target_pairs={{96,0},{97,1},{98,2},{99,3},{100,4},{101,5},{102,6},{103,7},{104,8... | collective-permute-start | bytes 3145736 | tf_op jit(solution)/shard_map/ppermute | solution.py:45
  108.0 14.9 %collective-permute-start.16 = (bf16[256,2048]{1,0:T(8,128)(2,1)S(1)}, bf16[256,2048]{1,0:T(8,128)(2,1)S(1)}, u32[]{:S(2)}, u32[]{:S(2)}) collective-permute-start(bf16[256,2048]{1,0:T(8,128)(2,1)S(1)} %pad_maximum_fusion.refs_0_.refs_4_), channel_id=1, source_target_pairs={{32,0},{33,1},{34,2},{35,3},{36,4},{37,5},{38,6},{39,7},{40,8},{41... | collective-permute-start | bytes 3145736 | tf_op jit(solution)/shard_map/ppermute | solution.py:45
  108.1 26.0 %collective-permute-start.18 = (bf16[256,2048]{1,0:T(8,128)(2,1)S(1)}, bf16[256,2048]{1,0:T(8,128)(2,1)S(1)}, u32[]{:S(2)}, u32[]{:S(2)}) collective-permute-start(bf16[256,2048]{1,0:T(8,128)(2,1)S(1)} %pad_maximum_fusion.refs_0_.refs_4_), channel_id=1, source_target_pairs={{16,0},{17,1},{18,2},{19,3},{20,4},{21,5},{22,6},{23,7},{24,8},{25... | collective-permute-start | bytes 3145736 | tf_op jit(solution)/shard_map/ppermute | solution.py:45
  109.5 24.7 %collective-permute-start.20 = (bf16[256,2048]{1,0:T(8,128)(2,1)S(1)}, bf16[256,2048]{1,0:T(8,128)(2,1)S(1)}, u32[]{:S(2)}, u32[]{:S(2)}) collective-permute-start(bf16[256,2048]{1,0:T(8,128)(2,1)S(1)} %get-tuple-element.66), channel_id=1, source_target_pairs={{32,0},{33,1},{34,2},{35,3},{36,4},{37,5},{38,6},{39,7},{40,8},{41... | collective-permute-start | bytes 3145736 | tf_op jit(solution)/shard_map/ppermute | solution.py:45
  122.9 11.2 %collective-permute-start.19 = (bf16[256,2048]{1,0:T(8,128)(2,1)S(1)}, bf16[256,2048]{1,0:T(8,128)(2,1)S(1)}, u32[]{:S(2)}, u32[]{:S(2)}) collective-permute-start(bf16[256,2048]{1,0:T(8,128)(2,1)S(1)} %collective-permute-done.16.refs_1_.refs_5_), channel_id=1, source_target_pairs={{16,0},{17,1},{18,2},{19,3},{20,4},{21,5},{22,6},{23,7},{24,8},{25... | collective-permute-start | bytes 3145736 | tf_op jit(solution)/shard_map/ppermute | solution.py:45
  134.6 16.1 %collective-permute-start.22 = (bf16[256,2048]{1,0:T(8,128)(2,1)S(1)}, bf16[256,2048]{1,0:T(8,128)(2,1)S(1)}, u32[]{:S(2)}, u32[]{:S(2)}) collective-permute-start(bf16[256,2048]{1,0:T(8,128)(2,1)S(1)} %add_convert_fusion), channel_id=1, source_target_pairs={{96,0},{97,1},{98,2},{99,3},{100,4},{101,5},{102,6},{103,7},{104,8... | collective-permute-start | bytes 3145736 | tf_op jit(solution)/shard_map/ppermute | solution.py:45
  137.9 16.0 %collective-permute-start.17 = (bf16[256,2048]{1,0:T(8,128)(2,1)S(1)}, bf16[256,2048]{1,0:T(8,128)(2,1)S(1)}, u32[]{:S(2)}, u32[]{:S(2)}) collective-permute-start(bf16[256,2048]{1,0:T(8,128)(2,1)S(1)} %get-tuple-element.65), channel_id=1, source_target_pairs={{12,0},{13,1},{14,2},{15,3},{8,4},{9,5},{10,6},{11,7},{4,8},{5,9},... | collective-permute-start | bytes 3145736 | tf_op jit(solution)/shard_map/ppermute | solution.py:45
  143.6 14.9 %collective-permute-start.21 = (bf16[256,2048]{1,0:T(8,128)(2,1)S(1)}, bf16[256,2048]{1,0:T(8,128)(2,1)S(1)}, u32[]{:S(2)}, u32[]{:S(2)}) collective-permute-start(bf16[256,2048]{1,0:T(8,128)(2,1)S(1)} %get-tuple-element.70), channel_id=1, source_target_pairs={{3,0},{2,1},{1,2},{0,3},{7,4},{6,5},{5,6},{4,7},{11,8},{10,9},{9,1... | collective-permute-start | bytes 3145736 | tf_op jit(solution)/shard_map/ppermute | solution.py:45
  151.7 23.8 %collective-permute-start.24 = (bf16[256,2048]{1,0:T(8,128)(2,1)S(1)}, bf16[256,2048]{1,0:T(8,128)(2,1)S(1)}, u32[]{:S(2)}, u32[]{:S(2)}) collective-permute-start(bf16[256,2048]{1,0:T(8,128)(2,1)S(1)} %pad_maximum_fusion.1.refs_0_.refs_4_), channel_id=1, source_target_pairs={{32,0},{33,1},{34,2},{35,3},{36,4},{37,5},{38,6},{39,7},{40,8},{41... | collective-permute-start | bytes 3145736 | tf_op jit(solution)/shard_map/ppermute | solution.py:45
  158.9 14.0 %collective-permute-start.25 = (bf16[128,2048]{1,0:T(8,128)(2,1)S(1)}, bf16[128,2048]{1,0:T(8,128)(2,1)S(1)}, u32[]{:S(2)}, u32[]{:S(2)}) collective-permute-start(bf16[128,2048]{1,0:T(8,128)(2,1)S(1)} %slice.230), channel_id=1, source_target_pairs={{1,0},{0,1},{3,2},{2,3},{5,4},{4,5},{7,6},{6,7},{9,8},{8,9},{11,10... | collective-permute-start | bytes 1572872 | tf_op jit(solution)/shard_map/ppermute | solution.py:45
  166.2 9.3 %collective-permute-start.23 = (bf16[128,2048]{1,0:T(8,128)(2,1)S(1)}, bf16[128,2048]{1,0:T(8,128)(2,1)S(1)}, u32[]{:S(2)}, u32[]{:S(2)}) collective-permute-start(bf16[128,2048]{1,0:T(8,128)(2,1)S(1)} %slice.231), channel_id=1, source_target_pairs={{4,0},{5,1},{6,2},{7,3},{0,4},{1,5},{2,6},{3,7},{12,8},{13,9},{14,... | collective-permute-start | bytes 1572872 | tf_op jit(solution)/shard_map/ppermute | solution.py:45
  166.3 9.6 %collective-permute-start.26 = (bf16[256,2048]{1,0:T(8,128)(2,1)S(1)}, bf16[256,2048]{1,0:T(8,128)(2,1)S(1)}, u32[]{:S(2)}, u32[]{:S(2)}) collective-permute-start(bf16[256,2048]{1,0:T(8,128)(2,1)S(1)} %pad_maximum_fusion.1.refs_0_.refs_4_), channel_id=1, source_target_pairs={{16,0},{17,1},{18,2},{19,3},{20,4},{21,5},{22,6},{23,7},{24,8},{25... | collective-permute-start | bytes 3145736 | tf_op jit(solution)/shard_map/ppermute | solution.py:45
  175.5 4.7 %collective-permute-start.27 = (bf16[256,2048]{1,0:T(8,128)(2,1)S(1)}, bf16[256,2048]{1,0:T(8,128)(2,1)S(1)}, u32[]{:S(2)}, u32[]{:S(2)}) collective-permute-start(bf16[256,2048]{1,0:T(8,128)(2,1)S(1)} %collective-permute-done.24.refs_1_.refs_5_), channel_id=1, source_target_pairs={{16,0},{17,1},{18,2},{19,3},{20,4},{21,5},{22,6},{23,7},{24,8},{25... | collective-permute-start | bytes 3145736 | tf_op jit(solution)/shard_map/ppermute | solution.py:45
  179.0 17.3 %collective-permute-start.28 = (bf16[256,2048]{1,0:T(8,128)(2,1)S(1)}, bf16[256,2048]{1,0:T(8,128)(2,1)S(1)}, u32[]{:S(2)}, u32[]{:S(2)}) collective-permute-start(bf16[256,2048]{1,0:T(8,128)(2,1)S(1)} %shard_map.92), channel_id=1, source_target_pairs={{12,0},{13,1},{14,2},{15,3},{8,4},{9,5},{10,6},{11,7},{4,8},{5,9},... | collective-permute-start | bytes 3145736 | tf_op jit(solution)/shard_map/ppermute | solution.py:45
  183.3 14.9 %collective-permute-start.29 = (bf16[256,2048]{1,0:T(8,128)(2,1)S(1)}, bf16[256,2048]{1,0:T(8,128)(2,1)S(1)}, u32[]{:S(2)}, u32[]{:S(2)}) collective-permute-start(bf16[256,2048]{1,0:T(8,128)(2,1)S(1)} %shard_map.93), channel_id=1, source_target_pairs={{3,0},{2,1},{1,2},{0,3},{7,4},{6,5},{5,6},{4,7},{11,8},{10,9},{9,1... | collective-permute-start | bytes 3145736 | tf_op jit(solution)/shard_map/ppermute | solution.py:45
  198.6 9.3 %collective-permute-start.33 = (bf16[128,2048]{1,0:T(8,128)(2,1)S(1)}, bf16[128,2048]{1,0:T(8,128)(2,1)S(1)}, u32[]{:S(2)}, u32[]{:S(2)}) collective-permute-start(bf16[128,2048]{1,0:T(8,128)(2,1)S(1)} %slice.228), channel_id=1, source_target_pairs={{1,0},{0,1},{3,2},{2,3},{5,4},{4,5},{7,6},{6,7},{9,8},{8,9},{11,10... | collective-permute-start | bytes 1572872 | tf_op jit(solution)/shard_map/ppermute | solution.py:45
  200.4 10.0 %collective-permute-start.30 = (bf16[128,2048]{1,0:T(8,128)(2,1)S(1)}, bf16[128,2048]{1,0:T(8,128)(2,1)S(1)}, u32[]{:S(2)}, u32[]{:S(2)}) collective-permute-start(bf16[128,2048]{1,0:T(8,128)(2,1)S(1)} %slice.229), channel_id=1, source_target_pairs={{4,0},{5,1},{6,2},{7,3},{0,4},{1,5},{2,6},{3,7},{12,8},{13,9},{14,... | collective-permute-start | bytes 1572872 | tf_op jit(solution)/shard_map/ppermute | solution.py:45
  208.2 10.5 %collective-permute-start.34 = (bf16[128,2048]{1,0:T(8,128)(2,1)S(1)}, bf16[128,2048]{1,0:T(8,128)(2,1)S(1)}, u32[]{:S(2)}, u32[]{:S(2)}) collective-permute-start(bf16[128,2048]{1,0:T(8,128)(2,1)S(1)} %pad_maximum_fusion.3), channel_id=1, source_target_pairs={{12,0},{13,1},{14,2},{15,3},{8,4},{9,5},{10,6},{11,7},{4,8},{5,9},... | collective-permute-start | bytes 1572872 | tf_op jit(solution)/shard_map/ppermute | solution.py:45
  210.7 11.1 %collective-permute-start.31 = (bf16[128,2048]{1,0:T(8,128)(2,1)S(1)}, bf16[128,2048]{1,0:T(8,128)(2,1)S(1)}, u32[]{:S(2)}, u32[]{:S(2)}) collective-permute-start(bf16[128,2048]{1,0:T(8,128)(2,1)S(1)} %pad_maximum_fusion.2), channel_id=1, source_target_pairs={{3,0},{2,1},{1,2},{0,3},{7,4},{6,5},{5,6},{4,7},{11,8},{10,9},{9,1... | collective-permute-start | bytes 1572872 | tf_op jit(solution)/shard_map/ppermute | solution.py:45
  218.8 6.5 %collective-permute-start.35 = (bf16[64,2048]{1,0:T(8,128)(2,1)S(1)}, bf16[64,2048]{1,0:T(8,128)(2,1)S(1)}, u32[]{:S(2)}, u32[]{:S(2)}) collective-permute-start(bf16[64,2048]{1,0:T(8,128)(2,1)S(1)} %fusion.12), channel_id=1, source_target_pairs={{4,0},{5,1},{6,2},{7,3},{0,4},{1,5},{2,6},{3,7},{12,8},{13,9},{14,... | collective-permute-start | bytes 786440 | tf_op jit(solution)/shard_map/ppermute | solution.py:45
  222.0 6.5 %collective-permute-start.32 = (bf16[64,2048]{1,0:T(8,128)(2,1)S(1)}, bf16[64,2048]{1,0:T(8,128)(2,1)S(1)}, u32[]{:S(2)}, u32[]{:S(2)}) collective-permute-start(bf16[64,2048]{1,0:T(8,128)(2,1)S(1)} %fusion.15), channel_id=1, source_target_pairs={{1,0},{0,1},{3,2},{2,3},{5,4},{4,5},{7,6},{6,7},{9,8},{8,9},{11,10... | collective-permute-start | bytes 786440 | tf_op jit(solution)/shard_map/ppermute | solution.py:45

commit v14 on v13

--- a/solution.py
+++ b/solution.py
@@ -321,7 +321,7 @@
     out_ref[...] = total + refs[8][...] if begun else total
 
 
-def grad_dot(lefts, left_part, rights, right_part, pairs, factor, begun=None, tile=256):
+def grad_dot(lefts, left_part, rights, right_part, pairs, factor, begun=None, tile=512):
     wide = lefts[0].shape[1] // 2
     tiles = wide // tile
     tokens = sum(a.shape[0] for a in lefts)
@@ -344,7 +344,7 @@
         out_specs=out_spec,
         out_shape=jax.ShapeDtypeStruct((wide, wide), F32),
         input_output_aliases=aliases,
-        compiler_params=pltpu.CompilerParams(vmem_limit_bytes=24 * 2**20),
+        compiler_params=pltpu.CompilerParams(vmem_limit_bytes=30 * 2**20),
         cost_estimate=cost(
             flops=2 * tokens * wide * wide,
             bytes_accessed=3 * tokens * wide + 2 * wide * wide,

time: 232 us -> 232 us (level)
  Pallas kernels: 70.5 us -> 67.6 us
    pallas_call x4, Pallas kernels: 24.1 us -> 21.3 us  [grad_dot(): pl.pallas_call(functools.partial(grad_kernel, pairs, block, factor, begun...]
    ppermute x36, waiting for transfers between devices: 99.7 us -> 102 us  [exchange(): return lax.ppermute(array, AXES, pairs)]
  transfers between devices with their start and end apart: 36 -> 36, of which waited for: 23 -> 23; matrix products, arithmetic and copies ran while one was open for 3% -> 3% of each run, Pallas kernels for 28% -> 26%
where the time goes in v14:
time: 232 us; the launch traced here: 230 us
  waiting for transfers between devices  102 us (44%)
  Pallas kernels  67.6 us (29%)
  starting transfers between devices  46.5 us (20%)
  local copies, waits for them, and re-layouts  6.83 us (3%)
  other arithmetic  5.41 us (2%)
    ppermute x36, waiting for transfers between devices, exchange(): return lax.ppermute(array, AXES, pairs)  102 us
    ppermute x36, starting transfers between devices, exchange(): return lax.ppermute(array, AXES, pairs)  46.5 us
    pallas_call x10, Pallas kernels, pair_dot(): pl.pallas_call(functools.partial(pair_kernel, keep, hidden, more is not N...  39.5 us
    pallas_call x4, Pallas kernels, grad_dot(): pl.pallas_call(functools.partial(grad_kernel, pairs, block, factor, begun...  21.3 us
    pallas_call x8, Pallas kernels, whole(): pl.pallas_call(kernel, in_specs=[pl.BlockSpec(memory_space=pltpu.SMEM)] +...  4.82 us
  transfers between devices with their start and end apart: 36, of which 23 were waited for; matrix products, arithmetic and copies ran while one was open for 3% of the time, Pallas kernels for 26%

profile of v14, /device:TPU:8, one launch (start us, length us, event | category | flops | bytes accessed | tf_op | source)
XLA Modules:
  0.0 230.0 jit_solution(14669414515687304911)
XLA Ops:
  3.8 1.6 collective-permute-start
  5.3 4.4 %collective-permute-done.2.b_ref = bf16[64,2048]{1,0:T(8,128)(2,1)S(1)} collective-permute-done((bf16[64,2048]{1,0:T(8,128)(2,1)S(1)}, bf16[64,2048]{1,0:T(8,128)(2,1)S(1)}, u32[]{:S(2)}, u32[]{:S(2)}) %collective-permute-start.2) | collective-permute-done | bytes 262176 | tf_op jit(solution)/shard_map/ppermute | solution.py:45
  10.3 1.7 collective-permute-start.3
  12.6 2.8 %collective-permute-start.1 = (bf16[128,2048]{1,0:T(8,128)(2,1)S(1)}, bf16[128,2048]{1,0:T(8,128)(2,1)S(1)}, u32[]{:S(2)}, u32[]{:S(2)}) collective-permute-start(bf16[128,2048]{1,0:T(8,128)(2,1)S(1)} %shard_map.76), channel_id=1, source_target_pairs={{12,0},{13,1},{14,2},{15,3},{8,4},{9,5},{10,6},{11,7},{4,8},{5,9},... | collective-permute-start | bytes 1572872 | tf_op jit(solution)/shard_map/ppermute | solution.py:45
  15.4 4.2 %collective-permute-done.3.c_ref = bf16[128,2048]{1,0:T(8,128)(2,1)S(1)} collective-permute-done((bf16[128,2048]{1,0:T(8,128)(2,1)S(1)}, bf16[128,2048]{1,0:T(8,128)(2,1)S(1)}, u32[]{:S(2)}, u32[]{:S(2)}) %collective-permute-start.3) | collective-permute-done | bytes 524320 | tf_op jit(solution)/shard_map/ppermute | solution.py:45
  21.0 2.0 collective-permute-done.1.c_ref
  24.8 1.9 collective-permute-start.4
  26.7 7.0 %collective-permute-done.6.b_ref = bf16[128,2048]{1,0:T(8,128)(2,1)S(1)} collective-permute-done((bf16[128,2048]{1,0:T(8,128)(2,1)S(1)}, bf16[128,2048]{1,0:T(8,128)(2,1)S(1)}, u32[]{:S(2)}, u32[]{:S(2)}) %collective-permute-start.6) | collective-permute-done | bytes 524320 | tf_op jit(solution)/shard_map/ppermute | solution.py:45
  34.3 2.8 %collective-permute-start.7 = (bf16[256,2048]{1,0:T(8,128)(2,1)S(1)}, bf16[256,2048]{1,0:T(8,128)(2,1)S(1)}, u32[]{:S(2)}, u32[]{:S(2)}) collective-permute-start(bf16[256,2048]{1,0:T(8,128)(2,1)S(1)} %shard_map.81.refs_0_.refs_2_.refs_6_), channel_id=1, source_target_pairs={{12,0},{13,1},{14,2},{15,3},{8,4},{9,5},{10,6},{11,7},{4,8},{5,9},... | collective-permute-start | bytes 3145736 | tf_op jit(solution)/shard_map/ppermute | solution.py:45
  38.4 2.7 %constant_dynamic-slice_fusion = (bf16[1024,1024]{1,0:T(8,128)(2,1)S(1)}, bf16[1024,1024]{1,0:T(8,128)(2,1)S(1)}) fusion(bf16[2048,1024]{1,0:T(8,128)(2,1)} %param.7, s32[]{:T(128)S(6)} %select_n.17, bf16[1024,2048]{1,0:T(8,128)(2,1)} %param.6), kind=kLoop, calls=%fused_computation.49 | loop fusion | bytes 8388612 | tf_op jit(solution)/shard_map/dynamic_slice | solution.py:372
  41.1 9.3 %collective-permute-done.7.refs_1_.refs_3_.refs_7_ = bf16[256,2048]{1,0:T(8,128)(2,1)S(1)} collective-permute-done((bf16[256,2048]{1,0:T(8,128)(2,1)S(1)}, bf16[256,2048]{1,0:T(8,128)(2,1)S(1)}, u32[]{:S(2)}, u32[]{:S(2)}) %collective-permute-start.7) | collective-permute-done | bytes 1048608 | tf_op jit(solution)/shard_map/ppermute | solution.py:45
  50.4 2.4 %collective-permute-done.5.refs_1_.refs_5_ = bf16[256,2048]{1,0:T(8,128)(2,1)} collective-permute-done((bf16[256,2048]{1,0:T(8,128)(2,1)S(1)}, bf16[256,2048]{1,0:T(8,128)(2,1)}, u32[]{:S(2)}, u32[]{:S(2)}) %collective-permute-start.5) | collective-permute-done | bytes 1048608 | tf_op jit(solution)/shard_map/ppermute | solution.py:45
  52.7 4.3 %shard_map.82 = bf16[512,2048]{1,0:T(8,128)(2,1)S(1)} custom-call(s32[2]{0:T(128)S(1)} %pad_add_fusion.place_ref, bf16[256,2048]{1,0:T(8,128)(2,1)S(1)} %shard_map.81.refs_0_.refs_2_.refs_6_, bf16[256,2048]{1,0:T(8,128)(2,1)S(1)} %collective-permute-done.7.refs_1_.refs_3_.refs_7_, bf16[1024,1024]{1,0:T(8,128)(2,1)S(1)} %get-tuple-element.123.refs_2_.refs_3_, ...), custom_call_target="tpu_custom_call" | custom-call | flops 2147483 | bytes 8388 | tf_op jit(solution)/shard_map/pallas_call | solution.py:291
  57.3 3.3 %collective-permute-start.12 = (bf16[128,2048]{1,0:T(8,128)(2,1)S(1)}, bf16[128,2048]{1,0:T(8,128)(2,1)S(1)}, u32[]{:S(2)}, u32[]{:S(2)}) collective-permute-start(bf16[128,2048]{1,0:T(8,128)(2,1)S(1)} %copy-done.3), channel_id=1, source_target_pairs={{1,0},{0,1},{3,2},{2,3},{5,4},{4,5},{7,6},{6,7},{9,8},{8,9},{11,10... | collective-permute-start | bytes 1572872 | tf_op jit(solution)/shard_map/ppermute | solution.py:45
  61.2 5.3 %shard_map.83 = (bf16[256,2048]{1,0:T(8,128)(2,1)S(1)}, bf16[256,2048]{1,0:T(8,128)(2,1)S(1)}) custom-call(s32[2]{0:T(128)S(1)} %pad_add_fusion.place_ref, bf16[256,2048]{1,0:T(8,128)(2,1)S(1)} %shard_map.80.refs_0_.refs_4_, bf16[256,2048]{1,0:T(8,128)(2,1)} %collective-permute-done.5.refs_1_.refs_5_, ...), custom_call_target="tpu_custom_call" | custom-call | flops 2147483 | bytes 8388 | tf_op jit(solution)/shard_map/pallas_call | solution.py:291
  67.2 2.4 %collective-permute-start.11 = (bf16[256,2048]{1,0:T(8,128)(2,1)S(1)}, bf16[256,2048]{1,0:T(8,128)(2,1)S(1)}, u32[]{:S(2)}, u32[]{:S(2)}) collective-permute-start(bf16[256,2048]{1,0:T(8,128)(2,1)S(1)} %shard_map.84.refs_0_.refs_2_.refs_6_), channel_id=1, source_target_pairs={{12,0},{13,1},{14,2},{15,3},{8,4},{9,5},{10,6},{11,7},{4,8},{5,9},... | collective-permute-start | bytes 3145736 | tf_op jit(solution)/shard_map/ppermute | solution.py:45
  70.3 2.0 collective-permute-start.9
  72.3 10.9 %collective-permute-done.11.refs_1_.refs_3_.refs_7_ = bf16[256,2048]{1,0:T(8,128)(2,1)S(1)} collective-permute-done((bf16[256,2048]{1,0:T(8,128)(2,1)S(1)}, bf16[256,2048]{1,0:T(8,128)(2,1)S(1)}, u32[]{:S(2)}, u32[]{:S(2)}) %collective-permute-start.11) | collective-permute-done | bytes 1048608 | tf_op jit(solution)/shard_map/ppermute | solution.py:45
  83.3 1.9 collective-permute-done.13.refs_1_.refs_5_
  85.1 4.3 %shard_map.86 = bf16[512,2048]{1,0:T(8,128)(2,1)S(1)} custom-call(s32[2]{0:T(128)S(1)} %pad_add_fusion.place_ref, bf16[256,2048]{1,0:T(8,128)(2,1)S(1)} %shard_map.84.refs_0_.refs_2_.refs_6_, bf16[256,2048]{1,0:T(8,128)(2,1)S(1)} %collective-permute-done.11.refs_1_.refs_3_.refs_7_, bf16[1024,1024]{1,0:T(8,128)(2,1)S(1)} %get-tuple-element.123.refs_2_.refs_3_, ...), custom_call_target="tpu_custom_call" | custom-call | flops 2147483 | bytes 8388 | tf_op jit(solution)/shard_map/pallas_call | solution.py:291
  89.9 4.3 %collective-permute-start.14 = (bf16[256,2048]{1,0:T(8,128)(2,1)S(1)}, bf16[256,2048]{1,0:T(8,128)(2,1)S(1)}, u32[]{:S(2)}, u32[]{:S(2)}) collective-permute-start(bf16[256,2048]{1,0:T(8,128)(2,1)S(1)} %add_convert_fusion.1), channel_id=1, source_target_pairs={{96,0},{97,1},{98,2},{99,3},{100,4},{101,5},{102,6},{103,7},{104,8... | collective-permute-start | bytes 3145736 | tf_op jit(solution)/shard_map/ppermute | solution.py:45
  94.2 4.4 %shard_map.87 = (bf16[256,2048]{1,0:T(8,128)(2,1)S(1)}, bf16[256,2048]{1,0:T(8,128)(2,1)S(1)}) custom-call(s32[2]{0:T(128)S(1)} %pad_add_fusion.place_ref, bf16[256,2048]{1,0:T(8,128)(2,1)S(1)} %shard_map.85.refs_0_.refs_4_, bf16[256,2048]{1,0:T(8,128)(2,1)S(1)} %collective-permute-done.13.refs_1_.refs_5_, ...), custom_call_target="tpu_custom_call" | custom-call | flops 2147483 | bytes 8388 | tf_op jit(solution)/shard_map/pallas_call | solution.py:291
  98.7 8.3 %collective-permute-done.14 = bf16[256,2048]{1,0:T(8,128)(2,1)S(1)} collective-permute-done((bf16[256,2048]{1,0:T(8,128)(2,1)S(1)}, bf16[256,2048]{1,0:T(8,128)(2,1)S(1)}, u32[]{:S(2)}, u32[]{:S(2)}) %collective-permute-start.14) | collective-permute-done | bytes 1048608 | tf_op jit(solution)/shard_map/ppermute | solution.py:45
  110.1 12.8 %collective-permute-done.16.refs_1_.refs_5_ = bf16[256,2048]{1,0:T(8,128)(2,1)S(1)} collective-permute-done((bf16[256,2048]{1,0:T(8,128)(2,1)S(1)}, bf16[256,2048]{1,0:T(8,128)(2,1)S(1)}, u32[]{:S(2)}, u32[]{:S(2)}) %collective-permute-start.16) | collective-permute-done | bytes 1048608 | tf_op jit(solution)/shard_map/ppermute | solution.py:45
  122.9 4.3 %shard_map.88 = (bf16[256,2048]{1,0:T(8,128)(2,1)S(1)}, bf16[256,2048]{1,0:T(8,128)(2,1)S(1)}) custom-call(s32[2]{0:T(128)S(1)} %pad_add_fusion.place_ref, bf16[256,2048]{1,0:T(8,128)(2,1)S(1)} %pad_maximum_fusion.refs_0_.refs_4_, bf16[256,2048]{1,0:T(8,128)(2,1)S(1)} %collective-permute-done.16.refs_1_.refs_5_, ...), custom_call_target="tpu_custom_call" | custom-call | flops 2147483 | bytes 8388 | tf_op jit(solution)/shard_map/pallas_call | solution.py:291
  127.2 6.9 %collective-permute-done.20 = bf16[256,2048]{1,0:T(8,128)(2,1)S(1)} collective-permute-done((bf16[256,2048]{1,0:T(8,128)(2,1)S(1)}, bf16[256,2048]{1,0:T(8,128)(2,1)S(1)}, u32[]{:S(2)}, u32[]{:S(2)}) %collective-permute-start.20) | collective-permute-done | bytes 1048608 | tf_op jit(solution)/shard_map/ppermute | solution.py:45
  134.5 3.3 %collective-permute-start.22 = (bf16[256,2048]{1,0:T(8,128)(2,1)S(1)}, bf16[256,2048]{1,0:T(8,128)(2,1)S(1)}, u32[]{:S(2)}, u32[]{:S(2)}) collective-permute-start(bf16[256,2048]{1,0:T(8,128)(2,1)S(1)} %add_convert_fusion), channel_id=1, source_target_pairs={{96,0},{97,1},{98,2},{99,3},{100,4},{101,5},{102,6},{103,7},{104,8... | collective-permute-start | bytes 3145736 | tf_op jit(solution)/shard_map/ppermute | solution.py:45
  139.3 4.3 %shard_map.89 = (bf16[256,2048]{1,0:T(8,128)(2,1)S(1)}, bf16[256,2048]{1,0:T(8,128)(2,1)S(1)}) custom-call(s32[2]{0:T(128)S(1)} %pad_add_fusion.place_ref, bf16[256,2048]{1,0:T(8,128)(2,1)S(1)} %collective-permute-done.18.refs_0_.refs_6_.refs_2_, bf16[256,2048]{1,0:T(8,128)(2,1)S(1)} %collective-permute-done.19.refs_1_.refs_7_.refs_3_, ...), custom_call_target="tpu_custom_call" | custom-call | flops 2147483 | bytes 8388 | tf_op jit(solution)/shard_map/pallas_call | solution.py:291
  143.7 5.1 %shard_map.90.refs_8_ = f32[1024,1024]{1,0:T(8,128)} custom-call(bf16[256,2048]{1,0:T(8,128)(2,1)S(1)} %shard_map.80.refs_0_.refs_4_, bf16[256,2048]{1,0:T(8,128)(2,1)} %collective-permute-done.5.refs_1_.refs_5_, bf16[256,2048]{1,0:T(8,128)(2,1)S(1)} %shard_map.81.refs_0_.refs_2_.refs_6_, ...), custom_call_target="tpu_custom_call" | custom-call | flops 2147483 | bytes 5242 | tf_op jit(solution)/shard_map/pallas_call | solution.py:340
  148.8 1.8 collective-permute-done.22
  151.8 2.1 collective-permute-done.17
  153.9 4.6 %collective-permute-done.21 = bf16[256,2048]{1,0:T(8,128)(2,1)S(1)} collective-permute-done((bf16[256,2048]{1,0:T(8,128)(2,1)S(1)}, bf16[256,2048]{1,0:T(8,128)(2,1)S(1)}, u32[]{:S(2)}, u32[]{:S(2)}) %collective-permute-start.21) | collective-permute-done | bytes 1048608 | tf_op jit(solution)/shard_map/ppermute | solution.py:45
  158.9 6.8 %collective-permute-start.25 = (bf16[128,2048]{1,0:T(8,128)(2,1)S(1)}, bf16[128,2048]{1,0:T(8,128)(2,1)S(1)}, u32[]{:S(2)}, u32[]{:S(2)}) collective-permute-start(bf16[128,2048]{1,0:T(8,128)(2,1)S(1)} %slice.230), channel_id=1, source_target_pairs={{1,0},{0,1},{3,2},{2,3},{5,4},{4,5},{7,6},{6,7},{9,8},{8,9},{11,10... | collective-permute-start | bytes 1572872 | tf_op jit(solution)/shard_map/ppermute | solution.py:45
  166.6 4.9 %shard_map.91.refs_8_ = f32[1024,1024]{1,0:T(8,128)} custom-call(bf16[256,2048]{1,0:T(8,128)(2,1)S(1)} %pad_maximum_fusion.refs_0_.refs_4_, bf16[256,2048]{1,0:T(8,128)(2,1)S(1)} %collective-permute-done.16.refs_1_.refs_5_, bf16[256,2048]{1,0:T(8,128)(2,1)S(1)} %collective-permute-done.18.refs_0_.refs_6_.refs_2_, ...), custom_call_target="tpu_custom_call" | custom-call | flops 2147483 | bytes 5242 | tf_op jit(solution)/shard_map/pallas_call | solution.py:340
  172.9 2.5 %collective-permute-done.23 = bf16[128,2048]{1,0:T(8,128)(2,1)S(1)} collective-permute-done((bf16[128,2048]{1,0:T(8,128)(2,1)S(1)}, bf16[128,2048]{1,0:T(8,128)(2,1)S(1)}, u32[]{:S(2)}, u32[]{:S(2)}) %collective-permute-start.23) | collective-permute-done | bytes 524320 | tf_op jit(solution)/shard_map/ppermute | solution.py:45
  175.8 3.1 %shard_map.92 = bf16[256,2048]{1,0:T(8,128)(2,1)S(1)} custom-call(s32[2]{0:T(128)S(1)} %pad_add_fusion.place_ref, bf16[256,2048]{1,0:T(8,128)(2,1)S(1)} %pad_maximum_fusion.1.refs_0_.refs_4_, bf16[256,2048]{1,0:T(8,128)(2,1)S(1)} %collective-permute-done.24.refs_1_.refs_5_, bf16[1024,1024]{1,0:T(8,128)(2,1)S(1)} %get-tuple-element.122.refs_3_.refs_2_, ...), custom_call_target="tpu_custom_call" | custom-call | flops 2147483 | bytes 8388 | tf_op jit(solution)/shard_map/pallas_call | solution.py:291
  180.2 3.1 %shard_map.93 = bf16[256,2048]{1,0:T(8,128)(2,1)S(1)} custom-call(s32[2]{0:T(128)S(1)} %pad_add_fusion.place_ref, bf16[256,2048]{1,0:T(8,128)(2,1)S(1)} %collective-permute-done.26.refs_0_.refs_6_.refs_2_, bf16[256,2048]{1,0:T(8,128)(2,1)S(1)} %collective-permute-done.27.refs_1_.refs_7_.refs_3_, bf16[1024,1024]{1,0:T(8,128)(2,1)S(1)} %get-tuple-element.122.refs_3_.refs_2_, ...), custom_call_target="tpu_custom_call" | custom-call | flops 2147483 | bytes 8388 | tf_op jit(solution)/shard_map/pallas_call | solution.py:291
  183.5 3.1 %shard_map.94 = bf16[256,2048]{1,0:T(8,128)(2,1)S(1)} custom-call(s32[2]{0:T(128)S(1)} %pad_add_fusion.place_ref, bf16[256,2048]{1,0:T(8,128)(2,1)S(1)} %pad_maximum_fusion.1.refs_0_.refs_4_, bf16[256,2048]{1,0:T(8,128)(2,1)S(1)} %collective-permute-done.24.refs_1_.refs_5_, bf16[1024,1024]{1,0:T(8,128)(2,1)S(1)} %get-tuple-element.122.refs_3_.refs_2_, ...), custom_call_target="tpu_custom_call" | custom-call | flops 2147483 | bytes 8388 | tf_op jit(solution)/shard_map/pallas_call | solution.py:291
  186.7 3.1 %shard_map.95 = bf16[256,2048]{1,0:T(8,128)(2,1)S(1)} custom-call(s32[2]{0:T(128)S(1)} %pad_add_fusion.place_ref, bf16[256,2048]{1,0:T(8,128)(2,1)S(1)} %collective-permute-done.26.refs_0_.refs_6_.refs_2_, bf16[256,2048]{1,0:T(8,128)(2,1)S(1)} %collective-permute-done.27.refs_1_.refs_7_.refs_3_, bf16[1024,1024]{1,0:T(8,128)(2,1)S(1)} %get-tuple-element.122.refs_3_.refs_2_, ...), custom_call_target="tpu_custom_call" | custom-call | flops 2147483 | bytes 8388 | tf_op jit(solution)/shard_map/pallas_call | solution.py:291
  189.8 5.6 %shard_map.96 = f32[1024,1024]{1,0:T(8,128)} custom-call(bf16[256,2048]{1,0:T(8,128)(2,1)S(1)} %shard_map.85.refs_0_.refs_4_, bf16[256,2048]{1,0:T(8,128)(2,1)S(1)} %collective-permute-done.13.refs_1_.refs_5_, bf16[256,2048]{1,0:T(8,128)(2,1)S(1)} %shard_map.84.refs_0_.refs_2_.refs_6_, ...), custom_call_target="tpu_custom_call", output_to_operand_aliasing={{}: (8, {})} | custom-call | flops 2147483 | bytes 5242 | tf_op jit(solution)/shard_map/pallas_call | solution.py:340
  195.5 2.7 %collective-permute-done.29 = bf16[256,2048]{1,0:T(8,128)(2,1)S(1)} collective-permute-done((bf16[256,2048]{1,0:T(8,128)(2,1)S(1)}, bf16[256,2048]{1,0:T(8,128)(2,1)S(1)}, u32[]{:S(2)}, u32[]{:S(2)}) %collective-permute-start.29) | collective-permute-done | bytes 1048608 | tf_op jit(solution)/shard_map/ppermute | solution.py:45
  200.8 5.6 %shard_map.97 = f32[1024,1024]{1,0:T(8,128)} custom-call(bf16[256,2048]{1,0:T(8,128)(2,1)S(1)} %pad_maximum_fusion.1.refs_0_.refs_4_, bf16[256,2048]{1,0:T(8,128)(2,1)S(1)} %collective-permute-done.24.refs_1_.refs_5_, bf16[256,2048]{1,0:T(8,128)(2,1)S(1)} %collective-permute-done.26.refs_0_.refs_6_.refs_2_, ...), custom_call_target="tpu_custom_call", output_to_operand_aliasing={{}: (8, {})} | custom-call | flops 2147483 | bytes 5242 | tf_op jit(solution)/shard_map/pallas_call | solution.py:340
  206.5 1.4 collective-permute-done.33
  208.1 2.2 collective-permute-start.34
  210.9 7.7 %collective-permute-done.34 = bf16[128,2048]{1,0:T(8,128)(2,1)S(1)} collective-permute-done((bf16[128,2048]{1,0:T(8,128)(2,1)S(1)}, bf16[128,2048]{1,0:T(8,128)(2,1)S(1)}, u32[]{:S(2)}, u32[]{:S(2)}) %collective-permute-start.34) | collective-permute-done | bytes 524320 | tf_op jit(solution)/shard_map/ppermute | solution.py:45
  218.9 2.9 %collective-permute-done.31 = bf16[128,2048]{1,0:T(8,128)(2,1)S(1)} collective-permute-done((bf16[128,2048]{1,0:T(8,128)(2,1)S(1)}, bf16[128,2048]{1,0:T(8,128)(2,1)S(1)}, u32[]{:S(2)}, u32[]{:S(2)}) %collective-permute-start.31) | collective-permute-done | bytes 524320 | tf_op jit(solution)/shard_map/ppermute | solution.py:45
  222.0 2.0 collective-permute-start.32
  225.3 3.1 %collective-permute-done.32 = bf16[64,2048]{1,0:T(8,128)(2,1)S(1)} collective-permute-done((bf16[64,2048]{1,0:T(8,128)(2,1)S(1)}, bf16[64,2048]{1,0:T(8,128)(2,1)S(1)}, u32[]{:S(2)}, u32[]{:S(2)}) %collective-permute-start.32) | collective-permute-done | bytes 262176 | tf_op jit(solution)/shard_map/ppermute | solution.py:45
  (100 shorter events, 29.2 us)
Async XLA Ops:
  0.7 1.0 copy-start.4
  1.7 0.9 copy-start.5
  3.3 6.5 %collective-permute-start.2 = (bf16[64,2048]{1,0:T(8,128)(2,1)S(1)}, bf16[64,2048]{1,0:T(8,128)(2,1)S(1)}, u32[]{:S(2)}, u32[]{:S(2)}) collective-permute-start(bf16[64,2048]{1,0:T(8,128)(2,1)S(1)} %get-tuple-element.49.a_ref), channel_id=1, source_target_pairs={{1,0},{0,1},{3,2},{2,3},{5,4},{4,5},{7,6},{6,7},{9,8},{8,9},{11,10... | collective-permute-start | bytes 786440 | tf_op jit(solution)/shard_map/ppermute | solution.py:45
  3.8 8.2 %collective-permute-start = (bf16[64,2048]{1,0:T(8,128)(2,1)S(1)}, bf16[64,2048]{1,0:T(8,128)(2,1)S(1)}, u32[]{:S(2)}, u32[]{:S(2)}) collective-permute-start(bf16[64,2048]{1,0:T(8,128)(2,1)S(1)} %get-tuple-element.47.a_ref), channel_id=1, source_target_pairs={{4,0},{5,1},{6,2},{7,3},{0,4},{1,5},{2,6},{3,7},{12,8},{13,9},{14,... | collective-permute-start | bytes 786440 | tf_op jit(solution)/shard_map/ppermute | solution.py:45
  10.3 9.3 %collective-permute-start.3 = (bf16[128,2048]{1,0:T(8,128)(2,1)S(1)}, bf16[128,2048]{1,0:T(8,128)(2,1)S(1)}, u32[]{:S(2)}, u32[]{:S(2)}) collective-permute-start(bf16[128,2048]{1,0:T(8,128)(2,1)S(1)} %shard_map.78), channel_id=1, source_target_pairs={{3,0},{2,1},{1,2},{0,3},{7,4},{6,5},{5,6},{4,7},{11,8},{10,9},{9,1... | collective-permute-start | bytes 1572872 | tf_op jit(solution)/shard_map/ppermute | solution.py:45
  12.6 10.5 %collective-permute-start.1 = (bf16[128,2048]{1,0:T(8,128)(2,1)S(1)}, bf16[128,2048]{1,0:T(8,128)(2,1)S(1)}, u32[]{:S(2)}, u32[]{:S(2)}) collective-permute-start(bf16[128,2048]{1,0:T(8,128)(2,1)S(1)} %shard_map.76), channel_id=1, source_target_pairs={{12,0},{13,1},{14,2},{15,3},{8,4},{9,5},{10,6},{11,7},{4,8},{5,9},... | collective-permute-start | bytes 1572872 | tf_op jit(solution)/shard_map/ppermute | solution.py:45
  20.2 0.8 copy-start
  23.7 0.8 copy-start.2
  24.5 9.2 %collective-permute-start.6 = (bf16[128,2048]{1,0:T(8,128)(2,1)S(1)}, bf16[128,2048]{1,0:T(8,128)(2,1)S(1)}, u32[]{:S(2)}, u32[]{:S(2)}) collective-permute-start(bf16[128,2048]{1,0:T(8,128)(2,1)S(1)} %get-tuple-element.52.a_ref), channel_id=1, source_target_pairs={{4,0},{5,1},{6,2},{7,3},{0,4},{1,5},{2,6},{3,7},{12,8},{13,9},{14,... | collective-permute-start | bytes 1572872 | tf_op jit(solution)/shard_map/ppermute | solution.py:45
  24.8 12.4 %collective-permute-start.4 = (bf16[128,2048]{1,0:T(8,128)(2,1)S(1)}, bf16[128,2048]{1,0:T(8,128)(2,1)S(1)}, u32[]{:S(2)}, u32[]{:S(2)}) collective-permute-start(bf16[128,2048]{1,0:T(8,128)(2,1)S(1)} %get-tuple-element.51.a_ref), channel_id=1, source_target_pairs={{1,0},{0,1},{3,2},{2,3},{5,4},{4,5},{7,6},{6,7},{9,8},{8,9},{11,10... | collective-permute-start | bytes 1572872 | tf_op jit(solution)/shard_map/ppermute | solution.py:45
  34.3 16.1 %collective-permute-start.7 = (bf16[256,2048]{1,0:T(8,128)(2,1)S(1)}, bf16[256,2048]{1,0:T(8,128)(2,1)S(1)}, u32[]{:S(2)}, u32[]{:S(2)}) collective-permute-start(bf16[256,2048]{1,0:T(8,128)(2,1)S(1)} %shard_map.81.refs_0_.refs_2_.refs_6_), channel_id=1, source_target_pairs={{12,0},{13,1},{14,2},{15,3},{8,4},{9,5},{10,6},{11,7},{4,8},{5,9},... | collective-permute-start | bytes 3145736 | tf_op jit(solution)/shard_map/ppermute | solution.py:45
  37.7 15.0 %collective-permute-start.5 = (bf16[256,2048]{1,0:T(8,128)(2,1)S(1)}, bf16[256,2048]{1,0:T(8,128)(2,1)}, u32[]{:S(2)}, u32[]{:S(2)}) collective-permute-start(bf16[256,2048]{1,0:T(8,128)(2,1)S(1)} %shard_map.80.refs_0_.refs_4_), channel_id=1, source_target_pairs={{3,0},{2,1},{1,2},{0,3},{7,4},{6,5},{5,6},{4,7},{11,8},{10,9},{9,1... | collective-permute-start | bytes 3145736 | tf_op jit(solution)/shard_map/ppermute | solution.py:45
  52.7 4.4 %copy-start.1 = (bf16[128,2048]{1,0:T(8,128)(2,1)S(1)}, bf16[128,2048]{1,0:T(8,128)(2,1)}, u32[]{:S(2)}) copy-start(bf16[128,2048]{1,0:T(8,128)(2,1)} %copy-done) | copy-start | bytes 1572868
  52.7 4.6 %copy-start.3 = (bf16[128,2048]{1,0:T(8,128)(2,1)S(1)}, bf16[128,2048]{1,0:T(8,128)(2,1)}, u32[]{:S(2)}) copy-start(bf16[128,2048]{1,0:T(8,128)(2,1)} %copy-done.2) | copy-start | bytes 1572868
  57.0 4.2 %collective-permute-start.8 = (bf16[512,2048]{1,0:T(8,128)(2,1)S(1)}, bf16[512,2048]{1,0:T(8,128)(2,1)S(1)}, u32[]{:S(2)}, u32[]{:S(2)}) collective-permute-start(bf16[512,2048]{1,0:T(8,128)(2,1)S(1)} %shard_map.82), channel_id=1, source_target_pairs={{16,0},{17,1},{18,2},{19,3},{20,4},{21,5},{22,6},{23,7},{24,8},{25... | collective-permute-start | bytes 6291464 | tf_op jit(solution)/shard_map/ppermute | solution.py:45
  57.1 9.4 %collective-permute-start.10 = (bf16[128,2048]{1,0:T(8,128)(2,1)S(1)}, bf16[128,2048]{1,0:T(8,128)(2,1)S(1)}, u32[]{:S(2)}, u32[]{:S(2)}) collective-permute-start(bf16[128,2048]{1,0:T(8,128)(2,1)S(1)} %copy-done.1), channel_id=1, source_target_pairs={{4,0},{5,1},{6,2},{7,3},{0,4},{1,5},{2,6},{3,7},{12,8},{13,9},{14,... | collective-permute-start | bytes 1572872 | tf_op jit(solution)/shard_map/ppermute | solution.py:45
  57.3 12.3 %collective-permute-start.12 = (bf16[128,2048]{1,0:T(8,128)(2,1)S(1)}, bf16[128,2048]{1,0:T(8,128)(2,1)S(1)}, u32[]{:S(2)}, u32[]{:S(2)}) collective-permute-start(bf16[128,2048]{1,0:T(8,128)(2,1)S(1)} %copy-done.3), channel_id=1, source_target_pairs={{1,0},{0,1},{3,2},{2,3},{5,4},{4,5},{7,6},{6,7},{9,8},{8,9},{11,10... | collective-permute-start | bytes 1572872 | tf_op jit(solution)/shard_map/ppermute | solution.py:45
  67.2 16.1 %collective-permute-start.11 = (bf16[256,2048]{1,0:T(8,128)(2,1)S(1)}, bf16[256,2048]{1,0:T(8,128)(2,1)S(1)}, u32[]{:S(2)}, u32[]{:S(2)}) collective-permute-start(bf16[256,2048]{1,0:T(8,128)(2,1)S(1)} %shard_map.84.refs_0_.refs_2_.refs_6_), channel_id=1, source_target_pairs={{12,0},{13,1},{14,2},{15,3},{8,4},{9,5},{10,6},{11,7},{4,8},{5,9},... | collective-permute-start | bytes 3145736 | tf_op jit(solution)/shard_map/ppermute | solution.py:45
  70.2 14.9 %collective-permute-start.13 = (bf16[256,2048]{1,0:T(8,128)(2,1)S(1)}, bf16[256,2048]{1,0:T(8,128)(2,1)S(1)}, u32[]{:S(2)}, u32[]{:S(2)}) collective-permute-start(bf16[256,2048]{1,0:T(8,128)(2,1)S(1)} %shard_map.85.refs_0_.refs_4_), channel_id=1, source_target_pairs={{3,0},{2,1},{1,2},{0,3},{7,4},{6,5},{5,6},{4,7},{11,8},{10,9},{9,1... | collective-permute-start | bytes 3145736 | tf_op jit(solution)/shard_map/ppermute | solution.py:45
  70.3 19.2 %collective-permute-start.9 = (bf16[256,2048]{1,0:T(8,128)(2,1)S(1)}, bf16[256,2048]{1,0:T(8,128)(2,1)S(1)}, u32[]{:S(2)}, u32[]{:S(2)}) collective-permute-start(bf16[256,2048]{1,0:T(8,128)(2,1)S(1)} %get-tuple-element.55), channel_id=1, source_target_pairs={{32,0},{33,1},{34,2},{35,3},{36,4},{37,5},{38,6},{39,7},{40,8},{41... | collective-permute-start | bytes 3145736 | tf_op jit(solution)/shard_map/ppermute | solution.py:45
  89.4 4.8 %collective-permute-start.15 = (bf16[512,2048]{1,0:T(8,128)(2,1)S(1)}, bf16[512,2048]{1,0:T(8,128)(2,1)S(1)}, u32[]{:S(2)}, u32[]{:S(2)}) collective-permute-start(bf16[512,2048]{1,0:T(8,128)(2,1)S(1)} %shard_map.86), channel_id=1, source_target_pairs={{16,0},{17,1},{18,2},{19,3},{20,4},{21,5},{22,6},{23,7},{24,8},{25... | collective-permute-start | bytes 6291464 | tf_op jit(solution)/shard_map/ppermute | solution.py:45
  89.9 17.1 %collective-permute-start.14 = (bf16[256,2048]{1,0:T(8,128)(2,1)S(1)}, bf16[256,2048]{1,0:T(8,128)(2,1)S(1)}, u32[]{:S(2)}, u32[]{:S(2)}) collective-permute-start(bf16[256,2048]{1,0:T(8,128)(2,1)S(1)} %add_convert_fusion.1), channel_id=1, source_target_pairs={{96,0},{97,1},{98,2},{99,3},{100,4},{101,5},{102,6},{103,7},{104,8... | collective-permute-start | bytes 3145736 | tf_op jit(solution)/shard_map/ppermute | solution.py:45
  108.0 14.9 %collective-permute-start.16 = (bf16[256,2048]{1,0:T(8,128)(2,1)S(1)}, bf16[256,2048]{1,0:T(8,128)(2,1)S(1)}, u32[]{:S(2)}, u32[]{:S(2)}) collective-permute-start(bf16[256,2048]{1,0:T(8,128)(2,1)S(1)} %pad_maximum_fusion.refs_0_.refs_4_), channel_id=1, source_target_pairs={{32,0},{33,1},{34,2},{35,3},{36,4},{37,5},{38,6},{39,7},{40,8},{41... | collective-permute-start | bytes 3145736 | tf_op jit(solution)/shard_map/ppermute | solution.py:45
  108.1 26.0 %collective-permute-start.18 = (bf16[256,2048]{1,0:T(8,128)(2,1)S(1)}, bf16[256,2048]{1,0:T(8,128)(2,1)S(1)}, u32[]{:S(2)}, u32[]{:S(2)}) collective-permute-start(bf16[256,2048]{1,0:T(8,128)(2,1)S(1)} %pad_maximum_fusion.refs_0_.refs_4_), channel_id=1, source_target_pairs={{16,0},{17,1},{18,2},{19,3},{20,4},{21,5},{22,6},{23,7},{24,8},{25... | collective-permute-start | bytes 3145736 | tf_op jit(solution)/shard_map/ppermute | solution.py:45
  109.5 24.7 %collective-permute-start.20 = (bf16[256,2048]{1,0:T(8,128)(2,1)S(1)}, bf16[256,2048]{1,0:T(8,128)(2,1)S(1)}, u32[]{:S(2)}, u32[]{:S(2)}) collective-permute-start(bf16[256,2048]{1,0:T(8,128)(2,1)S(1)} %get-tuple-element.66), channel_id=1, source_target_pairs={{32,0},{33,1},{34,2},{35,3},{36,4},{37,5},{38,6},{39,7},{40,8},{41... | collective-permute-start | bytes 3145736 | tf_op jit(solution)/shard_map/ppermute | solution.py:45
  122.9 11.2 %collective-permute-start.19 = (bf16[256,2048]{1,0:T(8,128)(2,1)S(1)}, bf16[256,2048]{1,0:T(8,128)(2,1)S(1)}, u32[]{:S(2)}, u32[]{:S(2)}) collective-permute-start(bf16[256,2048]{1,0:T(8,128)(2,1)S(1)} %collective-permute-done.16.refs_1_.refs_5_), channel_id=1, source_target_pairs={{16,0},{17,1},{18,2},{19,3},{20,4},{21,5},{22,6},{23,7},{24,8},{25... | collective-permute-start | bytes 3145736 | tf_op jit(solution)/shard_map/ppermute | solution.py:45
  134.5 16.1 %collective-permute-start.22 = (bf16[256,2048]{1,0:T(8,128)(2,1)S(1)}, bf16[256,2048]{1,0:T(8,128)(2,1)S(1)}, u32[]{:S(2)}, u32[]{:S(2)}) collective-permute-start(bf16[256,2048]{1,0:T(8,128)(2,1)S(1)} %add_convert_fusion), channel_id=1, source_target_pairs={{96,0},{97,1},{98,2},{99,3},{100,4},{101,5},{102,6},{103,7},{104,8... | collective-permute-start | bytes 3145736 | tf_op jit(solution)/shard_map/ppermute | solution.py:45
  137.9 16.0 %collective-permute-start.17 = (bf16[256,2048]{1,0:T(8,128)(2,1)S(1)}, bf16[256,2048]{1,0:T(8,128)(2,1)S(1)}, u32[]{:S(2)}, u32[]{:S(2)}) collective-permute-start(bf16[256,2048]{1,0:T(8,128)(2,1)S(1)} %get-tuple-element.65), channel_id=1, source_target_pairs={{12,0},{13,1},{14,2},{15,3},{8,4},{9,5},{10,6},{11,7},{4,8},{5,9},... | collective-permute-start | bytes 3145736 | tf_op jit(solution)/shard_map/ppermute | solution.py:45
  143.6 14.9 %collective-permute-start.21 = (bf16[256,2048]{1,0:T(8,128)(2,1)S(1)}, bf16[256,2048]{1,0:T(8,128)(2,1)S(1)}, u32[]{:S(2)}, u32[]{:S(2)}) collective-permute-start(bf16[256,2048]{1,0:T(8,128)(2,1)S(1)} %get-tuple-element.70), channel_id=1, source_target_pairs={{3,0},{2,1},{1,2},{0,3},{7,4},{6,5},{5,6},{4,7},{11,8},{10,9},{9,1... | collective-permute-start | bytes 3145736 | tf_op jit(solution)/shard_map/ppermute | solution.py:45
  151.7 23.7 %collective-permute-start.24 = (bf16[256,2048]{1,0:T(8,128)(2,1)S(1)}, bf16[256,2048]{1,0:T(8,128)(2,1)S(1)}, u32[]{:S(2)}, u32[]{:S(2)}) collective-permute-start(bf16[256,2048]{1,0:T(8,128)(2,1)S(1)} %pad_maximum_fusion.1.refs_0_.refs_4_), channel_id=1, source_target_pairs={{32,0},{33,1},{34,2},{35,3},{36,4},{37,5},{38,6},{39,7},{40,8},{41... | collective-permute-start | bytes 3145736 | tf_op jit(solution)/shard_map/ppermute | solution.py:45
  158.9 14.0 %collective-permute-start.25 = (bf16[128,2048]{1,0:T(8,128)(2,1)S(1)}, bf16[128,2048]{1,0:T(8,128)(2,1)S(1)}, u32[]{:S(2)}, u32[]{:S(2)}) collective-permute-start(bf16[128,2048]{1,0:T(8,128)(2,1)S(1)} %slice.230), channel_id=1, source_target_pairs={{1,0},{0,1},{3,2},{2,3},{5,4},{4,5},{7,6},{6,7},{9,8},{8,9},{11,10... | collective-permute-start | bytes 1572872 | tf_op jit(solution)/shard_map/ppermute | solution.py:45
  166.2 9.3 %collective-permute-start.23 = (bf16[128,2048]{1,0:T(8,128)(2,1)S(1)}, bf16[128,2048]{1,0:T(8,128)(2,1)S(1)}, u32[]{:S(2)}, u32[]{:S(2)}) collective-permute-start(bf16[128,2048]{1,0:T(8,128)(2,1)S(1)} %slice.231), channel_id=1, source_target_pairs={{4,0},{5,1},{6,2},{7,3},{0,4},{1,5},{2,6},{3,7},{12,8},{13,9},{14,... | collective-permute-start | bytes 1572872 | tf_op jit(solution)/shard_map/ppermute | solution.py:45
  166.3 9.6 %collective-permute-start.26 = (bf16[256,2048]{1,0:T(8,128)(2,1)S(1)}, bf16[256,2048]{1,0:T(8,128)(2,1)S(1)}, u32[]{:S(2)}, u32[]{:S(2)}) collective-permute-start(bf16[256,2048]{1,0:T(8,128)(2,1)S(1)} %pad_maximum_fusion.1.refs_0_.refs_4_), channel_id=1, source_target_pairs={{16,0},{17,1},{18,2},{19,3},{20,4},{21,5},{22,6},{23,7},{24,8},{25... | collective-permute-start | bytes 3145736 | tf_op jit(solution)/shard_map/ppermute | solution.py:45
  175.4 4.7 %collective-permute-start.27 = (bf16[256,2048]{1,0:T(8,128)(2,1)S(1)}, bf16[256,2048]{1,0:T(8,128)(2,1)S(1)}, u32[]{:S(2)}, u32[]{:S(2)}) collective-permute-start(bf16[256,2048]{1,0:T(8,128)(2,1)S(1)} %collective-permute-done.24.refs_1_.refs_5_), channel_id=1, source_target_pairs={{16,0},{17,1},{18,2},{19,3},{20,4},{21,5},{22,6},{23,7},{24,8},{25... | collective-permute-start | bytes 3145736 | tf_op jit(solution)/shard_map/ppermute | solution.py:45
  179.0 16.5 %collective-permute-start.28 = (bf16[256,2048]{1,0:T(8,128)(2,1)S(1)}, bf16[256,2048]{1,0:T(8,128)(2,1)S(1)}, u32[]{:S(2)}, u32[]{:S(2)}) collective-permute-start(bf16[256,2048]{1,0:T(8,128)(2,1)S(1)} %shard_map.92), channel_id=1, source_target_pairs={{12,0},{13,1},{14,2},{15,3},{8,4},{9,5},{10,6},{11,7},{4,8},{5,9},... | collective-permute-start | bytes 3145736 | tf_op jit(solution)/shard_map/ppermute | solution.py:45
  183.3 14.9 %collective-permute-start.29 = (bf16[256,2048]{1,0:T(8,128)(2,1)S(1)}, bf16[256,2048]{1,0:T(8,128)(2,1)S(1)}, u32[]{:S(2)}, u32[]{:S(2)}) collective-permute-start(bf16[256,2048]{1,0:T(8,128)(2,1)S(1)} %shard_map.93), channel_id=1, source_target_pairs={{3,0},{2,1},{1,2},{0,3},{7,4},{6,5},{5,6},{4,7},{11,8},{10,9},{9,1... | collective-permute-start | bytes 3145736 | tf_op jit(solution)/shard_map/ppermute | solution.py:45
  198.6 9.3 %collective-permute-start.33 = (bf16[128,2048]{1,0:T(8,128)(2,1)S(1)}, bf16[128,2048]{1,0:T(8,128)(2,1)S(1)}, u32[]{:S(2)}, u32[]{:S(2)}) collective-permute-start(bf16[128,2048]{1,0:T(8,128)(2,1)S(1)} %slice.228), channel_id=1, source_target_pairs={{1,0},{0,1},{3,2},{2,3},{5,4},{4,5},{7,6},{6,7},{9,8},{8,9},{11,10... | collective-permute-start | bytes 1572872 | tf_op jit(solution)/shard_map/ppermute | solution.py:45
  200.4 10.0 %collective-permute-start.30 = (bf16[128,2048]{1,0:T(8,128)(2,1)S(1)}, bf16[128,2048]{1,0:T(8,128)(2,1)S(1)}, u32[]{:S(2)}, u32[]{:S(2)}) collective-permute-start(bf16[128,2048]{1,0:T(8,128)(2,1)S(1)} %slice.229), channel_id=1, source_target_pairs={{4,0},{5,1},{6,2},{7,3},{0,4},{1,5},{2,6},{3,7},{12,8},{13,9},{14,... | collective-permute-start | bytes 1572872 | tf_op jit(solution)/shard_map/ppermute | solution.py:45
  208.1 10.5 %collective-permute-start.34 = (bf16[128,2048]{1,0:T(8,128)(2,1)S(1)}, bf16[128,2048]{1,0:T(8,128)(2,1)S(1)}, u32[]{:S(2)}, u32[]{:S(2)}) collective-permute-start(bf16[128,2048]{1,0:T(8,128)(2,1)S(1)} %pad_maximum_fusion.3), channel_id=1, source_target_pairs={{12,0},{13,1},{14,2},{15,3},{8,4},{9,5},{10,6},{11,7},{4,8},{5,9},... | collective-permute-start | bytes 1572872 | tf_op jit(solution)/shard_map/ppermute | solution.py:45
  210.7 11.1 %collective-permute-start.31 = (bf16[128,2048]{1,0:T(8,128)(2,1)S(1)}, bf16[128,2048]{1,0:T(8,128)(2,1)S(1)}, u32[]{:S(2)}, u32[]{:S(2)}) collective-permute-start(bf16[128,2048]{1,0:T(8,128)(2,1)S(1)} %pad_maximum_fusion.2), channel_id=1, source_target_pairs={{3,0},{2,1},{1,2},{0,3},{7,4},{6,5},{5,6},{4,7},{11,8},{10,9},{9,1... | collective-permute-start | bytes 1572872 | tf_op jit(solution)/shard_map/ppermute | solution.py:45
  218.8 6.5 %collective-permute-start.35 = (bf16[64,2048]{1,0:T(8,128)(2,1)S(1)}, bf16[64,2048]{1,0:T(8,128)(2,1)S(1)}, u32[]{:S(2)}, u32[]{:S(2)}) collective-permute-start(bf16[64,2048]{1,0:T(8,128)(2,1)S(1)} %fusion.12), channel_id=1, source_target_pairs={{4,0},{5,1},{6,2},{7,3},{0,4},{1,5},{2,6},{3,7},{12,8},{13,9},{14,... | collective-permute-start | bytes 786440 | tf_op jit(solution)/shard_map/ppermute | solution.py:45
  222.0 6.5 %collective-permute-start.32 = (bf16[64,2048]{1,0:T(8,128)(2,1)S(1)}, bf16[64,2048]{1,0:T(8,128)(2,1)S(1)}, u32[]{:S(2)}, u32[]{:S(2)}) collective-permute-start(bf16[64,2048]{1,0:T(8,128)(2,1)S(1)} %fusion.15), channel_id=1, source_target_pairs={{1,0},{0,1},{3,2},{2,3},{5,4},{4,5},{7,6},{6,7},{9,8},{8,9},{11,10... | collective-permute-start | bytes 786440 | tf_op jit(solution)/shard_map/ppermute | solution.py:45
